TPU v7x, 32 devices: a whole 2x2x4 slice. The times are simulated.
32 devices in a mesh: dp: 16 (over z, y, core), pre: 2 (over x).
Axes of the slice: x: 2, y: 2, z: 4, core: 2. Of those that a mesh axis runs over, the one named last changes fastest.
Arguments:
- inputs: bfloat16 [2048, 4096], P('dp'), may hold values from -12 to 12, as said below
- weight: bfloat16 [4096, 1024], P(None, 'pre'), may hold values from -0.09375 to 0.09375
- cotangent: bfloat16 [2048, 1024], P('dp', 'pre'), may hold values from -12 to 12, as said below
Outputs:
- outputs: bfloat16 [2048, 1024], P('dp', 'pre')
- update: bfloat16 [8, 512, 1024], P(None, 'pre')
Inputs may be any that keep to these rules, and one draw needn't show every extreme that they name: `inputs`: activations with unequal scales across features. `cotangent`: gradients with unequal scales across features.
All inputs are finite; a program needn't handle non-finite values.
Results may differ from a plain program's by a relative error of at most 0.0079.
Values may be sent and summed in bfloat16 or wider, within the bound.
No kernel may reach another device: no remote copies, remote signals or barrier semaphores. Data moves between devices by JAX's collectives and lax.ppermute only.
A program may use at most 64 MiB of HBM per device.

v0:
```python
import math

import jax
import jax.numpy as jnp
from jax import lax
from jax.sharding import PartitionSpec as P

D = 4096
BLOCK = 512
CB = 2
ITERS = 3


DAMPING = 0.1
HIGH = lax.Precision.HIGHEST


def batch_dot(former, latter):
    return jnp.einsum(
        "sij,sjk->sik", former, latter, precision=HIGH, preferred_element_type=jnp.float32
    )


def on_device(inputs, weight, cotangent):
    groups = lax.axis_size("dp")
    members = lax.axis_size("pre")
    group_id = lax.axis_index("dp")
    member_id = lax.axis_index("pre")
    slab_rows = BLOCK // members
    blocks_all = D // BLOCK * CB
    rounds = max(1, blocks_all // groups)
    sharers = max(1, groups // blocks_all)
    col_width = BLOCK // sharers
    copy_id = group_id // blocks_all
    outputs = jnp.dot(inputs, weight, preferred_element_type=jnp.float32).astype(jnp.bfloat16)
    partial_value = lax.dot_general(
        inputs, cotangent, (((0,), (0,)), ((), ())), preferred_element_type=jnp.float32
    )
    owned_ids = (group_id + groups * jnp.arange(rounds, dtype=jnp.int32)) % blocks_all
    row_offsets = owned_ids // CB * BLOCK
    col_offsets = owned_ids % CB * BLOCK
    gradient = lax.psum(partial_value, "dp")
    row_bands = jax.vmap(lambda offset: lax.dynamic_slice_in_dim(gradient, offset, BLOCK, 0))(
        row_offsets
    )
    wide_band = lax.all_gather(row_bands, "pre", axis=2, tiled=True)
    tile_grad = jax.vmap(
        lambda row_band, offset: lax.dynamic_slice_in_dim(row_band, offset, BLOCK, 1)
    )(wide_band, col_offsets)
    first_row = member_id * slab_rows
    own_rows = lax.dynamic_slice_in_dim(tile_grad, first_row, slab_rows, 1)
    own_cols = lax.dynamic_slice_in_dim(tile_grad, first_row, slab_rows, 2)
    left_rows = jnp.einsum(
        "sij,skj->sik", own_rows, tile_grad, precision=HIGH, preferred_element_type=jnp.float32
    )
    right_rows = jnp.einsum(
        "sji,sjk->sik", own_cols, tile_grad, precision=HIGH, preferred_element_type=jnp.float32
    )
    stat_rows = jnp.stack([left_rows, right_rows], axis=1).reshape(rounds * 2, slab_rows, BLOCK)
    tile_energy = jnp.sum(tile_grad * tile_grad, axis=(1, 2))
    energy = jnp.stack([tile_energy, tile_energy], axis=1).reshape(rounds * 2)
    unit_rows = (jnp.arange(BLOCK)[None, :] == (first_row + jnp.arange(slab_rows))[:, None]).astype(
        jnp.float32
    )
    unit_eye = jnp.eye(BLOCK, dtype=jnp.float32)
    state_rows = stat_rows + (DAMPING * energy / BLOCK)[:, None, None] * unit_rows[None]
    root_rows = unit_rows[None]
    for iteration in range(ITERS):
        full_state = lax.all_gather(state_rows, "pre", axis=1, tiled=True)
        if iteration == 0:
            frob_norm = jnp.sqrt(jnp.sum(full_state * full_state, axis=(1, 2)))
            full_state = full_state / frob_norm[:, None, None]
            state_rows = state_rows / frob_norm[:, None, None]
            root_rows = unit_rows[None] * (frob_norm ** (-0.25))[:, None, None]
        factor = (5.0 * unit_eye - full_state) * 0.25
        square = batch_dot(factor, factor)
        square_rows = lax.dynamic_slice_in_dim(square, first_row, slab_rows, 1)
        fourth_rows = batch_dot(square_rows, square)
        state_rows = batch_dot(fourth_rows, full_state)
        root_rows = batch_dot(root_rows, factor)
    root_half = root_rows.astype(jnp.bfloat16).reshape(rounds, 2, slab_rows, BLOCK)
    right_full = lax.all_gather(root_half[:, 1], "pre", axis=1, tiled=True)
    right_cols = lax.dynamic_slice_in_dim(right_full, copy_id * col_width, col_width, 2)
    tile_half = tile_grad.astype(jnp.bfloat16)
    half_prod = jnp.einsum(
        "sij,sjk->sik", root_half[:, 0], tile_half, preferred_element_type=jnp.float32
    ).astype(jnp.bfloat16)
    piece_rows = jnp.einsum(
        "sij,sjk->sik", half_prod, right_cols, preferred_element_type=jnp.float32
    )
    piece_rows = (piece_rows * math.sqrt(BLOCK)).astype(jnp.bfloat16)
    collected = lax.all_gather(piece_rows[None], "dp", axis=0, tiled=True)
    if sharers == 1:
        ordered = jnp.swapaxes(collected, 0, 1).reshape(blocks_all, slab_rows, BLOCK)
    else:
        ordered = (
            collected[:, 0]
            .reshape(sharers, blocks_all, slab_rows, col_width)
            .transpose(1, 2, 0, 3)
            .reshape(blocks_all, slab_rows, BLOCK)
        )
    update = (
        ordered.reshape(D // BLOCK, CB, slab_rows, BLOCK)
        .transpose(0, 2, 1, 3)
        .reshape(D // BLOCK, slab_rows, CB * BLOCK)
    )
    return (outputs, update)


def solution(mesh):
    placed = (P("dp", None), P(None, "pre"), P("dp", "pre"))
    return jax.shard_map(
        on_device,
        mesh=mesh,
        in_specs=placed,
        out_specs=(P("dp", "pre"), P(None, "pre", None)),
        check_vma=False,
    )
```

profile of v0, /device:TPU:0, one launch (start us, length us, event | category | flops | bytes accessed | tf_op | source)
XLA Modules:
  0.0 430.1 jit_solution(4179174358964834303)
XLA Ops:
  7.2 0.0 copy-start
  7.2 0.0 all-reduce.2.cloned.1.call-start
  7.2 1.2 copy-done
  8.4 5.4 %fusion.53 = f32[4096,512]{1,0:T(8,128)} fusion(bf16[128,4096]{1,0:T(8,128)(2,1)S(1)} %copy-done, bf16[128,512]{1,0:T(8,128)(2,1)} %param.5), kind=kOutput, calls=%fused_computation.67 | convolution fusion | flops 536870912 | bytes 9568256 | tf_op jit(solution)/shard_map/dot_general | solution.py:36
  13.8 0.0 all-reduce.2.cloned.1.call-update
  13.8 0.0 all-gather.15.cloned.1.call-start
  13.9 172.7 %all-reduce.2.cloned.1.call-done = f32[4096,512]{1,0:T(8,128)} async-done(((f32[4096,512]{1,0:T(8,128)}), f32[4096,512]{1,0:T(8,128)}) %all-reduce.2.cloned.1.call-update) | async-done | bytes 8388624 | tf_op jit(solution)/shard_map/psum | solution.py:42
  186.6 2.3 constant_dynamic-slice_fusion
  188.9 0.0 all-gather.15.cloned.1.call-update
  188.9 0.0 all-gather.9.cloned.1.call-start
  189.0 0.1 fusion.38
  189.1 0.0 copy-start.6
  189.1 32.9 %all-gather.15.cloned.1.call-done = f32[512,1024]{1,0:T(8,128)} async-done(((f32[512,512]{1,0:T(8,128)}), f32[512,1024]{1,0:T(8,128)}) %all-gather.15.cloned.1.call-update) | async-done | bytes 2097168 | tf_op jit(solution)/shard_map/all_gather | solution.py:46
  222.0 2.2 multiply_reduce_fusion.1
  224.3 0.7 fusion.45
  225.0 2.5 convolution_bitcast_fusion.1
  227.5 1.4 convolution_bitcast_fusion
  228.9 0.0 copy-done.6
  228.9 1.2 fusion.14
  230.2 0.0 all-gather.9.cloned.1.call-update
  230.2 0.2 all-gather.11.cloned.1.call-start
  230.4 0.1 fusion.30
  230.6 0.0 copy-start.2
  230.6 33.0 %all-gather.9.cloned.1.call-done = f32[2,512,512]{2,1,0:T(8,128)} async-done(((f32[2,256,512]{2,1,0:T(8,128)}), f32[2,512,512]{2,1,0:T(8,128)}) %all-gather.9.cloned.1.call-update) | async-done | bytes 2097168 | tf_op jit(solution)/shard_map/all_gather | solution.py:69
  263.6 2.1 multiply_reduce_fusion
  265.7 0.1 copy-done.5
  265.8 4.0 fusion.3
  269.8 1.9 fusion.17
  271.8 3.1 fusion.51
  274.9 0.0 all-gather.11.cloned.1.call-update
  274.9 0.3 all-gather.13.cloned.1.call-start
  275.2 33.0 %all-gather.11.cloned.1.call-done = f32[2,512,512]{2,1,0:T(8,128)} async-done(((f32[2,256,512]{2,1,0:T(8,128)}), f32[2,512,512]{2,1,0:T(8,128)}) %all-gather.11.cloned.1.call-update) | async-done | bytes 2097168 | tf_op jit(solution)/shard_map/all_gather | solution.py:69
  308.2 6.0 %fusion.5 = f32[2,512,512]{2,1,0:T(8,128)S(1)} fusion(f32[2,512,512]{2,1,0:T(8,128)} %all-gather.11.cloned.1.call-done, f32[512,512]{1,0:T(8,128)S(1)} %fusion.30), kind=kOutput, calls=%fused_computation.8 | convolution fusion | flops 3222274048 | bytes 5242880 | tf_op jit(solution)/shard_map/sij,sjk->sik/dot_general | solution.py:19
  314.1 1.9 fusion.15
  316.1 2.9 fusion.54
  319.0 0.0 all-gather.13.cloned.1.call-update
  319.1 0.3 all-gather.17.cloned.1.call-start
  319.4 0.0 copy-start.3
  319.4 4.5 %fusion.4 = f32[2,256,512]{2,1,0:T(8,128)S(1)} fusion(f32[512,512]{1,0:T(8,128)} %copy-done.2, f32[2]{0:T(128)S(1)} %get-tuple-element.25, f32[256,512]{1,0:T(8,128)} %copy-done.6, f32[2,512,512]{2,1,0:T(8,128)} %all-gather.9.cloned.1.call-done, f32[2]{0:T(128)S(1)} %get-tuple-element.24), kind=kOutput, calls=%fused_computation.7 | convolution fusion | flops 1612447744 | bytes 4718608 | tf_op jit(solution)/shard_map/sij,sjk->sik/dot_general | solution.py:19
  323.9 3.1 fusion.6
  326.9 25.4 %all-gather.13.cloned.1.call-done = f32[2,512,512]{2,1,0:T(8,128)} async-done(((f32[2,256,512]{2,1,0:T(8,128)}), f32[2,512,512]{2,1,0:T(8,128)}) %all-gather.13.cloned.1.call-update) | async-done | bytes 2097168 | tf_op jit(solution)/shard_map/all_gather | solution.py:69
  352.3 4.2 fusion.10
  356.6 8.7 %all-gather.1 = bf16[1,1,512,512]{3,2,1,0:T(8,128)(2,1)S(1)} all-gather(bf16[1,1,256,512]{3,2,1,0:T(8,128)(2,1)S(1)} %slice.37), channel_id=3, replica_groups=mesh['dp'=16,'pre'=2] {'pre'}, dimensions={2}, use_global_device_ids=true | all-gather | bytes 786432 | tf_op jit(solution)/shard_map/all_gather | solution.py:82
  365.3 2.4 fusion.13
  367.7 0.0 all-gather.17.cloned.1.call-update
  367.8 3.6 convolution_convert_fusion.1
  371.3 47.2 %all-gather.17.cloned.1.call-done = bf16[4096,512]{1,0:T(8,128)(2,1)} async-done(((bf16[256,512]{1,0:T(8,128)(2,1)}), bf16[4096,512]{1,0:T(8,128)(2,1)}) %all-gather.17.cloned.1.call-update) | async-done | bytes 4194320 | tf_op jit(solution)/shard_map/all_gather | solution.py:92
  418.5 4.8 %copy.6 = bf16[8,2,32,8,512]{4,3,1,2,0:T(8,128)(2,1)} copy(bf16[8,2,32,8,512]{4,3,2,1,0:T(8,128)(2,1)} %bitcast.39) | data formatting | bytes 8388608 | tf_op jit(solution)/shard_map/reshape | solution.py:105
  (10 shorter events, 0.1 us)
Async XLA Ops:
  7.2 1.2 copy-start
  7.2 179.5 %all-reduce.2.cloned.1.call-start = ((), (), s32[]{:S(2)}) async-start(), calls=%async_computation | async-start | bytes 16777216 | tf_op jit(solution)/shard_map/psum | solution.py:42
  13.8 208.2 %all-gather.15.cloned.1.call-start = ((), (), s32[]{:S(2)}) async-start(), calls=%async_computation.4 | async-start | bytes 3145728 | tf_op jit(solution)/shard_map/all_gather | solution.py:46
  188.9 74.7 %all-gather.9.cloned.1.call-start = ((), (), s32[]{:S(2)}) async-start(), calls=%async_computation.1 | async-start | bytes 3145728 | tf_op jit(solution)/shard_map/all_gather | solution.py:69
  189.1 39.8 %copy-start.6 = (f32[256,512]{1,0:T(8,128)}, f32[256,512]{1,0:T(8,128)S(1)}, u32[]{:S(2)}) copy-start(f32[256,512]{1,0:T(8,128)S(1)} %fusion.38) | copy-start | bytes 1572868
  222.0 5.5 %copy-start.4 = (f32[512,1024]{1,0:T(8,128)S(1)}, f32[512,1024]{1,0:T(8,128)}, u32[]{:S(2)}) copy-start(f32[512,1024]{1,0:T(8,128)} %all-gather.15.cloned.1.call-done) | copy-start | bytes 6291460
  230.2 78.0 %all-gather.11.cloned.1.call-start = ((), (), s32[]{:S(2)}) async-start(), calls=%async_computation.2 | async-start | bytes 3145728 | tf_op jit(solution)/shard_map/all_gather | solution.py:69
  230.6 77.6 %copy-start.2 = (f32[512,512]{1,0:T(8,128)}, f32[512,512]{1,0:T(8,128)S(1)}, u32[]{:S(2)}) copy-start(f32[512,512]{1,0:T(8,128)S(1)} %fusion.30) | copy-start | bytes 3145732
  263.6 2.2 copy-start.5
  274.9 77.4 %all-gather.13.cloned.1.call-start = ((), (), s32[]{:S(2)}) async-start(), calls=%async_computation.3 | async-start | bytes 3145728 | tf_op jit(solution)/shard_map/all_gather | solution.py:69
  314.1 2.0 copy-start.1
  319.1 99.4 %all-gather.17.cloned.1.call-start = ((), (), s32[]{:S(2)}) async-start(), calls=%async_computation.5 | async-start | bytes 4456448 | tf_op jit(solution)/shard_map/all_gather | solution.py:92
  319.4 4.5 %copy-start.3 = (f32[512,512]{1,0:T(8,128)S(1)}, f32[512,512]{1,0:T(8,128)}, u32[]{:S(2)}) copy-start(f32[512,512]{1,0:T(8,128)} %copy-done.2) | copy-start | bytes 3145732
Sparse Core Ops, SparseCore 0:
  14.0 172.6 all-reduce.1
  189.0 32.9 all-gather.14
  230.3 33.1 all-gather.8
  275.0 33.1 all-gather.10
  319.2 33.1 all-gather.12
  367.9 50.5 all-gather.16
where the time goes:
time: 430 us
  waiting for transfers between devices  344 us (80%)
  matrix products  47 us (11%)
  between operations  14.3 us (3%)
  blocking collectives  8.72 us (2%)
  local copies, waits for them, and re-layouts  8.37 us (2%)
  other arithmetic  6.52 us (2%)
    psum x1, waiting for transfers between devices, on_device(): gradient = lax.psum(partial_value, 'dp')  173 us
    all_gather x3, waiting for transfers between devices, on_device(): full_state = lax.all_gather(state_rows, 'pre', axis=1, tiled=True)  91.4 us
    all_gather x1, waiting for transfers between devices, on_device(): collected = lax.all_gather(piece_rows[None], 'dp', axis=0, tiled=True)  47.2 us
    all_gather x1, waiting for transfers between devices, on_device(): wide_band = lax.all_gather(row_bands, 'pre', axis=2, tiled=True)  32.9 us
    dot_general x9, matrix products, batch_dot(): jnp.einsum('sij,sjk->sik', former, latter, precision=HIGH, preferred_elem...  31.6 us
    all_gather x1, blocking collectives, on_device(): right_full = lax.all_gather(root_half[:, 1], 'pre', axis=1, tiled=True)  8.72 us
  transfers between devices with their start and end apart: 6, of which 6 were waited for; matrix products, arithmetic and copies ran while one was open for 3% of the time, Pallas kernels for 0%

commit v1 on v0

--- a/solution.py
+++ b/solution.py
@@ -3,6 +3,8 @@
 import jax
 import jax.numpy as jnp
 from jax import lax
+from jax.experimental import pallas as pl
+from jax.experimental.pallas import tpu as pltpu
 from jax.sharding import PartitionSpec as P
 
 D = 4096
@@ -21,7 +23,7 @@
     )
 
 
-def on_device(inputs, weight, cotangent):
+def on_device_general(inputs, weight, cotangent):
     groups = lax.axis_size("dp")
     members = lax.axis_size("pre")
     group_id = lax.axis_index("dp")
@@ -107,10 +109,300 @@
     return (outputs, update)
 
 
+def contract(former, latter, former_dim, latter_dim):
+    return lax.dot_general(
+        former,
+        latter,
+        (((former_dim,), (latter_dim,)), ((), ())),
+        preferred_element_type=jnp.float32,
+    )
+
+
+def product(former, latter):
+    return contract(former.astype(jnp.bfloat16), latter.astype(jnp.bfloat16), 1, 0)
+
+
+def total(array):
+    return jnp.sum(jnp.sum(array, axis=0, keepdims=True), axis=1, keepdims=True)
+
+
+def newton_step(state):
+    excess = product(state, state) * (1.0 / 16.0) - 0.625 * state
+    growth = 3.125 * excess + product(excess, excess)
+    return (625.0 / 256.0) * state + product(state, growth)
+
+
+def newton_kernel(side_ref, mine_ref, other_ref, tile_ref, root_ref, stat_ref):
+    tile = mine_ref[...] + other_ref[...]
+    tile_half = tile.astype(jnp.bfloat16)
+    tile_ref[...] = tile_half
+
+    @pl.when(side_ref[0] == 0)
+    def _():
+        stat_ref[...] = contract(tile_half, tile_half, 1, 1)
+
+    @pl.when(side_ref[0] != 0)
+    def _():
+        stat_ref[...] = contract(tile_half, tile_half, 0, 0)
+
+    order = tile.shape[0]
+    row_ids = lax.broadcasted_iota(jnp.int32, (order, order), 0)
+    col_ids = lax.broadcasted_iota(jnp.int32, (order, order), 1)
+    on_diagonal = row_ids == col_ids
+    damp = (DAMPING / order) * total(tile * tile)
+    matrix = stat_ref[...]
+    matrix = jnp.where(on_diagonal, matrix + damp, matrix)
+    norm = jnp.sqrt(total(matrix * matrix))
+    first = matrix / norm
+    second = newton_step(first)
+    third = newton_step(second)
+    cross = product(first, second) * (1.0 / 16.0) - (5.0 / 16.0) * (first + second)
+    last = product(cross, third)
+    root = 1.25 * cross - 0.25 * last - (25.0 / 64.0) * third
+    root = jnp.where(on_diagonal, root + 125.0 / 64.0, root)
+    scale = 1.0 / jnp.sqrt(jnp.sqrt(norm))
+    root_ref[...] = (root * scale).astype(jnp.bfloat16)
+
+
+OFFSETS = ((1, 4, 7, 2), (3, 5, 6, 2))
+
+
+def pack_kernel(place_ref, inputs_ref, *piece_refs):
+    for step, piece_ref in enumerate(piece_refs):
+        rows = piece_ref.shape[0]
+        last = step == len(piece_refs) - 1
+        first_row = pl.multiple_of(place_ref[0], rows) if last else 0
+        first_col = pl.multiple_of(place_ref[1 + step] * BLOCK, BLOCK)
+        piece_ref[...] = inputs_ref[pl.ds(first_row, rows), pl.ds(first_col, BLOCK)]
+
+
+def ring_band(position, bands):
+    position = (position + 2 * bands) % bands
+    return jnp.where(position < bands // 2, 2 * position, 2 * (bands - 1 - position) + 1)
+
+
+def tile_kernel(place_ref, own_ref, *refs):
+    hops = len(OFFSETS[0])
+    near_refs, far_refs = refs[:hops], refs[hops : 2 * hops]
+    cot_refs = refs[2 * hops : -3]
+    partial_ref, band_ref, cot_ref = refs[-3:]
+    plane, band, spot = place_ref[0], place_ref[1], place_ref[2]
+    tokens = own_ref.shape[0]
+
+    def put(to_ref, piece_ref, source, part):
+        rows = piece_ref.shape[0]
+        first_row = pl.multiple_of(source * tokens + part * rows, rows)
+        to_ref[pl.ds(first_row, rows), :] = piece_ref[...]
+
+    put(band_ref, own_ref, band, 0)
+    for hop in range(hops):
+        last = hop == hops - 1
+        for piece_ref, member in ((near_refs[hop], plane), (far_refs[hop], 1 - plane)):
+            offset = jnp.where(member == 0, OFFSETS[0][hop], OFFSETS[1][hop])
+            put(band_ref, piece_ref, band ^ offset, member if last else 0)
+    for step, piece_ref in enumerate(cot_refs):
+        put(cot_ref, piece_ref, ring_band(spot - step, len(cot_refs)), 0)
+    partial_ref[...] = contract(band_ref[...], cot_ref[...], 0, 0)
+
+
+def update_kernel(side_ref, mine_ref, other_ref, tile_ref, near_ref, far_ref):
+    rows = near_ref.shape[0]
+    tile = tile_ref[...]
+    core, plane = side_ref[0], side_ref[1]
+
+    def write(left_ref, right_ref):
+        for out_ref, member in ((near_ref, plane), (far_ref, 1 - plane)):
+            first_row = pl.multiple_of(member * rows, rows)
+            left = left_ref[pl.ds(first_row, rows), :]
+            half = contract(left, tile, 1, 0).astype(jnp.bfloat16)
+            piece = contract(half, right_ref[...], 1, 0) * math.sqrt(BLOCK)
+            out_ref[...] = piece.astype(jnp.bfloat16)
+
+    @pl.when(core == 0)
+    def _():
+        write(mine_ref, other_ref)
+
+    @pl.when(core != 0)
+    def _():
+        write(other_ref, mine_ref)
+
+
+def place_kernel(place_ref, *refs):
+    hops = (len(refs) - 4) // 4
+    update_ref, sems = refs[-2:]
+    core, plane, spot = place_ref[0], place_ref[1], place_ref[2]
+    bands = update_ref.shape[0]
+    ahead = 1 - 2 * core
+    copies = []
+
+    def put(piece_ref, position, part, chunk):
+        rows = piece_ref.shape[0]
+        member = plane if chunk == 0 else 1 - plane
+        first_row = pl.multiple_of(part * rows, rows)
+        first_col = pl.multiple_of(member * BLOCK, BLOCK)
+        to_ref = update_ref.at[
+            ring_band(position, bands), pl.ds(first_row, rows), pl.ds(first_col, BLOCK)
+        ]
+        copy = pltpu.make_async_copy(piece_ref, to_ref, sems.at[len(copies)])
+        copy.start()
+        copies.append(copy)
+
+    for chunk in range(2):
+        put(refs[chunk], spot, 0, chunk)
+    for hop in range(1, hops + 1):
+        last = hop == hops
+        for chunk in range(2):
+            mine_ref, other_ref = refs[2 + 4 * (hop - 1) + 2 * chunk :][:2]
+            put(mine_ref, spot - ahead * hop, core if last else 0, chunk)
+            put(other_ref, spot + ahead * hop, 1 - core if last else 0, chunk)
+    for copy in copies:
+        copy.wait()
+
+
+def call(kernel, out_shapes, scratch_shapes, *operands):
+    in_specs = [pl.BlockSpec(memory_space=pltpu.SMEM)]
+    in_specs += [pl.BlockSpec(memory_space=pltpu.VMEM)] * (len(operands) - 1)
+    return pl.pallas_call(
+        kernel,
+        out_shape=out_shapes,
+        in_specs=in_specs,
+        out_specs=[pl.BlockSpec(memory_space=pltpu.VMEM)] * len(out_shapes),
+        scratch_shapes=scratch_shapes,
+        compiler_params=pltpu.CompilerParams(vmem_limit_bytes=32 * 1024 * 1024),
+    )(*operands)
+
+
+def on_device_paired(inputs, weight, cotangent):
+    bands = D // BLOCK
+    groups = lax.axis_size("dp")
+    cores = groups // bands
+    members = lax.axis_size("pre")
+    core = lax.axis_index("dp") % cores
+    band = lax.axis_index("dp") // cores
+    plane = lax.axis_index("pre")
+    tokens = inputs.shape[0]
+    spot = jnp.where(band % 2 == 0, band // 2, bands - 1 - band // 2)
+
+    ring = list(range(0, bands, 2)) + list(range(bands - 1, 0, -2))
+
+    def shift(array, distance):
+        pairs = [
+            (ring[k] * cores + c, ring[(k + distance) % bands] * cores + c)
+            for k in range(bands)
+            for c in range(cores)
+        ]
+        return lax.ppermute(array, "dp", pairs)
+
+    def swap_core(array):
+        return lax.ppermute(array, "dp", [(g, g ^ 1) for g in range(groups)])
+
+    def swap_plane(array):
+        return lax.ppermute(array, "pre", [(c, members - 1 - c) for c in range(members)])
+
+    def around(array):
+        pieces = [array] + [None] * (bands - 1)
+        for step in range(1, bands // 2 + 1):
+            pieces[step] = shift(pieces[step - 1], 1)
+            if step < bands // 2:
+                pieces[bands - step] = shift(pieces[(bands - step + 1) % bands], -1)
+        return pieces
+
+    def deal(array, hop):
+        pairs = [
+            (
+                (k * cores + c) * members + m,
+                ((k ^ OFFSETS[m][hop]) * cores + c) * members + m,
+            )
+            for k in range(bands)
+            for c in range(cores)
+            for m in range(members)
+        ]
+        return lax.ppermute(array, ("dp", "pre"), pairs)
+
+    hops = range(len(OFFSETS[0]))
+    bands_out = [band ^ jnp.where(plane == 0, OFFSETS[0][hop], OFFSETS[1][hop]) for hop in hops]
+    own_band, *packed = call(
+        pack_kernel,
+        [jax.ShapeDtypeStruct((tokens, BLOCK), inputs.dtype)] * len(hops)
+        + [jax.ShapeDtypeStruct((tokens // 2, BLOCK), inputs.dtype)],
+        [],
+        jnp.stack([plane * (tokens // 2), band] + bands_out).astype(jnp.int32),
+        inputs,
+    )
+    cots = around(cotangent)
+    near = [deal(piece, hop) for hop, piece in zip(hops, packed)]
+    far = [swap_plane(piece) for piece in near]
+    outputs = jnp.dot(inputs, weight, preferred_element_type=jnp.float32).astype(jnp.bfloat16)
+    own_band, outputs = lax.optimization_barrier((own_band, outputs))
+    (partial_tile,) = call(
+        tile_kernel,
+        [jax.ShapeDtypeStruct((BLOCK, BLOCK), jnp.float32)],
+        [pltpu.VMEM((bands * tokens, BLOCK), inputs.dtype)] * 2,
+        jnp.stack([plane, band, spot]).astype(jnp.int32),
+        own_band,
+        *near,
+        *far,
+        *cots,
+    )
+    other_partial = swap_core(partial_tile)
+    side = jnp.stack([core, plane]).astype(jnp.int32)
+    tile_half, root = call(
+        newton_kernel,
+        [
+            jax.ShapeDtypeStruct((BLOCK, BLOCK), jnp.bfloat16),
+            jax.ShapeDtypeStruct((BLOCK, BLOCK), jnp.bfloat16),
+        ],
+        [pltpu.VMEM((BLOCK, BLOCK), jnp.float32)],
+        side,
+        partial_tile,
+        other_partial,
+    )
+    other_root = swap_core(root)
+    rows = BLOCK // members
+    near_piece, far_piece = call(
+        update_kernel,
+        [jax.ShapeDtypeStruct((rows, BLOCK), jnp.bfloat16)] * 2,
+        [],
+        side,
+        root,
+        other_root,
+        tile_half,
+    )
+
+    def turn(array):
+        pairs = [
+            (ring[k] * cores + c, ring[(k + 1 - 2 * c) % bands] * cores + c)
+            for k in range(bands)
+            for c in range(cores)
+        ]
+        return lax.ppermute(array, "dp", pairs)
+
+    half_way = bands // 2
+    heads = [near_piece, swap_plane(far_piece)]
+    pieces = list(heads)
+    for hop in range(1, half_way + 1):
+        for chunk in range(2):
+            head = heads[chunk]
+            if hop == half_way:
+                head = lax.dynamic_slice_in_dim(head.reshape(2, -1, BLOCK), core, 1, 0)[0]
+            heads[chunk] = turn(head)
+            pieces += [heads[chunk], swap_core(heads[chunk])]
+    update = pl.pallas_call(
+        place_kernel,
+        out_shape=jax.ShapeDtypeStruct((bands, rows, CB * BLOCK), jnp.bfloat16),
+        in_specs=[pl.BlockSpec(memory_space=pltpu.SMEM)]
+        + [pl.BlockSpec(memory_space=pltpu.VMEM)] * len(pieces),
+        out_specs=pl.BlockSpec(memory_space=pl.ANY),
+        scratch_shapes=[pltpu.SemaphoreType.DMA((len(pieces),))],
+    )(jnp.stack([core, plane, spot]).astype(jnp.int32), *pieces)
+    return (outputs, update)
+
+
 def solution(mesh):
     placed = (P("dp", None), P(None, "pre"), P("dp", "pre"))
+    paired = mesh.shape["dp"] == 2 * D // BLOCK and mesh.shape["pre"] == CB == 2
     return jax.shard_map(
-        on_device,
+        on_device_paired if paired else on_device_general,
         mesh=mesh,
         in_specs=placed,
         out_specs=(P("dp", "pre"), P(None, "pre", None)),

time: 430 us -> 85.6 us (0.20)
  waiting for transfers between devices: 344 us -> 28.6 us
  matrix products: 47 us -> 3.57 us
  starting transfers between devices: 0.91 us -> 37.4 us
  between operations: 14.3 us -> 0.89 us
  Pallas kernels: 0 us -> 12 us
  blocking collectives: 8.72 us -> 0 us
  local copies, waits for them, and re-layouts: 8.37 us -> 2.06 us
  other arithmetic: 6.52 us -> 0.76 us
    psum x1 -> x0, waiting for transfers between devices: 173 us -> none  [on_device(): gradient = lax.psum(partial_value, 'dp')]
    all_gather x5 -> x0, waiting for transfers between devices: 171 us -> none  [the longest x3 91.4 us: on_device(): full_state = lax.all_gather(state_rows, 'pre', axis=1, tiled=True)]
    dot_general x14 -> x1, matrix products: 47 us -> 3.57 us  [on_device_paired(): jnp.dot(inputs, weight, preferred_element_type=jnp.float32)]
    ppermute x0 -> x34, starting transfers between devices: none -> 37.4 us  [the longest x8 12.4 us: turn(): return lax.ppermute(array, 'dp', pairs)]
    ppermute x0 -> x34, waiting for transfers between devices: none -> 28.6 us  [the longest x8 11.9 us: turn(): return lax.ppermute(array, 'dp', pairs)]
    pallas_call x0 -> x5, Pallas kernels: none -> 12 us  [the longest x4 7.71 us: call(): pl.pallas_call(kernel, out_shape=out_shapes, in_specs=in_specs, out_specs...]
    all_gather x1 -> x0, blocking collectives: 8.72 us -> none  [on_device(): right_full = lax.all_gather(root_half[:, 1], 'pre', axis=1, tiled=True)]
    reshape x1 -> x0, local copies, waits for them, and re-layouts: 4.78 us -> none  [on_device(): update = ordered.reshape(D // BLOCK, CB, slab_rows, BLOCK).transpose(0, 2...]
  transfers between devices with their start and end apart: 6 -> 34, of which waited for: 6 -> 13; matrix products, arithmetic and copies ran while one was open for 3% -> 5% of each run, Pallas kernels for 0% -> 1%
where the time goes in v1:
time: 85.6 us; the launch traced here: 85.4 us
  starting transfers between devices  37.4 us (44%)
  waiting for transfers between devices  28.6 us (33%)
  Pallas kernels  12 us (14%)
  matrix products  3.57 us (4%)
  local copies, waits for them, and re-layouts  2.06 us (2%)
  between operations  0.89 us (1%)
    ppermute x8, starting transfers between devices, turn(): return lax.ppermute(array, 'dp', pairs)  12.4 us
    ppermute x8, waiting for transfers between devices, turn(): return lax.ppermute(array, 'dp', pairs)  11.9 us
    ppermute x7, starting transfers between devices, shift(): return lax.ppermute(array, 'dp', pairs)  8.61 us
    ppermute x4, starting transfers between devices, deal(): return lax.ppermute(array, ('dp', 'pre'), pairs)  8.11 us
    pallas_call x4, Pallas kernels, call(): pl.pallas_call(kernel, out_shape=out_shapes, in_specs=in_specs, out_specs...  7.71 us
    ppermute x5, starting transfers between devices, swap_plane(): lax.ppermute(array, 'pre', [(c, members - 1 - c) for c in range(members)])  6.39 us
    ppermute x4, waiting for transfers between devices, deal(): return lax.ppermute(array, ('dp', 'pre'), pairs)  6.26 us
    ppermute x5, waiting for transfers between devices, swap_plane(): lax.ppermute(array, 'pre', [(c, members - 1 - c) for c in range(members)])  5.4 us
  transfers between devices with their start and end apart: 34, of which 13 were waited for; matrix products, arithmetic and copies ran while one was open for 5% of the time, Pallas kernels for 1%

profile of v1, /device:TPU:0, one launch (start us, length us, event | category | flops | bytes accessed | tf_op | source)
XLA Modules:
  0.0 85.4 jit_solution(3048506535586618513)
XLA Ops:
  0.6 3.1 %collective-permute-start.8 = (bf16[128,512]{1,0:T(8,128)(2,1)}, bf16[128,512]{1,0:T(8,128)(2,1)S(1)}, u32[]{:S(2)}, u32[]{:S(2)}) collective-permute-start(bf16[128,512]{1,0:T(8,128)(2,1)} %refs_8_.1), channel_id=1, source_target_pairs={{0,8},{2,10},{8,16},{10,18},{16,24},{18,26},{24,28},{26,30},{28,20... | collective-permute-start | bytes 393224 | tf_op jit(solution)/shard_map/ppermute | solution.py:294
  3.8 1.2 %copy-done = bf16[128,4096]{1,0:T(8,128)(2,1)S(1)} copy-done((bf16[128,4096]{1,0:T(8,128)(2,1)S(1)}, bf16[128,4096]{1,0:T(8,128)(2,1)}, u32[]{:S(2)}) %copy-start) | copy-done | bytes 1048600
  5.0 0.6 shard_map.50
  5.6 2.1 %collective-permute-start.3 = (bf16[64,512]{1,0:T(8,128)(2,1)S(1)}, bf16[64,512]{1,0:T(8,128)(2,1)S(1)}, u32[]{:S(2)}, u32[]{:S(2)}) collective-permute-start(bf16[64,512]{1,0:T(8,128)(2,1)S(1)} %get-tuple-element.19), channel_id=1, source_target_pairs={{0,8},{1,9},{2,10},{3,11},{4,12},{5,13},{6,14},{7,15},{8,0},{9,1},... | collective-permute-start | bytes 196616 | tf_op jit(solution)/shard_map/ppermute | solution.py:320
  7.7 1.4 %collective-permute-start.9 = (bf16[128,512]{1,0:T(8,128)(2,1)S(1)}, bf16[128,512]{1,0:T(8,128)(2,1)S(1)}, u32[]{:S(2)}, u32[]{:S(2)}) collective-permute-start(bf16[128,512]{1,0:T(8,128)(2,1)S(1)} %collective-permute-done.8.refs_9_), channel_id=1, source_target_pairs={{0,8},{2,10},{8,16},{10,18},{16,24},{18,26},{24,28},{26,30},{28,20... | collective-permute-start | bytes 393224 | tf_op jit(solution)/shard_map/ppermute | solution.py:294
  9.2 1.1 %collective-permute-done.3.refs_3_ = bf16[64,512]{1,0:T(8,128)(2,1)S(1)} collective-permute-done((bf16[64,512]{1,0:T(8,128)(2,1)S(1)}, bf16[64,512]{1,0:T(8,128)(2,1)S(1)}, u32[]{:S(2)}, u32[]{:S(2)}) %collective-permute-start.3) | collective-permute-done | bytes 65568 | tf_op jit(solution)/shard_map/ppermute | solution.py:320
  10.3 1.6 %collective-permute-start.7 = (bf16[64,512]{1,0:T(8,128)(2,1)S(1)}, bf16[64,512]{1,0:T(8,128)(2,1)S(1)}, u32[]{:S(2)}, u32[]{:S(2)}) collective-permute-start(bf16[64,512]{1,0:T(8,128)(2,1)S(1)} %collective-permute-done.3.refs_3_), channel_id=1, source_target_pairs={{0,1},{1,0},{2,3},{3,2},{4,5},{5,4},{6,7},{7,6},{8,9},{9,8},{10,11... | collective-permute-start | bytes 196616 | tf_op jit(solution)/shard_map/ppermute | solution.py:300
  11.9 2.1 %collective-permute-start = (bf16[128,512]{1,0:T(8,128)(2,1)S(1)}, bf16[128,512]{1,0:T(8,128)(2,1)S(1)}, u32[]{:S(2)}, u32[]{:S(2)}) collective-permute-start(bf16[128,512]{1,0:T(8,128)(2,1)S(1)} %get-tuple-element.16), channel_id=1, source_target_pairs={{0,4},{1,13},{2,6},{3,15},{4,0},{5,9},{6,2},{7,11},{8,12},{9,5},{1... | collective-permute-start | bytes 393224 | tf_op jit(solution)/shard_map/ppermute | solution.py:320
  14.0 2.6 %collective-permute-start.1 = (bf16[128,512]{1,0:T(8,128)(2,1)S(1)}, bf16[128,512]{1,0:T(8,128)(2,1)S(1)}, u32[]{:S(2)}, u32[]{:S(2)}) collective-permute-start(bf16[128,512]{1,0:T(8,128)(2,1)S(1)} %get-tuple-element.17), channel_id=1, source_target_pairs={{0,16},{1,21},{2,18},{3,23},{4,20},{5,17},{6,22},{7,19},{8,24},{9,... | collective-permute-start | bytes 393224 | tf_op jit(solution)/shard_map/ppermute | solution.py:320
  16.6 1.3 %collective-permute-start.2 = (bf16[128,512]{1,0:T(8,128)(2,1)S(1)}, bf16[128,512]{1,0:T(8,128)(2,1)S(1)}, u32[]{:S(2)}, u32[]{:S(2)}) collective-permute-start(bf16[128,512]{1,0:T(8,128)(2,1)S(1)} %get-tuple-element.18), channel_id=1, source_target_pairs={{0,28},{1,25},{2,30},{3,27},{4,24},{5,29},{6,26},{7,31},{8,20},{9,... | collective-permute-start | bytes 393224 | tf_op jit(solution)/shard_map/ppermute | solution.py:320
  17.9 0.9 %collective-permute-start.13 = (bf16[128,512]{1,0:T(8,128)(2,1)S(1)}, bf16[128,512]{1,0:T(8,128)(2,1)S(1)}, u32[]{:S(2)}, u32[]{:S(2)}) collective-permute-start(bf16[128,512]{1,0:T(8,128)(2,1)S(1)} %collective-permute-done.12.refs_15_), channel_id=1, source_target_pairs={{0,4},{2,6},{8,0},{10,2},{16,8},{18,10},{24,16},{26,18},{28,24},{3... | collective-permute-start | bytes 393224 | tf_op jit(solution)/shard_map/ppermute | solution.py:294
  18.8 1.1 %collective-permute-start.10 = (bf16[128,512]{1,0:T(8,128)(2,1)S(1)}, bf16[128,512]{1,0:T(8,128)(2,1)S(1)}, u32[]{:S(2)}, u32[]{:S(2)}) collective-permute-start(bf16[128,512]{1,0:T(8,128)(2,1)S(1)} %collective-permute-done.9.refs_10_), channel_id=1, source_target_pairs={{0,8},{2,10},{8,16},{10,18},{16,24},{18,26},{24,28},{26,30},{28,20... | collective-permute-start | bytes 393224 | tf_op jit(solution)/shard_map/ppermute | solution.py:294
  20.0 0.5 collective-permute-start.4
  20.4 5.1 %collective-permute-done.1.refs_1_ = bf16[128,512]{1,0:T(8,128)(2,1)S(1)} collective-permute-done((bf16[128,512]{1,0:T(8,128)(2,1)S(1)}, bf16[128,512]{1,0:T(8,128)(2,1)S(1)}, u32[]{:S(2)}, u32[]{:S(2)}) %collective-permute-start.1) | collective-permute-done | bytes 131104 | tf_op jit(solution)/shard_map/ppermute | solution.py:320
  25.6 2.3 %collective-permute-start.5 = (bf16[128,512]{1,0:T(8,128)(2,1)S(1)}, bf16[128,512]{1,0:T(8,128)(2,1)S(1)}, u32[]{:S(2)}, u32[]{:S(2)}) collective-permute-start(bf16[128,512]{1,0:T(8,128)(2,1)S(1)} %collective-permute-done.1.refs_1_), channel_id=1, source_target_pairs={{0,1},{1,0},{2,3},{3,2},{4,5},{5,4},{6,7},{7,6},{8,9},{9,8},{10,11... | collective-permute-start | bytes 393224 | tf_op jit(solution)/shard_map/ppermute | solution.py:300
  27.9 0.4 collective-permute-start.14
  28.3 1.7 %collective-permute-start.11 = (bf16[128,512]{1,0:T(8,128)(2,1)S(1)}, bf16[128,512]{1,0:T(8,128)(2,1)S(1)}, u32[]{:S(2)}, u32[]{:S(2)}) collective-permute-start(bf16[128,512]{1,0:T(8,128)(2,1)S(1)} %collective-permute-done.10.refs_11_), channel_id=1, source_target_pairs={{0,8},{2,10},{8,16},{10,18},{16,24},{18,26},{24,28},{26,30},{28,20... | collective-permute-start | bytes 393224 | tf_op jit(solution)/shard_map/ppermute | solution.py:294
  29.9 3.6 %convolution_convert_fusion = bf16[128,512]{1,0:T(8,128)(2,1)} fusion(bf16[128,4096]{1,0:T(8,128)(2,1)S(1)} %copy-done, bf16[4096,512]{1,0:T(8,128)(2,1)} %param.4), kind=kOutput, calls=%fused_computation | convolution fusion | flops 536936448 | bytes 5373952 | tf_op jit(solution)/shard_map/dot_general | solution.py:335
  33.7 1.4 %shard_map.51.mine_ref = f32[512,512]{1,0:T(8,128)S(1)} custom-call(s32[3]{0:T(128)S(1)} %add_add_fusion.1.place_ref, bf16[128,512]{1,0:T(8,128)(2,1)S(1)} %get-tuple-element.15.own_ref, bf16[128,512]{1,0:T(8,128)(2,1)S(1)} %collective-permute-done.refs_0_, bf16[128,512]{1,0:T(8,128)(2,1)S(1)} %collective-permute-done.1.refs_1_, ...), custom_call_target="tpu_custom_call" | custom-call | tf_op jit(solution)/shard_map/pallas_call | solution.py:265
  35.2 2.6 %collective-permute-done.15.other_ref = f32[512,512]{1,0:T(8,128)S(1)} collective-permute-done((f32[512,512]{1,0:T(8,128)S(1)}, f32[512,512]{1,0:T(8,128)S(1)}, u32[]{:S(2)}, u32[]{:S(2)}) %collective-permute-start.15) | collective-permute-done | bytes 1048608 | tf_op jit(solution)/shard_map/ppermute | solution.py:297
  37.8 4.3 %shard_map.52 = (bf16[512,512]{1,0:T(8,128)(2,1)S(1)}, bf16[512,512]{1,0:T(8,128)(2,1)S(1)}) custom-call(s32[2]{0:T(128)S(1)} %pad_add_fusion.side_ref, f32[512,512]{1,0:T(8,128)S(1)} %shard_map.51.mine_ref, f32[512,512]{1,0:T(8,128)S(1)} %collective-permute-done.15.other_ref), custom_call_target="tpu_custom_call" | custom-call | tf_op jit(solution)/shard_map/pallas_call | solution.py:265
  42.1 0.3 collective-permute-start.16
  42.4 1.7 %collective-permute-done.16.other_ref = bf16[512,512]{1,0:T(8,128)(2,1)S(1)} collective-permute-done((bf16[512,512]{1,0:T(8,128)(2,1)S(1)}, bf16[512,512]{1,0:T(8,128)(2,1)S(1)}, u32[]{:S(2)}, u32[]{:S(2)}) %collective-permute-start.16) | collective-permute-done | bytes 524320 | tf_op jit(solution)/shard_map/ppermute | solution.py:297
  44.1 1.4 %shard_map.53 = (bf16[256,512]{1,0:T(8,128)(2,1)S(1)}, bf16[256,512]{1,0:T(8,128)(2,1)S(1)}) custom-call(s32[2]{0:T(128)S(1)} %pad_add_fusion.side_ref, bf16[512,512]{1,0:T(8,128)(2,1)S(1)} %get-tuple-element.20.mine_ref, bf16[512,512]{1,0:T(8,128)(2,1)S(1)} %collective-permute-done.16.other_ref, bf16[512,512]{1,0:T(8,128)(2,1)S(1)} %get-tuple-element.21.tile_ref), custom_call_target="tpu_custom_call" | custom-call | tf_op jit(solution)/shard_map/pallas_call | solution.py:265
  45.5 2.0 %collective-permute-start.17 = (bf16[256,512]{1,0:T(8,128)(2,1)S(1)}, bf16[256,512]{1,0:T(8,128)(2,1)S(1)}, u32[]{:S(2)}, u32[]{:S(2)}) collective-permute-start(bf16[256,512]{1,0:T(8,128)(2,1)S(1)} %get-tuple-element.23), channel_id=1, source_target_pairs={{0,1},{1,0},{2,3},{3,2},{4,5},{5,4},{6,7},{7,6},{8,9},{9,8},{10,11... | collective-permute-start | bytes 786440 | tf_op jit(solution)/shard_map/ppermute | solution.py:300
  47.5 1.3 %collective-permute-start.18 = (bf16[256,512]{1,0:T(8,128)(2,1)S(1)}, bf16[256,512]{1,0:T(8,128)(2,1)S(1)}, u32[]{:S(2)}, u32[]{:S(2)}) collective-permute-start(bf16[256,512]{1,0:T(8,128)(2,1)S(1)} %get-tuple-element.22.refs_0_), channel_id=1, source_target_pairs={{0,8},{2,6},{8,16},{10,2},{16,24},{18,10},{24,28},{26,18},{28,20},... | collective-permute-start | bytes 786440 | tf_op jit(solution)/shard_map/ppermute | solution.py:378
  48.8 5.4 %collective-permute-done.17.refs_1_ = bf16[256,512]{1,0:T(8,128)(2,1)S(1)} collective-permute-done((bf16[256,512]{1,0:T(8,128)(2,1)S(1)}, bf16[256,512]{1,0:T(8,128)(2,1)S(1)}, u32[]{:S(2)}, u32[]{:S(2)}) %collective-permute-start.17) | collective-permute-done | bytes 262176 | tf_op jit(solution)/shard_map/ppermute | solution.py:300
  54.2 1.5 %collective-permute-start.20 = (bf16[256,512]{1,0:T(8,128)(2,1)S(1)}, bf16[256,512]{1,0:T(8,128)(2,1)S(1)}, u32[]{:S(2)}, u32[]{:S(2)}) collective-permute-start(bf16[256,512]{1,0:T(8,128)(2,1)S(1)} %collective-permute-done.17.refs_1_), channel_id=1, source_target_pairs={{0,8},{2,6},{8,16},{10,2},{16,24},{18,10},{24,28},{26,18},{28,20},... | collective-permute-start | bytes 786440 | tf_op jit(solution)/shard_map/ppermute | solution.py:378
  55.7 1.8 %collective-permute-start.22 = (bf16[256,512]{1,0:T(8,128)(2,1)S(1)}, bf16[256,512]{1,0:T(8,128)(2,1)S(1)}, u32[]{:S(2)}, u32[]{:S(2)}) collective-permute-start(bf16[256,512]{1,0:T(8,128)(2,1)S(1)} %collective-permute-done.18.refs_2_), channel_id=1, source_target_pairs={{0,8},{2,6},{8,16},{10,2},{16,24},{18,10},{24,28},{26,18},{28,20},... | collective-permute-start | bytes 786440 | tf_op jit(solution)/shard_map/ppermute | solution.py:378
  57.6 3.0 %collective-permute-done.20.refs_4_ = bf16[256,512]{1,0:T(8,128)(2,1)S(1)} collective-permute-done((bf16[256,512]{1,0:T(8,128)(2,1)S(1)}, bf16[256,512]{1,0:T(8,128)(2,1)S(1)}, u32[]{:S(2)}, u32[]{:S(2)}) %collective-permute-start.20) | collective-permute-done | bytes 262176 | tf_op jit(solution)/shard_map/ppermute | solution.py:378
  60.6 1.5 %collective-permute-start.24 = (bf16[256,512]{1,0:T(8,128)(2,1)S(1)}, bf16[256,512]{1,0:T(8,128)(2,1)S(1)}, u32[]{:S(2)}, u32[]{:S(2)}) collective-permute-start(bf16[256,512]{1,0:T(8,128)(2,1)S(1)} %collective-permute-done.20.refs_4_), channel_id=1, source_target_pairs={{0,8},{2,6},{8,16},{10,2},{16,24},{18,10},{24,28},{26,18},{28,20},... | collective-permute-start | bytes 786440 | tf_op jit(solution)/shard_map/ppermute | solution.py:378
  62.1 1.3 %collective-permute-done.22.refs_6_ = bf16[256,512]{1,0:T(8,128)(2,1)S(1)} collective-permute-done((bf16[256,512]{1,0:T(8,128)(2,1)S(1)}, bf16[256,512]{1,0:T(8,128)(2,1)S(1)}, u32[]{:S(2)}, u32[]{:S(2)}) %collective-permute-start.22) | collective-permute-done | bytes 262176 | tf_op jit(solution)/shard_map/ppermute | solution.py:378
  63.4 1.5 %collective-permute-start.26 = (bf16[256,512]{1,0:T(8,128)(2,1)S(1)}, bf16[256,512]{1,0:T(8,128)(2,1)S(1)}, u32[]{:S(2)}, u32[]{:S(2)}) collective-permute-start(bf16[256,512]{1,0:T(8,128)(2,1)S(1)} %collective-permute-done.22.refs_6_), channel_id=1, source_target_pairs={{0,8},{2,6},{8,16},{10,2},{16,24},{18,10},{24,28},{26,18},{28,20},... | collective-permute-start | bytes 786440 | tf_op jit(solution)/shard_map/ppermute | solution.py:378
  64.9 2.0 %collective-permute-done.24.refs_8_ = bf16[256,512]{1,0:T(8,128)(2,1)S(1)} collective-permute-done((bf16[256,512]{1,0:T(8,128)(2,1)S(1)}, bf16[256,512]{1,0:T(8,128)(2,1)S(1)}, u32[]{:S(2)}, u32[]{:S(2)}) %collective-permute-start.24) | collective-permute-done | bytes 262176 | tf_op jit(solution)/shard_map/ppermute | solution.py:378
  66.9 1.5 %collective-permute-start.28 = (bf16[256,512]{1,0:T(8,128)(2,1)S(1)}, bf16[256,512]{1,0:T(8,128)(2,1)S(1)}, u32[]{:S(2)}, u32[]{:S(2)}) collective-permute-start(bf16[256,512]{1,0:T(8,128)(2,1)S(1)} %collective-permute-done.24.refs_8_), channel_id=1, source_target_pairs={{0,8},{2,6},{8,16},{10,2},{16,24},{18,10},{24,28},{26,18},{28,20},... | collective-permute-start | bytes 786440 | tf_op jit(solution)/shard_map/ppermute | solution.py:378
  68.5 0.5 collective-permute-start.21
  69.0 0.7 collective-permute-done.26.refs_10_
  69.8 1.6 %collective-permute-start.30 = (bf16[128,512]{1,0:T(8,128)(2,1)S(1)}, bf16[128,512]{1,0:T(8,128)(2,1)S(1)}, u32[]{:S(2)}, u32[]{:S(2)}) collective-permute-start(bf16[128,512]{1,0:T(8,128)(2,1)S(1)} %dynamic-slice_bitcast_fusion.1), channel_id=1, source_target_pairs={{0,8},{2,6},{8,16},{10,2},{16,24},{18,10},{24,28},{26,18},{28,20},... | collective-permute-start | bytes 393224 | tf_op jit(solution)/shard_map/ppermute | solution.py:378
  71.4 2.0 %collective-permute-done.28.refs_12_ = bf16[256,512]{1,0:T(8,128)(2,1)S(1)} collective-permute-done((bf16[256,512]{1,0:T(8,128)(2,1)S(1)}, bf16[256,512]{1,0:T(8,128)(2,1)S(1)}, u32[]{:S(2)}, u32[]{:S(2)}) %collective-permute-start.28) | collective-permute-done | bytes 262176 | tf_op jit(solution)/shard_map/ppermute | solution.py:378
  73.4 0.6 collective-permute-start.27
  73.9 1.5 %collective-permute-start.32 = (bf16[128,512]{1,0:T(8,128)(2,1)S(1)}, bf16[128,512]{1,0:T(8,128)(2,1)S(1)}, u32[]{:S(2)}, u32[]{:S(2)}) collective-permute-start(bf16[128,512]{1,0:T(8,128)(2,1)S(1)} %dynamic-slice_bitcast_fusion), channel_id=1, source_target_pairs={{0,8},{2,6},{8,16},{10,2},{16,24},{18,10},{24,28},{26,18},{28,20},... | collective-permute-start | bytes 393224 | tf_op jit(solution)/shard_map/ppermute | solution.py:378
  75.5 0.1 collective-permute-start.29
  75.6 0.4 collective-permute-start.31
  76.0 2.9 %collective-permute-done.32.refs_16_ = bf16[128,512]{1,0:T(8,128)(2,1)S(1)} collective-permute-done((bf16[128,512]{1,0:T(8,128)(2,1)S(1)}, bf16[128,512]{1,0:T(8,128)(2,1)S(1)}, u32[]{:S(2)}, u32[]{:S(2)}) %collective-permute-start.32) | collective-permute-done | bytes 131104 | tf_op jit(solution)/shard_map/ppermute | solution.py:378
  78.9 0.6 add_add_fusion.place_ref
  79.6 0.7 collective-permute-done.33.refs_17_
  80.3 0.6 copy-done.18
  81.0 4.3 %shard_map.54 = bf16[8,256,1024]{2,1,0:T(8,128)(2,1)} custom-call(s32[3]{0:T(128)} %add_add_fusion.place_ref, bf16[256,512]{1,0:T(8,128)(2,1)} %copy-done.1, bf16[256,512]{1,0:T(8,128)(2,1)} %copy-done.5, bf16[256,512]{1,0:T(8,128)(2,1)} %copy-done.6, bf16[256,512]{1,0:T(8,128)(2,1)} %copy-done.10, bf16[256,512]{1,0:T(8,128)(2,1)} %copy-done.7, ...), custom_call_target="tpu_custom_call" | custom-call | tf_op jit(solution)/shard_map/pallas_call | solution.py:390
  (70 shorter events, 0.6 us)
Async XLA Ops:
  0.6 7.1 %collective-permute-start.8 = (bf16[128,512]{1,0:T(8,128)(2,1)}, bf16[128,512]{1,0:T(8,128)(2,1)S(1)}, u32[]{:S(2)}, u32[]{:S(2)}) collective-permute-start(bf16[128,512]{1,0:T(8,128)(2,1)} %refs_8_.1), channel_id=1, source_target_pairs={{0,8},{2,10},{8,16},{10,18},{16,24},{18,26},{24,28},{26,30},{28,20... | collective-permute-start | bytes 393224 | tf_op jit(solution)/shard_map/ppermute | solution.py:294
  3.7 12.9 %collective-permute-start.12 = (bf16[128,512]{1,0:T(8,128)(2,1)}, bf16[128,512]{1,0:T(8,128)(2,1)S(1)}, u32[]{:S(2)}, u32[]{:S(2)}) collective-permute-start(bf16[128,512]{1,0:T(8,128)(2,1)} %refs_8_.1), channel_id=1, source_target_pairs={{0,4},{2,6},{8,0},{10,2},{16,8},{18,10},{24,16},{26,18},{28,24},{3... | collective-permute-start | bytes 393224 | tf_op jit(solution)/shard_map/ppermute | solution.py:294
  5.0 28.6 %copy-start.2 = (bf16[128,512]{1,0:T(8,128)(2,1)S(1)}, bf16[128,512]{1,0:T(8,128)(2,1)}, u32[]{:S(2)}) copy-start(bf16[128,512]{1,0:T(8,128)(2,1)} %refs_8_.1) | copy-start | bytes 393220
  5.6 4.7 %collective-permute-start.3 = (bf16[64,512]{1,0:T(8,128)(2,1)S(1)}, bf16[64,512]{1,0:T(8,128)(2,1)S(1)}, u32[]{:S(2)}, u32[]{:S(2)}) collective-permute-start(bf16[64,512]{1,0:T(8,128)(2,1)S(1)} %get-tuple-element.19), channel_id=1, source_target_pairs={{0,8},{1,9},{2,10},{3,11},{4,12},{5,13},{6,14},{7,15},{8,0},{9,1},... | collective-permute-start | bytes 196616 | tf_op jit(solution)/shard_map/ppermute | solution.py:320
  7.7 11.1 %collective-permute-start.9 = (bf16[128,512]{1,0:T(8,128)(2,1)S(1)}, bf16[128,512]{1,0:T(8,128)(2,1)S(1)}, u32[]{:S(2)}, u32[]{:S(2)}) collective-permute-start(bf16[128,512]{1,0:T(8,128)(2,1)S(1)} %collective-permute-done.8.refs_9_), channel_id=1, source_target_pairs={{0,8},{2,10},{8,16},{10,18},{16,24},{18,26},{24,28},{26,30},{28,20... | collective-permute-start | bytes 393224 | tf_op jit(solution)/shard_map/ppermute | solution.py:294
  10.3 7.6 %collective-permute-start.7 = (bf16[64,512]{1,0:T(8,128)(2,1)S(1)}, bf16[64,512]{1,0:T(8,128)(2,1)S(1)}, u32[]{:S(2)}, u32[]{:S(2)}) collective-permute-start(bf16[64,512]{1,0:T(8,128)(2,1)S(1)} %collective-permute-done.3.refs_3_), channel_id=1, source_target_pairs={{0,1},{1,0},{2,3},{3,2},{4,5},{5,4},{6,7},{7,6},{8,9},{9,8},{10,11... | collective-permute-start | bytes 196616 | tf_op jit(solution)/shard_map/ppermute | solution.py:300
  11.9 8.1 %collective-permute-start = (bf16[128,512]{1,0:T(8,128)(2,1)S(1)}, bf16[128,512]{1,0:T(8,128)(2,1)S(1)}, u32[]{:S(2)}, u32[]{:S(2)}) collective-permute-start(bf16[128,512]{1,0:T(8,128)(2,1)S(1)} %get-tuple-element.16), channel_id=1, source_target_pairs={{0,4},{1,13},{2,6},{3,15},{4,0},{5,9},{6,2},{7,11},{8,12},{9,5},{1... | collective-permute-start | bytes 393224 | tf_op jit(solution)/shard_map/ppermute | solution.py:320
  14.0 11.6 %collective-permute-start.1 = (bf16[128,512]{1,0:T(8,128)(2,1)S(1)}, bf16[128,512]{1,0:T(8,128)(2,1)S(1)}, u32[]{:S(2)}, u32[]{:S(2)}) collective-permute-start(bf16[128,512]{1,0:T(8,128)(2,1)S(1)} %get-tuple-element.17), channel_id=1, source_target_pairs={{0,16},{1,21},{2,18},{3,23},{4,20},{5,17},{6,22},{7,19},{8,24},{9,... | collective-permute-start | bytes 393224 | tf_op jit(solution)/shard_map/ppermute | solution.py:320
  16.6 11.2 %collective-permute-start.2 = (bf16[128,512]{1,0:T(8,128)(2,1)S(1)}, bf16[128,512]{1,0:T(8,128)(2,1)S(1)}, u32[]{:S(2)}, u32[]{:S(2)}) collective-permute-start(bf16[128,512]{1,0:T(8,128)(2,1)S(1)} %get-tuple-element.18), channel_id=1, source_target_pairs={{0,28},{1,25},{2,30},{3,27},{4,24},{5,29},{6,26},{7,31},{8,20},{9,... | collective-permute-start | bytes 393224 | tf_op jit(solution)/shard_map/ppermute | solution.py:320
  17.9 10.0 %collective-permute-start.13 = (bf16[128,512]{1,0:T(8,128)(2,1)S(1)}, bf16[128,512]{1,0:T(8,128)(2,1)S(1)}, u32[]{:S(2)}, u32[]{:S(2)}) collective-permute-start(bf16[128,512]{1,0:T(8,128)(2,1)S(1)} %collective-permute-done.12.refs_15_), channel_id=1, source_target_pairs={{0,4},{2,6},{8,0},{10,2},{16,8},{18,10},{24,16},{26,18},{28,24},{3... | collective-permute-start | bytes 393224 | tf_op jit(solution)/shard_map/ppermute | solution.py:294
  18.8 9.5 %collective-permute-start.10 = (bf16[128,512]{1,0:T(8,128)(2,1)S(1)}, bf16[128,512]{1,0:T(8,128)(2,1)S(1)}, u32[]{:S(2)}, u32[]{:S(2)}) collective-permute-start(bf16[128,512]{1,0:T(8,128)(2,1)S(1)} %collective-permute-done.9.refs_10_), channel_id=1, source_target_pairs={{0,8},{2,10},{8,16},{10,18},{16,24},{18,26},{24,28},{26,30},{28,20... | collective-permute-start | bytes 393224 | tf_op jit(solution)/shard_map/ppermute | solution.py:294
  20.0 13.6 %collective-permute-start.4 = (bf16[128,512]{1,0:T(8,128)(2,1)S(1)}, bf16[128,512]{1,0:T(8,128)(2,1)S(1)}, u32[]{:S(2)}, u32[]{:S(2)}) collective-permute-start(bf16[128,512]{1,0:T(8,128)(2,1)S(1)} %collective-permute-done.refs_0_), channel_id=1, source_target_pairs={{0,1},{1,0},{2,3},{3,2},{4,5},{5,4},{6,7},{7,6},{8,9},{9,8},{10,11... | collective-permute-start | bytes 393224 | tf_op jit(solution)/shard_map/ppermute | solution.py:300
  25.6 8.0 %collective-permute-start.5 = (bf16[128,512]{1,0:T(8,128)(2,1)S(1)}, bf16[128,512]{1,0:T(8,128)(2,1)S(1)}, u32[]{:S(2)}, u32[]{:S(2)}) collective-permute-start(bf16[128,512]{1,0:T(8,128)(2,1)S(1)} %collective-permute-done.1.refs_1_), channel_id=1, source_target_pairs={{0,1},{1,0},{2,3},{3,2},{4,5},{5,4},{6,7},{7,6},{8,9},{9,8},{10,11... | collective-permute-start | bytes 393224 | tf_op jit(solution)/shard_map/ppermute | solution.py:300
  27.8 5.7 %collective-permute-start.6 = (bf16[128,512]{1,0:T(8,128)(2,1)S(1)}, bf16[128,512]{1,0:T(8,128)(2,1)S(1)}, u32[]{:S(2)}, u32[]{:S(2)}) collective-permute-start(bf16[128,512]{1,0:T(8,128)(2,1)S(1)} %collective-permute-done.2.refs_2_), channel_id=1, source_target_pairs={{0,1},{1,0},{2,3},{3,2},{4,5},{5,4},{6,7},{7,6},{8,9},{9,8},{10,11... | collective-permute-start | bytes 393224 | tf_op jit(solution)/shard_map/ppermute | solution.py:300
  27.9 5.7 %collective-permute-start.14 = (bf16[128,512]{1,0:T(8,128)(2,1)S(1)}, bf16[128,512]{1,0:T(8,128)(2,1)S(1)}, u32[]{:S(2)}, u32[]{:S(2)}) collective-permute-start(bf16[128,512]{1,0:T(8,128)(2,1)S(1)} %collective-permute-done.13.refs_14_), channel_id=1, source_target_pairs={{0,4},{2,6},{8,0},{10,2},{16,8},{18,10},{24,16},{26,18},{28,24},{3... | collective-permute-start | bytes 393224 | tf_op jit(solution)/shard_map/ppermute | solution.py:294
  28.3 5.4 %collective-permute-start.11 = (bf16[128,512]{1,0:T(8,128)(2,1)S(1)}, bf16[128,512]{1,0:T(8,128)(2,1)S(1)}, u32[]{:S(2)}, u32[]{:S(2)}) collective-permute-start(bf16[128,512]{1,0:T(8,128)(2,1)S(1)} %collective-permute-done.10.refs_11_), channel_id=1, source_target_pairs={{0,8},{2,10},{8,16},{10,18},{16,24},{18,26},{24,28},{26,30},{28,20... | collective-permute-start | bytes 393224 | tf_op jit(solution)/shard_map/ppermute | solution.py:294
  35.1 2.7 %collective-permute-start.15 = (f32[512,512]{1,0:T(8,128)S(1)}, f32[512,512]{1,0:T(8,128)S(1)}, u32[]{:S(2)}, u32[]{:S(2)}) collective-permute-start(f32[512,512]{1,0:T(8,128)S(1)} %shard_map.51.mine_ref), channel_id=1, source_target_pairs={{0,2},{2,0},{4,6},{6,4},{8,10},{10,8},{12,14},{14,12},{16,18},{18,... | collective-permute-start | bytes 3145736 | tf_op jit(solution)/shard_map/ppermute | solution.py:297
  42.1 2.0 %collective-permute-start.16 = (bf16[512,512]{1,0:T(8,128)(2,1)S(1)}, bf16[512,512]{1,0:T(8,128)(2,1)S(1)}, u32[]{:S(2)}, u32[]{:S(2)}) collective-permute-start(bf16[512,512]{1,0:T(8,128)(2,1)S(1)} %get-tuple-element.20.mine_ref), channel_id=1, source_target_pairs={{0,2},{2,0},{4,6},{6,4},{8,10},{10,8},{12,14},{14,12},{16,18},{18,... | collective-permute-start | bytes 1572872 | tf_op jit(solution)/shard_map/ppermute | solution.py:297
  45.5 35.4 %copy-start.1 = (bf16[256,512]{1,0:T(8,128)(2,1)}, bf16[256,512]{1,0:T(8,128)(2,1)S(1)}, u32[]{:S(2)}) copy-start(bf16[256,512]{1,0:T(8,128)(2,1)S(1)} %get-tuple-element.22.refs_0_) | copy-start | bytes 786436
  45.5 8.7 %collective-permute-start.17 = (bf16[256,512]{1,0:T(8,128)(2,1)S(1)}, bf16[256,512]{1,0:T(8,128)(2,1)S(1)}, u32[]{:S(2)}, u32[]{:S(2)}) collective-permute-start(bf16[256,512]{1,0:T(8,128)(2,1)S(1)} %get-tuple-element.23), channel_id=1, source_target_pairs={{0,1},{1,0},{2,3},{3,2},{4,5},{5,4},{6,7},{7,6},{8,9},{9,8},{10,11... | collective-permute-start | bytes 786440 | tf_op jit(solution)/shard_map/ppermute | solution.py:300
  47.5 8.2 %collective-permute-start.18 = (bf16[256,512]{1,0:T(8,128)(2,1)S(1)}, bf16[256,512]{1,0:T(8,128)(2,1)S(1)}, u32[]{:S(2)}, u32[]{:S(2)}) collective-permute-start(bf16[256,512]{1,0:T(8,128)(2,1)S(1)} %get-tuple-element.22.refs_0_), channel_id=1, source_target_pairs={{0,8},{2,6},{8,16},{10,2},{16,24},{18,10},{24,28},{26,18},{28,20},... | collective-permute-start | bytes 786440 | tf_op jit(solution)/shard_map/ppermute | solution.py:378
  54.2 26.7 %copy-start.5 = (bf16[256,512]{1,0:T(8,128)(2,1)}, bf16[256,512]{1,0:T(8,128)(2,1)S(1)}, u32[]{:S(2)}) copy-start(bf16[256,512]{1,0:T(8,128)(2,1)S(1)} %collective-permute-done.17.refs_1_) | copy-start | bytes 786436
  54.2 6.4 %collective-permute-start.20 = (bf16[256,512]{1,0:T(8,128)(2,1)S(1)}, bf16[256,512]{1,0:T(8,128)(2,1)S(1)}, u32[]{:S(2)}, u32[]{:S(2)}) collective-permute-start(bf16[256,512]{1,0:T(8,128)(2,1)S(1)} %collective-permute-done.17.refs_1_), channel_id=1, source_target_pairs={{0,8},{2,6},{8,16},{10,2},{16,24},{18,10},{24,28},{26,18},{28,20},... | collective-permute-start | bytes 786440 | tf_op jit(solution)/shard_map/ppermute | solution.py:378
  55.7 25.2 %copy-start.6 = (bf16[256,512]{1,0:T(8,128)(2,1)}, bf16[256,512]{1,0:T(8,128)(2,1)S(1)}, u32[]{:S(2)}) copy-start(bf16[256,512]{1,0:T(8,128)(2,1)S(1)} %collective-permute-done.18.refs_2_) | copy-start | bytes 786436
  55.7 7.6 %collective-permute-start.22 = (bf16[256,512]{1,0:T(8,128)(2,1)S(1)}, bf16[256,512]{1,0:T(8,128)(2,1)S(1)}, u32[]{:S(2)}, u32[]{:S(2)}) collective-permute-start(bf16[256,512]{1,0:T(8,128)(2,1)S(1)} %collective-permute-done.18.refs_2_), channel_id=1, source_target_pairs={{0,8},{2,6},{8,16},{10,2},{16,24},{18,10},{24,28},{26,18},{28,20},... | collective-permute-start | bytes 786440 | tf_op jit(solution)/shard_map/ppermute | solution.py:378
  60.6 20.4 %copy-start.7 = (bf16[256,512]{1,0:T(8,128)(2,1)}, bf16[256,512]{1,0:T(8,128)(2,1)S(1)}, u32[]{:S(2)}) copy-start(bf16[256,512]{1,0:T(8,128)(2,1)S(1)} %collective-permute-done.20.refs_4_) | copy-start | bytes 786436
  60.6 6.4 %collective-permute-start.24 = (bf16[256,512]{1,0:T(8,128)(2,1)S(1)}, bf16[256,512]{1,0:T(8,128)(2,1)S(1)}, u32[]{:S(2)}, u32[]{:S(2)}) collective-permute-start(bf16[256,512]{1,0:T(8,128)(2,1)S(1)} %collective-permute-done.20.refs_4_), channel_id=1, source_target_pairs={{0,8},{2,6},{8,16},{10,2},{16,24},{18,10},{24,28},{26,18},{28,20},... | collective-permute-start | bytes 786440 | tf_op jit(solution)/shard_map/ppermute | solution.py:378
  63.4 17.6 %copy-start.8 = (bf16[256,512]{1,0:T(8,128)(2,1)}, bf16[256,512]{1,0:T(8,128)(2,1)S(1)}, u32[]{:S(2)}) copy-start(bf16[256,512]{1,0:T(8,128)(2,1)S(1)} %collective-permute-done.22.refs_6_) | copy-start | bytes 786436
  63.4 6.4 %collective-permute-start.26 = (bf16[256,512]{1,0:T(8,128)(2,1)S(1)}, bf16[256,512]{1,0:T(8,128)(2,1)S(1)}, u32[]{:S(2)}, u32[]{:S(2)}) collective-permute-start(bf16[256,512]{1,0:T(8,128)(2,1)S(1)} %collective-permute-done.22.refs_6_), channel_id=1, source_target_pairs={{0,8},{2,6},{8,16},{10,2},{16,24},{18,10},{24,28},{26,18},{28,20},... | collective-permute-start | bytes 786440 | tf_op jit(solution)/shard_map/ppermute | solution.py:378
  66.9 14.0 %copy-start.9 = (bf16[256,512]{1,0:T(8,128)(2,1)}, bf16[256,512]{1,0:T(8,128)(2,1)S(1)}, u32[]{:S(2)}) copy-start(bf16[256,512]{1,0:T(8,128)(2,1)S(1)} %collective-permute-done.24.refs_8_) | copy-start | bytes 786436
  66.9 6.4 %collective-permute-start.28 = (bf16[256,512]{1,0:T(8,128)(2,1)S(1)}, bf16[256,512]{1,0:T(8,128)(2,1)S(1)}, u32[]{:S(2)}, u32[]{:S(2)}) collective-permute-start(bf16[256,512]{1,0:T(8,128)(2,1)S(1)} %collective-permute-done.24.refs_8_), channel_id=1, source_target_pairs={{0,8},{2,6},{8,16},{10,2},{16,24},{18,10},{24,28},{26,18},{28,20},... | collective-permute-start | bytes 786440 | tf_op jit(solution)/shard_map/ppermute | solution.py:378
  68.5 4.8 %collective-permute-start.19 = (bf16[256,512]{1,0:T(8,128)(2,1)S(1)}, bf16[256,512]{1,0:T(8,128)(2,1)S(1)}, u32[]{:S(2)}, u32[]{:S(2)}) collective-permute-start(bf16[256,512]{1,0:T(8,128)(2,1)S(1)} %collective-permute-done.18.refs_2_), channel_id=1, source_target_pairs={{0,2},{2,0},{4,6},{6,4},{8,10},{10,8},{12,14},{14,12},{16,18},{18,... | collective-permute-start | bytes 786440 | tf_op jit(solution)/shard_map/ppermute | solution.py:297
  68.5 5.4 %collective-permute-start.21 = (bf16[256,512]{1,0:T(8,128)(2,1)S(1)}, bf16[256,512]{1,0:T(8,128)(2,1)S(1)}, u32[]{:S(2)}, u32[]{:S(2)}) collective-permute-start(bf16[256,512]{1,0:T(8,128)(2,1)S(1)} %collective-permute-done.20.refs_4_), channel_id=1, source_target_pairs={{0,2},{2,0},{4,6},{6,4},{8,10},{10,8},{12,14},{14,12},{16,18},{18,... | collective-permute-start | bytes 786440 | tf_op jit(solution)/shard_map/ppermute | solution.py:297
  69.0 6.5 %collective-permute-start.23 = (bf16[256,512]{1,0:T(8,128)(2,1)S(1)}, bf16[256,512]{1,0:T(8,128)(2,1)S(1)}, u32[]{:S(2)}, u32[]{:S(2)}) collective-permute-start(bf16[256,512]{1,0:T(8,128)(2,1)S(1)} %collective-permute-done.22.refs_6_), channel_id=1, source_target_pairs={{0,2},{2,0},{4,6},{6,4},{8,10},{10,8},{12,14},{14,12},{16,18},{18,... | collective-permute-start | bytes 786440 | tf_op jit(solution)/shard_map/ppermute | solution.py:297
  69.7 11.2 %copy-start.3 = (bf16[256,512]{1,0:T(8,128)(2,1)}, bf16[256,512]{1,0:T(8,128)(2,1)S(1)}, u32[]{:S(2)}) copy-start(bf16[256,512]{1,0:T(8,128)(2,1)S(1)} %collective-permute-done.26.refs_10_) | copy-start | bytes 786436
  69.8 5.8 %collective-permute-start.30 = (bf16[128,512]{1,0:T(8,128)(2,1)S(1)}, bf16[128,512]{1,0:T(8,128)(2,1)S(1)}, u32[]{:S(2)}, u32[]{:S(2)}) collective-permute-start(bf16[128,512]{1,0:T(8,128)(2,1)S(1)} %dynamic-slice_bitcast_fusion.1), channel_id=1, source_target_pairs={{0,8},{2,6},{8,16},{10,2},{16,24},{18,10},{24,28},{26,18},{28,20},... | collective-permute-start | bytes 393224 | tf_op jit(solution)/shard_map/ppermute | solution.py:378
  73.3 7.7 %copy-start.4 = (bf16[256,512]{1,0:T(8,128)(2,1)}, bf16[256,512]{1,0:T(8,128)(2,1)S(1)}, u32[]{:S(2)}) copy-start(bf16[256,512]{1,0:T(8,128)(2,1)S(1)} %collective-permute-done.28.refs_12_) | copy-start | bytes 786436
  73.3 6.2 %collective-permute-start.25 = (bf16[256,512]{1,0:T(8,128)(2,1)S(1)}, bf16[256,512]{1,0:T(8,128)(2,1)S(1)}, u32[]{:S(2)}, u32[]{:S(2)}) collective-permute-start(bf16[256,512]{1,0:T(8,128)(2,1)S(1)} %collective-permute-done.24.refs_8_), channel_id=1, source_target_pairs={{0,2},{2,0},{4,6},{6,4},{8,10},{10,8},{12,14},{14,12},{16,18},{18,... | collective-permute-start | bytes 786440 | tf_op jit(solution)/shard_map/ppermute | solution.py:297
  73.3 7.6 %copy-start.10 = (bf16[256,512]{1,0:T(8,128)(2,1)}, bf16[256,512]{1,0:T(8,128)(2,1)S(1)}, u32[]{:S(2)}) copy-start(bf16[256,512]{1,0:T(8,128)(2,1)S(1)} %collective-permute-done.19.refs_3_) | copy-start | bytes 786436
  73.4 6.2 %collective-permute-start.27 = (bf16[256,512]{1,0:T(8,128)(2,1)S(1)}, bf16[256,512]{1,0:T(8,128)(2,1)S(1)}, u32[]{:S(2)}, u32[]{:S(2)}) collective-permute-start(bf16[256,512]{1,0:T(8,128)(2,1)S(1)} %collective-permute-done.26.refs_10_), channel_id=1, source_target_pairs={{0,2},{2,0},{4,6},{6,4},{8,10},{10,8},{12,14},{14,12},{16,18},{18,... | collective-permute-start | bytes 786440 | tf_op jit(solution)/shard_map/ppermute | solution.py:297
  73.9 7.1 %copy-start.11 = (bf16[256,512]{1,0:T(8,128)(2,1)}, bf16[256,512]{1,0:T(8,128)(2,1)S(1)}, u32[]{:S(2)}) copy-start(bf16[256,512]{1,0:T(8,128)(2,1)S(1)} %collective-permute-done.21.refs_5_) | copy-start | bytes 786436
  73.9 5.0 %collective-permute-start.32 = (bf16[128,512]{1,0:T(8,128)(2,1)S(1)}, bf16[128,512]{1,0:T(8,128)(2,1)S(1)}, u32[]{:S(2)}, u32[]{:S(2)}) collective-permute-start(bf16[128,512]{1,0:T(8,128)(2,1)S(1)} %dynamic-slice_bitcast_fusion), channel_id=1, source_target_pairs={{0,8},{2,6},{8,16},{10,2},{16,24},{18,10},{24,28},{26,18},{28,20},... | collective-permute-start | bytes 393224 | tf_op jit(solution)/shard_map/ppermute | solution.py:378
  75.5 5.5 %copy-start.12 = (bf16[256,512]{1,0:T(8,128)(2,1)}, bf16[256,512]{1,0:T(8,128)(2,1)S(1)}, u32[]{:S(2)}) copy-start(bf16[256,512]{1,0:T(8,128)(2,1)S(1)} %collective-permute-done.23.refs_7_) | copy-start | bytes 786436
  75.5 5.4 %collective-permute-start.29 = (bf16[256,512]{1,0:T(8,128)(2,1)S(1)}, bf16[256,512]{1,0:T(8,128)(2,1)}, u32[]{:S(2)}, u32[]{:S(2)}) collective-permute-start(bf16[256,512]{1,0:T(8,128)(2,1)S(1)} %collective-permute-done.28.refs_12_), channel_id=1, source_target_pairs={{0,2},{2,0},{4,6},{6,4},{8,10},{10,8},{12,14},{14,12},{16,18},{18,... | collective-permute-start | bytes 786440 | tf_op jit(solution)/shard_map/ppermute | solution.py:297
  75.6 5.4 %copy-start.15 = (bf16[128,512]{1,0:T(8,128)(2,1)}, bf16[128,512]{1,0:T(8,128)(2,1)S(1)}, u32[]{:S(2)}) copy-start(bf16[128,512]{1,0:T(8,128)(2,1)S(1)} %collective-permute-done.30.refs_14_) | copy-start | bytes 393220
  75.6 4.0 %collective-permute-start.31 = (bf16[128,512]{1,0:T(8,128)(2,1)S(1)}, bf16[128,512]{1,0:T(8,128)(2,1)S(1)}, u32[]{:S(2)}, u32[]{:S(2)}) collective-permute-start(bf16[128,512]{1,0:T(8,128)(2,1)S(1)} %collective-permute-done.30.refs_14_), channel_id=1, source_target_pairs={{0,2},{2,0},{4,6},{6,4},{8,10},{10,8},{12,14},{14,12},{16,18},{18,... | collective-permute-start | bytes 393224 | tf_op jit(solution)/shard_map/ppermute | solution.py:297
  78.9 1.3 %collective-permute-start.33 = (bf16[128,512]{1,0:T(8,128)(2,1)S(1)}, bf16[128,512]{1,0:T(8,128)(2,1)S(1)}, u32[]{:S(2)}, u32[]{:S(2)}) collective-permute-start(bf16[128,512]{1,0:T(8,128)(2,1)S(1)} %collective-permute-done.32.refs_16_), channel_id=1, source_target_pairs={{0,2},{2,0},{4,6},{6,4},{8,10},{10,8},{12,14},{14,12},{16,18},{18,... | collective-permute-start | bytes 393224 | tf_op jit(solution)/shard_map/ppermute | solution.py:297
  79.5 1.5 %copy-start.14 = (bf16[256,512]{1,0:T(8,128)(2,1)}, bf16[256,512]{1,0:T(8,128)(2,1)S(1)}, u32[]{:S(2)}) copy-start(bf16[256,512]{1,0:T(8,128)(2,1)S(1)} %collective-permute-done.27.refs_11_) | copy-start | bytes 786436
  (5 other events, 4.8 us)

commit v2 on v1

--- a/solution.py
+++ b/solution.py
@@ -164,7 +164,7 @@
     root_ref[...] = (root * scale).astype(jnp.bfloat16)
 
 
-OFFSETS = ((1, 4, 7, 2), (3, 5, 6, 2))
+OFFSETS = ((4, 7, 1, 2), (5, 6, 3, 2))
 
 
 def pack_kernel(place_ref, inputs_ref, *piece_refs):
@@ -206,14 +206,17 @@
 
 
 def update_kernel(side_ref, mine_ref, other_ref, tile_ref, near_ref, far_ref):
-    rows = near_ref.shape[0]
+    rows, far_rows = near_ref.shape[0], far_ref.shape[0]
     tile = tile_ref[...]
     core, plane = side_ref[0], side_ref[1]
 
     def write(left_ref, right_ref):
-        for out_ref, member in ((near_ref, plane), (far_ref, 1 - plane)):
-            first_row = pl.multiple_of(member * rows, rows)
-            left = left_ref[pl.ds(first_row, rows), :]
+        for out_ref, first_row in (
+            (near_ref, plane * rows),
+            (far_ref, (1 - plane) * rows + core * far_rows),
+        ):
+            count = out_ref.shape[0]
+            left = left_ref[pl.ds(pl.multiple_of(first_row, count), count), :]
             half = contract(left, tile, 1, 0).astype(jnp.bfloat16)
             piece = contract(half, right_ref[...], 1, 0) * math.sqrt(BLOCK)
             out_ref[...] = piece.astype(jnp.bfloat16)
@@ -299,14 +302,6 @@
     def swap_plane(array):
         return lax.ppermute(array, "pre", [(c, members - 1 - c) for c in range(members)])
 
-    def around(array):
-        pieces = [array] + [None] * (bands - 1)
-        for step in range(1, bands // 2 + 1):
-            pieces[step] = shift(pieces[step - 1], 1)
-            if step < bands // 2:
-                pieces[bands - step] = shift(pieces[(bands - step + 1) % bands], -1)
-        return pieces
-
     def deal(array, hop):
         pairs = [
             (
@@ -329,8 +324,15 @@
         jnp.stack([plane * (tokens // 2), band] + bands_out).astype(jnp.int32),
         inputs,
     )
-    cots = around(cotangent)
     near = [deal(piece, hop) for hop, piece in zip(hops, packed)]
+    cots = [cotangent] + [None] * (bands - 1)
+    for step in range(1, bands // 2 + 1):
+        behind, further = cots[step - 1], cots[(bands - step + 1) % bands]
+        if step == 3:
+            behind, further, near[0] = lax.optimization_barrier((behind, further, near[0]))
+        cots[step] = shift(behind, 1)
+        if step < bands // 2:
+            cots[bands - step] = shift(further, -1)
     far = [swap_plane(piece) for piece in near]
     outputs = jnp.dot(inputs, weight, preferred_element_type=jnp.float32).astype(jnp.bfloat16)
     own_band, outputs = lax.optimization_barrier((own_band, outputs))
@@ -361,7 +363,10 @@
     rows = BLOCK // members
     near_piece, far_piece = call(
         update_kernel,
-        [jax.ShapeDtypeStruct((rows, BLOCK), jnp.bfloat16)] * 2,
+        [
+            jax.ShapeDtypeStruct((rows, BLOCK), jnp.bfloat16),
+            jax.ShapeDtypeStruct((rows // cores, BLOCK), jnp.bfloat16),
+        ],
         [],
         side,
         root,
@@ -378,7 +383,14 @@
         return lax.ppermute(array, "dp", pairs)
 
     half_way = bands // 2
-    heads = [near_piece, swap_plane(far_piece)]
+    crossed = swap_plane(far_piece)
+    other_crossed = swap_core(crossed)
+    far_head = jnp.where(
+        core == 0,
+        jnp.concatenate([crossed, other_crossed]),
+        jnp.concatenate([other_crossed, crossed]),
+    )
+    heads = [near_piece, far_head]
     pieces = list(heads)
     for hop in range(1, half_way + 1):
         for chunk in range(2):
@@ -391,9 +403,10 @@
         place_kernel,
         out_shape=jax.ShapeDtypeStruct((bands, rows, CB * BLOCK), jnp.bfloat16),
         in_specs=[pl.BlockSpec(memory_space=pltpu.SMEM)]
-        + [pl.BlockSpec(memory_space=pltpu.VMEM)] * len(pieces),
+        + [pl.BlockSpec(memory_space=pl.ANY)] * len(pieces),
         out_specs=pl.BlockSpec(memory_space=pl.ANY),
         scratch_shapes=[pltpu.SemaphoreType.DMA((len(pieces),))],
+        compiler_params=pltpu.CompilerParams(vmem_limit_bytes=1024 * 1024),
     )(jnp.stack([core, plane, spot]).astype(jnp.int32), *pieces)
     return (outputs, update)
 

time: 85.6 us -> 84.7 us (0.989)
  waiting for transfers between devices: 28.6 us -> 35.5 us
  starting transfers between devices: 37.4 us -> 32.8 us
  Pallas kernels: 12 us -> 10.3 us
    ppermute x8, waiting for transfers between devices: 11.9 us -> 17.6 us  [turn(): return lax.ppermute(array, 'dp', pairs)]
    ppermute x8, starting transfers between devices: 12.4 us -> 8.35 us  [turn(): return lax.ppermute(array, 'dp', pairs)]
    ppermute x4, waiting for transfers between devices: 6.26 us -> 4.58 us  [deal(): return lax.ppermute(array, ('dp', 'pre'), pairs)]
    pallas_call x1, Pallas kernels: 4.31 us -> 2.7 us  [on_device_paired(): pl.pallas_call(place_kernel, out_shape=jax.ShapeDtypeStruct((bands, rows,...]
    ppermute x7, waiting for transfers between devices: 0.09 us -> 1.52 us  [shift(): return lax.ppermute(array, 'dp', pairs)]
    ppermute x10 -> x11, waiting for transfers between devices: 4.98 us -> 5.88 us  [swap_core(): return lax.ppermute(array, 'dp', [(g, g ^ 1) for g in range(groups)])]
    unnamed x38 -> x4, local copies, waits for them, and re-layouts: 1.96 us -> 1.23 us
    ppermute x10 -> x11, starting transfers between devices: 1.93 us -> 1.41 us  [swap_core(): return lax.ppermute(array, 'dp', [(g, g ^ 1) for g in range(groups)])]
  transfers between devices with their start and end apart: 34 -> 35, of which waited for: 13 -> 19; matrix products, arithmetic and copies ran while one was open for 5% -> 5% of each run, Pallas kernels for 1% -> 1%
where the time goes in v2:
time: 84.7 us; the launch traced here: 84.5 us
  waiting for transfers between devices  35.5 us (42%)
  starting transfers between devices  32.8 us (39%)
  Pallas kernels  10.3 us (12%)
  matrix products  3.56 us (4%)
  local copies, waits for them, and re-layouts  1.33 us (2%)
    ppermute x8, waiting for transfers between devices, turn(): return lax.ppermute(array, 'dp', pairs)  17.6 us
    ppermute x8, starting transfers between devices, turn(): return lax.ppermute(array, 'dp', pairs)  8.35 us
    ppermute x7, starting transfers between devices, shift(): return lax.ppermute(array, 'dp', pairs)  8.26 us
    ppermute x4, starting transfers between devices, deal(): return lax.ppermute(array, ('dp', 'pre'), pairs)  7.84 us
    pallas_call x4, Pallas kernels, call(): pl.pallas_call(kernel, out_shape=out_shapes, in_specs=in_specs, out_specs...  7.62 us
    ppermute x5, starting transfers between devices, swap_plane(): lax.ppermute(array, 'pre', [(c, members - 1 - c) for c in range(members)])  6.95 us
    ppermute x11, waiting for transfers between devices, swap_core(): return lax.ppermute(array, 'dp', [(g, g ^ 1) for g in range(groups)])  5.88 us
    ppermute x5, waiting for transfers between devices, swap_plane(): lax.ppermute(array, 'pre', [(c, members - 1 - c) for c in range(members)])  5.84 us
  transfers between devices with their start and end apart: 35, of which 19 were waited for; matrix products, arithmetic and copies ran while one was open for 5% of the time, Pallas kernels for 1%

profile of v2, /device:TPU:0, one launch (start us, length us, event | category | flops | bytes accessed | tf_op | source)
XLA Modules:
  0.0 84.5 jit_solution(8075776610296133678)
XLA Ops:
  0.6 3.1 %collective-permute-start = (bf16[128,512]{1,0:T(8,128)(2,1)}, bf16[128,512]{1,0:T(8,128)(2,1)S(1)}, u32[]{:S(2)}, u32[]{:S(2)}) collective-permute-start(bf16[128,512]{1,0:T(8,128)(2,1)} %refs_8_.1), channel_id=1, source_target_pairs={{0,8},{2,10},{8,16},{10,18},{16,24},{18,26},{24,28},{26,30},{28,20... | collective-permute-start | bytes 393224 | tf_op jit(solution)/shard_map/ppermute | solution.py:297
  3.8 1.2 %copy-done = bf16[128,4096]{1,0:T(8,128)(2,1)S(1)} copy-done((bf16[128,4096]{1,0:T(8,128)(2,1)S(1)}, bf16[128,4096]{1,0:T(8,128)(2,1)}, u32[]{:S(2)}) %copy-start) | copy-done | bytes 1048600
  5.0 0.6 shard_map.50
  5.6 3.1 %collective-permute-start.4 = (bf16[128,512]{1,0:T(8,128)(2,1)S(1)}, bf16[128,512]{1,0:T(8,128)(2,1)S(1)}, u32[]{:S(2)}, u32[]{:S(2)}) collective-permute-start(bf16[128,512]{1,0:T(8,128)(2,1)S(1)} %get-tuple-element.19), channel_id=1, source_target_pairs={{0,16},{1,21},{2,18},{3,23},{4,20},{5,17},{6,22},{7,19},{8,24},{9,... | collective-permute-start | bytes 393224 | tf_op jit(solution)/shard_map/ppermute | solution.py:315
  8.7 1.6 %collective-permute-start.1 = (bf16[128,512]{1,0:T(8,128)(2,1)S(1)}, bf16[128,512]{1,0:T(8,128)(2,1)S(1)}, u32[]{:S(2)}, u32[]{:S(2)}) collective-permute-start(bf16[128,512]{1,0:T(8,128)(2,1)S(1)} %collective-permute-done.refs_9_), channel_id=1, source_target_pairs={{0,8},{2,10},{8,16},{10,18},{16,24},{18,26},{24,28},{26,30},{28,20... | collective-permute-start | bytes 393224 | tf_op jit(solution)/shard_map/ppermute | solution.py:297
  10.3 0.5 collective-permute-start.3
  10.7 3.4 %collective-permute-start.5 = (bf16[128,512]{1,0:T(8,128)(2,1)S(1)}, bf16[128,512]{1,0:T(8,128)(2,1)S(1)}, u32[]{:S(2)}, u32[]{:S(2)}) collective-permute-start(bf16[128,512]{1,0:T(8,128)(2,1)S(1)} %get-tuple-element.21), channel_id=1, source_target_pairs={{0,28},{1,25},{2,30},{3,27},{4,24},{5,29},{6,26},{7,31},{8,20},{9,... | collective-permute-start | bytes 393224 | tf_op jit(solution)/shard_map/ppermute | solution.py:315
  14.2 1.3 %collective-permute-start.6 = (bf16[128,512]{1,0:T(8,128)(2,1)S(1)}, bf16[128,512]{1,0:T(8,128)(2,1)S(1)}, u32[]{:S(2)}, u32[]{:S(2)}) collective-permute-start(bf16[128,512]{1,0:T(8,128)(2,1)S(1)} %get-tuple-element.22), channel_id=1, source_target_pairs={{0,4},{1,13},{2,6},{3,15},{4,0},{5,9},{6,2},{7,11},{8,12},{9,5},{1... | collective-permute-start | bytes 393224 | tf_op jit(solution)/shard_map/ppermute | solution.py:315
  15.5 3.8 %collective-permute-done.4.refs_0_ = bf16[128,512]{1,0:T(8,128)(2,1)S(1)} collective-permute-done((bf16[128,512]{1,0:T(8,128)(2,1)S(1)}, bf16[128,512]{1,0:T(8,128)(2,1)S(1)}, u32[]{:S(2)}, u32[]{:S(2)}) %collective-permute-start.4) | collective-permute-done | bytes 131104 | tf_op jit(solution)/shard_map/ppermute | solution.py:315
  19.3 1.4 %collective-permute-done.3.refs_14_ = bf16[128,512]{1,0:T(8,128)(2,1)S(1)} collective-permute-done((bf16[128,512]{1,0:T(8,128)(2,1)S(1)}, bf16[128,512]{1,0:T(8,128)(2,1)S(1)}, u32[]{:S(2)}, u32[]{:S(2)}) %collective-permute-start.3) | collective-permute-done | bytes 131104 | tf_op jit(solution)/shard_map/ppermute | solution.py:297
  20.7 2.1 %collective-permute-start.12 = (bf16[128,512]{1,0:T(8,128)(2,1)S(1)}, bf16[128,512]{1,0:T(8,128)(2,1)S(1)}, u32[]{:S(2)}, u32[]{:S(2)}) collective-permute-start(bf16[128,512]{1,0:T(8,128)(2,1)S(1)} %collective-permute-done.1.refs_10_), channel_id=1, source_target_pairs={{0,8},{2,10},{8,16},{10,18},{16,24},{18,26},{24,28},{26,30},{28,20... | collective-permute-start | bytes 393224 | tf_op jit(solution)/shard_map/ppermute | solution.py:297
  22.8 0.7 collective-permute-done.7.refs_3_
  23.6 1.9 %collective-permute-start.11 = (bf16[64,512]{1,0:T(8,128)(2,1)S(1)}, bf16[64,512]{1,0:T(8,128)(2,1)S(1)}, u32[]{:S(2)}, u32[]{:S(2)}) collective-permute-start(bf16[64,512]{1,0:T(8,128)(2,1)S(1)} %collective-permute-done.7.refs_3_), channel_id=1, source_target_pairs={{0,1},{1,0},{2,3},{3,2},{4,5},{5,4},{6,7},{7,6},{8,9},{9,8},{10,11... | collective-permute-start | bytes 196616 | tf_op jit(solution)/shard_map/ppermute | solution.py:303
  25.6 1.9 %collective-permute-start.10 = (bf16[128,512]{1,0:T(8,128)(2,1)S(1)}, bf16[128,512]{1,0:T(8,128)(2,1)S(1)}, u32[]{:S(2)}, u32[]{:S(2)}) collective-permute-start(bf16[128,512]{1,0:T(8,128)(2,1)S(1)} %collective-permute-done.6.refs_2_), channel_id=1, source_target_pairs={{0,1},{1,0},{2,3},{3,2},{4,5},{5,4},{6,7},{7,6},{8,9},{9,8},{10,11... | collective-permute-start | bytes 393224 | tf_op jit(solution)/shard_map/ppermute | solution.py:303
  27.6 0.4 collective-permute-start.14
  28.0 0.6 collective-permute-done.11.refs_7_
  28.5 2.0 %collective-permute-start.8 = (bf16[128,512]{1,0:T(8,128)(2,1)S(1)}, bf16[128,512]{1,0:T(8,128)(2,1)S(1)}, u32[]{:S(2)}, u32[]{:S(2)}) collective-permute-start(bf16[128,512]{1,0:T(8,128)(2,1)S(1)} %collective-permute-done.4.refs_0_), channel_id=1, source_target_pairs={{0,1},{1,0},{2,3},{3,2},{4,5},{5,4},{6,7},{7,6},{8,9},{9,8},{10,11... | collective-permute-start | bytes 393224 | tf_op jit(solution)/shard_map/ppermute | solution.py:303
  30.6 0.6 collective-permute-start.13
  31.2 3.6 %convolution_convert_fusion = bf16[128,512]{1,0:T(8,128)(2,1)} fusion(bf16[128,4096]{1,0:T(8,128)(2,1)S(1)} %copy-done, bf16[4096,512]{1,0:T(8,128)(2,1)} %param.4), kind=kOutput, calls=%fused_computation | convolution fusion | flops 536936448 | bytes 5373952 | tf_op jit(solution)/shard_map/dot_general | solution.py:337
  34.9 0.6 collective-permute-done.8.refs_4_
  35.5 1.4 %shard_map.51.mine_ref = f32[512,512]{1,0:T(8,128)S(1)} custom-call(s32[3]{0:T(128)S(1)} %add_add_fusion.1.place_ref, bf16[128,512]{1,0:T(8,128)(2,1)S(1)} %get-tuple-element.18.own_ref, bf16[128,512]{1,0:T(8,128)(2,1)S(1)} %collective-permute-done.4.refs_0_, bf16[128,512]{1,0:T(8,128)(2,1)S(1)} %collective-permute-done.5.refs_1_, ...), custom_call_target="tpu_custom_call" | custom-call | tf_op jit(solution)/shard_map/pallas_call | solution.py:268
  37.1 2.6 %collective-permute-done.15.other_ref = f32[512,512]{1,0:T(8,128)S(1)} collective-permute-done((f32[512,512]{1,0:T(8,128)S(1)}, f32[512,512]{1,0:T(8,128)S(1)}, u32[]{:S(2)}, u32[]{:S(2)}) %collective-permute-start.15) | collective-permute-done | bytes 1048608 | tf_op jit(solution)/shard_map/ppermute | solution.py:300
  39.7 4.3 %shard_map.52 = (bf16[512,512]{1,0:T(8,128)(2,1)S(1)}, bf16[512,512]{1,0:T(8,128)(2,1)S(1)}) custom-call(s32[2]{0:T(128)S(1)} %pad_add_fusion.side_ref, f32[512,512]{1,0:T(8,128)S(1)} %shard_map.51.mine_ref, f32[512,512]{1,0:T(8,128)S(1)} %collective-permute-done.15.other_ref), custom_call_target="tpu_custom_call" | custom-call | tf_op jit(solution)/shard_map/pallas_call | solution.py:268
  44.2 1.7 %collective-permute-done.16.other_ref = bf16[512,512]{1,0:T(8,128)(2,1)S(1)} collective-permute-done((bf16[512,512]{1,0:T(8,128)(2,1)S(1)}, bf16[512,512]{1,0:T(8,128)(2,1)S(1)}, u32[]{:S(2)}, u32[]{:S(2)}) %collective-permute-start.16) | collective-permute-done | bytes 524320 | tf_op jit(solution)/shard_map/ppermute | solution.py:300
  46.0 1.3 %shard_map.53 = (bf16[256,512]{1,0:T(8,128)(2,1)S(1)}, bf16[128,512]{1,0:T(8,128)(2,1)S(1)}) custom-call(s32[2]{0:T(128)S(1)} %pad_add_fusion.side_ref, bf16[512,512]{1,0:T(8,128)(2,1)S(1)} %get-tuple-element.26.mine_ref, bf16[512,512]{1,0:T(8,128)(2,1)S(1)} %collective-permute-done.16.other_ref, bf16[512,512]{1,0:T(8,128)(2,1)S(1)} %get-tuple-element.27.tile_ref), custom_call_target="tpu_custom_call" | custom-call | tf_op jit(solution)/shard_map/pallas_call | solution.py:268
  47.3 0.9 %collective-permute-start.17 = (bf16[128,512]{1,0:T(8,128)(2,1)S(1)}, bf16[128,512]{1,0:T(8,128)(2,1)S(1)}, u32[]{:S(2)}, u32[]{:S(2)}) collective-permute-start(bf16[128,512]{1,0:T(8,128)(2,1)S(1)} %get-tuple-element.29), channel_id=1, source_target_pairs={{0,1},{1,0},{2,3},{3,2},{4,5},{5,4},{6,7},{7,6},{8,9},{9,8},{10,11... | collective-permute-start | bytes 393224 | tf_op jit(solution)/shard_map/ppermute | solution.py:303
  48.2 4.7 %collective-permute-done.17 = bf16[128,512]{1,0:T(8,128)(2,1)S(1)} collective-permute-done((bf16[128,512]{1,0:T(8,128)(2,1)S(1)}, bf16[128,512]{1,0:T(8,128)(2,1)S(1)}, u32[]{:S(2)}, u32[]{:S(2)}) %collective-permute-start.17) | collective-permute-done | bytes 131104 | tf_op jit(solution)/shard_map/ppermute | solution.py:303
  52.9 1.0 %collective-permute-start.19 = (bf16[256,512]{1,0:T(8,128)(2,1)S(1)}, bf16[256,512]{1,0:T(8,128)(2,1)S(1)}, u32[]{:S(2)}, u32[]{:S(2)}) collective-permute-start(bf16[256,512]{1,0:T(8,128)(2,1)S(1)} %get-tuple-element.28.refs_0_), channel_id=1, source_target_pairs={{0,8},{2,6},{8,16},{10,2},{16,24},{18,10},{24,28},{26,18},{28,20},... | collective-permute-start | bytes 786440 | tf_op jit(solution)/shard_map/ppermute | solution.py:383
  54.0 0.3 collective-permute-done.18
  54.4 1.1 %collective-permute-start.21 = (bf16[256,512]{1,0:T(8,128)(2,1)S(1)}, bf16[256,512]{1,0:T(8,128)(2,1)S(1)}, u32[]{:S(2)}, u32[]{:S(2)}) collective-permute-start(bf16[256,512]{1,0:T(8,128)(2,1)S(1)} %maximum_select_fusion.refs_1_), channel_id=1, source_target_pairs={{0,8},{2,6},{8,16},{10,2},{16,24},{18,10},{24,28},{26,18},{28,20},... | collective-permute-start | bytes 786440 | tf_op jit(solution)/shard_map/ppermute | solution.py:383
  55.4 3.9 %collective-permute-done.19.refs_2_ = bf16[256,512]{1,0:T(8,128)(2,1)S(1)} collective-permute-done((bf16[256,512]{1,0:T(8,128)(2,1)S(1)}, bf16[256,512]{1,0:T(8,128)(2,1)S(1)}, u32[]{:S(2)}, u32[]{:S(2)}) %collective-permute-start.19) | collective-permute-done | bytes 262176 | tf_op jit(solution)/shard_map/ppermute | solution.py:383
  59.3 1.0 %collective-permute-start.23 = (bf16[256,512]{1,0:T(8,128)(2,1)S(1)}, bf16[256,512]{1,0:T(8,128)(2,1)S(1)}, u32[]{:S(2)}, u32[]{:S(2)}) collective-permute-start(bf16[256,512]{1,0:T(8,128)(2,1)S(1)} %collective-permute-done.19.refs_2_), channel_id=1, source_target_pairs={{0,8},{2,6},{8,16},{10,2},{16,24},{18,10},{24,28},{26,18},{28,20},... | collective-permute-start | bytes 786440 | tf_op jit(solution)/shard_map/ppermute | solution.py:383
  60.4 1.8 %collective-permute-done.21.refs_4_ = bf16[256,512]{1,0:T(8,128)(2,1)S(1)} collective-permute-done((bf16[256,512]{1,0:T(8,128)(2,1)S(1)}, bf16[256,512]{1,0:T(8,128)(2,1)S(1)}, u32[]{:S(2)}, u32[]{:S(2)}) %collective-permute-start.21) | collective-permute-done | bytes 262176 | tf_op jit(solution)/shard_map/ppermute | solution.py:383
  62.1 1.0 %collective-permute-start.25 = (bf16[256,512]{1,0:T(8,128)(2,1)S(1)}, bf16[256,512]{1,0:T(8,128)(2,1)S(1)}, u32[]{:S(2)}, u32[]{:S(2)}) collective-permute-start(bf16[256,512]{1,0:T(8,128)(2,1)S(1)} %collective-permute-done.21.refs_4_), channel_id=1, source_target_pairs={{0,8},{2,6},{8,16},{10,2},{16,24},{18,10},{24,28},{26,18},{28,20},... | collective-permute-start | bytes 786440 | tf_op jit(solution)/shard_map/ppermute | solution.py:383
  63.2 2.5 %collective-permute-done.23.refs_6_ = bf16[256,512]{1,0:T(8,128)(2,1)S(1)} collective-permute-done((bf16[256,512]{1,0:T(8,128)(2,1)S(1)}, bf16[256,512]{1,0:T(8,128)(2,1)S(1)}, u32[]{:S(2)}, u32[]{:S(2)}) %collective-permute-start.23) | collective-permute-done | bytes 262176 | tf_op jit(solution)/shard_map/ppermute | solution.py:383
  65.7 1.0 %collective-permute-start.27 = (bf16[256,512]{1,0:T(8,128)(2,1)S(1)}, bf16[256,512]{1,0:T(8,128)(2,1)S(1)}, u32[]{:S(2)}, u32[]{:S(2)}) collective-permute-start(bf16[256,512]{1,0:T(8,128)(2,1)S(1)} %collective-permute-done.23.refs_6_), channel_id=1, source_target_pairs={{0,8},{2,6},{8,16},{10,2},{16,24},{18,10},{24,28},{26,18},{28,20},... | collective-permute-start | bytes 786440 | tf_op jit(solution)/shard_map/ppermute | solution.py:383
  66.7 1.8 %collective-permute-done.25.refs_8_ = bf16[256,512]{1,0:T(8,128)(2,1)S(1)} collective-permute-done((bf16[256,512]{1,0:T(8,128)(2,1)S(1)}, bf16[256,512]{1,0:T(8,128)(2,1)S(1)}, u32[]{:S(2)}, u32[]{:S(2)}) %collective-permute-start.25) | collective-permute-done | bytes 262176 | tf_op jit(solution)/shard_map/ppermute | solution.py:383
  68.5 1.0 %collective-permute-start.29 = (bf16[256,512]{1,0:T(8,128)(2,1)S(1)}, bf16[256,512]{1,0:T(8,128)(2,1)S(1)}, u32[]{:S(2)}, u32[]{:S(2)}) collective-permute-start(bf16[256,512]{1,0:T(8,128)(2,1)S(1)} %collective-permute-done.25.refs_8_), channel_id=1, source_target_pairs={{0,8},{2,6},{8,16},{10,2},{16,24},{18,10},{24,28},{26,18},{28,20},... | collective-permute-start | bytes 786440 | tf_op jit(solution)/shard_map/ppermute | solution.py:383
  69.5 0.5 collective-permute-start.24
  70.0 2.0 %collective-permute-done.27.refs_10_ = bf16[256,512]{1,0:T(8,128)(2,1)S(1)} collective-permute-done((bf16[256,512]{1,0:T(8,128)(2,1)S(1)}, bf16[256,512]{1,0:T(8,128)(2,1)S(1)}, u32[]{:S(2)}, u32[]{:S(2)}) %collective-permute-start.27) | collective-permute-done | bytes 262176 | tf_op jit(solution)/shard_map/ppermute | solution.py:383
  72.1 1.1 %collective-permute-start.31 = (bf16[128,512]{1,0:T(8,128)(2,1)S(1)}, bf16[128,512]{1,0:T(8,128)(2,1)S(1)}, u32[]{:S(2)}, u32[]{:S(2)}) collective-permute-start(bf16[128,512]{1,0:T(8,128)(2,1)S(1)} %dynamic-slice_bitcast_fusion.1), channel_id=1, source_target_pairs={{0,8},{2,6},{8,16},{10,2},{16,24},{18,10},{24,28},{26,18},{28,20},... | collective-permute-start | bytes 393224 | tf_op jit(solution)/shard_map/ppermute | solution.py:383
  73.2 1.7 %collective-permute-done.29.refs_12_ = bf16[256,512]{1,0:T(8,128)(2,1)S(1)} collective-permute-done((bf16[256,512]{1,0:T(8,128)(2,1)S(1)}, bf16[256,512]{1,0:T(8,128)(2,1)S(1)}, u32[]{:S(2)}, u32[]{:S(2)}) %collective-permute-start.29) | collective-permute-done | bytes 262176 | tf_op jit(solution)/shard_map/ppermute | solution.py:383
  74.9 0.6 collective-permute-start.26
  75.5 1.0 %collective-permute-start.33 = (bf16[128,512]{1,0:T(8,128)(2,1)S(1)}, bf16[128,512]{1,0:T(8,128)(2,1)S(1)}, u32[]{:S(2)}, u32[]{:S(2)}) collective-permute-start(bf16[128,512]{1,0:T(8,128)(2,1)S(1)} %dynamic-slice_bitcast_fusion), channel_id=1, source_target_pairs={{0,8},{2,6},{8,16},{10,2},{16,24},{18,10},{24,28},{26,18},{28,20},... | collective-permute-start | bytes 393224 | tf_op jit(solution)/shard_map/ppermute | solution.py:383
  76.5 0.6 collective-permute-done.31.refs_14_
  77.1 3.3 %collective-permute-done.33.refs_16_ = bf16[128,512]{1,0:T(8,128)(2,1)S(1)} collective-permute-done((bf16[128,512]{1,0:T(8,128)(2,1)S(1)}, bf16[128,512]{1,0:T(8,128)(2,1)S(1)}, u32[]{:S(2)}, u32[]{:S(2)}) %collective-permute-start.33) | collective-permute-done | bytes 131104 | tf_op jit(solution)/shard_map/ppermute | solution.py:383
  80.5 1.3 %collective-permute-done.34.refs_17_ = bf16[128,512]{1,0:T(8,128)(2,1)S(1)} collective-permute-done((bf16[128,512]{1,0:T(8,128)(2,1)S(1)}, bf16[128,512]{1,0:T(8,128)(2,1)S(1)}, u32[]{:S(2)}, u32[]{:S(2)}) %collective-permute-start.34) | collective-permute-done | bytes 131104 | tf_op jit(solution)/shard_map/ppermute | solution.py:300
  81.8 2.7 %shard_map.54 = bf16[8,256,1024]{2,1,0:T(8,128)(2,1)} custom-call(s32[3]{0:T(128)S(1)} %add_add_fusion.place_ref, bf16[256,512]{1,0:T(8,128)(2,1)S(1)} %get-tuple-element.28.refs_0_, bf16[256,512]{1,0:T(8,128)(2,1)S(1)} %maximum_select_fusion.refs_1_, bf16[256,512]{1,0:T(8,128)(2,1)S(1)} %collective-permute-done.19.refs_2_, ...), custom_call_target="tpu_custom_call" | custom-call | tf_op jit(solution)/shard_map/pallas_call | solution.py:402
  (39 shorter events, 0.9 us)
Async XLA Ops:
  0.6 8.1 %collective-permute-start = (bf16[128,512]{1,0:T(8,128)(2,1)}, bf16[128,512]{1,0:T(8,128)(2,1)S(1)}, u32[]{:S(2)}, u32[]{:S(2)}) collective-permute-start(bf16[128,512]{1,0:T(8,128)(2,1)} %refs_8_.1), channel_id=1, source_target_pairs={{0,8},{2,10},{8,16},{10,18},{16,24},{18,26},{24,28},{26,30},{28,20... | collective-permute-start | bytes 393224 | tf_op jit(solution)/shard_map/ppermute | solution.py:297
  3.7 6.6 %collective-permute-start.2 = (bf16[128,512]{1,0:T(8,128)(2,1)}, bf16[128,512]{1,0:T(8,128)(2,1)S(1)}, u32[]{:S(2)}, u32[]{:S(2)}) collective-permute-start(bf16[128,512]{1,0:T(8,128)(2,1)} %refs_8_.1), channel_id=1, source_target_pairs={{0,4},{2,6},{8,0},{10,2},{16,8},{18,10},{24,16},{26,18},{28,24},{3... | collective-permute-start | bytes 393224 | tf_op jit(solution)/shard_map/ppermute | solution.py:297
  3.8 1.2 %copy-start = (bf16[128,4096]{1,0:T(8,128)(2,1)S(1)}, bf16[128,4096]{1,0:T(8,128)(2,1)}, u32[]{:S(2)}) copy-start(bf16[128,4096]{1,0:T(8,128)(2,1)} %inputs_ref.1) | copy-start | bytes 3145732
  5.0 30.5 %copy-start.1 = (bf16[128,512]{1,0:T(8,128)(2,1)S(1)}, bf16[128,512]{1,0:T(8,128)(2,1)}, u32[]{:S(2)}) copy-start(bf16[128,512]{1,0:T(8,128)(2,1)} %refs_8_.1) | copy-start | bytes 393220
  5.6 13.7 %collective-permute-start.4 = (bf16[128,512]{1,0:T(8,128)(2,1)S(1)}, bf16[128,512]{1,0:T(8,128)(2,1)S(1)}, u32[]{:S(2)}, u32[]{:S(2)}) collective-permute-start(bf16[128,512]{1,0:T(8,128)(2,1)S(1)} %get-tuple-element.19), channel_id=1, source_target_pairs={{0,16},{1,21},{2,18},{3,23},{4,20},{5,17},{6,22},{7,19},{8,24},{9,... | collective-permute-start | bytes 393224 | tf_op jit(solution)/shard_map/ppermute | solution.py:315
  8.7 10.6 %collective-permute-start.1 = (bf16[128,512]{1,0:T(8,128)(2,1)S(1)}, bf16[128,512]{1,0:T(8,128)(2,1)S(1)}, u32[]{:S(2)}, u32[]{:S(2)}) collective-permute-start(bf16[128,512]{1,0:T(8,128)(2,1)S(1)} %collective-permute-done.refs_9_), channel_id=1, source_target_pairs={{0,8},{2,10},{8,16},{10,18},{16,24},{18,26},{24,28},{26,30},{28,20... | collective-permute-start | bytes 393224 | tf_op jit(solution)/shard_map/ppermute | solution.py:297
  10.3 10.4 %collective-permute-start.3 = (bf16[128,512]{1,0:T(8,128)(2,1)S(1)}, bf16[128,512]{1,0:T(8,128)(2,1)S(1)}, u32[]{:S(2)}, u32[]{:S(2)}) collective-permute-start(bf16[128,512]{1,0:T(8,128)(2,1)S(1)} %collective-permute-done.2.refs_15_), channel_id=1, source_target_pairs={{0,4},{2,6},{8,0},{10,2},{16,8},{18,10},{24,16},{26,18},{28,24},{3... | collective-permute-start | bytes 393224 | tf_op jit(solution)/shard_map/ppermute | solution.py:297
  10.7 14.8 %collective-permute-start.5 = (bf16[128,512]{1,0:T(8,128)(2,1)S(1)}, bf16[128,512]{1,0:T(8,128)(2,1)S(1)}, u32[]{:S(2)}, u32[]{:S(2)}) collective-permute-start(bf16[128,512]{1,0:T(8,128)(2,1)S(1)} %get-tuple-element.21), channel_id=1, source_target_pairs={{0,28},{1,25},{2,30},{3,27},{4,24},{5,29},{6,26},{7,31},{8,20},{9,... | collective-permute-start | bytes 393224 | tf_op jit(solution)/shard_map/ppermute | solution.py:315
  14.2 11.5 %collective-permute-start.6 = (bf16[128,512]{1,0:T(8,128)(2,1)S(1)}, bf16[128,512]{1,0:T(8,128)(2,1)S(1)}, u32[]{:S(2)}, u32[]{:S(2)}) collective-permute-start(bf16[128,512]{1,0:T(8,128)(2,1)S(1)} %get-tuple-element.22), channel_id=1, source_target_pairs={{0,4},{1,13},{2,6},{3,15},{4,0},{5,9},{6,2},{7,11},{8,12},{9,5},{1... | collective-permute-start | bytes 393224 | tf_op jit(solution)/shard_map/ppermute | solution.py:315
  19.3 4.3 %collective-permute-start.7 = (bf16[64,512]{1,0:T(8,128)(2,1)S(1)}, bf16[64,512]{1,0:T(8,128)(2,1)S(1)}, u32[]{:S(2)}, u32[]{:S(2)}) collective-permute-start(bf16[64,512]{1,0:T(8,128)(2,1)S(1)} %get-tuple-element.23), channel_id=1, source_target_pairs={{0,8},{1,9},{2,10},{3,11},{4,12},{5,13},{6,14},{7,15},{8,0},{9,1},... | collective-permute-start | bytes 196616 | tf_op jit(solution)/shard_map/ppermute | solution.py:315
  20.7 9.8 %collective-permute-start.12 = (bf16[128,512]{1,0:T(8,128)(2,1)S(1)}, bf16[128,512]{1,0:T(8,128)(2,1)S(1)}, u32[]{:S(2)}, u32[]{:S(2)}) collective-permute-start(bf16[128,512]{1,0:T(8,128)(2,1)S(1)} %collective-permute-done.1.refs_10_), channel_id=1, source_target_pairs={{0,8},{2,10},{8,16},{10,18},{16,24},{18,26},{24,28},{26,30},{28,20... | collective-permute-start | bytes 393224 | tf_op jit(solution)/shard_map/ppermute | solution.py:297
  23.6 4.9 %collective-permute-start.11 = (bf16[64,512]{1,0:T(8,128)(2,1)S(1)}, bf16[64,512]{1,0:T(8,128)(2,1)S(1)}, u32[]{:S(2)}, u32[]{:S(2)}) collective-permute-start(bf16[64,512]{1,0:T(8,128)(2,1)S(1)} %collective-permute-done.7.refs_3_), channel_id=1, source_target_pairs={{0,1},{1,0},{2,3},{3,2},{4,5},{5,4},{6,7},{7,6},{8,9},{9,8},{10,11... | collective-permute-start | bytes 196616 | tf_op jit(solution)/shard_map/ppermute | solution.py:303
  25.5 9.3 %collective-permute-start.9 = (bf16[128,512]{1,0:T(8,128)(2,1)S(1)}, bf16[128,512]{1,0:T(8,128)(2,1)S(1)}, u32[]{:S(2)}, u32[]{:S(2)}) collective-permute-start(bf16[128,512]{1,0:T(8,128)(2,1)S(1)} %collective-permute-done.5.refs_1_), channel_id=1, source_target_pairs={{0,1},{1,0},{2,3},{3,2},{4,5},{5,4},{6,7},{7,6},{8,9},{9,8},{10,11... | collective-permute-start | bytes 393224 | tf_op jit(solution)/shard_map/ppermute | solution.py:303
  25.6 9.2 %collective-permute-start.10 = (bf16[128,512]{1,0:T(8,128)(2,1)S(1)}, bf16[128,512]{1,0:T(8,128)(2,1)S(1)}, u32[]{:S(2)}, u32[]{:S(2)}) collective-permute-start(bf16[128,512]{1,0:T(8,128)(2,1)S(1)} %collective-permute-done.6.refs_2_), channel_id=1, source_target_pairs={{0,1},{1,0},{2,3},{3,2},{4,5},{5,4},{6,7},{7,6},{8,9},{9,8},{10,11... | collective-permute-start | bytes 393224 | tf_op jit(solution)/shard_map/ppermute | solution.py:303
  27.6 7.3 %collective-permute-start.14 = (bf16[128,512]{1,0:T(8,128)(2,1)S(1)}, bf16[128,512]{1,0:T(8,128)(2,1)S(1)}, u32[]{:S(2)}, u32[]{:S(2)}) collective-permute-start(bf16[128,512]{1,0:T(8,128)(2,1)S(1)} %collective-permute-done.3.refs_14_), channel_id=1, source_target_pairs={{0,4},{2,6},{8,0},{10,2},{16,8},{18,10},{24,16},{26,18},{28,24},{3... | collective-permute-start | bytes 393224 | tf_op jit(solution)/shard_map/ppermute | solution.py:297
  28.5 6.9 %collective-permute-start.8 = (bf16[128,512]{1,0:T(8,128)(2,1)S(1)}, bf16[128,512]{1,0:T(8,128)(2,1)S(1)}, u32[]{:S(2)}, u32[]{:S(2)}) collective-permute-start(bf16[128,512]{1,0:T(8,128)(2,1)S(1)} %collective-permute-done.4.refs_0_), channel_id=1, source_target_pairs={{0,1},{1,0},{2,3},{3,2},{4,5},{5,4},{6,7},{7,6},{8,9},{9,8},{10,11... | collective-permute-start | bytes 393224 | tf_op jit(solution)/shard_map/ppermute | solution.py:303
  30.6 5.0 %collective-permute-start.13 = (bf16[128,512]{1,0:T(8,128)(2,1)S(1)}, bf16[128,512]{1,0:T(8,128)(2,1)S(1)}, u32[]{:S(2)}, u32[]{:S(2)}) collective-permute-start(bf16[128,512]{1,0:T(8,128)(2,1)S(1)} %collective-permute-done.12.refs_11_), channel_id=1, source_target_pairs={{0,8},{2,10},{8,16},{10,18},{16,24},{18,26},{24,28},{26,30},{28,20... | collective-permute-start | bytes 393224 | tf_op jit(solution)/shard_map/ppermute | solution.py:297
  37.0 2.7 %collective-permute-start.15 = (f32[512,512]{1,0:T(8,128)S(1)}, f32[512,512]{1,0:T(8,128)S(1)}, u32[]{:S(2)}, u32[]{:S(2)}) collective-permute-start(f32[512,512]{1,0:T(8,128)S(1)} %shard_map.51.mine_ref), channel_id=1, source_target_pairs={{0,2},{2,0},{4,6},{6,4},{8,10},{10,8},{12,14},{14,12},{16,18},{18,... | collective-permute-start | bytes 3145736 | tf_op jit(solution)/shard_map/ppermute | solution.py:300
  44.0 2.0 %collective-permute-start.16 = (bf16[512,512]{1,0:T(8,128)(2,1)S(1)}, bf16[512,512]{1,0:T(8,128)(2,1)S(1)}, u32[]{:S(2)}, u32[]{:S(2)}) collective-permute-start(bf16[512,512]{1,0:T(8,128)(2,1)S(1)} %get-tuple-element.26.mine_ref), channel_id=1, source_target_pairs={{0,2},{2,0},{4,6},{6,4},{8,10},{10,8},{12,14},{14,12},{16,18},{18,... | collective-permute-start | bytes 1572872 | tf_op jit(solution)/shard_map/ppermute | solution.py:300
  47.3 5.6 %collective-permute-start.17 = (bf16[128,512]{1,0:T(8,128)(2,1)S(1)}, bf16[128,512]{1,0:T(8,128)(2,1)S(1)}, u32[]{:S(2)}, u32[]{:S(2)}) collective-permute-start(bf16[128,512]{1,0:T(8,128)(2,1)S(1)} %get-tuple-element.29), channel_id=1, source_target_pairs={{0,1},{1,0},{2,3},{3,2},{4,5},{5,4},{6,7},{7,6},{8,9},{9,8},{10,11... | collective-permute-start | bytes 393224 | tf_op jit(solution)/shard_map/ppermute | solution.py:303
  52.9 1.3 %collective-permute-start.18 = (bf16[128,512]{1,0:T(8,128)(2,1)S(1)}, bf16[128,512]{1,0:T(8,128)(2,1)S(1)}, u32[]{:S(2)}, u32[]{:S(2)}) collective-permute-start(bf16[128,512]{1,0:T(8,128)(2,1)S(1)} %collective-permute-done.17), channel_id=1, source_target_pairs={{0,2},{2,0},{4,6},{6,4},{8,10},{10,8},{12,14},{14,12},{16,18},{18,... | collective-permute-start | bytes 393224 | tf_op jit(solution)/shard_map/ppermute | solution.py:300
  52.9 6.4 %collective-permute-start.19 = (bf16[256,512]{1,0:T(8,128)(2,1)S(1)}, bf16[256,512]{1,0:T(8,128)(2,1)S(1)}, u32[]{:S(2)}, u32[]{:S(2)}) collective-permute-start(bf16[256,512]{1,0:T(8,128)(2,1)S(1)} %get-tuple-element.28.refs_0_), channel_id=1, source_target_pairs={{0,8},{2,6},{8,16},{10,2},{16,24},{18,10},{24,28},{26,18},{28,20},... | collective-permute-start | bytes 786440 | tf_op jit(solution)/shard_map/ppermute | solution.py:383
  54.4 7.8 %collective-permute-start.21 = (bf16[256,512]{1,0:T(8,128)(2,1)S(1)}, bf16[256,512]{1,0:T(8,128)(2,1)S(1)}, u32[]{:S(2)}, u32[]{:S(2)}) collective-permute-start(bf16[256,512]{1,0:T(8,128)(2,1)S(1)} %maximum_select_fusion.refs_1_), channel_id=1, source_target_pairs={{0,8},{2,6},{8,16},{10,2},{16,24},{18,10},{24,28},{26,18},{28,20},... | collective-permute-start | bytes 786440 | tf_op jit(solution)/shard_map/ppermute | solution.py:383
  59.3 6.4 %collective-permute-start.23 = (bf16[256,512]{1,0:T(8,128)(2,1)S(1)}, bf16[256,512]{1,0:T(8,128)(2,1)S(1)}, u32[]{:S(2)}, u32[]{:S(2)}) collective-permute-start(bf16[256,512]{1,0:T(8,128)(2,1)S(1)} %collective-permute-done.19.refs_2_), channel_id=1, source_target_pairs={{0,8},{2,6},{8,16},{10,2},{16,24},{18,10},{24,28},{26,18},{28,20},... | collective-permute-start | bytes 786440 | tf_op jit(solution)/shard_map/ppermute | solution.py:383
  62.1 6.4 %collective-permute-start.25 = (bf16[256,512]{1,0:T(8,128)(2,1)S(1)}, bf16[256,512]{1,0:T(8,128)(2,1)S(1)}, u32[]{:S(2)}, u32[]{:S(2)}) collective-permute-start(bf16[256,512]{1,0:T(8,128)(2,1)S(1)} %collective-permute-done.21.refs_4_), channel_id=1, source_target_pairs={{0,8},{2,6},{8,16},{10,2},{16,24},{18,10},{24,28},{26,18},{28,20},... | collective-permute-start | bytes 786440 | tf_op jit(solution)/shard_map/ppermute | solution.py:383
  65.7 6.4 %collective-permute-start.27 = (bf16[256,512]{1,0:T(8,128)(2,1)S(1)}, bf16[256,512]{1,0:T(8,128)(2,1)S(1)}, u32[]{:S(2)}, u32[]{:S(2)}) collective-permute-start(bf16[256,512]{1,0:T(8,128)(2,1)S(1)} %collective-permute-done.23.refs_6_), channel_id=1, source_target_pairs={{0,8},{2,6},{8,16},{10,2},{16,24},{18,10},{24,28},{26,18},{28,20},... | collective-permute-start | bytes 786440 | tf_op jit(solution)/shard_map/ppermute | solution.py:383
  68.5 6.4 %collective-permute-start.29 = (bf16[256,512]{1,0:T(8,128)(2,1)S(1)}, bf16[256,512]{1,0:T(8,128)(2,1)S(1)}, u32[]{:S(2)}, u32[]{:S(2)}) collective-permute-start(bf16[256,512]{1,0:T(8,128)(2,1)S(1)} %collective-permute-done.25.refs_8_), channel_id=1, source_target_pairs={{0,8},{2,6},{8,16},{10,2},{16,24},{18,10},{24,28},{26,18},{28,20},... | collective-permute-start | bytes 786440 | tf_op jit(solution)/shard_map/ppermute | solution.py:383
  69.5 5.4 %collective-permute-start.20 = (bf16[256,512]{1,0:T(8,128)(2,1)S(1)}, bf16[256,512]{1,0:T(8,128)(2,1)S(1)}, u32[]{:S(2)}, u32[]{:S(2)}) collective-permute-start(bf16[256,512]{1,0:T(8,128)(2,1)S(1)} %collective-permute-done.19.refs_2_), channel_id=1, source_target_pairs={{0,2},{2,0},{4,6},{6,4},{8,10},{10,8},{12,14},{14,12},{16,18},{18,... | collective-permute-start | bytes 786440 | tf_op jit(solution)/shard_map/ppermute | solution.py:300
  69.5 5.9 %collective-permute-start.24 = (bf16[256,512]{1,0:T(8,128)(2,1)S(1)}, bf16[256,512]{1,0:T(8,128)(2,1)S(1)}, u32[]{:S(2)}, u32[]{:S(2)}) collective-permute-start(bf16[256,512]{1,0:T(8,128)(2,1)S(1)} %collective-permute-done.23.refs_6_), channel_id=1, source_target_pairs={{0,2},{2,0},{4,6},{6,4},{8,10},{10,8},{12,14},{14,12},{16,18},{18,... | collective-permute-start | bytes 786440 | tf_op jit(solution)/shard_map/ppermute | solution.py:300
  70.0 6.5 %collective-permute-start.22 = (bf16[256,512]{1,0:T(8,128)(2,1)S(1)}, bf16[256,512]{1,0:T(8,128)(2,1)S(1)}, u32[]{:S(2)}, u32[]{:S(2)}) collective-permute-start(bf16[256,512]{1,0:T(8,128)(2,1)S(1)} %collective-permute-done.21.refs_4_), channel_id=1, source_target_pairs={{0,2},{2,0},{4,6},{6,4},{8,10},{10,8},{12,14},{14,12},{16,18},{18,... | collective-permute-start | bytes 786440 | tf_op jit(solution)/shard_map/ppermute | solution.py:300
  72.1 5.0 %collective-permute-start.31 = (bf16[128,512]{1,0:T(8,128)(2,1)S(1)}, bf16[128,512]{1,0:T(8,128)(2,1)S(1)}, u32[]{:S(2)}, u32[]{:S(2)}) collective-permute-start(bf16[128,512]{1,0:T(8,128)(2,1)S(1)} %dynamic-slice_bitcast_fusion.1), channel_id=1, source_target_pairs={{0,8},{2,6},{8,16},{10,2},{16,24},{18,10},{24,28},{26,18},{28,20},... | collective-permute-start | bytes 393224 | tf_op jit(solution)/shard_map/ppermute | solution.py:383
  74.9 5.7 %collective-permute-start.28 = (bf16[256,512]{1,0:T(8,128)(2,1)S(1)}, bf16[256,512]{1,0:T(8,128)(2,1)S(1)}, u32[]{:S(2)}, u32[]{:S(2)}) collective-permute-start(bf16[256,512]{1,0:T(8,128)(2,1)S(1)} %collective-permute-done.27.refs_10_), channel_id=1, source_target_pairs={{0,2},{2,0},{4,6},{6,4},{8,10},{10,8},{12,14},{14,12},{16,18},{18,... | collective-permute-start | bytes 786440 | tf_op jit(solution)/shard_map/ppermute | solution.py:300
  74.9 5.6 %collective-permute-start.26 = (bf16[256,512]{1,0:T(8,128)(2,1)S(1)}, bf16[256,512]{1,0:T(8,128)(2,1)S(1)}, u32[]{:S(2)}, u32[]{:S(2)}) collective-permute-start(bf16[256,512]{1,0:T(8,128)(2,1)S(1)} %collective-permute-done.25.refs_8_), channel_id=1, source_target_pairs={{0,2},{2,0},{4,6},{6,4},{8,10},{10,8},{12,14},{14,12},{16,18},{18,... | collective-permute-start | bytes 786440 | tf_op jit(solution)/shard_map/ppermute | solution.py:300
  75.5 5.0 %collective-permute-start.33 = (bf16[128,512]{1,0:T(8,128)(2,1)S(1)}, bf16[128,512]{1,0:T(8,128)(2,1)S(1)}, u32[]{:S(2)}, u32[]{:S(2)}) collective-permute-start(bf16[128,512]{1,0:T(8,128)(2,1)S(1)} %dynamic-slice_bitcast_fusion), channel_id=1, source_target_pairs={{0,8},{2,6},{8,16},{10,2},{16,24},{18,10},{24,28},{26,18},{28,20},... | collective-permute-start | bytes 393224 | tf_op jit(solution)/shard_map/ppermute | solution.py:383
  76.5 5.3 %collective-permute-start.30 = (bf16[256,512]{1,0:T(8,128)(2,1)S(1)}, bf16[256,512]{1,0:T(8,128)(2,1)S(1)}, u32[]{:S(2)}, u32[]{:S(2)}) collective-permute-start(bf16[256,512]{1,0:T(8,128)(2,1)S(1)} %collective-permute-done.29.refs_12_), channel_id=1, source_target_pairs={{0,2},{2,0},{4,6},{6,4},{8,10},{10,8},{12,14},{14,12},{16,18},{18,... | collective-permute-start | bytes 786440 | tf_op jit(solution)/shard_map/ppermute | solution.py:300
  77.1 3.4 %collective-permute-start.32 = (bf16[128,512]{1,0:T(8,128)(2,1)S(1)}, bf16[128,512]{1,0:T(8,128)(2,1)S(1)}, u32[]{:S(2)}, u32[]{:S(2)}) collective-permute-start(bf16[128,512]{1,0:T(8,128)(2,1)S(1)} %collective-permute-done.31.refs_14_), channel_id=1, source_target_pairs={{0,2},{2,0},{4,6},{6,4},{8,10},{10,8},{12,14},{14,12},{16,18},{18,... | collective-permute-start | bytes 393224 | tf_op jit(solution)/shard_map/ppermute | solution.py:300
  80.4 1.3 %collective-permute-start.34 = (bf16[128,512]{1,0:T(8,128)(2,1)S(1)}, bf16[128,512]{1,0:T(8,128)(2,1)S(1)}, u32[]{:S(2)}, u32[]{:S(2)}) collective-permute-start(bf16[128,512]{1,0:T(8,128)(2,1)S(1)} %collective-permute-done.33.refs_16_), channel_id=1, source_target_pairs={{0,2},{2,0},{4,6},{6,4},{8,10},{10,8},{12,14},{14,12},{16,18},{18,... | collective-permute-start | bytes 393224 | tf_op jit(solution)/shard_map/ppermute | solution.py:300

commit v3 on v2

--- a/solution.py
+++ b/solution.py
@@ -1,3 +1,4 @@
+import functools
 import math
 
 import jax
@@ -230,36 +231,43 @@
         write(other_ref, mine_ref)
 
 
-def place_kernel(place_ref, *refs):
-    hops = (len(refs) - 4) // 4
+def place_kernel(plan, place_ref, *refs):
     update_ref, sems = refs[-2:]
+    pieces = refs[-2 - len(plan) : -2]
     core, plane, spot = place_ref[0], place_ref[1], place_ref[2]
     bands = update_ref.shape[0]
     ahead = 1 - 2 * core
     copies = []
-
-    def put(piece_ref, position, part, chunk):
-        rows = piece_ref.shape[0]
+    for index, (hop, chunk, other, half) in enumerate(plan):
+        rows = pieces[index].shape[0]
         member = plane if chunk == 0 else 1 - plane
+        position = spot + ahead * hop if other else spot - ahead * hop
+        part = 0
+        if half:
+            part = 1 - core if other else core
         first_row = pl.multiple_of(part * rows, rows)
         first_col = pl.multiple_of(member * BLOCK, BLOCK)
         to_ref = update_ref.at[
             ring_band(position, bands), pl.ds(first_row, rows), pl.ds(first_col, BLOCK)
         ]
-        copy = pltpu.make_async_copy(piece_ref, to_ref, sems.at[len(copies)])
-        copy.start()
-        copies.append(copy)
-
-    for chunk in range(2):
-        put(refs[chunk], spot, 0, chunk)
-    for hop in range(1, hops + 1):
-        last = hop == hops
-        for chunk in range(2):
-            mine_ref, other_ref = refs[2 + 4 * (hop - 1) + 2 * chunk :][:2]
-            put(mine_ref, spot - ahead * hop, core if last else 0, chunk)
-            put(other_ref, spot + ahead * hop, 1 - core if last else 0, chunk)
+        copies.append(pltpu.make_async_copy(pieces[index], to_ref, sems.at[index]))
+        copies[-1].start()
     for copy in copies:
         copy.wait()
+
+
+def put_pieces(plan, shape, place, pieces, update=None):
+    operands = ([] if update is None else [update]) + pieces
+    return pl.pallas_call(
+        functools.partial(place_kernel, plan),
+        out_shape=jax.ShapeDtypeStruct(shape, jnp.bfloat16),
+        in_specs=[pl.BlockSpec(memory_space=pltpu.SMEM)]
+        + [pl.BlockSpec(memory_space=pl.ANY)] * len(operands),
+        out_specs=pl.BlockSpec(memory_space=pl.ANY),
+        scratch_shapes=[pltpu.SemaphoreType.DMA((len(pieces),))],
+        input_output_aliases={} if update is None else {1: 0},
+        compiler_params=pltpu.CompilerParams(vmem_limit_bytes=1024 * 1024),
+    )(place, *operands)
 
 
 def call(kernel, out_shapes, scratch_shapes, *operands):
@@ -324,18 +332,19 @@
         jnp.stack([plane * (tokens // 2), band] + bands_out).astype(jnp.int32),
         inputs,
     )
+    outputs = jnp.dot(inputs, weight, preferred_element_type=jnp.float32).astype(jnp.bfloat16)
     near = [deal(piece, hop) for hop, piece in zip(hops, packed)]
     cots = [cotangent] + [None] * (bands - 1)
     for step in range(1, bands // 2 + 1):
         behind, further = cots[step - 1], cots[(bands - step + 1) % bands]
         if step == 3:
-            behind, further, near[0] = lax.optimization_barrier((behind, further, near[0]))
+            behind, further, near[0], outputs = lax.optimization_barrier(
+                (behind, further, near[0], outputs)
+            )
         cots[step] = shift(behind, 1)
         if step < bands // 2:
             cots[bands - step] = shift(further, -1)
     far = [swap_plane(piece) for piece in near]
-    outputs = jnp.dot(inputs, weight, preferred_element_type=jnp.float32).astype(jnp.bfloat16)
-    own_band, outputs = lax.optimization_barrier((own_band, outputs))
     (partial_tile,) = call(
         tile_kernel,
         [jax.ShapeDtypeStruct((BLOCK, BLOCK), jnp.float32)],
@@ -383,7 +392,7 @@
         return lax.ppermute(array, "dp", pairs)
 
     half_way = bands // 2
-    crossed = swap_plane(far_piece)
+    crossed, first_turn = lax.optimization_barrier((swap_plane(far_piece), turn(near_piece)))
     other_crossed = swap_core(crossed)
     far_head = jnp.where(
         core == 0,
@@ -391,23 +400,24 @@
         jnp.concatenate([other_crossed, crossed]),
     )
     heads = [near_piece, far_head]
-    pieces = list(heads)
+    plan, pieces = [(0, 0, False, False), (0, 1, False, False)], list(heads)
+    place = jnp.stack([core, plane, spot]).astype(jnp.int32)
+    shape = (bands, rows, CB * BLOCK)
+    update = None
     for hop in range(1, half_way + 1):
+        half = hop == half_way
         for chunk in range(2):
             head = heads[chunk]
-            if hop == half_way:
+            if half:
                 head = lax.dynamic_slice_in_dim(head.reshape(2, -1, BLOCK), core, 1, 0)[0]
-            heads[chunk] = turn(head)
+            heads[chunk] = first_turn if (hop, chunk) == (1, 0) else turn(head)
             pieces += [heads[chunk], swap_core(heads[chunk])]
-    update = pl.pallas_call(
-        place_kernel,
-        out_shape=jax.ShapeDtypeStruct((bands, rows, CB * BLOCK), jnp.bfloat16),
-        in_specs=[pl.BlockSpec(memory_space=pltpu.SMEM)]
-        + [pl.BlockSpec(memory_space=pl.ANY)] * len(pieces),
-        out_specs=pl.BlockSpec(memory_space=pl.ANY),
-        scratch_shapes=[pltpu.SemaphoreType.DMA((len(pieces),))],
-        compiler_params=pltpu.CompilerParams(vmem_limit_bytes=1024 * 1024),
-    )(jnp.stack([core, plane, spot]).astype(jnp.int32), *pieces)
+            plan += [(hop, chunk, False, half), (hop, chunk, True, half)]
+        if hop == half_way - 1:
+            update = put_pieces(plan[:-4], shape, place, pieces[:-4])
+            update, *heads = lax.optimization_barrier((update, *heads))
+            plan, pieces = plan[-4:], pieces[-4:]
+    update = put_pieces(plan, shape, place, pieces, update)
     return (outputs, update)
 
 

time: 84.7 us -> 86.3 us (1.019)
  starting transfers between devices: 32.8 us -> 36.5 us
  waiting for transfers between devices: 35.5 us -> 32.2 us
  Pallas kernels: 10.3 us -> 11.5 us
    ppermute x8, waiting for transfers between devices: 17.6 us -> 13.8 us  [turn(): return lax.ppermute(array, 'dp', pairs)]
    ppermute x7, starting transfers between devices: 8.26 us -> 11.9 us  [shift(): return lax.ppermute(array, 'dp', pairs)]
    ppermute x8, starting transfers between devices: 8.35 us -> 11.1 us  [turn(): return lax.ppermute(array, 'dp', pairs)]
    ppermute x4, waiting for transfers between devices: 4.58 us -> 2.35 us  [deal(): return lax.ppermute(array, ('dp', 'pre'), pairs)]
    ppermute x5, waiting for transfers between devices: 5.84 us -> 7.72 us  [swap_plane(): lax.ppermute(array, 'pre', [(c, members - 1 - c) for c in range(members)])]
    ppermute x4, starting transfers between devices: 7.84 us -> 5.99 us  [deal(): return lax.ppermute(array, ('dp', 'pre'), pairs)]
    pallas_call x1 -> x2, Pallas kernels: 2.7 us -> 3.87 us  [put_pieces(): pl.pallas_call(functools.partial(place_kernel, plan), out_shape=jax.Shape...]
    ppermute x11, waiting for transfers between devices: 5.88 us -> 6.97 us  [swap_core(): return lax.ppermute(array, 'dp', [(g, g ^ 1) for g in range(groups)])]
  transfers between devices with their start and end apart: 35 -> 35, of which waited for: 19 -> 18; matrix products, arithmetic and copies ran while one was open for 5% -> 5% of each run, Pallas kernels for 1% -> 3%
where the time goes in v3:
time: 86.3 us; the launch traced here: 86.1 us
  starting transfers between devices  36.5 us (42%)
  waiting for transfers between devices  32.2 us (37%)
  Pallas kernels  11.5 us (13%)
  matrix products  3.57 us (4%)
  local copies, waits for them, and re-layouts  1.34 us (2%)
    ppermute x8, waiting for transfers between devices, turn(): return lax.ppermute(array, 'dp', pairs)  13.8 us
    ppermute x7, starting transfers between devices, shift(): return lax.ppermute(array, 'dp', pairs)  11.9 us
    ppermute x8, starting transfers between devices, turn(): return lax.ppermute(array, 'dp', pairs)  11.1 us
    ppermute x5, waiting for transfers between devices, swap_plane(): lax.ppermute(array, 'pre', [(c, members - 1 - c) for c in range(members)])  7.72 us
    pallas_call x4, Pallas kernels, call(): pl.pallas_call(kernel, out_shape=out_shapes, in_specs=in_specs, out_specs...  7.62 us
    ppermute x11, waiting for transfers between devices, swap_core(): return lax.ppermute(array, 'dp', [(g, g ^ 1) for g in range(groups)])  6.97 us
    ppermute x5, starting transfers between devices, swap_plane(): lax.ppermute(array, 'pre', [(c, members - 1 - c) for c in range(members)])  6.71 us
    ppermute x4, starting transfers between devices, deal(): return lax.ppermute(array, ('dp', 'pre'), pairs)  5.99 us
  transfers between devices with their start and end apart: 35, of which 18 were waited for; matrix products, arithmetic and copies ran while one was open for 5% of the time, Pallas kernels for 3%

profile of v3, /device:TPU:0, one launch (start us, length us, event | category | flops | bytes accessed | tf_op | source)
XLA Modules:
  0.0 86.1 jit_solution(6049124470018064664)
XLA Ops:
  0.6 3.1 %collective-permute-start = (bf16[128,512]{1,0:T(8,128)(2,1)}, bf16[128,512]{1,0:T(8,128)(2,1)S(1)}, u32[]{:S(2)}, u32[]{:S(2)}) collective-permute-start(bf16[128,512]{1,0:T(8,128)(2,1)} %refs_8_.1), channel_id=1, source_target_pairs={{0,8},{2,10},{8,16},{10,18},{16,24},{18,26},{24,28},{26,30},{28,20... | collective-permute-start | bytes 393224 | tf_op jit(solution)/shard_map/ppermute | solution.py:305
  3.8 1.2 %copy-done = bf16[128,4096]{1,0:T(8,128)(2,1)S(1)} copy-done((bf16[128,4096]{1,0:T(8,128)(2,1)S(1)}, bf16[128,4096]{1,0:T(8,128)(2,1)}, u32[]{:S(2)}) %copy-start) | copy-done | bytes 1048600
  5.0 0.6 shard_map.50
  5.6 3.1 %collective-permute-start.4 = (bf16[128,512]{1,0:T(8,128)(2,1)S(1)}, bf16[128,512]{1,0:T(8,128)(2,1)S(1)}, u32[]{:S(2)}, u32[]{:S(2)}) collective-permute-start(bf16[128,512]{1,0:T(8,128)(2,1)S(1)} %get-tuple-element.20), channel_id=1, source_target_pairs={{0,16},{1,21},{2,18},{3,23},{4,20},{5,17},{6,22},{7,19},{8,24},{9,... | collective-permute-start | bytes 393224 | tf_op jit(solution)/shard_map/ppermute | solution.py:323
  8.7 2.3 %collective-permute-start.5 = (bf16[128,512]{1,0:T(8,128)(2,1)S(1)}, bf16[128,512]{1,0:T(8,128)(2,1)S(1)}, u32[]{:S(2)}, u32[]{:S(2)}) collective-permute-start(bf16[128,512]{1,0:T(8,128)(2,1)S(1)} %get-tuple-element.24), channel_id=1, source_target_pairs={{0,28},{1,25},{2,30},{3,27},{4,24},{5,29},{6,26},{7,31},{8,20},{9,... | collective-permute-start | bytes 393224 | tf_op jit(solution)/shard_map/ppermute | solution.py:323
  11.0 0.5 collective-permute-start.6
  11.5 0.3 collective-permute-start.1
  11.8 1.7 %collective-permute-start.3 = (bf16[128,512]{1,0:T(8,128)(2,1)S(1)}, bf16[128,512]{1,0:T(8,128)(2,1)S(1)}, u32[]{:S(2)}, u32[]{:S(2)}) collective-permute-start(bf16[128,512]{1,0:T(8,128)(2,1)S(1)} %collective-permute-done.2.refs_15_), channel_id=1, source_target_pairs={{0,4},{2,6},{8,0},{10,2},{16,8},{18,10},{24,16},{26,18},{28,24},{3... | collective-permute-start | bytes 393224 | tf_op jit(solution)/shard_map/ppermute | solution.py:305
  13.6 3.6 %convolution_convert_fusion = bf16[128,512]{1,0:T(8,128)(2,1)} fusion(bf16[128,4096]{1,0:T(8,128)(2,1)S(1)} %copy-done, bf16[4096,512]{1,0:T(8,128)(2,1)} %param.4), kind=kOutput, calls=%fused_computation | convolution fusion | flops 536936448 | bytes 5373952 | tf_op jit(solution)/shard_map/dot_general | solution.py:335
  17.1 2.3 %collective-permute-done.4.refs_0_ = bf16[128,512]{1,0:T(8,128)(2,1)S(1)} collective-permute-done((bf16[128,512]{1,0:T(8,128)(2,1)S(1)}, bf16[128,512]{1,0:T(8,128)(2,1)S(1)}, u32[]{:S(2)}, u32[]{:S(2)}) %collective-permute-start.4) | collective-permute-done | bytes 131104 | tf_op jit(solution)/shard_map/ppermute | solution.py:323
  19.6 1.2 %collective-permute-done.1.refs_10_ = bf16[128,512]{1,0:T(8,128)(2,1)S(1)} collective-permute-done((bf16[128,512]{1,0:T(8,128)(2,1)S(1)}, bf16[128,512]{1,0:T(8,128)(2,1)S(1)}, u32[]{:S(2)}, u32[]{:S(2)}) %collective-permute-start.1) | collective-permute-done | bytes 131104 | tf_op jit(solution)/shard_map/ppermute | solution.py:305
  20.9 3.6 %collective-permute-start.12 = (bf16[128,512]{1,0:T(8,128)(2,1)S(1)}, bf16[128,512]{1,0:T(8,128)(2,1)S(1)}, u32[]{:S(2)}, u32[]{:S(2)}) collective-permute-start(bf16[128,512]{1,0:T(8,128)(2,1)S(1)} %collective-permute-done.1.refs_10_), channel_id=1, source_target_pairs={{0,8},{2,10},{8,16},{10,18},{16,24},{18,26},{24,28},{26,30},{28,20... | collective-permute-start | bytes 393224 | tf_op jit(solution)/shard_map/ppermute | solution.py:305
  24.5 1.6 %collective-permute-start.11 = (bf16[64,512]{1,0:T(8,128)(2,1)S(1)}, bf16[64,512]{1,0:T(8,128)(2,1)S(1)}, u32[]{:S(2)}, u32[]{:S(2)}) collective-permute-start(bf16[64,512]{1,0:T(8,128)(2,1)S(1)} %collective-permute-done.7.refs_3_), channel_id=1, source_target_pairs={{0,1},{1,0},{2,3},{3,2},{4,5},{5,4},{6,7},{7,6},{8,9},{9,8},{10,11... | collective-permute-start | bytes 196616 | tf_op jit(solution)/shard_map/ppermute | solution.py:311
  26.1 0.5 collective-permute-start.9
  26.5 1.6 %collective-permute-start.10 = (bf16[128,512]{1,0:T(8,128)(2,1)S(1)}, bf16[128,512]{1,0:T(8,128)(2,1)S(1)}, u32[]{:S(2)}, u32[]{:S(2)}) collective-permute-start(bf16[128,512]{1,0:T(8,128)(2,1)S(1)} %collective-permute-done.6.refs_2_), channel_id=1, source_target_pairs={{0,1},{1,0},{2,3},{3,2},{4,5},{5,4},{6,7},{7,6},{8,9},{9,8},{10,11... | collective-permute-start | bytes 393224 | tf_op jit(solution)/shard_map/ppermute | solution.py:311
  28.1 0.7 collective-permute-start.14
  28.8 0.7 collective-permute-done.11.refs_7_
  29.4 1.6 %collective-permute-start.8 = (bf16[128,512]{1,0:T(8,128)(2,1)S(1)}, bf16[128,512]{1,0:T(8,128)(2,1)S(1)}, u32[]{:S(2)}, u32[]{:S(2)}) collective-permute-start(bf16[128,512]{1,0:T(8,128)(2,1)S(1)} %collective-permute-done.4.refs_0_), channel_id=1, source_target_pairs={{0,1},{1,0},{2,3},{3,2},{4,5},{5,4},{6,7},{7,6},{8,9},{9,8},{10,11... | collective-permute-start | bytes 393224 | tf_op jit(solution)/shard_map/ppermute | solution.py:311
  31.1 2.5 %collective-permute-start.13 = (bf16[128,512]{1,0:T(8,128)(2,1)S(1)}, bf16[128,512]{1,0:T(8,128)(2,1)S(1)}, u32[]{:S(2)}, u32[]{:S(2)}) collective-permute-start(bf16[128,512]{1,0:T(8,128)(2,1)S(1)} %collective-permute-done.12.refs_11_), channel_id=1, source_target_pairs={{0,8},{2,10},{8,16},{10,18},{16,24},{18,26},{24,28},{26,30},{28,20... | collective-permute-start | bytes 393224 | tf_op jit(solution)/shard_map/ppermute | solution.py:305
  33.6 1.7 %collective-permute-done.10.refs_6_ = bf16[128,512]{1,0:T(8,128)(2,1)S(1)} collective-permute-done((bf16[128,512]{1,0:T(8,128)(2,1)S(1)}, bf16[128,512]{1,0:T(8,128)(2,1)S(1)}, u32[]{:S(2)}, u32[]{:S(2)}) %collective-permute-start.10) | collective-permute-done | bytes 131104 | tf_op jit(solution)/shard_map/ppermute | solution.py:311
  35.3 1.9 %collective-permute-done.8.refs_4_ = bf16[128,512]{1,0:T(8,128)(2,1)S(1)} collective-permute-done((bf16[128,512]{1,0:T(8,128)(2,1)S(1)}, bf16[128,512]{1,0:T(8,128)(2,1)S(1)}, u32[]{:S(2)}, u32[]{:S(2)}) %collective-permute-start.8) | collective-permute-done | bytes 131104 | tf_op jit(solution)/shard_map/ppermute | solution.py:311
  37.2 1.4 %shard_map.51.mine_ref = f32[512,512]{1,0:T(8,128)S(1)} custom-call(s32[3]{0:T(128)S(1)} %add_add_fusion.1.place_ref, bf16[128,512]{1,0:T(8,128)(2,1)S(1)} %get-tuple-element.22.own_ref, bf16[128,512]{1,0:T(8,128)(2,1)S(1)} %collective-permute-done.4.refs_0_, bf16[128,512]{1,0:T(8,128)(2,1)S(1)} %collective-permute-done.5.refs_1_, ...), custom_call_target="tpu_custom_call" | custom-call | tf_op jit(solution)/shard_map/pallas_call | solution.py:276
  38.8 2.6 %collective-permute-done.15.other_ref = f32[512,512]{1,0:T(8,128)S(1)} collective-permute-done((f32[512,512]{1,0:T(8,128)S(1)}, f32[512,512]{1,0:T(8,128)S(1)}, u32[]{:S(2)}, u32[]{:S(2)}) %collective-permute-start.15) | collective-permute-done | bytes 1048608 | tf_op jit(solution)/shard_map/ppermute | solution.py:308
  41.3 4.3 %shard_map.52 = (bf16[512,512]{1,0:T(8,128)(2,1)S(1)}, bf16[512,512]{1,0:T(8,128)(2,1)S(1)}) custom-call(s32[2]{0:T(128)S(1)} %pad_add_fusion.side_ref, f32[512,512]{1,0:T(8,128)S(1)} %shard_map.51.mine_ref, f32[512,512]{1,0:T(8,128)S(1)} %collective-permute-done.15.other_ref), custom_call_target="tpu_custom_call" | custom-call | tf_op jit(solution)/shard_map/pallas_call | solution.py:276
  45.9 1.7 %collective-permute-done.16.other_ref = bf16[512,512]{1,0:T(8,128)(2,1)S(1)} collective-permute-done((bf16[512,512]{1,0:T(8,128)(2,1)S(1)}, bf16[512,512]{1,0:T(8,128)(2,1)S(1)}, u32[]{:S(2)}, u32[]{:S(2)}) %collective-permute-start.16) | collective-permute-done | bytes 524320 | tf_op jit(solution)/shard_map/ppermute | solution.py:308
  47.6 1.3 %shard_map.53 = (bf16[256,512]{1,0:T(8,128)(2,1)S(1)}, bf16[128,512]{1,0:T(8,128)(2,1)S(1)}) custom-call(s32[2]{0:T(128)S(1)} %pad_add_fusion.side_ref, bf16[512,512]{1,0:T(8,128)(2,1)S(1)} %get-tuple-element.29.mine_ref, bf16[512,512]{1,0:T(8,128)(2,1)S(1)} %collective-permute-done.16.other_ref, bf16[512,512]{1,0:T(8,128)(2,1)S(1)} %get-tuple-element.30.tile_ref), custom_call_target="tpu_custom_call" | custom-call | tf_op jit(solution)/shard_map/pallas_call | solution.py:276
  49.0 2.1 %collective-permute-start.18 = (bf16[256,512]{1,0:T(8,128)(2,1)S(1)}, bf16[256,512]{1,0:T(8,128)(2,1)S(1)}, u32[]{:S(2)}, u32[]{:S(2)}) collective-permute-start(bf16[256,512]{1,0:T(8,128)(2,1)S(1)} %get-tuple-element.31.refs_0_), channel_id=1, source_target_pairs={{0,8},{2,6},{8,16},{10,2},{16,24},{18,10},{24,28},{26,18},{28,20},... | collective-permute-start | bytes 786440 | tf_op jit(solution)/shard_map/ppermute | solution.py:392
  51.0 1.5 %collective-permute-start.17 = (bf16[128,512]{1,0:T(8,128)(2,1)S(1)}, bf16[128,512]{1,0:T(8,128)(2,1)S(1)}, u32[]{:S(2)}, u32[]{:S(2)}) collective-permute-start(bf16[128,512]{1,0:T(8,128)(2,1)S(1)} %get-tuple-element.32), channel_id=1, source_target_pairs={{0,1},{1,0},{2,3},{3,2},{4,5},{5,4},{6,7},{7,6},{8,9},{9,8},{10,11... | collective-permute-start | bytes 393224 | tf_op jit(solution)/shard_map/ppermute | solution.py:311
  52.5 3.5 %collective-permute-done.17 = bf16[128,512]{1,0:T(8,128)(2,1)S(1)} collective-permute-done((bf16[128,512]{1,0:T(8,128)(2,1)S(1)}, bf16[128,512]{1,0:T(8,128)(2,1)S(1)}, u32[]{:S(2)}, u32[]{:S(2)}) %collective-permute-start.17) | collective-permute-done | bytes 131104 | tf_op jit(solution)/shard_map/ppermute | solution.py:311
  56.0 1.3 %collective-permute-done.19 = bf16[128,512]{1,0:T(8,128)(2,1)S(1)} collective-permute-done((bf16[128,512]{1,0:T(8,128)(2,1)S(1)}, bf16[128,512]{1,0:T(8,128)(2,1)S(1)}, u32[]{:S(2)}, u32[]{:S(2)}) %collective-permute-start.19) | collective-permute-done | bytes 131104 | tf_op jit(solution)/shard_map/ppermute | solution.py:308
  57.4 1.5 %collective-permute-start.21 = (bf16[256,512]{1,0:T(8,128)(2,1)S(1)}, bf16[256,512]{1,0:T(8,128)(2,1)S(1)}, u32[]{:S(2)}, u32[]{:S(2)}) collective-permute-start(bf16[256,512]{1,0:T(8,128)(2,1)S(1)} %maximum_select_fusion.refs_1_), channel_id=1, source_target_pairs={{0,8},{2,6},{8,16},{10,2},{16,24},{18,10},{24,28},{26,18},{28,20},... | collective-permute-start | bytes 786440 | tf_op jit(solution)/shard_map/ppermute | solution.py:392
  58.9 1.0 %collective-permute-start.23 = (bf16[256,512]{1,0:T(8,128)(2,1)S(1)}, bf16[256,512]{1,0:T(8,128)(2,1)S(1)}, u32[]{:S(2)}, u32[]{:S(2)}) collective-permute-start(bf16[256,512]{1,0:T(8,128)(2,1)S(1)} %collective-permute-done.18.refs_2_), channel_id=1, source_target_pairs={{0,8},{2,6},{8,16},{10,2},{16,24},{18,10},{24,28},{26,18},{28,20},... | collective-permute-start | bytes 786440 | tf_op jit(solution)/shard_map/ppermute | solution.py:392
  59.8 4.0 %collective-permute-done.21.refs_4_ = bf16[256,512]{1,0:T(8,128)(2,1)S(1)} collective-permute-done((bf16[256,512]{1,0:T(8,128)(2,1)S(1)}, bf16[256,512]{1,0:T(8,128)(2,1)S(1)}, u32[]{:S(2)}, u32[]{:S(2)}) %collective-permute-start.21) | collective-permute-done | bytes 262176 | tf_op jit(solution)/shard_map/ppermute | solution.py:392
  63.8 1.4 %collective-permute-start.25 = (bf16[256,512]{1,0:T(8,128)(2,1)S(1)}, bf16[256,512]{1,0:T(8,128)(2,1)S(1)}, u32[]{:S(2)}, u32[]{:S(2)}) collective-permute-start(bf16[256,512]{1,0:T(8,128)(2,1)S(1)} %collective-permute-done.21.refs_4_), channel_id=1, source_target_pairs={{0,8},{2,6},{8,16},{10,2},{16,24},{18,10},{24,28},{26,18},{28,20},... | collective-permute-start | bytes 786440 | tf_op jit(solution)/shard_map/ppermute | solution.py:392
  65.2 1.4 %collective-permute-done.23.refs_6_ = bf16[256,512]{1,0:T(8,128)(2,1)S(1)} collective-permute-done((bf16[256,512]{1,0:T(8,128)(2,1)S(1)}, bf16[256,512]{1,0:T(8,128)(2,1)S(1)}, u32[]{:S(2)}, u32[]{:S(2)}) %collective-permute-start.23) | collective-permute-done | bytes 262176 | tf_op jit(solution)/shard_map/ppermute | solution.py:392
  66.6 1.4 %collective-permute-start.27 = (bf16[256,512]{1,0:T(8,128)(2,1)S(1)}, bf16[256,512]{1,0:T(8,128)(2,1)S(1)}, u32[]{:S(2)}, u32[]{:S(2)}) collective-permute-start(bf16[256,512]{1,0:T(8,128)(2,1)S(1)} %collective-permute-done.23.refs_6_), channel_id=1, source_target_pairs={{0,8},{2,6},{8,16},{10,2},{16,24},{18,10},{24,28},{26,18},{28,20},... | collective-permute-start | bytes 786440 | tf_op jit(solution)/shard_map/ppermute | solution.py:392
  68.0 0.5 collective-permute-start.22
  68.5 1.7 %collective-permute-done.25.refs_8_ = bf16[256,512]{1,0:T(8,128)(2,1)S(1)} collective-permute-done((bf16[256,512]{1,0:T(8,128)(2,1)S(1)}, bf16[256,512]{1,0:T(8,128)(2,1)S(1)}, u32[]{:S(2)}, u32[]{:S(2)}) %collective-permute-start.25) | collective-permute-done | bytes 262176 | tf_op jit(solution)/shard_map/ppermute | solution.py:392
  70.2 1.4 %collective-permute-start.28 = (bf16[256,512]{1,0:T(8,128)(2,1)S(1)}, bf16[256,512]{1,0:T(8,128)(2,1)S(1)}, u32[]{:S(2)}, u32[]{:S(2)}) collective-permute-start(bf16[256,512]{1,0:T(8,128)(2,1)S(1)} %collective-permute-done.25.refs_8_), channel_id=1, source_target_pairs={{0,8},{2,6},{8,16},{10,2},{16,24},{18,10},{24,28},{26,18},{28,20},... | collective-permute-start | bytes 786440 | tf_op jit(solution)/shard_map/ppermute | solution.py:392
  71.7 1.3 %collective-permute-done.27.refs_1_ = bf16[256,512]{1,0:T(8,128)(2,1)S(1)} collective-permute-done((bf16[256,512]{1,0:T(8,128)(2,1)S(1)}, bf16[256,512]{1,0:T(8,128)(2,1)S(1)}, u32[]{:S(2)}, u32[]{:S(2)}) %collective-permute-start.27) | collective-permute-done | bytes 262176 | tf_op jit(solution)/shard_map/ppermute | solution.py:392
  73.0 2.1 %shard_map.54.refs_0_ = bf16[8,256,1024]{2,1,0:T(8,128)(2,1)} custom-call(s32[3]{0:T(128)S(1)} %add_add_fusion.place_ref, bf16[256,512]{1,0:T(8,128)(2,1)S(1)} %get-tuple-element.31.refs_0_, bf16[256,512]{1,0:T(8,128)(2,1)S(1)} %maximum_select_fusion.refs_1_, bf16[256,512]{1,0:T(8,128)(2,1)S(1)} %collective-permute-done.18.refs_2_, ...), custom_call_target="tpu_custom_call" | custom-call | tf_op jit(solution)/shard_map/pallas_call | solution.py:261
  75.2 1.4 %collective-permute-done.28.refs_3_ = bf16[256,512]{1,0:T(8,128)(2,1)S(1)} collective-permute-done((bf16[256,512]{1,0:T(8,128)(2,1)S(1)}, bf16[256,512]{1,0:T(8,128)(2,1)S(1)}, u32[]{:S(2)}, u32[]{:S(2)}) %collective-permute-start.28) | collective-permute-done | bytes 262176 | tf_op jit(solution)/shard_map/ppermute | solution.py:392
  76.6 1.5 %collective-permute-start.33 = (bf16[128,512]{1,0:T(8,128)(2,1)S(1)}, bf16[128,512]{1,0:T(8,128)(2,1)S(1)}, u32[]{:S(2)}, u32[]{:S(2)}) collective-permute-start(bf16[128,512]{1,0:T(8,128)(2,1)S(1)} %dynamic-slice_bitcast_fusion), channel_id=1, source_target_pairs={{0,8},{2,6},{8,16},{10,2},{16,24},{18,10},{24,28},{26,18},{28,20},... | collective-permute-start | bytes 393224 | tf_op jit(solution)/shard_map/ppermute | solution.py:392
  78.1 1.0 %collective-permute-start.31 = (bf16[128,512]{1,0:T(8,128)(2,1)S(1)}, bf16[128,512]{1,0:T(8,128)(2,1)S(1)}, u32[]{:S(2)}, u32[]{:S(2)}) collective-permute-start(bf16[128,512]{1,0:T(8,128)(2,1)S(1)} %dynamic-slice_bitcast_fusion.1), channel_id=1, source_target_pairs={{0,8},{2,6},{8,16},{10,2},{16,24},{18,10},{24,28},{26,18},{28,20},... | collective-permute-start | bytes 393224 | tf_op jit(solution)/shard_map/ppermute | solution.py:392
  79.0 2.6 %collective-permute-done.33.refs_7_ = bf16[128,512]{1,0:T(8,128)(2,1)S(1)} collective-permute-done((bf16[128,512]{1,0:T(8,128)(2,1)S(1)}, bf16[128,512]{1,0:T(8,128)(2,1)S(1)}, u32[]{:S(2)}, u32[]{:S(2)}) %collective-permute-start.33) | collective-permute-done | bytes 131104 | tf_op jit(solution)/shard_map/ppermute | solution.py:392
  81.6 1.4 %collective-permute-done.31.refs_5_ = bf16[128,512]{1,0:T(8,128)(2,1)S(1)} collective-permute-done((bf16[128,512]{1,0:T(8,128)(2,1)S(1)}, bf16[128,512]{1,0:T(8,128)(2,1)S(1)}, u32[]{:S(2)}, u32[]{:S(2)}) %collective-permute-start.31) | collective-permute-done | bytes 131104 | tf_op jit(solution)/shard_map/ppermute | solution.py:392
  83.1 1.3 %collective-permute-done.32.refs_6_ = bf16[128,512]{1,0:T(8,128)(2,1)S(1)} collective-permute-done((bf16[128,512]{1,0:T(8,128)(2,1)S(1)}, bf16[128,512]{1,0:T(8,128)(2,1)S(1)}, u32[]{:S(2)}, u32[]{:S(2)}) %collective-permute-start.32) | collective-permute-done | bytes 131104 | tf_op jit(solution)/shard_map/ppermute | solution.py:308
  84.4 1.8 %shard_map.55 = bf16[8,256,1024]{2,1,0:T(8,128)(2,1)} custom-call(s32[3]{0:T(128)S(1)} %add_add_fusion.place_ref, bf16[8,256,1024]{2,1,0:T(8,128)(2,1)} %shard_map.54.refs_0_, bf16[256,512]{1,0:T(8,128)(2,1)S(1)} %collective-permute-done.27.refs_1_, bf16[256,512]{1,0:T(8,128)(2,1)S(1)} %collective-permute-done.29.refs_2_, ...), custom_call_target="tpu_custom_call", output_to_operand_aliasing={{}: (1, {})} | custom-call | tf_op jit(solution)/shard_map/pallas_call | solution.py:261
  (40 shorter events, 1.0 us)
Async XLA Ops:
  0.6 10.9 %collective-permute-start = (bf16[128,512]{1,0:T(8,128)(2,1)}, bf16[128,512]{1,0:T(8,128)(2,1)S(1)}, u32[]{:S(2)}, u32[]{:S(2)}) collective-permute-start(bf16[128,512]{1,0:T(8,128)(2,1)} %refs_8_.1), channel_id=1, source_target_pairs={{0,8},{2,10},{8,16},{10,18},{16,24},{18,26},{24,28},{26,30},{28,20... | collective-permute-start | bytes 393224 | tf_op jit(solution)/shard_map/ppermute | solution.py:305
  3.7 8.1 %collective-permute-start.2 = (bf16[128,512]{1,0:T(8,128)(2,1)}, bf16[128,512]{1,0:T(8,128)(2,1)S(1)}, u32[]{:S(2)}, u32[]{:S(2)}) collective-permute-start(bf16[128,512]{1,0:T(8,128)(2,1)} %refs_8_.1), channel_id=1, source_target_pairs={{0,4},{2,6},{8,0},{10,2},{16,8},{18,10},{24,16},{26,18},{28,24},{3... | collective-permute-start | bytes 393224 | tf_op jit(solution)/shard_map/ppermute | solution.py:305
  3.8 1.2 %copy-start = (bf16[128,4096]{1,0:T(8,128)(2,1)S(1)}, bf16[128,4096]{1,0:T(8,128)(2,1)}, u32[]{:S(2)}) copy-start(bf16[128,4096]{1,0:T(8,128)(2,1)} %inputs_ref.1) | copy-start | bytes 3145732
  5.0 32.2 %copy-start.1 = (bf16[128,512]{1,0:T(8,128)(2,1)S(1)}, bf16[128,512]{1,0:T(8,128)(2,1)}, u32[]{:S(2)}) copy-start(bf16[128,512]{1,0:T(8,128)(2,1)} %refs_8_.1) | copy-start | bytes 393220
  5.6 13.9 %collective-permute-start.4 = (bf16[128,512]{1,0:T(8,128)(2,1)S(1)}, bf16[128,512]{1,0:T(8,128)(2,1)S(1)}, u32[]{:S(2)}, u32[]{:S(2)}) collective-permute-start(bf16[128,512]{1,0:T(8,128)(2,1)S(1)} %get-tuple-element.20), channel_id=1, source_target_pairs={{0,16},{1,21},{2,18},{3,23},{4,20},{5,17},{6,22},{7,19},{8,24},{9,... | collective-permute-start | bytes 393224 | tf_op jit(solution)/shard_map/ppermute | solution.py:323
  8.7 17.4 %collective-permute-start.5 = (bf16[128,512]{1,0:T(8,128)(2,1)S(1)}, bf16[128,512]{1,0:T(8,128)(2,1)S(1)}, u32[]{:S(2)}, u32[]{:S(2)}) collective-permute-start(bf16[128,512]{1,0:T(8,128)(2,1)S(1)} %get-tuple-element.24), channel_id=1, source_target_pairs={{0,28},{1,25},{2,30},{3,27},{4,24},{5,29},{6,26},{7,31},{8,20},{9,... | collective-permute-start | bytes 393224 | tf_op jit(solution)/shard_map/ppermute | solution.py:323
  11.0 15.5 %collective-permute-start.6 = (bf16[128,512]{1,0:T(8,128)(2,1)S(1)}, bf16[128,512]{1,0:T(8,128)(2,1)S(1)}, u32[]{:S(2)}, u32[]{:S(2)}) collective-permute-start(bf16[128,512]{1,0:T(8,128)(2,1)S(1)} %get-tuple-element.25), channel_id=1, source_target_pairs={{0,4},{1,13},{2,6},{3,15},{4,0},{5,9},{6,2},{7,11},{8,12},{9,5},{1... | collective-permute-start | bytes 393224 | tf_op jit(solution)/shard_map/ppermute | solution.py:323
  11.5 9.2 %collective-permute-start.1 = (bf16[128,512]{1,0:T(8,128)(2,1)S(1)}, bf16[128,512]{1,0:T(8,128)(2,1)S(1)}, u32[]{:S(2)}, u32[]{:S(2)}) collective-permute-start(bf16[128,512]{1,0:T(8,128)(2,1)S(1)} %collective-permute-done.refs_9_), channel_id=1, source_target_pairs={{0,8},{2,10},{8,16},{10,18},{16,24},{18,26},{24,28},{26,30},{28,20... | collective-permute-start | bytes 393224 | tf_op jit(solution)/shard_map/ppermute | solution.py:305
  11.8 9.1 %collective-permute-start.3 = (bf16[128,512]{1,0:T(8,128)(2,1)S(1)}, bf16[128,512]{1,0:T(8,128)(2,1)S(1)}, u32[]{:S(2)}, u32[]{:S(2)}) collective-permute-start(bf16[128,512]{1,0:T(8,128)(2,1)S(1)} %collective-permute-done.2.refs_15_), channel_id=1, source_target_pairs={{0,4},{2,6},{8,0},{10,2},{16,8},{18,10},{24,16},{26,18},{28,24},{3... | collective-permute-start | bytes 393224 | tf_op jit(solution)/shard_map/ppermute | solution.py:305
  19.5 5.0 %collective-permute-start.7 = (bf16[64,512]{1,0:T(8,128)(2,1)S(1)}, bf16[64,512]{1,0:T(8,128)(2,1)S(1)}, u32[]{:S(2)}, u32[]{:S(2)}) collective-permute-start(bf16[64,512]{1,0:T(8,128)(2,1)S(1)} %get-tuple-element.26), channel_id=1, source_target_pairs={{0,8},{1,9},{2,10},{3,11},{4,12},{5,13},{6,14},{7,15},{8,0},{9,1},... | collective-permute-start | bytes 196616 | tf_op jit(solution)/shard_map/ppermute | solution.py:323
  20.9 10.2 %collective-permute-start.12 = (bf16[128,512]{1,0:T(8,128)(2,1)S(1)}, bf16[128,512]{1,0:T(8,128)(2,1)S(1)}, u32[]{:S(2)}, u32[]{:S(2)}) collective-permute-start(bf16[128,512]{1,0:T(8,128)(2,1)S(1)} %collective-permute-done.1.refs_10_), channel_id=1, source_target_pairs={{0,8},{2,10},{8,16},{10,18},{16,24},{18,26},{24,28},{26,30},{28,20... | collective-permute-start | bytes 393224 | tf_op jit(solution)/shard_map/ppermute | solution.py:305
  24.5 4.9 %collective-permute-start.11 = (bf16[64,512]{1,0:T(8,128)(2,1)S(1)}, bf16[64,512]{1,0:T(8,128)(2,1)S(1)}, u32[]{:S(2)}, u32[]{:S(2)}) collective-permute-start(bf16[64,512]{1,0:T(8,128)(2,1)S(1)} %collective-permute-done.7.refs_3_), channel_id=1, source_target_pairs={{0,1},{1,0},{2,3},{3,2},{4,5},{5,4},{6,7},{7,6},{8,9},{9,8},{10,11... | collective-permute-start | bytes 196616 | tf_op jit(solution)/shard_map/ppermute | solution.py:311
  26.1 7.6 %collective-permute-start.9 = (bf16[128,512]{1,0:T(8,128)(2,1)S(1)}, bf16[128,512]{1,0:T(8,128)(2,1)S(1)}, u32[]{:S(2)}, u32[]{:S(2)}) collective-permute-start(bf16[128,512]{1,0:T(8,128)(2,1)S(1)} %collective-permute-done.5.refs_1_), channel_id=1, source_target_pairs={{0,1},{1,0},{2,3},{3,2},{4,5},{5,4},{6,7},{7,6},{8,9},{9,8},{10,11... | collective-permute-start | bytes 393224 | tf_op jit(solution)/shard_map/ppermute | solution.py:311
  26.5 8.8 %collective-permute-start.10 = (bf16[128,512]{1,0:T(8,128)(2,1)S(1)}, bf16[128,512]{1,0:T(8,128)(2,1)S(1)}, u32[]{:S(2)}, u32[]{:S(2)}) collective-permute-start(bf16[128,512]{1,0:T(8,128)(2,1)S(1)} %collective-permute-done.6.refs_2_), channel_id=1, source_target_pairs={{0,1},{1,0},{2,3},{3,2},{4,5},{5,4},{6,7},{7,6},{8,9},{9,8},{10,11... | collective-permute-start | bytes 393224 | tf_op jit(solution)/shard_map/ppermute | solution.py:311
  28.1 7.2 %collective-permute-start.14 = (bf16[128,512]{1,0:T(8,128)(2,1)S(1)}, bf16[128,512]{1,0:T(8,128)(2,1)S(1)}, u32[]{:S(2)}, u32[]{:S(2)}) collective-permute-start(bf16[128,512]{1,0:T(8,128)(2,1)S(1)} %collective-permute-done.3.refs_14_), channel_id=1, source_target_pairs={{0,4},{2,6},{8,0},{10,2},{16,8},{18,10},{24,16},{26,18},{28,24},{3... | collective-permute-start | bytes 393224 | tf_op jit(solution)/shard_map/ppermute | solution.py:305
  29.4 7.8 %collective-permute-start.8 = (bf16[128,512]{1,0:T(8,128)(2,1)S(1)}, bf16[128,512]{1,0:T(8,128)(2,1)S(1)}, u32[]{:S(2)}, u32[]{:S(2)}) collective-permute-start(bf16[128,512]{1,0:T(8,128)(2,1)S(1)} %collective-permute-done.4.refs_0_), channel_id=1, source_target_pairs={{0,1},{1,0},{2,3},{3,2},{4,5},{5,4},{6,7},{7,6},{8,9},{9,8},{10,11... | collective-permute-start | bytes 393224 | tf_op jit(solution)/shard_map/ppermute | solution.py:311
  31.1 6.1 %collective-permute-start.13 = (bf16[128,512]{1,0:T(8,128)(2,1)S(1)}, bf16[128,512]{1,0:T(8,128)(2,1)S(1)}, u32[]{:S(2)}, u32[]{:S(2)}) collective-permute-start(bf16[128,512]{1,0:T(8,128)(2,1)S(1)} %collective-permute-done.12.refs_11_), channel_id=1, source_target_pairs={{0,8},{2,10},{8,16},{10,18},{16,24},{18,26},{24,28},{26,30},{28,20... | collective-permute-start | bytes 393224 | tf_op jit(solution)/shard_map/ppermute | solution.py:305
  38.6 2.7 %collective-permute-start.15 = (f32[512,512]{1,0:T(8,128)S(1)}, f32[512,512]{1,0:T(8,128)S(1)}, u32[]{:S(2)}, u32[]{:S(2)}) collective-permute-start(f32[512,512]{1,0:T(8,128)S(1)} %shard_map.51.mine_ref), channel_id=1, source_target_pairs={{0,2},{2,0},{4,6},{6,4},{8,10},{10,8},{12,14},{14,12},{16,18},{18,... | collective-permute-start | bytes 3145736 | tf_op jit(solution)/shard_map/ppermute | solution.py:308
  45.6 2.0 %collective-permute-start.16 = (bf16[512,512]{1,0:T(8,128)(2,1)S(1)}, bf16[512,512]{1,0:T(8,128)(2,1)S(1)}, u32[]{:S(2)}, u32[]{:S(2)}) collective-permute-start(bf16[512,512]{1,0:T(8,128)(2,1)S(1)} %get-tuple-element.29.mine_ref), channel_id=1, source_target_pairs={{0,2},{2,0},{4,6},{6,4},{8,10},{10,8},{12,14},{14,12},{16,18},{18,... | collective-permute-start | bytes 1572872 | tf_op jit(solution)/shard_map/ppermute | solution.py:308
  49.0 7.0 %collective-permute-start.18 = (bf16[256,512]{1,0:T(8,128)(2,1)S(1)}, bf16[256,512]{1,0:T(8,128)(2,1)S(1)}, u32[]{:S(2)}, u32[]{:S(2)}) collective-permute-start(bf16[256,512]{1,0:T(8,128)(2,1)S(1)} %get-tuple-element.31.refs_0_), channel_id=1, source_target_pairs={{0,8},{2,6},{8,16},{10,2},{16,24},{18,10},{24,28},{26,18},{28,20},... | collective-permute-start | bytes 786440 | tf_op jit(solution)/shard_map/ppermute | solution.py:392
  51.0 5.0 %collective-permute-start.17 = (bf16[128,512]{1,0:T(8,128)(2,1)S(1)}, bf16[128,512]{1,0:T(8,128)(2,1)S(1)}, u32[]{:S(2)}, u32[]{:S(2)}) collective-permute-start(bf16[128,512]{1,0:T(8,128)(2,1)S(1)} %get-tuple-element.32), channel_id=1, source_target_pairs={{0,1},{1,0},{2,3},{3,2},{4,5},{5,4},{6,7},{7,6},{8,9},{9,8},{10,11... | collective-permute-start | bytes 393224 | tf_op jit(solution)/shard_map/ppermute | solution.py:311
  56.0 1.3 %collective-permute-start.19 = (bf16[128,512]{1,0:T(8,128)(2,1)S(1)}, bf16[128,512]{1,0:T(8,128)(2,1)S(1)}, u32[]{:S(2)}, u32[]{:S(2)}) collective-permute-start(bf16[128,512]{1,0:T(8,128)(2,1)S(1)} %collective-permute-done.17), channel_id=1, source_target_pairs={{0,2},{2,0},{4,6},{6,4},{8,10},{10,8},{12,14},{14,12},{16,18},{18,... | collective-permute-start | bytes 393224 | tf_op jit(solution)/shard_map/ppermute | solution.py:308
  57.4 6.4 %collective-permute-start.21 = (bf16[256,512]{1,0:T(8,128)(2,1)S(1)}, bf16[256,512]{1,0:T(8,128)(2,1)S(1)}, u32[]{:S(2)}, u32[]{:S(2)}) collective-permute-start(bf16[256,512]{1,0:T(8,128)(2,1)S(1)} %maximum_select_fusion.refs_1_), channel_id=1, source_target_pairs={{0,8},{2,6},{8,16},{10,2},{16,24},{18,10},{24,28},{26,18},{28,20},... | collective-permute-start | bytes 786440 | tf_op jit(solution)/shard_map/ppermute | solution.py:392
  58.9 7.8 %collective-permute-start.23 = (bf16[256,512]{1,0:T(8,128)(2,1)S(1)}, bf16[256,512]{1,0:T(8,128)(2,1)S(1)}, u32[]{:S(2)}, u32[]{:S(2)}) collective-permute-start(bf16[256,512]{1,0:T(8,128)(2,1)S(1)} %collective-permute-done.18.refs_2_), channel_id=1, source_target_pairs={{0,8},{2,6},{8,16},{10,2},{16,24},{18,10},{24,28},{26,18},{28,20},... | collective-permute-start | bytes 786440 | tf_op jit(solution)/shard_map/ppermute | solution.py:392
  63.8 6.4 %collective-permute-start.25 = (bf16[256,512]{1,0:T(8,128)(2,1)S(1)}, bf16[256,512]{1,0:T(8,128)(2,1)S(1)}, u32[]{:S(2)}, u32[]{:S(2)}) collective-permute-start(bf16[256,512]{1,0:T(8,128)(2,1)S(1)} %collective-permute-done.21.refs_4_), channel_id=1, source_target_pairs={{0,8},{2,6},{8,16},{10,2},{16,24},{18,10},{24,28},{26,18},{28,20},... | collective-permute-start | bytes 786440 | tf_op jit(solution)/shard_map/ppermute | solution.py:392
  65.2 5.0 %collective-permute-start.20 = (bf16[256,512]{1,0:T(8,128)(2,1)S(1)}, bf16[256,512]{1,0:T(8,128)(2,1)S(1)}, u32[]{:S(2)}, u32[]{:S(2)}) collective-permute-start(bf16[256,512]{1,0:T(8,128)(2,1)S(1)} %collective-permute-done.18.refs_2_), channel_id=1, source_target_pairs={{0,2},{2,0},{4,6},{6,4},{8,10},{10,8},{12,14},{14,12},{16,18},{18,... | collective-permute-start | bytes 786440 | tf_op jit(solution)/shard_map/ppermute | solution.py:308
  66.6 6.4 %collective-permute-start.27 = (bf16[256,512]{1,0:T(8,128)(2,1)S(1)}, bf16[256,512]{1,0:T(8,128)(2,1)S(1)}, u32[]{:S(2)}, u32[]{:S(2)}) collective-permute-start(bf16[256,512]{1,0:T(8,128)(2,1)S(1)} %collective-permute-done.23.refs_6_), channel_id=1, source_target_pairs={{0,8},{2,6},{8,16},{10,2},{16,24},{18,10},{24,28},{26,18},{28,20},... | collective-permute-start | bytes 786440 | tf_op jit(solution)/shard_map/ppermute | solution.py:392
  68.0 5.0 %collective-permute-start.24 = (bf16[256,512]{1,0:T(8,128)(2,1)S(1)}, bf16[256,512]{1,0:T(8,128)(2,1)S(1)}, u32[]{:S(2)}, u32[]{:S(2)}) collective-permute-start(bf16[256,512]{1,0:T(8,128)(2,1)S(1)} %collective-permute-done.23.refs_6_), channel_id=1, source_target_pairs={{0,2},{2,0},{4,6},{6,4},{8,10},{10,8},{12,14},{14,12},{16,18},{18,... | collective-permute-start | bytes 786440 | tf_op jit(solution)/shard_map/ppermute | solution.py:308
  68.0 5.0 %collective-permute-start.22 = (bf16[256,512]{1,0:T(8,128)(2,1)S(1)}, bf16[256,512]{1,0:T(8,128)(2,1)S(1)}, u32[]{:S(2)}, u32[]{:S(2)}) collective-permute-start(bf16[256,512]{1,0:T(8,128)(2,1)S(1)} %collective-permute-done.21.refs_4_), channel_id=1, source_target_pairs={{0,2},{2,0},{4,6},{6,4},{8,10},{10,8},{12,14},{14,12},{16,18},{18,... | collective-permute-start | bytes 786440 | tf_op jit(solution)/shard_map/ppermute | solution.py:308
  70.2 2.8 %collective-permute-start.26 = (bf16[256,512]{1,0:T(8,128)(2,1)S(1)}, bf16[256,512]{1,0:T(8,128)(2,1)S(1)}, u32[]{:S(2)}, u32[]{:S(2)}) collective-permute-start(bf16[256,512]{1,0:T(8,128)(2,1)S(1)} %collective-permute-done.25.refs_8_), channel_id=1, source_target_pairs={{0,2},{2,0},{4,6},{6,4},{8,10},{10,8},{12,14},{14,12},{16,18},{18,... | collective-permute-start | bytes 786440 | tf_op jit(solution)/shard_map/ppermute | solution.py:308
  70.2 6.4 %collective-permute-start.28 = (bf16[256,512]{1,0:T(8,128)(2,1)S(1)}, bf16[256,512]{1,0:T(8,128)(2,1)S(1)}, u32[]{:S(2)}, u32[]{:S(2)}) collective-permute-start(bf16[256,512]{1,0:T(8,128)(2,1)S(1)} %collective-permute-done.25.refs_8_), channel_id=1, source_target_pairs={{0,8},{2,6},{8,16},{10,2},{16,24},{18,10},{24,28},{26,18},{28,20},... | collective-permute-start | bytes 786440 | tf_op jit(solution)/shard_map/ppermute | solution.py:392
  73.0 10.0 %collective-permute-start.29 = (bf16[256,512]{1,0:T(8,128)(2,1)S(1)}, bf16[256,512]{1,0:T(8,128)(2,1)S(1)}, u32[]{:S(2)}, u32[]{:S(2)}) collective-permute-start(bf16[256,512]{1,0:T(8,128)(2,1)S(1)} %collective-permute-done.27.refs_1_), channel_id=1, source_target_pairs={{0,2},{2,0},{4,6},{6,4},{8,10},{10,8},{12,14},{14,12},{16,18},{18,... | collective-permute-start | bytes 786440 | tf_op jit(solution)/shard_map/ppermute | solution.py:308
  76.6 5.0 %collective-permute-start.33 = (bf16[128,512]{1,0:T(8,128)(2,1)S(1)}, bf16[128,512]{1,0:T(8,128)(2,1)S(1)}, u32[]{:S(2)}, u32[]{:S(2)}) collective-permute-start(bf16[128,512]{1,0:T(8,128)(2,1)S(1)} %dynamic-slice_bitcast_fusion), channel_id=1, source_target_pairs={{0,8},{2,6},{8,16},{10,2},{16,24},{18,10},{24,28},{26,18},{28,20},... | collective-permute-start | bytes 393224 | tf_op jit(solution)/shard_map/ppermute | solution.py:392
  78.1 5.0 %collective-permute-start.30 = (bf16[256,512]{1,0:T(8,128)(2,1)S(1)}, bf16[256,512]{1,0:T(8,128)(2,1)S(1)}, u32[]{:S(2)}, u32[]{:S(2)}) collective-permute-start(bf16[256,512]{1,0:T(8,128)(2,1)S(1)} %collective-permute-done.28.refs_3_), channel_id=1, source_target_pairs={{0,2},{2,0},{4,6},{6,4},{8,10},{10,8},{12,14},{14,12},{16,18},{18,... | collective-permute-start | bytes 786440 | tf_op jit(solution)/shard_map/ppermute | solution.py:308
  78.1 5.0 %collective-permute-start.31 = (bf16[128,512]{1,0:T(8,128)(2,1)S(1)}, bf16[128,512]{1,0:T(8,128)(2,1)S(1)}, u32[]{:S(2)}, u32[]{:S(2)}) collective-permute-start(bf16[128,512]{1,0:T(8,128)(2,1)S(1)} %dynamic-slice_bitcast_fusion.1), channel_id=1, source_target_pairs={{0,8},{2,6},{8,16},{10,2},{16,24},{18,10},{24,28},{26,18},{28,20},... | collective-permute-start | bytes 393224 | tf_op jit(solution)/shard_map/ppermute | solution.py:392
  81.6 1.4 %collective-permute-start.34 = (bf16[128,512]{1,0:T(8,128)(2,1)S(1)}, bf16[128,512]{1,0:T(8,128)(2,1)S(1)}, u32[]{:S(2)}, u32[]{:S(2)}) collective-permute-start(bf16[128,512]{1,0:T(8,128)(2,1)S(1)} %collective-permute-done.33.refs_7_), channel_id=1, source_target_pairs={{0,2},{2,0},{4,6},{6,4},{8,10},{10,8},{12,14},{14,12},{16,18},{18,... | collective-permute-start | bytes 393224 | tf_op jit(solution)/shard_map/ppermute | solution.py:308
  83.0 1.3 %collective-permute-start.32 = (bf16[128,512]{1,0:T(8,128)(2,1)S(1)}, bf16[128,512]{1,0:T(8,128)(2,1)S(1)}, u32[]{:S(2)}, u32[]{:S(2)}) collective-permute-start(bf16[128,512]{1,0:T(8,128)(2,1)S(1)} %collective-permute-done.31.refs_5_), channel_id=1, source_target_pairs={{0,2},{2,0},{4,6},{6,4},{8,10},{10,8},{12,14},{14,12},{16,18},{18,... | collective-permute-start | bytes 393224 | tf_op jit(solution)/shard_map/ppermute | solution.py:308

commit v4 on v3

--- a/solution.py
+++ b/solution.py
@@ -187,7 +187,7 @@
     near_refs, far_refs = refs[:hops], refs[hops : 2 * hops]
     cot_refs = refs[2 * hops : -3]
     partial_ref, band_ref, cot_ref = refs[-3:]
-    plane, band, spot = place_ref[0], place_ref[1], place_ref[2]
+    plane, band = place_ref[0], place_ref[1]
     tokens = own_ref.shape[0]
 
     def put(to_ref, piece_ref, source, part):
@@ -201,8 +201,9 @@
         for piece_ref, member in ((near_refs[hop], plane), (far_refs[hop], 1 - plane)):
             offset = jnp.where(member == 0, OFFSETS[0][hop], OFFSETS[1][hop])
             put(band_ref, piece_ref, band ^ offset, member if last else 0)
-    for step, piece_ref in enumerate(cot_refs):
-        put(cot_ref, piece_ref, ring_band(spot - step, len(cot_refs)), 0)
+    for offset, pair_ref in enumerate(cot_refs):
+        for part, source in enumerate((band ^ offset, band ^ offset ^ 4)):
+            put(cot_ref, pair_ref.at[pl.ds(part * tokens, tokens)], source, 0)
     partial_ref[...] = contract(band_ref[...], cot_ref[...], 0, 0)
 
 
@@ -231,21 +232,22 @@
         write(other_ref, mine_ref)
 
 
+WHOLE, MINE, OTHERS = 0, 1, -1
+
+
 def place_kernel(plan, place_ref, *refs):
-    update_ref, sems = refs[-2:]
-    pieces = refs[-2 - len(plan) : -2]
+    pieces = refs[: len(plan)]
+    update_ref, sems = refs[len(plan) :]
     core, plane, spot = place_ref[0], place_ref[1], place_ref[2]
     bands = update_ref.shape[0]
     ahead = 1 - 2 * core
     copies = []
-    for index, (hop, chunk, other, half) in enumerate(plan):
+    for index, (hop, chunk, other, part) in enumerate(plan):
         rows = pieces[index].shape[0]
         member = plane if chunk == 0 else 1 - plane
         position = spot + ahead * hop if other else spot - ahead * hop
-        part = 0
-        if half:
-            part = 1 - core if other else core
-        first_row = pl.multiple_of(part * rows, rows)
+        number = {WHOLE: 0, MINE: core, OTHERS: 1 - core}[part]
+        first_row = pl.multiple_of(number * rows, rows)
         first_col = pl.multiple_of(member * BLOCK, BLOCK)
         to_ref = update_ref.at[
             ring_band(position, bands), pl.ds(first_row, rows), pl.ds(first_col, BLOCK)
@@ -256,18 +258,16 @@
         copy.wait()
 
 
-def put_pieces(plan, shape, place, pieces, update=None):
-    operands = ([] if update is None else [update]) + pieces
+def put_pieces(plan, shape, place, pieces):
     return pl.pallas_call(
         functools.partial(place_kernel, plan),
         out_shape=jax.ShapeDtypeStruct(shape, jnp.bfloat16),
         in_specs=[pl.BlockSpec(memory_space=pltpu.SMEM)]
-        + [pl.BlockSpec(memory_space=pl.ANY)] * len(operands),
+        + [pl.BlockSpec(memory_space=pl.ANY)] * len(pieces),
         out_specs=pl.BlockSpec(memory_space=pl.ANY),
         scratch_shapes=[pltpu.SemaphoreType.DMA((len(pieces),))],
-        input_output_aliases={} if update is None else {1: 0},
         compiler_params=pltpu.CompilerParams(vmem_limit_bytes=1024 * 1024),
-    )(place, *operands)
+    )(place, *pieces)
 
 
 def call(kernel, out_shapes, scratch_shapes, *operands):
@@ -296,14 +296,6 @@
 
     ring = list(range(0, bands, 2)) + list(range(bands - 1, 0, -2))
 
-    def shift(array, distance):
-        pairs = [
-            (ring[k] * cores + c, ring[(k + distance) % bands] * cores + c)
-            for k in range(bands)
-            for c in range(cores)
-        ]
-        return lax.ppermute(array, "dp", pairs)
-
     def swap_core(array):
         return lax.ppermute(array, "dp", [(g, g ^ 1) for g in range(groups)])
 
@@ -332,24 +324,25 @@
         jnp.stack([plane * (tokens // 2), band] + bands_out).astype(jnp.int32),
         inputs,
     )
+    def exchange(array, offset):
+        pairs = [
+            (k * cores + c, (k ^ offset) * cores + c) for k in range(bands) for c in range(cores)
+        ]
+        return lax.ppermute(array, "dp", pairs)
+
     outputs = jnp.dot(inputs, weight, preferred_element_type=jnp.float32).astype(jnp.bfloat16)
-    near = [deal(piece, hop) for hop, piece in zip(hops, packed)]
-    cots = [cotangent] + [None] * (bands - 1)
-    for step in range(1, bands // 2 + 1):
-        behind, further = cots[step - 1], cots[(bands - step + 1) % bands]
-        if step == 3:
-            behind, further, near[0], outputs = lax.optimization_barrier(
-                (behind, further, near[0], outputs)
-            )
-        cots[step] = shift(behind, 1)
-        if step < bands // 2:
-            cots[bands - step] = shift(further, -1)
+    far_cot, outputs, packed = lax.optimization_barrier((exchange(cotangent, 4), outputs, packed))
+    pair = jnp.concatenate([cotangent, far_cot])
+    near = [deal(packed[0], 0), deal(packed[1], 1)]
+    next_pair, packed = lax.optimization_barrier((exchange(pair, 2), packed))
+    cots = [pair, exchange(pair, 1), next_pair, exchange(next_pair, 1)]
+    near += [deal(packed[2], 2), deal(packed[3], 3)]
     far = [swap_plane(piece) for piece in near]
     (partial_tile,) = call(
         tile_kernel,
         [jax.ShapeDtypeStruct((BLOCK, BLOCK), jnp.float32)],
         [pltpu.VMEM((bands * tokens, BLOCK), inputs.dtype)] * 2,
-        jnp.stack([plane, band, spot]).astype(jnp.int32),
+        jnp.stack([plane, band]).astype(jnp.int32),
         own_band,
         *near,
         *far,
@@ -392,32 +385,29 @@
         return lax.ppermute(array, "dp", pairs)
 
     half_way = bands // 2
-    crossed, first_turn = lax.optimization_barrier((swap_plane(far_piece), turn(near_piece)))
+    near_turned, crossed = lax.optimization_barrier((turn(near_piece), swap_plane(far_piece)))
     other_crossed = swap_core(crossed)
-    far_head = jnp.where(
-        core == 0,
-        jnp.concatenate([crossed, other_crossed]),
-        jnp.concatenate([other_crossed, crossed]),
-    )
-    heads = [near_piece, far_head]
-    plan, pieces = [(0, 0, False, False), (0, 1, False, False)], list(heads)
-    place = jnp.stack([core, plane, spot]).astype(jnp.int32)
-    shape = (bands, rows, CB * BLOCK)
-    update = None
+    heads = [near_piece, crossed, other_crossed]
+    parts = [WHOLE, MINE, OTHERS]
+    plan = [(0, min(k, 1), False, parts[k]) for k in range(3)]
+    pieces = list(heads)
     for hop in range(1, half_way + 1):
-        half = hop == half_way
-        for chunk in range(2):
-            head = heads[chunk]
-            if half:
-                head = lax.dynamic_slice_in_dim(head.reshape(2, -1, BLOCK), core, 1, 0)[0]
-            heads[chunk] = first_turn if (hop, chunk) == (1, 0) else turn(head)
-            pieces += [heads[chunk], swap_core(heads[chunk])]
-            plan += [(hop, chunk, False, half), (hop, chunk, True, half)]
-        if hop == half_way - 1:
-            update = put_pieces(plan[:-4], shape, place, pieces[:-4])
-            update, *heads = lax.optimization_barrier((update, *heads))
-            plan, pieces = plan[-4:], pieces[-4:]
-    update = put_pieces(plan, shape, place, pieces, update)
+        for k, part in enumerate(parts):
+            chunk = min(k, 1)
+            if hop == half_way and part == OTHERS:
+                continue
+            if hop == half_way and part == WHOLE:
+                heads[k] = lax.dynamic_slice_in_dim(heads[k].reshape(2, -1, BLOCK), core, 1, 0)[0]
+                part = MINE
+            heads[k] = near_turned if (hop, k) == (1, 0) else turn(heads[k])
+            pieces += [heads[k], swap_core(heads[k])]
+            plan += [(hop, chunk, False, part), (hop, chunk, True, -part)]
+    update = put_pieces(
+        plan,
+        (bands, rows, CB * BLOCK),
+        jnp.stack([core, plane, spot]).astype(jnp.int32),
+        pieces,
+    )
     return (outputs, update)
 
 

time: 86.3 us -> 108 us (1.25)
  Pallas kernels: 11.5 us -> 29.4 us
  waiting for transfers between devices: 32.2 us -> 36.2 us
  local copies, waits for them, and re-layouts: 1.34 us -> 0.12 us
    pallas_call x2 -> x1, Pallas kernels: 3.87 us -> 21.8 us  [put_pieces(): pl.pallas_call(functools.partial(place_kernel, plan), out_shape=jax.Shape...]
    ppermute x8 -> x11, starting transfers between devices: 11.1 us -> 17.1 us  [turn(): return lax.ppermute(array, 'dp', pairs)]
    ppermute x4, waiting for transfers between devices: 2.35 us -> 8.3 us  [deal(): return lax.ppermute(array, ('dp', 'pre'), pairs)]
    ppermute x7 -> x4, starting transfers between devices: 11.9 us -> 5.96 us  [exchange(): return lax.ppermute(array, 'dp', pairs)]
    ppermute x8 -> x11, waiting for transfers between devices: 13.8 us -> 10.9 us  [turn(): return lax.ppermute(array, 'dp', pairs)]
    ppermute x4, starting transfers between devices: 5.99 us -> 7.98 us  [deal(): return lax.ppermute(array, ('dp', 'pre'), pairs)]
    ppermute x5, starting transfers between devices: 6.71 us -> 4.86 us  [swap_plane(): lax.ppermute(array, 'pre', [(c, members - 1 - c) for c in range(members)])]
    ppermute x5, waiting for transfers between devices: 7.72 us -> 9.16 us  [swap_plane(): lax.ppermute(array, 'pre', [(c, members - 1 - c) for c in range(members)])]
  transfers between devices with their start and end apart: 35 -> 38, of which waited for: 18 -> 16; matrix products, arithmetic and copies ran while one was open for 5% -> 4% of each run, Pallas kernels for 3% -> 1%
where the time goes in v4:
time: 108 us; the launch traced here: 107 us
  starting transfers between devices  36.8 us (34%)
  waiting for transfers between devices  36.2 us (34%)
  Pallas kernels  29.4 us (27%)
  matrix products  3.89 us (4%)
    pallas_call x1, Pallas kernels, put_pieces(): pl.pallas_call(functools.partial(place_kernel, plan), out_shape=jax.Shape...  21.8 us
    ppermute x11, starting transfers between devices, turn(): return lax.ppermute(array, 'dp', pairs)  17.1 us
    ppermute x11, waiting for transfers between devices, turn(): return lax.ppermute(array, 'dp', pairs)  10.9 us
    ppermute x5, waiting for transfers between devices, swap_plane(): lax.ppermute(array, 'pre', [(c, members - 1 - c) for c in range(members)])  9.16 us
    ppermute x4, waiting for transfers between devices, deal(): return lax.ppermute(array, ('dp', 'pre'), pairs)  8.3 us
    ppermute x4, starting transfers between devices, deal(): return lax.ppermute(array, ('dp', 'pre'), pairs)  7.98 us
    pallas_call x4, Pallas kernels, call(): pl.pallas_call(kernel, out_shape=out_shapes, in_specs=in_specs, out_specs...  7.62 us
    ppermute x4, starting transfers between devices, exchange(): return lax.ppermute(array, 'dp', pairs)  5.96 us
  transfers between devices with their start and end apart: 38, of which 16 were waited for; matrix products, arithmetic and copies ran while one was open for 4% of the time, Pallas kernels for 1%

profile of v4, /device:TPU:0, one launch (start us, length us, event | category | flops | bytes accessed | tf_op | source)
XLA Modules:
  0.0 107.4 jit_solution(9974382341335208677)
XLA Ops:
  0.6 4.1 %collective-permute-start = (bf16[128,512]{1,0:T(8,128)(2,1)}, bf16[128,512]{1,0:T(8,128)(2,1)S(1)}, u32[]{:S(2)}, u32[]{:S(2)}) collective-permute-start(bf16[128,512]{1,0:T(8,128)(2,1)} %param.5), channel_id=1, source_target_pairs={{0,16},{2,18},{4,20},{6,22},{8,24},{10,26},{12,28},{14,30},{16,0},... | collective-permute-start | bytes 393224 | tf_op jit(solution)/shard_map/ppermute | solution.py:331
  4.8 3.9 %convolution_convert_fusion = bf16[128,512]{1,0:T(8,128)(2,1)} fusion(bf16[128,4096]{1,0:T(8,128)(2,1)} %inputs_ref.1, bf16[4096,512]{1,0:T(8,128)(2,1)} %param.4), kind=kOutput, calls=%fused_computation | convolution fusion | flops 536936448 | bytes 5373952 | tf_op jit(solution)/shard_map/dot_general | solution.py:333
  8.6 0.1 stack.49.place_ref
  8.7 0.6 shard_map.50
  9.3 1.9 %collective-permute-done = bf16[128,512]{1,0:T(8,128)(2,1)S(1)} collective-permute-done((bf16[128,512]{1,0:T(8,128)(2,1)}, bf16[128,512]{1,0:T(8,128)(2,1)S(1)}, u32[]{:S(2)}, u32[]{:S(2)}) %collective-permute-start) | collective-permute-done | bytes 131104 | tf_op jit(solution)/shard_map/ppermute | solution.py:331
  11.3 0.9 collective-permute-start.3
  12.2 3.3 %collective-permute-start.1 = (bf16[128,512]{1,0:T(8,128)(2,1)S(1)}, bf16[128,512]{1,0:T(8,128)(2,1)S(1)}, u32[]{:S(2)}, u32[]{:S(2)}) collective-permute-start(bf16[128,512]{1,0:T(8,128)(2,1)S(1)} %get-tuple-element.28), channel_id=1, source_target_pairs={{0,16},{1,21},{2,18},{3,23},{4,20},{5,17},{6,22},{7,19},{8,24},{9,... | collective-permute-start | bytes 393224 | tf_op jit(solution)/shard_map/ppermute | solution.py:315
  15.4 1.3 %collective-permute-start.2 = (bf16[128,512]{1,0:T(8,128)(2,1)S(1)}, bf16[128,512]{1,0:T(8,128)(2,1)S(1)}, u32[]{:S(2)}, u32[]{:S(2)}) collective-permute-start(bf16[128,512]{1,0:T(8,128)(2,1)S(1)} %get-tuple-element.29), channel_id=1, source_target_pairs={{0,28},{1,25},{2,30},{3,27},{4,24},{5,29},{6,26},{7,31},{8,20},{9,... | collective-permute-start | bytes 393224 | tf_op jit(solution)/shard_map/ppermute | solution.py:315
  16.7 0.5 collective-permute-start.10
  17.2 4.5 %collective-permute-done.1.refs_0_ = bf16[128,512]{1,0:T(8,128)(2,1)S(1)} collective-permute-done((bf16[128,512]{1,0:T(8,128)(2,1)S(1)}, bf16[128,512]{1,0:T(8,128)(2,1)S(1)}, u32[]{:S(2)}, u32[]{:S(2)}) %collective-permute-start.1) | collective-permute-done | bytes 131104 | tf_op jit(solution)/shard_map/ppermute | solution.py:315
  21.7 1.5 %collective-permute-start.6 = (bf16[128,512]{1,0:T(8,128)(2,1)S(1)}, bf16[128,512]{1,0:T(8,128)(2,1)S(1)}, u32[]{:S(2)}, u32[]{:S(2)}) collective-permute-start(bf16[128,512]{1,0:T(8,128)(2,1)S(1)} %collective-permute-done.1.refs_0_), channel_id=1, source_target_pairs={{0,1},{1,0},{2,3},{3,2},{4,5},{5,4},{6,7},{7,6},{8,9},{9,8},{10,11... | collective-permute-start | bytes 393224 | tf_op jit(solution)/shard_map/ppermute | solution.py:303
  23.2 1.5 %collective-permute-start.4 = (bf16[128,512]{1,0:T(8,128)(2,1)S(1)}, bf16[128,512]{1,0:T(8,128)(2,1)S(1)}, u32[]{:S(2)}, u32[]{:S(2)}) collective-permute-start(bf16[128,512]{1,0:T(8,128)(2,1)S(1)} %get-tuple-element.33), channel_id=1, source_target_pairs={{0,4},{1,13},{2,6},{3,15},{4,0},{5,9},{6,2},{7,11},{8,12},{9,5},{1... | collective-permute-start | bytes 393224 | tf_op jit(solution)/shard_map/ppermute | solution.py:315
  24.7 0.5 collective-permute-start.11
  25.2 2.8 %collective-permute-done.2.refs_1_ = bf16[128,512]{1,0:T(8,128)(2,1)S(1)} collective-permute-done((bf16[128,512]{1,0:T(8,128)(2,1)S(1)}, bf16[128,512]{1,0:T(8,128)(2,1)S(1)}, u32[]{:S(2)}, u32[]{:S(2)}) %collective-permute-start.2) | collective-permute-done | bytes 131104 | tf_op jit(solution)/shard_map/ppermute | solution.py:315
  28.1 1.9 %collective-permute-start.5 = (bf16[64,512]{1,0:T(8,128)(2,1)S(1)}, bf16[64,512]{1,0:T(8,128)(2,1)S(1)}, u32[]{:S(2)}, u32[]{:S(2)}) collective-permute-start(bf16[64,512]{1,0:T(8,128)(2,1)S(1)} %get-tuple-element.34), channel_id=1, source_target_pairs={{0,8},{1,9},{2,10},{3,11},{4,12},{5,13},{6,14},{7,15},{8,0},{9,1},... | collective-permute-start | bytes 196616 | tf_op jit(solution)/shard_map/ppermute | solution.py:315
  30.0 1.0 collective-permute-done.4.refs_2_
  30.9 1.9 %collective-permute-start.8 = (bf16[128,512]{1,0:T(8,128)(2,1)S(1)}, bf16[128,512]{1,0:T(8,128)(2,1)S(1)}, u32[]{:S(2)}, u32[]{:S(2)}) collective-permute-start(bf16[128,512]{1,0:T(8,128)(2,1)S(1)} %collective-permute-done.4.refs_2_), channel_id=1, source_target_pairs={{0,1},{1,0},{2,3},{3,2},{4,5},{5,4},{6,7},{7,6},{8,9},{9,8},{10,11... | collective-permute-start | bytes 393224 | tf_op jit(solution)/shard_map/ppermute | solution.py:303
  32.8 0.8 collective-permute-start.9
  33.7 2.5 %collective-permute-done.7.refs_5_ = bf16[128,512]{1,0:T(8,128)(2,1)S(1)} collective-permute-done((bf16[128,512]{1,0:T(8,128)(2,1)S(1)}, bf16[128,512]{1,0:T(8,128)(2,1)S(1)}, u32[]{:S(2)}, u32[]{:S(2)}) %collective-permute-start.7) | collective-permute-done | bytes 131104 | tf_op jit(solution)/shard_map/ppermute | solution.py:303
  36.3 2.3 %collective-permute-done.9.refs_7_ = bf16[64,512]{1,0:T(8,128)(2,1)S(1)} collective-permute-done((bf16[64,512]{1,0:T(8,128)(2,1)S(1)}, bf16[64,512]{1,0:T(8,128)(2,1)S(1)}, u32[]{:S(2)}, u32[]{:S(2)}) %collective-permute-start.9) | collective-permute-done | bytes 65568 | tf_op jit(solution)/shard_map/ppermute | solution.py:303
  38.6 1.4 %shard_map.51.mine_ref = f32[512,512]{1,0:T(8,128)S(1)} custom-call(s32[2]{0:T(128)S(1)} %pad_add_fusion.2.place_ref, bf16[128,512]{1,0:T(8,128)(2,1)S(1)} %get-tuple-element.27.own_ref, bf16[128,512]{1,0:T(8,128)(2,1)S(1)} %collective-permute-done.1.refs_0_, bf16[128,512]{1,0:T(8,128)(2,1)S(1)} %collective-permute-done.2.refs_1_, ...), custom_call_target="tpu_custom_call" | custom-call | tf_op jit(solution)/shard_map/pallas_call | solution.py:276
  40.1 0.1 pad_add_fusion.1.side_ref
  40.1 2.6 %collective-permute-done.12.other_ref = f32[512,512]{1,0:T(8,128)S(1)} collective-permute-done((f32[512,512]{1,0:T(8,128)S(1)}, f32[512,512]{1,0:T(8,128)S(1)}, u32[]{:S(2)}, u32[]{:S(2)}) %collective-permute-start.12) | collective-permute-done | bytes 1048608 | tf_op jit(solution)/shard_map/ppermute | solution.py:300
  42.7 4.3 %shard_map.52 = (bf16[512,512]{1,0:T(8,128)(2,1)S(1)}, bf16[512,512]{1,0:T(8,128)(2,1)S(1)}) custom-call(s32[2]{0:T(128)S(1)} %pad_add_fusion.1.side_ref, f32[512,512]{1,0:T(8,128)S(1)} %shard_map.51.mine_ref, f32[512,512]{1,0:T(8,128)S(1)} %collective-permute-done.12.other_ref), custom_call_target="tpu_custom_call" | custom-call | tf_op jit(solution)/shard_map/pallas_call | solution.py:276
  47.0 0.3 collective-permute-start.13
  47.2 1.7 %collective-permute-done.13.other_ref = bf16[512,512]{1,0:T(8,128)(2,1)S(1)} collective-permute-done((bf16[512,512]{1,0:T(8,128)(2,1)S(1)}, bf16[512,512]{1,0:T(8,128)(2,1)S(1)}, u32[]{:S(2)}, u32[]{:S(2)}) %collective-permute-start.13) | collective-permute-done | bytes 524320 | tf_op jit(solution)/shard_map/ppermute | solution.py:300
  49.0 1.3 %shard_map.53 = (bf16[256,512]{1,0:T(8,128)(2,1)S(1)}, bf16[128,512]{1,0:T(8,128)(2,1)S(1)}) custom-call(s32[2]{0:T(128)S(1)} %pad_add_fusion.1.side_ref, bf16[512,512]{1,0:T(8,128)(2,1)S(1)} %get-tuple-element.36.mine_ref, bf16[512,512]{1,0:T(8,128)(2,1)S(1)} %collective-permute-done.13.other_ref, bf16[512,512]{1,0:T(8,128)(2,1)S(1)} %get-tuple-element.37.tile_ref), custom_call_target="tpu_custom_call" | custom-call | tf_op jit(solution)/shard_map/pallas_call | solution.py:276
  50.3 1.5 %collective-permute-start.14 = (bf16[256,512]{1,0:T(8,128)(2,1)S(1)}, bf16[256,512]{1,0:T(8,128)(2,1)S(1)}, u32[]{:S(2)}, u32[]{:S(2)}) collective-permute-start(bf16[256,512]{1,0:T(8,128)(2,1)S(1)} %get-tuple-element.38.refs_0_), channel_id=1, source_target_pairs={{0,8},{2,6},{8,16},{10,2},{16,24},{18,10},{24,28},{26,18},{28,20},... | collective-permute-start | bytes 786440 | tf_op jit(solution)/shard_map/ppermute | solution.py:385
  51.8 0.6 collective-permute-start.15
  52.5 4.3 %collective-permute-done.15.refs_1_ = bf16[128,512]{1,0:T(8,128)(2,1)S(1)} collective-permute-done((bf16[128,512]{1,0:T(8,128)(2,1)S(1)}, bf16[128,512]{1,0:T(8,128)(2,1)S(1)}, u32[]{:S(2)}, u32[]{:S(2)}) %collective-permute-start.15) | collective-permute-done | bytes 131104 | tf_op jit(solution)/shard_map/ppermute | solution.py:303
  56.8 1.4 %collective-permute-start.22 = (bf16[256,512]{1,0:T(8,128)(2,1)S(1)}, bf16[256,512]{1,0:T(8,128)(2,1)S(1)}, u32[]{:S(2)}, u32[]{:S(2)}) collective-permute-start(bf16[256,512]{1,0:T(8,128)(2,1)S(1)} %collective-permute-done.14.refs_3_), channel_id=1, source_target_pairs={{0,8},{2,6},{8,16},{10,2},{16,24},{18,10},{24,28},{26,18},{28,20},... | collective-permute-start | bytes 786440 | tf_op jit(solution)/shard_map/ppermute | solution.py:385
  58.2 1.4 %collective-permute-start.18 = (bf16[128,512]{1,0:T(8,128)(2,1)S(1)}, bf16[128,512]{1,0:T(8,128)(2,1)S(1)}, u32[]{:S(2)}, u32[]{:S(2)}) collective-permute-start(bf16[128,512]{1,0:T(8,128)(2,1)S(1)} %collective-permute-done.15.refs_1_), channel_id=1, source_target_pairs={{0,8},{2,6},{8,16},{10,2},{16,24},{18,10},{24,28},{26,18},{28,20},... | collective-permute-start | bytes 393224 | tf_op jit(solution)/shard_map/ppermute | solution.py:385
  59.6 3.5 %collective-permute-done.22.refs_9_ = bf16[256,512]{1,0:T(8,128)(2,1)S(1)} collective-permute-done((bf16[256,512]{1,0:T(8,128)(2,1)S(1)}, bf16[256,512]{1,0:T(8,128)(2,1)S(1)}, u32[]{:S(2)}, u32[]{:S(2)}) %collective-permute-start.22) | collective-permute-done | bytes 262176 | tf_op jit(solution)/shard_map/ppermute | solution.py:385
  63.2 1.4 %collective-permute-start.28 = (bf16[256,512]{1,0:T(8,128)(2,1)S(1)}, bf16[256,512]{1,0:T(8,128)(2,1)S(1)}, u32[]{:S(2)}, u32[]{:S(2)}) collective-permute-start(bf16[256,512]{1,0:T(8,128)(2,1)S(1)} %collective-permute-done.22.refs_9_), channel_id=1, source_target_pairs={{0,8},{2,6},{8,16},{10,2},{16,24},{18,10},{24,28},{26,18},{28,20},... | collective-permute-start | bytes 786440 | tf_op jit(solution)/shard_map/ppermute | solution.py:385
  64.6 1.4 %collective-permute-start.24 = (bf16[128,512]{1,0:T(8,128)(2,1)S(1)}, bf16[128,512]{1,0:T(8,128)(2,1)S(1)}, u32[]{:S(2)}, u32[]{:S(2)}) collective-permute-start(bf16[128,512]{1,0:T(8,128)(2,1)S(1)} %collective-permute-done.18.refs_5_), channel_id=1, source_target_pairs={{0,8},{2,6},{8,16},{10,2},{16,24},{18,10},{24,28},{26,18},{28,20},... | collective-permute-start | bytes 393224 | tf_op jit(solution)/shard_map/ppermute | solution.py:385
  66.0 2.1 %collective-permute-start.20 = (bf16[128,512]{1,0:T(8,128)(2,1)S(1)}, bf16[128,512]{1,0:T(8,128)(2,1)S(1)}, u32[]{:S(2)}, u32[]{:S(2)}) collective-permute-start(bf16[128,512]{1,0:T(8,128)(2,1)S(1)} %collective-permute-done.16.refs_2_), channel_id=1, source_target_pairs={{0,8},{2,6},{8,16},{10,2},{16,24},{18,10},{24,28},{26,18},{28,20},... | collective-permute-start | bytes 393224 | tf_op jit(solution)/shard_map/ppermute | solution.py:385
  68.1 2.8 %collective-permute-done.24.refs_11_ = bf16[128,512]{1,0:T(8,128)(2,1)S(1)} collective-permute-done((bf16[128,512]{1,0:T(8,128)(2,1)S(1)}, bf16[128,512]{1,0:T(8,128)(2,1)S(1)}, u32[]{:S(2)}, u32[]{:S(2)}) %collective-permute-start.24) | collective-permute-done | bytes 131104 | tf_op jit(solution)/shard_map/ppermute | solution.py:385
  71.0 1.4 %collective-permute-start.30 = (bf16[128,512]{1,0:T(8,128)(2,1)S(1)}, bf16[128,512]{1,0:T(8,128)(2,1)S(1)}, u32[]{:S(2)}, u32[]{:S(2)}) collective-permute-start(bf16[128,512]{1,0:T(8,128)(2,1)S(1)} %collective-permute-done.24.refs_11_), channel_id=1, source_target_pairs={{0,8},{2,6},{8,16},{10,2},{16,24},{18,10},{24,28},{26,18},{28,20},... | collective-permute-start | bytes 393224 | tf_op jit(solution)/shard_map/ppermute | solution.py:385
  72.4 1.5 %collective-permute-start.26 = (bf16[128,512]{1,0:T(8,128)(2,1)S(1)}, bf16[128,512]{1,0:T(8,128)(2,1)S(1)}, u32[]{:S(2)}, u32[]{:S(2)}) collective-permute-start(bf16[128,512]{1,0:T(8,128)(2,1)S(1)} %collective-permute-done.20.refs_7_), channel_id=1, source_target_pairs={{0,8},{2,6},{8,16},{10,2},{16,24},{18,10},{24,28},{26,18},{28,20},... | collective-permute-start | bytes 393224 | tf_op jit(solution)/shard_map/ppermute | solution.py:385
  73.9 2.1 %collective-permute-done.30.refs_17_ = bf16[128,512]{1,0:T(8,128)(2,1)S(1)} collective-permute-done((bf16[128,512]{1,0:T(8,128)(2,1)S(1)}, bf16[128,512]{1,0:T(8,128)(2,1)S(1)}, u32[]{:S(2)}, u32[]{:S(2)}) %collective-permute-start.30) | collective-permute-done | bytes 131104 | tf_op jit(solution)/shard_map/ppermute | solution.py:385
  75.9 1.4 %collective-permute-start.36 = (bf16[128,512]{1,0:T(8,128)(2,1)S(1)}, bf16[128,512]{1,0:T(8,128)(2,1)S(1)}, u32[]{:S(2)}, u32[]{:S(2)}) collective-permute-start(bf16[128,512]{1,0:T(8,128)(2,1)S(1)} %collective-permute-done.30.refs_17_), channel_id=1, source_target_pairs={{0,8},{2,6},{8,16},{10,2},{16,24},{18,10},{24,28},{26,18},{28,20},... | collective-permute-start | bytes 393224 | tf_op jit(solution)/shard_map/ppermute | solution.py:385
  77.4 1.4 %collective-permute-start.32 = (bf16[128,512]{1,0:T(8,128)(2,1)S(1)}, bf16[128,512]{1,0:T(8,128)(2,1)S(1)}, u32[]{:S(2)}, u32[]{:S(2)}) collective-permute-start(bf16[128,512]{1,0:T(8,128)(2,1)S(1)} %collective-permute-done.26.refs_13_), channel_id=1, source_target_pairs={{0,8},{2,6},{8,16},{10,2},{16,24},{18,10},{24,28},{26,18},{28,20},... | collective-permute-start | bytes 393224 | tf_op jit(solution)/shard_map/ppermute | solution.py:385
  78.8 2.1 %collective-permute-start.34 = (bf16[128,512]{1,0:T(8,128)(2,1)S(1)}, bf16[128,512]{1,0:T(8,128)(2,1)}, u32[]{:S(2)}, u32[]{:S(2)}) collective-permute-start(bf16[128,512]{1,0:T(8,128)(2,1)S(1)} %dynamic-slice_bitcast_fusion), channel_id=1, source_target_pairs={{0,8},{2,6},{8,16},{10,2},{16,24},{18,10},{24,28},{26,18},{28,20},... | collective-permute-start | bytes 393224 | tf_op jit(solution)/shard_map/ppermute | solution.py:385
  80.9 0.5 collective-permute-start.27
  81.5 0.9 collective-permute-done.32.refs_19_
  82.4 1.5 %collective-permute-done.34.refs_21_ = bf16[128,512]{1,0:T(8,128)(2,1)} collective-permute-done((bf16[128,512]{1,0:T(8,128)(2,1)S(1)}, bf16[128,512]{1,0:T(8,128)(2,1)}, u32[]{:S(2)}, u32[]{:S(2)}) %collective-permute-start.34) | collective-permute-done | bytes 131104 | tf_op jit(solution)/shard_map/ppermute | solution.py:385
  84.0 1.6 %collective-permute-done.35.refs_22_ = bf16[128,512]{1,0:T(8,128)(2,1)} collective-permute-done((bf16[128,512]{1,0:T(8,128)(2,1)}, bf16[128,512]{1,0:T(8,128)(2,1)}, u32[]{:S(2)}, u32[]{:S(2)}) %collective-permute-start.35) | collective-permute-done | bytes 131104 | tf_op jit(solution)/shard_map/ppermute | solution.py:300
  85.6 21.8 %shard_map.54 = bf16[8,256,1024]{2,1,0:T(8,128)(2,1)} custom-call(s32[3]{0:T(128)S(1)} %pad_add_fusion.place_ref, bf16[256,512]{1,0:T(8,128)(2,1)S(1)} %get-tuple-element.38.refs_0_, bf16[128,512]{1,0:T(8,128)(2,1)S(1)} %collective-permute-done.15.refs_1_, bf16[128,512]{1,0:T(8,128)(2,1)S(1)} %collective-permute-done.16.refs_2_, ...), custom_call_target="tpu_custom_call" | custom-call | tf_op jit(solution)/shard_map/pallas_call | solution.py:262
  (45 shorter events, 0.5 us)
Async XLA Ops:
  0.6 8.7 %copy-start.1 = (bf16[128,512]{1,0:T(8,128)(2,1)S(1)}, bf16[128,512]{1,0:T(8,128)(2,1)}, u32[]{:S(2)}) copy-start(bf16[128,512]{1,0:T(8,128)(2,1)} %param.5) | copy-start | bytes 393220
  0.6 8.1 %copy-start = (bf16[128,4096]{1,0:T(8,128)(2,1)S(1)}, bf16[128,4096]{1,0:T(8,128)(2,1)}, u32[]{:S(2)}) copy-start(bf16[128,4096]{1,0:T(8,128)(2,1)} %inputs_ref.1) | copy-start | bytes 3145732
  0.6 10.6 %collective-permute-start = (bf16[128,512]{1,0:T(8,128)(2,1)}, bf16[128,512]{1,0:T(8,128)(2,1)S(1)}, u32[]{:S(2)}, u32[]{:S(2)}) collective-permute-start(bf16[128,512]{1,0:T(8,128)(2,1)} %param.5), channel_id=1, source_target_pairs={{0,16},{2,18},{4,20},{6,22},{8,24},{10,26},{12,28},{14,30},{16,0},... | collective-permute-start | bytes 393224 | tf_op jit(solution)/shard_map/ppermute | solution.py:331
  11.3 11.9 %collective-permute-start.3 = (bf16[256,512]{1,0:T(8,128)(2,1)S(1)}, bf16[256,512]{1,0:T(8,128)(2,1)S(1)}, u32[]{:S(2)}, u32[]{:S(2)}) collective-permute-start(bf16[256,512]{1,0:T(8,128)(2,1)S(1)} %constant_dynamic-update-slice_fusion.refs_8_), channel_id=1, source_target_pairs={{0,8},{2,10},{4,12},{6,14},{8,0},{10,2},{12,4},{14,6},{16,24},{18,... | collective-permute-start | bytes 786440 | tf_op jit(solution)/shard_map/ppermute | solution.py:331
  12.2 9.5 %collective-permute-start.1 = (bf16[128,512]{1,0:T(8,128)(2,1)S(1)}, bf16[128,512]{1,0:T(8,128)(2,1)S(1)}, u32[]{:S(2)}, u32[]{:S(2)}) collective-permute-start(bf16[128,512]{1,0:T(8,128)(2,1)S(1)} %get-tuple-element.28), channel_id=1, source_target_pairs={{0,16},{1,21},{2,18},{3,23},{4,20},{5,17},{6,22},{7,19},{8,24},{9,... | collective-permute-start | bytes 393224 | tf_op jit(solution)/shard_map/ppermute | solution.py:315
  15.4 12.6 %collective-permute-start.2 = (bf16[128,512]{1,0:T(8,128)(2,1)S(1)}, bf16[128,512]{1,0:T(8,128)(2,1)S(1)}, u32[]{:S(2)}, u32[]{:S(2)}) collective-permute-start(bf16[128,512]{1,0:T(8,128)(2,1)S(1)} %get-tuple-element.29), channel_id=1, source_target_pairs={{0,28},{1,25},{2,30},{3,27},{4,24},{5,29},{6,26},{7,31},{8,20},{9,... | collective-permute-start | bytes 393224 | tf_op jit(solution)/shard_map/ppermute | solution.py:315
  16.7 19.5 %collective-permute-start.10 = (bf16[256,512]{1,0:T(8,128)(2,1)S(1)}, bf16[256,512]{1,0:T(8,128)(2,1)S(1)}, u32[]{:S(2)}, u32[]{:S(2)}) collective-permute-start(bf16[256,512]{1,0:T(8,128)(2,1)S(1)} %constant_dynamic-update-slice_fusion.refs_8_), channel_id=1, source_target_pairs={{0,4},{2,6},{4,0},{6,2},{8,12},{10,14},{12,8},{14,10},{16,20},{18,... | collective-permute-start | bytes 786440 | tf_op jit(solution)/shard_map/ppermute | solution.py:331
  21.7 8.2 %collective-permute-start.6 = (bf16[128,512]{1,0:T(8,128)(2,1)S(1)}, bf16[128,512]{1,0:T(8,128)(2,1)S(1)}, u32[]{:S(2)}, u32[]{:S(2)}) collective-permute-start(bf16[128,512]{1,0:T(8,128)(2,1)S(1)} %collective-permute-done.1.refs_0_), channel_id=1, source_target_pairs={{0,1},{1,0},{2,3},{3,2},{4,5},{5,4},{6,7},{7,6},{8,9},{9,8},{10,11... | collective-permute-start | bytes 393224 | tf_op jit(solution)/shard_map/ppermute | solution.py:303
  23.2 7.7 %collective-permute-start.4 = (bf16[128,512]{1,0:T(8,128)(2,1)S(1)}, bf16[128,512]{1,0:T(8,128)(2,1)S(1)}, u32[]{:S(2)}, u32[]{:S(2)}) collective-permute-start(bf16[128,512]{1,0:T(8,128)(2,1)S(1)} %get-tuple-element.33), channel_id=1, source_target_pairs={{0,4},{1,13},{2,6},{3,15},{4,0},{5,9},{6,2},{7,11},{8,12},{9,5},{1... | collective-permute-start | bytes 393224 | tf_op jit(solution)/shard_map/ppermute | solution.py:315
  24.7 13.8 %collective-permute-start.11 = (bf16[256,512]{1,0:T(8,128)(2,1)S(1)}, bf16[256,512]{1,0:T(8,128)(2,1)S(1)}, u32[]{:S(2)}, u32[]{:S(2)}) collective-permute-start(bf16[256,512]{1,0:T(8,128)(2,1)S(1)} %collective-permute-done.3.refs_10_), channel_id=1, source_target_pairs={{0,4},{2,6},{4,0},{6,2},{8,12},{10,14},{12,8},{14,10},{16,20},{18,... | collective-permute-start | bytes 786440 | tf_op jit(solution)/shard_map/ppermute | solution.py:331
  28.1 4.8 %collective-permute-start.5 = (bf16[64,512]{1,0:T(8,128)(2,1)S(1)}, bf16[64,512]{1,0:T(8,128)(2,1)S(1)}, u32[]{:S(2)}, u32[]{:S(2)}) collective-permute-start(bf16[64,512]{1,0:T(8,128)(2,1)S(1)} %get-tuple-element.34), channel_id=1, source_target_pairs={{0,8},{1,9},{2,10},{3,11},{4,12},{5,13},{6,14},{7,15},{8,0},{9,1},... | collective-permute-start | bytes 196616 | tf_op jit(solution)/shard_map/ppermute | solution.py:315
  30.0 6.3 %collective-permute-start.7 = (bf16[128,512]{1,0:T(8,128)(2,1)S(1)}, bf16[128,512]{1,0:T(8,128)(2,1)S(1)}, u32[]{:S(2)}, u32[]{:S(2)}) collective-permute-start(bf16[128,512]{1,0:T(8,128)(2,1)S(1)} %collective-permute-done.2.refs_1_), channel_id=1, source_target_pairs={{0,1},{1,0},{2,3},{3,2},{4,5},{5,4},{6,7},{7,6},{8,9},{9,8},{10,11... | collective-permute-start | bytes 393224 | tf_op jit(solution)/shard_map/ppermute | solution.py:303
  30.9 7.6 %collective-permute-start.8 = (bf16[128,512]{1,0:T(8,128)(2,1)S(1)}, bf16[128,512]{1,0:T(8,128)(2,1)S(1)}, u32[]{:S(2)}, u32[]{:S(2)}) collective-permute-start(bf16[128,512]{1,0:T(8,128)(2,1)S(1)} %collective-permute-done.4.refs_2_), channel_id=1, source_target_pairs={{0,1},{1,0},{2,3},{3,2},{4,5},{5,4},{6,7},{7,6},{8,9},{9,8},{10,11... | collective-permute-start | bytes 393224 | tf_op jit(solution)/shard_map/ppermute | solution.py:303
  32.8 5.7 %collective-permute-start.9 = (bf16[64,512]{1,0:T(8,128)(2,1)S(1)}, bf16[64,512]{1,0:T(8,128)(2,1)S(1)}, u32[]{:S(2)}, u32[]{:S(2)}) collective-permute-start(bf16[64,512]{1,0:T(8,128)(2,1)S(1)} %collective-permute-done.5.refs_3_), channel_id=1, source_target_pairs={{0,1},{1,0},{2,3},{3,2},{4,5},{5,4},{6,7},{7,6},{8,9},{9,8},{10,11... | collective-permute-start | bytes 196616 | tf_op jit(solution)/shard_map/ppermute | solution.py:303
  40.0 2.7 %collective-permute-start.12 = (f32[512,512]{1,0:T(8,128)S(1)}, f32[512,512]{1,0:T(8,128)S(1)}, u32[]{:S(2)}, u32[]{:S(2)}) collective-permute-start(f32[512,512]{1,0:T(8,128)S(1)} %shard_map.51.mine_ref), channel_id=1, source_target_pairs={{0,2},{2,0},{4,6},{6,4},{8,10},{10,8},{12,14},{14,12},{16,18},{18,... | collective-permute-start | bytes 3145736 | tf_op jit(solution)/shard_map/ppermute | solution.py:300
  47.0 2.0 %collective-permute-start.13 = (bf16[512,512]{1,0:T(8,128)(2,1)S(1)}, bf16[512,512]{1,0:T(8,128)(2,1)S(1)}, u32[]{:S(2)}, u32[]{:S(2)}) collective-permute-start(bf16[512,512]{1,0:T(8,128)(2,1)S(1)} %get-tuple-element.36.mine_ref), channel_id=1, source_target_pairs={{0,2},{2,0},{4,6},{6,4},{8,10},{10,8},{12,14},{14,12},{16,18},{18,... | collective-permute-start | bytes 1572872 | tf_op jit(solution)/shard_map/ppermute | solution.py:300
  50.3 6.5 %collective-permute-start.14 = (bf16[256,512]{1,0:T(8,128)(2,1)S(1)}, bf16[256,512]{1,0:T(8,128)(2,1)S(1)}, u32[]{:S(2)}, u32[]{:S(2)}) collective-permute-start(bf16[256,512]{1,0:T(8,128)(2,1)S(1)} %get-tuple-element.38.refs_0_), channel_id=1, source_target_pairs={{0,8},{2,6},{8,16},{10,2},{16,24},{18,10},{24,28},{26,18},{28,20},... | collective-permute-start | bytes 786440 | tf_op jit(solution)/shard_map/ppermute | solution.py:385
  51.8 5.0 %collective-permute-start.15 = (bf16[128,512]{1,0:T(8,128)(2,1)S(1)}, bf16[128,512]{1,0:T(8,128)(2,1)S(1)}, u32[]{:S(2)}, u32[]{:S(2)}) collective-permute-start(bf16[128,512]{1,0:T(8,128)(2,1)S(1)} %get-tuple-element.39), channel_id=1, source_target_pairs={{0,1},{1,0},{2,3},{3,2},{4,5},{5,4},{6,7},{7,6},{8,9},{9,8},{10,11... | collective-permute-start | bytes 393224 | tf_op jit(solution)/shard_map/ppermute | solution.py:303
  56.8 6.4 %collective-permute-start.22 = (bf16[256,512]{1,0:T(8,128)(2,1)S(1)}, bf16[256,512]{1,0:T(8,128)(2,1)S(1)}, u32[]{:S(2)}, u32[]{:S(2)}) collective-permute-start(bf16[256,512]{1,0:T(8,128)(2,1)S(1)} %collective-permute-done.14.refs_3_), channel_id=1, source_target_pairs={{0,8},{2,6},{8,16},{10,2},{16,24},{18,10},{24,28},{26,18},{28,20},... | collective-permute-start | bytes 786440 | tf_op jit(solution)/shard_map/ppermute | solution.py:385
  58.2 9.9 %collective-permute-start.17 = (bf16[256,512]{1,0:T(8,128)(2,1)S(1)}, bf16[256,512]{1,0:T(8,128)(2,1)S(1)}, u32[]{:S(2)}, u32[]{:S(2)}) collective-permute-start(bf16[256,512]{1,0:T(8,128)(2,1)S(1)} %collective-permute-done.14.refs_3_), channel_id=1, source_target_pairs={{0,2},{2,0},{4,6},{6,4},{8,10},{10,8},{12,14},{14,12},{16,18},{18,... | collective-permute-start | bytes 786440 | tf_op jit(solution)/shard_map/ppermute | solution.py:300
  58.2 6.4 %collective-permute-start.18 = (bf16[128,512]{1,0:T(8,128)(2,1)S(1)}, bf16[128,512]{1,0:T(8,128)(2,1)S(1)}, u32[]{:S(2)}, u32[]{:S(2)}) collective-permute-start(bf16[128,512]{1,0:T(8,128)(2,1)S(1)} %collective-permute-done.15.refs_1_), channel_id=1, source_target_pairs={{0,8},{2,6},{8,16},{10,2},{16,24},{18,10},{24,28},{26,18},{28,20},... | collective-permute-start | bytes 393224 | tf_op jit(solution)/shard_map/ppermute | solution.py:385
  59.6 6.4 %collective-permute-start.16 = (bf16[128,512]{1,0:T(8,128)(2,1)S(1)}, bf16[128,512]{1,0:T(8,128)(2,1)S(1)}, u32[]{:S(2)}, u32[]{:S(2)}) collective-permute-start(bf16[128,512]{1,0:T(8,128)(2,1)S(1)} %collective-permute-done.15.refs_1_), channel_id=1, source_target_pairs={{0,2},{2,0},{4,6},{6,4},{8,10},{10,8},{12,14},{14,12},{16,18},{18,... | collective-permute-start | bytes 393224 | tf_op jit(solution)/shard_map/ppermute | solution.py:300
  63.2 10.7 %collective-permute-start.28 = (bf16[256,512]{1,0:T(8,128)(2,1)S(1)}, bf16[256,512]{1,0:T(8,128)(2,1)S(1)}, u32[]{:S(2)}, u32[]{:S(2)}) collective-permute-start(bf16[256,512]{1,0:T(8,128)(2,1)S(1)} %collective-permute-done.22.refs_9_), channel_id=1, source_target_pairs={{0,8},{2,6},{8,16},{10,2},{16,24},{18,10},{24,28},{26,18},{28,20},... | collective-permute-start | bytes 786440 | tf_op jit(solution)/shard_map/ppermute | solution.py:385
  64.6 6.4 %collective-permute-start.24 = (bf16[128,512]{1,0:T(8,128)(2,1)S(1)}, bf16[128,512]{1,0:T(8,128)(2,1)S(1)}, u32[]{:S(2)}, u32[]{:S(2)}) collective-permute-start(bf16[128,512]{1,0:T(8,128)(2,1)S(1)} %collective-permute-done.18.refs_5_), channel_id=1, source_target_pairs={{0,8},{2,6},{8,16},{10,2},{16,24},{18,10},{24,28},{26,18},{28,20},... | collective-permute-start | bytes 393224 | tf_op jit(solution)/shard_map/ppermute | solution.py:385
  66.0 6.4 %collective-permute-start.19 = (bf16[128,512]{1,0:T(8,128)(2,1)S(1)}, bf16[128,512]{1,0:T(8,128)(2,1)S(1)}, u32[]{:S(2)}, u32[]{:S(2)}) collective-permute-start(bf16[128,512]{1,0:T(8,128)(2,1)S(1)} %collective-permute-done.18.refs_5_), channel_id=1, source_target_pairs={{0,2},{2,0},{4,6},{6,4},{8,10},{10,8},{12,14},{14,12},{16,18},{18,... | collective-permute-start | bytes 393224 | tf_op jit(solution)/shard_map/ppermute | solution.py:300
  66.0 6.4 %collective-permute-start.20 = (bf16[128,512]{1,0:T(8,128)(2,1)S(1)}, bf16[128,512]{1,0:T(8,128)(2,1)S(1)}, u32[]{:S(2)}, u32[]{:S(2)}) collective-permute-start(bf16[128,512]{1,0:T(8,128)(2,1)S(1)} %collective-permute-done.16.refs_2_), channel_id=1, source_target_pairs={{0,8},{2,6},{8,16},{10,2},{16,24},{18,10},{24,28},{26,18},{28,20},... | collective-permute-start | bytes 393224 | tf_op jit(solution)/shard_map/ppermute | solution.py:385
  68.1 12.8 %collective-permute-start.23 = (bf16[256,512]{1,0:T(8,128)(2,1)S(1)}, bf16[256,512]{1,0:T(8,128)(2,1)S(1)}, u32[]{:S(2)}, u32[]{:S(2)}) collective-permute-start(bf16[256,512]{1,0:T(8,128)(2,1)S(1)} %collective-permute-done.22.refs_9_), channel_id=1, source_target_pairs={{0,2},{2,0},{4,6},{6,4},{8,10},{10,8},{12,14},{14,12},{16,18},{18,... | collective-permute-start | bytes 786440 | tf_op jit(solution)/shard_map/ppermute | solution.py:300
  71.0 5.0 %collective-permute-start.30 = (bf16[128,512]{1,0:T(8,128)(2,1)S(1)}, bf16[128,512]{1,0:T(8,128)(2,1)S(1)}, u32[]{:S(2)}, u32[]{:S(2)}) collective-permute-start(bf16[128,512]{1,0:T(8,128)(2,1)S(1)} %collective-permute-done.24.refs_11_), channel_id=1, source_target_pairs={{0,8},{2,6},{8,16},{10,2},{16,24},{18,10},{24,28},{26,18},{28,20},... | collective-permute-start | bytes 393224 | tf_op jit(solution)/shard_map/ppermute | solution.py:385
  72.4 5.0 %collective-permute-start.25 = (bf16[128,512]{1,0:T(8,128)(2,1)S(1)}, bf16[128,512]{1,0:T(8,128)(2,1)S(1)}, u32[]{:S(2)}, u32[]{:S(2)}) collective-permute-start(bf16[128,512]{1,0:T(8,128)(2,1)S(1)} %collective-permute-done.24.refs_11_), channel_id=1, source_target_pairs={{0,2},{2,0},{4,6},{6,4},{8,10},{10,8},{12,14},{14,12},{16,18},{18,... | collective-permute-start | bytes 393224 | tf_op jit(solution)/shard_map/ppermute | solution.py:300
  72.4 5.0 %collective-permute-start.26 = (bf16[128,512]{1,0:T(8,128)(2,1)S(1)}, bf16[128,512]{1,0:T(8,128)(2,1)S(1)}, u32[]{:S(2)}, u32[]{:S(2)}) collective-permute-start(bf16[128,512]{1,0:T(8,128)(2,1)S(1)} %collective-permute-done.20.refs_7_), channel_id=1, source_target_pairs={{0,8},{2,6},{8,16},{10,2},{16,24},{18,10},{24,28},{26,18},{28,20},... | collective-permute-start | bytes 393224 | tf_op jit(solution)/shard_map/ppermute | solution.py:385
  73.9 5.0 %collective-permute-start.21 = (bf16[128,512]{1,0:T(8,128)(2,1)S(1)}, bf16[128,512]{1,0:T(8,128)(2,1)S(1)}, u32[]{:S(2)}, u32[]{:S(2)}) collective-permute-start(bf16[128,512]{1,0:T(8,128)(2,1)S(1)} %collective-permute-done.20.refs_7_), channel_id=1, source_target_pairs={{0,2},{2,0},{4,6},{6,4},{8,10},{10,8},{12,14},{14,12},{16,18},{18,... | collective-permute-start | bytes 393224 | tf_op jit(solution)/shard_map/ppermute | solution.py:300
  75.9 5.0 %collective-permute-start.36 = (bf16[128,512]{1,0:T(8,128)(2,1)S(1)}, bf16[128,512]{1,0:T(8,128)(2,1)S(1)}, u32[]{:S(2)}, u32[]{:S(2)}) collective-permute-start(bf16[128,512]{1,0:T(8,128)(2,1)S(1)} %collective-permute-done.30.refs_17_), channel_id=1, source_target_pairs={{0,8},{2,6},{8,16},{10,2},{16,24},{18,10},{24,28},{26,18},{28,20},... | collective-permute-start | bytes 393224 | tf_op jit(solution)/shard_map/ppermute | solution.py:385
  77.3 4.1 %collective-permute-start.31 = (bf16[128,512]{1,0:T(8,128)(2,1)S(1)}, bf16[128,512]{1,0:T(8,128)(2,1)S(1)}, u32[]{:S(2)}, u32[]{:S(2)}) collective-permute-start(bf16[128,512]{1,0:T(8,128)(2,1)S(1)} %collective-permute-done.30.refs_17_), channel_id=1, source_target_pairs={{0,2},{2,0},{4,6},{6,4},{8,10},{10,8},{12,14},{14,12},{16,18},{18,... | collective-permute-start | bytes 393224 | tf_op jit(solution)/shard_map/ppermute | solution.py:300
  77.4 5.0 %collective-permute-start.32 = (bf16[128,512]{1,0:T(8,128)(2,1)S(1)}, bf16[128,512]{1,0:T(8,128)(2,1)S(1)}, u32[]{:S(2)}, u32[]{:S(2)}) collective-permute-start(bf16[128,512]{1,0:T(8,128)(2,1)S(1)} %collective-permute-done.26.refs_13_), channel_id=1, source_target_pairs={{0,8},{2,6},{8,16},{10,2},{16,24},{18,10},{24,28},{26,18},{28,20},... | collective-permute-start | bytes 393224 | tf_op jit(solution)/shard_map/ppermute | solution.py:385
  78.8 5.1 %collective-permute-start.34 = (bf16[128,512]{1,0:T(8,128)(2,1)S(1)}, bf16[128,512]{1,0:T(8,128)(2,1)}, u32[]{:S(2)}, u32[]{:S(2)}) collective-permute-start(bf16[128,512]{1,0:T(8,128)(2,1)S(1)} %dynamic-slice_bitcast_fusion), channel_id=1, source_target_pairs={{0,8},{2,6},{8,16},{10,2},{16,24},{18,10},{24,28},{26,18},{28,20},... | collective-permute-start | bytes 393224 | tf_op jit(solution)/shard_map/ppermute | solution.py:385
  80.9 4.7 %collective-permute-start.29 = (bf16[256,512]{1,0:T(8,128)(2,1)S(1)}, bf16[256,512]{1,0:T(8,128)(2,1)S(1)}, u32[]{:S(2)}, u32[]{:S(2)}) collective-permute-start(bf16[256,512]{1,0:T(8,128)(2,1)S(1)} %collective-permute-done.28.refs_15_), channel_id=1, source_target_pairs={{0,2},{2,0},{4,6},{6,4},{8,10},{10,8},{12,14},{14,12},{16,18},{18,... | collective-permute-start | bytes 786440 | tf_op jit(solution)/shard_map/ppermute | solution.py:300
  80.9 3.0 %collective-permute-start.27 = (bf16[128,512]{1,0:T(8,128)(2,1)S(1)}, bf16[128,512]{1,0:T(8,128)(2,1)}, u32[]{:S(2)}, u32[]{:S(2)}) collective-permute-start(bf16[128,512]{1,0:T(8,128)(2,1)S(1)} %collective-permute-done.26.refs_13_), channel_id=1, source_target_pairs={{0,2},{2,0},{4,6},{6,4},{8,10},{10,8},{12,14},{14,12},{16,18},{18,... | collective-permute-start | bytes 393224 | tf_op jit(solution)/shard_map/ppermute | solution.py:300
  81.4 2.5 %collective-permute-start.37 = (bf16[128,512]{1,0:T(8,128)(2,1)S(1)}, bf16[128,512]{1,0:T(8,128)(2,1)}, u32[]{:S(2)}, u32[]{:S(2)}) collective-permute-start(bf16[128,512]{1,0:T(8,128)(2,1)S(1)} %collective-permute-done.36.refs_23_), channel_id=1, source_target_pairs={{0,2},{2,0},{4,6},{6,4},{8,10},{10,8},{12,14},{14,12},{16,18},{18,... | collective-permute-start | bytes 393224 | tf_op jit(solution)/shard_map/ppermute | solution.py:300
  82.4 1.6 %collective-permute-start.33 = (bf16[128,512]{1,0:T(8,128)(2,1)S(1)}, bf16[128,512]{1,0:T(8,128)(2,1)}, u32[]{:S(2)}, u32[]{:S(2)}) collective-permute-start(bf16[128,512]{1,0:T(8,128)(2,1)S(1)} %collective-permute-done.32.refs_19_), channel_id=1, source_target_pairs={{0,2},{2,0},{4,6},{6,4},{8,10},{10,8},{12,14},{14,12},{16,18},{18,... | collective-permute-start | bytes 393224 | tf_op jit(solution)/shard_map/ppermute | solution.py:300
  83.9 1.7 %collective-permute-start.35 = (bf16[128,512]{1,0:T(8,128)(2,1)}, bf16[128,512]{1,0:T(8,128)(2,1)}, u32[]{:S(2)}, u32[]{:S(2)}) collective-permute-start(bf16[128,512]{1,0:T(8,128)(2,1)} %collective-permute-done.34.refs_21_), channel_id=1, source_target_pairs={{0,2},{2,0},{4,6},{6,4},{8,10},{10,8},{12,14},{14,12},{16,18},{18,... | collective-permute-start | bytes 393224 | tf_op jit(solution)/shard_map/ppermute | solution.py:300

commit v5 on v4

--- a/solution.py
+++ b/solution.py
@@ -1,4 +1,3 @@
-import functools
 import math
 
 import jax
@@ -207,18 +206,18 @@
     partial_ref[...] = contract(band_ref[...], cot_ref[...], 0, 0)
 
 
-def update_kernel(side_ref, mine_ref, other_ref, tile_ref, near_ref, far_ref):
-    rows, far_rows = near_ref.shape[0], far_ref.shape[0]
+def update_kernel(side_ref, mine_ref, other_ref, tile_ref, near_ref, next_ref, far_ref):
+    rows = near_ref.shape[0]
     tile = tile_ref[...]
     core, plane = side_ref[0], side_ref[1]
 
     def write(left_ref, right_ref):
-        for out_ref, first_row in (
-            (near_ref, plane * rows),
-            (far_ref, (1 - plane) * rows + core * far_rows),
+        for out_ref, part in (
+            (near_ref, 2 * plane + core),
+            (next_ref, 2 * plane + 1 - core),
+            (far_ref, 2 * (1 - plane) + core),
         ):
-            count = out_ref.shape[0]
-            left = left_ref[pl.ds(pl.multiple_of(first_row, count), count), :]
+            left = left_ref[pl.ds(pl.multiple_of(part * rows, rows), rows), :]
             half = contract(left, tile, 1, 0).astype(jnp.bfloat16)
             piece = contract(half, right_ref[...], 1, 0) * math.sqrt(BLOCK)
             out_ref[...] = piece.astype(jnp.bfloat16)
@@ -230,44 +229,6 @@
     @pl.when(core != 0)
     def _():
         write(other_ref, mine_ref)
-
-
-WHOLE, MINE, OTHERS = 0, 1, -1
-
-
-def place_kernel(plan, place_ref, *refs):
-    pieces = refs[: len(plan)]
-    update_ref, sems = refs[len(plan) :]
-    core, plane, spot = place_ref[0], place_ref[1], place_ref[2]
-    bands = update_ref.shape[0]
-    ahead = 1 - 2 * core
-    copies = []
-    for index, (hop, chunk, other, part) in enumerate(plan):
-        rows = pieces[index].shape[0]
-        member = plane if chunk == 0 else 1 - plane
-        position = spot + ahead * hop if other else spot - ahead * hop
-        number = {WHOLE: 0, MINE: core, OTHERS: 1 - core}[part]
-        first_row = pl.multiple_of(number * rows, rows)
-        first_col = pl.multiple_of(member * BLOCK, BLOCK)
-        to_ref = update_ref.at[
-            ring_band(position, bands), pl.ds(first_row, rows), pl.ds(first_col, BLOCK)
-        ]
-        copies.append(pltpu.make_async_copy(pieces[index], to_ref, sems.at[index]))
-        copies[-1].start()
-    for copy in copies:
-        copy.wait()
-
-
-def put_pieces(plan, shape, place, pieces):
-    return pl.pallas_call(
-        functools.partial(place_kernel, plan),
-        out_shape=jax.ShapeDtypeStruct(shape, jnp.bfloat16),
-        in_specs=[pl.BlockSpec(memory_space=pltpu.SMEM)]
-        + [pl.BlockSpec(memory_space=pl.ANY)] * len(pieces),
-        out_specs=pl.BlockSpec(memory_space=pl.ANY),
-        scratch_shapes=[pltpu.SemaphoreType.DMA((len(pieces),))],
-        compiler_params=pltpu.CompilerParams(vmem_limit_bytes=1024 * 1024),
-    )(place, *pieces)
 
 
 def call(kernel, out_shapes, scratch_shapes, *operands):
@@ -292,6 +253,7 @@
     band = lax.axis_index("dp") // cores
     plane = lax.axis_index("pre")
     tokens = inputs.shape[0]
+    ahead = 1 - 2 * core
     spot = jnp.where(band % 2 == 0, band // 2, bands - 1 - band // 2)
 
     ring = list(range(0, bands, 2)) + list(range(bands - 1, 0, -2))
@@ -331,12 +293,10 @@
         return lax.ppermute(array, "dp", pairs)
 
     outputs = jnp.dot(inputs, weight, preferred_element_type=jnp.float32).astype(jnp.bfloat16)
-    far_cot, outputs, packed = lax.optimization_barrier((exchange(cotangent, 4), outputs, packed))
+    far_cot, outputs = lax.optimization_barrier((exchange(cotangent, 4), outputs))
+    near = [deal(piece, hop) for hop, piece in zip(hops, packed)]
     pair = jnp.concatenate([cotangent, far_cot])
-    near = [deal(packed[0], 0), deal(packed[1], 1)]
-    next_pair, packed = lax.optimization_barrier((exchange(pair, 2), packed))
-    cots = [pair, exchange(pair, 1), next_pair, exchange(next_pair, 1)]
-    near += [deal(packed[2], 2), deal(packed[3], 3)]
+    cots = [pair] + [exchange(pair, offset) for offset in (1, 2, 3)]
     far = [swap_plane(piece) for piece in near]
     (partial_tile,) = call(
         tile_kernel,
@@ -362,13 +322,10 @@
         other_partial,
     )
     other_root = swap_core(root)
-    rows = BLOCK // members
-    near_piece, far_piece = call(
+    rows = BLOCK // members // cores
+    near_piece, next_piece, far_piece = call(
         update_kernel,
-        [
-            jax.ShapeDtypeStruct((rows, BLOCK), jnp.bfloat16),
-            jax.ShapeDtypeStruct((rows // cores, BLOCK), jnp.bfloat16),
-        ],
+        [jax.ShapeDtypeStruct((rows, BLOCK), jnp.bfloat16)] * 3,
         [],
         side,
         root,
@@ -385,28 +342,29 @@
         return lax.ppermute(array, "dp", pairs)
 
     half_way = bands // 2
-    near_turned, crossed = lax.optimization_barrier((turn(near_piece), swap_plane(far_piece)))
-    other_crossed = swap_core(crossed)
-    heads = [near_piece, crossed, other_crossed]
-    parts = [WHOLE, MINE, OTHERS]
-    plan = [(0, min(k, 1), False, parts[k]) for k in range(3)]
-    pieces = list(heads)
-    for hop in range(1, half_way + 1):
-        for k, part in enumerate(parts):
-            chunk = min(k, 1)
-            if hop == half_way and part == OTHERS:
+    crossed = swap_plane(far_piece)
+    heads = [near_piece, next_piece, crossed, swap_core(crossed)]
+    columns = [jnp.zeros((bands, cores, rows, BLOCK), jnp.bfloat16)] * 2
+
+    def put(chunk, piece, position, half):
+        columns[chunk] = lax.dynamic_update_slice(
+            columns[chunk], piece[None, None], (ring_band(position, bands), half, 0, 0)
+        )
+
+    for hop in range(half_way + 1):
+        for k, head in enumerate(heads):
+            chunk, half = k // 2, (core if k % 2 == 0 else 1 - core)
+            if hop == half_way and k % 2 == 1:
                 continue
-            if hop == half_way and part == WHOLE:
-                heads[k] = lax.dynamic_slice_in_dim(heads[k].reshape(2, -1, BLOCK), core, 1, 0)[0]
-                part = MINE
-            heads[k] = near_turned if (hop, k) == (1, 0) else turn(heads[k])
-            pieces += [heads[k], swap_core(heads[k])]
-            plan += [(hop, chunk, False, part), (hop, chunk, True, -part)]
-    update = put_pieces(
-        plan,
-        (bands, rows, CB * BLOCK),
-        jnp.stack([core, plane, spot]).astype(jnp.int32),
-        pieces,
+            if hop > 0:
+                heads[k] = head = turn(head)
+                put(chunk, swap_core(head), spot + ahead * hop, 1 - half)
+            put(chunk, head, spot - ahead * hop, half)
+    former, latter = (column.reshape(bands, cores * rows, BLOCK) for column in columns)
+    update = jnp.where(
+        plane == 0,
+        jnp.concatenate([former, latter], axis=-1),
+        jnp.concatenate([latter, former], axis=-1),
     )
     return (outputs, update)
 

time: 108 us -> 79.8 us (0.74)
  Pallas kernels: 29.4 us -> 7.76 us
  waiting for transfers between devices: 36.2 us -> 14.8 us
  starting transfers between devices: 36.8 us -> 47.1 us
  other arithmetic: 0.23 us -> 2.84 us
  local copies, waits for them, and re-layouts: 0.12 us -> 2.23 us
    pallas_call x1 -> x0, Pallas kernels: 21.8 us -> none  [put_pieces(): pl.pallas_call(functools.partial(place_kernel, plan), out_shape=jax.Shape...]
    ppermute x4, waiting for transfers between devices: 8.3 us -> 0.01 us  [deal(): return lax.ppermute(array, ('dp', 'pre'), pairs)]
    ppermute x11 -> x14, waiting for transfers between devices: 10.9 us -> 4.22 us  [turn(): return lax.ppermute(array, 'dp', pairs)]
    ppermute x5, starting transfers between devices: 4.86 us -> 11.3 us  [swap_plane(): lax.ppermute(array, 'pre', [(c, members - 1 - c) for c in range(members)])]
    ppermute x5, waiting for transfers between devices: 9.16 us -> 4.99 us  [swap_plane(): lax.ppermute(array, 'pre', [(c, members - 1 - c) for c in range(members)])]
    ppermute x11 -> x14, starting transfers between devices: 17.1 us -> 20.2 us  [turn(): return lax.ppermute(array, 'dp', pairs)]
    select_n x0 -> x1, other arithmetic: none -> 2.68 us  [on_device_paired(): jnp.where(plane == 0, jnp.concatenate([former, latter], axis=-1), jnp.con...]
    ppermute x4, starting transfers between devices: 7.98 us -> 5.91 us  [deal(): return lax.ppermute(array, ('dp', 'pre'), pairs)]
  transfers between devices with their start and end apart: 38 -> 44, of which waited for: 16 -> 14; matrix products, arithmetic and copies ran while one was open for 4% -> 6% of each run, Pallas kernels for 1% -> 1%
where the time goes in v5:
time: 79.8 us; the launch traced here: 79.6 us
  starting transfers between devices  47.1 us (59%)
  waiting for transfers between devices  14.8 us (19%)
  Pallas kernels  7.76 us (10%)
  matrix products  3.62 us (5%)
  other arithmetic  2.84 us (4%)
  local copies, waits for them, and re-layouts  2.23 us (3%)
  between operations  1.22 us (2%)
    ppermute x14, starting transfers between devices, turn(): return lax.ppermute(array, 'dp', pairs)  20.2 us
    ppermute x5, starting transfers between devices, swap_plane(): lax.ppermute(array, 'pre', [(c, members - 1 - c) for c in range(members)])  11.3 us
    pallas_call x4, Pallas kernels, call(): pl.pallas_call(kernel, out_shape=out_shapes, in_specs=in_specs, out_specs...  7.76 us
    ppermute x4, starting transfers between devices, exchange(): return lax.ppermute(array, 'dp', pairs)  7.49 us
    ppermute x4, starting transfers between devices, deal(): return lax.ppermute(array, ('dp', 'pre'), pairs)  5.91 us
    ppermute x17, waiting for transfers between devices, swap_core(): return lax.ppermute(array, 'dp', [(g, g ^ 1) for g in range(groups)])  5.55 us
    ppermute x5, waiting for transfers between devices, swap_plane(): lax.ppermute(array, 'pre', [(c, members - 1 - c) for c in range(members)])  4.99 us
    ppermute x14, waiting for transfers between devices, turn(): return lax.ppermute(array, 'dp', pairs)  4.22 us
  transfers between devices with their start and end apart: 44, of which 14 were waited for; matrix products, arithmetic and copies ran while one was open for 6% of the time, Pallas kernels for 1%

profile of v5, /device:TPU:0, one launch (start us, length us, event | category | flops | bytes accessed | tf_op | source)
XLA Modules:
  0.0 79.6 jit_solution(8597925463455770348)
XLA Ops:
  0.6 4.1 %collective-permute-start = (bf16[128,512]{1,0:T(8,128)(2,1)}, bf16[128,512]{1,0:T(8,128)(2,1)S(1)}, u32[]{:S(2)}, u32[]{:S(2)}) collective-permute-start(bf16[128,512]{1,0:T(8,128)(2,1)} %param.5), channel_id=1, source_target_pairs={{0,16},{2,18},{4,20},{6,22},{8,24},{10,26},{12,28},{14,30},{16,0},... | collective-permute-start | bytes 393224 | tf_op jit(solution)/shard_map/ppermute | solution.py:293
  4.8 1.2 %copy-done = bf16[128,4096]{1,0:T(8,128)(2,1)S(1)} copy-done((bf16[128,4096]{1,0:T(8,128)(2,1)S(1)}, bf16[128,4096]{1,0:T(8,128)(2,1)}, u32[]{:S(2)}) %copy-start) | copy-done | bytes 1048600
  6.0 0.6 shard_map.50
  6.6 1.6 %collective-permute-start.4 = (bf16[64,512]{1,0:T(8,128)(2,1)S(1)}, bf16[64,512]{1,0:T(8,128)(2,1)S(1)}, u32[]{:S(2)}, u32[]{:S(2)}) collective-permute-start(bf16[64,512]{1,0:T(8,128)(2,1)S(1)} %get-tuple-element.19), channel_id=1, source_target_pairs={{0,8},{1,9},{2,10},{3,11},{4,12},{5,13},{6,14},{7,15},{8,0},{9,1},... | collective-permute-start | bytes 196616 | tf_op jit(solution)/shard_map/ppermute | solution.py:277
  8.3 0.3 collective-permute-start.1
  8.6 3.4 %collective-permute-start.2 = (bf16[128,512]{1,0:T(8,128)(2,1)S(1)}, bf16[128,512]{1,0:T(8,128)(2,1)S(1)}, u32[]{:S(2)}, u32[]{:S(2)}) collective-permute-start(bf16[128,512]{1,0:T(8,128)(2,1)S(1)} %get-tuple-element.17), channel_id=1, source_target_pairs={{0,28},{1,25},{2,30},{3,27},{4,24},{5,29},{6,26},{7,31},{8,20},{9,... | collective-permute-start | bytes 393224 | tf_op jit(solution)/shard_map/ppermute | solution.py:277
  12.0 0.5 collective-permute-start.3
  12.6 3.6 %convolution_convert_fusion = bf16[128,512]{1,0:T(8,128)(2,1)} fusion(bf16[128,4096]{1,0:T(8,128)(2,1)S(1)} %copy-done, bf16[4096,512]{1,0:T(8,128)(2,1)} %param.4), kind=kOutput, calls=%fused_computation.1 | convolution fusion | flops 536936448 | bytes 5373952 | tf_op jit(solution)/shard_map/dot_general | solution.py:295
  16.2 1.7 %collective-permute-start.8 = (bf16[64,512]{1,0:T(8,128)(2,1)S(1)}, bf16[64,512]{1,0:T(8,128)(2,1)S(1)}, u32[]{:S(2)}, u32[]{:S(2)}) collective-permute-start(bf16[64,512]{1,0:T(8,128)(2,1)S(1)} %collective-permute-done.4.refs_3_), channel_id=1, source_target_pairs={{0,1},{1,0},{2,3},{3,2},{4,5},{5,4},{6,7},{7,6},{8,9},{9,8},{10,11... | collective-permute-start | bytes 196616 | tf_op jit(solution)/shard_map/ppermute | solution.py:265
  17.9 2.4 %collective-permute-start.11 = (bf16[256,512]{1,0:T(8,128)(2,1)S(1)}, bf16[256,512]{1,0:T(8,128)(2,1)S(1)}, u32[]{:S(2)}, u32[]{:S(2)}) collective-permute-start(bf16[256,512]{1,0:T(8,128)(2,1)S(1)} %constant_dynamic-update-slice_fusion.refs_8_), channel_id=1, source_target_pairs={{0,12},{2,14},{4,8},{6,10},{8,4},{10,6},{12,0},{14,2},{16,28},{18,... | collective-permute-start | bytes 786440 | tf_op jit(solution)/shard_map/ppermute | solution.py:293
  20.3 2.2 %collective-permute-start.5 = (bf16[128,512]{1,0:T(8,128)(2,1)S(1)}, bf16[128,512]{1,0:T(8,128)(2,1)S(1)}, u32[]{:S(2)}, u32[]{:S(2)}) collective-permute-start(bf16[128,512]{1,0:T(8,128)(2,1)S(1)} %collective-permute-done.1.refs_0_), channel_id=1, source_target_pairs={{0,1},{1,0},{2,3},{3,2},{4,5},{5,4},{6,7},{7,6},{8,9},{9,8},{10,11... | collective-permute-start | bytes 393224 | tf_op jit(solution)/shard_map/ppermute | solution.py:265
  22.5 1.0 %collective-permute-start.9 = (bf16[256,512]{1,0:T(8,128)(2,1)S(1)}, bf16[256,512]{1,0:T(8,128)(2,1)S(1)}, u32[]{:S(2)}, u32[]{:S(2)}) collective-permute-start(bf16[256,512]{1,0:T(8,128)(2,1)S(1)} %constant_dynamic-update-slice_fusion.refs_8_), channel_id=1, source_target_pairs={{0,4},{2,6},{4,0},{6,2},{8,12},{10,14},{12,8},{14,10},{16,20},{18,... | collective-permute-start | bytes 786440 | tf_op jit(solution)/shard_map/ppermute | solution.py:293
  23.5 1.7 %collective-permute-start.6 = (bf16[128,512]{1,0:T(8,128)(2,1)S(1)}, bf16[128,512]{1,0:T(8,128)(2,1)S(1)}, u32[]{:S(2)}, u32[]{:S(2)}) collective-permute-start(bf16[128,512]{1,0:T(8,128)(2,1)S(1)} %collective-permute-done.2.refs_1_), channel_id=1, source_target_pairs={{0,1},{1,0},{2,3},{3,2},{4,5},{5,4},{6,7},{7,6},{8,9},{9,8},{10,11... | collective-permute-start | bytes 393224 | tf_op jit(solution)/shard_map/ppermute | solution.py:265
  25.2 1.2 %collective-permute-done.5.refs_4_ = bf16[128,512]{1,0:T(8,128)(2,1)S(1)} collective-permute-done((bf16[128,512]{1,0:T(8,128)(2,1)S(1)}, bf16[128,512]{1,0:T(8,128)(2,1)S(1)}, u32[]{:S(2)}, u32[]{:S(2)}) %collective-permute-start.5) | collective-permute-done | bytes 131104 | tf_op jit(solution)/shard_map/ppermute | solution.py:265
  26.4 2.5 %collective-permute-start.7 = (bf16[128,512]{1,0:T(8,128)(2,1)S(1)}, bf16[128,512]{1,0:T(8,128)(2,1)S(1)}, u32[]{:S(2)}, u32[]{:S(2)}) collective-permute-start(bf16[128,512]{1,0:T(8,128)(2,1)S(1)} %collective-permute-done.3.refs_2_), channel_id=1, source_target_pairs={{0,1},{1,0},{2,3},{3,2},{4,5},{5,4},{6,7},{7,6},{8,9},{9,8},{10,11... | collective-permute-start | bytes 393224 | tf_op jit(solution)/shard_map/ppermute | solution.py:265
  29.0 0.8 collective-permute-done.6.refs_5_
  29.7 2.1 %collective-permute-done.7.refs_6_ = bf16[128,512]{1,0:T(8,128)(2,1)S(1)} collective-permute-done((bf16[128,512]{1,0:T(8,128)(2,1)S(1)}, bf16[128,512]{1,0:T(8,128)(2,1)S(1)}, u32[]{:S(2)}, u32[]{:S(2)}) %collective-permute-start.7) | collective-permute-done | bytes 131104 | tf_op jit(solution)/shard_map/ppermute | solution.py:265
  31.9 1.4 %shard_map.51.mine_ref = f32[512,512]{1,0:T(8,128)S(1)} custom-call(s32[2]{0:T(128)S(1)} %pad_add_fusion.1.place_ref, bf16[128,512]{1,0:T(8,128)(2,1)S(1)} %get-tuple-element.15.own_ref, bf16[128,512]{1,0:T(8,128)(2,1)S(1)} %collective-permute-done.1.refs_0_, bf16[128,512]{1,0:T(8,128)(2,1)S(1)} %collective-permute-done.2.refs_1_, ...), custom_call_target="tpu_custom_call" | custom-call | tf_op jit(solution)/shard_map/pallas_call | solution.py:237
  33.5 2.6 %collective-permute-done.12.other_ref = f32[512,512]{1,0:T(8,128)S(1)} collective-permute-done((f32[512,512]{1,0:T(8,128)S(1)}, f32[512,512]{1,0:T(8,128)S(1)}, u32[]{:S(2)}, u32[]{:S(2)}) %collective-permute-start.12) | collective-permute-done | bytes 1048608 | tf_op jit(solution)/shard_map/ppermute | solution.py:262
  36.0 4.3 %shard_map.52 = (bf16[512,512]{1,0:T(8,128)(2,1)S(1)}, bf16[512,512]{1,0:T(8,128)(2,1)S(1)}) custom-call(s32[2]{0:T(128)S(1)} %pad_add_fusion.side_ref, f32[512,512]{1,0:T(8,128)S(1)} %shard_map.51.mine_ref, f32[512,512]{1,0:T(8,128)S(1)} %collective-permute-done.12.other_ref), custom_call_target="tpu_custom_call" | custom-call | tf_op jit(solution)/shard_map/pallas_call | solution.py:237
  40.3 0.2 collective-permute-start.13
  40.7 1.6 %collective-permute-done.13.other_ref = bf16[512,512]{1,0:T(8,128)(2,1)S(1)} collective-permute-done((bf16[512,512]{1,0:T(8,128)(2,1)S(1)}, bf16[512,512]{1,0:T(8,128)(2,1)S(1)}, u32[]{:S(2)}, u32[]{:S(2)}) %collective-permute-start.13) | collective-permute-done | bytes 524320 | tf_op jit(solution)/shard_map/ppermute | solution.py:262
  42.3 1.5 %shard_map.53 = (bf16[128,512]{1,0:T(8,128)(2,1)S(1)}, bf16[128,512]{1,0:T(8,128)(2,1)S(1)}, bf16[128,512]{1,0:T(8,128)(2,1)S(1)}) custom-call(s32[2]{0:T(128)S(1)} %pad_add_fusion.side_ref, bf16[512,512]{1,0:T(8,128)(2,1)S(1)} %get-tuple-element.21.mine_ref, bf16[512,512]{1,0:T(8,128)(2,1)S(1)} %collective-permute-done.13.other_ref, ...), custom_call_target="tpu_custom_call" | custom-call | tf_op jit(solution)/shard_map/pallas_call | solution.py:237
  43.8 3.3 %collective-permute-start.28 = (bf16[128,512]{1,0:T(8,128)(2,1)S(1)}, bf16[128,512]{1,0:T(8,128)(2,1)S(1)}, u32[]{:S(2)}, u32[]{:S(2)}) collective-permute-start(bf16[128,512]{1,0:T(8,128)(2,1)S(1)} %get-tuple-element.25), channel_id=1, source_target_pairs={{0,1},{1,0},{2,3},{3,2},{4,5},{5,4},{6,7},{7,6},{8,9},{9,8},{10,11... | collective-permute-start | bytes 393224 | tf_op jit(solution)/shard_map/ppermute | solution.py:265
  47.1 0.6 collective-permute-start.14
  47.7 2.1 %collective-permute-start.16 = (bf16[128,512]{1,0:T(8,128)(2,1)S(1)}, bf16[128,512]{1,0:T(8,128)(2,1)S(1)}, u32[]{:S(2)}, u32[]{:S(2)}) collective-permute-start(bf16[128,512]{1,0:T(8,128)(2,1)S(1)} %get-tuple-element.24), channel_id=1, source_target_pairs={{0,8},{2,6},{8,16},{10,2},{16,24},{18,10},{24,28},{26,18},{28,20},... | collective-permute-start | bytes 393224 | tf_op jit(solution)/shard_map/ppermute | solution.py:342
  50.0 0.9 %collective-permute-done.28 = bf16[128,512]{1,0:T(8,128)(2,1)S(1)} collective-permute-done((bf16[128,512]{1,0:T(8,128)(2,1)S(1)}, bf16[128,512]{1,0:T(8,128)(2,1)S(1)}, u32[]{:S(2)}, u32[]{:S(2)}) %collective-permute-start.28) | collective-permute-done | bytes 131104 | tf_op jit(solution)/shard_map/ppermute | solution.py:265
  50.9 2.3 %collective-permute-start.30 = (bf16[128,512]{1,0:T(8,128)(2,1)S(1)}, bf16[128,512]{1,0:T(8,128)(2,1)S(1)}, u32[]{:S(2)}, u32[]{:S(2)}) collective-permute-start(bf16[128,512]{1,0:T(8,128)(2,1)S(1)} %collective-permute-done.28), channel_id=1, source_target_pairs={{0,8},{2,6},{8,16},{10,2},{16,24},{18,10},{24,28},{26,18},{28,20},... | collective-permute-start | bytes 393224 | tf_op jit(solution)/shard_map/ppermute | solution.py:342
  53.2 2.1 %collective-permute-start.18 = (bf16[128,512]{1,0:T(8,128)(2,1)S(1)}, bf16[128,512]{1,0:T(8,128)(2,1)S(1)}, u32[]{:S(2)}, u32[]{:S(2)}) collective-permute-start(bf16[128,512]{1,0:T(8,128)(2,1)S(1)} %collective-permute-done.14), channel_id=1, source_target_pairs={{0,8},{2,6},{8,16},{10,2},{16,24},{18,10},{24,28},{26,18},{28,20},... | collective-permute-start | bytes 393224 | tf_op jit(solution)/shard_map/ppermute | solution.py:342
  55.3 0.5 collective-permute-start.20
  56.1 2.1 %collective-permute-start.34 = (bf16[128,512]{1,0:T(8,128)(2,1)S(1)}, bf16[128,512]{1,0:T(8,128)(2,1)S(1)}, u32[]{:S(2)}, u32[]{:S(2)}) collective-permute-start(bf16[128,512]{1,0:T(8,128)(2,1)S(1)} %collective-permute-done.30), channel_id=1, source_target_pairs={{0,8},{2,6},{8,16},{10,2},{16,24},{18,10},{24,28},{26,18},{28,20},... | collective-permute-start | bytes 393224 | tf_op jit(solution)/shard_map/ppermute | solution.py:342
  58.4 2.1 %collective-permute-start.32 = (bf16[128,512]{1,0:T(8,128)(2,1)S(1)}, bf16[128,512]{1,0:T(8,128)(2,1)S(1)}, u32[]{:S(2)}, u32[]{:S(2)}) collective-permute-start(bf16[128,512]{1,0:T(8,128)(2,1)S(1)} %collective-permute-done.29), channel_id=1, source_target_pairs={{0,8},{2,6},{8,16},{10,2},{16,24},{18,10},{24,28},{26,18},{28,20},... | collective-permute-start | bytes 393224 | tf_op jit(solution)/shard_map/ppermute | solution.py:342
  60.5 1.2 %collective-permute-start.22 = (bf16[128,512]{1,0:T(8,128)(2,1)S(1)}, bf16[128,512]{1,0:T(8,128)(2,1)S(1)}, u32[]{:S(2)}, u32[]{:S(2)}) collective-permute-start(bf16[128,512]{1,0:T(8,128)(2,1)S(1)} %collective-permute-done.18), channel_id=1, source_target_pairs={{0,8},{2,6},{8,16},{10,2},{16,24},{18,10},{24,28},{26,18},{28,20},... | collective-permute-start | bytes 393224 | tf_op jit(solution)/shard_map/ppermute | solution.py:342
  61.8 1.1 %collective-permute-start.24 = (bf16[128,512]{1,0:T(8,128)(2,1)S(1)}, bf16[128,512]{1,0:T(8,128)(2,1)S(1)}, u32[]{:S(2)}, u32[]{:S(2)}) collective-permute-start(bf16[128,512]{1,0:T(8,128)(2,1)S(1)} %collective-permute-done.20), channel_id=1, source_target_pairs={{0,8},{2,6},{8,16},{10,2},{16,24},{18,10},{24,28},{26,18},{28,20},... | collective-permute-start | bytes 393224 | tf_op jit(solution)/shard_map/ppermute | solution.py:342
  63.1 1.1 %collective-permute-start.38 = (bf16[128,512]{1,0:T(8,128)(2,1)S(1)}, bf16[128,512]{1,0:T(8,128)(2,1)S(1)}, u32[]{:S(2)}, u32[]{:S(2)}) collective-permute-start(bf16[128,512]{1,0:T(8,128)(2,1)S(1)} %collective-permute-done.34), channel_id=1, source_target_pairs={{0,8},{2,6},{8,16},{10,2},{16,24},{18,10},{24,28},{26,18},{28,20},... | collective-permute-start | bytes 393224 | tf_op jit(solution)/shard_map/ppermute | solution.py:342
  64.4 0.5 collective-permute-start.33
  64.9 0.6 collective-permute-done.22
  65.5 1.4 %collective-permute-start.36 = (bf16[128,512]{1,0:T(8,128)(2,1)S(1)}, bf16[128,512]{1,0:T(8,128)(2,1)S(1)}, u32[]{:S(2)}, u32[]{:S(2)}) collective-permute-start(bf16[128,512]{1,0:T(8,128)(2,1)S(1)} %collective-permute-done.32), channel_id=1, source_target_pairs={{0,8},{2,6},{8,16},{10,2},{16,24},{18,10},{24,28},{26,18},{28,20},... | collective-permute-start | bytes 393224 | tf_op jit(solution)/shard_map/ppermute | solution.py:342
  66.9 1.2 %collective-permute-start.26 = (bf16[128,512]{1,0:T(8,128)(2,1)S(1)}, bf16[128,512]{1,0:T(8,128)(2,1)S(1)}, u32[]{:S(2)}, u32[]{:S(2)}) collective-permute-start(bf16[128,512]{1,0:T(8,128)(2,1)S(1)} %collective-permute-done.22), channel_id=1, source_target_pairs={{0,8},{2,6},{8,16},{10,2},{16,24},{18,10},{24,28},{26,18},{28,20},... | collective-permute-start | bytes 393224 | tf_op jit(solution)/shard_map/ppermute | solution.py:342
  68.3 0.4 collective-permute-start.25
  68.7 1.0 %collective-permute-start.42 = (bf16[128,512]{1,0:T(8,128)(2,1)S(1)}, bf16[128,512]{1,0:T(8,128)(2,1)S(1)}, u32[]{:S(2)}, u32[]{:S(2)}) collective-permute-start(bf16[128,512]{1,0:T(8,128)(2,1)S(1)} %collective-permute-done.38), channel_id=1, source_target_pairs={{0,8},{2,6},{8,16},{10,2},{16,24},{18,10},{24,28},{26,18},{28,20},... | collective-permute-start | bytes 393224 | tf_op jit(solution)/shard_map/ppermute | solution.py:342
  69.8 0.7 collective-permute-done.36
  70.4 1.4 %collective-permute-start.40 = (bf16[128,512]{1,0:T(8,128)(2,1)S(1)}, bf16[128,512]{1,0:T(8,128)(2,1)S(1)}, u32[]{:S(2)}, u32[]{:S(2)}) collective-permute-start(bf16[128,512]{1,0:T(8,128)(2,1)S(1)} %collective-permute-done.36), channel_id=1, source_target_pairs={{0,8},{2,6},{8,16},{10,2},{16,24},{18,10},{24,28},{26,18},{28,20},... | collective-permute-start | bytes 393224 | tf_op jit(solution)/shard_map/ppermute | solution.py:342
  72.0 0.5 collective-permute-start.27
  72.5 1.1 %collective-permute-done.42 = bf16[128,512]{1,0:T(8,128)(2,1)S(1)} collective-permute-done((bf16[128,512]{1,0:T(8,128)(2,1)S(1)}, bf16[128,512]{1,0:T(8,128)(2,1)S(1)}, u32[]{:S(2)}, u32[]{:S(2)}) %collective-permute-start.42) | collective-permute-done | bytes 131104 | tf_op jit(solution)/shard_map/ppermute | solution.py:342
  73.7 1.7 %collective-permute-done.40 = bf16[128,512]{1,0:T(8,128)(2,1)S(1)} collective-permute-done((bf16[128,512]{1,0:T(8,128)(2,1)S(1)}, bf16[128,512]{1,0:T(8,128)(2,1)S(1)}, u32[]{:S(2)}, u32[]{:S(2)}) %collective-permute-start.40) | collective-permute-done | bytes 131104 | tf_op jit(solution)/shard_map/ppermute | solution.py:342
  75.5 1.2 %collective-permute-done.41 = bf16[128,512]{1,0:T(8,128)(2,1)S(1)} collective-permute-done((bf16[128,512]{1,0:T(8,128)(2,1)S(1)}, bf16[128,512]{1,0:T(8,128)(2,1)S(1)}, u32[]{:S(2)}, u32[]{:S(2)}) %collective-permute-start.41) | collective-permute-done | bytes 131104 | tf_op jit(solution)/shard_map/ppermute | solution.py:262
  76.9 2.7 %maximum_select_fusion = bf16[8,256,1024]{2,1,0:T(8,128)(2,1)} fusion(bf16[8,256,512]{2,1,0:T(8,128)(2,1)S(1)} %bitcast.76, bf16[8,256,512]{2,1,0:T(8,128)(2,1)S(1)} %bitcast.77, pred[]{:T(512)S(6)} %eq.45), kind=kLoop, calls=%fused_computation | loop fusion | flops 18874368 | bytes 8388609 | tf_op jit(solution)/shard_map/jit(_where)/select_n | solution.py:364
  (88 shorter events, 2.1 us)
Async XLA Ops:
  0.6 17.2 %collective-permute-start = (bf16[128,512]{1,0:T(8,128)(2,1)}, bf16[128,512]{1,0:T(8,128)(2,1)S(1)}, u32[]{:S(2)}, u32[]{:S(2)}) collective-permute-start(bf16[128,512]{1,0:T(8,128)(2,1)} %param.5), channel_id=1, source_target_pairs={{0,16},{2,18},{4,20},{6,22},{8,24},{10,26},{12,28},{14,30},{16,0},... | collective-permute-start | bytes 393224 | tf_op jit(solution)/shard_map/ppermute | solution.py:293
  4.8 1.2 %copy-start = (bf16[128,4096]{1,0:T(8,128)(2,1)S(1)}, bf16[128,4096]{1,0:T(8,128)(2,1)}, u32[]{:S(2)}) copy-start(bf16[128,4096]{1,0:T(8,128)(2,1)} %inputs_ref.1) | copy-start | bytes 3145732
  6.6 9.6 %collective-permute-start.4 = (bf16[64,512]{1,0:T(8,128)(2,1)S(1)}, bf16[64,512]{1,0:T(8,128)(2,1)S(1)}, u32[]{:S(2)}, u32[]{:S(2)}) collective-permute-start(bf16[64,512]{1,0:T(8,128)(2,1)S(1)} %get-tuple-element.19), channel_id=1, source_target_pairs={{0,8},{1,9},{2,10},{3,11},{4,12},{5,13},{6,14},{7,15},{8,0},{9,1},... | collective-permute-start | bytes 196616 | tf_op jit(solution)/shard_map/ppermute | solution.py:277
  8.3 12.0 %collective-permute-start.1 = (bf16[128,512]{1,0:T(8,128)(2,1)S(1)}, bf16[128,512]{1,0:T(8,128)(2,1)S(1)}, u32[]{:S(2)}, u32[]{:S(2)}) collective-permute-start(bf16[128,512]{1,0:T(8,128)(2,1)S(1)} %get-tuple-element.16), channel_id=1, source_target_pairs={{0,16},{1,21},{2,18},{3,23},{4,20},{5,17},{6,22},{7,19},{8,24},{9,... | collective-permute-start | bytes 393224 | tf_op jit(solution)/shard_map/ppermute | solution.py:277
  8.6 13.9 %collective-permute-start.2 = (bf16[128,512]{1,0:T(8,128)(2,1)S(1)}, bf16[128,512]{1,0:T(8,128)(2,1)S(1)}, u32[]{:S(2)}, u32[]{:S(2)}) collective-permute-start(bf16[128,512]{1,0:T(8,128)(2,1)S(1)} %get-tuple-element.17), channel_id=1, source_target_pairs={{0,28},{1,25},{2,30},{3,27},{4,24},{5,29},{6,26},{7,31},{8,20},{9,... | collective-permute-start | bytes 393224 | tf_op jit(solution)/shard_map/ppermute | solution.py:277
  12.0 4.1 %copy-start.1 = (bf16[128,512]{1,0:T(8,128)(2,1)S(1)}, bf16[128,512]{1,0:T(8,128)(2,1)}, u32[]{:S(2)}) copy-start(bf16[128,512]{1,0:T(8,128)(2,1)} %param.5) | copy-start | bytes 393220
  12.0 11.5 %collective-permute-start.3 = (bf16[128,512]{1,0:T(8,128)(2,1)S(1)}, bf16[128,512]{1,0:T(8,128)(2,1)S(1)}, u32[]{:S(2)}, u32[]{:S(2)}) collective-permute-start(bf16[128,512]{1,0:T(8,128)(2,1)S(1)} %get-tuple-element.18), channel_id=1, source_target_pairs={{0,4},{1,13},{2,6},{3,15},{4,0},{5,9},{6,2},{7,11},{8,12},{9,5},{1... | collective-permute-start | bytes 393224 | tf_op jit(solution)/shard_map/ppermute | solution.py:277
  16.2 6.3 %collective-permute-start.8 = (bf16[64,512]{1,0:T(8,128)(2,1)S(1)}, bf16[64,512]{1,0:T(8,128)(2,1)S(1)}, u32[]{:S(2)}, u32[]{:S(2)}) collective-permute-start(bf16[64,512]{1,0:T(8,128)(2,1)S(1)} %collective-permute-done.4.refs_3_), channel_id=1, source_target_pairs={{0,1},{1,0},{2,3},{3,2},{4,5},{5,4},{6,7},{7,6},{8,9},{9,8},{10,11... | collective-permute-start | bytes 196616 | tf_op jit(solution)/shard_map/ppermute | solution.py:265
  17.9 14.0 %collective-permute-start.11 = (bf16[256,512]{1,0:T(8,128)(2,1)S(1)}, bf16[256,512]{1,0:T(8,128)(2,1)S(1)}, u32[]{:S(2)}, u32[]{:S(2)}) collective-permute-start(bf16[256,512]{1,0:T(8,128)(2,1)S(1)} %constant_dynamic-update-slice_fusion.refs_8_), channel_id=1, source_target_pairs={{0,12},{2,14},{4,8},{6,10},{8,4},{10,6},{12,0},{14,2},{16,28},{18,... | collective-permute-start | bytes 786440 | tf_op jit(solution)/shard_map/ppermute | solution.py:293
  20.3 6.1 %collective-permute-start.5 = (bf16[128,512]{1,0:T(8,128)(2,1)S(1)}, bf16[128,512]{1,0:T(8,128)(2,1)S(1)}, u32[]{:S(2)}, u32[]{:S(2)}) collective-permute-start(bf16[128,512]{1,0:T(8,128)(2,1)S(1)} %collective-permute-done.1.refs_0_), channel_id=1, source_target_pairs={{0,1},{1,0},{2,3},{3,2},{4,5},{5,4},{6,7},{7,6},{8,9},{9,8},{10,11... | collective-permute-start | bytes 393224 | tf_op jit(solution)/shard_map/ppermute | solution.py:265
  22.5 9.4 %collective-permute-start.10 = (bf16[256,512]{1,0:T(8,128)(2,1)S(1)}, bf16[256,512]{1,0:T(8,128)(2,1)S(1)}, u32[]{:S(2)}, u32[]{:S(2)}) collective-permute-start(bf16[256,512]{1,0:T(8,128)(2,1)S(1)} %constant_dynamic-update-slice_fusion.refs_8_), channel_id=1, source_target_pairs={{0,8},{2,10},{4,12},{6,14},{8,0},{10,2},{12,4},{14,6},{16,24},{18,... | collective-permute-start | bytes 786440 | tf_op jit(solution)/shard_map/ppermute | solution.py:293
  22.5 9.4 %collective-permute-start.9 = (bf16[256,512]{1,0:T(8,128)(2,1)S(1)}, bf16[256,512]{1,0:T(8,128)(2,1)S(1)}, u32[]{:S(2)}, u32[]{:S(2)}) collective-permute-start(bf16[256,512]{1,0:T(8,128)(2,1)S(1)} %constant_dynamic-update-slice_fusion.refs_8_), channel_id=1, source_target_pairs={{0,4},{2,6},{4,0},{6,2},{8,12},{10,14},{12,8},{14,10},{16,20},{18,... | collective-permute-start | bytes 786440 | tf_op jit(solution)/shard_map/ppermute | solution.py:293
  23.5 6.2 %collective-permute-start.6 = (bf16[128,512]{1,0:T(8,128)(2,1)S(1)}, bf16[128,512]{1,0:T(8,128)(2,1)S(1)}, u32[]{:S(2)}, u32[]{:S(2)}) collective-permute-start(bf16[128,512]{1,0:T(8,128)(2,1)S(1)} %collective-permute-done.2.refs_1_), channel_id=1, source_target_pairs={{0,1},{1,0},{2,3},{3,2},{4,5},{5,4},{6,7},{7,6},{8,9},{9,8},{10,11... | collective-permute-start | bytes 393224 | tf_op jit(solution)/shard_map/ppermute | solution.py:265
  26.4 5.4 %collective-permute-start.7 = (bf16[128,512]{1,0:T(8,128)(2,1)S(1)}, bf16[128,512]{1,0:T(8,128)(2,1)S(1)}, u32[]{:S(2)}, u32[]{:S(2)}) collective-permute-start(bf16[128,512]{1,0:T(8,128)(2,1)S(1)} %collective-permute-done.3.refs_2_), channel_id=1, source_target_pairs={{0,1},{1,0},{2,3},{3,2},{4,5},{5,4},{6,7},{7,6},{8,9},{9,8},{10,11... | collective-permute-start | bytes 393224 | tf_op jit(solution)/shard_map/ppermute | solution.py:265
  33.3 2.7 %collective-permute-start.12 = (f32[512,512]{1,0:T(8,128)S(1)}, f32[512,512]{1,0:T(8,128)S(1)}, u32[]{:S(2)}, u32[]{:S(2)}) collective-permute-start(f32[512,512]{1,0:T(8,128)S(1)} %shard_map.51.mine_ref), channel_id=1, source_target_pairs={{0,2},{2,0},{4,6},{6,4},{8,10},{10,8},{12,14},{14,12},{16,18},{18,... | collective-permute-start | bytes 3145736 | tf_op jit(solution)/shard_map/ppermute | solution.py:262
  40.3 2.0 %collective-permute-start.13 = (bf16[512,512]{1,0:T(8,128)(2,1)S(1)}, bf16[512,512]{1,0:T(8,128)(2,1)S(1)}, u32[]{:S(2)}, u32[]{:S(2)}) collective-permute-start(bf16[512,512]{1,0:T(8,128)(2,1)S(1)} %get-tuple-element.21.mine_ref), channel_id=1, source_target_pairs={{0,2},{2,0},{4,6},{6,4},{8,10},{10,8},{12,14},{14,12},{16,18},{18,... | collective-permute-start | bytes 1572872 | tf_op jit(solution)/shard_map/ppermute | solution.py:262
  43.8 7.1 %collective-permute-start.28 = (bf16[128,512]{1,0:T(8,128)(2,1)S(1)}, bf16[128,512]{1,0:T(8,128)(2,1)S(1)}, u32[]{:S(2)}, u32[]{:S(2)}) collective-permute-start(bf16[128,512]{1,0:T(8,128)(2,1)S(1)} %get-tuple-element.25), channel_id=1, source_target_pairs={{0,1},{1,0},{2,3},{3,2},{4,5},{5,4},{6,7},{7,6},{8,9},{9,8},{10,11... | collective-permute-start | bytes 393224 | tf_op jit(solution)/shard_map/ppermute | solution.py:265
  47.1 6.2 %collective-permute-start.14 = (bf16[128,512]{1,0:T(8,128)(2,1)S(1)}, bf16[128,512]{1,0:T(8,128)(2,1)S(1)}, u32[]{:S(2)}, u32[]{:S(2)}) collective-permute-start(bf16[128,512]{1,0:T(8,128)(2,1)S(1)} %get-tuple-element.23), channel_id=1, source_target_pairs={{0,8},{2,6},{8,16},{10,2},{16,24},{18,10},{24,28},{26,18},{28,20},... | collective-permute-start | bytes 393224 | tf_op jit(solution)/shard_map/ppermute | solution.py:342
  47.7 7.6 %collective-permute-start.16 = (bf16[128,512]{1,0:T(8,128)(2,1)S(1)}, bf16[128,512]{1,0:T(8,128)(2,1)S(1)}, u32[]{:S(2)}, u32[]{:S(2)}) collective-permute-start(bf16[128,512]{1,0:T(8,128)(2,1)S(1)} %get-tuple-element.24), channel_id=1, source_target_pairs={{0,8},{2,6},{8,16},{10,2},{16,24},{18,10},{24,28},{26,18},{28,20},... | collective-permute-start | bytes 393224 | tf_op jit(solution)/shard_map/ppermute | solution.py:342
  50.9 5.1 %collective-permute-start.30 = (bf16[128,512]{1,0:T(8,128)(2,1)S(1)}, bf16[128,512]{1,0:T(8,128)(2,1)S(1)}, u32[]{:S(2)}, u32[]{:S(2)}) collective-permute-start(bf16[128,512]{1,0:T(8,128)(2,1)S(1)} %collective-permute-done.28), channel_id=1, source_target_pairs={{0,8},{2,6},{8,16},{10,2},{16,24},{18,10},{24,28},{26,18},{28,20},... | collective-permute-start | bytes 393224 | tf_op jit(solution)/shard_map/ppermute | solution.py:342
  53.2 2.9 %collective-permute-start.29 = (bf16[128,512]{1,0:T(8,128)(2,1)S(1)}, bf16[128,512]{1,0:T(8,128)(2,1)S(1)}, u32[]{:S(2)}, u32[]{:S(2)}) collective-permute-start(bf16[128,512]{1,0:T(8,128)(2,1)S(1)} %collective-permute-done.28), channel_id=1, source_target_pairs={{0,2},{2,0},{4,6},{6,4},{8,10},{10,8},{12,14},{14,12},{16,18},{18,... | collective-permute-start | bytes 393224 | tf_op jit(solution)/shard_map/ppermute | solution.py:262
  53.2 5.1 %collective-permute-start.18 = (bf16[128,512]{1,0:T(8,128)(2,1)S(1)}, bf16[128,512]{1,0:T(8,128)(2,1)S(1)}, u32[]{:S(2)}, u32[]{:S(2)}) collective-permute-start(bf16[128,512]{1,0:T(8,128)(2,1)S(1)} %collective-permute-done.14), channel_id=1, source_target_pairs={{0,8},{2,6},{8,16},{10,2},{16,24},{18,10},{24,28},{26,18},{28,20},... | collective-permute-start | bytes 393224 | tf_op jit(solution)/shard_map/ppermute | solution.py:342
  55.3 2.9 %collective-permute-start.15 = (bf16[128,512]{1,0:T(8,128)(2,1)S(1)}, bf16[128,512]{1,0:T(8,128)(2,1)S(1)}, u32[]{:S(2)}, u32[]{:S(2)}) collective-permute-start(bf16[128,512]{1,0:T(8,128)(2,1)S(1)} %collective-permute-done.14), channel_id=1, source_target_pairs={{0,2},{2,0},{4,6},{6,4},{8,10},{10,8},{12,14},{14,12},{16,18},{18,... | collective-permute-start | bytes 393224 | tf_op jit(solution)/shard_map/ppermute | solution.py:262
  55.3 6.4 %collective-permute-start.20 = (bf16[128,512]{1,0:T(8,128)(2,1)S(1)}, bf16[128,512]{1,0:T(8,128)(2,1)S(1)}, u32[]{:S(2)}, u32[]{:S(2)}) collective-permute-start(bf16[128,512]{1,0:T(8,128)(2,1)S(1)} %collective-permute-done.16), channel_id=1, source_target_pairs={{0,8},{2,6},{8,16},{10,2},{16,24},{18,10},{24,28},{26,18},{28,20},... | collective-permute-start | bytes 393224 | tf_op jit(solution)/shard_map/ppermute | solution.py:342
  56.1 4.4 %collective-permute-start.17 = (bf16[128,512]{1,0:T(8,128)(2,1)S(1)}, bf16[128,512]{1,0:T(8,128)(2,1)S(1)}, u32[]{:S(2)}, u32[]{:S(2)}) collective-permute-start(bf16[128,512]{1,0:T(8,128)(2,1)S(1)} %collective-permute-done.16), channel_id=1, source_target_pairs={{0,2},{2,0},{4,6},{6,4},{8,10},{10,8},{12,14},{14,12},{16,18},{18,... | collective-permute-start | bytes 393224 | tf_op jit(solution)/shard_map/ppermute | solution.py:262
  56.1 6.8 %collective-permute-start.34 = (bf16[128,512]{1,0:T(8,128)(2,1)S(1)}, bf16[128,512]{1,0:T(8,128)(2,1)S(1)}, u32[]{:S(2)}, u32[]{:S(2)}) collective-permute-start(bf16[128,512]{1,0:T(8,128)(2,1)S(1)} %collective-permute-done.30), channel_id=1, source_target_pairs={{0,8},{2,6},{8,16},{10,2},{16,24},{18,10},{24,28},{26,18},{28,20},... | collective-permute-start | bytes 393224 | tf_op jit(solution)/shard_map/ppermute | solution.py:342
  58.2 3.6 %collective-permute-start.31 = (bf16[128,512]{1,0:T(8,128)(2,1)S(1)}, bf16[128,512]{1,0:T(8,128)(2,1)S(1)}, u32[]{:S(2)}, u32[]{:S(2)}) collective-permute-start(bf16[128,512]{1,0:T(8,128)(2,1)S(1)} %collective-permute-done.30), channel_id=1, source_target_pairs={{0,2},{2,0},{4,6},{6,4},{8,10},{10,8},{12,14},{14,12},{16,18},{18,... | collective-permute-start | bytes 393224 | tf_op jit(solution)/shard_map/ppermute | solution.py:262
  58.4 5.9 %collective-permute-start.32 = (bf16[128,512]{1,0:T(8,128)(2,1)S(1)}, bf16[128,512]{1,0:T(8,128)(2,1)S(1)}, u32[]{:S(2)}, u32[]{:S(2)}) collective-permute-start(bf16[128,512]{1,0:T(8,128)(2,1)S(1)} %collective-permute-done.29), channel_id=1, source_target_pairs={{0,8},{2,6},{8,16},{10,2},{16,24},{18,10},{24,28},{26,18},{28,20},... | collective-permute-start | bytes 393224 | tf_op jit(solution)/shard_map/ppermute | solution.py:342
  60.5 5.0 %collective-permute-start.22 = (bf16[128,512]{1,0:T(8,128)(2,1)S(1)}, bf16[128,512]{1,0:T(8,128)(2,1)S(1)}, u32[]{:S(2)}, u32[]{:S(2)}) collective-permute-start(bf16[128,512]{1,0:T(8,128)(2,1)S(1)} %collective-permute-done.18), channel_id=1, source_target_pairs={{0,8},{2,6},{8,16},{10,2},{16,24},{18,10},{24,28},{26,18},{28,20},... | collective-permute-start | bytes 393224 | tf_op jit(solution)/shard_map/ppermute | solution.py:342
  61.7 1.4 %collective-permute-start.19 = (bf16[128,512]{1,0:T(8,128)(2,1)S(1)}, bf16[128,512]{1,0:T(8,128)(2,1)S(1)}, u32[]{:S(2)}, u32[]{:S(2)}) collective-permute-start(bf16[128,512]{1,0:T(8,128)(2,1)S(1)} %collective-permute-done.18), channel_id=1, source_target_pairs={{0,2},{2,0},{4,6},{6,4},{8,10},{10,8},{12,14},{14,12},{16,18},{18,... | collective-permute-start | bytes 393224 | tf_op jit(solution)/shard_map/ppermute | solution.py:262
  61.8 6.3 %collective-permute-start.24 = (bf16[128,512]{1,0:T(8,128)(2,1)S(1)}, bf16[128,512]{1,0:T(8,128)(2,1)S(1)}, u32[]{:S(2)}, u32[]{:S(2)}) collective-permute-start(bf16[128,512]{1,0:T(8,128)(2,1)S(1)} %collective-permute-done.20), channel_id=1, source_target_pairs={{0,8},{2,6},{8,16},{10,2},{16,24},{18,10},{24,28},{26,18},{28,20},... | collective-permute-start | bytes 393224 | tf_op jit(solution)/shard_map/ppermute | solution.py:342
  63.0 1.4 %collective-permute-start.21 = (bf16[128,512]{1,0:T(8,128)(2,1)S(1)}, bf16[128,512]{1,0:T(8,128)(2,1)S(1)}, u32[]{:S(2)}, u32[]{:S(2)}) collective-permute-start(bf16[128,512]{1,0:T(8,128)(2,1)S(1)} %collective-permute-done.20), channel_id=1, source_target_pairs={{0,2},{2,0},{4,6},{6,4},{8,10},{10,8},{12,14},{14,12},{16,18},{18,... | collective-permute-start | bytes 393224 | tf_op jit(solution)/shard_map/ppermute | solution.py:262
  63.1 5.1 %collective-permute-start.38 = (bf16[128,512]{1,0:T(8,128)(2,1)S(1)}, bf16[128,512]{1,0:T(8,128)(2,1)S(1)}, u32[]{:S(2)}, u32[]{:S(2)}) collective-permute-start(bf16[128,512]{1,0:T(8,128)(2,1)S(1)} %collective-permute-done.34), channel_id=1, source_target_pairs={{0,8},{2,6},{8,16},{10,2},{16,24},{18,10},{24,28},{26,18},{28,20},... | collective-permute-start | bytes 393224 | tf_op jit(solution)/shard_map/ppermute | solution.py:342
  64.3 4.4 %collective-permute-start.35 = (bf16[128,512]{1,0:T(8,128)(2,1)S(1)}, bf16[128,512]{1,0:T(8,128)(2,1)S(1)}, u32[]{:S(2)}, u32[]{:S(2)}) collective-permute-start(bf16[128,512]{1,0:T(8,128)(2,1)S(1)} %collective-permute-done.34), channel_id=1, source_target_pairs={{0,2},{2,0},{4,6},{6,4},{8,10},{10,8},{12,14},{14,12},{16,18},{18,... | collective-permute-start | bytes 393224 | tf_op jit(solution)/shard_map/ppermute | solution.py:262
  64.4 2.5 %collective-permute-start.33 = (bf16[128,512]{1,0:T(8,128)(2,1)S(1)}, bf16[128,512]{1,0:T(8,128)(2,1)S(1)}, u32[]{:S(2)}, u32[]{:S(2)}) collective-permute-start(bf16[128,512]{1,0:T(8,128)(2,1)S(1)} %collective-permute-done.32), channel_id=1, source_target_pairs={{0,2},{2,0},{4,6},{6,4},{8,10},{10,8},{12,14},{14,12},{16,18},{18,... | collective-permute-start | bytes 393224 | tf_op jit(solution)/shard_map/ppermute | solution.py:262
  65.5 5.0 %collective-permute-start.36 = (bf16[128,512]{1,0:T(8,128)(2,1)S(1)}, bf16[128,512]{1,0:T(8,128)(2,1)S(1)}, u32[]{:S(2)}, u32[]{:S(2)}) collective-permute-start(bf16[128,512]{1,0:T(8,128)(2,1)S(1)} %collective-permute-done.32), channel_id=1, source_target_pairs={{0,8},{2,6},{8,16},{10,2},{16,24},{18,10},{24,28},{26,18},{28,20},... | collective-permute-start | bytes 393224 | tf_op jit(solution)/shard_map/ppermute | solution.py:342
  66.9 5.0 %collective-permute-start.26 = (bf16[128,512]{1,0:T(8,128)(2,1)S(1)}, bf16[128,512]{1,0:T(8,128)(2,1)S(1)}, u32[]{:S(2)}, u32[]{:S(2)}) collective-permute-start(bf16[128,512]{1,0:T(8,128)(2,1)S(1)} %collective-permute-done.22), channel_id=1, source_target_pairs={{0,8},{2,6},{8,16},{10,2},{16,24},{18,10},{24,28},{26,18},{28,20},... | collective-permute-start | bytes 393224 | tf_op jit(solution)/shard_map/ppermute | solution.py:342
  68.1 2.3 %collective-permute-start.23 = (bf16[128,512]{1,0:T(8,128)(2,1)S(1)}, bf16[128,512]{1,0:T(8,128)(2,1)S(1)}, u32[]{:S(2)}, u32[]{:S(2)}) collective-permute-start(bf16[128,512]{1,0:T(8,128)(2,1)S(1)} %collective-permute-done.22), channel_id=1, source_target_pairs={{0,2},{2,0},{4,6},{6,4},{8,10},{10,8},{12,14},{14,12},{16,18},{18,... | collective-permute-start | bytes 393224 | tf_op jit(solution)/shard_map/ppermute | solution.py:262
  68.3 3.7 %collective-permute-start.25 = (bf16[128,512]{1,0:T(8,128)(2,1)S(1)}, bf16[128,512]{1,0:T(8,128)(2,1)S(1)}, u32[]{:S(2)}, u32[]{:S(2)}) collective-permute-start(bf16[128,512]{1,0:T(8,128)(2,1)S(1)} %collective-permute-done.24), channel_id=1, source_target_pairs={{0,2},{2,0},{4,6},{6,4},{8,10},{10,8},{12,14},{14,12},{16,18},{18,... | collective-permute-start | bytes 393224 | tf_op jit(solution)/shard_map/ppermute | solution.py:262
  68.7 5.0 %collective-permute-start.42 = (bf16[128,512]{1,0:T(8,128)(2,1)S(1)}, bf16[128,512]{1,0:T(8,128)(2,1)S(1)}, u32[]{:S(2)}, u32[]{:S(2)}) collective-permute-start(bf16[128,512]{1,0:T(8,128)(2,1)S(1)} %collective-permute-done.38), channel_id=1, source_target_pairs={{0,8},{2,6},{8,16},{10,2},{16,24},{18,10},{24,28},{26,18},{28,20},... | collective-permute-start | bytes 393224 | tf_op jit(solution)/shard_map/ppermute | solution.py:342
  70.4 5.0 %collective-permute-start.39 = (bf16[128,512]{1,0:T(8,128)(2,1)S(1)}, bf16[128,512]{1,0:T(8,128)(2,1)S(1)}, u32[]{:S(2)}, u32[]{:S(2)}) collective-permute-start(bf16[128,512]{1,0:T(8,128)(2,1)S(1)} %collective-permute-done.38), channel_id=1, source_target_pairs={{0,2},{2,0},{4,6},{6,4},{8,10},{10,8},{12,14},{14,12},{16,18},{18,... | collective-permute-start | bytes 393224 | tf_op jit(solution)/shard_map/ppermute | solution.py:262
  70.4 5.0 %collective-permute-start.40 = (bf16[128,512]{1,0:T(8,128)(2,1)S(1)}, bf16[128,512]{1,0:T(8,128)(2,1)S(1)}, u32[]{:S(2)}, u32[]{:S(2)}) collective-permute-start(bf16[128,512]{1,0:T(8,128)(2,1)S(1)} %collective-permute-done.36), channel_id=1, source_target_pairs={{0,8},{2,6},{8,16},{10,2},{16,24},{18,10},{24,28},{26,18},{28,20},... | collective-permute-start | bytes 393224 | tf_op jit(solution)/shard_map/ppermute | solution.py:342
  71.9 3.5 %collective-permute-start.37 = (bf16[128,512]{1,0:T(8,128)(2,1)S(1)}, bf16[128,512]{1,0:T(8,128)(2,1)S(1)}, u32[]{:S(2)}, u32[]{:S(2)}) collective-permute-start(bf16[128,512]{1,0:T(8,128)(2,1)S(1)} %collective-permute-done.36), channel_id=1, source_target_pairs={{0,2},{2,0},{4,6},{6,4},{8,10},{10,8},{12,14},{14,12},{16,18},{18,... | collective-permute-start | bytes 393224 | tf_op jit(solution)/shard_map/ppermute | solution.py:262
  72.0 4.8 %collective-permute-start.27 = (bf16[128,512]{1,0:T(8,128)(2,1)S(1)}, bf16[128,512]{1,0:T(8,128)(2,1)S(1)}, u32[]{:S(2)}, u32[]{:S(2)}) collective-permute-start(bf16[128,512]{1,0:T(8,128)(2,1)S(1)} %collective-permute-done.26), channel_id=1, source_target_pairs={{0,2},{2,0},{4,6},{6,4},{8,10},{10,8},{12,14},{14,12},{16,18},{18,... | collective-permute-start | bytes 393224 | tf_op jit(solution)/shard_map/ppermute | solution.py:262
  73.7 3.2 %collective-permute-start.43 = (bf16[128,512]{1,0:T(8,128)(2,1)S(1)}, bf16[128,512]{1,0:T(8,128)(2,1)S(1)}, u32[]{:S(2)}, u32[]{:S(2)}) collective-permute-start(bf16[128,512]{1,0:T(8,128)(2,1)S(1)} %collective-permute-done.42), channel_id=1, source_target_pairs={{0,2},{2,0},{4,6},{6,4},{8,10},{10,8},{12,14},{14,12},{16,18},{18,... | collective-permute-start | bytes 393224 | tf_op jit(solution)/shard_map/ppermute | solution.py:262
  75.4 1.3 %collective-permute-start.41 = (bf16[128,512]{1,0:T(8,128)(2,1)S(1)}, bf16[128,512]{1,0:T(8,128)(2,1)S(1)}, u32[]{:S(2)}, u32[]{:S(2)}) collective-permute-start(bf16[128,512]{1,0:T(8,128)(2,1)S(1)} %collective-permute-done.40), channel_id=1, source_target_pairs={{0,2},{2,0},{4,6},{6,4},{8,10},{10,8},{12,14},{14,12},{16,18},{18,... | collective-permute-start | bytes 393224 | tf_op jit(solution)/shard_map/ppermute | solution.py:262

commit v6 on v5

--- a/solution.py
+++ b/solution.py
@@ -126,42 +126,51 @@
     return jnp.sum(jnp.sum(array, axis=0, keepdims=True), axis=1, keepdims=True)
 
 
-def newton_step(state):
-    excess = product(state, state) * (1.0 / 16.0) - 0.625 * state
-    growth = 3.125 * excess + product(excess, excess)
-    return (625.0 / 256.0) * state + product(state, growth)
-
-
-def newton_kernel(side_ref, mine_ref, other_ref, tile_ref, root_ref, stat_ref):
-    tile = mine_ref[...] + other_ref[...]
+def newton_step(states):
+    excesses = [product(m, m) * (1.0 / 16.0) - 0.625 * m for m in states]
+    growths = [3.125 * e + product(e, e) for e in excesses]
+    return [(625.0 / 256.0) * m + product(m, g) for m, g in zip(states, growths)]
+
+
+def inverse_roots(tile):
     tile_half = tile.astype(jnp.bfloat16)
-    tile_ref[...] = tile_half
-
-    @pl.when(side_ref[0] == 0)
-    def _():
-        stat_ref[...] = contract(tile_half, tile_half, 1, 1)
-
-    @pl.when(side_ref[0] != 0)
-    def _():
-        stat_ref[...] = contract(tile_half, tile_half, 0, 0)
-
     order = tile.shape[0]
     row_ids = lax.broadcasted_iota(jnp.int32, (order, order), 0)
     col_ids = lax.broadcasted_iota(jnp.int32, (order, order), 1)
     on_diagonal = row_ids == col_ids
     damp = (DAMPING / order) * total(tile * tile)
-    matrix = stat_ref[...]
-    matrix = jnp.where(on_diagonal, matrix + damp, matrix)
-    norm = jnp.sqrt(total(matrix * matrix))
-    first = matrix / norm
-    second = newton_step(first)
-    third = newton_step(second)
-    cross = product(first, second) * (1.0 / 16.0) - (5.0 / 16.0) * (first + second)
-    last = product(cross, third)
-    root = 1.25 * cross - 0.25 * last - (25.0 / 64.0) * third
-    root = jnp.where(on_diagonal, root + 125.0 / 64.0, root)
-    scale = 1.0 / jnp.sqrt(jnp.sqrt(norm))
-    root_ref[...] = (root * scale).astype(jnp.bfloat16)
+    stats = [contract(tile_half, tile_half, 1, 1), contract(tile_half, tile_half, 0, 0)]
+    stats = [jnp.where(on_diagonal, stat + damp, stat) for stat in stats]
+    norms = [jnp.sqrt(total(stat * stat)) for stat in stats]
+    firsts = [stat / norm for stat, norm in zip(stats, norms)]
+    seconds = newton_step(firsts)
+    thirds = newton_step(seconds)
+    crosses = [
+        product(m, n) * (1.0 / 16.0) - (5.0 / 16.0) * (m + n) for m, n in zip(firsts, seconds)
+    ]
+    roots = []
+    for cross, third, norm in zip(crosses, thirds, norms):
+        root = 1.25 * cross - 0.25 * product(cross, third) - (25.0 / 64.0) * third
+        root = jnp.where(on_diagonal, root + 125.0 / 64.0, root)
+        roots.append((root / jnp.sqrt(jnp.sqrt(norm))).astype(jnp.bfloat16))
+    return roots
+
+
+def update_kernel(side_ref, mine_ref, other_ref, near_ref, next_ref, far_ref, left_ref):
+    tile = mine_ref[...] + other_ref[...]
+    tile_half = tile.astype(jnp.bfloat16)
+    left_ref[...], right = inverse_roots(tile)
+    rows = near_ref.shape[0]
+    core, plane = side_ref[0], side_ref[1]
+    for out_ref, part in (
+        (near_ref, 2 * plane + core),
+        (next_ref, 2 * plane + 1 - core),
+        (far_ref, 2 * (1 - plane) + core),
+    ):
+        left = left_ref[pl.ds(pl.multiple_of(part * rows, rows), rows), :]
+        half = contract(left, tile_half, 1, 0).astype(jnp.bfloat16)
+        piece = contract(half, right, 1, 0) * math.sqrt(BLOCK)
+        out_ref[...] = piece.astype(jnp.bfloat16)
 
 
 OFFSETS = ((4, 7, 1, 2), (5, 6, 3, 2))
@@ -204,31 +213,6 @@
         for part, source in enumerate((band ^ offset, band ^ offset ^ 4)):
             put(cot_ref, pair_ref.at[pl.ds(part * tokens, tokens)], source, 0)
     partial_ref[...] = contract(band_ref[...], cot_ref[...], 0, 0)
-
-
-def update_kernel(side_ref, mine_ref, other_ref, tile_ref, near_ref, next_ref, far_ref):
-    rows = near_ref.shape[0]
-    tile = tile_ref[...]
-    core, plane = side_ref[0], side_ref[1]
-
-    def write(left_ref, right_ref):
-        for out_ref, part in (
-            (near_ref, 2 * plane + core),
-            (next_ref, 2 * plane + 1 - core),
-            (far_ref, 2 * (1 - plane) + core),
-        ):
-            left = left_ref[pl.ds(pl.multiple_of(part * rows, rows), rows), :]
-            half = contract(left, tile, 1, 0).astype(jnp.bfloat16)
-            piece = contract(half, right_ref[...], 1, 0) * math.sqrt(BLOCK)
-            out_ref[...] = piece.astype(jnp.bfloat16)
-
-    @pl.when(core == 0)
-    def _():
-        write(mine_ref, other_ref)
-
-    @pl.when(core != 0)
-    def _():
-        write(other_ref, mine_ref)
 
 
 def call(kernel, out_shapes, scratch_shapes, *operands):
@@ -310,27 +294,14 @@
     )
     other_partial = swap_core(partial_tile)
     side = jnp.stack([core, plane]).astype(jnp.int32)
-    tile_half, root = call(
-        newton_kernel,
-        [
-            jax.ShapeDtypeStruct((BLOCK, BLOCK), jnp.bfloat16),
-            jax.ShapeDtypeStruct((BLOCK, BLOCK), jnp.bfloat16),
-        ],
-        [pltpu.VMEM((BLOCK, BLOCK), jnp.float32)],
-        side,
-        partial_tile,
-        other_partial,
-    )
-    other_root = swap_core(root)
     rows = BLOCK // members // cores
     near_piece, next_piece, far_piece = call(
         update_kernel,
         [jax.ShapeDtypeStruct((rows, BLOCK), jnp.bfloat16)] * 3,
-        [],
+        [pltpu.VMEM((BLOCK, BLOCK), jnp.bfloat16)],
         side,
-        root,
-        other_root,
-        tile_half,
+        partial_tile,
+        other_partial,
     )
 
     def turn(array):

time: 79.8 us -> 79.4 us (level)
  waiting for transfers between devices: 14.8 us -> 12.9 us
  Pallas kernels: 7.76 us -> 9.42 us
    ppermute x17 -> x16, waiting for transfers between devices: 5.55 us -> 3.65 us  [swap_core(): return lax.ppermute(array, 'dp', [(g, g ^ 1) for g in range(groups)])]
    pallas_call x4 -> x3, Pallas kernels: 7.76 us -> 9.42 us  [call(): pl.pallas_call(kernel, out_shape=out_shapes, in_specs=in_specs, out_specs...]
    ppermute x17 -> x16, starting transfers between devices: 2.21 us -> 1.97 us  [swap_core(): return lax.ppermute(array, 'dp', [(g, g ^ 1) for g in range(groups)])]
  transfers between devices with their start and end apart: 44 -> 43, of which waited for: 14 -> 13; matrix products, arithmetic and copies ran while one was open for 6% -> 6% of each run, Pallas kernels for 1% -> 1%
where the time goes in v6:
time: 79.4 us; the launch traced here: 79.2 us
  starting transfers between devices  46.9 us (59%)
  waiting for transfers between devices  12.9 us (16%)
  Pallas kernels  9.42 us (12%)
  matrix products  3.57 us (4%)
  other arithmetic  2.81 us (4%)
  local copies, waits for them, and re-layouts  2.23 us (3%)
  between operations  1.37 us (2%)
    ppermute x14, starting transfers between devices, turn(): return lax.ppermute(array, 'dp', pairs)  20.2 us
    ppermute x5, starting transfers between devices, swap_plane(): lax.ppermute(array, 'pre', [(c, members - 1 - c) for c in range(members)])  11.4 us
    pallas_call x3, Pallas kernels, call(): pl.pallas_call(kernel, out_shape=out_shapes, in_specs=in_specs, out_specs...  9.42 us
    ppermute x4, starting transfers between devices, exchange(): return lax.ppermute(array, 'dp', pairs)  7.49 us
    ppermute x4, starting transfers between devices, deal(): return lax.ppermute(array, ('dp', 'pre'), pairs)  5.91 us
    ppermute x5, waiting for transfers between devices, swap_plane(): lax.ppermute(array, 'pre', [(c, members - 1 - c) for c in range(members)])  4.94 us
    ppermute x14, waiting for transfers between devices, turn(): return lax.ppermute(array, 'dp', pairs)  4.21 us
    ppermute x16, waiting for transfers between devices, swap_core(): return lax.ppermute(array, 'dp', [(g, g ^ 1) for g in range(groups)])  3.65 us
  transfers between devices with their start and end apart: 43, of which 13 were waited for; matrix products, arithmetic and copies ran while one was open for 6% of the time, Pallas kernels for 1%

profile of v6, /device:TPU:0, one launch (start us, length us, event | category | flops | bytes accessed | tf_op | source)
XLA Modules:
  0.0 79.2 jit_solution(13139144464492975696)
XLA Ops:
  0.6 4.1 %collective-permute-start = (bf16[128,512]{1,0:T(8,128)(2,1)}, bf16[128,512]{1,0:T(8,128)(2,1)S(1)}, u32[]{:S(2)}, u32[]{:S(2)}) collective-permute-start(bf16[128,512]{1,0:T(8,128)(2,1)} %param.5), channel_id=1, source_target_pairs={{0,16},{2,18},{4,20},{6,22},{8,24},{10,26},{12,28},{14,30},{16,0},... | collective-permute-start | bytes 393224 | tf_op jit(solution)/shard_map/ppermute | solution.py:277
  4.8 1.2 %copy-done = bf16[128,4096]{1,0:T(8,128)(2,1)S(1)} copy-done((bf16[128,4096]{1,0:T(8,128)(2,1)S(1)}, bf16[128,4096]{1,0:T(8,128)(2,1)}, u32[]{:S(2)}) %copy-start) | copy-done | bytes 1048600
  6.0 0.6 shard_map.50
  6.6 1.6 %collective-permute-start.4 = (bf16[64,512]{1,0:T(8,128)(2,1)S(1)}, bf16[64,512]{1,0:T(8,128)(2,1)S(1)}, u32[]{:S(2)}, u32[]{:S(2)}) collective-permute-start(bf16[64,512]{1,0:T(8,128)(2,1)S(1)} %get-tuple-element.17), channel_id=1, source_target_pairs={{0,8},{1,9},{2,10},{3,11},{4,12},{5,13},{6,14},{7,15},{8,0},{9,1},... | collective-permute-start | bytes 196616 | tf_op jit(solution)/shard_map/ppermute | solution.py:261
  8.3 0.3 collective-permute-start.1
  8.6 3.4 %collective-permute-start.2 = (bf16[128,512]{1,0:T(8,128)(2,1)S(1)}, bf16[128,512]{1,0:T(8,128)(2,1)S(1)}, u32[]{:S(2)}, u32[]{:S(2)}) collective-permute-start(bf16[128,512]{1,0:T(8,128)(2,1)S(1)} %get-tuple-element.15), channel_id=1, source_target_pairs={{0,28},{1,25},{2,30},{3,27},{4,24},{5,29},{6,26},{7,31},{8,20},{9,... | collective-permute-start | bytes 393224 | tf_op jit(solution)/shard_map/ppermute | solution.py:261
  12.0 0.5 collective-permute-start.3
  12.6 3.6 %convolution_convert_fusion = bf16[128,512]{1,0:T(8,128)(2,1)} fusion(bf16[128,4096]{1,0:T(8,128)(2,1)S(1)} %copy-done, bf16[4096,512]{1,0:T(8,128)(2,1)} %param.4), kind=kOutput, calls=%fused_computation.1 | convolution fusion | flops 536936448 | bytes 5373952 | tf_op jit(solution)/shard_map/dot_general | solution.py:279
  16.1 1.7 %collective-permute-start.8 = (bf16[64,512]{1,0:T(8,128)(2,1)S(1)}, bf16[64,512]{1,0:T(8,128)(2,1)S(1)}, u32[]{:S(2)}, u32[]{:S(2)}) collective-permute-start(bf16[64,512]{1,0:T(8,128)(2,1)S(1)} %collective-permute-done.4.refs_3_), channel_id=1, source_target_pairs={{0,1},{1,0},{2,3},{3,2},{4,5},{5,4},{6,7},{7,6},{8,9},{9,8},{10,11... | collective-permute-start | bytes 196616 | tf_op jit(solution)/shard_map/ppermute | solution.py:249
  17.8 2.4 %collective-permute-start.11 = (bf16[256,512]{1,0:T(8,128)(2,1)S(1)}, bf16[256,512]{1,0:T(8,128)(2,1)S(1)}, u32[]{:S(2)}, u32[]{:S(2)}) collective-permute-start(bf16[256,512]{1,0:T(8,128)(2,1)S(1)} %constant_dynamic-update-slice_fusion.refs_8_), channel_id=1, source_target_pairs={{0,12},{2,14},{4,8},{6,10},{8,4},{10,6},{12,0},{14,2},{16,28},{18,... | collective-permute-start | bytes 786440 | tf_op jit(solution)/shard_map/ppermute | solution.py:277
  20.2 2.3 %collective-permute-start.5 = (bf16[128,512]{1,0:T(8,128)(2,1)S(1)}, bf16[128,512]{1,0:T(8,128)(2,1)S(1)}, u32[]{:S(2)}, u32[]{:S(2)}) collective-permute-start(bf16[128,512]{1,0:T(8,128)(2,1)S(1)} %collective-permute-done.1.refs_0_), channel_id=1, source_target_pairs={{0,1},{1,0},{2,3},{3,2},{4,5},{5,4},{6,7},{7,6},{8,9},{9,8},{10,11... | collective-permute-start | bytes 393224 | tf_op jit(solution)/shard_map/ppermute | solution.py:249
  22.5 1.0 %collective-permute-start.9 = (bf16[256,512]{1,0:T(8,128)(2,1)S(1)}, bf16[256,512]{1,0:T(8,128)(2,1)S(1)}, u32[]{:S(2)}, u32[]{:S(2)}) collective-permute-start(bf16[256,512]{1,0:T(8,128)(2,1)S(1)} %constant_dynamic-update-slice_fusion.refs_8_), channel_id=1, source_target_pairs={{0,4},{2,6},{4,0},{6,2},{8,12},{10,14},{12,8},{14,10},{16,20},{18,... | collective-permute-start | bytes 786440 | tf_op jit(solution)/shard_map/ppermute | solution.py:277
  23.5 1.7 %collective-permute-start.6 = (bf16[128,512]{1,0:T(8,128)(2,1)S(1)}, bf16[128,512]{1,0:T(8,128)(2,1)S(1)}, u32[]{:S(2)}, u32[]{:S(2)}) collective-permute-start(bf16[128,512]{1,0:T(8,128)(2,1)S(1)} %collective-permute-done.2.refs_1_), channel_id=1, source_target_pairs={{0,1},{1,0},{2,3},{3,2},{4,5},{5,4},{6,7},{7,6},{8,9},{9,8},{10,11... | collective-permute-start | bytes 393224 | tf_op jit(solution)/shard_map/ppermute | solution.py:249
  25.2 1.2 %collective-permute-done.5.refs_4_ = bf16[128,512]{1,0:T(8,128)(2,1)S(1)} collective-permute-done((bf16[128,512]{1,0:T(8,128)(2,1)S(1)}, bf16[128,512]{1,0:T(8,128)(2,1)S(1)}, u32[]{:S(2)}, u32[]{:S(2)}) %collective-permute-start.5) | collective-permute-done | bytes 131104 | tf_op jit(solution)/shard_map/ppermute | solution.py:249
  26.4 2.5 %collective-permute-start.7 = (bf16[128,512]{1,0:T(8,128)(2,1)S(1)}, bf16[128,512]{1,0:T(8,128)(2,1)S(1)}, u32[]{:S(2)}, u32[]{:S(2)}) collective-permute-start(bf16[128,512]{1,0:T(8,128)(2,1)S(1)} %collective-permute-done.3.refs_2_), channel_id=1, source_target_pairs={{0,1},{1,0},{2,3},{3,2},{4,5},{5,4},{6,7},{7,6},{8,9},{9,8},{10,11... | collective-permute-start | bytes 393224 | tf_op jit(solution)/shard_map/ppermute | solution.py:249
  29.0 0.8 collective-permute-done.6.refs_5_
  29.7 2.1 %collective-permute-done.7.refs_6_ = bf16[128,512]{1,0:T(8,128)(2,1)S(1)} collective-permute-done((bf16[128,512]{1,0:T(8,128)(2,1)S(1)}, bf16[128,512]{1,0:T(8,128)(2,1)S(1)}, u32[]{:S(2)}, u32[]{:S(2)}) %collective-permute-start.7) | collective-permute-done | bytes 131104 | tf_op jit(solution)/shard_map/ppermute | solution.py:249
  31.9 1.4 %shard_map.51.mine_ref = f32[512,512]{1,0:T(8,128)S(1)} custom-call(s32[2]{0:T(128)S(1)} %pad_add_fusion.1.place_ref, bf16[128,512]{1,0:T(8,128)(2,1)S(1)} %get-tuple-element.13.own_ref, bf16[128,512]{1,0:T(8,128)(2,1)S(1)} %collective-permute-done.1.refs_0_, bf16[128,512]{1,0:T(8,128)(2,1)S(1)} %collective-permute-done.2.refs_1_, ...), custom_call_target="tpu_custom_call" | custom-call | tf_op jit(solution)/shard_map/pallas_call | solution.py:221
  33.8 2.3 %collective-permute-done.12.other_ref = f32[512,512]{1,0:T(8,128)S(1)} collective-permute-done((f32[512,512]{1,0:T(8,128)S(1)}, f32[512,512]{1,0:T(8,128)S(1)}, u32[]{:S(2)}, u32[]{:S(2)}) %collective-permute-start.12) | collective-permute-done | bytes 1048608 | tf_op jit(solution)/shard_map/ppermute | solution.py:246
  36.0 7.4 %shard_map.52 = (bf16[128,512]{1,0:T(8,128)(2,1)S(1)}, bf16[128,512]{1,0:T(8,128)(2,1)S(1)}, bf16[128,512]{1,0:T(8,128)(2,1)S(1)}) custom-call(s32[2]{0:T(128)S(1)} %pad_add_fusion.side_ref, f32[512,512]{1,0:T(8,128)S(1)} %shard_map.51.mine_ref, f32[512,512]{1,0:T(8,128)S(1)} %collective-permute-done.12.other_ref), custom_call_target="tpu_custom_call" | custom-call | tf_op jit(solution)/shard_map/pallas_call | solution.py:221
  43.5 3.3 %collective-permute-start.27 = (bf16[128,512]{1,0:T(8,128)(2,1)S(1)}, bf16[128,512]{1,0:T(8,128)(2,1)S(1)}, u32[]{:S(2)}, u32[]{:S(2)}) collective-permute-start(bf16[128,512]{1,0:T(8,128)(2,1)S(1)} %get-tuple-element.21), channel_id=1, source_target_pairs={{0,1},{1,0},{2,3},{3,2},{4,5},{5,4},{6,7},{7,6},{8,9},{9,8},{10,11... | collective-permute-start | bytes 393224 | tf_op jit(solution)/shard_map/ppermute | solution.py:249
  46.7 0.6 collective-permute-start.13
  47.4 2.1 %collective-permute-start.15 = (bf16[128,512]{1,0:T(8,128)(2,1)S(1)}, bf16[128,512]{1,0:T(8,128)(2,1)S(1)}, u32[]{:S(2)}, u32[]{:S(2)}) collective-permute-start(bf16[128,512]{1,0:T(8,128)(2,1)S(1)} %get-tuple-element.20), channel_id=1, source_target_pairs={{0,8},{2,6},{8,16},{10,2},{16,24},{18,10},{24,28},{26,18},{28,20},... | collective-permute-start | bytes 393224 | tf_op jit(solution)/shard_map/ppermute | solution.py:313
  49.5 0.2 broadcast_in_dim.99.clone.1
  49.7 0.8 %collective-permute-done.27 = bf16[128,512]{1,0:T(8,128)(2,1)S(1)} collective-permute-done((bf16[128,512]{1,0:T(8,128)(2,1)S(1)}, bf16[128,512]{1,0:T(8,128)(2,1)S(1)}, u32[]{:S(2)}, u32[]{:S(2)}) %collective-permute-start.27) | collective-permute-done | bytes 131104 | tf_op jit(solution)/shard_map/ppermute | solution.py:249
  50.5 2.3 %collective-permute-start.29 = (bf16[128,512]{1,0:T(8,128)(2,1)S(1)}, bf16[128,512]{1,0:T(8,128)(2,1)S(1)}, u32[]{:S(2)}, u32[]{:S(2)}) collective-permute-start(bf16[128,512]{1,0:T(8,128)(2,1)S(1)} %collective-permute-done.27), channel_id=1, source_target_pairs={{0,8},{2,6},{8,16},{10,2},{16,24},{18,10},{24,28},{26,18},{28,20},... | collective-permute-start | bytes 393224 | tf_op jit(solution)/shard_map/ppermute | solution.py:313
  52.8 2.1 %collective-permute-start.17 = (bf16[128,512]{1,0:T(8,128)(2,1)S(1)}, bf16[128,512]{1,0:T(8,128)(2,1)S(1)}, u32[]{:S(2)}, u32[]{:S(2)}) collective-permute-start(bf16[128,512]{1,0:T(8,128)(2,1)S(1)} %collective-permute-done.13), channel_id=1, source_target_pairs={{0,8},{2,6},{8,16},{10,2},{16,24},{18,10},{24,28},{26,18},{28,20},... | collective-permute-start | bytes 393224 | tf_op jit(solution)/shard_map/ppermute | solution.py:313
  54.9 0.5 collective-permute-start.19
  55.4 0.2 broadcast_in_dim.99.clone
  55.8 2.0 %collective-permute-start.33 = (bf16[128,512]{1,0:T(8,128)(2,1)S(1)}, bf16[128,512]{1,0:T(8,128)(2,1)S(1)}, u32[]{:S(2)}, u32[]{:S(2)}) collective-permute-start(bf16[128,512]{1,0:T(8,128)(2,1)S(1)} %collective-permute-done.29), channel_id=1, source_target_pairs={{0,8},{2,6},{8,16},{10,2},{16,24},{18,10},{24,28},{26,18},{28,20},... | collective-permute-start | bytes 393224 | tf_op jit(solution)/shard_map/ppermute | solution.py:313
  58.0 2.1 %collective-permute-start.31 = (bf16[128,512]{1,0:T(8,128)(2,1)S(1)}, bf16[128,512]{1,0:T(8,128)(2,1)S(1)}, u32[]{:S(2)}, u32[]{:S(2)}) collective-permute-start(bf16[128,512]{1,0:T(8,128)(2,1)S(1)} %collective-permute-done.28), channel_id=1, source_target_pairs={{0,8},{2,6},{8,16},{10,2},{16,24},{18,10},{24,28},{26,18},{28,20},... | collective-permute-start | bytes 393224 | tf_op jit(solution)/shard_map/ppermute | solution.py:313
  60.1 1.2 %collective-permute-start.21 = (bf16[128,512]{1,0:T(8,128)(2,1)S(1)}, bf16[128,512]{1,0:T(8,128)(2,1)S(1)}, u32[]{:S(2)}, u32[]{:S(2)}) collective-permute-start(bf16[128,512]{1,0:T(8,128)(2,1)S(1)} %collective-permute-done.17), channel_id=1, source_target_pairs={{0,8},{2,6},{8,16},{10,2},{16,24},{18,10},{24,28},{26,18},{28,20},... | collective-permute-start | bytes 393224 | tf_op jit(solution)/shard_map/ppermute | solution.py:313
  61.4 1.1 %collective-permute-start.23 = (bf16[128,512]{1,0:T(8,128)(2,1)S(1)}, bf16[128,512]{1,0:T(8,128)(2,1)S(1)}, u32[]{:S(2)}, u32[]{:S(2)}) collective-permute-start(bf16[128,512]{1,0:T(8,128)(2,1)S(1)} %collective-permute-done.19), channel_id=1, source_target_pairs={{0,8},{2,6},{8,16},{10,2},{16,24},{18,10},{24,28},{26,18},{28,20},... | collective-permute-start | bytes 393224 | tf_op jit(solution)/shard_map/ppermute | solution.py:313
  62.8 1.1 %collective-permute-start.37 = (bf16[128,512]{1,0:T(8,128)(2,1)S(1)}, bf16[128,512]{1,0:T(8,128)(2,1)S(1)}, u32[]{:S(2)}, u32[]{:S(2)}) collective-permute-start(bf16[128,512]{1,0:T(8,128)(2,1)S(1)} %collective-permute-done.33), channel_id=1, source_target_pairs={{0,8},{2,6},{8,16},{10,2},{16,24},{18,10},{24,28},{26,18},{28,20},... | collective-permute-start | bytes 393224 | tf_op jit(solution)/shard_map/ppermute | solution.py:313
  64.0 0.5 collective-permute-start.32
  64.5 0.6 collective-permute-done.21
  65.1 1.4 %collective-permute-start.35 = (bf16[128,512]{1,0:T(8,128)(2,1)S(1)}, bf16[128,512]{1,0:T(8,128)(2,1)S(1)}, u32[]{:S(2)}, u32[]{:S(2)}) collective-permute-start(bf16[128,512]{1,0:T(8,128)(2,1)S(1)} %collective-permute-done.31), channel_id=1, source_target_pairs={{0,8},{2,6},{8,16},{10,2},{16,24},{18,10},{24,28},{26,18},{28,20},... | collective-permute-start | bytes 393224 | tf_op jit(solution)/shard_map/ppermute | solution.py:313
  66.5 1.2 %collective-permute-start.25 = (bf16[128,512]{1,0:T(8,128)(2,1)S(1)}, bf16[128,512]{1,0:T(8,128)(2,1)S(1)}, u32[]{:S(2)}, u32[]{:S(2)}) collective-permute-start(bf16[128,512]{1,0:T(8,128)(2,1)S(1)} %collective-permute-done.21), channel_id=1, source_target_pairs={{0,8},{2,6},{8,16},{10,2},{16,24},{18,10},{24,28},{26,18},{28,20},... | collective-permute-start | bytes 393224 | tf_op jit(solution)/shard_map/ppermute | solution.py:313
  67.8 0.1 collective-permute-done.37
  67.9 0.4 collective-permute-start.24
  68.3 1.0 %collective-permute-start.41 = (bf16[128,512]{1,0:T(8,128)(2,1)S(1)}, bf16[128,512]{1,0:T(8,128)(2,1)S(1)}, u32[]{:S(2)}, u32[]{:S(2)}) collective-permute-start(bf16[128,512]{1,0:T(8,128)(2,1)S(1)} %collective-permute-done.37), channel_id=1, source_target_pairs={{0,8},{2,6},{8,16},{10,2},{16,24},{18,10},{24,28},{26,18},{28,20},... | collective-permute-start | bytes 393224 | tf_op jit(solution)/shard_map/ppermute | solution.py:313
  69.4 0.7 collective-permute-done.35
  70.1 1.4 %collective-permute-start.39 = (bf16[128,512]{1,0:T(8,128)(2,1)S(1)}, bf16[128,512]{1,0:T(8,128)(2,1)S(1)}, u32[]{:S(2)}, u32[]{:S(2)}) collective-permute-start(bf16[128,512]{1,0:T(8,128)(2,1)S(1)} %collective-permute-done.35), channel_id=1, source_target_pairs={{0,8},{2,6},{8,16},{10,2},{16,24},{18,10},{24,28},{26,18},{28,20},... | collective-permute-start | bytes 393224 | tf_op jit(solution)/shard_map/ppermute | solution.py:313
  71.6 0.5 collective-permute-start.26
  72.1 1.1 %collective-permute-done.41 = bf16[128,512]{1,0:T(8,128)(2,1)S(1)} collective-permute-done((bf16[128,512]{1,0:T(8,128)(2,1)S(1)}, bf16[128,512]{1,0:T(8,128)(2,1)S(1)}, u32[]{:S(2)}, u32[]{:S(2)}) %collective-permute-start.41) | collective-permute-done | bytes 131104 | tf_op jit(solution)/shard_map/ppermute | solution.py:313
  73.3 1.7 %collective-permute-done.39 = bf16[128,512]{1,0:T(8,128)(2,1)S(1)} collective-permute-done((bf16[128,512]{1,0:T(8,128)(2,1)S(1)}, bf16[128,512]{1,0:T(8,128)(2,1)S(1)}, u32[]{:S(2)}, u32[]{:S(2)}) %collective-permute-start.39) | collective-permute-done | bytes 131104 | tf_op jit(solution)/shard_map/ppermute | solution.py:313
  75.1 1.2 %collective-permute-done.40 = bf16[128,512]{1,0:T(8,128)(2,1)S(1)} collective-permute-done((bf16[128,512]{1,0:T(8,128)(2,1)S(1)}, bf16[128,512]{1,0:T(8,128)(2,1)S(1)}, u32[]{:S(2)}, u32[]{:S(2)}) %collective-permute-start.40) | collective-permute-done | bytes 131104 | tf_op jit(solution)/shard_map/ppermute | solution.py:246
  76.5 2.7 %maximum_select_fusion = bf16[8,256,1024]{2,1,0:T(8,128)(2,1)} fusion(bf16[8,256,512]{2,1,0:T(8,128)(2,1)S(1)} %bitcast.76, bf16[8,256,512]{2,1,0:T(8,128)(2,1)S(1)} %bitcast.77, pred[]{:T(512)S(6)} %eq.45), kind=kLoop, calls=%fused_computation | loop fusion | flops 18874368 | bytes 8388609 | tf_op jit(solution)/shard_map/jit(_where)/select_n | solution.py:335
  (85 shorter events, 1.6 us)
Async XLA Ops:
  0.6 17.2 %collective-permute-start = (bf16[128,512]{1,0:T(8,128)(2,1)}, bf16[128,512]{1,0:T(8,128)(2,1)S(1)}, u32[]{:S(2)}, u32[]{:S(2)}) collective-permute-start(bf16[128,512]{1,0:T(8,128)(2,1)} %param.5), channel_id=1, source_target_pairs={{0,16},{2,18},{4,20},{6,22},{8,24},{10,26},{12,28},{14,30},{16,0},... | collective-permute-start | bytes 393224 | tf_op jit(solution)/shard_map/ppermute | solution.py:277
  4.8 1.2 %copy-start = (bf16[128,4096]{1,0:T(8,128)(2,1)S(1)}, bf16[128,4096]{1,0:T(8,128)(2,1)}, u32[]{:S(2)}) copy-start(bf16[128,4096]{1,0:T(8,128)(2,1)} %inputs_ref.1) | copy-start | bytes 3145732
  6.6 9.5 %collective-permute-start.4 = (bf16[64,512]{1,0:T(8,128)(2,1)S(1)}, bf16[64,512]{1,0:T(8,128)(2,1)S(1)}, u32[]{:S(2)}, u32[]{:S(2)}) collective-permute-start(bf16[64,512]{1,0:T(8,128)(2,1)S(1)} %get-tuple-element.17), channel_id=1, source_target_pairs={{0,8},{1,9},{2,10},{3,11},{4,12},{5,13},{6,14},{7,15},{8,0},{9,1},... | collective-permute-start | bytes 196616 | tf_op jit(solution)/shard_map/ppermute | solution.py:261
  8.3 11.9 %collective-permute-start.1 = (bf16[128,512]{1,0:T(8,128)(2,1)S(1)}, bf16[128,512]{1,0:T(8,128)(2,1)S(1)}, u32[]{:S(2)}, u32[]{:S(2)}) collective-permute-start(bf16[128,512]{1,0:T(8,128)(2,1)S(1)} %get-tuple-element.14), channel_id=1, source_target_pairs={{0,16},{1,21},{2,18},{3,23},{4,20},{5,17},{6,22},{7,19},{8,24},{9,... | collective-permute-start | bytes 393224 | tf_op jit(solution)/shard_map/ppermute | solution.py:261
  8.6 13.9 %collective-permute-start.2 = (bf16[128,512]{1,0:T(8,128)(2,1)S(1)}, bf16[128,512]{1,0:T(8,128)(2,1)S(1)}, u32[]{:S(2)}, u32[]{:S(2)}) collective-permute-start(bf16[128,512]{1,0:T(8,128)(2,1)S(1)} %get-tuple-element.15), channel_id=1, source_target_pairs={{0,28},{1,25},{2,30},{3,27},{4,24},{5,29},{6,26},{7,31},{8,20},{9,... | collective-permute-start | bytes 393224 | tf_op jit(solution)/shard_map/ppermute | solution.py:261
  12.0 4.1 %copy-start.1 = (bf16[128,512]{1,0:T(8,128)(2,1)S(1)}, bf16[128,512]{1,0:T(8,128)(2,1)}, u32[]{:S(2)}) copy-start(bf16[128,512]{1,0:T(8,128)(2,1)} %param.5) | copy-start | bytes 393220
  12.0 11.5 %collective-permute-start.3 = (bf16[128,512]{1,0:T(8,128)(2,1)S(1)}, bf16[128,512]{1,0:T(8,128)(2,1)S(1)}, u32[]{:S(2)}, u32[]{:S(2)}) collective-permute-start(bf16[128,512]{1,0:T(8,128)(2,1)S(1)} %get-tuple-element.16), channel_id=1, source_target_pairs={{0,4},{1,13},{2,6},{3,15},{4,0},{5,9},{6,2},{7,11},{8,12},{9,5},{1... | collective-permute-start | bytes 393224 | tf_op jit(solution)/shard_map/ppermute | solution.py:261
  16.1 6.3 %collective-permute-start.8 = (bf16[64,512]{1,0:T(8,128)(2,1)S(1)}, bf16[64,512]{1,0:T(8,128)(2,1)S(1)}, u32[]{:S(2)}, u32[]{:S(2)}) collective-permute-start(bf16[64,512]{1,0:T(8,128)(2,1)S(1)} %collective-permute-done.4.refs_3_), channel_id=1, source_target_pairs={{0,1},{1,0},{2,3},{3,2},{4,5},{5,4},{6,7},{7,6},{8,9},{9,8},{10,11... | collective-permute-start | bytes 196616 | tf_op jit(solution)/shard_map/ppermute | solution.py:249
  17.8 14.0 %collective-permute-start.11 = (bf16[256,512]{1,0:T(8,128)(2,1)S(1)}, bf16[256,512]{1,0:T(8,128)(2,1)S(1)}, u32[]{:S(2)}, u32[]{:S(2)}) collective-permute-start(bf16[256,512]{1,0:T(8,128)(2,1)S(1)} %constant_dynamic-update-slice_fusion.refs_8_), channel_id=1, source_target_pairs={{0,12},{2,14},{4,8},{6,10},{8,4},{10,6},{12,0},{14,2},{16,28},{18,... | collective-permute-start | bytes 786440 | tf_op jit(solution)/shard_map/ppermute | solution.py:277
  20.2 6.2 %collective-permute-start.5 = (bf16[128,512]{1,0:T(8,128)(2,1)S(1)}, bf16[128,512]{1,0:T(8,128)(2,1)S(1)}, u32[]{:S(2)}, u32[]{:S(2)}) collective-permute-start(bf16[128,512]{1,0:T(8,128)(2,1)S(1)} %collective-permute-done.1.refs_0_), channel_id=1, source_target_pairs={{0,1},{1,0},{2,3},{3,2},{4,5},{5,4},{6,7},{7,6},{8,9},{9,8},{10,11... | collective-permute-start | bytes 393224 | tf_op jit(solution)/shard_map/ppermute | solution.py:249
  22.5 9.4 %collective-permute-start.10 = (bf16[256,512]{1,0:T(8,128)(2,1)S(1)}, bf16[256,512]{1,0:T(8,128)(2,1)S(1)}, u32[]{:S(2)}, u32[]{:S(2)}) collective-permute-start(bf16[256,512]{1,0:T(8,128)(2,1)S(1)} %constant_dynamic-update-slice_fusion.refs_8_), channel_id=1, source_target_pairs={{0,8},{2,10},{4,12},{6,14},{8,0},{10,2},{12,4},{14,6},{16,24},{18,... | collective-permute-start | bytes 786440 | tf_op jit(solution)/shard_map/ppermute | solution.py:277
  22.5 9.4 %collective-permute-start.9 = (bf16[256,512]{1,0:T(8,128)(2,1)S(1)}, bf16[256,512]{1,0:T(8,128)(2,1)S(1)}, u32[]{:S(2)}, u32[]{:S(2)}) collective-permute-start(bf16[256,512]{1,0:T(8,128)(2,1)S(1)} %constant_dynamic-update-slice_fusion.refs_8_), channel_id=1, source_target_pairs={{0,4},{2,6},{4,0},{6,2},{8,12},{10,14},{12,8},{14,10},{16,20},{18,... | collective-permute-start | bytes 786440 | tf_op jit(solution)/shard_map/ppermute | solution.py:277
  23.5 6.2 %collective-permute-start.6 = (bf16[128,512]{1,0:T(8,128)(2,1)S(1)}, bf16[128,512]{1,0:T(8,128)(2,1)S(1)}, u32[]{:S(2)}, u32[]{:S(2)}) collective-permute-start(bf16[128,512]{1,0:T(8,128)(2,1)S(1)} %collective-permute-done.2.refs_1_), channel_id=1, source_target_pairs={{0,1},{1,0},{2,3},{3,2},{4,5},{5,4},{6,7},{7,6},{8,9},{9,8},{10,11... | collective-permute-start | bytes 393224 | tf_op jit(solution)/shard_map/ppermute | solution.py:249
  26.4 5.4 %collective-permute-start.7 = (bf16[128,512]{1,0:T(8,128)(2,1)S(1)}, bf16[128,512]{1,0:T(8,128)(2,1)S(1)}, u32[]{:S(2)}, u32[]{:S(2)}) collective-permute-start(bf16[128,512]{1,0:T(8,128)(2,1)S(1)} %collective-permute-done.3.refs_2_), channel_id=1, source_target_pairs={{0,1},{1,0},{2,3},{3,2},{4,5},{5,4},{6,7},{7,6},{8,9},{9,8},{10,11... | collective-permute-start | bytes 393224 | tf_op jit(solution)/shard_map/ppermute | solution.py:249
  33.3 2.7 %collective-permute-start.12 = (f32[512,512]{1,0:T(8,128)S(1)}, f32[512,512]{1,0:T(8,128)S(1)}, u32[]{:S(2)}, u32[]{:S(2)}) collective-permute-start(f32[512,512]{1,0:T(8,128)S(1)} %shard_map.51.mine_ref), channel_id=1, source_target_pairs={{0,2},{2,0},{4,6},{6,4},{8,10},{10,8},{12,14},{14,12},{16,18},{18,... | collective-permute-start | bytes 3145736 | tf_op jit(solution)/shard_map/ppermute | solution.py:246
  43.5 7.1 %collective-permute-start.27 = (bf16[128,512]{1,0:T(8,128)(2,1)S(1)}, bf16[128,512]{1,0:T(8,128)(2,1)S(1)}, u32[]{:S(2)}, u32[]{:S(2)}) collective-permute-start(bf16[128,512]{1,0:T(8,128)(2,1)S(1)} %get-tuple-element.21), channel_id=1, source_target_pairs={{0,1},{1,0},{2,3},{3,2},{4,5},{5,4},{6,7},{7,6},{8,9},{9,8},{10,11... | collective-permute-start | bytes 393224 | tf_op jit(solution)/shard_map/ppermute | solution.py:249
  46.7 6.1 %collective-permute-start.13 = (bf16[128,512]{1,0:T(8,128)(2,1)S(1)}, bf16[128,512]{1,0:T(8,128)(2,1)S(1)}, u32[]{:S(2)}, u32[]{:S(2)}) collective-permute-start(bf16[128,512]{1,0:T(8,128)(2,1)S(1)} %get-tuple-element.19), channel_id=1, source_target_pairs={{0,8},{2,6},{8,16},{10,2},{16,24},{18,10},{24,28},{26,18},{28,20},... | collective-permute-start | bytes 393224 | tf_op jit(solution)/shard_map/ppermute | solution.py:313
  47.4 7.6 %collective-permute-start.15 = (bf16[128,512]{1,0:T(8,128)(2,1)S(1)}, bf16[128,512]{1,0:T(8,128)(2,1)S(1)}, u32[]{:S(2)}, u32[]{:S(2)}) collective-permute-start(bf16[128,512]{1,0:T(8,128)(2,1)S(1)} %get-tuple-element.20), channel_id=1, source_target_pairs={{0,8},{2,6},{8,16},{10,2},{16,24},{18,10},{24,28},{26,18},{28,20},... | collective-permute-start | bytes 393224 | tf_op jit(solution)/shard_map/ppermute | solution.py:313
  50.5 5.1 %collective-permute-start.29 = (bf16[128,512]{1,0:T(8,128)(2,1)S(1)}, bf16[128,512]{1,0:T(8,128)(2,1)S(1)}, u32[]{:S(2)}, u32[]{:S(2)}) collective-permute-start(bf16[128,512]{1,0:T(8,128)(2,1)S(1)} %collective-permute-done.27), channel_id=1, source_target_pairs={{0,8},{2,6},{8,16},{10,2},{16,24},{18,10},{24,28},{26,18},{28,20},... | collective-permute-start | bytes 393224 | tf_op jit(solution)/shard_map/ppermute | solution.py:313
  52.8 2.9 %collective-permute-start.28 = (bf16[128,512]{1,0:T(8,128)(2,1)S(1)}, bf16[128,512]{1,0:T(8,128)(2,1)S(1)}, u32[]{:S(2)}, u32[]{:S(2)}) collective-permute-start(bf16[128,512]{1,0:T(8,128)(2,1)S(1)} %collective-permute-done.27), channel_id=1, source_target_pairs={{0,2},{2,0},{4,6},{6,4},{8,10},{10,8},{12,14},{14,12},{16,18},{18,... | collective-permute-start | bytes 393224 | tf_op jit(solution)/shard_map/ppermute | solution.py:246
  52.8 5.1 %collective-permute-start.17 = (bf16[128,512]{1,0:T(8,128)(2,1)S(1)}, bf16[128,512]{1,0:T(8,128)(2,1)S(1)}, u32[]{:S(2)}, u32[]{:S(2)}) collective-permute-start(bf16[128,512]{1,0:T(8,128)(2,1)S(1)} %collective-permute-done.13), channel_id=1, source_target_pairs={{0,8},{2,6},{8,16},{10,2},{16,24},{18,10},{24,28},{26,18},{28,20},... | collective-permute-start | bytes 393224 | tf_op jit(solution)/shard_map/ppermute | solution.py:313
  54.9 2.9 %collective-permute-start.14 = (bf16[128,512]{1,0:T(8,128)(2,1)S(1)}, bf16[128,512]{1,0:T(8,128)(2,1)S(1)}, u32[]{:S(2)}, u32[]{:S(2)}) collective-permute-start(bf16[128,512]{1,0:T(8,128)(2,1)S(1)} %collective-permute-done.13), channel_id=1, source_target_pairs={{0,2},{2,0},{4,6},{6,4},{8,10},{10,8},{12,14},{14,12},{16,18},{18,... | collective-permute-start | bytes 393224 | tf_op jit(solution)/shard_map/ppermute | solution.py:246
  54.9 6.4 %collective-permute-start.19 = (bf16[128,512]{1,0:T(8,128)(2,1)S(1)}, bf16[128,512]{1,0:T(8,128)(2,1)S(1)}, u32[]{:S(2)}, u32[]{:S(2)}) collective-permute-start(bf16[128,512]{1,0:T(8,128)(2,1)S(1)} %collective-permute-done.15), channel_id=1, source_target_pairs={{0,8},{2,6},{8,16},{10,2},{16,24},{18,10},{24,28},{26,18},{28,20},... | collective-permute-start | bytes 393224 | tf_op jit(solution)/shard_map/ppermute | solution.py:313
  55.7 4.4 %collective-permute-start.16 = (bf16[128,512]{1,0:T(8,128)(2,1)S(1)}, bf16[128,512]{1,0:T(8,128)(2,1)S(1)}, u32[]{:S(2)}, u32[]{:S(2)}) collective-permute-start(bf16[128,512]{1,0:T(8,128)(2,1)S(1)} %collective-permute-done.15), channel_id=1, source_target_pairs={{0,2},{2,0},{4,6},{6,4},{8,10},{10,8},{12,14},{14,12},{16,18},{18,... | collective-permute-start | bytes 393224 | tf_op jit(solution)/shard_map/ppermute | solution.py:246
  55.8 6.8 %collective-permute-start.33 = (bf16[128,512]{1,0:T(8,128)(2,1)S(1)}, bf16[128,512]{1,0:T(8,128)(2,1)S(1)}, u32[]{:S(2)}, u32[]{:S(2)}) collective-permute-start(bf16[128,512]{1,0:T(8,128)(2,1)S(1)} %collective-permute-done.29), channel_id=1, source_target_pairs={{0,8},{2,6},{8,16},{10,2},{16,24},{18,10},{24,28},{26,18},{28,20},... | collective-permute-start | bytes 393224 | tf_op jit(solution)/shard_map/ppermute | solution.py:313
  57.8 3.6 %collective-permute-start.30 = (bf16[128,512]{1,0:T(8,128)(2,1)S(1)}, bf16[128,512]{1,0:T(8,128)(2,1)S(1)}, u32[]{:S(2)}, u32[]{:S(2)}) collective-permute-start(bf16[128,512]{1,0:T(8,128)(2,1)S(1)} %collective-permute-done.29), channel_id=1, source_target_pairs={{0,2},{2,0},{4,6},{6,4},{8,10},{10,8},{12,14},{14,12},{16,18},{18,... | collective-permute-start | bytes 393224 | tf_op jit(solution)/shard_map/ppermute | solution.py:246
  58.0 5.9 %collective-permute-start.31 = (bf16[128,512]{1,0:T(8,128)(2,1)S(1)}, bf16[128,512]{1,0:T(8,128)(2,1)S(1)}, u32[]{:S(2)}, u32[]{:S(2)}) collective-permute-start(bf16[128,512]{1,0:T(8,128)(2,1)S(1)} %collective-permute-done.28), channel_id=1, source_target_pairs={{0,8},{2,6},{8,16},{10,2},{16,24},{18,10},{24,28},{26,18},{28,20},... | collective-permute-start | bytes 393224 | tf_op jit(solution)/shard_map/ppermute | solution.py:313
  60.1 5.0 %collective-permute-start.21 = (bf16[128,512]{1,0:T(8,128)(2,1)S(1)}, bf16[128,512]{1,0:T(8,128)(2,1)S(1)}, u32[]{:S(2)}, u32[]{:S(2)}) collective-permute-start(bf16[128,512]{1,0:T(8,128)(2,1)S(1)} %collective-permute-done.17), channel_id=1, source_target_pairs={{0,8},{2,6},{8,16},{10,2},{16,24},{18,10},{24,28},{26,18},{28,20},... | collective-permute-start | bytes 393224 | tf_op jit(solution)/shard_map/ppermute | solution.py:313
  61.3 1.4 %collective-permute-start.18 = (bf16[128,512]{1,0:T(8,128)(2,1)S(1)}, bf16[128,512]{1,0:T(8,128)(2,1)S(1)}, u32[]{:S(2)}, u32[]{:S(2)}) collective-permute-start(bf16[128,512]{1,0:T(8,128)(2,1)S(1)} %collective-permute-done.17), channel_id=1, source_target_pairs={{0,2},{2,0},{4,6},{6,4},{8,10},{10,8},{12,14},{14,12},{16,18},{18,... | collective-permute-start | bytes 393224 | tf_op jit(solution)/shard_map/ppermute | solution.py:246
  61.4 6.3 %collective-permute-start.23 = (bf16[128,512]{1,0:T(8,128)(2,1)S(1)}, bf16[128,512]{1,0:T(8,128)(2,1)S(1)}, u32[]{:S(2)}, u32[]{:S(2)}) collective-permute-start(bf16[128,512]{1,0:T(8,128)(2,1)S(1)} %collective-permute-done.19), channel_id=1, source_target_pairs={{0,8},{2,6},{8,16},{10,2},{16,24},{18,10},{24,28},{26,18},{28,20},... | collective-permute-start | bytes 393224 | tf_op jit(solution)/shard_map/ppermute | solution.py:313
  62.6 1.4 %collective-permute-start.20 = (bf16[128,512]{1,0:T(8,128)(2,1)S(1)}, bf16[128,512]{1,0:T(8,128)(2,1)S(1)}, u32[]{:S(2)}, u32[]{:S(2)}) collective-permute-start(bf16[128,512]{1,0:T(8,128)(2,1)S(1)} %collective-permute-done.19), channel_id=1, source_target_pairs={{0,2},{2,0},{4,6},{6,4},{8,10},{10,8},{12,14},{14,12},{16,18},{18,... | collective-permute-start | bytes 393224 | tf_op jit(solution)/shard_map/ppermute | solution.py:246
  62.8 5.1 %collective-permute-start.37 = (bf16[128,512]{1,0:T(8,128)(2,1)S(1)}, bf16[128,512]{1,0:T(8,128)(2,1)S(1)}, u32[]{:S(2)}, u32[]{:S(2)}) collective-permute-start(bf16[128,512]{1,0:T(8,128)(2,1)S(1)} %collective-permute-done.33), channel_id=1, source_target_pairs={{0,8},{2,6},{8,16},{10,2},{16,24},{18,10},{24,28},{26,18},{28,20},... | collective-permute-start | bytes 393224 | tf_op jit(solution)/shard_map/ppermute | solution.py:313
  63.9 4.4 %collective-permute-start.34 = (bf16[128,512]{1,0:T(8,128)(2,1)S(1)}, bf16[128,512]{1,0:T(8,128)(2,1)S(1)}, u32[]{:S(2)}, u32[]{:S(2)}) collective-permute-start(bf16[128,512]{1,0:T(8,128)(2,1)S(1)} %collective-permute-done.33), channel_id=1, source_target_pairs={{0,2},{2,0},{4,6},{6,4},{8,10},{10,8},{12,14},{14,12},{16,18},{18,... | collective-permute-start | bytes 393224 | tf_op jit(solution)/shard_map/ppermute | solution.py:246
  64.0 2.5 %collective-permute-start.32 = (bf16[128,512]{1,0:T(8,128)(2,1)S(1)}, bf16[128,512]{1,0:T(8,128)(2,1)S(1)}, u32[]{:S(2)}, u32[]{:S(2)}) collective-permute-start(bf16[128,512]{1,0:T(8,128)(2,1)S(1)} %collective-permute-done.31), channel_id=1, source_target_pairs={{0,2},{2,0},{4,6},{6,4},{8,10},{10,8},{12,14},{14,12},{16,18},{18,... | collective-permute-start | bytes 393224 | tf_op jit(solution)/shard_map/ppermute | solution.py:246
  65.1 5.0 %collective-permute-start.35 = (bf16[128,512]{1,0:T(8,128)(2,1)S(1)}, bf16[128,512]{1,0:T(8,128)(2,1)S(1)}, u32[]{:S(2)}, u32[]{:S(2)}) collective-permute-start(bf16[128,512]{1,0:T(8,128)(2,1)S(1)} %collective-permute-done.31), channel_id=1, source_target_pairs={{0,8},{2,6},{8,16},{10,2},{16,24},{18,10},{24,28},{26,18},{28,20},... | collective-permute-start | bytes 393224 | tf_op jit(solution)/shard_map/ppermute | solution.py:313
  66.5 5.0 %collective-permute-start.25 = (bf16[128,512]{1,0:T(8,128)(2,1)S(1)}, bf16[128,512]{1,0:T(8,128)(2,1)S(1)}, u32[]{:S(2)}, u32[]{:S(2)}) collective-permute-start(bf16[128,512]{1,0:T(8,128)(2,1)S(1)} %collective-permute-done.21), channel_id=1, source_target_pairs={{0,8},{2,6},{8,16},{10,2},{16,24},{18,10},{24,28},{26,18},{28,20},... | collective-permute-start | bytes 393224 | tf_op jit(solution)/shard_map/ppermute | solution.py:313
  67.7 2.3 %collective-permute-start.22 = (bf16[128,512]{1,0:T(8,128)(2,1)S(1)}, bf16[128,512]{1,0:T(8,128)(2,1)S(1)}, u32[]{:S(2)}, u32[]{:S(2)}) collective-permute-start(bf16[128,512]{1,0:T(8,128)(2,1)S(1)} %collective-permute-done.21), channel_id=1, source_target_pairs={{0,2},{2,0},{4,6},{6,4},{8,10},{10,8},{12,14},{14,12},{16,18},{18,... | collective-permute-start | bytes 393224 | tf_op jit(solution)/shard_map/ppermute | solution.py:246
  67.9 3.7 %collective-permute-start.24 = (bf16[128,512]{1,0:T(8,128)(2,1)S(1)}, bf16[128,512]{1,0:T(8,128)(2,1)S(1)}, u32[]{:S(2)}, u32[]{:S(2)}) collective-permute-start(bf16[128,512]{1,0:T(8,128)(2,1)S(1)} %collective-permute-done.23), channel_id=1, source_target_pairs={{0,2},{2,0},{4,6},{6,4},{8,10},{10,8},{12,14},{14,12},{16,18},{18,... | collective-permute-start | bytes 393224 | tf_op jit(solution)/shard_map/ppermute | solution.py:246
  68.3 5.0 %collective-permute-start.41 = (bf16[128,512]{1,0:T(8,128)(2,1)S(1)}, bf16[128,512]{1,0:T(8,128)(2,1)S(1)}, u32[]{:S(2)}, u32[]{:S(2)}) collective-permute-start(bf16[128,512]{1,0:T(8,128)(2,1)S(1)} %collective-permute-done.37), channel_id=1, source_target_pairs={{0,8},{2,6},{8,16},{10,2},{16,24},{18,10},{24,28},{26,18},{28,20},... | collective-permute-start | bytes 393224 | tf_op jit(solution)/shard_map/ppermute | solution.py:313
  70.0 5.0 %collective-permute-start.38 = (bf16[128,512]{1,0:T(8,128)(2,1)S(1)}, bf16[128,512]{1,0:T(8,128)(2,1)S(1)}, u32[]{:S(2)}, u32[]{:S(2)}) collective-permute-start(bf16[128,512]{1,0:T(8,128)(2,1)S(1)} %collective-permute-done.37), channel_id=1, source_target_pairs={{0,2},{2,0},{4,6},{6,4},{8,10},{10,8},{12,14},{14,12},{16,18},{18,... | collective-permute-start | bytes 393224 | tf_op jit(solution)/shard_map/ppermute | solution.py:246
  70.1 5.0 %collective-permute-start.39 = (bf16[128,512]{1,0:T(8,128)(2,1)S(1)}, bf16[128,512]{1,0:T(8,128)(2,1)S(1)}, u32[]{:S(2)}, u32[]{:S(2)}) collective-permute-start(bf16[128,512]{1,0:T(8,128)(2,1)S(1)} %collective-permute-done.35), channel_id=1, source_target_pairs={{0,8},{2,6},{8,16},{10,2},{16,24},{18,10},{24,28},{26,18},{28,20},... | collective-permute-start | bytes 393224 | tf_op jit(solution)/shard_map/ppermute | solution.py:313
  71.5 3.5 %collective-permute-start.36 = (bf16[128,512]{1,0:T(8,128)(2,1)S(1)}, bf16[128,512]{1,0:T(8,128)(2,1)S(1)}, u32[]{:S(2)}, u32[]{:S(2)}) collective-permute-start(bf16[128,512]{1,0:T(8,128)(2,1)S(1)} %collective-permute-done.35), channel_id=1, source_target_pairs={{0,2},{2,0},{4,6},{6,4},{8,10},{10,8},{12,14},{14,12},{16,18},{18,... | collective-permute-start | bytes 393224 | tf_op jit(solution)/shard_map/ppermute | solution.py:246
  71.6 4.8 %collective-permute-start.26 = (bf16[128,512]{1,0:T(8,128)(2,1)S(1)}, bf16[128,512]{1,0:T(8,128)(2,1)S(1)}, u32[]{:S(2)}, u32[]{:S(2)}) collective-permute-start(bf16[128,512]{1,0:T(8,128)(2,1)S(1)} %collective-permute-done.25), channel_id=1, source_target_pairs={{0,2},{2,0},{4,6},{6,4},{8,10},{10,8},{12,14},{14,12},{16,18},{18,... | collective-permute-start | bytes 393224 | tf_op jit(solution)/shard_map/ppermute | solution.py:246
  73.3 3.2 %collective-permute-start.42 = (bf16[128,512]{1,0:T(8,128)(2,1)S(1)}, bf16[128,512]{1,0:T(8,128)(2,1)S(1)}, u32[]{:S(2)}, u32[]{:S(2)}) collective-permute-start(bf16[128,512]{1,0:T(8,128)(2,1)S(1)} %collective-permute-done.41), channel_id=1, source_target_pairs={{0,2},{2,0},{4,6},{6,4},{8,10},{10,8},{12,14},{14,12},{16,18},{18,... | collective-permute-start | bytes 393224 | tf_op jit(solution)/shard_map/ppermute | solution.py:246
  75.0 1.3 %collective-permute-start.40 = (bf16[128,512]{1,0:T(8,128)(2,1)S(1)}, bf16[128,512]{1,0:T(8,128)(2,1)S(1)}, u32[]{:S(2)}, u32[]{:S(2)}) collective-permute-start(bf16[128,512]{1,0:T(8,128)(2,1)S(1)} %collective-permute-done.39), channel_id=1, source_target_pairs={{0,2},{2,0},{4,6},{6,4},{8,10},{10,8},{12,14},{14,12},{16,18},{18,... | collective-permute-start | bytes 393224 | tf_op jit(solution)/shard_map/ppermute | solution.py:246

commit v7 on v6

--- a/solution.py
+++ b/solution.py
@@ -173,16 +173,14 @@
         out_ref[...] = piece.astype(jnp.bfloat16)
 
 
-OFFSETS = ((4, 7, 1, 2), (5, 6, 3, 2))
+OFFSETS = ((4, 7, 2), (5, 6, 3))
+SHARED = 1
 
 
 def pack_kernel(place_ref, inputs_ref, *piece_refs):
     for step, piece_ref in enumerate(piece_refs):
-        rows = piece_ref.shape[0]
-        last = step == len(piece_refs) - 1
-        first_row = pl.multiple_of(place_ref[0], rows) if last else 0
-        first_col = pl.multiple_of(place_ref[1 + step] * BLOCK, BLOCK)
-        piece_ref[...] = inputs_ref[pl.ds(first_row, rows), pl.ds(first_col, BLOCK)]
+        first_col = pl.multiple_of(place_ref[step] * BLOCK, BLOCK)
+        piece_ref[...] = inputs_ref[:, pl.ds(first_col, BLOCK)]
 
 
 def ring_band(position, bands):
@@ -190,7 +188,7 @@
     return jnp.where(position < bands // 2, 2 * position, 2 * (bands - 1 - position) + 1)
 
 
-def tile_kernel(place_ref, own_ref, *refs):
+def tile_kernel(place_ref, own_ref, shared_ref, *refs):
     hops = len(OFFSETS[0])
     near_refs, far_refs = refs[:hops], refs[hops : 2 * hops]
     cot_refs = refs[2 * hops : -3]
@@ -198,20 +196,18 @@
     plane, band = place_ref[0], place_ref[1]
     tokens = own_ref.shape[0]
 
-    def put(to_ref, piece_ref, source, part):
-        rows = piece_ref.shape[0]
-        first_row = pl.multiple_of(source * tokens + part * rows, rows)
-        to_ref[pl.ds(first_row, rows), :] = piece_ref[...]
-
-    put(band_ref, own_ref, band, 0)
+    def put(to_ref, piece_ref, source):
+        first_row = pl.multiple_of(source * tokens, tokens)
+        to_ref[pl.ds(first_row, tokens), :] = piece_ref[...]
+
+    put(band_ref, own_ref, band)
+    put(band_ref, shared_ref, band ^ SHARED)
     for hop in range(hops):
-        last = hop == hops - 1
         for piece_ref, member in ((near_refs[hop], plane), (far_refs[hop], 1 - plane)):
-            offset = jnp.where(member == 0, OFFSETS[0][hop], OFFSETS[1][hop])
-            put(band_ref, piece_ref, band ^ offset, member if last else 0)
+            put(band_ref, piece_ref, band ^ jnp.where(member == 0, OFFSETS[0][hop], OFFSETS[1][hop]))
     for offset, pair_ref in enumerate(cot_refs):
         for part, source in enumerate((band ^ offset, band ^ offset ^ 4)):
-            put(cot_ref, pair_ref.at[pl.ds(part * tokens, tokens)], source, 0)
+            put(cot_ref, pair_ref.at[pl.ds(part * tokens, tokens)], source)
     partial_ref[...] = contract(band_ref[...], cot_ref[...], 0, 0)
 
 
@@ -262,14 +258,14 @@
 
     hops = range(len(OFFSETS[0]))
     bands_out = [band ^ jnp.where(plane == 0, OFFSETS[0][hop], OFFSETS[1][hop]) for hop in hops]
-    own_band, *packed = call(
+    *packed, own_band = call(
         pack_kernel,
-        [jax.ShapeDtypeStruct((tokens, BLOCK), inputs.dtype)] * len(hops)
-        + [jax.ShapeDtypeStruct((tokens // 2, BLOCK), inputs.dtype)],
+        [jax.ShapeDtypeStruct((tokens, BLOCK), inputs.dtype)] * (len(hops) + 2),
         [],
-        jnp.stack([plane * (tokens // 2), band] + bands_out).astype(jnp.int32),
+        jnp.stack(bands_out + [band ^ SHARED, band]).astype(jnp.int32),
         inputs,
     )
+
     def exchange(array, offset):
         pairs = [
             (k * cores + c, (k ^ offset) * cores + c) for k in range(bands) for c in range(cores)
@@ -278,7 +274,8 @@
 
     outputs = jnp.dot(inputs, weight, preferred_element_type=jnp.float32).astype(jnp.bfloat16)
     far_cot, outputs = lax.optimization_barrier((exchange(cotangent, 4), outputs))
-    near = [deal(piece, hop) for hop, piece in zip(hops, packed)]
+    near = [deal(packed[hop], hop) for hop in hops]
+    shared = exchange(packed[-1], SHARED)
     pair = jnp.concatenate([cotangent, far_cot])
     cots = [pair] + [exchange(pair, offset) for offset in (1, 2, 3)]
     far = [swap_plane(piece) for piece in near]
@@ -288,6 +285,7 @@
         [pltpu.VMEM((bands * tokens, BLOCK), inputs.dtype)] * 2,
         jnp.stack([plane, band]).astype(jnp.int32),
         own_band,
+        shared,
         *near,
         *far,
         *cots,

time: 79.4 us -> 79.4 us (level)
  waiting for transfers between devices: 12.9 us -> 17.3 us
  starting transfers between devices: 46.9 us -> 42.5 us
    ppermute x5 -> x4, starting transfers between devices: 11.4 us -> 6.98 us  [swap_plane(): lax.ppermute(array, 'pre', [(c, members - 1 - c) for c in range(members)])]
    ppermute x4 -> x3, starting transfers between devices: 5.91 us -> 3.88 us  [deal(): return lax.ppermute(array, ('dp', 'pre'), pairs)]
    ppermute x4 -> x5, starting transfers between devices: 7.49 us -> 9.35 us  [exchange(): return lax.ppermute(array, 'dp', pairs)]
    ppermute x4 -> x3, waiting for transfers between devices: 0.01 us -> 1.79 us  [deal(): return lax.ppermute(array, ('dp', 'pre'), pairs)]
    ppermute x4 -> x5, waiting for transfers between devices: 0.07 us -> 1.36 us  [exchange(): return lax.ppermute(array, 'dp', pairs)]
    ppermute x5 -> x4, waiting for transfers between devices: 4.94 us -> 6.21 us  [swap_plane(): lax.ppermute(array, 'pre', [(c, members - 1 - c) for c in range(members)])]
  transfers between devices with their start and end apart: 43 -> 42, of which waited for: 13 -> 15; matrix products, arithmetic and copies ran while one was open for 6% -> 6% of each run, Pallas kernels for 1% -> 1%
where the time goes in v7:
time: 79.4 us; the launch traced here: 79.2 us
  starting transfers between devices  42.5 us (54%)
  waiting for transfers between devices  17.3 us (22%)
  Pallas kernels  9.42 us (12%)
  matrix products  3.6 us (5%)
  other arithmetic  2.81 us (4%)
  local copies, waits for them, and re-layouts  2.23 us (3%)
  between operations  1.36 us (2%)
    ppermute x14, starting transfers between devices, turn(): return lax.ppermute(array, 'dp', pairs)  20.4 us
    pallas_call x3, Pallas kernels, call(): pl.pallas_call(kernel, out_shape=out_shapes, in_specs=in_specs, out_specs...  9.42 us
    ppermute x5, starting transfers between devices, exchange(): return lax.ppermute(array, 'dp', pairs)  9.35 us
    ppermute x4, starting transfers between devices, swap_plane(): lax.ppermute(array, 'pre', [(c, members - 1 - c) for c in range(members)])  6.98 us
    ppermute x4, waiting for transfers between devices, swap_plane(): lax.ppermute(array, 'pre', [(c, members - 1 - c) for c in range(members)])  6.21 us
    ppermute x14, waiting for transfers between devices, turn(): return lax.ppermute(array, 'dp', pairs)  4.28 us
    ppermute x3, starting transfers between devices, deal(): return lax.ppermute(array, ('dp', 'pre'), pairs)  3.88 us
    ppermute x16, waiting for transfers between devices, swap_core(): return lax.ppermute(array, 'dp', [(g, g ^ 1) for g in range(groups)])  3.65 us
  transfers between devices with their start and end apart: 42, of which 15 were waited for; matrix products, arithmetic and copies ran while one was open for 6% of the time, Pallas kernels for 1%

profile of v7, /device:TPU:0, one launch (start us, length us, event | category | flops | bytes accessed | tf_op | source)
XLA Modules:
  0.0 79.2 jit_solution(15464267436403794582)
XLA Ops:
  0.6 4.1 %collective-permute-start = (bf16[128,512]{1,0:T(8,128)(2,1)}, bf16[128,512]{1,0:T(8,128)(2,1)S(1)}, u32[]{:S(2)}, u32[]{:S(2)}) collective-permute-start(bf16[128,512]{1,0:T(8,128)(2,1)} %param.5), channel_id=1, source_target_pairs={{0,16},{2,18},{4,20},{6,22},{8,24},{10,26},{12,28},{14,30},{16,0},... | collective-permute-start | bytes 393224 | tf_op jit(solution)/shard_map/ppermute | solution.py:273
  4.8 1.2 %copy-done = bf16[128,4096]{1,0:T(8,128)(2,1)S(1)} copy-done((bf16[128,4096]{1,0:T(8,128)(2,1)S(1)}, bf16[128,4096]{1,0:T(8,128)(2,1)}, u32[]{:S(2)}) %copy-start) | copy-done | bytes 1048600
  6.0 0.6 shard_map.50
  6.6 1.6 %collective-permute-start.1 = (bf16[128,512]{1,0:T(8,128)(2,1)S(1)}, bf16[128,512]{1,0:T(8,128)(2,1)S(1)}, u32[]{:S(2)}, u32[]{:S(2)}) collective-permute-start(bf16[128,512]{1,0:T(8,128)(2,1)S(1)} %get-tuple-element.14), channel_id=1, source_target_pairs={{0,4},{2,6},{4,0},{6,2},{8,12},{10,14},{12,8},{14,10},{16,20},{18,... | collective-permute-start | bytes 393224 | tf_op jit(solution)/shard_map/ppermute | solution.py:273
  8.2 0.3 collective-permute-start.2
  8.6 3.5 %collective-permute-start.3 = (bf16[128,512]{1,0:T(8,128)(2,1)S(1)}, bf16[128,512]{1,0:T(8,128)(2,1)S(1)}, u32[]{:S(2)}, u32[]{:S(2)}) collective-permute-start(bf16[128,512]{1,0:T(8,128)(2,1)S(1)} %get-tuple-element.16), channel_id=1, source_target_pairs={{0,28},{1,25},{2,30},{3,27},{4,24},{5,29},{6,26},{7,31},{8,20},{9,... | collective-permute-start | bytes 393224 | tf_op jit(solution)/shard_map/ppermute | solution.py:257
  12.1 3.6 %convolution_convert_fusion = bf16[128,512]{1,0:T(8,128)(2,1)} fusion(bf16[128,4096]{1,0:T(8,128)(2,1)S(1)} %copy-done, bf16[4096,512]{1,0:T(8,128)(2,1)} %param.4), kind=kOutput, calls=%fused_computation.1 | convolution fusion | flops 536936448 | bytes 5373952 | tf_op jit(solution)/shard_map/dot_general | solution.py:275
  15.8 3.0 %collective-permute-start.10 = (bf16[256,512]{1,0:T(8,128)(2,1)S(1)}, bf16[256,512]{1,0:T(8,128)(2,1)S(1)}, u32[]{:S(2)}, u32[]{:S(2)}) collective-permute-start(bf16[256,512]{1,0:T(8,128)(2,1)S(1)} %constant_dynamic-update-slice_fusion.refs_6_), channel_id=1, source_target_pairs={{0,12},{2,14},{4,8},{6,10},{8,4},{10,6},{12,0},{14,2},{16,28},{18,... | collective-permute-start | bytes 786440 | tf_op jit(solution)/shard_map/ppermute | solution.py:273
  18.8 1.8 %collective-permute-done.2.refs_0_ = bf16[128,512]{1,0:T(8,128)(2,1)S(1)} collective-permute-done((bf16[128,512]{1,0:T(8,128)(2,1)S(1)}, bf16[128,512]{1,0:T(8,128)(2,1)S(1)}, u32[]{:S(2)}, u32[]{:S(2)}) %collective-permute-start.2) | collective-permute-done | bytes 131104 | tf_op jit(solution)/shard_map/ppermute | solution.py:257
  20.6 2.4 %collective-permute-start.5 = (bf16[128,512]{1,0:T(8,128)(2,1)S(1)}, bf16[128,512]{1,0:T(8,128)(2,1)S(1)}, u32[]{:S(2)}, u32[]{:S(2)}) collective-permute-start(bf16[128,512]{1,0:T(8,128)(2,1)S(1)} %collective-permute-done.2.refs_0_), channel_id=1, source_target_pairs={{0,1},{1,0},{2,3},{3,2},{4,5},{5,4},{6,7},{7,6},{8,9},{9,8},{10,11... | collective-permute-start | bytes 393224 | tf_op jit(solution)/shard_map/ppermute | solution.py:245
  23.0 0.6 collective-permute-start.8
  23.6 1.0 %collective-permute-start.6 = (bf16[128,512]{1,0:T(8,128)(2,1)S(1)}, bf16[128,512]{1,0:T(8,128)(2,1)S(1)}, u32[]{:S(2)}, u32[]{:S(2)}) collective-permute-start(bf16[128,512]{1,0:T(8,128)(2,1)S(1)} %collective-permute-done.3.refs_1_), channel_id=1, source_target_pairs={{0,1},{1,0},{2,3},{3,2},{4,5},{5,4},{6,7},{7,6},{8,9},{9,8},{10,11... | collective-permute-start | bytes 393224 | tf_op jit(solution)/shard_map/ppermute | solution.py:245
  24.6 2.3 %collective-permute-done.5.refs_3_ = bf16[128,512]{1,0:T(8,128)(2,1)S(1)} collective-permute-done((bf16[128,512]{1,0:T(8,128)(2,1)S(1)}, bf16[128,512]{1,0:T(8,128)(2,1)S(1)}, u32[]{:S(2)}, u32[]{:S(2)}) %collective-permute-start.5) | collective-permute-done | bytes 131104 | tf_op jit(solution)/shard_map/ppermute | solution.py:245
  26.8 2.5 %collective-permute-start.7 = (bf16[128,512]{1,0:T(8,128)(2,1)S(1)}, bf16[128,512]{1,0:T(8,128)(2,1)S(1)}, u32[]{:S(2)}, u32[]{:S(2)}) collective-permute-start(bf16[128,512]{1,0:T(8,128)(2,1)S(1)} %collective-permute-done.4.refs_2_), channel_id=1, source_target_pairs={{0,1},{1,0},{2,3},{3,2},{4,5},{5,4},{6,7},{7,6},{8,9},{9,8},{10,11... | collective-permute-start | bytes 393224 | tf_op jit(solution)/shard_map/ppermute | solution.py:245
  29.4 0.6 collective-permute-done.6.refs_4_
  30.0 2.2 %collective-permute-done.7.refs_5_ = bf16[128,512]{1,0:T(8,128)(2,1)S(1)} collective-permute-done((bf16[128,512]{1,0:T(8,128)(2,1)S(1)}, bf16[128,512]{1,0:T(8,128)(2,1)S(1)}, u32[]{:S(2)}, u32[]{:S(2)}) %collective-permute-start.7) | collective-permute-done | bytes 131104 | tf_op jit(solution)/shard_map/ppermute | solution.py:245
  32.3 1.4 %collective-permute-done.8.refs_7_ = bf16[256,512]{1,0:T(8,128)(2,1)S(1)} collective-permute-done((bf16[256,512]{1,0:T(8,128)(2,1)S(1)}, bf16[256,512]{1,0:T(8,128)(2,1)S(1)}, u32[]{:S(2)}, u32[]{:S(2)}) %collective-permute-start.8) | collective-permute-done | bytes 262176 | tf_op jit(solution)/shard_map/ppermute | solution.py:273
  33.6 1.4 %shard_map.51.mine_ref = f32[512,512]{1,0:T(8,128)S(1)} custom-call(s32[2]{0:T(128)S(1)} %pad_add_fusion.1.place_ref, bf16[128,512]{1,0:T(8,128)(2,1)S(1)} %get-tuple-element.13.own_ref, bf16[128,512]{1,0:T(8,128)(2,1)S(1)} %collective-permute-done.1.shared_ref, bf16[128,512]{1,0:T(8,128)(2,1)S(1)} %collective-permute-done.2.refs_0_, ...), custom_call_target="tpu_custom_call" | custom-call | tf_op jit(solution)/shard_map/pallas_call | solution.py:217
  35.5 2.3 %collective-permute-done.11.other_ref = f32[512,512]{1,0:T(8,128)S(1)} collective-permute-done((f32[512,512]{1,0:T(8,128)S(1)}, f32[512,512]{1,0:T(8,128)S(1)}, u32[]{:S(2)}, u32[]{:S(2)}) %collective-permute-start.11) | collective-permute-done | bytes 1048608 | tf_op jit(solution)/shard_map/ppermute | solution.py:242
  37.8 7.4 %shard_map.52 = (bf16[128,512]{1,0:T(8,128)(2,1)S(1)}, bf16[128,512]{1,0:T(8,128)(2,1)S(1)}, bf16[128,512]{1,0:T(8,128)(2,1)S(1)}) custom-call(s32[2]{0:T(128)S(1)} %pad_add_fusion.side_ref, f32[512,512]{1,0:T(8,128)S(1)} %shard_map.51.mine_ref, f32[512,512]{1,0:T(8,128)S(1)} %collective-permute-done.11.other_ref), custom_call_target="tpu_custom_call" | custom-call | tf_op jit(solution)/shard_map/pallas_call | solution.py:217
  45.2 1.1 %collective-permute-start.26 = (bf16[128,512]{1,0:T(8,128)(2,1)S(1)}, bf16[128,512]{1,0:T(8,128)(2,1)S(1)}, u32[]{:S(2)}, u32[]{:S(2)}) collective-permute-start(bf16[128,512]{1,0:T(8,128)(2,1)S(1)} %get-tuple-element.21), channel_id=1, source_target_pairs={{0,1},{1,0},{2,3},{3,2},{4,5},{5,4},{6,7},{7,6},{8,9},{9,8},{10,11... | collective-permute-start | bytes 393224 | tf_op jit(solution)/shard_map/ppermute | solution.py:245
  46.4 3.1 %collective-permute-start.14 = (bf16[128,512]{1,0:T(8,128)(2,1)S(1)}, bf16[128,512]{1,0:T(8,128)(2,1)S(1)}, u32[]{:S(2)}, u32[]{:S(2)}) collective-permute-start(bf16[128,512]{1,0:T(8,128)(2,1)S(1)} %get-tuple-element.20), channel_id=1, source_target_pairs={{0,8},{2,6},{8,16},{10,2},{16,24},{18,10},{24,28},{26,18},{28,20},... | collective-permute-start | bytes 393224 | tf_op jit(solution)/shard_map/ppermute | solution.py:311
  49.5 0.2 broadcast_in_dim.99.clone.1
  49.7 1.1 %collective-permute-done.26 = bf16[128,512]{1,0:T(8,128)(2,1)S(1)} collective-permute-done((bf16[128,512]{1,0:T(8,128)(2,1)S(1)}, bf16[128,512]{1,0:T(8,128)(2,1)S(1)}, u32[]{:S(2)}, u32[]{:S(2)}) %collective-permute-start.26) | collective-permute-done | bytes 131104 | tf_op jit(solution)/shard_map/ppermute | solution.py:245
  50.8 1.1 %collective-permute-start.28 = (bf16[128,512]{1,0:T(8,128)(2,1)S(1)}, bf16[128,512]{1,0:T(8,128)(2,1)S(1)}, u32[]{:S(2)}, u32[]{:S(2)}) collective-permute-start(bf16[128,512]{1,0:T(8,128)(2,1)S(1)} %collective-permute-done.26), channel_id=1, source_target_pairs={{0,8},{2,6},{8,16},{10,2},{16,24},{18,10},{24,28},{26,18},{28,20},... | collective-permute-start | bytes 393224 | tf_op jit(solution)/shard_map/ppermute | solution.py:311
  51.9 3.1 %collective-permute-start.16 = (bf16[128,512]{1,0:T(8,128)(2,1)S(1)}, bf16[128,512]{1,0:T(8,128)(2,1)S(1)}, u32[]{:S(2)}, u32[]{:S(2)}) collective-permute-start(bf16[128,512]{1,0:T(8,128)(2,1)S(1)} %collective-permute-done.12), channel_id=1, source_target_pairs={{0,8},{2,6},{8,16},{10,2},{16,24},{18,10},{24,28},{26,18},{28,20},... | collective-permute-start | bytes 393224 | tf_op jit(solution)/shard_map/ppermute | solution.py:311
  55.0 0.5 collective-permute-start.18
  55.5 0.2 broadcast_in_dim.99.clone
  55.8 1.8 %collective-permute-start.32 = (bf16[128,512]{1,0:T(8,128)(2,1)S(1)}, bf16[128,512]{1,0:T(8,128)(2,1)S(1)}, u32[]{:S(2)}, u32[]{:S(2)}) collective-permute-start(bf16[128,512]{1,0:T(8,128)(2,1)S(1)} %collective-permute-done.28), channel_id=1, source_target_pairs={{0,8},{2,6},{8,16},{10,2},{16,24},{18,10},{24,28},{26,18},{28,20},... | collective-permute-start | bytes 393224 | tf_op jit(solution)/shard_map/ppermute | solution.py:311
  57.8 2.4 %collective-permute-start.30 = (bf16[128,512]{1,0:T(8,128)(2,1)S(1)}, bf16[128,512]{1,0:T(8,128)(2,1)S(1)}, u32[]{:S(2)}, u32[]{:S(2)}) collective-permute-start(bf16[128,512]{1,0:T(8,128)(2,1)S(1)} %collective-permute-done.27), channel_id=1, source_target_pairs={{0,8},{2,6},{8,16},{10,2},{16,24},{18,10},{24,28},{26,18},{28,20},... | collective-permute-start | bytes 393224 | tf_op jit(solution)/shard_map/ppermute | solution.py:311
  60.2 1.2 %collective-permute-start.20 = (bf16[128,512]{1,0:T(8,128)(2,1)S(1)}, bf16[128,512]{1,0:T(8,128)(2,1)S(1)}, u32[]{:S(2)}, u32[]{:S(2)}) collective-permute-start(bf16[128,512]{1,0:T(8,128)(2,1)S(1)} %collective-permute-done.16), channel_id=1, source_target_pairs={{0,8},{2,6},{8,16},{10,2},{16,24},{18,10},{24,28},{26,18},{28,20},... | collective-permute-start | bytes 393224 | tf_op jit(solution)/shard_map/ppermute | solution.py:311
  61.5 1.1 %collective-permute-start.22 = (bf16[128,512]{1,0:T(8,128)(2,1)S(1)}, bf16[128,512]{1,0:T(8,128)(2,1)S(1)}, u32[]{:S(2)}, u32[]{:S(2)}) collective-permute-start(bf16[128,512]{1,0:T(8,128)(2,1)S(1)} %collective-permute-done.18), channel_id=1, source_target_pairs={{0,8},{2,6},{8,16},{10,2},{16,24},{18,10},{24,28},{26,18},{28,20},... | collective-permute-start | bytes 393224 | tf_op jit(solution)/shard_map/ppermute | solution.py:311
  62.8 1.1 %collective-permute-start.36 = (bf16[128,512]{1,0:T(8,128)(2,1)S(1)}, bf16[128,512]{1,0:T(8,128)(2,1)S(1)}, u32[]{:S(2)}, u32[]{:S(2)}) collective-permute-start(bf16[128,512]{1,0:T(8,128)(2,1)S(1)} %collective-permute-done.32), channel_id=1, source_target_pairs={{0,8},{2,6},{8,16},{10,2},{16,24},{18,10},{24,28},{26,18},{28,20},... | collective-permute-start | bytes 393224 | tf_op jit(solution)/shard_map/ppermute | solution.py:311
  63.9 0.1 collective-permute-start.33
  64.1 0.5 collective-permute-start.31
  64.6 0.6 collective-permute-done.20
  65.1 1.4 %collective-permute-start.34 = (bf16[128,512]{1,0:T(8,128)(2,1)S(1)}, bf16[128,512]{1,0:T(8,128)(2,1)S(1)}, u32[]{:S(2)}, u32[]{:S(2)}) collective-permute-start(bf16[128,512]{1,0:T(8,128)(2,1)S(1)} %collective-permute-done.30), channel_id=1, source_target_pairs={{0,8},{2,6},{8,16},{10,2},{16,24},{18,10},{24,28},{26,18},{28,20},... | collective-permute-start | bytes 393224 | tf_op jit(solution)/shard_map/ppermute | solution.py:311
  66.6 1.2 %collective-permute-start.24 = (bf16[128,512]{1,0:T(8,128)(2,1)S(1)}, bf16[128,512]{1,0:T(8,128)(2,1)S(1)}, u32[]{:S(2)}, u32[]{:S(2)}) collective-permute-start(bf16[128,512]{1,0:T(8,128)(2,1)S(1)} %collective-permute-done.20), channel_id=1, source_target_pairs={{0,8},{2,6},{8,16},{10,2},{16,24},{18,10},{24,28},{26,18},{28,20},... | collective-permute-start | bytes 393224 | tf_op jit(solution)/shard_map/ppermute | solution.py:311
  67.9 0.1 collective-permute-done.36
  68.0 0.4 collective-permute-start.23
  68.4 1.0 %collective-permute-start.40 = (bf16[128,512]{1,0:T(8,128)(2,1)S(1)}, bf16[128,512]{1,0:T(8,128)(2,1)S(1)}, u32[]{:S(2)}, u32[]{:S(2)}) collective-permute-start(bf16[128,512]{1,0:T(8,128)(2,1)S(1)} %collective-permute-done.36), channel_id=1, source_target_pairs={{0,8},{2,6},{8,16},{10,2},{16,24},{18,10},{24,28},{26,18},{28,20},... | collective-permute-start | bytes 393224 | tf_op jit(solution)/shard_map/ppermute | solution.py:311
  69.5 0.7 collective-permute-done.34
  70.1 1.4 %collective-permute-start.38 = (bf16[128,512]{1,0:T(8,128)(2,1)S(1)}, bf16[128,512]{1,0:T(8,128)(2,1)S(1)}, u32[]{:S(2)}, u32[]{:S(2)}) collective-permute-start(bf16[128,512]{1,0:T(8,128)(2,1)S(1)} %collective-permute-done.34), channel_id=1, source_target_pairs={{0,8},{2,6},{8,16},{10,2},{16,24},{18,10},{24,28},{26,18},{28,20},... | collective-permute-start | bytes 393224 | tf_op jit(solution)/shard_map/ppermute | solution.py:311
  71.7 0.5 collective-permute-start.25
  72.2 1.1 %collective-permute-done.40 = bf16[128,512]{1,0:T(8,128)(2,1)S(1)} collective-permute-done((bf16[128,512]{1,0:T(8,128)(2,1)S(1)}, bf16[128,512]{1,0:T(8,128)(2,1)S(1)}, u32[]{:S(2)}, u32[]{:S(2)}) %collective-permute-start.40) | collective-permute-done | bytes 131104 | tf_op jit(solution)/shard_map/ppermute | solution.py:311
  73.3 1.7 %collective-permute-done.38 = bf16[128,512]{1,0:T(8,128)(2,1)S(1)} collective-permute-done((bf16[128,512]{1,0:T(8,128)(2,1)S(1)}, bf16[128,512]{1,0:T(8,128)(2,1)S(1)}, u32[]{:S(2)}, u32[]{:S(2)}) %collective-permute-start.38) | collective-permute-done | bytes 131104 | tf_op jit(solution)/shard_map/ppermute | solution.py:311
  75.2 1.2 %collective-permute-done.39 = bf16[128,512]{1,0:T(8,128)(2,1)S(1)} collective-permute-done((bf16[128,512]{1,0:T(8,128)(2,1)S(1)}, bf16[128,512]{1,0:T(8,128)(2,1)S(1)}, u32[]{:S(2)}, u32[]{:S(2)}) %collective-permute-start.39) | collective-permute-done | bytes 131104 | tf_op jit(solution)/shard_map/ppermute | solution.py:242
  76.6 2.7 %maximum_select_fusion = bf16[8,256,1024]{2,1,0:T(8,128)(2,1)} fusion(bf16[8,256,512]{2,1,0:T(8,128)(2,1)S(1)} %bitcast.75, bf16[8,256,512]{2,1,0:T(8,128)(2,1)S(1)} %bitcast.76, pred[]{:T(512)S(6)} %eq.44), kind=kLoop, calls=%fused_computation | loop fusion | flops 18874368 | bytes 8388609 | tf_op jit(solution)/shard_map/jit(_where)/select_n | solution.py:333
  (83 shorter events, 1.5 us)
Async XLA Ops:
  0.6 15.1 %collective-permute-start = (bf16[128,512]{1,0:T(8,128)(2,1)}, bf16[128,512]{1,0:T(8,128)(2,1)S(1)}, u32[]{:S(2)}, u32[]{:S(2)}) collective-permute-start(bf16[128,512]{1,0:T(8,128)(2,1)} %param.5), channel_id=1, source_target_pairs={{0,16},{2,18},{4,20},{6,22},{8,24},{10,26},{12,28},{14,30},{16,0},... | collective-permute-start | bytes 393224 | tf_op jit(solution)/shard_map/ppermute | solution.py:273
  4.8 1.2 %copy-start = (bf16[128,4096]{1,0:T(8,128)(2,1)S(1)}, bf16[128,4096]{1,0:T(8,128)(2,1)}, u32[]{:S(2)}) copy-start(bf16[128,4096]{1,0:T(8,128)(2,1)} %inputs_ref.1) | copy-start | bytes 3145732
  6.6 16.4 %collective-permute-start.1 = (bf16[128,512]{1,0:T(8,128)(2,1)S(1)}, bf16[128,512]{1,0:T(8,128)(2,1)S(1)}, u32[]{:S(2)}, u32[]{:S(2)}) collective-permute-start(bf16[128,512]{1,0:T(8,128)(2,1)S(1)} %get-tuple-element.14), channel_id=1, source_target_pairs={{0,4},{2,6},{4,0},{6,2},{8,12},{10,14},{12,8},{14,10},{16,20},{18,... | collective-permute-start | bytes 393224 | tf_op jit(solution)/shard_map/ppermute | solution.py:273
  8.2 12.4 %collective-permute-start.2 = (bf16[128,512]{1,0:T(8,128)(2,1)S(1)}, bf16[128,512]{1,0:T(8,128)(2,1)S(1)}, u32[]{:S(2)}, u32[]{:S(2)}) collective-permute-start(bf16[128,512]{1,0:T(8,128)(2,1)S(1)} %get-tuple-element.15), channel_id=1, source_target_pairs={{0,16},{1,21},{2,18},{3,23},{4,20},{5,17},{6,22},{7,19},{8,24},{9,... | collective-permute-start | bytes 393224 | tf_op jit(solution)/shard_map/ppermute | solution.py:257
  8.6 14.4 %collective-permute-start.3 = (bf16[128,512]{1,0:T(8,128)(2,1)S(1)}, bf16[128,512]{1,0:T(8,128)(2,1)S(1)}, u32[]{:S(2)}, u32[]{:S(2)}) collective-permute-start(bf16[128,512]{1,0:T(8,128)(2,1)S(1)} %get-tuple-element.16), channel_id=1, source_target_pairs={{0,28},{1,25},{2,30},{3,27},{4,24},{5,29},{6,26},{7,31},{8,20},{9,... | collective-permute-start | bytes 393224 | tf_op jit(solution)/shard_map/ppermute | solution.py:257
  12.1 3.6 %copy-start.1 = (bf16[128,512]{1,0:T(8,128)(2,1)S(1)}, bf16[128,512]{1,0:T(8,128)(2,1)}, u32[]{:S(2)}) copy-start(bf16[128,512]{1,0:T(8,128)(2,1)} %param.5) | copy-start | bytes 393220
  12.1 11.5 %collective-permute-start.4 = (bf16[128,512]{1,0:T(8,128)(2,1)S(1)}, bf16[128,512]{1,0:T(8,128)(2,1)S(1)}, u32[]{:S(2)}, u32[]{:S(2)}) collective-permute-start(bf16[128,512]{1,0:T(8,128)(2,1)S(1)} %get-tuple-element.17), channel_id=1, source_target_pairs={{0,8},{1,13},{2,10},{3,15},{4,12},{5,9},{6,14},{7,11},{8,0},{9,5},... | collective-permute-start | bytes 393224 | tf_op jit(solution)/shard_map/ppermute | solution.py:257
  15.8 16.5 %collective-permute-start.10 = (bf16[256,512]{1,0:T(8,128)(2,1)S(1)}, bf16[256,512]{1,0:T(8,128)(2,1)S(1)}, u32[]{:S(2)}, u32[]{:S(2)}) collective-permute-start(bf16[256,512]{1,0:T(8,128)(2,1)S(1)} %constant_dynamic-update-slice_fusion.refs_6_), channel_id=1, source_target_pairs={{0,12},{2,14},{4,8},{6,10},{8,4},{10,6},{12,0},{14,2},{16,28},{18,... | collective-permute-start | bytes 786440 | tf_op jit(solution)/shard_map/ppermute | solution.py:273
  20.6 6.2 %collective-permute-start.5 = (bf16[128,512]{1,0:T(8,128)(2,1)S(1)}, bf16[128,512]{1,0:T(8,128)(2,1)S(1)}, u32[]{:S(2)}, u32[]{:S(2)}) collective-permute-start(bf16[128,512]{1,0:T(8,128)(2,1)S(1)} %collective-permute-done.2.refs_0_), channel_id=1, source_target_pairs={{0,1},{1,0},{2,3},{3,2},{4,5},{5,4},{6,7},{7,6},{8,9},{9,8},{10,11... | collective-permute-start | bytes 393224 | tf_op jit(solution)/shard_map/ppermute | solution.py:245
  23.0 9.3 %collective-permute-start.9 = (bf16[256,512]{1,0:T(8,128)(2,1)S(1)}, bf16[256,512]{1,0:T(8,128)(2,1)S(1)}, u32[]{:S(2)}, u32[]{:S(2)}) collective-permute-start(bf16[256,512]{1,0:T(8,128)(2,1)S(1)} %constant_dynamic-update-slice_fusion.refs_6_), channel_id=1, source_target_pairs={{0,8},{2,10},{4,12},{6,14},{8,0},{10,2},{12,4},{14,6},{16,24},{18,... | collective-permute-start | bytes 786440 | tf_op jit(solution)/shard_map/ppermute | solution.py:273
  23.0 10.6 %collective-permute-start.8 = (bf16[256,512]{1,0:T(8,128)(2,1)S(1)}, bf16[256,512]{1,0:T(8,128)(2,1)S(1)}, u32[]{:S(2)}, u32[]{:S(2)}) collective-permute-start(bf16[256,512]{1,0:T(8,128)(2,1)S(1)} %constant_dynamic-update-slice_fusion.refs_6_), channel_id=1, source_target_pairs={{0,4},{2,6},{4,0},{6,2},{8,12},{10,14},{12,8},{14,10},{16,20},{18,... | collective-permute-start | bytes 786440 | tf_op jit(solution)/shard_map/ppermute | solution.py:273
  23.6 6.4 %collective-permute-start.6 = (bf16[128,512]{1,0:T(8,128)(2,1)S(1)}, bf16[128,512]{1,0:T(8,128)(2,1)S(1)}, u32[]{:S(2)}, u32[]{:S(2)}) collective-permute-start(bf16[128,512]{1,0:T(8,128)(2,1)S(1)} %collective-permute-done.3.refs_1_), channel_id=1, source_target_pairs={{0,1},{1,0},{2,3},{3,2},{4,5},{5,4},{6,7},{7,6},{8,9},{9,8},{10,11... | collective-permute-start | bytes 393224 | tf_op jit(solution)/shard_map/ppermute | solution.py:245
  26.8 5.4 %collective-permute-start.7 = (bf16[128,512]{1,0:T(8,128)(2,1)S(1)}, bf16[128,512]{1,0:T(8,128)(2,1)S(1)}, u32[]{:S(2)}, u32[]{:S(2)}) collective-permute-start(bf16[128,512]{1,0:T(8,128)(2,1)S(1)} %collective-permute-done.4.refs_2_), channel_id=1, source_target_pairs={{0,1},{1,0},{2,3},{3,2},{4,5},{5,4},{6,7},{7,6},{8,9},{9,8},{10,11... | collective-permute-start | bytes 393224 | tf_op jit(solution)/shard_map/ppermute | solution.py:245
  35.0 2.7 %collective-permute-start.11 = (f32[512,512]{1,0:T(8,128)S(1)}, f32[512,512]{1,0:T(8,128)S(1)}, u32[]{:S(2)}, u32[]{:S(2)}) collective-permute-start(f32[512,512]{1,0:T(8,128)S(1)} %shard_map.51.mine_ref), channel_id=1, source_target_pairs={{0,2},{2,0},{4,6},{6,4},{8,10},{10,8},{12,14},{14,12},{16,18},{18,... | collective-permute-start | bytes 3145736 | tf_op jit(solution)/shard_map/ppermute | solution.py:242
  45.2 5.6 %collective-permute-start.26 = (bf16[128,512]{1,0:T(8,128)(2,1)S(1)}, bf16[128,512]{1,0:T(8,128)(2,1)S(1)}, u32[]{:S(2)}, u32[]{:S(2)}) collective-permute-start(bf16[128,512]{1,0:T(8,128)(2,1)S(1)} %get-tuple-element.21), channel_id=1, source_target_pairs={{0,1},{1,0},{2,3},{3,2},{4,5},{5,4},{6,7},{7,6},{8,9},{9,8},{10,11... | collective-permute-start | bytes 393224 | tf_op jit(solution)/shard_map/ppermute | solution.py:245
  46.3 5.6 %collective-permute-start.12 = (bf16[128,512]{1,0:T(8,128)(2,1)S(1)}, bf16[128,512]{1,0:T(8,128)(2,1)S(1)}, u32[]{:S(2)}, u32[]{:S(2)}) collective-permute-start(bf16[128,512]{1,0:T(8,128)(2,1)S(1)} %get-tuple-element.19), channel_id=1, source_target_pairs={{0,8},{2,6},{8,16},{10,2},{16,24},{18,10},{24,28},{26,18},{28,20},... | collective-permute-start | bytes 393224 | tf_op jit(solution)/shard_map/ppermute | solution.py:311
  46.4 8.6 %collective-permute-start.14 = (bf16[128,512]{1,0:T(8,128)(2,1)S(1)}, bf16[128,512]{1,0:T(8,128)(2,1)S(1)}, u32[]{:S(2)}, u32[]{:S(2)}) collective-permute-start(bf16[128,512]{1,0:T(8,128)(2,1)S(1)} %get-tuple-element.20), channel_id=1, source_target_pairs={{0,8},{2,6},{8,16},{10,2},{16,24},{18,10},{24,28},{26,18},{28,20},... | collective-permute-start | bytes 393224 | tf_op jit(solution)/shard_map/ppermute | solution.py:311
  50.8 5.0 %collective-permute-start.28 = (bf16[128,512]{1,0:T(8,128)(2,1)S(1)}, bf16[128,512]{1,0:T(8,128)(2,1)S(1)}, u32[]{:S(2)}, u32[]{:S(2)}) collective-permute-start(bf16[128,512]{1,0:T(8,128)(2,1)S(1)} %collective-permute-done.26), channel_id=1, source_target_pairs={{0,8},{2,6},{8,16},{10,2},{16,24},{18,10},{24,28},{26,18},{28,20},... | collective-permute-start | bytes 393224 | tf_op jit(solution)/shard_map/ppermute | solution.py:311
  51.9 3.9 %collective-permute-start.27 = (bf16[128,512]{1,0:T(8,128)(2,1)S(1)}, bf16[128,512]{1,0:T(8,128)(2,1)S(1)}, u32[]{:S(2)}, u32[]{:S(2)}) collective-permute-start(bf16[128,512]{1,0:T(8,128)(2,1)S(1)} %collective-permute-done.26), channel_id=1, source_target_pairs={{0,2},{2,0},{4,6},{6,4},{8,10},{10,8},{12,14},{14,12},{16,18},{18,... | collective-permute-start | bytes 393224 | tf_op jit(solution)/shard_map/ppermute | solution.py:242
  51.9 5.9 %collective-permute-start.16 = (bf16[128,512]{1,0:T(8,128)(2,1)S(1)}, bf16[128,512]{1,0:T(8,128)(2,1)S(1)}, u32[]{:S(2)}, u32[]{:S(2)}) collective-permute-start(bf16[128,512]{1,0:T(8,128)(2,1)S(1)} %collective-permute-done.12), channel_id=1, source_target_pairs={{0,8},{2,6},{8,16},{10,2},{16,24},{18,10},{24,28},{26,18},{28,20},... | collective-permute-start | bytes 393224 | tf_op jit(solution)/shard_map/ppermute | solution.py:311
  55.0 2.7 %collective-permute-start.13 = (bf16[128,512]{1,0:T(8,128)(2,1)S(1)}, bf16[128,512]{1,0:T(8,128)(2,1)S(1)}, u32[]{:S(2)}, u32[]{:S(2)}) collective-permute-start(bf16[128,512]{1,0:T(8,128)(2,1)S(1)} %collective-permute-done.12), channel_id=1, source_target_pairs={{0,2},{2,0},{4,6},{6,4},{8,10},{10,8},{12,14},{14,12},{16,18},{18,... | collective-permute-start | bytes 393224 | tf_op jit(solution)/shard_map/ppermute | solution.py:242
  55.0 6.4 %collective-permute-start.18 = (bf16[128,512]{1,0:T(8,128)(2,1)S(1)}, bf16[128,512]{1,0:T(8,128)(2,1)S(1)}, u32[]{:S(2)}, u32[]{:S(2)}) collective-permute-start(bf16[128,512]{1,0:T(8,128)(2,1)S(1)} %collective-permute-done.14), channel_id=1, source_target_pairs={{0,8},{2,6},{8,16},{10,2},{16,24},{18,10},{24,28},{26,18},{28,20},... | collective-permute-start | bytes 393224 | tf_op jit(solution)/shard_map/ppermute | solution.py:311
  55.8 4.4 %collective-permute-start.15 = (bf16[128,512]{1,0:T(8,128)(2,1)S(1)}, bf16[128,512]{1,0:T(8,128)(2,1)S(1)}, u32[]{:S(2)}, u32[]{:S(2)}) collective-permute-start(bf16[128,512]{1,0:T(8,128)(2,1)S(1)} %collective-permute-done.14), channel_id=1, source_target_pairs={{0,2},{2,0},{4,6},{6,4},{8,10},{10,8},{12,14},{14,12},{16,18},{18,... | collective-permute-start | bytes 393224 | tf_op jit(solution)/shard_map/ppermute | solution.py:242
  55.8 6.8 %collective-permute-start.32 = (bf16[128,512]{1,0:T(8,128)(2,1)S(1)}, bf16[128,512]{1,0:T(8,128)(2,1)S(1)}, u32[]{:S(2)}, u32[]{:S(2)}) collective-permute-start(bf16[128,512]{1,0:T(8,128)(2,1)S(1)} %collective-permute-done.28), channel_id=1, source_target_pairs={{0,8},{2,6},{8,16},{10,2},{16,24},{18,10},{24,28},{26,18},{28,20},... | collective-permute-start | bytes 393224 | tf_op jit(solution)/shard_map/ppermute | solution.py:311
  57.7 3.8 %collective-permute-start.29 = (bf16[128,512]{1,0:T(8,128)(2,1)S(1)}, bf16[128,512]{1,0:T(8,128)(2,1)S(1)}, u32[]{:S(2)}, u32[]{:S(2)}) collective-permute-start(bf16[128,512]{1,0:T(8,128)(2,1)S(1)} %collective-permute-done.28), channel_id=1, source_target_pairs={{0,2},{2,0},{4,6},{6,4},{8,10},{10,8},{12,14},{14,12},{16,18},{18,... | collective-permute-start | bytes 393224 | tf_op jit(solution)/shard_map/ppermute | solution.py:242
  57.8 6.1 %collective-permute-start.30 = (bf16[128,512]{1,0:T(8,128)(2,1)S(1)}, bf16[128,512]{1,0:T(8,128)(2,1)S(1)}, u32[]{:S(2)}, u32[]{:S(2)}) collective-permute-start(bf16[128,512]{1,0:T(8,128)(2,1)S(1)} %collective-permute-done.27), channel_id=1, source_target_pairs={{0,8},{2,6},{8,16},{10,2},{16,24},{18,10},{24,28},{26,18},{28,20},... | collective-permute-start | bytes 393224 | tf_op jit(solution)/shard_map/ppermute | solution.py:311
  60.2 5.0 %collective-permute-start.20 = (bf16[128,512]{1,0:T(8,128)(2,1)S(1)}, bf16[128,512]{1,0:T(8,128)(2,1)S(1)}, u32[]{:S(2)}, u32[]{:S(2)}) collective-permute-start(bf16[128,512]{1,0:T(8,128)(2,1)S(1)} %collective-permute-done.16), channel_id=1, source_target_pairs={{0,8},{2,6},{8,16},{10,2},{16,24},{18,10},{24,28},{26,18},{28,20},... | collective-permute-start | bytes 393224 | tf_op jit(solution)/shard_map/ppermute | solution.py:311
  61.4 1.4 %collective-permute-start.17 = (bf16[128,512]{1,0:T(8,128)(2,1)S(1)}, bf16[128,512]{1,0:T(8,128)(2,1)S(1)}, u32[]{:S(2)}, u32[]{:S(2)}) collective-permute-start(bf16[128,512]{1,0:T(8,128)(2,1)S(1)} %collective-permute-done.16), channel_id=1, source_target_pairs={{0,2},{2,0},{4,6},{6,4},{8,10},{10,8},{12,14},{14,12},{16,18},{18,... | collective-permute-start | bytes 393224 | tf_op jit(solution)/shard_map/ppermute | solution.py:242
  61.5 6.3 %collective-permute-start.22 = (bf16[128,512]{1,0:T(8,128)(2,1)S(1)}, bf16[128,512]{1,0:T(8,128)(2,1)S(1)}, u32[]{:S(2)}, u32[]{:S(2)}) collective-permute-start(bf16[128,512]{1,0:T(8,128)(2,1)S(1)} %collective-permute-done.18), channel_id=1, source_target_pairs={{0,8},{2,6},{8,16},{10,2},{16,24},{18,10},{24,28},{26,18},{28,20},... | collective-permute-start | bytes 393224 | tf_op jit(solution)/shard_map/ppermute | solution.py:311
  62.7 1.4 %collective-permute-start.19 = (bf16[128,512]{1,0:T(8,128)(2,1)S(1)}, bf16[128,512]{1,0:T(8,128)(2,1)S(1)}, u32[]{:S(2)}, u32[]{:S(2)}) collective-permute-start(bf16[128,512]{1,0:T(8,128)(2,1)S(1)} %collective-permute-done.18), channel_id=1, source_target_pairs={{0,2},{2,0},{4,6},{6,4},{8,10},{10,8},{12,14},{14,12},{16,18},{18,... | collective-permute-start | bytes 393224 | tf_op jit(solution)/shard_map/ppermute | solution.py:242
  62.8 5.1 %collective-permute-start.36 = (bf16[128,512]{1,0:T(8,128)(2,1)S(1)}, bf16[128,512]{1,0:T(8,128)(2,1)S(1)}, u32[]{:S(2)}, u32[]{:S(2)}) collective-permute-start(bf16[128,512]{1,0:T(8,128)(2,1)S(1)} %collective-permute-done.32), channel_id=1, source_target_pairs={{0,8},{2,6},{8,16},{10,2},{16,24},{18,10},{24,28},{26,18},{28,20},... | collective-permute-start | bytes 393224 | tf_op jit(solution)/shard_map/ppermute | solution.py:311
  63.9 4.4 %collective-permute-start.33 = (bf16[128,512]{1,0:T(8,128)(2,1)S(1)}, bf16[128,512]{1,0:T(8,128)(2,1)S(1)}, u32[]{:S(2)}, u32[]{:S(2)}) collective-permute-start(bf16[128,512]{1,0:T(8,128)(2,1)S(1)} %collective-permute-done.32), channel_id=1, source_target_pairs={{0,2},{2,0},{4,6},{6,4},{8,10},{10,8},{12,14},{14,12},{16,18},{18,... | collective-permute-start | bytes 393224 | tf_op jit(solution)/shard_map/ppermute | solution.py:242
  64.1 2.5 %collective-permute-start.31 = (bf16[128,512]{1,0:T(8,128)(2,1)S(1)}, bf16[128,512]{1,0:T(8,128)(2,1)S(1)}, u32[]{:S(2)}, u32[]{:S(2)}) collective-permute-start(bf16[128,512]{1,0:T(8,128)(2,1)S(1)} %collective-permute-done.30), channel_id=1, source_target_pairs={{0,2},{2,0},{4,6},{6,4},{8,10},{10,8},{12,14},{14,12},{16,18},{18,... | collective-permute-start | bytes 393224 | tf_op jit(solution)/shard_map/ppermute | solution.py:242
  65.1 5.0 %collective-permute-start.34 = (bf16[128,512]{1,0:T(8,128)(2,1)S(1)}, bf16[128,512]{1,0:T(8,128)(2,1)S(1)}, u32[]{:S(2)}, u32[]{:S(2)}) collective-permute-start(bf16[128,512]{1,0:T(8,128)(2,1)S(1)} %collective-permute-done.30), channel_id=1, source_target_pairs={{0,8},{2,6},{8,16},{10,2},{16,24},{18,10},{24,28},{26,18},{28,20},... | collective-permute-start | bytes 393224 | tf_op jit(solution)/shard_map/ppermute | solution.py:311
  66.6 5.0 %collective-permute-start.24 = (bf16[128,512]{1,0:T(8,128)(2,1)S(1)}, bf16[128,512]{1,0:T(8,128)(2,1)S(1)}, u32[]{:S(2)}, u32[]{:S(2)}) collective-permute-start(bf16[128,512]{1,0:T(8,128)(2,1)S(1)} %collective-permute-done.20), channel_id=1, source_target_pairs={{0,8},{2,6},{8,16},{10,2},{16,24},{18,10},{24,28},{26,18},{28,20},... | collective-permute-start | bytes 393224 | tf_op jit(solution)/shard_map/ppermute | solution.py:311
  67.8 2.3 %collective-permute-start.21 = (bf16[128,512]{1,0:T(8,128)(2,1)S(1)}, bf16[128,512]{1,0:T(8,128)(2,1)S(1)}, u32[]{:S(2)}, u32[]{:S(2)}) collective-permute-start(bf16[128,512]{1,0:T(8,128)(2,1)S(1)} %collective-permute-done.20), channel_id=1, source_target_pairs={{0,2},{2,0},{4,6},{6,4},{8,10},{10,8},{12,14},{14,12},{16,18},{18,... | collective-permute-start | bytes 393224 | tf_op jit(solution)/shard_map/ppermute | solution.py:242
  68.0 3.7 %collective-permute-start.23 = (bf16[128,512]{1,0:T(8,128)(2,1)S(1)}, bf16[128,512]{1,0:T(8,128)(2,1)S(1)}, u32[]{:S(2)}, u32[]{:S(2)}) collective-permute-start(bf16[128,512]{1,0:T(8,128)(2,1)S(1)} %collective-permute-done.22), channel_id=1, source_target_pairs={{0,2},{2,0},{4,6},{6,4},{8,10},{10,8},{12,14},{14,12},{16,18},{18,... | collective-permute-start | bytes 393224 | tf_op jit(solution)/shard_map/ppermute | solution.py:242
  68.4 5.0 %collective-permute-start.40 = (bf16[128,512]{1,0:T(8,128)(2,1)S(1)}, bf16[128,512]{1,0:T(8,128)(2,1)S(1)}, u32[]{:S(2)}, u32[]{:S(2)}) collective-permute-start(bf16[128,512]{1,0:T(8,128)(2,1)S(1)} %collective-permute-done.36), channel_id=1, source_target_pairs={{0,8},{2,6},{8,16},{10,2},{16,24},{18,10},{24,28},{26,18},{28,20},... | collective-permute-start | bytes 393224 | tf_op jit(solution)/shard_map/ppermute | solution.py:311
  70.1 5.0 %collective-permute-start.37 = (bf16[128,512]{1,0:T(8,128)(2,1)S(1)}, bf16[128,512]{1,0:T(8,128)(2,1)S(1)}, u32[]{:S(2)}, u32[]{:S(2)}) collective-permute-start(bf16[128,512]{1,0:T(8,128)(2,1)S(1)} %collective-permute-done.36), channel_id=1, source_target_pairs={{0,2},{2,0},{4,6},{6,4},{8,10},{10,8},{12,14},{14,12},{16,18},{18,... | collective-permute-start | bytes 393224 | tf_op jit(solution)/shard_map/ppermute | solution.py:242
  70.1 5.0 %collective-permute-start.38 = (bf16[128,512]{1,0:T(8,128)(2,1)S(1)}, bf16[128,512]{1,0:T(8,128)(2,1)S(1)}, u32[]{:S(2)}, u32[]{:S(2)}) collective-permute-start(bf16[128,512]{1,0:T(8,128)(2,1)S(1)} %collective-permute-done.34), channel_id=1, source_target_pairs={{0,8},{2,6},{8,16},{10,2},{16,24},{18,10},{24,28},{26,18},{28,20},... | collective-permute-start | bytes 393224 | tf_op jit(solution)/shard_map/ppermute | solution.py:311
  71.6 3.5 %collective-permute-start.35 = (bf16[128,512]{1,0:T(8,128)(2,1)S(1)}, bf16[128,512]{1,0:T(8,128)(2,1)S(1)}, u32[]{:S(2)}, u32[]{:S(2)}) collective-permute-start(bf16[128,512]{1,0:T(8,128)(2,1)S(1)} %collective-permute-done.34), channel_id=1, source_target_pairs={{0,2},{2,0},{4,6},{6,4},{8,10},{10,8},{12,14},{14,12},{16,18},{18,... | collective-permute-start | bytes 393224 | tf_op jit(solution)/shard_map/ppermute | solution.py:242
  71.7 4.8 %collective-permute-start.25 = (bf16[128,512]{1,0:T(8,128)(2,1)S(1)}, bf16[128,512]{1,0:T(8,128)(2,1)S(1)}, u32[]{:S(2)}, u32[]{:S(2)}) collective-permute-start(bf16[128,512]{1,0:T(8,128)(2,1)S(1)} %collective-permute-done.24), channel_id=1, source_target_pairs={{0,2},{2,0},{4,6},{6,4},{8,10},{10,8},{12,14},{14,12},{16,18},{18,... | collective-permute-start | bytes 393224 | tf_op jit(solution)/shard_map/ppermute | solution.py:242
  73.3 3.2 %collective-permute-start.41 = (bf16[128,512]{1,0:T(8,128)(2,1)S(1)}, bf16[128,512]{1,0:T(8,128)(2,1)S(1)}, u32[]{:S(2)}, u32[]{:S(2)}) collective-permute-start(bf16[128,512]{1,0:T(8,128)(2,1)S(1)} %collective-permute-done.40), channel_id=1, source_target_pairs={{0,2},{2,0},{4,6},{6,4},{8,10},{10,8},{12,14},{14,12},{16,18},{18,... | collective-permute-start | bytes 393224 | tf_op jit(solution)/shard_map/ppermute | solution.py:242
  75.1 1.3 %collective-permute-start.39 = (bf16[128,512]{1,0:T(8,128)(2,1)S(1)}, bf16[128,512]{1,0:T(8,128)(2,1)S(1)}, u32[]{:S(2)}, u32[]{:S(2)}) collective-permute-start(bf16[128,512]{1,0:T(8,128)(2,1)S(1)} %collective-permute-done.38), channel_id=1, source_target_pairs={{0,2},{2,0},{4,6},{6,4},{8,10},{10,8},{12,14},{14,12},{16,18},{18,... | collective-permute-start | bytes 393224 | tf_op jit(solution)/shard_map/ppermute | solution.py:242

commit v8 on v7

--- a/solution.py
+++ b/solution.py
@@ -272,13 +272,14 @@
         ]
         return lax.ppermute(array, "dp", pairs)
 
-    outputs = jnp.dot(inputs, weight, preferred_element_type=jnp.float32).astype(jnp.bfloat16)
-    far_cot, outputs = lax.optimization_barrier((exchange(cotangent, 4), outputs))
+    far_cot = exchange(cotangent, 4)
     near = [deal(packed[hop], hop) for hop in hops]
     shared = exchange(packed[-1], SHARED)
     pair = jnp.concatenate([cotangent, far_cot])
     cots = [pair] + [exchange(pair, offset) for offset in (1, 2, 3)]
     far = [swap_plane(piece) for piece in near]
+    outputs = jnp.dot(inputs, weight, preferred_element_type=jnp.float32).astype(jnp.bfloat16)
+    own_band, outputs = lax.optimization_barrier((own_band, outputs))
     (partial_tile,) = call(
         tile_kernel,
         [jax.ShapeDtypeStruct((BLOCK, BLOCK), jnp.float32)],
@@ -312,23 +313,25 @@
 
     half_way = bands // 2
     crossed = swap_plane(far_piece)
-    heads = [near_piece, next_piece, crossed, swap_core(crossed)]
+    heads = [near_piece[None], crossed[None], jnp.stack([next_piece, swap_core(crossed)])]
+    chunks = [(0,), (1,), (0, 1)]
+    halves = [core, core, 1 - core]
     columns = [jnp.zeros((bands, cores, rows, BLOCK), jnp.bfloat16)] * 2
 
-    def put(chunk, piece, position, half):
-        columns[chunk] = lax.dynamic_update_slice(
-            columns[chunk], piece[None, None], (ring_band(position, bands), half, 0, 0)
-        )
+    def put(parts, pieces, position, half):
+        for chunk, piece in zip(parts, pieces):
+            columns[chunk] = lax.dynamic_update_slice(
+                columns[chunk], piece[None, None], (ring_band(position, bands), half, 0, 0)
+            )
 
     for hop in range(half_way + 1):
         for k, head in enumerate(heads):
-            chunk, half = k // 2, (core if k % 2 == 0 else 1 - core)
-            if hop == half_way and k % 2 == 1:
+            if hop == half_way and k == 2:
                 continue
             if hop > 0:
                 heads[k] = head = turn(head)
-                put(chunk, swap_core(head), spot + ahead * hop, 1 - half)
-            put(chunk, head, spot - ahead * hop, half)
+                put(chunks[k], swap_core(head), spot + ahead * hop, 1 - halves[k])
+            put(chunks[k], head, spot - ahead * hop, halves[k])
     former, latter = (column.reshape(bands, cores * rows, BLOCK) for column in columns)
     update = jnp.where(
         plane == 0,

time: 79.4 us -> 87.4 us (1.10)
  waiting for transfers between devices: 17.3 us -> 28.7 us
  starting transfers between devices: 42.5 us -> 38.3 us
    ppermute x14 -> x11, waiting for transfers between devices: 4.28 us -> 10.3 us  [turn(): return lax.ppermute(array, 'dp', pairs)]
    ppermute x3, waiting for transfers between devices: 1.79 us -> 7.45 us  [deal(): return lax.ppermute(array, ('dp', 'pre'), pairs)]
    ppermute x5, starting transfers between devices: 9.35 us -> 5.41 us  [exchange(): return lax.ppermute(array, 'dp', pairs)]
    ppermute x14 -> x11, starting transfers between devices: 20.4 us -> 16.5 us  [turn(): return lax.ppermute(array, 'dp', pairs)]
    ppermute x3, starting transfers between devices: 3.88 us -> 7.65 us  [deal(): return lax.ppermute(array, ('dp', 'pre'), pairs)]
    ppermute x4, waiting for transfers between devices: 6.21 us -> 4.17 us  [swap_plane(): lax.ppermute(array, 'pre', [(c, members - 1 - c) for c in range(members)])]
    ppermute x16 -> x13, waiting for transfers between devices: 3.65 us -> 4.82 us  [swap_core(): return lax.ppermute(array, 'dp', [(g, g ^ 1) for g in range(groups)])]
    unnamed x5 -> x3, local copies, waits for them, and re-layouts: 1.24 us -> 2.14 us
  transfers between devices with their start and end apart: 42 -> 36, of which waited for: 15 -> 14; matrix products, arithmetic and copies ran while one was open for 6% -> 6% of each run, Pallas kernels for 1% -> 0%
where the time goes in v8:
time: 87.4 us; the launch traced here: 87.2 us
  starting transfers between devices  38.3 us (44%)
  waiting for transfers between devices  28.7 us (33%)
  Pallas kernels  9.42 us (11%)
  matrix products  3.57 us (4%)
  local copies, waits for them, and re-layouts  3.09 us (4%)
  other arithmetic  2.84 us (3%)
  between operations  1.29 us (1%)
    ppermute x11, starting transfers between devices, turn(): return lax.ppermute(array, 'dp', pairs)  16.5 us
    ppermute x11, waiting for transfers between devices, turn(): return lax.ppermute(array, 'dp', pairs)  10.3 us
    pallas_call x3, Pallas kernels, call(): pl.pallas_call(kernel, out_shape=out_shapes, in_specs=in_specs, out_specs...  9.42 us
    ppermute x3, starting transfers between devices, deal(): return lax.ppermute(array, ('dp', 'pre'), pairs)  7.65 us
    ppermute x3, waiting for transfers between devices, deal(): return lax.ppermute(array, ('dp', 'pre'), pairs)  7.45 us
    ppermute x4, starting transfers between devices, swap_plane(): lax.ppermute(array, 'pre', [(c, members - 1 - c) for c in range(members)])  7.03 us
    ppermute x5, starting transfers between devices, exchange(): return lax.ppermute(array, 'dp', pairs)  5.41 us
    ppermute x13, waiting for transfers between devices, swap_core(): return lax.ppermute(array, 'dp', [(g, g ^ 1) for g in range(groups)])  4.82 us
  transfers between devices with their start and end apart: 36, of which 14 were waited for; matrix products, arithmetic and copies ran while one was open for 6% of the time, Pallas kernels for 0%

profile of v8, /device:TPU:0, one launch (start us, length us, event | category | flops | bytes accessed | tf_op | source)
XLA Modules:
  0.0 87.2 jit_solution(11259882550537731527)
XLA Ops:
  0.7 0.1 stack.46.place_ref
  0.7 1.2 %copy-done = bf16[128,4096]{1,0:T(8,128)(2,1)S(1)} copy-done((bf16[128,4096]{1,0:T(8,128)(2,1)S(1)}, bf16[128,4096]{1,0:T(8,128)(2,1)}, u32[]{:S(2)}) %copy-start) | copy-done | bytes 1048600
  2.0 0.6 shard_map.50
  2.6 4.1 %collective-permute-start.1 = (bf16[128,512]{1,0:T(8,128)(2,1)S(1)}, bf16[128,512]{1,0:T(8,128)(2,1)S(1)}, u32[]{:S(2)}, u32[]{:S(2)}) collective-permute-start(bf16[128,512]{1,0:T(8,128)(2,1)S(1)} %get-tuple-element.16), channel_id=1, source_target_pairs={{0,16},{1,21},{2,18},{3,23},{4,20},{5,17},{6,22},{7,19},{8,24},{9,... | collective-permute-start | bytes 393224 | tf_op jit(solution)/shard_map/ppermute | solution.py:257
  6.7 0.1 collective-permute-start.7
  6.7 1.8 %collective-permute-start = (bf16[128,512]{1,0:T(8,128)(2,1)S(1)}, bf16[128,512]{1,0:T(8,128)(2,1)S(1)}, u32[]{:S(2)}, u32[]{:S(2)}) collective-permute-start(bf16[128,512]{1,0:T(8,128)(2,1)S(1)} %get-tuple-element.15), channel_id=1, source_target_pairs={{0,4},{2,6},{4,0},{6,2},{8,12},{10,14},{12,8},{14,10},{16,20},{18,... | collective-permute-start | bytes 393224 | tf_op jit(solution)/shard_map/ppermute | solution.py:273
  8.5 3.5 %collective-permute-start.2 = (bf16[128,512]{1,0:T(8,128)(2,1)S(1)}, bf16[128,512]{1,0:T(8,128)(2,1)S(1)}, u32[]{:S(2)}, u32[]{:S(2)}) collective-permute-start(bf16[128,512]{1,0:T(8,128)(2,1)S(1)} %get-tuple-element.17), channel_id=1, source_target_pairs={{0,28},{1,25},{2,30},{3,27},{4,24},{5,29},{6,26},{7,31},{8,20},{9,... | collective-permute-start | bytes 393224 | tf_op jit(solution)/shard_map/ppermute | solution.py:257
  12.1 7.4 %collective-permute-done.1.refs_0_ = bf16[128,512]{1,0:T(8,128)(2,1)S(1)} collective-permute-done((bf16[128,512]{1,0:T(8,128)(2,1)S(1)}, bf16[128,512]{1,0:T(8,128)(2,1)S(1)}, u32[]{:S(2)}, u32[]{:S(2)}) %collective-permute-start.1) | collective-permute-done | bytes 131104 | tf_op jit(solution)/shard_map/ppermute | solution.py:257
  19.5 2.7 %collective-permute-start.4 = (bf16[128,512]{1,0:T(8,128)(2,1)S(1)}, bf16[128,512]{1,0:T(8,128)(2,1)S(1)}, u32[]{:S(2)}, u32[]{:S(2)}) collective-permute-start(bf16[128,512]{1,0:T(8,128)(2,1)S(1)} %collective-permute-done.1.refs_0_), channel_id=1, source_target_pairs={{0,1},{1,0},{2,3},{3,2},{4,5},{5,4},{6,7},{7,6},{8,9},{9,8},{10,11... | collective-permute-start | bytes 393224 | tf_op jit(solution)/shard_map/ppermute | solution.py:245
  22.3 0.9 %constant_dynamic-update-slice_fusion.1 = bf16[256,512]{1,0:T(8,128)(2,1)S(1)} fusion(bf16[128,512]{1,0:T(8,128)(2,1)} %param.5), kind=kLoop, calls=%fused_computation.48 | loop fusion | bytes 262144
  23.2 1.6 %collective-permute-start.8 = (bf16[256,512]{1,0:T(8,128)(2,1)S(1)}, bf16[256,512]{1,0:T(8,128)(2,1)S(1)}, u32[]{:S(2)}, u32[]{:S(2)}) collective-permute-start(bf16[256,512]{1,0:T(8,128)(2,1)S(1)} %constant_dynamic-update-slice_fusion.refs_6_), channel_id=1, source_target_pairs={{0,4},{2,6},{4,0},{6,2},{8,12},{10,14},{12,8},{14,10},{16,20},{18,... | collective-permute-start | bytes 786440 | tf_op jit(solution)/shard_map/ppermute | solution.py:273
  24.8 2.0 %collective-permute-start.10 = (bf16[256,512]{1,0:T(8,128)(2,1)S(1)}, bf16[256,512]{1,0:T(8,128)(2,1)S(1)}, u32[]{:S(2)}, u32[]{:S(2)}) collective-permute-start(bf16[256,512]{1,0:T(8,128)(2,1)S(1)} %constant_dynamic-update-slice_fusion.refs_6_), channel_id=1, source_target_pairs={{0,12},{2,14},{4,8},{6,10},{8,4},{10,6},{12,0},{14,2},{16,28},{18,... | collective-permute-start | bytes 786440 | tf_op jit(solution)/shard_map/ppermute | solution.py:273
  26.8 1.9 %collective-permute-start.5 = (bf16[128,512]{1,0:T(8,128)(2,1)S(1)}, bf16[128,512]{1,0:T(8,128)(2,1)S(1)}, u32[]{:S(2)}, u32[]{:S(2)}) collective-permute-start(bf16[128,512]{1,0:T(8,128)(2,1)S(1)} %collective-permute-done.2.refs_1_), channel_id=1, source_target_pairs={{0,1},{1,0},{2,3},{3,2},{4,5},{5,4},{6,7},{7,6},{8,9},{9,8},{10,11... | collective-permute-start | bytes 393224 | tf_op jit(solution)/shard_map/ppermute | solution.py:245
  28.6 0.2 collective-permute-start.6
  28.8 3.6 %convolution_convert_fusion = bf16[128,512]{1,0:T(8,128)(2,1)} fusion(bf16[128,4096]{1,0:T(8,128)(2,1)S(1)} %copy-done, bf16[4096,512]{1,0:T(8,128)(2,1)} %param.4), kind=kOutput, calls=%fused_computation.1 | convolution fusion | flops 536936448 | bytes 5373952 | tf_op jit(solution)/shard_map/dot_general | solution.py:281
  32.4 0.1 pad_add_fusion.1.place_ref
  32.5 1.4 %collective-permute-done.6.refs_5_ = bf16[128,512]{1,0:T(8,128)(2,1)S(1)} collective-permute-done((bf16[128,512]{1,0:T(8,128)(2,1)S(1)}, bf16[128,512]{1,0:T(8,128)(2,1)S(1)}, u32[]{:S(2)}, u32[]{:S(2)}) %collective-permute-start.6) | collective-permute-done | bytes 131104 | tf_op jit(solution)/shard_map/ppermute | solution.py:245
  33.9 1.9 %collective-permute-done.10.refs_9_ = bf16[256,512]{1,0:T(8,128)(2,1)S(1)} collective-permute-done((bf16[256,512]{1,0:T(8,128)(2,1)S(1)}, bf16[256,512]{1,0:T(8,128)(2,1)S(1)}, u32[]{:S(2)}, u32[]{:S(2)}) %collective-permute-start.10) | collective-permute-done | bytes 262176 | tf_op jit(solution)/shard_map/ppermute | solution.py:273
  35.9 1.4 %shard_map.51.mine_ref = f32[512,512]{1,0:T(8,128)S(1)} custom-call(s32[2]{0:T(128)S(1)} %pad_add_fusion.1.place_ref, bf16[128,512]{1,0:T(8,128)(2,1)S(1)} %get-tuple-element.14.own_ref, bf16[128,512]{1,0:T(8,128)(2,1)S(1)} %collective-permute-done.shared_ref, bf16[128,512]{1,0:T(8,128)(2,1)S(1)} %collective-permute-done.1.refs_0_, ...), custom_call_target="tpu_custom_call" | custom-call | tf_op jit(solution)/shard_map/pallas_call | solution.py:217
  37.6 0.1 pad_add_fusion.side_ref
  37.7 2.3 %collective-permute-done.11.other_ref = f32[512,512]{1,0:T(8,128)S(1)} collective-permute-done((f32[512,512]{1,0:T(8,128)S(1)}, f32[512,512]{1,0:T(8,128)S(1)}, u32[]{:S(2)}, u32[]{:S(2)}) %collective-permute-start.11) | collective-permute-done | bytes 1048608 | tf_op jit(solution)/shard_map/ppermute | solution.py:242
  40.0 7.4 %shard_map.52 = (bf16[128,512]{1,0:T(8,128)(2,1)S(1)}, bf16[128,512]{1,0:T(8,128)(2,1)S(1)}, bf16[128,512]{1,0:T(8,128)(2,1)S(1)}) custom-call(s32[2]{0:T(128)S(1)} %pad_add_fusion.side_ref, f32[512,512]{1,0:T(8,128)S(1)} %shard_map.51.mine_ref, f32[512,512]{1,0:T(8,128)S(1)} %collective-permute-done.11.other_ref), custom_call_target="tpu_custom_call" | custom-call | tf_op jit(solution)/shard_map/pallas_call | solution.py:217
  47.4 1.8 %collective-permute-start.12 = (bf16[1,128,512]{2,1,0:T(8,128)(2,1)S(1)}, bf16[1,128,512]{2,1,0:T(8,128)(2,1)S(1)}, u32[]{:S(2)}, u32[]{:S(2)}) collective-permute-start(bf16[1,128,512]{2,1,0:T(8,128)(2,1)S(1)} %bitcast.104), channel_id=1, source_target_pairs={{0,8},{2,6},{8,16},{10,2},{16,24},{18,10},{24,28},{26,18},{28,20},... | collective-permute-start | bytes 393224 | tf_op jit(solution)/shard_map/ppermute | solution.py:312
  49.2 2.3 %collective-permute-start.14 = (bf16[128,512]{1,0:T(8,128)(2,1)S(1)}, bf16[128,512]{1,0:T(8,128)(2,1)S(1)}, u32[]{:S(2)}, u32[]{:S(2)}) collective-permute-start(bf16[128,512]{1,0:T(8,128)(2,1)S(1)} %get-tuple-element.21), channel_id=1, source_target_pairs={{0,1},{1,0},{2,3},{3,2},{4,5},{5,4},{6,7},{7,6},{8,9},{9,8},{10,11... | collective-permute-start | bytes 393224 | tf_op jit(solution)/shard_map/ppermute | solution.py:245
  51.4 0.2 broadcast_in_dim.9.clone
  51.7 2.7 %collective-permute-done.14 = bf16[128,512]{1,0:T(8,128)(2,1)S(1)} collective-permute-done((bf16[128,512]{1,0:T(8,128)(2,1)S(1)}, bf16[128,512]{1,0:T(8,128)(2,1)S(1)}, u32[]{:S(2)}, u32[]{:S(2)}) %collective-permute-start.14) | collective-permute-done | bytes 131104 | tf_op jit(solution)/shard_map/ppermute | solution.py:245
  54.4 2.1 %collective-permute-start.28 = (bf16[1,128,512]{2,1,0:T(8,128)(2,1)S(1)}, bf16[1,128,512]{2,1,0:T(8,128)(2,1)S(1)}, u32[]{:S(2)}, u32[]{:S(2)}) collective-permute-start(bf16[1,128,512]{2,1,0:T(8,128)(2,1)S(1)} %bitcast.108), channel_id=1, source_target_pairs={{0,8},{2,6},{8,16},{10,2},{16,24},{18,10},{24,28},{26,18},{28,20},... | collective-permute-start | bytes 393224 | tf_op jit(solution)/shard_map/ppermute | solution.py:312
  56.5 0.5 collective-permute-start.13
  57.0 1.7 %collective-permute-start.18 = (bf16[1,128,512]{2,1,0:T(8,128)(2,1)S(1)}, bf16[1,128,512]{2,1,0:T(8,128)(2,1)S(1)}, u32[]{:S(2)}, u32[]{:S(2)}) collective-permute-start(bf16[1,128,512]{2,1,0:T(8,128)(2,1)S(1)} %collective-permute-done.12), channel_id=1, source_target_pairs={{0,8},{2,6},{8,16},{10,2},{16,24},{18,10},{24,28},{26,18},{28,20},... | collective-permute-start | bytes 393224 | tf_op jit(solution)/shard_map/ppermute | solution.py:312
  58.7 0.2 broadcast_in_dim.9.clone.1
  59.0 1.4 %collective-permute-start.16 = (bf16[2,128,512]{2,1,0:T(8,128)(2,1)S(1)}, bf16[2,128,512]{2,1,0:T(8,128)(2,1)S(1)}, u32[]{:S(2)}, u32[]{:S(2)}) collective-permute-start(bf16[2,128,512]{2,1,0:T(8,128)(2,1)S(1)} %pad_maximum_fusion), channel_id=1, source_target_pairs={{0,8},{2,6},{8,16},{10,2},{16,24},{18,10},{24,28},{26,18},{28,20},... | collective-permute-start | bytes 786440 | tf_op jit(solution)/shard_map/ppermute | solution.py:312
  60.4 1.3 %collective-permute-start.30 = (bf16[1,128,512]{2,1,0:T(8,128)(2,1)S(1)}, bf16[1,128,512]{2,1,0:T(8,128)(2,1)S(1)}, u32[]{:S(2)}, u32[]{:S(2)}) collective-permute-start(bf16[1,128,512]{2,1,0:T(8,128)(2,1)S(1)} %collective-permute-done.28), channel_id=1, source_target_pairs={{0,8},{2,6},{8,16},{10,2},{16,24},{18,10},{24,28},{26,18},{28,20},... | collective-permute-start | bytes 393224 | tf_op jit(solution)/shard_map/ppermute | solution.py:312
  61.7 0.3 collective-permute-done.18
  62.0 1.8 %collective-permute-start.22 = (bf16[1,128,512]{2,1,0:T(8,128)(2,1)S(1)}, bf16[1,128,512]{2,1,0:T(8,128)(2,1)S(1)}, u32[]{:S(2)}, u32[]{:S(2)}) collective-permute-start(bf16[1,128,512]{2,1,0:T(8,128)(2,1)S(1)} %collective-permute-done.18), channel_id=1, source_target_pairs={{0,8},{2,6},{8,16},{10,2},{16,24},{18,10},{24,28},{26,18},{28,20},... | collective-permute-start | bytes 393224 | tf_op jit(solution)/shard_map/ppermute | solution.py:312
  63.8 3.0 %collective-permute-done.30 = bf16[1,128,512]{2,1,0:T(8,128)(2,1)S(1)} collective-permute-done((bf16[1,128,512]{2,1,0:T(8,128)(2,1)S(1)}, bf16[1,128,512]{2,1,0:T(8,128)(2,1)S(1)}, u32[]{:S(2)}, u32[]{:S(2)}) %collective-permute-start.30) | collective-permute-done | bytes 131104 | tf_op jit(solution)/shard_map/ppermute | solution.py:312
  66.9 1.3 %collective-permute-start.32 = (bf16[1,128,512]{2,1,0:T(8,128)(2,1)S(1)}, bf16[1,128,512]{2,1,0:T(8,128)(2,1)S(1)}, u32[]{:S(2)}, u32[]{:S(2)}) collective-permute-start(bf16[1,128,512]{2,1,0:T(8,128)(2,1)S(1)} %collective-permute-done.30), channel_id=1, source_target_pairs={{0,8},{2,6},{8,16},{10,2},{16,24},{18,10},{24,28},{26,18},{28,20},... | collective-permute-start | bytes 393224 | tf_op jit(solution)/shard_map/ppermute | solution.py:312
  68.3 0.5 collective-permute-start.17
  68.8 1.2 %collective-permute-done.17 = bf16[2,128,512]{2,1,0:T(8,128)(2,1)S(1)} collective-permute-done((bf16[2,128,512]{2,1,0:T(8,128)(2,1)S(1)}, bf16[2,128,512]{2,1,0:T(8,128)(2,1)S(1)}, u32[]{:S(2)}, u32[]{:S(2)}) %collective-permute-start.17) | collective-permute-done | bytes 262176 | tf_op jit(solution)/shard_map/ppermute | solution.py:242
  70.0 1.3 %collective-permute-start.20 = (bf16[2,128,512]{2,1,0:T(8,128)(2,1)S(1)}, bf16[2,128,512]{2,1,0:T(8,128)(2,1)S(1)}, u32[]{:S(2)}, u32[]{:S(2)}) collective-permute-start(bf16[2,128,512]{2,1,0:T(8,128)(2,1)S(1)} %collective-permute-done.16), channel_id=1, source_target_pairs={{0,8},{2,6},{8,16},{10,2},{16,24},{18,10},{24,28},{26,18},{28,20},... | collective-permute-start | bytes 786440 | tf_op jit(solution)/shard_map/ppermute | solution.py:312
  71.4 1.3 %collective-permute-start.26 = (bf16[1,128,512]{2,1,0:T(8,128)(2,1)S(1)}, bf16[1,128,512]{2,1,0:T(8,128)(2,1)S(1)}, u32[]{:S(2)}, u32[]{:S(2)}) collective-permute-start(bf16[1,128,512]{2,1,0:T(8,128)(2,1)S(1)} %collective-permute-done.22), channel_id=1, source_target_pairs={{0,8},{2,6},{8,16},{10,2},{16,24},{18,10},{24,28},{26,18},{28,20},... | collective-permute-start | bytes 393224 | tf_op jit(solution)/shard_map/ppermute | solution.py:312
  72.7 1.1 %collective-permute-start.34 = (bf16[1,128,512]{2,1,0:T(8,128)(2,1)S(1)}, bf16[1,128,512]{2,1,0:T(8,128)(2,1)S(1)}, u32[]{:S(2)}, u32[]{:S(2)}) collective-permute-start(bf16[1,128,512]{2,1,0:T(8,128)(2,1)S(1)} %collective-permute-done.32), channel_id=1, source_target_pairs={{0,8},{2,6},{8,16},{10,2},{16,24},{18,10},{24,28},{26,18},{28,20},... | collective-permute-start | bytes 393224 | tf_op jit(solution)/shard_map/ppermute | solution.py:312
  73.8 2.6 %collective-permute-done.20 = bf16[2,128,512]{2,1,0:T(8,128)(2,1)S(1)} collective-permute-done((bf16[2,128,512]{2,1,0:T(8,128)(2,1)S(1)}, bf16[2,128,512]{2,1,0:T(8,128)(2,1)S(1)}, u32[]{:S(2)}, u32[]{:S(2)}) %collective-permute-start.20) | collective-permute-done | bytes 262176 | tf_op jit(solution)/shard_map/ppermute | solution.py:312
  76.4 1.4 %collective-permute-start.24 = (bf16[2,128,512]{2,1,0:T(8,128)(2,1)S(1)}, bf16[2,128,512]{2,1,0:T(8,128)(2,1)S(1)}, u32[]{:S(2)}, u32[]{:S(2)}) collective-permute-start(bf16[2,128,512]{2,1,0:T(8,128)(2,1)S(1)} %collective-permute-done.20), channel_id=1, source_target_pairs={{0,8},{2,6},{8,16},{10,2},{16,24},{18,10},{24,28},{26,18},{28,20},... | collective-permute-start | bytes 786440 | tf_op jit(solution)/shard_map/ppermute | solution.py:312
  77.9 1.2 %collective-permute-done.34 = bf16[1,128,512]{2,1,0:T(8,128)(2,1)S(1)} collective-permute-done((bf16[1,128,512]{2,1,0:T(8,128)(2,1)S(1)}, bf16[1,128,512]{2,1,0:T(8,128)(2,1)S(1)}, u32[]{:S(2)}, u32[]{:S(2)}) %collective-permute-start.34) | collective-permute-done | bytes 131104 | tf_op jit(solution)/shard_map/ppermute | solution.py:312
  79.2 0.5 collective-permute-start.35
  79.7 3.2 %collective-permute-done.24 = bf16[2,128,512]{2,1,0:T(8,128)(2,1)S(1)} collective-permute-done((bf16[2,128,512]{2,1,0:T(8,128)(2,1)S(1)}, bf16[2,128,512]{2,1,0:T(8,128)(2,1)S(1)}, u32[]{:S(2)}, u32[]{:S(2)}) %collective-permute-start.24) | collective-permute-done | bytes 262176 | tf_op jit(solution)/shard_map/ppermute | solution.py:312
  83.0 1.3 %collective-permute-done.25 = bf16[2,128,512]{2,1,0:T(8,128)(2,1)S(1)} collective-permute-done((bf16[2,128,512]{2,1,0:T(8,128)(2,1)S(1)}, bf16[2,128,512]{2,1,0:T(8,128)(2,1)S(1)}, u32[]{:S(2)}, u32[]{:S(2)}) %collective-permute-start.25) | collective-permute-done | bytes 262176 | tf_op jit(solution)/shard_map/ppermute | solution.py:242
  84.5 2.7 %maximum_select_fusion = bf16[8,256,1024]{2,1,0:T(8,128)(2,1)} fusion(bf16[8,256,512]{2,1,0:T(8,128)(2,1)S(1)} %bitcast.105, bf16[8,256,512]{2,1,0:T(8,128)(2,1)S(1)} %bitcast.106, pred[]{:T(512)S(6)} %eq.44), kind=kLoop, calls=%fused_computation | loop fusion | flops 18874368 | bytes 8388609 | tf_op jit(solution)/shard_map/jit(_where)/select_n | solution.py:336
  (64 shorter events, 0.9 us)
Async XLA Ops:
  0.7 1.2 %copy-start = (bf16[128,4096]{1,0:T(8,128)(2,1)S(1)}, bf16[128,4096]{1,0:T(8,128)(2,1)}, u32[]{:S(2)}) copy-start(bf16[128,4096]{1,0:T(8,128)(2,1)} %inputs_ref.1) | copy-start | bytes 3145732
  2.6 17.0 %collective-permute-start.1 = (bf16[128,512]{1,0:T(8,128)(2,1)S(1)}, bf16[128,512]{1,0:T(8,128)(2,1)S(1)}, u32[]{:S(2)}, u32[]{:S(2)}) collective-permute-start(bf16[128,512]{1,0:T(8,128)(2,1)S(1)} %get-tuple-element.16), channel_id=1, source_target_pairs={{0,16},{1,21},{2,18},{3,23},{4,20},{5,17},{6,22},{7,19},{8,24},{9,... | collective-permute-start | bytes 393224 | tf_op jit(solution)/shard_map/ppermute | solution.py:257
  6.7 16.5 %collective-permute-start.7 = (bf16[128,512]{1,0:T(8,128)(2,1)}, bf16[128,512]{1,0:T(8,128)(2,1)S(1)}, u32[]{:S(2)}, u32[]{:S(2)}) collective-permute-start(bf16[128,512]{1,0:T(8,128)(2,1)} %param.5), channel_id=1, source_target_pairs={{0,16},{2,18},{4,20},{6,22},{8,24},{10,26},{12,28},{14,30},{16,0},... | collective-permute-start | bytes 393224 | tf_op jit(solution)/shard_map/ppermute | solution.py:273
  6.7 18.0 %collective-permute-start = (bf16[128,512]{1,0:T(8,128)(2,1)S(1)}, bf16[128,512]{1,0:T(8,128)(2,1)S(1)}, u32[]{:S(2)}, u32[]{:S(2)}) collective-permute-start(bf16[128,512]{1,0:T(8,128)(2,1)S(1)} %get-tuple-element.15), channel_id=1, source_target_pairs={{0,4},{2,6},{4,0},{6,2},{8,12},{10,14},{12,8},{14,10},{16,20},{18,... | collective-permute-start | bytes 393224 | tf_op jit(solution)/shard_map/ppermute | solution.py:273
  8.5 16.3 %collective-permute-start.2 = (bf16[128,512]{1,0:T(8,128)(2,1)S(1)}, bf16[128,512]{1,0:T(8,128)(2,1)S(1)}, u32[]{:S(2)}, u32[]{:S(2)}) collective-permute-start(bf16[128,512]{1,0:T(8,128)(2,1)S(1)} %get-tuple-element.17), channel_id=1, source_target_pairs={{0,28},{1,25},{2,30},{3,27},{4,24},{5,29},{6,26},{7,31},{8,20},{9,... | collective-permute-start | bytes 393224 | tf_op jit(solution)/shard_map/ppermute | solution.py:257
  12.1 14.7 %collective-permute-start.3 = (bf16[128,512]{1,0:T(8,128)(2,1)S(1)}, bf16[128,512]{1,0:T(8,128)(2,1)S(1)}, u32[]{:S(2)}, u32[]{:S(2)}) collective-permute-start(bf16[128,512]{1,0:T(8,128)(2,1)S(1)} %get-tuple-element.18), channel_id=1, source_target_pairs={{0,8},{1,13},{2,10},{3,15},{4,12},{5,9},{6,14},{7,11},{8,0},{9,5},... | collective-permute-start | bytes 393224 | tf_op jit(solution)/shard_map/ppermute | solution.py:257
  19.5 9.1 %collective-permute-start.4 = (bf16[128,512]{1,0:T(8,128)(2,1)S(1)}, bf16[128,512]{1,0:T(8,128)(2,1)S(1)}, u32[]{:S(2)}, u32[]{:S(2)}) collective-permute-start(bf16[128,512]{1,0:T(8,128)(2,1)S(1)} %collective-permute-done.1.refs_0_), channel_id=1, source_target_pairs={{0,1},{1,0},{2,3},{3,2},{4,5},{5,4},{6,7},{7,6},{8,9},{9,8},{10,11... | collective-permute-start | bytes 393224 | tf_op jit(solution)/shard_map/ppermute | solution.py:245
  23.2 10.7 %collective-permute-start.8 = (bf16[256,512]{1,0:T(8,128)(2,1)S(1)}, bf16[256,512]{1,0:T(8,128)(2,1)S(1)}, u32[]{:S(2)}, u32[]{:S(2)}) collective-permute-start(bf16[256,512]{1,0:T(8,128)(2,1)S(1)} %constant_dynamic-update-slice_fusion.refs_6_), channel_id=1, source_target_pairs={{0,4},{2,6},{4,0},{6,2},{8,12},{10,14},{12,8},{14,10},{16,20},{18,... | collective-permute-start | bytes 786440 | tf_op jit(solution)/shard_map/ppermute | solution.py:273
  24.8 9.1 %collective-permute-start.9 = (bf16[256,512]{1,0:T(8,128)(2,1)S(1)}, bf16[256,512]{1,0:T(8,128)(2,1)S(1)}, u32[]{:S(2)}, u32[]{:S(2)}) collective-permute-start(bf16[256,512]{1,0:T(8,128)(2,1)S(1)} %constant_dynamic-update-slice_fusion.refs_6_), channel_id=1, source_target_pairs={{0,8},{2,10},{4,12},{6,14},{8,0},{10,2},{12,4},{14,6},{16,24},{18,... | collective-permute-start | bytes 786440 | tf_op jit(solution)/shard_map/ppermute | solution.py:273
  24.8 11.1 %collective-permute-start.10 = (bf16[256,512]{1,0:T(8,128)(2,1)S(1)}, bf16[256,512]{1,0:T(8,128)(2,1)S(1)}, u32[]{:S(2)}, u32[]{:S(2)}) collective-permute-start(bf16[256,512]{1,0:T(8,128)(2,1)S(1)} %constant_dynamic-update-slice_fusion.refs_6_), channel_id=1, source_target_pairs={{0,12},{2,14},{4,8},{6,10},{8,4},{10,6},{12,0},{14,2},{16,28},{18,... | collective-permute-start | bytes 786440 | tf_op jit(solution)/shard_map/ppermute | solution.py:273
  26.8 5.7 %collective-permute-start.5 = (bf16[128,512]{1,0:T(8,128)(2,1)S(1)}, bf16[128,512]{1,0:T(8,128)(2,1)S(1)}, u32[]{:S(2)}, u32[]{:S(2)}) collective-permute-start(bf16[128,512]{1,0:T(8,128)(2,1)S(1)} %collective-permute-done.2.refs_1_), channel_id=1, source_target_pairs={{0,1},{1,0},{2,3},{3,2},{4,5},{5,4},{6,7},{7,6},{8,9},{9,8},{10,11... | collective-permute-start | bytes 393224 | tf_op jit(solution)/shard_map/ppermute | solution.py:245
  28.6 5.3 %collective-permute-start.6 = (bf16[128,512]{1,0:T(8,128)(2,1)S(1)}, bf16[128,512]{1,0:T(8,128)(2,1)S(1)}, u32[]{:S(2)}, u32[]{:S(2)}) collective-permute-start(bf16[128,512]{1,0:T(8,128)(2,1)S(1)} %collective-permute-done.3.refs_2_), channel_id=1, source_target_pairs={{0,1},{1,0},{2,3},{3,2},{4,5},{5,4},{6,7},{7,6},{8,9},{9,8},{10,11... | collective-permute-start | bytes 393224 | tf_op jit(solution)/shard_map/ppermute | solution.py:245
  37.3 2.7 %collective-permute-start.11 = (f32[512,512]{1,0:T(8,128)S(1)}, f32[512,512]{1,0:T(8,128)S(1)}, u32[]{:S(2)}, u32[]{:S(2)}) collective-permute-start(f32[512,512]{1,0:T(8,128)S(1)} %shard_map.51.mine_ref), channel_id=1, source_target_pairs={{0,2},{2,0},{4,6},{6,4},{8,10},{10,8},{12,14},{14,12},{16,18},{18,... | collective-permute-start | bytes 3145736 | tf_op jit(solution)/shard_map/ppermute | solution.py:242
  47.4 9.1 %collective-permute-start.12 = (bf16[1,128,512]{2,1,0:T(8,128)(2,1)S(1)}, bf16[1,128,512]{2,1,0:T(8,128)(2,1)S(1)}, u32[]{:S(2)}, u32[]{:S(2)}) collective-permute-start(bf16[1,128,512]{2,1,0:T(8,128)(2,1)S(1)} %bitcast.104), channel_id=1, source_target_pairs={{0,8},{2,6},{8,16},{10,2},{16,24},{18,10},{24,28},{26,18},{28,20},... | collective-permute-start | bytes 393224 | tf_op jit(solution)/shard_map/ppermute | solution.py:312
  49.2 5.2 %collective-permute-start.14 = (bf16[128,512]{1,0:T(8,128)(2,1)S(1)}, bf16[128,512]{1,0:T(8,128)(2,1)S(1)}, u32[]{:S(2)}, u32[]{:S(2)}) collective-permute-start(bf16[128,512]{1,0:T(8,128)(2,1)S(1)} %get-tuple-element.21), channel_id=1, source_target_pairs={{0,1},{1,0},{2,3},{3,2},{4,5},{5,4},{6,7},{7,6},{8,9},{9,8},{10,11... | collective-permute-start | bytes 393224 | tf_op jit(solution)/shard_map/ppermute | solution.py:245
  54.4 6.0 %collective-permute-start.28 = (bf16[1,128,512]{2,1,0:T(8,128)(2,1)S(1)}, bf16[1,128,512]{2,1,0:T(8,128)(2,1)S(1)}, u32[]{:S(2)}, u32[]{:S(2)}) collective-permute-start(bf16[1,128,512]{2,1,0:T(8,128)(2,1)S(1)} %bitcast.108), channel_id=1, source_target_pairs={{0,8},{2,6},{8,16},{10,2},{16,24},{18,10},{24,28},{26,18},{28,20},... | collective-permute-start | bytes 393224 | tf_op jit(solution)/shard_map/ppermute | solution.py:312
  56.5 2.5 %collective-permute-start.15 = (bf16[128,512]{1,0:T(8,128)(2,1)S(1)}, bf16[128,512]{1,0:T(8,128)(2,1)S(1)}, u32[]{:S(2)}, u32[]{:S(2)}) collective-permute-start(bf16[128,512]{1,0:T(8,128)(2,1)S(1)} %collective-permute-done.14), channel_id=1, source_target_pairs={{0,2},{2,0},{4,6},{6,4},{8,10},{10,8},{12,14},{14,12},{16,18},{18,... | collective-permute-start | bytes 393224 | tf_op jit(solution)/shard_map/ppermute | solution.py:242
  56.5 5.5 %collective-permute-start.13 = (bf16[1,128,512]{2,1,0:T(8,128)(2,1)S(1)}, bf16[1,128,512]{2,1,0:T(8,128)(2,1)S(1)}, u32[]{:S(2)}, u32[]{:S(2)}) collective-permute-start(bf16[1,128,512]{2,1,0:T(8,128)(2,1)S(1)} %collective-permute-done.12), channel_id=1, source_target_pairs={{0,2},{2,0},{4,6},{6,4},{8,10},{10,8},{12,14},{14,12},{16,18},{18,... | collective-permute-start | bytes 393224 | tf_op jit(solution)/shard_map/ppermute | solution.py:242
  57.0 5.0 %collective-permute-start.18 = (bf16[1,128,512]{2,1,0:T(8,128)(2,1)S(1)}, bf16[1,128,512]{2,1,0:T(8,128)(2,1)S(1)}, u32[]{:S(2)}, u32[]{:S(2)}) collective-permute-start(bf16[1,128,512]{2,1,0:T(8,128)(2,1)S(1)} %collective-permute-done.12), channel_id=1, source_target_pairs={{0,8},{2,6},{8,16},{10,2},{16,24},{18,10},{24,28},{26,18},{28,20},... | collective-permute-start | bytes 393224 | tf_op jit(solution)/shard_map/ppermute | solution.py:312
  59.0 9.2 %collective-permute-start.16 = (bf16[2,128,512]{2,1,0:T(8,128)(2,1)S(1)}, bf16[2,128,512]{2,1,0:T(8,128)(2,1)S(1)}, u32[]{:S(2)}, u32[]{:S(2)}) collective-permute-start(bf16[2,128,512]{2,1,0:T(8,128)(2,1)S(1)} %pad_maximum_fusion), channel_id=1, source_target_pairs={{0,8},{2,6},{8,16},{10,2},{16,24},{18,10},{24,28},{26,18},{28,20},... | collective-permute-start | bytes 786440 | tf_op jit(solution)/shard_map/ppermute | solution.py:312
  60.4 6.4 %collective-permute-start.29 = (bf16[1,128,512]{2,1,0:T(8,128)(2,1)S(1)}, bf16[1,128,512]{2,1,0:T(8,128)(2,1)S(1)}, u32[]{:S(2)}, u32[]{:S(2)}) collective-permute-start(bf16[1,128,512]{2,1,0:T(8,128)(2,1)S(1)} %collective-permute-done.28), channel_id=1, source_target_pairs={{0,2},{2,0},{4,6},{6,4},{8,10},{10,8},{12,14},{14,12},{16,18},{18,... | collective-permute-start | bytes 393224 | tf_op jit(solution)/shard_map/ppermute | solution.py:242
  60.4 6.4 %collective-permute-start.30 = (bf16[1,128,512]{2,1,0:T(8,128)(2,1)S(1)}, bf16[1,128,512]{2,1,0:T(8,128)(2,1)S(1)}, u32[]{:S(2)}, u32[]{:S(2)}) collective-permute-start(bf16[1,128,512]{2,1,0:T(8,128)(2,1)S(1)} %collective-permute-done.28), channel_id=1, source_target_pairs={{0,8},{2,6},{8,16},{10,2},{16,24},{18,10},{24,28},{26,18},{28,20},... | collective-permute-start | bytes 393224 | tf_op jit(solution)/shard_map/ppermute | solution.py:312
  62.0 9.4 %collective-permute-start.19 = (bf16[1,128,512]{2,1,0:T(8,128)(2,1)S(1)}, bf16[1,128,512]{2,1,0:T(8,128)(2,1)S(1)}, u32[]{:S(2)}, u32[]{:S(2)}) collective-permute-start(bf16[1,128,512]{2,1,0:T(8,128)(2,1)S(1)} %collective-permute-done.18), channel_id=1, source_target_pairs={{0,2},{2,0},{4,6},{6,4},{8,10},{10,8},{12,14},{14,12},{16,18},{18,... | collective-permute-start | bytes 393224 | tf_op jit(solution)/shard_map/ppermute | solution.py:242
  62.0 6.2 %collective-permute-start.22 = (bf16[1,128,512]{2,1,0:T(8,128)(2,1)S(1)}, bf16[1,128,512]{2,1,0:T(8,128)(2,1)S(1)}, u32[]{:S(2)}, u32[]{:S(2)}) collective-permute-start(bf16[1,128,512]{2,1,0:T(8,128)(2,1)S(1)} %collective-permute-done.18), channel_id=1, source_target_pairs={{0,8},{2,6},{8,16},{10,2},{16,24},{18,10},{24,28},{26,18},{28,20},... | collective-permute-start | bytes 393224 | tf_op jit(solution)/shard_map/ppermute | solution.py:312
  66.9 9.5 %collective-permute-start.31 = (bf16[1,128,512]{2,1,0:T(8,128)(2,1)S(1)}, bf16[1,128,512]{2,1,0:T(8,128)(2,1)S(1)}, u32[]{:S(2)}, u32[]{:S(2)}) collective-permute-start(bf16[1,128,512]{2,1,0:T(8,128)(2,1)S(1)} %collective-permute-done.30), channel_id=1, source_target_pairs={{0,2},{2,0},{4,6},{6,4},{8,10},{10,8},{12,14},{14,12},{16,18},{18,... | collective-permute-start | bytes 393224 | tf_op jit(solution)/shard_map/ppermute | solution.py:242
  66.9 5.9 %collective-permute-start.32 = (bf16[1,128,512]{2,1,0:T(8,128)(2,1)S(1)}, bf16[1,128,512]{2,1,0:T(8,128)(2,1)S(1)}, u32[]{:S(2)}, u32[]{:S(2)}) collective-permute-start(bf16[1,128,512]{2,1,0:T(8,128)(2,1)S(1)} %collective-permute-done.30), channel_id=1, source_target_pairs={{0,8},{2,6},{8,16},{10,2},{16,24},{18,10},{24,28},{26,18},{28,20},... | collective-permute-start | bytes 393224 | tf_op jit(solution)/shard_map/ppermute | solution.py:312
  68.3 14.6 %collective-permute-start.23 = (bf16[1,128,512]{2,1,0:T(8,128)(2,1)S(1)}, bf16[1,128,512]{2,1,0:T(8,128)(2,1)S(1)}, u32[]{:S(2)}, u32[]{:S(2)}) collective-permute-start(bf16[1,128,512]{2,1,0:T(8,128)(2,1)S(1)} %collective-permute-done.22), channel_id=1, source_target_pairs={{0,2},{2,0},{4,6},{6,4},{8,10},{10,8},{12,14},{14,12},{16,18},{18,... | collective-permute-start | bytes 393224 | tf_op jit(solution)/shard_map/ppermute | solution.py:242
  68.3 1.7 %collective-permute-start.17 = (bf16[2,128,512]{2,1,0:T(8,128)(2,1)S(1)}, bf16[2,128,512]{2,1,0:T(8,128)(2,1)S(1)}, u32[]{:S(2)}, u32[]{:S(2)}) collective-permute-start(bf16[2,128,512]{2,1,0:T(8,128)(2,1)S(1)} %collective-permute-done.16), channel_id=1, source_target_pairs={{0,2},{2,0},{4,6},{6,4},{8,10},{10,8},{12,14},{14,12},{16,18},{18,... | collective-permute-start | bytes 786440 | tf_op jit(solution)/shard_map/ppermute | solution.py:242
  70.0 6.4 %collective-permute-start.20 = (bf16[2,128,512]{2,1,0:T(8,128)(2,1)S(1)}, bf16[2,128,512]{2,1,0:T(8,128)(2,1)S(1)}, u32[]{:S(2)}, u32[]{:S(2)}) collective-permute-start(bf16[2,128,512]{2,1,0:T(8,128)(2,1)S(1)} %collective-permute-done.16), channel_id=1, source_target_pairs={{0,8},{2,6},{8,16},{10,2},{16,24},{18,10},{24,28},{26,18},{28,20},... | collective-permute-start | bytes 786440 | tf_op jit(solution)/shard_map/ppermute | solution.py:312
  71.4 6.5 %collective-permute-start.26 = (bf16[1,128,512]{2,1,0:T(8,128)(2,1)S(1)}, bf16[1,128,512]{2,1,0:T(8,128)(2,1)S(1)}, u32[]{:S(2)}, u32[]{:S(2)}) collective-permute-start(bf16[1,128,512]{2,1,0:T(8,128)(2,1)S(1)} %collective-permute-done.22), channel_id=1, source_target_pairs={{0,8},{2,6},{8,16},{10,2},{16,24},{18,10},{24,28},{26,18},{28,20},... | collective-permute-start | bytes 393224 | tf_op jit(solution)/shard_map/ppermute | solution.py:312
  72.7 6.4 %collective-permute-start.34 = (bf16[1,128,512]{2,1,0:T(8,128)(2,1)S(1)}, bf16[1,128,512]{2,1,0:T(8,128)(2,1)S(1)}, u32[]{:S(2)}, u32[]{:S(2)}) collective-permute-start(bf16[1,128,512]{2,1,0:T(8,128)(2,1)S(1)} %collective-permute-done.32), channel_id=1, source_target_pairs={{0,8},{2,6},{8,16},{10,2},{16,24},{18,10},{24,28},{26,18},{28,20},... | collective-permute-start | bytes 393224 | tf_op jit(solution)/shard_map/ppermute | solution.py:312
  76.4 2.8 %collective-permute-start.21 = (bf16[2,128,512]{2,1,0:T(8,128)(2,1)S(1)}, bf16[2,128,512]{2,1,0:T(8,128)(2,1)S(1)}, u32[]{:S(2)}, u32[]{:S(2)}) collective-permute-start(bf16[2,128,512]{2,1,0:T(8,128)(2,1)S(1)} %collective-permute-done.20), channel_id=1, source_target_pairs={{0,2},{2,0},{4,6},{6,4},{8,10},{10,8},{12,14},{14,12},{16,18},{18,... | collective-permute-start | bytes 786440 | tf_op jit(solution)/shard_map/ppermute | solution.py:242
  76.4 6.4 %collective-permute-start.24 = (bf16[2,128,512]{2,1,0:T(8,128)(2,1)S(1)}, bf16[2,128,512]{2,1,0:T(8,128)(2,1)S(1)}, u32[]{:S(2)}, u32[]{:S(2)}) collective-permute-start(bf16[2,128,512]{2,1,0:T(8,128)(2,1)S(1)} %collective-permute-done.20), channel_id=1, source_target_pairs={{0,8},{2,6},{8,16},{10,2},{16,24},{18,10},{24,28},{26,18},{28,20},... | collective-permute-start | bytes 786440 | tf_op jit(solution)/shard_map/ppermute | solution.py:312
  77.9 5.1 %collective-permute-start.33 = (bf16[1,128,512]{2,1,0:T(8,128)(2,1)S(1)}, bf16[1,128,512]{2,1,0:T(8,128)(2,1)S(1)}, u32[]{:S(2)}, u32[]{:S(2)}) collective-permute-start(bf16[1,128,512]{2,1,0:T(8,128)(2,1)S(1)} %collective-permute-done.32), channel_id=1, source_target_pairs={{0,2},{2,0},{4,6},{6,4},{8,10},{10,8},{12,14},{14,12},{16,18},{18,... | collective-permute-start | bytes 393224 | tf_op jit(solution)/shard_map/ppermute | solution.py:242
  79.2 5.3 %collective-permute-start.27 = (bf16[1,128,512]{2,1,0:T(8,128)(2,1)S(1)}, bf16[1,128,512]{2,1,0:T(8,128)(2,1)S(1)}, u32[]{:S(2)}, u32[]{:S(2)}) collective-permute-start(bf16[1,128,512]{2,1,0:T(8,128)(2,1)S(1)} %collective-permute-done.26), channel_id=1, source_target_pairs={{0,2},{2,0},{4,6},{6,4},{8,10},{10,8},{12,14},{14,12},{16,18},{18,... | collective-permute-start | bytes 393224 | tf_op jit(solution)/shard_map/ppermute | solution.py:242
  79.2 5.3 %collective-permute-start.35 = (bf16[1,128,512]{2,1,0:T(8,128)(2,1)S(1)}, bf16[1,128,512]{2,1,0:T(8,128)(2,1)S(1)}, u32[]{:S(2)}, u32[]{:S(2)}) collective-permute-start(bf16[1,128,512]{2,1,0:T(8,128)(2,1)S(1)} %collective-permute-done.34), channel_id=1, source_target_pairs={{0,2},{2,0},{4,6},{6,4},{8,10},{10,8},{12,14},{14,12},{16,18},{18,... | collective-permute-start | bytes 393224 | tf_op jit(solution)/shard_map/ppermute | solution.py:242
  82.8 1.5 %collective-permute-start.25 = (bf16[2,128,512]{2,1,0:T(8,128)(2,1)S(1)}, bf16[2,128,512]{2,1,0:T(8,128)(2,1)S(1)}, u32[]{:S(2)}, u32[]{:S(2)}) collective-permute-start(bf16[2,128,512]{2,1,0:T(8,128)(2,1)S(1)} %collective-permute-done.24), channel_id=1, source_target_pairs={{0,2},{2,0},{4,6},{6,4},{8,10},{10,8},{12,14},{14,12},{16,18},{18,... | collective-permute-start | bytes 786440 | tf_op jit(solution)/shard_map/ppermute | solution.py:242

commit v9 on v7

--- a/solution.py
+++ b/solution.py
@@ -272,13 +272,25 @@
         ]
         return lax.ppermute(array, "dp", pairs)
 
-    outputs = jnp.dot(inputs, weight, preferred_element_type=jnp.float32).astype(jnp.bfloat16)
-    far_cot, outputs = lax.optimization_barrier((exchange(cotangent, 4), outputs))
+    def project(columns):
+        out = jnp.dot(inputs, weight[:, columns], preferred_element_type=jnp.float32)
+        return out.astype(jnp.bfloat16)
+
+    head_columns = weight.shape[1] // 4
+    far_cot, head_outputs = lax.optimization_barrier(
+        (exchange(cotangent, 4), project(slice(0, head_columns)))
+    )
     near = [deal(packed[hop], hop) for hop in hops]
     shared = exchange(packed[-1], SHARED)
     pair = jnp.concatenate([cotangent, far_cot])
     cots = [pair] + [exchange(pair, offset) for offset in (1, 2, 3)]
     far = [swap_plane(piece) for piece in near]
+    rows = BLOCK // members // cores
+    columns = [jnp.zeros((bands, cores, rows, BLOCK), jnp.bfloat16) for _ in range(2)]
+    own_band, tail_outputs, *columns = lax.optimization_barrier(
+        (own_band, project(slice(head_columns, None)), *columns)
+    )
+    outputs = jnp.concatenate([head_outputs, tail_outputs], axis=1)
     (partial_tile,) = call(
         tile_kernel,
         [jax.ShapeDtypeStruct((BLOCK, BLOCK), jnp.float32)],
@@ -292,7 +304,6 @@
     )
     other_partial = swap_core(partial_tile)
     side = jnp.stack([core, plane]).astype(jnp.int32)
-    rows = BLOCK // members // cores
     near_piece, next_piece, far_piece = call(
         update_kernel,
         [jax.ShapeDtypeStruct((rows, BLOCK), jnp.bfloat16)] * 3,
@@ -313,7 +324,6 @@
     half_way = bands // 2
     crossed = swap_plane(far_piece)
     heads = [near_piece, next_piece, crossed, swap_core(crossed)]
-    columns = [jnp.zeros((bands, cores, rows, BLOCK), jnp.bfloat16)] * 2
 
     def put(chunk, piece, position, half):
         columns[chunk] = lax.dynamic_update_slice(

time: 79.4 us -> 92.6 us (1.17)
  local copies, waits for them, and re-layouts: 2.23 us -> 13.7 us
    dynamic_update_slice x31, local copies, waits for them, and re-layouts: 0.51 us -> 9.53 us  [put(): lax.dynamic_update_slice(columns[chunk], piece[None, None], (ring_band(po...]
    ppermute x4, waiting for transfers between devices: 6.21 us -> 2.22 us  [swap_plane(): lax.ppermute(array, 'pre', [(c, members - 1 - c) for c in range(members)])]
    ppermute x5, waiting for transfers between devices: 1.36 us -> 5.07 us  [exchange(): return lax.ppermute(array, 'dp', pairs)]
    unnamed x5 -> x12, local copies, waits for them, and re-layouts: 1.24 us -> 3.89 us
    ppermute x3, starting transfers between devices: 3.88 us -> 6.41 us  [deal(): return lax.ppermute(array, ('dp', 'pre'), pairs)]
    ppermute x16, waiting for transfers between devices: 3.65 us -> 1.21 us  [swap_core(): return lax.ppermute(array, 'dp', [(g, g ^ 1) for g in range(groups)])]
    ppermute x5, starting transfers between devices: 9.35 us -> 7.1 us  [exchange(): return lax.ppermute(array, 'dp', pairs)]
    ppermute x14, waiting for transfers between devices: 4.28 us -> 6.2 us  [turn(): return lax.ppermute(array, 'dp', pairs)]
  transfers between devices with their start and end apart: 42 -> 42, of which waited for: 15 -> 10; matrix products, arithmetic and copies ran while one was open for 6% -> 17% of each run, Pallas kernels for 1% -> 0%
where the time goes in v9:
time: 92.6 us; the launch traced here: 92.4 us
  starting transfers between devices  42.1 us (45%)
  waiting for transfers between devices  18.1 us (20%)
  local copies, waits for them, and re-layouts  13.7 us (15%)
  Pallas kernels  9.42 us (10%)
  matrix products  4.25 us (5%)
  other arithmetic  3.52 us (4%)
  between operations  1.2 us (1%)
    ppermute x14, starting transfers between devices, turn(): return lax.ppermute(array, 'dp', pairs)  19.3 us
    dynamic_update_slice x31, local copies, waits for them, and re-layouts, put(): lax.dynamic_update_slice(columns[chunk], piece[None, None], (ring_band(po...  9.53 us
    pallas_call x3, Pallas kernels, call(): pl.pallas_call(kernel, out_shape=out_shapes, in_specs=in_specs, out_specs...  9.42 us
    ppermute x4, starting transfers between devices, swap_plane(): lax.ppermute(array, 'pre', [(c, members - 1 - c) for c in range(members)])  8.72 us
    ppermute x5, starting transfers between devices, exchange(): return lax.ppermute(array, 'dp', pairs)  7.1 us
    ppermute x3, starting transfers between devices, deal(): return lax.ppermute(array, ('dp', 'pre'), pairs)  6.41 us
    ppermute x14, waiting for transfers between devices, turn(): return lax.ppermute(array, 'dp', pairs)  6.2 us
    ppermute x5, waiting for transfers between devices, exchange(): return lax.ppermute(array, 'dp', pairs)  5.07 us
  transfers between devices with their start and end apart: 42, of which 10 were waited for; matrix products, arithmetic and copies ran while one was open for 17% of the time, Pallas kernels for 0%

profile of v9, /device:TPU:0, one launch (start us, length us, event | category | flops | bytes accessed | tf_op | source)
XLA Modules:
  0.0 92.4 jit_solution(5620023333120235359)
XLA Ops:
  0.7 1.2 %copy-done = bf16[128,4096]{1,0:T(8,128)(2,1)S(1)} copy-done((bf16[128,4096]{1,0:T(8,128)(2,1)S(1)}, bf16[128,4096]{1,0:T(8,128)(2,1)}, u32[]{:S(2)}) %copy-start) | copy-done | bytes 1048600
  2.6 4.1 %collective-permute-start.2 = (bf16[128,512]{1,0:T(8,128)(2,1)S(1)}, bf16[128,512]{1,0:T(8,128)(2,1)S(1)}, u32[]{:S(2)}, u32[]{:S(2)}) collective-permute-start(bf16[128,512]{1,0:T(8,128)(2,1)S(1)} %get-tuple-element.22), channel_id=1, source_target_pairs={{0,16},{1,21},{2,18},{3,23},{4,20},{5,17},{6,22},{7,19},{8,24},{9,... | collective-permute-start | bytes 393224 | tf_op jit(solution)/shard_map/ppermute | solution.py:257
  6.7 2.3 %collective-permute-start.3 = (bf16[128,512]{1,0:T(8,128)(2,1)S(1)}, bf16[128,512]{1,0:T(8,128)(2,1)S(1)}, u32[]{:S(2)}, u32[]{:S(2)}) collective-permute-start(bf16[128,512]{1,0:T(8,128)(2,1)S(1)} %get-tuple-element.23), channel_id=1, source_target_pairs={{0,28},{1,25},{2,30},{3,27},{4,24},{5,29},{6,26},{7,31},{8,20},{9,... | collective-permute-start | bytes 393224 | tf_op jit(solution)/shard_map/ppermute | solution.py:257
  9.0 0.8 collective-permute-start.1
  9.8 2.8 %collective-permute-start = (bf16[128,512]{1,0:T(8,128)(2,1)}, bf16[128,512]{1,0:T(8,128)(2,1)S(1)}, u32[]{:S(2)}, u32[]{:S(2)}) collective-permute-start(bf16[128,512]{1,0:T(8,128)(2,1)} %param.5), channel_id=1, source_target_pairs={{0,16},{2,18},{4,20},{6,22},{8,24},{10,26},{12,28},{14,30},{16,0},... | collective-permute-start | bytes 393224 | tf_op jit(solution)/shard_map/ppermute | solution.py:273
  12.5 1.6 %convolution_convert_fusion = bf16[128,128]{1,0:T(8,128)(2,1)S(1)} fusion(bf16[128,4096]{1,0:T(8,128)(2,1)S(1)} %copy-done, bf16[4096,512]{1,0:T(8,128)(2,1)} %param.4), kind=kOutput, calls=%fused_computation.4 | convolution fusion | flops 134234112 | bytes 2129920 | tf_op jit(solution)/shard_map/dot_general | solution.py:276
  14.2 3.4 %collective-permute-done.2.refs_0_ = bf16[128,512]{1,0:T(8,128)(2,1)S(1)} collective-permute-done((bf16[128,512]{1,0:T(8,128)(2,1)S(1)}, bf16[128,512]{1,0:T(8,128)(2,1)S(1)}, u32[]{:S(2)}, u32[]{:S(2)}) %collective-permute-start.2) | collective-permute-done | bytes 131104 | tf_op jit(solution)/shard_map/ppermute | solution.py:257
  17.6 4.6 %collective-permute-start.5 = (bf16[128,512]{1,0:T(8,128)(2,1)S(1)}, bf16[128,512]{1,0:T(8,128)(2,1)S(1)}, u32[]{:S(2)}, u32[]{:S(2)}) collective-permute-start(bf16[128,512]{1,0:T(8,128)(2,1)S(1)} %collective-permute-done.2.refs_0_), channel_id=1, source_target_pairs={{0,1},{1,0},{2,3},{3,2},{4,5},{5,4},{6,7},{7,6},{8,9},{9,8},{10,11... | collective-permute-start | bytes 393224 | tf_op jit(solution)/shard_map/ppermute | solution.py:245
  22.2 2.0 %collective-permute-done = bf16[128,512]{1,0:T(8,128)(2,1)S(1)} collective-permute-done((bf16[128,512]{1,0:T(8,128)(2,1)}, bf16[128,512]{1,0:T(8,128)(2,1)S(1)}, u32[]{:S(2)}, u32[]{:S(2)}) %collective-permute-start) | collective-permute-done | bytes 131104 | tf_op jit(solution)/shard_map/ppermute | solution.py:273
  24.3 1.8 %collective-permute-start.10 = (bf16[256,512]{1,0:T(8,128)(2,1)S(1)}, bf16[256,512]{1,0:T(8,128)(2,1)S(1)}, u32[]{:S(2)}, u32[]{:S(2)}) collective-permute-start(bf16[256,512]{1,0:T(8,128)(2,1)S(1)} %constant_dynamic-update-slice_fusion.refs_6_), channel_id=1, source_target_pairs={{0,12},{2,14},{4,8},{6,10},{8,4},{10,6},{12,0},{14,2},{16,28},{18,... | collective-permute-start | bytes 786440 | tf_op jit(solution)/shard_map/ppermute | solution.py:273
  26.6 1.2 %collective-permute-start.9 = (bf16[256,512]{1,0:T(8,128)(2,1)S(1)}, bf16[256,512]{1,0:T(8,128)(2,1)S(1)}, u32[]{:S(2)}, u32[]{:S(2)}) collective-permute-start(bf16[256,512]{1,0:T(8,128)(2,1)S(1)} %constant_dynamic-update-slice_fusion.refs_6_), channel_id=1, source_target_pairs={{0,8},{2,10},{4,12},{6,14},{8,0},{10,2},{12,4},{14,6},{16,24},{18,... | collective-permute-start | bytes 786440 | tf_op jit(solution)/shard_map/ppermute | solution.py:273
  27.8 2.5 %collective-permute-start.6 = (bf16[128,512]{1,0:T(8,128)(2,1)S(1)}, bf16[128,512]{1,0:T(8,128)(2,1)S(1)}, u32[]{:S(2)}, u32[]{:S(2)}) collective-permute-start(bf16[128,512]{1,0:T(8,128)(2,1)S(1)} %collective-permute-done.3.refs_1_), channel_id=1, source_target_pairs={{0,1},{1,0},{2,3},{3,2},{4,5},{5,4},{6,7},{7,6},{8,9},{9,8},{10,11... | collective-permute-start | bytes 393224 | tf_op jit(solution)/shard_map/ppermute | solution.py:245
  30.4 2.6 %fusion.2 = bf16[128,384]{1,0:T(8,128)(2,1)S(1)} fusion(bf16[128,4096]{1,0:T(8,128)(2,1)S(1)} %copy-done, bf16[4096,512]{1,0:T(8,128)(2,1)} %param.4), kind=kOutput, calls=%fused_computation.3 | convolution fusion | flops 402702336 | bytes 4292608 | tf_op jit(solution)/shard_map/dot_general | solution.py:276
  33.7 1.6 %collective-permute-done.7.refs_5_ = bf16[128,512]{1,0:T(8,128)(2,1)S(1)} collective-permute-done((bf16[128,512]{1,0:T(8,128)(2,1)S(1)}, bf16[128,512]{1,0:T(8,128)(2,1)S(1)}, u32[]{:S(2)}, u32[]{:S(2)}) %collective-permute-start.7) | collective-permute-done | bytes 131104 | tf_op jit(solution)/shard_map/ppermute | solution.py:245
  35.3 3.0 %collective-permute-done.8.refs_7_ = bf16[256,512]{1,0:T(8,128)(2,1)S(1)} collective-permute-done((bf16[256,512]{1,0:T(8,128)(2,1)S(1)}, bf16[256,512]{1,0:T(8,128)(2,1)S(1)}, u32[]{:S(2)}, u32[]{:S(2)}) %collective-permute-start.8) | collective-permute-done | bytes 262176 | tf_op jit(solution)/shard_map/ppermute | solution.py:273
  38.3 1.4 %shard_map.51.mine_ref = f32[512,512]{1,0:T(8,128)S(1)} custom-call(s32[2]{0:T(128)S(1)} %pad_add_fusion.1.place_ref, bf16[128,512]{1,0:T(8,128)(2,1)S(1)} %get-tuple-element.20.own_ref, bf16[128,512]{1,0:T(8,128)(2,1)S(1)} %collective-permute-done.1.shared_ref, bf16[128,512]{1,0:T(8,128)(2,1)S(1)} %collective-permute-done.2.refs_0_, ...), custom_call_target="tpu_custom_call" | custom-call | tf_op jit(solution)/shard_map/pallas_call | solution.py:217
  40.3 1.3 %copy-done.1 = bf16[8,2,128,512]{3,2,1,0:T(8,128)(2,1)} copy-done((bf16[8,2,128,512]{3,2,1,0:T(8,128)(2,1)}, bf16[8,2,128,512]{3,2,1,0:T(8,128)(2,1)S(1)}, u32[]{:S(2)}) %copy-start.1) | copy-done | bytes 2097176
  41.6 1.3 %copy.20 = bf16[8,2,128,512]{3,2,1,0:T(8,128)(2,1)} copy(bf16[8,2,128,512]{3,2,1,0:T(8,128)(2,1)S(1)} %broadcast.16) | data formatting | bytes 4194304
  43.0 0.7 pad_maximum_fusion
  43.7 7.4 %shard_map.52 = (bf16[128,512]{1,0:T(8,128)(2,1)S(1)}, bf16[128,512]{1,0:T(8,128)(2,1)S(1)}, bf16[128,512]{1,0:T(8,128)(2,1)S(1)}) custom-call(s32[2]{0:T(128)S(1)} %pad_add_fusion.side_ref, f32[512,512]{1,0:T(8,128)S(1)} %shard_map.51.mine_ref, f32[512,512]{1,0:T(8,128)S(1)} %collective-permute-done.11.other_ref), custom_call_target="tpu_custom_call" | custom-call | tf_op jit(solution)/shard_map/pallas_call | solution.py:217
  51.2 1.7 %collective-permute-start.12 = (bf16[128,512]{1,0:T(8,128)(2,1)S(1)}, bf16[128,512]{1,0:T(8,128)(2,1)S(1)}, u32[]{:S(2)}, u32[]{:S(2)}) collective-permute-start(bf16[128,512]{1,0:T(8,128)(2,1)S(1)} %get-tuple-element.26), channel_id=1, source_target_pairs={{0,8},{2,6},{8,16},{10,2},{16,24},{18,10},{24,28},{26,18},{28,20},... | collective-permute-start | bytes 393224 | tf_op jit(solution)/shard_map/ppermute | solution.py:322
  52.9 2.1 %collective-permute-start.14 = (bf16[128,512]{1,0:T(8,128)(2,1)S(1)}, bf16[128,512]{1,0:T(8,128)(2,1)S(1)}, u32[]{:S(2)}, u32[]{:S(2)}) collective-permute-start(bf16[128,512]{1,0:T(8,128)(2,1)S(1)} %get-tuple-element.27), channel_id=1, source_target_pairs={{0,8},{2,6},{8,16},{10,2},{16,24},{18,10},{24,28},{26,18},{28,20},... | collective-permute-start | bytes 393224 | tf_op jit(solution)/shard_map/ppermute | solution.py:322
  54.9 1.5 %collective-permute-start.26 = (bf16[128,512]{1,0:T(8,128)(2,1)S(1)}, bf16[128,512]{1,0:T(8,128)(2,1)S(1)}, u32[]{:S(2)}, u32[]{:S(2)}) collective-permute-start(bf16[128,512]{1,0:T(8,128)(2,1)S(1)} %get-tuple-element.29), channel_id=1, source_target_pairs={{0,1},{1,0},{2,3},{3,2},{4,5},{5,4},{6,7},{7,6},{8,9},{9,8},{10,11... | collective-permute-start | bytes 393224 | tf_op jit(solution)/shard_map/ppermute | solution.py:245
  57.1 0.7 bitcast_dynamic-update-slice_fusion.30
  57.8 1.8 %collective-permute-start.16 = (bf16[128,512]{1,0:T(8,128)(2,1)S(1)}, bf16[128,512]{1,0:T(8,128)(2,1)S(1)}, u32[]{:S(2)}, u32[]{:S(2)}) collective-permute-start(bf16[128,512]{1,0:T(8,128)(2,1)S(1)} %collective-permute-done.12), channel_id=1, source_target_pairs={{0,8},{2,6},{8,16},{10,2},{16,24},{18,10},{24,28},{26,18},{28,20},... | collective-permute-start | bytes 393224 | tf_op jit(solution)/shard_map/ppermute | solution.py:322
  59.6 1.4 %collective-permute-start.18 = (bf16[128,512]{1,0:T(8,128)(2,1)S(1)}, bf16[128,512]{1,0:T(8,128)(2,1)S(1)}, u32[]{:S(2)}, u32[]{:S(2)}) collective-permute-start(bf16[128,512]{1,0:T(8,128)(2,1)S(1)} %collective-permute-done.14), channel_id=1, source_target_pairs={{0,8},{2,6},{8,16},{10,2},{16,24},{18,10},{24,28},{26,18},{28,20},... | collective-permute-start | bytes 393224 | tf_op jit(solution)/shard_map/ppermute | solution.py:322
  61.0 0.9 collective-permute-start.28
  61.9 0.8 collective-permute-done.16
  64.1 1.8 %collective-permute-start.20 = (bf16[128,512]{1,0:T(8,128)(2,1)S(1)}, bf16[128,512]{1,0:T(8,128)(2,1)S(1)}, u32[]{:S(2)}, u32[]{:S(2)}) collective-permute-start(bf16[128,512]{1,0:T(8,128)(2,1)S(1)} %collective-permute-done.16), channel_id=1, source_target_pairs={{0,8},{2,6},{8,16},{10,2},{16,24},{18,10},{24,28},{26,18},{28,20},... | collective-permute-start | bytes 393224 | tf_op jit(solution)/shard_map/ppermute | solution.py:322
  65.9 0.7 bitcast_dynamic-update-slice_fusion.27
  66.5 0.7 bitcast_dynamic-update-slice_fusion.26
  67.2 1.4 %collective-permute-start.22 = (bf16[128,512]{1,0:T(8,128)(2,1)S(1)}, bf16[128,512]{1,0:T(8,128)(2,1)S(1)}, u32[]{:S(2)}, u32[]{:S(2)}) collective-permute-start(bf16[128,512]{1,0:T(8,128)(2,1)S(1)} %collective-permute-done.18), channel_id=1, source_target_pairs={{0,8},{2,6},{8,16},{10,2},{16,24},{18,10},{24,28},{26,18},{28,20},... | collective-permute-start | bytes 393224 | tf_op jit(solution)/shard_map/ppermute | solution.py:322
  68.6 0.9 collective-permute-start.30
  70.8 1.4 %collective-permute-start.32 = (bf16[128,512]{1,0:T(8,128)(2,1)S(1)}, bf16[128,512]{1,0:T(8,128)(2,1)S(1)}, u32[]{:S(2)}, u32[]{:S(2)}) collective-permute-start(bf16[128,512]{1,0:T(8,128)(2,1)S(1)} %collective-permute-done.28), channel_id=1, source_target_pairs={{0,8},{2,6},{8,16},{10,2},{16,24},{18,10},{24,28},{26,18},{28,20},... | collective-permute-start | bytes 393224 | tf_op jit(solution)/shard_map/ppermute | solution.py:322
  72.3 1.4 %collective-permute-done.30 = bf16[128,512]{1,0:T(8,128)(2,1)S(1)} collective-permute-done((bf16[128,512]{1,0:T(8,128)(2,1)S(1)}, bf16[128,512]{1,0:T(8,128)(2,1)S(1)}, u32[]{:S(2)}, u32[]{:S(2)}) %collective-permute-start.30) | collective-permute-done | bytes 131104 | tf_op jit(solution)/shard_map/ppermute | solution.py:322
  74.3 0.7 bitcast_dynamic-update-slice_fusion.22
  75.0 1.3 %collective-permute-start.34 = (bf16[128,512]{1,0:T(8,128)(2,1)S(1)}, bf16[128,512]{1,0:T(8,128)(2,1)S(1)}, u32[]{:S(2)}, u32[]{:S(2)}) collective-permute-start(bf16[128,512]{1,0:T(8,128)(2,1)S(1)} %collective-permute-done.30), channel_id=1, source_target_pairs={{0,8},{2,6},{8,16},{10,2},{16,24},{18,10},{24,28},{26,18},{28,20},... | collective-permute-start | bytes 393224 | tf_op jit(solution)/shard_map/ppermute | solution.py:322
  76.9 0.9 %collective-permute-start.36 = (bf16[128,512]{1,0:T(8,128)(2,1)S(1)}, bf16[128,512]{1,0:T(8,128)(2,1)S(1)}, u32[]{:S(2)}, u32[]{:S(2)}) collective-permute-start(bf16[128,512]{1,0:T(8,128)(2,1)S(1)} %collective-permute-done.32), channel_id=1, source_target_pairs={{0,8},{2,6},{8,16},{10,2},{16,24},{18,10},{24,28},{26,18},{28,20},... | collective-permute-start | bytes 393224 | tf_op jit(solution)/shard_map/ppermute | solution.py:322
  77.8 0.7 bitcast_dynamic-update-slice_fusion.21
  78.5 0.7 bitcast_dynamic-update-slice_fusion.20
  79.2 1.3 %collective-permute-start.24 = (bf16[128,512]{1,0:T(8,128)(2,1)S(1)}, bf16[128,512]{1,0:T(8,128)(2,1)S(1)}, u32[]{:S(2)}, u32[]{:S(2)}) collective-permute-start(bf16[128,512]{1,0:T(8,128)(2,1)S(1)} %collective-permute-done.20), channel_id=1, source_target_pairs={{0,8},{2,6},{8,16},{10,2},{16,24},{18,10},{24,28},{26,18},{28,20},... | collective-permute-start | bytes 393224 | tf_op jit(solution)/shard_map/ppermute | solution.py:322
  81.2 0.7 bitcast_dynamic-update-slice_fusion.18
  81.9 0.9 collective-permute-start.38
  82.8 1.4 %collective-permute-start.40 = (bf16[128,512]{1,0:T(8,128)(2,1)S(1)}, bf16[128,512]{1,0:T(8,128)(2,1)S(1)}, u32[]{:S(2)}, u32[]{:S(2)}) collective-permute-start(bf16[128,512]{1,0:T(8,128)(2,1)S(1)} %collective-permute-done.36), channel_id=1, source_target_pairs={{0,8},{2,6},{8,16},{10,2},{16,24},{18,10},{24,28},{26,18},{28,20},... | collective-permute-start | bytes 393224 | tf_op jit(solution)/shard_map/ppermute | solution.py:322
  84.3 2.6 %collective-permute-done.38 = bf16[128,512]{1,0:T(8,128)(2,1)S(1)} collective-permute-done((bf16[128,512]{1,0:T(8,128)(2,1)S(1)}, bf16[128,512]{1,0:T(8,128)(2,1)S(1)}, u32[]{:S(2)}, u32[]{:S(2)}) %collective-permute-start.38) | collective-permute-done | bytes 131104 | tf_op jit(solution)/shard_map/ppermute | solution.py:322
  86.8 1.4 %collective-permute-done.40 = bf16[128,512]{1,0:T(8,128)(2,1)S(1)} collective-permute-done((bf16[128,512]{1,0:T(8,128)(2,1)S(1)}, bf16[128,512]{1,0:T(8,128)(2,1)S(1)}, u32[]{:S(2)}, u32[]{:S(2)}) %collective-permute-start.40) | collective-permute-done | bytes 131104 | tf_op jit(solution)/shard_map/ppermute | solution.py:322
  88.4 1.2 %collective-permute-done.41 = bf16[128,512]{1,0:T(8,128)(2,1)S(1)} collective-permute-done((bf16[128,512]{1,0:T(8,128)(2,1)S(1)}, bf16[128,512]{1,0:T(8,128)(2,1)S(1)}, u32[]{:S(2)}, u32[]{:S(2)}) %collective-permute-start.41) | collective-permute-done | bytes 131104 | tf_op jit(solution)/shard_map/ppermute | solution.py:242
  89.7 2.7 %maximum_select_fusion = bf16[8,256,1024]{2,1,0:T(8,128)(2,1)} fusion(bf16[8,256,512]{2,1,0:T(8,128)(2,1)S(1)} %bitcast.75, bf16[8,256,512]{2,1,0:T(8,128)(2,1)S(1)} %bitcast.76, pred[]{:T(512)S(6)} %eq.44), kind=kLoop, calls=%fused_computation | loop fusion | flops 18874368 | bytes 8388609 | tf_op jit(solution)/shard_map/jit(_where)/select_n | solution.py:343
  (91 shorter events, 7.9 us)
Async XLA Ops:
  0.7 1.2 %copy-start = (bf16[128,4096]{1,0:T(8,128)(2,1)S(1)}, bf16[128,4096]{1,0:T(8,128)(2,1)}, u32[]{:S(2)}) copy-start(bf16[128,4096]{1,0:T(8,128)(2,1)} %inputs_ref.1) | copy-start | bytes 3145732
  2.0 20.2 %copy-start.4 = (bf16[128,512]{1,0:T(8,128)(2,1)S(1)}, bf16[128,512]{1,0:T(8,128)(2,1)}, u32[]{:S(2)}) copy-start(bf16[128,512]{1,0:T(8,128)(2,1)} %param.5) | copy-start | bytes 393220
  2.6 15.0 %collective-permute-start.2 = (bf16[128,512]{1,0:T(8,128)(2,1)S(1)}, bf16[128,512]{1,0:T(8,128)(2,1)S(1)}, u32[]{:S(2)}, u32[]{:S(2)}) collective-permute-start(bf16[128,512]{1,0:T(8,128)(2,1)S(1)} %get-tuple-element.22), channel_id=1, source_target_pairs={{0,16},{1,21},{2,18},{3,23},{4,20},{5,17},{6,22},{7,19},{8,24},{9,... | collective-permute-start | bytes 393224 | tf_op jit(solution)/shard_map/ppermute | solution.py:257
  6.7 19.4 %collective-permute-start.3 = (bf16[128,512]{1,0:T(8,128)(2,1)S(1)}, bf16[128,512]{1,0:T(8,128)(2,1)S(1)}, u32[]{:S(2)}, u32[]{:S(2)}) collective-permute-start(bf16[128,512]{1,0:T(8,128)(2,1)S(1)} %get-tuple-element.23), channel_id=1, source_target_pairs={{0,28},{1,25},{2,30},{3,27},{4,24},{5,29},{6,26},{7,31},{8,20},{9,... | collective-permute-start | bytes 393224 | tf_op jit(solution)/shard_map/ppermute | solution.py:257
  9.0 17.7 %collective-permute-start.4 = (bf16[128,512]{1,0:T(8,128)(2,1)S(1)}, bf16[128,512]{1,0:T(8,128)(2,1)S(1)}, u32[]{:S(2)}, u32[]{:S(2)}) collective-permute-start(bf16[128,512]{1,0:T(8,128)(2,1)S(1)} %get-tuple-element.24), channel_id=1, source_target_pairs={{0,8},{1,13},{2,10},{3,15},{4,12},{5,9},{6,14},{7,11},{8,0},{9,5},... | collective-permute-start | bytes 393224 | tf_op jit(solution)/shard_map/ppermute | solution.py:257
  9.0 18.9 %collective-permute-start.1 = (bf16[128,512]{1,0:T(8,128)(2,1)S(1)}, bf16[128,512]{1,0:T(8,128)(2,1)S(1)}, u32[]{:S(2)}, u32[]{:S(2)}) collective-permute-start(bf16[128,512]{1,0:T(8,128)(2,1)S(1)} %get-tuple-element.21), channel_id=1, source_target_pairs={{0,4},{2,6},{4,0},{6,2},{8,12},{10,14},{12,8},{14,10},{16,20},{18,... | collective-permute-start | bytes 393224 | tf_op jit(solution)/shard_map/ppermute | solution.py:273
  9.8 14.5 %collective-permute-start = (bf16[128,512]{1,0:T(8,128)(2,1)}, bf16[128,512]{1,0:T(8,128)(2,1)S(1)}, u32[]{:S(2)}, u32[]{:S(2)}) collective-permute-start(bf16[128,512]{1,0:T(8,128)(2,1)} %param.5), channel_id=1, source_target_pairs={{0,16},{2,18},{4,20},{6,22},{8,24},{10,26},{12,28},{14,30},{16,0},... | collective-permute-start | bytes 393224 | tf_op jit(solution)/shard_map/ppermute | solution.py:273
  17.6 12.7 %collective-permute-start.5 = (bf16[128,512]{1,0:T(8,128)(2,1)S(1)}, bf16[128,512]{1,0:T(8,128)(2,1)S(1)}, u32[]{:S(2)}, u32[]{:S(2)}) collective-permute-start(bf16[128,512]{1,0:T(8,128)(2,1)S(1)} %collective-permute-done.2.refs_0_), channel_id=1, source_target_pairs={{0,1},{1,0},{2,3},{3,2},{4,5},{5,4},{6,7},{7,6},{8,9},{9,8},{10,11... | collective-permute-start | bytes 393224 | tf_op jit(solution)/shard_map/ppermute | solution.py:245
  24.3 11.0 %collective-permute-start.10 = (bf16[256,512]{1,0:T(8,128)(2,1)S(1)}, bf16[256,512]{1,0:T(8,128)(2,1)S(1)}, u32[]{:S(2)}, u32[]{:S(2)}) collective-permute-start(bf16[256,512]{1,0:T(8,128)(2,1)S(1)} %constant_dynamic-update-slice_fusion.refs_6_), channel_id=1, source_target_pairs={{0,12},{2,14},{4,8},{6,10},{8,4},{10,6},{12,0},{14,2},{16,28},{18,... | collective-permute-start | bytes 786440 | tf_op jit(solution)/shard_map/ppermute | solution.py:273
  26.1 12.2 %collective-permute-start.8 = (bf16[256,512]{1,0:T(8,128)(2,1)S(1)}, bf16[256,512]{1,0:T(8,128)(2,1)S(1)}, u32[]{:S(2)}, u32[]{:S(2)}) collective-permute-start(bf16[256,512]{1,0:T(8,128)(2,1)S(1)} %constant_dynamic-update-slice_fusion.refs_6_), channel_id=1, source_target_pairs={{0,4},{2,6},{4,0},{6,2},{8,12},{10,14},{12,8},{14,10},{16,20},{18,... | collective-permute-start | bytes 786440 | tf_op jit(solution)/shard_map/ppermute | solution.py:273
  26.6 11.7 %collective-permute-start.9 = (bf16[256,512]{1,0:T(8,128)(2,1)S(1)}, bf16[256,512]{1,0:T(8,128)(2,1)S(1)}, u32[]{:S(2)}, u32[]{:S(2)}) collective-permute-start(bf16[256,512]{1,0:T(8,128)(2,1)S(1)} %constant_dynamic-update-slice_fusion.refs_6_), channel_id=1, source_target_pairs={{0,8},{2,10},{4,12},{6,14},{8,0},{10,2},{12,4},{14,6},{16,24},{18,... | collective-permute-start | bytes 786440 | tf_op jit(solution)/shard_map/ppermute | solution.py:273
  27.8 5.9 %collective-permute-start.6 = (bf16[128,512]{1,0:T(8,128)(2,1)S(1)}, bf16[128,512]{1,0:T(8,128)(2,1)S(1)}, u32[]{:S(2)}, u32[]{:S(2)}) collective-permute-start(bf16[128,512]{1,0:T(8,128)(2,1)S(1)} %collective-permute-done.3.refs_1_), channel_id=1, source_target_pairs={{0,1},{1,0},{2,3},{3,2},{4,5},{5,4},{6,7},{7,6},{8,9},{9,8},{10,11... | collective-permute-start | bytes 393224 | tf_op jit(solution)/shard_map/ppermute | solution.py:245
  30.3 5.0 %collective-permute-start.7 = (bf16[128,512]{1,0:T(8,128)(2,1)S(1)}, bf16[128,512]{1,0:T(8,128)(2,1)S(1)}, u32[]{:S(2)}, u32[]{:S(2)}) collective-permute-start(bf16[128,512]{1,0:T(8,128)(2,1)S(1)} %collective-permute-done.4.refs_2_), channel_id=1, source_target_pairs={{0,1},{1,0},{2,3},{3,2},{4,5},{5,4},{6,7},{7,6},{8,9},{9,8},{10,11... | collective-permute-start | bytes 393224 | tf_op jit(solution)/shard_map/ppermute | solution.py:245
  39.7 4.0 %collective-permute-start.11 = (f32[512,512]{1,0:T(8,128)S(1)}, f32[512,512]{1,0:T(8,128)S(1)}, u32[]{:S(2)}, u32[]{:S(2)}) collective-permute-start(f32[512,512]{1,0:T(8,128)S(1)} %shard_map.51.mine_ref), channel_id=1, source_target_pairs={{0,2},{2,0},{4,6},{6,4},{8,10},{10,8},{12,14},{14,12},{16,18},{18,... | collective-permute-start | bytes 3145736 | tf_op jit(solution)/shard_map/ppermute | solution.py:242
  40.3 1.3 %copy-start.1 = (bf16[8,2,128,512]{3,2,1,0:T(8,128)(2,1)}, bf16[8,2,128,512]{3,2,1,0:T(8,128)(2,1)S(1)}, u32[]{:S(2)}) copy-start(bf16[8,2,128,512]{3,2,1,0:T(8,128)(2,1)S(1)} %broadcast.16) | copy-start | bytes 6291460
  43.0 18.0 %copy-start.2 = (bf16[8,2,128,512]{3,2,1,0:T(8,128)(2,1)S(1)}, bf16[8,2,128,512]{3,2,1,0:T(8,128)(2,1)}, u32[]{:S(2)}) copy-start(bf16[8,2,128,512]{3,2,1,0:T(8,128)(2,1)} %copy-done.1) | copy-start | bytes 6291460
  51.2 6.6 %collective-permute-start.12 = (bf16[128,512]{1,0:T(8,128)(2,1)S(1)}, bf16[128,512]{1,0:T(8,128)(2,1)S(1)}, u32[]{:S(2)}, u32[]{:S(2)}) collective-permute-start(bf16[128,512]{1,0:T(8,128)(2,1)S(1)} %get-tuple-element.26), channel_id=1, source_target_pairs={{0,8},{2,6},{8,16},{10,2},{16,24},{18,10},{24,28},{26,18},{28,20},... | collective-permute-start | bytes 393224 | tf_op jit(solution)/shard_map/ppermute | solution.py:322
  52.9 6.7 %collective-permute-start.14 = (bf16[128,512]{1,0:T(8,128)(2,1)S(1)}, bf16[128,512]{1,0:T(8,128)(2,1)S(1)}, u32[]{:S(2)}, u32[]{:S(2)}) collective-permute-start(bf16[128,512]{1,0:T(8,128)(2,1)S(1)} %get-tuple-element.27), channel_id=1, source_target_pairs={{0,8},{2,6},{8,16},{10,2},{16,24},{18,10},{24,28},{26,18},{28,20},... | collective-permute-start | bytes 393224 | tf_op jit(solution)/shard_map/ppermute | solution.py:322
  54.9 6.1 %collective-permute-start.26 = (bf16[128,512]{1,0:T(8,128)(2,1)S(1)}, bf16[128,512]{1,0:T(8,128)(2,1)S(1)}, u32[]{:S(2)}, u32[]{:S(2)}) collective-permute-start(bf16[128,512]{1,0:T(8,128)(2,1)S(1)} %get-tuple-element.29), channel_id=1, source_target_pairs={{0,1},{1,0},{2,3},{3,2},{4,5},{5,4},{6,7},{7,6},{8,9},{9,8},{10,11... | collective-permute-start | bytes 393224 | tf_op jit(solution)/shard_map/ppermute | solution.py:245
  57.8 3.2 %collective-permute-start.13 = (bf16[128,512]{1,0:T(8,128)(2,1)S(1)}, bf16[128,512]{1,0:T(8,128)(2,1)S(1)}, u32[]{:S(2)}, u32[]{:S(2)}) collective-permute-start(bf16[128,512]{1,0:T(8,128)(2,1)S(1)} %collective-permute-done.12), channel_id=1, source_target_pairs={{0,2},{2,0},{4,6},{6,4},{8,10},{10,8},{12,14},{14,12},{16,18},{18,... | collective-permute-start | bytes 393224 | tf_op jit(solution)/shard_map/ppermute | solution.py:242
  57.8 5.0 %collective-permute-start.16 = (bf16[128,512]{1,0:T(8,128)(2,1)S(1)}, bf16[128,512]{1,0:T(8,128)(2,1)S(1)}, u32[]{:S(2)}, u32[]{:S(2)}) collective-permute-start(bf16[128,512]{1,0:T(8,128)(2,1)S(1)} %collective-permute-done.12), channel_id=1, source_target_pairs={{0,8},{2,6},{8,16},{10,2},{16,24},{18,10},{24,28},{26,18},{28,20},... | collective-permute-start | bytes 393224 | tf_op jit(solution)/shard_map/ppermute | solution.py:322
  59.6 4.5 %collective-permute-start.15 = (bf16[128,512]{1,0:T(8,128)(2,1)S(1)}, bf16[128,512]{1,0:T(8,128)(2,1)S(1)}, u32[]{:S(2)}, u32[]{:S(2)}) collective-permute-start(bf16[128,512]{1,0:T(8,128)(2,1)S(1)} %collective-permute-done.14), channel_id=1, source_target_pairs={{0,2},{2,0},{4,6},{6,4},{8,10},{10,8},{12,14},{14,12},{16,18},{18,... | collective-permute-start | bytes 393224 | tf_op jit(solution)/shard_map/ppermute | solution.py:242
  59.6 6.3 %collective-permute-start.18 = (bf16[128,512]{1,0:T(8,128)(2,1)S(1)}, bf16[128,512]{1,0:T(8,128)(2,1)S(1)}, u32[]{:S(2)}, u32[]{:S(2)}) collective-permute-start(bf16[128,512]{1,0:T(8,128)(2,1)S(1)} %collective-permute-done.14), channel_id=1, source_target_pairs={{0,8},{2,6},{8,16},{10,2},{16,24},{18,10},{24,28},{26,18},{28,20},... | collective-permute-start | bytes 393224 | tf_op jit(solution)/shard_map/ppermute | solution.py:322
  61.0 6.2 %collective-permute-start.27 = (bf16[128,512]{1,0:T(8,128)(2,1)S(1)}, bf16[128,512]{1,0:T(8,128)(2,1)S(1)}, u32[]{:S(2)}, u32[]{:S(2)}) collective-permute-start(bf16[128,512]{1,0:T(8,128)(2,1)S(1)} %collective-permute-done.26), channel_id=1, source_target_pairs={{0,2},{2,0},{4,6},{6,4},{8,10},{10,8},{12,14},{14,12},{16,18},{18,... | collective-permute-start | bytes 393224 | tf_op jit(solution)/shard_map/ppermute | solution.py:242
  61.0 7.6 %collective-permute-start.28 = (bf16[128,512]{1,0:T(8,128)(2,1)S(1)}, bf16[128,512]{1,0:T(8,128)(2,1)S(1)}, u32[]{:S(2)}, u32[]{:S(2)}) collective-permute-start(bf16[128,512]{1,0:T(8,128)(2,1)S(1)} %collective-permute-done.26), channel_id=1, source_target_pairs={{0,8},{2,6},{8,16},{10,2},{16,24},{18,10},{24,28},{26,18},{28,20},... | collective-permute-start | bytes 393224 | tf_op jit(solution)/shard_map/ppermute | solution.py:322
  62.8 6.8 %collective-permute-start.17 = (bf16[128,512]{1,0:T(8,128)(2,1)S(1)}, bf16[128,512]{1,0:T(8,128)(2,1)S(1)}, u32[]{:S(2)}, u32[]{:S(2)}) collective-permute-start(bf16[128,512]{1,0:T(8,128)(2,1)S(1)} %collective-permute-done.16), channel_id=1, source_target_pairs={{0,2},{2,0},{4,6},{6,4},{8,10},{10,8},{12,14},{14,12},{16,18},{18,... | collective-permute-start | bytes 393224 | tf_op jit(solution)/shard_map/ppermute | solution.py:242
  64.1 10.9 %collective-permute-start.20 = (bf16[128,512]{1,0:T(8,128)(2,1)S(1)}, bf16[128,512]{1,0:T(8,128)(2,1)S(1)}, u32[]{:S(2)}, u32[]{:S(2)}) collective-permute-start(bf16[128,512]{1,0:T(8,128)(2,1)S(1)} %collective-permute-done.16), channel_id=1, source_target_pairs={{0,8},{2,6},{8,16},{10,2},{16,24},{18,10},{24,28},{26,18},{28,20},... | collective-permute-start | bytes 393224 | tf_op jit(solution)/shard_map/ppermute | solution.py:322
  65.9 5.0 %collective-permute-start.19 = (bf16[128,512]{1,0:T(8,128)(2,1)S(1)}, bf16[128,512]{1,0:T(8,128)(2,1)S(1)}, u32[]{:S(2)}, u32[]{:S(2)}) collective-permute-start(bf16[128,512]{1,0:T(8,128)(2,1)S(1)} %collective-permute-done.18), channel_id=1, source_target_pairs={{0,2},{2,0},{4,6},{6,4},{8,10},{10,8},{12,14},{14,12},{16,18},{18,... | collective-permute-start | bytes 393224 | tf_op jit(solution)/shard_map/ppermute | solution.py:242
  67.2 9.7 %collective-permute-start.22 = (bf16[128,512]{1,0:T(8,128)(2,1)S(1)}, bf16[128,512]{1,0:T(8,128)(2,1)S(1)}, u32[]{:S(2)}, u32[]{:S(2)}) collective-permute-start(bf16[128,512]{1,0:T(8,128)(2,1)S(1)} %collective-permute-done.18), channel_id=1, source_target_pairs={{0,8},{2,6},{8,16},{10,2},{16,24},{18,10},{24,28},{26,18},{28,20},... | collective-permute-start | bytes 393224 | tf_op jit(solution)/shard_map/ppermute | solution.py:322
  68.6 5.0 %collective-permute-start.30 = (bf16[128,512]{1,0:T(8,128)(2,1)S(1)}, bf16[128,512]{1,0:T(8,128)(2,1)S(1)}, u32[]{:S(2)}, u32[]{:S(2)}) collective-permute-start(bf16[128,512]{1,0:T(8,128)(2,1)S(1)} %collective-permute-done.27), channel_id=1, source_target_pairs={{0,8},{2,6},{8,16},{10,2},{16,24},{18,10},{24,28},{26,18},{28,20},... | collective-permute-start | bytes 393224 | tf_op jit(solution)/shard_map/ppermute | solution.py:322
  69.5 6.8 %collective-permute-start.29 = (bf16[128,512]{1,0:T(8,128)(2,1)S(1)}, bf16[128,512]{1,0:T(8,128)(2,1)S(1)}, u32[]{:S(2)}, u32[]{:S(2)}) collective-permute-start(bf16[128,512]{1,0:T(8,128)(2,1)S(1)} %collective-permute-done.28), channel_id=1, source_target_pairs={{0,2},{2,0},{4,6},{6,4},{8,10},{10,8},{12,14},{14,12},{16,18},{18,... | collective-permute-start | bytes 393224 | tf_op jit(solution)/shard_map/ppermute | solution.py:242
  70.8 5.5 %collective-permute-start.32 = (bf16[128,512]{1,0:T(8,128)(2,1)S(1)}, bf16[128,512]{1,0:T(8,128)(2,1)S(1)}, u32[]{:S(2)}, u32[]{:S(2)}) collective-permute-start(bf16[128,512]{1,0:T(8,128)(2,1)S(1)} %collective-permute-done.28), channel_id=1, source_target_pairs={{0,8},{2,6},{8,16},{10,2},{16,24},{18,10},{24,28},{26,18},{28,20},... | collective-permute-start | bytes 393224 | tf_op jit(solution)/shard_map/ppermute | solution.py:322
  73.7 8.2 %collective-permute-start.31 = (bf16[128,512]{1,0:T(8,128)(2,1)S(1)}, bf16[128,512]{1,0:T(8,128)(2,1)S(1)}, u32[]{:S(2)}, u32[]{:S(2)}) collective-permute-start(bf16[128,512]{1,0:T(8,128)(2,1)S(1)} %collective-permute-done.30), channel_id=1, source_target_pairs={{0,2},{2,0},{4,6},{6,4},{8,10},{10,8},{12,14},{14,12},{16,18},{18,... | collective-permute-start | bytes 393224 | tf_op jit(solution)/shard_map/ppermute | solution.py:242
  75.0 5.5 %collective-permute-start.34 = (bf16[128,512]{1,0:T(8,128)(2,1)S(1)}, bf16[128,512]{1,0:T(8,128)(2,1)S(1)}, u32[]{:S(2)}, u32[]{:S(2)}) collective-permute-start(bf16[128,512]{1,0:T(8,128)(2,1)S(1)} %collective-permute-done.30), channel_id=1, source_target_pairs={{0,8},{2,6},{8,16},{10,2},{16,24},{18,10},{24,28},{26,18},{28,20},... | collective-permute-start | bytes 393224 | tf_op jit(solution)/shard_map/ppermute | solution.py:322
  76.3 1.5 %collective-permute-start.21 = (bf16[128,512]{1,0:T(8,128)(2,1)S(1)}, bf16[128,512]{1,0:T(8,128)(2,1)S(1)}, u32[]{:S(2)}, u32[]{:S(2)}) collective-permute-start(bf16[128,512]{1,0:T(8,128)(2,1)S(1)} %collective-permute-done.20), channel_id=1, source_target_pairs={{0,2},{2,0},{4,6},{6,4},{8,10},{10,8},{12,14},{14,12},{16,18},{18,... | collective-permute-start | bytes 393224 | tf_op jit(solution)/shard_map/ppermute | solution.py:242
  76.3 6.5 %collective-permute-start.33 = (bf16[128,512]{1,0:T(8,128)(2,1)S(1)}, bf16[128,512]{1,0:T(8,128)(2,1)S(1)}, u32[]{:S(2)}, u32[]{:S(2)}) collective-permute-start(bf16[128,512]{1,0:T(8,128)(2,1)S(1)} %collective-permute-done.32), channel_id=1, source_target_pairs={{0,2},{2,0},{4,6},{6,4},{8,10},{10,8},{12,14},{14,12},{16,18},{18,... | collective-permute-start | bytes 393224 | tf_op jit(solution)/shard_map/ppermute | solution.py:242
  76.9 5.9 %collective-permute-start.36 = (bf16[128,512]{1,0:T(8,128)(2,1)S(1)}, bf16[128,512]{1,0:T(8,128)(2,1)S(1)}, u32[]{:S(2)}, u32[]{:S(2)}) collective-permute-start(bf16[128,512]{1,0:T(8,128)(2,1)S(1)} %collective-permute-done.32), channel_id=1, source_target_pairs={{0,8},{2,6},{8,16},{10,2},{16,24},{18,10},{24,28},{26,18},{28,20},... | collective-permute-start | bytes 393224 | tf_op jit(solution)/shard_map/ppermute | solution.py:322
  77.8 1.3 %collective-permute-start.23 = (bf16[128,512]{1,0:T(8,128)(2,1)S(1)}, bf16[128,512]{1,0:T(8,128)(2,1)S(1)}, u32[]{:S(2)}, u32[]{:S(2)}) collective-permute-start(bf16[128,512]{1,0:T(8,128)(2,1)S(1)} %collective-permute-done.22), channel_id=1, source_target_pairs={{0,2},{2,0},{4,6},{6,4},{8,10},{10,8},{12,14},{14,12},{16,18},{18,... | collective-permute-start | bytes 393224 | tf_op jit(solution)/shard_map/ppermute | solution.py:242
  79.2 5.0 %collective-permute-start.24 = (bf16[128,512]{1,0:T(8,128)(2,1)S(1)}, bf16[128,512]{1,0:T(8,128)(2,1)S(1)}, u32[]{:S(2)}, u32[]{:S(2)}) collective-permute-start(bf16[128,512]{1,0:T(8,128)(2,1)S(1)} %collective-permute-done.20), channel_id=1, source_target_pairs={{0,8},{2,6},{8,16},{10,2},{16,24},{18,10},{24,28},{26,18},{28,20},... | collective-permute-start | bytes 393224 | tf_op jit(solution)/shard_map/ppermute | solution.py:322
  80.5 7.7 %collective-permute-start.35 = (bf16[128,512]{1,0:T(8,128)(2,1)S(1)}, bf16[128,512]{1,0:T(8,128)(2,1)S(1)}, u32[]{:S(2)}, u32[]{:S(2)}) collective-permute-start(bf16[128,512]{1,0:T(8,128)(2,1)S(1)} %collective-permute-done.34), channel_id=1, source_target_pairs={{0,2},{2,0},{4,6},{6,4},{8,10},{10,8},{12,14},{14,12},{16,18},{18,... | collective-permute-start | bytes 393224 | tf_op jit(solution)/shard_map/ppermute | solution.py:242
  81.9 7.7 %copy-start.3 = (bf16[8,2,128,512]{3,2,1,0:T(8,128)(2,1)S(1)}, bf16[8,2,128,512]{3,2,1,0:T(8,128)(2,1)}, u32[]{:S(2)}) copy-start(bf16[8,2,128,512]{3,2,1,0:T(8,128)(2,1)} %bitcast_dynamic-update-slice_fusion.18) | copy-start | bytes 6291460
  81.9 5.0 %collective-permute-start.38 = (bf16[128,512]{1,0:T(8,128)(2,1)S(1)}, bf16[128,512]{1,0:T(8,128)(2,1)S(1)}, u32[]{:S(2)}, u32[]{:S(2)}) collective-permute-start(bf16[128,512]{1,0:T(8,128)(2,1)S(1)} %collective-permute-done.34), channel_id=1, source_target_pairs={{0,8},{2,6},{8,16},{10,2},{16,24},{18,10},{24,28},{26,18},{28,20},... | collective-permute-start | bytes 393224 | tf_op jit(solution)/shard_map/ppermute | solution.py:322
  82.8 5.5 %collective-permute-start.37 = (bf16[128,512]{1,0:T(8,128)(2,1)S(1)}, bf16[128,512]{1,0:T(8,128)(2,1)S(1)}, u32[]{:S(2)}, u32[]{:S(2)}) collective-permute-start(bf16[128,512]{1,0:T(8,128)(2,1)S(1)} %collective-permute-done.36), channel_id=1, source_target_pairs={{0,2},{2,0},{4,6},{6,4},{8,10},{10,8},{12,14},{14,12},{16,18},{18,... | collective-permute-start | bytes 393224 | tf_op jit(solution)/shard_map/ppermute | solution.py:242
  82.8 5.4 %collective-permute-start.40 = (bf16[128,512]{1,0:T(8,128)(2,1)S(1)}, bf16[128,512]{1,0:T(8,128)(2,1)S(1)}, u32[]{:S(2)}, u32[]{:S(2)}) collective-permute-start(bf16[128,512]{1,0:T(8,128)(2,1)S(1)} %collective-permute-done.36), channel_id=1, source_target_pairs={{0,8},{2,6},{8,16},{10,2},{16,24},{18,10},{24,28},{26,18},{28,20},... | collective-permute-start | bytes 393224 | tf_op jit(solution)/shard_map/ppermute | solution.py:322
  84.2 4.2 %collective-permute-start.25 = (bf16[128,512]{1,0:T(8,128)(2,1)S(1)}, bf16[128,512]{1,0:T(8,128)(2,1)S(1)}, u32[]{:S(2)}, u32[]{:S(2)}) collective-permute-start(bf16[128,512]{1,0:T(8,128)(2,1)S(1)} %collective-permute-done.24), channel_id=1, source_target_pairs={{0,2},{2,0},{4,6},{6,4},{8,10},{10,8},{12,14},{14,12},{16,18},{18,... | collective-permute-start | bytes 393224 | tf_op jit(solution)/shard_map/ppermute | solution.py:242
  86.8 1.5 %collective-permute-start.39 = (bf16[128,512]{1,0:T(8,128)(2,1)S(1)}, bf16[128,512]{1,0:T(8,128)(2,1)S(1)}, u32[]{:S(2)}, u32[]{:S(2)}) collective-permute-start(bf16[128,512]{1,0:T(8,128)(2,1)S(1)} %collective-permute-done.38), channel_id=1, source_target_pairs={{0,2},{2,0},{4,6},{6,4},{8,10},{10,8},{12,14},{14,12},{16,18},{18,... | collective-permute-start | bytes 393224 | tf_op jit(solution)/shard_map/ppermute | solution.py:242
  88.2 1.3 %collective-permute-start.41 = (bf16[128,512]{1,0:T(8,128)(2,1)S(1)}, bf16[128,512]{1,0:T(8,128)(2,1)S(1)}, u32[]{:S(2)}, u32[]{:S(2)}) collective-permute-start(bf16[128,512]{1,0:T(8,128)(2,1)S(1)} %collective-permute-done.40), channel_id=1, source_target_pairs={{0,2},{2,0},{4,6},{6,4},{8,10},{10,8},{12,14},{14,12},{16,18},{18,... | collective-permute-start | bytes 393224 | tf_op jit(solution)/shard_map/ppermute | solution.py:242

commit v10 on v7

--- a/solution.py
+++ b/solution.py
@@ -320,20 +320,30 @@
             columns[chunk], piece[None, None], (ring_band(position, bands), half, 0, 0)
         )
 
-    for hop in range(half_way + 1):
+    def join(own, other):
+        return jnp.where(
+            plane == 0,
+            jnp.concatenate([own, other], axis=-1),
+            jnp.concatenate([other, own], axis=-1),
+        )
+
+    for hop in range(half_way):
         for k, head in enumerate(heads):
             chunk, half = k // 2, (core if k % 2 == 0 else 1 - core)
-            if hop == half_way and k % 2 == 1:
-                continue
             if hop > 0:
                 heads[k] = head = turn(head)
                 put(chunk, swap_core(head), spot + ahead * hop, 1 - half)
             put(chunk, head, spot - ahead * hop, half)
-    former, latter = (column.reshape(bands, cores * rows, BLOCK) for column in columns)
-    update = jnp.where(
-        plane == 0,
-        jnp.concatenate([former, latter], axis=-1),
-        jnp.concatenate([latter, former], axis=-1),
+    update = join(*(column.reshape(bands, cores * rows, BLOCK) for column in columns))
+    opposite = []
+    for head in heads[::2]:
+        mine = turn(head)
+        other = swap_core(mine)
+        opposite.append(
+            jnp.where(core == 0, jnp.concatenate([mine, other]), jnp.concatenate([other, mine]))
+        )
+    update = lax.dynamic_update_slice(
+        update, join(*opposite)[None], (ring_band(spot + half_way, bands), 0, 0)
     )
     return (outputs, update)
 

time: 79.4 us -> 80.2 us (1.010)
  local copies, waits for them, and re-layouts: 2.23 us -> 4.18 us
  other arithmetic: 2.81 us -> 1.7 us
    unnamed x5 -> x7, local copies, waits for them, and re-layouts: 1.24 us -> 3.25 us
    select_n x1, other arithmetic: 2.66 us -> 1.27 us  [join(): jnp.where(plane == 0, jnp.concatenate([own, other], axis=-1), jnp.concate...]
  transfers between devices with their start and end apart: 42 -> 42, of which waited for: 15 -> 15; matrix products, arithmetic and copies ran while one was open for 6% -> 8% of each run, Pallas kernels for 1% -> 1%
where the time goes in v10:
time: 80.2 us; the launch traced here: 80 us
  starting transfers between devices  42.5 us (53%)
  waiting for transfers between devices  17.2 us (21%)
  Pallas kernels  9.42 us (12%)
  local copies, waits for them, and re-layouts  4.18 us (5%)
  matrix products  3.6 us (4%)
  other arithmetic  1.7 us (2%)
  between operations  1.35 us (2%)
    ppermute x14, starting transfers between devices, turn(): return lax.ppermute(array, 'dp', pairs)  20.4 us
    pallas_call x3, Pallas kernels, call(): pl.pallas_call(kernel, out_shape=out_shapes, in_specs=in_specs, out_specs...  9.42 us
    ppermute x5, starting transfers between devices, exchange(): return lax.ppermute(array, 'dp', pairs)  9.35 us
    ppermute x4, starting transfers between devices, swap_plane(): lax.ppermute(array, 'pre', [(c, members - 1 - c) for c in range(members)])  6.98 us
    ppermute x4, waiting for transfers between devices, swap_plane(): lax.ppermute(array, 'pre', [(c, members - 1 - c) for c in range(members)])  6.2 us
    ppermute x14, waiting for transfers between devices, turn(): return lax.ppermute(array, 'dp', pairs)  4.28 us
    ppermute x3, starting transfers between devices, deal(): return lax.ppermute(array, ('dp', 'pre'), pairs)  3.88 us
    ppermute x16, waiting for transfers between devices, swap_core(): return lax.ppermute(array, 'dp', [(g, g ^ 1) for g in range(groups)])  3.61 us
  transfers between devices with their start and end apart: 42, of which 15 were waited for; matrix products, arithmetic and copies ran while one was open for 8% of the time, Pallas kernels for 1%

profile of v10, /device:TPU:0, one launch (start us, length us, event | category | flops | bytes accessed | tf_op | source)
XLA Modules:
  0.0 80.0 jit_solution(14854726374559830817)
XLA Ops:
  0.6 4.1 %collective-permute-start = (bf16[128,512]{1,0:T(8,128)(2,1)}, bf16[128,512]{1,0:T(8,128)(2,1)S(1)}, u32[]{:S(2)}, u32[]{:S(2)}) collective-permute-start(bf16[128,512]{1,0:T(8,128)(2,1)} %param.5), channel_id=1, source_target_pairs={{0,16},{2,18},{4,20},{6,22},{8,24},{10,26},{12,28},{14,30},{16,0},... | collective-permute-start | bytes 393224 | tf_op jit(solution)/shard_map/ppermute | solution.py:273
  4.8 1.2 %copy-done = bf16[128,4096]{1,0:T(8,128)(2,1)S(1)} copy-done((bf16[128,4096]{1,0:T(8,128)(2,1)S(1)}, bf16[128,4096]{1,0:T(8,128)(2,1)}, u32[]{:S(2)}) %copy-start) | copy-done | bytes 1048600
  6.0 0.6 shard_map.50
  6.6 1.6 %collective-permute-start.1 = (bf16[128,512]{1,0:T(8,128)(2,1)S(1)}, bf16[128,512]{1,0:T(8,128)(2,1)S(1)}, u32[]{:S(2)}, u32[]{:S(2)}) collective-permute-start(bf16[128,512]{1,0:T(8,128)(2,1)S(1)} %get-tuple-element.14), channel_id=1, source_target_pairs={{0,4},{2,6},{4,0},{6,2},{8,12},{10,14},{12,8},{14,10},{16,20},{18,... | collective-permute-start | bytes 393224 | tf_op jit(solution)/shard_map/ppermute | solution.py:273
  8.2 0.3 collective-permute-start.2
  8.6 3.5 %collective-permute-start.3 = (bf16[128,512]{1,0:T(8,128)(2,1)S(1)}, bf16[128,512]{1,0:T(8,128)(2,1)S(1)}, u32[]{:S(2)}, u32[]{:S(2)}) collective-permute-start(bf16[128,512]{1,0:T(8,128)(2,1)S(1)} %get-tuple-element.16), channel_id=1, source_target_pairs={{0,28},{1,25},{2,30},{3,27},{4,24},{5,29},{6,26},{7,31},{8,20},{9,... | collective-permute-start | bytes 393224 | tf_op jit(solution)/shard_map/ppermute | solution.py:257
  12.1 3.6 %convolution_convert_fusion = bf16[128,512]{1,0:T(8,128)(2,1)} fusion(bf16[128,4096]{1,0:T(8,128)(2,1)S(1)} %copy-done, bf16[4096,512]{1,0:T(8,128)(2,1)} %param.4), kind=kOutput, calls=%fused_computation.1 | convolution fusion | flops 536936448 | bytes 5373952 | tf_op jit(solution)/shard_map/dot_general | solution.py:275
  15.8 3.0 %collective-permute-start.10 = (bf16[256,512]{1,0:T(8,128)(2,1)S(1)}, bf16[256,512]{1,0:T(8,128)(2,1)S(1)}, u32[]{:S(2)}, u32[]{:S(2)}) collective-permute-start(bf16[256,512]{1,0:T(8,128)(2,1)S(1)} %constant_dynamic-update-slice_fusion.refs_6_), channel_id=1, source_target_pairs={{0,12},{2,14},{4,8},{6,10},{8,4},{10,6},{12,0},{14,2},{16,28},{18,... | collective-permute-start | bytes 786440 | tf_op jit(solution)/shard_map/ppermute | solution.py:273
  18.8 1.8 %collective-permute-done.2.refs_0_ = bf16[128,512]{1,0:T(8,128)(2,1)S(1)} collective-permute-done((bf16[128,512]{1,0:T(8,128)(2,1)S(1)}, bf16[128,512]{1,0:T(8,128)(2,1)S(1)}, u32[]{:S(2)}, u32[]{:S(2)}) %collective-permute-start.2) | collective-permute-done | bytes 131104 | tf_op jit(solution)/shard_map/ppermute | solution.py:257
  20.6 2.4 %collective-permute-start.5 = (bf16[128,512]{1,0:T(8,128)(2,1)S(1)}, bf16[128,512]{1,0:T(8,128)(2,1)S(1)}, u32[]{:S(2)}, u32[]{:S(2)}) collective-permute-start(bf16[128,512]{1,0:T(8,128)(2,1)S(1)} %collective-permute-done.2.refs_0_), channel_id=1, source_target_pairs={{0,1},{1,0},{2,3},{3,2},{4,5},{5,4},{6,7},{7,6},{8,9},{9,8},{10,11... | collective-permute-start | bytes 393224 | tf_op jit(solution)/shard_map/ppermute | solution.py:245
  23.0 0.6 collective-permute-start.8
  23.6 1.0 %collective-permute-start.6 = (bf16[128,512]{1,0:T(8,128)(2,1)S(1)}, bf16[128,512]{1,0:T(8,128)(2,1)S(1)}, u32[]{:S(2)}, u32[]{:S(2)}) collective-permute-start(bf16[128,512]{1,0:T(8,128)(2,1)S(1)} %collective-permute-done.3.refs_1_), channel_id=1, source_target_pairs={{0,1},{1,0},{2,3},{3,2},{4,5},{5,4},{6,7},{7,6},{8,9},{9,8},{10,11... | collective-permute-start | bytes 393224 | tf_op jit(solution)/shard_map/ppermute | solution.py:245
  24.6 2.3 %collective-permute-done.5.refs_3_ = bf16[128,512]{1,0:T(8,128)(2,1)S(1)} collective-permute-done((bf16[128,512]{1,0:T(8,128)(2,1)S(1)}, bf16[128,512]{1,0:T(8,128)(2,1)S(1)}, u32[]{:S(2)}, u32[]{:S(2)}) %collective-permute-start.5) | collective-permute-done | bytes 131104 | tf_op jit(solution)/shard_map/ppermute | solution.py:245
  26.8 2.5 %collective-permute-start.7 = (bf16[128,512]{1,0:T(8,128)(2,1)S(1)}, bf16[128,512]{1,0:T(8,128)(2,1)S(1)}, u32[]{:S(2)}, u32[]{:S(2)}) collective-permute-start(bf16[128,512]{1,0:T(8,128)(2,1)S(1)} %collective-permute-done.4.refs_2_), channel_id=1, source_target_pairs={{0,1},{1,0},{2,3},{3,2},{4,5},{5,4},{6,7},{7,6},{8,9},{9,8},{10,11... | collective-permute-start | bytes 393224 | tf_op jit(solution)/shard_map/ppermute | solution.py:245
  29.4 0.6 collective-permute-done.6.refs_4_
  30.0 2.2 %collective-permute-done.7.refs_5_ = bf16[128,512]{1,0:T(8,128)(2,1)S(1)} collective-permute-done((bf16[128,512]{1,0:T(8,128)(2,1)S(1)}, bf16[128,512]{1,0:T(8,128)(2,1)S(1)}, u32[]{:S(2)}, u32[]{:S(2)}) %collective-permute-start.7) | collective-permute-done | bytes 131104 | tf_op jit(solution)/shard_map/ppermute | solution.py:245
  32.3 1.4 %collective-permute-done.8.refs_7_ = bf16[256,512]{1,0:T(8,128)(2,1)S(1)} collective-permute-done((bf16[256,512]{1,0:T(8,128)(2,1)S(1)}, bf16[256,512]{1,0:T(8,128)(2,1)S(1)}, u32[]{:S(2)}, u32[]{:S(2)}) %collective-permute-start.8) | collective-permute-done | bytes 262176 | tf_op jit(solution)/shard_map/ppermute | solution.py:273
  33.6 1.4 %shard_map.51.mine_ref = f32[512,512]{1,0:T(8,128)S(1)} custom-call(s32[2]{0:T(128)S(1)} %pad_add_fusion.1.place_ref, bf16[128,512]{1,0:T(8,128)(2,1)S(1)} %get-tuple-element.13.own_ref, bf16[128,512]{1,0:T(8,128)(2,1)S(1)} %collective-permute-done.1.shared_ref, bf16[128,512]{1,0:T(8,128)(2,1)S(1)} %collective-permute-done.2.refs_0_, ...), custom_call_target="tpu_custom_call" | custom-call | tf_op jit(solution)/shard_map/pallas_call | solution.py:217
  35.5 2.3 %collective-permute-done.11.other_ref = f32[512,512]{1,0:T(8,128)S(1)} collective-permute-done((f32[512,512]{1,0:T(8,128)S(1)}, f32[512,512]{1,0:T(8,128)S(1)}, u32[]{:S(2)}, u32[]{:S(2)}) %collective-permute-start.11) | collective-permute-done | bytes 1048608 | tf_op jit(solution)/shard_map/ppermute | solution.py:242
  37.8 7.4 %shard_map.52 = (bf16[128,512]{1,0:T(8,128)(2,1)S(1)}, bf16[128,512]{1,0:T(8,128)(2,1)S(1)}, bf16[128,512]{1,0:T(8,128)(2,1)S(1)}) custom-call(s32[2]{0:T(128)S(1)} %pad_add_fusion.side_ref, f32[512,512]{1,0:T(8,128)S(1)} %shard_map.51.mine_ref, f32[512,512]{1,0:T(8,128)S(1)} %collective-permute-done.11.other_ref), custom_call_target="tpu_custom_call" | custom-call | tf_op jit(solution)/shard_map/pallas_call | solution.py:217
  45.2 1.1 %collective-permute-start.24 = (bf16[128,512]{1,0:T(8,128)(2,1)S(1)}, bf16[128,512]{1,0:T(8,128)(2,1)S(1)}, u32[]{:S(2)}, u32[]{:S(2)}) collective-permute-start(bf16[128,512]{1,0:T(8,128)(2,1)S(1)} %get-tuple-element.21), channel_id=1, source_target_pairs={{0,1},{1,0},{2,3},{3,2},{4,5},{5,4},{6,7},{7,6},{8,9},{9,8},{10,11... | collective-permute-start | bytes 393224 | tf_op jit(solution)/shard_map/ppermute | solution.py:245
  46.4 3.1 %collective-permute-start.14 = (bf16[128,512]{1,0:T(8,128)(2,1)S(1)}, bf16[128,512]{1,0:T(8,128)(2,1)S(1)}, u32[]{:S(2)}, u32[]{:S(2)}) collective-permute-start(bf16[128,512]{1,0:T(8,128)(2,1)S(1)} %get-tuple-element.20), channel_id=1, source_target_pairs={{0,8},{2,6},{8,16},{10,2},{16,24},{18,10},{24,28},{26,18},{28,20},... | collective-permute-start | bytes 393224 | tf_op jit(solution)/shard_map/ppermute | solution.py:311
  49.5 0.2 broadcast_in_dim.88.clone.1
  49.8 1.1 %collective-permute-done.24 = bf16[128,512]{1,0:T(8,128)(2,1)S(1)} collective-permute-done((bf16[128,512]{1,0:T(8,128)(2,1)S(1)}, bf16[128,512]{1,0:T(8,128)(2,1)S(1)}, u32[]{:S(2)}, u32[]{:S(2)}) %collective-permute-start.24) | collective-permute-done | bytes 131104 | tf_op jit(solution)/shard_map/ppermute | solution.py:245
  50.8 1.1 %collective-permute-start.26 = (bf16[128,512]{1,0:T(8,128)(2,1)S(1)}, bf16[128,512]{1,0:T(8,128)(2,1)S(1)}, u32[]{:S(2)}, u32[]{:S(2)}) collective-permute-start(bf16[128,512]{1,0:T(8,128)(2,1)S(1)} %collective-permute-done.24), channel_id=1, source_target_pairs={{0,8},{2,6},{8,16},{10,2},{16,24},{18,10},{24,28},{26,18},{28,20},... | collective-permute-start | bytes 393224 | tf_op jit(solution)/shard_map/ppermute | solution.py:311
  51.9 3.1 %collective-permute-start.16 = (bf16[128,512]{1,0:T(8,128)(2,1)S(1)}, bf16[128,512]{1,0:T(8,128)(2,1)S(1)}, u32[]{:S(2)}, u32[]{:S(2)}) collective-permute-start(bf16[128,512]{1,0:T(8,128)(2,1)S(1)} %collective-permute-done.12), channel_id=1, source_target_pairs={{0,8},{2,6},{8,16},{10,2},{16,24},{18,10},{24,28},{26,18},{28,20},... | collective-permute-start | bytes 393224 | tf_op jit(solution)/shard_map/ppermute | solution.py:311
  55.0 0.5 collective-permute-start.18
  55.5 0.2 broadcast_in_dim.88.clone
  55.8 1.8 %collective-permute-start.30 = (bf16[128,512]{1,0:T(8,128)(2,1)S(1)}, bf16[128,512]{1,0:T(8,128)(2,1)S(1)}, u32[]{:S(2)}, u32[]{:S(2)}) collective-permute-start(bf16[128,512]{1,0:T(8,128)(2,1)S(1)} %collective-permute-done.26), channel_id=1, source_target_pairs={{0,8},{2,6},{8,16},{10,2},{16,24},{18,10},{24,28},{26,18},{28,20},... | collective-permute-start | bytes 393224 | tf_op jit(solution)/shard_map/ppermute | solution.py:311
  57.8 2.4 %collective-permute-start.28 = (bf16[128,512]{1,0:T(8,128)(2,1)S(1)}, bf16[128,512]{1,0:T(8,128)(2,1)S(1)}, u32[]{:S(2)}, u32[]{:S(2)}) collective-permute-start(bf16[128,512]{1,0:T(8,128)(2,1)S(1)} %collective-permute-done.25), channel_id=1, source_target_pairs={{0,8},{2,6},{8,16},{10,2},{16,24},{18,10},{24,28},{26,18},{28,20},... | collective-permute-start | bytes 393224 | tf_op jit(solution)/shard_map/ppermute | solution.py:311
  60.2 1.2 %collective-permute-start.20 = (bf16[128,512]{1,0:T(8,128)(2,1)S(1)}, bf16[128,512]{1,0:T(8,128)(2,1)S(1)}, u32[]{:S(2)}, u32[]{:S(2)}) collective-permute-start(bf16[128,512]{1,0:T(8,128)(2,1)S(1)} %collective-permute-done.16), channel_id=1, source_target_pairs={{0,8},{2,6},{8,16},{10,2},{16,24},{18,10},{24,28},{26,18},{28,20},... | collective-permute-start | bytes 393224 | tf_op jit(solution)/shard_map/ppermute | solution.py:311
  61.5 1.1 %collective-permute-start.22 = (bf16[128,512]{1,0:T(8,128)(2,1)S(1)}, bf16[128,512]{1,0:T(8,128)(2,1)S(1)}, u32[]{:S(2)}, u32[]{:S(2)}) collective-permute-start(bf16[128,512]{1,0:T(8,128)(2,1)S(1)} %collective-permute-done.18), channel_id=1, source_target_pairs={{0,8},{2,6},{8,16},{10,2},{16,24},{18,10},{24,28},{26,18},{28,20},... | collective-permute-start | bytes 393224 | tf_op jit(solution)/shard_map/ppermute | solution.py:311
  62.8 1.1 %collective-permute-start.34 = (bf16[128,512]{1,0:T(8,128)(2,1)S(1)}, bf16[128,512]{1,0:T(8,128)(2,1)S(1)}, u32[]{:S(2)}, u32[]{:S(2)}) collective-permute-start(bf16[128,512]{1,0:T(8,128)(2,1)S(1)} %collective-permute-done.30), channel_id=1, source_target_pairs={{0,8},{2,6},{8,16},{10,2},{16,24},{18,10},{24,28},{26,18},{28,20},... | collective-permute-start | bytes 393224 | tf_op jit(solution)/shard_map/ppermute | solution.py:311
  64.1 0.5 collective-permute-start.29
  64.6 0.6 collective-permute-done.20
  65.1 1.4 %collective-permute-start.32 = (bf16[128,512]{1,0:T(8,128)(2,1)S(1)}, bf16[128,512]{1,0:T(8,128)(2,1)S(1)}, u32[]{:S(2)}, u32[]{:S(2)}) collective-permute-start(bf16[128,512]{1,0:T(8,128)(2,1)S(1)} %collective-permute-done.28), channel_id=1, source_target_pairs={{0,8},{2,6},{8,16},{10,2},{16,24},{18,10},{24,28},{26,18},{28,20},... | collective-permute-start | bytes 393224 | tf_op jit(solution)/shard_map/ppermute | solution.py:311
  66.6 1.2 %collective-permute-start.38 = (bf16[128,512]{1,0:T(8,128)(2,1)S(1)}, bf16[128,512]{1,0:T(8,128)(2,1)S(1)}, u32[]{:S(2)}, u32[]{:S(2)}) collective-permute-start(bf16[128,512]{1,0:T(8,128)(2,1)S(1)} %collective-permute-done.20), channel_id=1, source_target_pairs={{0,8},{2,6},{8,16},{10,2},{16,24},{18,10},{24,28},{26,18},{28,20},... | collective-permute-start | bytes 393224 | tf_op jit(solution)/shard_map/ppermute | solution.py:311
  68.0 0.4 collective-permute-start.23
  68.4 1.0 %collective-permute-start.40 = (bf16[128,512]{1,0:T(8,128)(2,1)S(1)}, bf16[128,512]{1,0:T(8,128)(2,1)S(1)}, u32[]{:S(2)}, u32[]{:S(2)}) collective-permute-start(bf16[128,512]{1,0:T(8,128)(2,1)S(1)} %collective-permute-done.34), channel_id=1, source_target_pairs={{0,8},{2,6},{8,16},{10,2},{16,24},{18,10},{24,28},{26,18},{28,20},... | collective-permute-start | bytes 393224 | tf_op jit(solution)/shard_map/ppermute | solution.py:311
  69.5 0.7 collective-permute-done.32
  70.1 1.4 %collective-permute-start.36 = (bf16[128,512]{1,0:T(8,128)(2,1)S(1)}, bf16[128,512]{1,0:T(8,128)(2,1)S(1)}, u32[]{:S(2)}, u32[]{:S(2)}) collective-permute-start(bf16[128,512]{1,0:T(8,128)(2,1)S(1)} %collective-permute-done.32), channel_id=1, source_target_pairs={{0,8},{2,6},{8,16},{10,2},{16,24},{18,10},{24,28},{26,18},{28,20},... | collective-permute-start | bytes 393224 | tf_op jit(solution)/shard_map/ppermute | solution.py:311
  71.7 0.5 collective-permute-start.39
  72.2 1.1 %collective-permute-done.40 = bf16[128,512]{1,0:T(8,128)(2,1)S(1)} collective-permute-done((bf16[128,512]{1,0:T(8,128)(2,1)S(1)}, bf16[128,512]{1,0:T(8,128)(2,1)S(1)}, u32[]{:S(2)}, u32[]{:S(2)}) %collective-permute-start.40) | collective-permute-done | bytes 131104 | tf_op jit(solution)/shard_map/ppermute | solution.py:311
  73.3 1.7 %collective-permute-done.36 = bf16[128,512]{1,0:T(8,128)(2,1)S(1)} collective-permute-done((bf16[128,512]{1,0:T(8,128)(2,1)S(1)}, bf16[128,512]{1,0:T(8,128)(2,1)S(1)}, u32[]{:S(2)}, u32[]{:S(2)}) %collective-permute-start.36) | collective-permute-done | bytes 131104 | tf_op jit(solution)/shard_map/ppermute | solution.py:311
  75.3 1.2 %collective-permute-done.37 = bf16[128,512]{1,0:T(8,128)(2,1)S(1)} collective-permute-done((bf16[128,512]{1,0:T(8,128)(2,1)S(1)}, bf16[128,512]{1,0:T(8,128)(2,1)S(1)}, u32[]{:S(2)}, u32[]{:S(2)}) %collective-permute-start.37) | collective-permute-done | bytes 131104 | tf_op jit(solution)/shard_map/ppermute | solution.py:242
  76.5 1.3 %maximum_select_fusion = bf16[8,256,1024]{2,1,0:T(8,128)(2,1)S(1)} fusion(bf16[8,256,512]{2,1,0:T(8,128)(2,1)S(1)} %bitcast.71, bf16[8,256,512]{2,1,0:T(8,128)(2,1)S(1)} %bitcast.72, pred[]{:T(512)S(6)} %eq.46), kind=kLoop, calls=%fused_computation | loop fusion | flops 18874368 | bytes 8388609 | tf_op jit(solution)/shard_map/jit(_where)/select_n | solution.py:324
  77.8 0.2 fusion
  78.0 2.0 %copy-done.1 = bf16[8,256,1024]{2,1,0:T(8,128)(2,1)} copy-done((bf16[8,256,1024]{2,1,0:T(8,128)(2,1)}, bf16[8,256,1024]{2,1,0:T(8,128)(2,1)S(1)}, u32[]{:S(2)}) %copy-start.1) | copy-done | bytes 4194328
  (85 shorter events, 1.8 us)
Async XLA Ops:
  0.6 15.1 %collective-permute-start = (bf16[128,512]{1,0:T(8,128)(2,1)}, bf16[128,512]{1,0:T(8,128)(2,1)S(1)}, u32[]{:S(2)}, u32[]{:S(2)}) collective-permute-start(bf16[128,512]{1,0:T(8,128)(2,1)} %param.5), channel_id=1, source_target_pairs={{0,16},{2,18},{4,20},{6,22},{8,24},{10,26},{12,28},{14,30},{16,0},... | collective-permute-start | bytes 393224 | tf_op jit(solution)/shard_map/ppermute | solution.py:273
  4.8 1.2 %copy-start = (bf16[128,4096]{1,0:T(8,128)(2,1)S(1)}, bf16[128,4096]{1,0:T(8,128)(2,1)}, u32[]{:S(2)}) copy-start(bf16[128,4096]{1,0:T(8,128)(2,1)} %inputs_ref.1) | copy-start | bytes 3145732
  6.6 16.4 %collective-permute-start.1 = (bf16[128,512]{1,0:T(8,128)(2,1)S(1)}, bf16[128,512]{1,0:T(8,128)(2,1)S(1)}, u32[]{:S(2)}, u32[]{:S(2)}) collective-permute-start(bf16[128,512]{1,0:T(8,128)(2,1)S(1)} %get-tuple-element.14), channel_id=1, source_target_pairs={{0,4},{2,6},{4,0},{6,2},{8,12},{10,14},{12,8},{14,10},{16,20},{18,... | collective-permute-start | bytes 393224 | tf_op jit(solution)/shard_map/ppermute | solution.py:273
  8.2 12.4 %collective-permute-start.2 = (bf16[128,512]{1,0:T(8,128)(2,1)S(1)}, bf16[128,512]{1,0:T(8,128)(2,1)S(1)}, u32[]{:S(2)}, u32[]{:S(2)}) collective-permute-start(bf16[128,512]{1,0:T(8,128)(2,1)S(1)} %get-tuple-element.15), channel_id=1, source_target_pairs={{0,16},{1,21},{2,18},{3,23},{4,20},{5,17},{6,22},{7,19},{8,24},{9,... | collective-permute-start | bytes 393224 | tf_op jit(solution)/shard_map/ppermute | solution.py:257
  8.6 14.4 %collective-permute-start.3 = (bf16[128,512]{1,0:T(8,128)(2,1)S(1)}, bf16[128,512]{1,0:T(8,128)(2,1)S(1)}, u32[]{:S(2)}, u32[]{:S(2)}) collective-permute-start(bf16[128,512]{1,0:T(8,128)(2,1)S(1)} %get-tuple-element.16), channel_id=1, source_target_pairs={{0,28},{1,25},{2,30},{3,27},{4,24},{5,29},{6,26},{7,31},{8,20},{9,... | collective-permute-start | bytes 393224 | tf_op jit(solution)/shard_map/ppermute | solution.py:257
  12.1 3.6 %copy-start.2 = (bf16[128,512]{1,0:T(8,128)(2,1)S(1)}, bf16[128,512]{1,0:T(8,128)(2,1)}, u32[]{:S(2)}) copy-start(bf16[128,512]{1,0:T(8,128)(2,1)} %param.5) | copy-start | bytes 393220
  12.1 11.5 %collective-permute-start.4 = (bf16[128,512]{1,0:T(8,128)(2,1)S(1)}, bf16[128,512]{1,0:T(8,128)(2,1)S(1)}, u32[]{:S(2)}, u32[]{:S(2)}) collective-permute-start(bf16[128,512]{1,0:T(8,128)(2,1)S(1)} %get-tuple-element.17), channel_id=1, source_target_pairs={{0,8},{1,13},{2,10},{3,15},{4,12},{5,9},{6,14},{7,11},{8,0},{9,5},... | collective-permute-start | bytes 393224 | tf_op jit(solution)/shard_map/ppermute | solution.py:257
  15.8 16.5 %collective-permute-start.10 = (bf16[256,512]{1,0:T(8,128)(2,1)S(1)}, bf16[256,512]{1,0:T(8,128)(2,1)S(1)}, u32[]{:S(2)}, u32[]{:S(2)}) collective-permute-start(bf16[256,512]{1,0:T(8,128)(2,1)S(1)} %constant_dynamic-update-slice_fusion.refs_6_), channel_id=1, source_target_pairs={{0,12},{2,14},{4,8},{6,10},{8,4},{10,6},{12,0},{14,2},{16,28},{18,... | collective-permute-start | bytes 786440 | tf_op jit(solution)/shard_map/ppermute | solution.py:273
  20.6 6.2 %collective-permute-start.5 = (bf16[128,512]{1,0:T(8,128)(2,1)S(1)}, bf16[128,512]{1,0:T(8,128)(2,1)S(1)}, u32[]{:S(2)}, u32[]{:S(2)}) collective-permute-start(bf16[128,512]{1,0:T(8,128)(2,1)S(1)} %collective-permute-done.2.refs_0_), channel_id=1, source_target_pairs={{0,1},{1,0},{2,3},{3,2},{4,5},{5,4},{6,7},{7,6},{8,9},{9,8},{10,11... | collective-permute-start | bytes 393224 | tf_op jit(solution)/shard_map/ppermute | solution.py:245
  23.0 9.3 %collective-permute-start.9 = (bf16[256,512]{1,0:T(8,128)(2,1)S(1)}, bf16[256,512]{1,0:T(8,128)(2,1)S(1)}, u32[]{:S(2)}, u32[]{:S(2)}) collective-permute-start(bf16[256,512]{1,0:T(8,128)(2,1)S(1)} %constant_dynamic-update-slice_fusion.refs_6_), channel_id=1, source_target_pairs={{0,8},{2,10},{4,12},{6,14},{8,0},{10,2},{12,4},{14,6},{16,24},{18,... | collective-permute-start | bytes 786440 | tf_op jit(solution)/shard_map/ppermute | solution.py:273
  23.0 10.6 %collective-permute-start.8 = (bf16[256,512]{1,0:T(8,128)(2,1)S(1)}, bf16[256,512]{1,0:T(8,128)(2,1)S(1)}, u32[]{:S(2)}, u32[]{:S(2)}) collective-permute-start(bf16[256,512]{1,0:T(8,128)(2,1)S(1)} %constant_dynamic-update-slice_fusion.refs_6_), channel_id=1, source_target_pairs={{0,4},{2,6},{4,0},{6,2},{8,12},{10,14},{12,8},{14,10},{16,20},{18,... | collective-permute-start | bytes 786440 | tf_op jit(solution)/shard_map/ppermute | solution.py:273
  23.6 6.4 %collective-permute-start.6 = (bf16[128,512]{1,0:T(8,128)(2,1)S(1)}, bf16[128,512]{1,0:T(8,128)(2,1)S(1)}, u32[]{:S(2)}, u32[]{:S(2)}) collective-permute-start(bf16[128,512]{1,0:T(8,128)(2,1)S(1)} %collective-permute-done.3.refs_1_), channel_id=1, source_target_pairs={{0,1},{1,0},{2,3},{3,2},{4,5},{5,4},{6,7},{7,6},{8,9},{9,8},{10,11... | collective-permute-start | bytes 393224 | tf_op jit(solution)/shard_map/ppermute | solution.py:245
  26.8 5.4 %collective-permute-start.7 = (bf16[128,512]{1,0:T(8,128)(2,1)S(1)}, bf16[128,512]{1,0:T(8,128)(2,1)S(1)}, u32[]{:S(2)}, u32[]{:S(2)}) collective-permute-start(bf16[128,512]{1,0:T(8,128)(2,1)S(1)} %collective-permute-done.4.refs_2_), channel_id=1, source_target_pairs={{0,1},{1,0},{2,3},{3,2},{4,5},{5,4},{6,7},{7,6},{8,9},{9,8},{10,11... | collective-permute-start | bytes 393224 | tf_op jit(solution)/shard_map/ppermute | solution.py:245
  35.0 2.7 %collective-permute-start.11 = (f32[512,512]{1,0:T(8,128)S(1)}, f32[512,512]{1,0:T(8,128)S(1)}, u32[]{:S(2)}, u32[]{:S(2)}) collective-permute-start(f32[512,512]{1,0:T(8,128)S(1)} %shard_map.51.mine_ref), channel_id=1, source_target_pairs={{0,2},{2,0},{4,6},{6,4},{8,10},{10,8},{12,14},{14,12},{16,18},{18,... | collective-permute-start | bytes 3145736 | tf_op jit(solution)/shard_map/ppermute | solution.py:242
  45.2 5.6 %collective-permute-start.24 = (bf16[128,512]{1,0:T(8,128)(2,1)S(1)}, bf16[128,512]{1,0:T(8,128)(2,1)S(1)}, u32[]{:S(2)}, u32[]{:S(2)}) collective-permute-start(bf16[128,512]{1,0:T(8,128)(2,1)S(1)} %get-tuple-element.21), channel_id=1, source_target_pairs={{0,1},{1,0},{2,3},{3,2},{4,5},{5,4},{6,7},{7,6},{8,9},{9,8},{10,11... | collective-permute-start | bytes 393224 | tf_op jit(solution)/shard_map/ppermute | solution.py:245
  46.3 5.6 %collective-permute-start.12 = (bf16[128,512]{1,0:T(8,128)(2,1)S(1)}, bf16[128,512]{1,0:T(8,128)(2,1)S(1)}, u32[]{:S(2)}, u32[]{:S(2)}) collective-permute-start(bf16[128,512]{1,0:T(8,128)(2,1)S(1)} %get-tuple-element.19), channel_id=1, source_target_pairs={{0,8},{2,6},{8,16},{10,2},{16,24},{18,10},{24,28},{26,18},{28,20},... | collective-permute-start | bytes 393224 | tf_op jit(solution)/shard_map/ppermute | solution.py:311
  46.4 8.6 %collective-permute-start.14 = (bf16[128,512]{1,0:T(8,128)(2,1)S(1)}, bf16[128,512]{1,0:T(8,128)(2,1)S(1)}, u32[]{:S(2)}, u32[]{:S(2)}) collective-permute-start(bf16[128,512]{1,0:T(8,128)(2,1)S(1)} %get-tuple-element.20), channel_id=1, source_target_pairs={{0,8},{2,6},{8,16},{10,2},{16,24},{18,10},{24,28},{26,18},{28,20},... | collective-permute-start | bytes 393224 | tf_op jit(solution)/shard_map/ppermute | solution.py:311
  50.8 5.0 %collective-permute-start.26 = (bf16[128,512]{1,0:T(8,128)(2,1)S(1)}, bf16[128,512]{1,0:T(8,128)(2,1)S(1)}, u32[]{:S(2)}, u32[]{:S(2)}) collective-permute-start(bf16[128,512]{1,0:T(8,128)(2,1)S(1)} %collective-permute-done.24), channel_id=1, source_target_pairs={{0,8},{2,6},{8,16},{10,2},{16,24},{18,10},{24,28},{26,18},{28,20},... | collective-permute-start | bytes 393224 | tf_op jit(solution)/shard_map/ppermute | solution.py:311
  51.9 3.9 %collective-permute-start.25 = (bf16[128,512]{1,0:T(8,128)(2,1)S(1)}, bf16[128,512]{1,0:T(8,128)(2,1)S(1)}, u32[]{:S(2)}, u32[]{:S(2)}) collective-permute-start(bf16[128,512]{1,0:T(8,128)(2,1)S(1)} %collective-permute-done.24), channel_id=1, source_target_pairs={{0,2},{2,0},{4,6},{6,4},{8,10},{10,8},{12,14},{14,12},{16,18},{18,... | collective-permute-start | bytes 393224 | tf_op jit(solution)/shard_map/ppermute | solution.py:242
  51.9 5.9 %collective-permute-start.16 = (bf16[128,512]{1,0:T(8,128)(2,1)S(1)}, bf16[128,512]{1,0:T(8,128)(2,1)S(1)}, u32[]{:S(2)}, u32[]{:S(2)}) collective-permute-start(bf16[128,512]{1,0:T(8,128)(2,1)S(1)} %collective-permute-done.12), channel_id=1, source_target_pairs={{0,8},{2,6},{8,16},{10,2},{16,24},{18,10},{24,28},{26,18},{28,20},... | collective-permute-start | bytes 393224 | tf_op jit(solution)/shard_map/ppermute | solution.py:311
  55.0 2.7 %collective-permute-start.13 = (bf16[128,512]{1,0:T(8,128)(2,1)S(1)}, bf16[128,512]{1,0:T(8,128)(2,1)S(1)}, u32[]{:S(2)}, u32[]{:S(2)}) collective-permute-start(bf16[128,512]{1,0:T(8,128)(2,1)S(1)} %collective-permute-done.12), channel_id=1, source_target_pairs={{0,2},{2,0},{4,6},{6,4},{8,10},{10,8},{12,14},{14,12},{16,18},{18,... | collective-permute-start | bytes 393224 | tf_op jit(solution)/shard_map/ppermute | solution.py:242
  55.0 6.4 %collective-permute-start.18 = (bf16[128,512]{1,0:T(8,128)(2,1)S(1)}, bf16[128,512]{1,0:T(8,128)(2,1)S(1)}, u32[]{:S(2)}, u32[]{:S(2)}) collective-permute-start(bf16[128,512]{1,0:T(8,128)(2,1)S(1)} %collective-permute-done.14), channel_id=1, source_target_pairs={{0,8},{2,6},{8,16},{10,2},{16,24},{18,10},{24,28},{26,18},{28,20},... | collective-permute-start | bytes 393224 | tf_op jit(solution)/shard_map/ppermute | solution.py:311
  55.8 4.4 %collective-permute-start.15 = (bf16[128,512]{1,0:T(8,128)(2,1)S(1)}, bf16[128,512]{1,0:T(8,128)(2,1)S(1)}, u32[]{:S(2)}, u32[]{:S(2)}) collective-permute-start(bf16[128,512]{1,0:T(8,128)(2,1)S(1)} %collective-permute-done.14), channel_id=1, source_target_pairs={{0,2},{2,0},{4,6},{6,4},{8,10},{10,8},{12,14},{14,12},{16,18},{18,... | collective-permute-start | bytes 393224 | tf_op jit(solution)/shard_map/ppermute | solution.py:242
  55.8 6.8 %collective-permute-start.30 = (bf16[128,512]{1,0:T(8,128)(2,1)S(1)}, bf16[128,512]{1,0:T(8,128)(2,1)S(1)}, u32[]{:S(2)}, u32[]{:S(2)}) collective-permute-start(bf16[128,512]{1,0:T(8,128)(2,1)S(1)} %collective-permute-done.26), channel_id=1, source_target_pairs={{0,8},{2,6},{8,16},{10,2},{16,24},{18,10},{24,28},{26,18},{28,20},... | collective-permute-start | bytes 393224 | tf_op jit(solution)/shard_map/ppermute | solution.py:311
  57.7 3.8 %collective-permute-start.27 = (bf16[128,512]{1,0:T(8,128)(2,1)S(1)}, bf16[128,512]{1,0:T(8,128)(2,1)S(1)}, u32[]{:S(2)}, u32[]{:S(2)}) collective-permute-start(bf16[128,512]{1,0:T(8,128)(2,1)S(1)} %collective-permute-done.26), channel_id=1, source_target_pairs={{0,2},{2,0},{4,6},{6,4},{8,10},{10,8},{12,14},{14,12},{16,18},{18,... | collective-permute-start | bytes 393224 | tf_op jit(solution)/shard_map/ppermute | solution.py:242
  57.8 6.1 %collective-permute-start.28 = (bf16[128,512]{1,0:T(8,128)(2,1)S(1)}, bf16[128,512]{1,0:T(8,128)(2,1)S(1)}, u32[]{:S(2)}, u32[]{:S(2)}) collective-permute-start(bf16[128,512]{1,0:T(8,128)(2,1)S(1)} %collective-permute-done.25), channel_id=1, source_target_pairs={{0,8},{2,6},{8,16},{10,2},{16,24},{18,10},{24,28},{26,18},{28,20},... | collective-permute-start | bytes 393224 | tf_op jit(solution)/shard_map/ppermute | solution.py:311
  60.2 5.0 %collective-permute-start.20 = (bf16[128,512]{1,0:T(8,128)(2,1)S(1)}, bf16[128,512]{1,0:T(8,128)(2,1)S(1)}, u32[]{:S(2)}, u32[]{:S(2)}) collective-permute-start(bf16[128,512]{1,0:T(8,128)(2,1)S(1)} %collective-permute-done.16), channel_id=1, source_target_pairs={{0,8},{2,6},{8,16},{10,2},{16,24},{18,10},{24,28},{26,18},{28,20},... | collective-permute-start | bytes 393224 | tf_op jit(solution)/shard_map/ppermute | solution.py:311
  61.4 1.4 %collective-permute-start.17 = (bf16[128,512]{1,0:T(8,128)(2,1)S(1)}, bf16[128,512]{1,0:T(8,128)(2,1)S(1)}, u32[]{:S(2)}, u32[]{:S(2)}) collective-permute-start(bf16[128,512]{1,0:T(8,128)(2,1)S(1)} %collective-permute-done.16), channel_id=1, source_target_pairs={{0,2},{2,0},{4,6},{6,4},{8,10},{10,8},{12,14},{14,12},{16,18},{18,... | collective-permute-start | bytes 393224 | tf_op jit(solution)/shard_map/ppermute | solution.py:242
  61.5 6.3 %collective-permute-start.22 = (bf16[128,512]{1,0:T(8,128)(2,1)S(1)}, bf16[128,512]{1,0:T(8,128)(2,1)S(1)}, u32[]{:S(2)}, u32[]{:S(2)}) collective-permute-start(bf16[128,512]{1,0:T(8,128)(2,1)S(1)} %collective-permute-done.18), channel_id=1, source_target_pairs={{0,8},{2,6},{8,16},{10,2},{16,24},{18,10},{24,28},{26,18},{28,20},... | collective-permute-start | bytes 393224 | tf_op jit(solution)/shard_map/ppermute | solution.py:311
  62.7 1.4 %collective-permute-start.19 = (bf16[128,512]{1,0:T(8,128)(2,1)S(1)}, bf16[128,512]{1,0:T(8,128)(2,1)S(1)}, u32[]{:S(2)}, u32[]{:S(2)}) collective-permute-start(bf16[128,512]{1,0:T(8,128)(2,1)S(1)} %collective-permute-done.18), channel_id=1, source_target_pairs={{0,2},{2,0},{4,6},{6,4},{8,10},{10,8},{12,14},{14,12},{16,18},{18,... | collective-permute-start | bytes 393224 | tf_op jit(solution)/shard_map/ppermute | solution.py:242
  62.8 5.1 %collective-permute-start.34 = (bf16[128,512]{1,0:T(8,128)(2,1)S(1)}, bf16[128,512]{1,0:T(8,128)(2,1)S(1)}, u32[]{:S(2)}, u32[]{:S(2)}) collective-permute-start(bf16[128,512]{1,0:T(8,128)(2,1)S(1)} %collective-permute-done.30), channel_id=1, source_target_pairs={{0,8},{2,6},{8,16},{10,2},{16,24},{18,10},{24,28},{26,18},{28,20},... | collective-permute-start | bytes 393224 | tf_op jit(solution)/shard_map/ppermute | solution.py:311
  63.9 4.4 %collective-permute-start.31 = (bf16[128,512]{1,0:T(8,128)(2,1)S(1)}, bf16[128,512]{1,0:T(8,128)(2,1)S(1)}, u32[]{:S(2)}, u32[]{:S(2)}) collective-permute-start(bf16[128,512]{1,0:T(8,128)(2,1)S(1)} %collective-permute-done.30), channel_id=1, source_target_pairs={{0,2},{2,0},{4,6},{6,4},{8,10},{10,8},{12,14},{14,12},{16,18},{18,... | collective-permute-start | bytes 393224 | tf_op jit(solution)/shard_map/ppermute | solution.py:242
  64.1 2.5 %collective-permute-start.29 = (bf16[128,512]{1,0:T(8,128)(2,1)S(1)}, bf16[128,512]{1,0:T(8,128)(2,1)S(1)}, u32[]{:S(2)}, u32[]{:S(2)}) collective-permute-start(bf16[128,512]{1,0:T(8,128)(2,1)S(1)} %collective-permute-done.28), channel_id=1, source_target_pairs={{0,2},{2,0},{4,6},{6,4},{8,10},{10,8},{12,14},{14,12},{16,18},{18,... | collective-permute-start | bytes 393224 | tf_op jit(solution)/shard_map/ppermute | solution.py:242
  65.1 5.0 %collective-permute-start.32 = (bf16[128,512]{1,0:T(8,128)(2,1)S(1)}, bf16[128,512]{1,0:T(8,128)(2,1)S(1)}, u32[]{:S(2)}, u32[]{:S(2)}) collective-permute-start(bf16[128,512]{1,0:T(8,128)(2,1)S(1)} %collective-permute-done.28), channel_id=1, source_target_pairs={{0,8},{2,6},{8,16},{10,2},{16,24},{18,10},{24,28},{26,18},{28,20},... | collective-permute-start | bytes 393224 | tf_op jit(solution)/shard_map/ppermute | solution.py:311
  66.6 5.0 %collective-permute-start.38 = (bf16[128,512]{1,0:T(8,128)(2,1)S(1)}, bf16[128,512]{1,0:T(8,128)(2,1)S(1)}, u32[]{:S(2)}, u32[]{:S(2)}) collective-permute-start(bf16[128,512]{1,0:T(8,128)(2,1)S(1)} %collective-permute-done.20), channel_id=1, source_target_pairs={{0,8},{2,6},{8,16},{10,2},{16,24},{18,10},{24,28},{26,18},{28,20},... | collective-permute-start | bytes 393224 | tf_op jit(solution)/shard_map/ppermute | solution.py:311
  67.8 2.3 %collective-permute-start.21 = (bf16[128,512]{1,0:T(8,128)(2,1)S(1)}, bf16[128,512]{1,0:T(8,128)(2,1)S(1)}, u32[]{:S(2)}, u32[]{:S(2)}) collective-permute-start(bf16[128,512]{1,0:T(8,128)(2,1)S(1)} %collective-permute-done.20), channel_id=1, source_target_pairs={{0,2},{2,0},{4,6},{6,4},{8,10},{10,8},{12,14},{14,12},{16,18},{18,... | collective-permute-start | bytes 393224 | tf_op jit(solution)/shard_map/ppermute | solution.py:242
  68.0 3.7 %collective-permute-start.23 = (bf16[128,512]{1,0:T(8,128)(2,1)S(1)}, bf16[128,512]{1,0:T(8,128)(2,1)S(1)}, u32[]{:S(2)}, u32[]{:S(2)}) collective-permute-start(bf16[128,512]{1,0:T(8,128)(2,1)S(1)} %collective-permute-done.22), channel_id=1, source_target_pairs={{0,2},{2,0},{4,6},{6,4},{8,10},{10,8},{12,14},{14,12},{16,18},{18,... | collective-permute-start | bytes 393224 | tf_op jit(solution)/shard_map/ppermute | solution.py:242
  68.4 5.0 %collective-permute-start.40 = (bf16[128,512]{1,0:T(8,128)(2,1)S(1)}, bf16[128,512]{1,0:T(8,128)(2,1)S(1)}, u32[]{:S(2)}, u32[]{:S(2)}) collective-permute-start(bf16[128,512]{1,0:T(8,128)(2,1)S(1)} %collective-permute-done.34), channel_id=1, source_target_pairs={{0,8},{2,6},{8,16},{10,2},{16,24},{18,10},{24,28},{26,18},{28,20},... | collective-permute-start | bytes 393224 | tf_op jit(solution)/shard_map/ppermute | solution.py:311
  70.1 5.0 %collective-permute-start.35 = (bf16[128,512]{1,0:T(8,128)(2,1)S(1)}, bf16[128,512]{1,0:T(8,128)(2,1)S(1)}, u32[]{:S(2)}, u32[]{:S(2)}) collective-permute-start(bf16[128,512]{1,0:T(8,128)(2,1)S(1)} %collective-permute-done.34), channel_id=1, source_target_pairs={{0,2},{2,0},{4,6},{6,4},{8,10},{10,8},{12,14},{14,12},{16,18},{18,... | collective-permute-start | bytes 393224 | tf_op jit(solution)/shard_map/ppermute | solution.py:242
  70.1 5.0 %collective-permute-start.36 = (bf16[128,512]{1,0:T(8,128)(2,1)S(1)}, bf16[128,512]{1,0:T(8,128)(2,1)S(1)}, u32[]{:S(2)}, u32[]{:S(2)}) collective-permute-start(bf16[128,512]{1,0:T(8,128)(2,1)S(1)} %collective-permute-done.32), channel_id=1, source_target_pairs={{0,8},{2,6},{8,16},{10,2},{16,24},{18,10},{24,28},{26,18},{28,20},... | collective-permute-start | bytes 393224 | tf_op jit(solution)/shard_map/ppermute | solution.py:311
  71.6 3.5 %collective-permute-start.33 = (bf16[128,512]{1,0:T(8,128)(2,1)S(1)}, bf16[128,512]{1,0:T(8,128)(2,1)S(1)}, u32[]{:S(2)}, u32[]{:S(2)}) collective-permute-start(bf16[128,512]{1,0:T(8,128)(2,1)S(1)} %collective-permute-done.32), channel_id=1, source_target_pairs={{0,2},{2,0},{4,6},{6,4},{8,10},{10,8},{12,14},{14,12},{16,18},{18,... | collective-permute-start | bytes 393224 | tf_op jit(solution)/shard_map/ppermute | solution.py:242
  71.7 3.5 %collective-permute-start.39 = (bf16[128,512]{1,0:T(8,128)(2,1)S(1)}, bf16[128,512]{1,0:T(8,128)(2,1)S(1)}, u32[]{:S(2)}, u32[]{:S(2)}) collective-permute-start(bf16[128,512]{1,0:T(8,128)(2,1)S(1)} %collective-permute-done.38), channel_id=1, source_target_pairs={{0,2},{2,0},{4,6},{6,4},{8,10},{10,8},{12,14},{14,12},{16,18},{18,... | collective-permute-start | bytes 393224 | tf_op jit(solution)/shard_map/ppermute | solution.py:242
  73.3 4.4 %collective-permute-start.41 = (bf16[128,512]{1,0:T(8,128)(2,1)S(1)}, bf16[128,512]{1,0:T(8,128)(2,1)S(1)}, u32[]{:S(2)}, u32[]{:S(2)}) collective-permute-start(bf16[128,512]{1,0:T(8,128)(2,1)S(1)} %collective-permute-done.40), channel_id=1, source_target_pairs={{0,2},{2,0},{4,6},{6,4},{8,10},{10,8},{12,14},{14,12},{16,18},{18,... | collective-permute-start | bytes 393224 | tf_op jit(solution)/shard_map/ppermute | solution.py:242
  75.1 1.3 %collective-permute-start.37 = (bf16[128,512]{1,0:T(8,128)(2,1)S(1)}, bf16[128,512]{1,0:T(8,128)(2,1)S(1)}, u32[]{:S(2)}, u32[]{:S(2)}) collective-permute-start(bf16[128,512]{1,0:T(8,128)(2,1)S(1)} %collective-permute-done.36), channel_id=1, source_target_pairs={{0,2},{2,0},{4,6},{6,4},{8,10},{10,8},{12,14},{14,12},{16,18},{18,... | collective-permute-start | bytes 393224 | tf_op jit(solution)/shard_map/ppermute | solution.py:242
  78.0 2.0 %copy-start.1 = (bf16[8,256,1024]{2,1,0:T(8,128)(2,1)}, bf16[8,256,1024]{2,1,0:T(8,128)(2,1)S(1)}, u32[]{:S(2)}) copy-start(bf16[8,256,1024]{2,1,0:T(8,128)(2,1)S(1)} %fusion) | copy-start | bytes 12582916

commit v11 on v7

--- a/solution.py
+++ b/solution.py
@@ -142,7 +142,7 @@
     stats = [contract(tile_half, tile_half, 1, 1), contract(tile_half, tile_half, 0, 0)]
     stats = [jnp.where(on_diagonal, stat + damp, stat) for stat in stats]
     norms = [jnp.sqrt(total(stat * stat)) for stat in stats]
-    firsts = [stat / norm for stat, norm in zip(stats, norms)]
+    firsts = [stat * (1.0 / norm) for stat, norm in zip(stats, norms)]
     seconds = newton_step(firsts)
     thirds = newton_step(seconds)
     crosses = [
@@ -152,7 +152,8 @@
     for cross, third, norm in zip(crosses, thirds, norms):
         root = 1.25 * cross - 0.25 * product(cross, third) - (25.0 / 64.0) * third
         root = jnp.where(on_diagonal, root + 125.0 / 64.0, root)
-        roots.append((root / jnp.sqrt(jnp.sqrt(norm))).astype(jnp.bfloat16))
+        scale = 1.0 / jnp.sqrt(jnp.sqrt(norm))
+        roots.append((root * scale).astype(jnp.bfloat16))
     return roots
 
 
@@ -312,7 +313,7 @@
 
     half_way = bands // 2
     crossed = swap_plane(far_piece)
-    heads = [near_piece, next_piece, crossed, swap_core(crossed)]
+    heads = [crossed, swap_core(crossed), near_piece, next_piece]
     columns = [jnp.zeros((bands, cores, rows, BLOCK), jnp.bfloat16)] * 2
 
     def put(chunk, piece, position, half):
@@ -329,7 +330,7 @@
                 heads[k] = head = turn(head)
                 put(chunk, swap_core(head), spot + ahead * hop, 1 - half)
             put(chunk, head, spot - ahead * hop, half)
-    former, latter = (column.reshape(bands, cores * rows, BLOCK) for column in columns)
+    latter, former = (column.reshape(bands, cores * rows, BLOCK) for column in columns)
     update = jnp.where(
         plane == 0,
         jnp.concatenate([former, latter], axis=-1),

time: 79.4 us -> 79.4 us (level)
  no operation moved by 1% of the time
where the time goes in v11:
time: 79.4 us; the launch traced here: 79.2 us
  starting transfers between devices  42.5 us (54%)
  waiting for transfers between devices  17.3 us (22%)
  Pallas kernels  9.42 us (12%)
  matrix products  3.6 us (5%)
  other arithmetic  2.81 us (4%)
  local copies, waits for them, and re-layouts  2.23 us (3%)
  between operations  1.36 us (2%)
    ppermute x14, starting transfers between devices, turn(): return lax.ppermute(array, 'dp', pairs)  20.4 us
    pallas_call x3, Pallas kernels, call(): pl.pallas_call(kernel, out_shape=out_shapes, in_specs=in_specs, out_specs...  9.42 us
    ppermute x5, starting transfers between devices, exchange(): return lax.ppermute(array, 'dp', pairs)  9.35 us
    ppermute x4, starting transfers between devices, swap_plane(): lax.ppermute(array, 'pre', [(c, members - 1 - c) for c in range(members)])  6.98 us
    ppermute x4, waiting for transfers between devices, swap_plane(): lax.ppermute(array, 'pre', [(c, members - 1 - c) for c in range(members)])  6.21 us
    ppermute x14, waiting for transfers between devices, turn(): return lax.ppermute(array, 'dp', pairs)  4.28 us
    ppermute x3, starting transfers between devices, deal(): return lax.ppermute(array, ('dp', 'pre'), pairs)  3.88 us
    ppermute x16, waiting for transfers between devices, swap_core(): return lax.ppermute(array, 'dp', [(g, g ^ 1) for g in range(groups)])  3.65 us
  transfers between devices with their start and end apart: 42, of which 15 were waited for; matrix products, arithmetic and copies ran while one was open for 6% of the time, Pallas kernels for 1%

profile of v11, /device:TPU:0, one launch (start us, length us, event | category | flops | bytes accessed | tf_op | source)
XLA Modules:
  0.0 79.2 jit_solution(15464267436403794582)
XLA Ops:
  0.6 4.1 %collective-permute-start = (bf16[128,512]{1,0:T(8,128)(2,1)}, bf16[128,512]{1,0:T(8,128)(2,1)S(1)}, u32[]{:S(2)}, u32[]{:S(2)}) collective-permute-start(bf16[128,512]{1,0:T(8,128)(2,1)} %param.5), channel_id=1, source_target_pairs={{0,16},{2,18},{4,20},{6,22},{8,24},{10,26},{12,28},{14,30},{16,0},... | collective-permute-start | bytes 393224 | tf_op jit(solution)/shard_map/ppermute | solution.py:274
  4.8 1.2 %copy-done = bf16[128,4096]{1,0:T(8,128)(2,1)S(1)} copy-done((bf16[128,4096]{1,0:T(8,128)(2,1)S(1)}, bf16[128,4096]{1,0:T(8,128)(2,1)}, u32[]{:S(2)}) %copy-start) | copy-done | bytes 1048600
  6.0 0.6 shard_map.50
  6.6 1.6 %collective-permute-start.1 = (bf16[128,512]{1,0:T(8,128)(2,1)S(1)}, bf16[128,512]{1,0:T(8,128)(2,1)S(1)}, u32[]{:S(2)}, u32[]{:S(2)}) collective-permute-start(bf16[128,512]{1,0:T(8,128)(2,1)S(1)} %get-tuple-element.14), channel_id=1, source_target_pairs={{0,4},{2,6},{4,0},{6,2},{8,12},{10,14},{12,8},{14,10},{16,20},{18,... | collective-permute-start | bytes 393224 | tf_op jit(solution)/shard_map/ppermute | solution.py:274
  8.2 0.3 collective-permute-start.2
  8.6 3.5 %collective-permute-start.3 = (bf16[128,512]{1,0:T(8,128)(2,1)S(1)}, bf16[128,512]{1,0:T(8,128)(2,1)S(1)}, u32[]{:S(2)}, u32[]{:S(2)}) collective-permute-start(bf16[128,512]{1,0:T(8,128)(2,1)S(1)} %get-tuple-element.16), channel_id=1, source_target_pairs={{0,28},{1,25},{2,30},{3,27},{4,24},{5,29},{6,26},{7,31},{8,20},{9,... | collective-permute-start | bytes 393224 | tf_op jit(solution)/shard_map/ppermute | solution.py:258
  12.1 3.6 %convolution_convert_fusion = bf16[128,512]{1,0:T(8,128)(2,1)} fusion(bf16[128,4096]{1,0:T(8,128)(2,1)S(1)} %copy-done, bf16[4096,512]{1,0:T(8,128)(2,1)} %param.4), kind=kOutput, calls=%fused_computation.1 | convolution fusion | flops 536936448 | bytes 5373952 | tf_op jit(solution)/shard_map/dot_general | solution.py:276
  15.8 3.0 %collective-permute-start.10 = (bf16[256,512]{1,0:T(8,128)(2,1)S(1)}, bf16[256,512]{1,0:T(8,128)(2,1)S(1)}, u32[]{:S(2)}, u32[]{:S(2)}) collective-permute-start(bf16[256,512]{1,0:T(8,128)(2,1)S(1)} %constant_dynamic-update-slice_fusion.refs_6_), channel_id=1, source_target_pairs={{0,12},{2,14},{4,8},{6,10},{8,4},{10,6},{12,0},{14,2},{16,28},{18,... | collective-permute-start | bytes 786440 | tf_op jit(solution)/shard_map/ppermute | solution.py:274
  18.8 1.8 %collective-permute-done.2.refs_0_ = bf16[128,512]{1,0:T(8,128)(2,1)S(1)} collective-permute-done((bf16[128,512]{1,0:T(8,128)(2,1)S(1)}, bf16[128,512]{1,0:T(8,128)(2,1)S(1)}, u32[]{:S(2)}, u32[]{:S(2)}) %collective-permute-start.2) | collective-permute-done | bytes 131104 | tf_op jit(solution)/shard_map/ppermute | solution.py:258
  20.6 2.4 %collective-permute-start.5 = (bf16[128,512]{1,0:T(8,128)(2,1)S(1)}, bf16[128,512]{1,0:T(8,128)(2,1)S(1)}, u32[]{:S(2)}, u32[]{:S(2)}) collective-permute-start(bf16[128,512]{1,0:T(8,128)(2,1)S(1)} %collective-permute-done.2.refs_0_), channel_id=1, source_target_pairs={{0,1},{1,0},{2,3},{3,2},{4,5},{5,4},{6,7},{7,6},{8,9},{9,8},{10,11... | collective-permute-start | bytes 393224 | tf_op jit(solution)/shard_map/ppermute | solution.py:246
  23.0 0.6 collective-permute-start.8
  23.6 1.0 %collective-permute-start.6 = (bf16[128,512]{1,0:T(8,128)(2,1)S(1)}, bf16[128,512]{1,0:T(8,128)(2,1)S(1)}, u32[]{:S(2)}, u32[]{:S(2)}) collective-permute-start(bf16[128,512]{1,0:T(8,128)(2,1)S(1)} %collective-permute-done.3.refs_1_), channel_id=1, source_target_pairs={{0,1},{1,0},{2,3},{3,2},{4,5},{5,4},{6,7},{7,6},{8,9},{9,8},{10,11... | collective-permute-start | bytes 393224 | tf_op jit(solution)/shard_map/ppermute | solution.py:246
  24.6 2.3 %collective-permute-done.5.refs_3_ = bf16[128,512]{1,0:T(8,128)(2,1)S(1)} collective-permute-done((bf16[128,512]{1,0:T(8,128)(2,1)S(1)}, bf16[128,512]{1,0:T(8,128)(2,1)S(1)}, u32[]{:S(2)}, u32[]{:S(2)}) %collective-permute-start.5) | collective-permute-done | bytes 131104 | tf_op jit(solution)/shard_map/ppermute | solution.py:246
  26.8 2.5 %collective-permute-start.7 = (bf16[128,512]{1,0:T(8,128)(2,1)S(1)}, bf16[128,512]{1,0:T(8,128)(2,1)S(1)}, u32[]{:S(2)}, u32[]{:S(2)}) collective-permute-start(bf16[128,512]{1,0:T(8,128)(2,1)S(1)} %collective-permute-done.4.refs_2_), channel_id=1, source_target_pairs={{0,1},{1,0},{2,3},{3,2},{4,5},{5,4},{6,7},{7,6},{8,9},{9,8},{10,11... | collective-permute-start | bytes 393224 | tf_op jit(solution)/shard_map/ppermute | solution.py:246
  29.4 0.6 collective-permute-done.6.refs_4_
  30.0 2.2 %collective-permute-done.7.refs_5_ = bf16[128,512]{1,0:T(8,128)(2,1)S(1)} collective-permute-done((bf16[128,512]{1,0:T(8,128)(2,1)S(1)}, bf16[128,512]{1,0:T(8,128)(2,1)S(1)}, u32[]{:S(2)}, u32[]{:S(2)}) %collective-permute-start.7) | collective-permute-done | bytes 131104 | tf_op jit(solution)/shard_map/ppermute | solution.py:246
  32.3 1.4 %collective-permute-done.8.refs_7_ = bf16[256,512]{1,0:T(8,128)(2,1)S(1)} collective-permute-done((bf16[256,512]{1,0:T(8,128)(2,1)S(1)}, bf16[256,512]{1,0:T(8,128)(2,1)S(1)}, u32[]{:S(2)}, u32[]{:S(2)}) %collective-permute-start.8) | collective-permute-done | bytes 262176 | tf_op jit(solution)/shard_map/ppermute | solution.py:274
  33.6 1.4 %shard_map.51.mine_ref = f32[512,512]{1,0:T(8,128)S(1)} custom-call(s32[2]{0:T(128)S(1)} %pad_add_fusion.1.place_ref, bf16[128,512]{1,0:T(8,128)(2,1)S(1)} %get-tuple-element.13.own_ref, bf16[128,512]{1,0:T(8,128)(2,1)S(1)} %collective-permute-done.1.shared_ref, bf16[128,512]{1,0:T(8,128)(2,1)S(1)} %collective-permute-done.2.refs_0_, ...), custom_call_target="tpu_custom_call" | custom-call | tf_op jit(solution)/shard_map/pallas_call | solution.py:218
  35.5 2.3 %collective-permute-done.11.other_ref = f32[512,512]{1,0:T(8,128)S(1)} collective-permute-done((f32[512,512]{1,0:T(8,128)S(1)}, f32[512,512]{1,0:T(8,128)S(1)}, u32[]{:S(2)}, u32[]{:S(2)}) %collective-permute-start.11) | collective-permute-done | bytes 1048608 | tf_op jit(solution)/shard_map/ppermute | solution.py:243
  37.8 7.4 %shard_map.52 = (bf16[128,512]{1,0:T(8,128)(2,1)S(1)}, bf16[128,512]{1,0:T(8,128)(2,1)S(1)}, bf16[128,512]{1,0:T(8,128)(2,1)S(1)}) custom-call(s32[2]{0:T(128)S(1)} %pad_add_fusion.side_ref, f32[512,512]{1,0:T(8,128)S(1)} %shard_map.51.mine_ref, f32[512,512]{1,0:T(8,128)S(1)} %collective-permute-done.11.other_ref), custom_call_target="tpu_custom_call" | custom-call | tf_op jit(solution)/shard_map/pallas_call | solution.py:218
  45.2 1.1 %collective-permute-start.26 = (bf16[128,512]{1,0:T(8,128)(2,1)S(1)}, bf16[128,512]{1,0:T(8,128)(2,1)S(1)}, u32[]{:S(2)}, u32[]{:S(2)}) collective-permute-start(bf16[128,512]{1,0:T(8,128)(2,1)S(1)} %get-tuple-element.21), channel_id=1, source_target_pairs={{0,1},{1,0},{2,3},{3,2},{4,5},{5,4},{6,7},{7,6},{8,9},{9,8},{10,11... | collective-permute-start | bytes 393224 | tf_op jit(solution)/shard_map/ppermute | solution.py:246
  46.4 3.1 %collective-permute-start.14 = (bf16[128,512]{1,0:T(8,128)(2,1)S(1)}, bf16[128,512]{1,0:T(8,128)(2,1)S(1)}, u32[]{:S(2)}, u32[]{:S(2)}) collective-permute-start(bf16[128,512]{1,0:T(8,128)(2,1)S(1)} %get-tuple-element.20), channel_id=1, source_target_pairs={{0,8},{2,6},{8,16},{10,2},{16,24},{18,10},{24,28},{26,18},{28,20},... | collective-permute-start | bytes 393224 | tf_op jit(solution)/shard_map/ppermute | solution.py:312
  49.5 0.2 broadcast_in_dim.99.clone.1
  49.7 1.1 %collective-permute-done.26 = bf16[128,512]{1,0:T(8,128)(2,1)S(1)} collective-permute-done((bf16[128,512]{1,0:T(8,128)(2,1)S(1)}, bf16[128,512]{1,0:T(8,128)(2,1)S(1)}, u32[]{:S(2)}, u32[]{:S(2)}) %collective-permute-start.26) | collective-permute-done | bytes 131104 | tf_op jit(solution)/shard_map/ppermute | solution.py:246
  50.8 1.1 %collective-permute-start.28 = (bf16[128,512]{1,0:T(8,128)(2,1)S(1)}, bf16[128,512]{1,0:T(8,128)(2,1)S(1)}, u32[]{:S(2)}, u32[]{:S(2)}) collective-permute-start(bf16[128,512]{1,0:T(8,128)(2,1)S(1)} %collective-permute-done.26), channel_id=1, source_target_pairs={{0,8},{2,6},{8,16},{10,2},{16,24},{18,10},{24,28},{26,18},{28,20},... | collective-permute-start | bytes 393224 | tf_op jit(solution)/shard_map/ppermute | solution.py:312
  51.9 3.1 %collective-permute-start.16 = (bf16[128,512]{1,0:T(8,128)(2,1)S(1)}, bf16[128,512]{1,0:T(8,128)(2,1)S(1)}, u32[]{:S(2)}, u32[]{:S(2)}) collective-permute-start(bf16[128,512]{1,0:T(8,128)(2,1)S(1)} %collective-permute-done.12), channel_id=1, source_target_pairs={{0,8},{2,6},{8,16},{10,2},{16,24},{18,10},{24,28},{26,18},{28,20},... | collective-permute-start | bytes 393224 | tf_op jit(solution)/shard_map/ppermute | solution.py:312
  55.0 0.5 collective-permute-start.18
  55.5 0.2 broadcast_in_dim.99.clone
  55.8 1.8 %collective-permute-start.32 = (bf16[128,512]{1,0:T(8,128)(2,1)S(1)}, bf16[128,512]{1,0:T(8,128)(2,1)S(1)}, u32[]{:S(2)}, u32[]{:S(2)}) collective-permute-start(bf16[128,512]{1,0:T(8,128)(2,1)S(1)} %collective-permute-done.28), channel_id=1, source_target_pairs={{0,8},{2,6},{8,16},{10,2},{16,24},{18,10},{24,28},{26,18},{28,20},... | collective-permute-start | bytes 393224 | tf_op jit(solution)/shard_map/ppermute | solution.py:312
  57.8 2.4 %collective-permute-start.30 = (bf16[128,512]{1,0:T(8,128)(2,1)S(1)}, bf16[128,512]{1,0:T(8,128)(2,1)S(1)}, u32[]{:S(2)}, u32[]{:S(2)}) collective-permute-start(bf16[128,512]{1,0:T(8,128)(2,1)S(1)} %collective-permute-done.27), channel_id=1, source_target_pairs={{0,8},{2,6},{8,16},{10,2},{16,24},{18,10},{24,28},{26,18},{28,20},... | collective-permute-start | bytes 393224 | tf_op jit(solution)/shard_map/ppermute | solution.py:312
  60.2 1.2 %collective-permute-start.20 = (bf16[128,512]{1,0:T(8,128)(2,1)S(1)}, bf16[128,512]{1,0:T(8,128)(2,1)S(1)}, u32[]{:S(2)}, u32[]{:S(2)}) collective-permute-start(bf16[128,512]{1,0:T(8,128)(2,1)S(1)} %collective-permute-done.16), channel_id=1, source_target_pairs={{0,8},{2,6},{8,16},{10,2},{16,24},{18,10},{24,28},{26,18},{28,20},... | collective-permute-start | bytes 393224 | tf_op jit(solution)/shard_map/ppermute | solution.py:312
  61.5 1.1 %collective-permute-start.22 = (bf16[128,512]{1,0:T(8,128)(2,1)S(1)}, bf16[128,512]{1,0:T(8,128)(2,1)S(1)}, u32[]{:S(2)}, u32[]{:S(2)}) collective-permute-start(bf16[128,512]{1,0:T(8,128)(2,1)S(1)} %collective-permute-done.18), channel_id=1, source_target_pairs={{0,8},{2,6},{8,16},{10,2},{16,24},{18,10},{24,28},{26,18},{28,20},... | collective-permute-start | bytes 393224 | tf_op jit(solution)/shard_map/ppermute | solution.py:312
  62.8 1.1 %collective-permute-start.36 = (bf16[128,512]{1,0:T(8,128)(2,1)S(1)}, bf16[128,512]{1,0:T(8,128)(2,1)S(1)}, u32[]{:S(2)}, u32[]{:S(2)}) collective-permute-start(bf16[128,512]{1,0:T(8,128)(2,1)S(1)} %collective-permute-done.32), channel_id=1, source_target_pairs={{0,8},{2,6},{8,16},{10,2},{16,24},{18,10},{24,28},{26,18},{28,20},... | collective-permute-start | bytes 393224 | tf_op jit(solution)/shard_map/ppermute | solution.py:312
  63.9 0.1 collective-permute-start.33
  64.1 0.5 collective-permute-start.31
  64.6 0.6 collective-permute-done.20
  65.1 1.4 %collective-permute-start.34 = (bf16[128,512]{1,0:T(8,128)(2,1)S(1)}, bf16[128,512]{1,0:T(8,128)(2,1)S(1)}, u32[]{:S(2)}, u32[]{:S(2)}) collective-permute-start(bf16[128,512]{1,0:T(8,128)(2,1)S(1)} %collective-permute-done.30), channel_id=1, source_target_pairs={{0,8},{2,6},{8,16},{10,2},{16,24},{18,10},{24,28},{26,18},{28,20},... | collective-permute-start | bytes 393224 | tf_op jit(solution)/shard_map/ppermute | solution.py:312
  66.6 1.2 %collective-permute-start.24 = (bf16[128,512]{1,0:T(8,128)(2,1)S(1)}, bf16[128,512]{1,0:T(8,128)(2,1)S(1)}, u32[]{:S(2)}, u32[]{:S(2)}) collective-permute-start(bf16[128,512]{1,0:T(8,128)(2,1)S(1)} %collective-permute-done.20), channel_id=1, source_target_pairs={{0,8},{2,6},{8,16},{10,2},{16,24},{18,10},{24,28},{26,18},{28,20},... | collective-permute-start | bytes 393224 | tf_op jit(solution)/shard_map/ppermute | solution.py:312
  67.9 0.1 collective-permute-done.36
  68.0 0.4 collective-permute-start.23
  68.4 1.0 %collective-permute-start.40 = (bf16[128,512]{1,0:T(8,128)(2,1)S(1)}, bf16[128,512]{1,0:T(8,128)(2,1)S(1)}, u32[]{:S(2)}, u32[]{:S(2)}) collective-permute-start(bf16[128,512]{1,0:T(8,128)(2,1)S(1)} %collective-permute-done.36), channel_id=1, source_target_pairs={{0,8},{2,6},{8,16},{10,2},{16,24},{18,10},{24,28},{26,18},{28,20},... | collective-permute-start | bytes 393224 | tf_op jit(solution)/shard_map/ppermute | solution.py:312
  69.5 0.7 collective-permute-done.34
  70.1 1.4 %collective-permute-start.38 = (bf16[128,512]{1,0:T(8,128)(2,1)S(1)}, bf16[128,512]{1,0:T(8,128)(2,1)S(1)}, u32[]{:S(2)}, u32[]{:S(2)}) collective-permute-start(bf16[128,512]{1,0:T(8,128)(2,1)S(1)} %collective-permute-done.34), channel_id=1, source_target_pairs={{0,8},{2,6},{8,16},{10,2},{16,24},{18,10},{24,28},{26,18},{28,20},... | collective-permute-start | bytes 393224 | tf_op jit(solution)/shard_map/ppermute | solution.py:312
  71.7 0.5 collective-permute-start.25
  72.2 1.1 %collective-permute-done.40 = bf16[128,512]{1,0:T(8,128)(2,1)S(1)} collective-permute-done((bf16[128,512]{1,0:T(8,128)(2,1)S(1)}, bf16[128,512]{1,0:T(8,128)(2,1)S(1)}, u32[]{:S(2)}, u32[]{:S(2)}) %collective-permute-start.40) | collective-permute-done | bytes 131104 | tf_op jit(solution)/shard_map/ppermute | solution.py:312
  73.3 1.7 %collective-permute-done.38 = bf16[128,512]{1,0:T(8,128)(2,1)S(1)} collective-permute-done((bf16[128,512]{1,0:T(8,128)(2,1)S(1)}, bf16[128,512]{1,0:T(8,128)(2,1)S(1)}, u32[]{:S(2)}, u32[]{:S(2)}) %collective-permute-start.38) | collective-permute-done | bytes 131104 | tf_op jit(solution)/shard_map/ppermute | solution.py:312
  75.2 1.2 %collective-permute-done.39 = bf16[128,512]{1,0:T(8,128)(2,1)S(1)} collective-permute-done((bf16[128,512]{1,0:T(8,128)(2,1)S(1)}, bf16[128,512]{1,0:T(8,128)(2,1)S(1)}, u32[]{:S(2)}, u32[]{:S(2)}) %collective-permute-start.39) | collective-permute-done | bytes 131104 | tf_op jit(solution)/shard_map/ppermute | solution.py:243
  76.6 2.7 %maximum_select_fusion = bf16[8,256,1024]{2,1,0:T(8,128)(2,1)} fusion(bf16[8,256,512]{2,1,0:T(8,128)(2,1)S(1)} %bitcast.75, bf16[8,256,512]{2,1,0:T(8,128)(2,1)S(1)} %bitcast.76, pred[]{:T(512)S(6)} %eq.44), kind=kLoop, calls=%fused_computation | loop fusion | flops 18874368 | bytes 8388609 | tf_op jit(solution)/shard_map/jit(_where)/select_n | solution.py:334
  (83 shorter events, 1.5 us)
Async XLA Ops:
  0.6 15.1 %collective-permute-start = (bf16[128,512]{1,0:T(8,128)(2,1)}, bf16[128,512]{1,0:T(8,128)(2,1)S(1)}, u32[]{:S(2)}, u32[]{:S(2)}) collective-permute-start(bf16[128,512]{1,0:T(8,128)(2,1)} %param.5), channel_id=1, source_target_pairs={{0,16},{2,18},{4,20},{6,22},{8,24},{10,26},{12,28},{14,30},{16,0},... | collective-permute-start | bytes 393224 | tf_op jit(solution)/shard_map/ppermute | solution.py:274
  4.8 1.2 %copy-start = (bf16[128,4096]{1,0:T(8,128)(2,1)S(1)}, bf16[128,4096]{1,0:T(8,128)(2,1)}, u32[]{:S(2)}) copy-start(bf16[128,4096]{1,0:T(8,128)(2,1)} %inputs_ref.1) | copy-start | bytes 3145732
  6.6 16.4 %collective-permute-start.1 = (bf16[128,512]{1,0:T(8,128)(2,1)S(1)}, bf16[128,512]{1,0:T(8,128)(2,1)S(1)}, u32[]{:S(2)}, u32[]{:S(2)}) collective-permute-start(bf16[128,512]{1,0:T(8,128)(2,1)S(1)} %get-tuple-element.14), channel_id=1, source_target_pairs={{0,4},{2,6},{4,0},{6,2},{8,12},{10,14},{12,8},{14,10},{16,20},{18,... | collective-permute-start | bytes 393224 | tf_op jit(solution)/shard_map/ppermute | solution.py:274
  8.2 12.4 %collective-permute-start.2 = (bf16[128,512]{1,0:T(8,128)(2,1)S(1)}, bf16[128,512]{1,0:T(8,128)(2,1)S(1)}, u32[]{:S(2)}, u32[]{:S(2)}) collective-permute-start(bf16[128,512]{1,0:T(8,128)(2,1)S(1)} %get-tuple-element.15), channel_id=1, source_target_pairs={{0,16},{1,21},{2,18},{3,23},{4,20},{5,17},{6,22},{7,19},{8,24},{9,... | collective-permute-start | bytes 393224 | tf_op jit(solution)/shard_map/ppermute | solution.py:258
  8.6 14.4 %collective-permute-start.3 = (bf16[128,512]{1,0:T(8,128)(2,1)S(1)}, bf16[128,512]{1,0:T(8,128)(2,1)S(1)}, u32[]{:S(2)}, u32[]{:S(2)}) collective-permute-start(bf16[128,512]{1,0:T(8,128)(2,1)S(1)} %get-tuple-element.16), channel_id=1, source_target_pairs={{0,28},{1,25},{2,30},{3,27},{4,24},{5,29},{6,26},{7,31},{8,20},{9,... | collective-permute-start | bytes 393224 | tf_op jit(solution)/shard_map/ppermute | solution.py:258
  12.1 3.6 %copy-start.1 = (bf16[128,512]{1,0:T(8,128)(2,1)S(1)}, bf16[128,512]{1,0:T(8,128)(2,1)}, u32[]{:S(2)}) copy-start(bf16[128,512]{1,0:T(8,128)(2,1)} %param.5) | copy-start | bytes 393220
  12.1 11.5 %collective-permute-start.4 = (bf16[128,512]{1,0:T(8,128)(2,1)S(1)}, bf16[128,512]{1,0:T(8,128)(2,1)S(1)}, u32[]{:S(2)}, u32[]{:S(2)}) collective-permute-start(bf16[128,512]{1,0:T(8,128)(2,1)S(1)} %get-tuple-element.17), channel_id=1, source_target_pairs={{0,8},{1,13},{2,10},{3,15},{4,12},{5,9},{6,14},{7,11},{8,0},{9,5},... | collective-permute-start | bytes 393224 | tf_op jit(solution)/shard_map/ppermute | solution.py:258
  15.8 16.5 %collective-permute-start.10 = (bf16[256,512]{1,0:T(8,128)(2,1)S(1)}, bf16[256,512]{1,0:T(8,128)(2,1)S(1)}, u32[]{:S(2)}, u32[]{:S(2)}) collective-permute-start(bf16[256,512]{1,0:T(8,128)(2,1)S(1)} %constant_dynamic-update-slice_fusion.refs_6_), channel_id=1, source_target_pairs={{0,12},{2,14},{4,8},{6,10},{8,4},{10,6},{12,0},{14,2},{16,28},{18,... | collective-permute-start | bytes 786440 | tf_op jit(solution)/shard_map/ppermute | solution.py:274
  20.6 6.2 %collective-permute-start.5 = (bf16[128,512]{1,0:T(8,128)(2,1)S(1)}, bf16[128,512]{1,0:T(8,128)(2,1)S(1)}, u32[]{:S(2)}, u32[]{:S(2)}) collective-permute-start(bf16[128,512]{1,0:T(8,128)(2,1)S(1)} %collective-permute-done.2.refs_0_), channel_id=1, source_target_pairs={{0,1},{1,0},{2,3},{3,2},{4,5},{5,4},{6,7},{7,6},{8,9},{9,8},{10,11... | collective-permute-start | bytes 393224 | tf_op jit(solution)/shard_map/ppermute | solution.py:246
  23.0 9.3 %collective-permute-start.9 = (bf16[256,512]{1,0:T(8,128)(2,1)S(1)}, bf16[256,512]{1,0:T(8,128)(2,1)S(1)}, u32[]{:S(2)}, u32[]{:S(2)}) collective-permute-start(bf16[256,512]{1,0:T(8,128)(2,1)S(1)} %constant_dynamic-update-slice_fusion.refs_6_), channel_id=1, source_target_pairs={{0,8},{2,10},{4,12},{6,14},{8,0},{10,2},{12,4},{14,6},{16,24},{18,... | collective-permute-start | bytes 786440 | tf_op jit(solution)/shard_map/ppermute | solution.py:274
  23.0 10.6 %collective-permute-start.8 = (bf16[256,512]{1,0:T(8,128)(2,1)S(1)}, bf16[256,512]{1,0:T(8,128)(2,1)S(1)}, u32[]{:S(2)}, u32[]{:S(2)}) collective-permute-start(bf16[256,512]{1,0:T(8,128)(2,1)S(1)} %constant_dynamic-update-slice_fusion.refs_6_), channel_id=1, source_target_pairs={{0,4},{2,6},{4,0},{6,2},{8,12},{10,14},{12,8},{14,10},{16,20},{18,... | collective-permute-start | bytes 786440 | tf_op jit(solution)/shard_map/ppermute | solution.py:274
  23.6 6.4 %collective-permute-start.6 = (bf16[128,512]{1,0:T(8,128)(2,1)S(1)}, bf16[128,512]{1,0:T(8,128)(2,1)S(1)}, u32[]{:S(2)}, u32[]{:S(2)}) collective-permute-start(bf16[128,512]{1,0:T(8,128)(2,1)S(1)} %collective-permute-done.3.refs_1_), channel_id=1, source_target_pairs={{0,1},{1,0},{2,3},{3,2},{4,5},{5,4},{6,7},{7,6},{8,9},{9,8},{10,11... | collective-permute-start | bytes 393224 | tf_op jit(solution)/shard_map/ppermute | solution.py:246
  26.8 5.4 %collective-permute-start.7 = (bf16[128,512]{1,0:T(8,128)(2,1)S(1)}, bf16[128,512]{1,0:T(8,128)(2,1)S(1)}, u32[]{:S(2)}, u32[]{:S(2)}) collective-permute-start(bf16[128,512]{1,0:T(8,128)(2,1)S(1)} %collective-permute-done.4.refs_2_), channel_id=1, source_target_pairs={{0,1},{1,0},{2,3},{3,2},{4,5},{5,4},{6,7},{7,6},{8,9},{9,8},{10,11... | collective-permute-start | bytes 393224 | tf_op jit(solution)/shard_map/ppermute | solution.py:246
  35.0 2.7 %collective-permute-start.11 = (f32[512,512]{1,0:T(8,128)S(1)}, f32[512,512]{1,0:T(8,128)S(1)}, u32[]{:S(2)}, u32[]{:S(2)}) collective-permute-start(f32[512,512]{1,0:T(8,128)S(1)} %shard_map.51.mine_ref), channel_id=1, source_target_pairs={{0,2},{2,0},{4,6},{6,4},{8,10},{10,8},{12,14},{14,12},{16,18},{18,... | collective-permute-start | bytes 3145736 | tf_op jit(solution)/shard_map/ppermute | solution.py:243
  45.2 5.6 %collective-permute-start.26 = (bf16[128,512]{1,0:T(8,128)(2,1)S(1)}, bf16[128,512]{1,0:T(8,128)(2,1)S(1)}, u32[]{:S(2)}, u32[]{:S(2)}) collective-permute-start(bf16[128,512]{1,0:T(8,128)(2,1)S(1)} %get-tuple-element.21), channel_id=1, source_target_pairs={{0,1},{1,0},{2,3},{3,2},{4,5},{5,4},{6,7},{7,6},{8,9},{9,8},{10,11... | collective-permute-start | bytes 393224 | tf_op jit(solution)/shard_map/ppermute | solution.py:246
  46.3 5.6 %collective-permute-start.12 = (bf16[128,512]{1,0:T(8,128)(2,1)S(1)}, bf16[128,512]{1,0:T(8,128)(2,1)S(1)}, u32[]{:S(2)}, u32[]{:S(2)}) collective-permute-start(bf16[128,512]{1,0:T(8,128)(2,1)S(1)} %get-tuple-element.19), channel_id=1, source_target_pairs={{0,8},{2,6},{8,16},{10,2},{16,24},{18,10},{24,28},{26,18},{28,20},... | collective-permute-start | bytes 393224 | tf_op jit(solution)/shard_map/ppermute | solution.py:312
  46.4 8.6 %collective-permute-start.14 = (bf16[128,512]{1,0:T(8,128)(2,1)S(1)}, bf16[128,512]{1,0:T(8,128)(2,1)S(1)}, u32[]{:S(2)}, u32[]{:S(2)}) collective-permute-start(bf16[128,512]{1,0:T(8,128)(2,1)S(1)} %get-tuple-element.20), channel_id=1, source_target_pairs={{0,8},{2,6},{8,16},{10,2},{16,24},{18,10},{24,28},{26,18},{28,20},... | collective-permute-start | bytes 393224 | tf_op jit(solution)/shard_map/ppermute | solution.py:312
  50.8 5.0 %collective-permute-start.28 = (bf16[128,512]{1,0:T(8,128)(2,1)S(1)}, bf16[128,512]{1,0:T(8,128)(2,1)S(1)}, u32[]{:S(2)}, u32[]{:S(2)}) collective-permute-start(bf16[128,512]{1,0:T(8,128)(2,1)S(1)} %collective-permute-done.26), channel_id=1, source_target_pairs={{0,8},{2,6},{8,16},{10,2},{16,24},{18,10},{24,28},{26,18},{28,20},... | collective-permute-start | bytes 393224 | tf_op jit(solution)/shard_map/ppermute | solution.py:312
  51.9 3.9 %collective-permute-start.27 = (bf16[128,512]{1,0:T(8,128)(2,1)S(1)}, bf16[128,512]{1,0:T(8,128)(2,1)S(1)}, u32[]{:S(2)}, u32[]{:S(2)}) collective-permute-start(bf16[128,512]{1,0:T(8,128)(2,1)S(1)} %collective-permute-done.26), channel_id=1, source_target_pairs={{0,2},{2,0},{4,6},{6,4},{8,10},{10,8},{12,14},{14,12},{16,18},{18,... | collective-permute-start | bytes 393224 | tf_op jit(solution)/shard_map/ppermute | solution.py:243
  51.9 5.9 %collective-permute-start.16 = (bf16[128,512]{1,0:T(8,128)(2,1)S(1)}, bf16[128,512]{1,0:T(8,128)(2,1)S(1)}, u32[]{:S(2)}, u32[]{:S(2)}) collective-permute-start(bf16[128,512]{1,0:T(8,128)(2,1)S(1)} %collective-permute-done.12), channel_id=1, source_target_pairs={{0,8},{2,6},{8,16},{10,2},{16,24},{18,10},{24,28},{26,18},{28,20},... | collective-permute-start | bytes 393224 | tf_op jit(solution)/shard_map/ppermute | solution.py:312
  55.0 2.7 %collective-permute-start.13 = (bf16[128,512]{1,0:T(8,128)(2,1)S(1)}, bf16[128,512]{1,0:T(8,128)(2,1)S(1)}, u32[]{:S(2)}, u32[]{:S(2)}) collective-permute-start(bf16[128,512]{1,0:T(8,128)(2,1)S(1)} %collective-permute-done.12), channel_id=1, source_target_pairs={{0,2},{2,0},{4,6},{6,4},{8,10},{10,8},{12,14},{14,12},{16,18},{18,... | collective-permute-start | bytes 393224 | tf_op jit(solution)/shard_map/ppermute | solution.py:243
  55.0 6.4 %collective-permute-start.18 = (bf16[128,512]{1,0:T(8,128)(2,1)S(1)}, bf16[128,512]{1,0:T(8,128)(2,1)S(1)}, u32[]{:S(2)}, u32[]{:S(2)}) collective-permute-start(bf16[128,512]{1,0:T(8,128)(2,1)S(1)} %collective-permute-done.14), channel_id=1, source_target_pairs={{0,8},{2,6},{8,16},{10,2},{16,24},{18,10},{24,28},{26,18},{28,20},... | collective-permute-start | bytes 393224 | tf_op jit(solution)/shard_map/ppermute | solution.py:312
  55.8 4.4 %collective-permute-start.15 = (bf16[128,512]{1,0:T(8,128)(2,1)S(1)}, bf16[128,512]{1,0:T(8,128)(2,1)S(1)}, u32[]{:S(2)}, u32[]{:S(2)}) collective-permute-start(bf16[128,512]{1,0:T(8,128)(2,1)S(1)} %collective-permute-done.14), channel_id=1, source_target_pairs={{0,2},{2,0},{4,6},{6,4},{8,10},{10,8},{12,14},{14,12},{16,18},{18,... | collective-permute-start | bytes 393224 | tf_op jit(solution)/shard_map/ppermute | solution.py:243
  55.8 6.8 %collective-permute-start.32 = (bf16[128,512]{1,0:T(8,128)(2,1)S(1)}, bf16[128,512]{1,0:T(8,128)(2,1)S(1)}, u32[]{:S(2)}, u32[]{:S(2)}) collective-permute-start(bf16[128,512]{1,0:T(8,128)(2,1)S(1)} %collective-permute-done.28), channel_id=1, source_target_pairs={{0,8},{2,6},{8,16},{10,2},{16,24},{18,10},{24,28},{26,18},{28,20},... | collective-permute-start | bytes 393224 | tf_op jit(solution)/shard_map/ppermute | solution.py:312
  57.7 3.8 %collective-permute-start.29 = (bf16[128,512]{1,0:T(8,128)(2,1)S(1)}, bf16[128,512]{1,0:T(8,128)(2,1)S(1)}, u32[]{:S(2)}, u32[]{:S(2)}) collective-permute-start(bf16[128,512]{1,0:T(8,128)(2,1)S(1)} %collective-permute-done.28), channel_id=1, source_target_pairs={{0,2},{2,0},{4,6},{6,4},{8,10},{10,8},{12,14},{14,12},{16,18},{18,... | collective-permute-start | bytes 393224 | tf_op jit(solution)/shard_map/ppermute | solution.py:243
  57.8 6.1 %collective-permute-start.30 = (bf16[128,512]{1,0:T(8,128)(2,1)S(1)}, bf16[128,512]{1,0:T(8,128)(2,1)S(1)}, u32[]{:S(2)}, u32[]{:S(2)}) collective-permute-start(bf16[128,512]{1,0:T(8,128)(2,1)S(1)} %collective-permute-done.27), channel_id=1, source_target_pairs={{0,8},{2,6},{8,16},{10,2},{16,24},{18,10},{24,28},{26,18},{28,20},... | collective-permute-start | bytes 393224 | tf_op jit(solution)/shard_map/ppermute | solution.py:312
  60.2 5.0 %collective-permute-start.20 = (bf16[128,512]{1,0:T(8,128)(2,1)S(1)}, bf16[128,512]{1,0:T(8,128)(2,1)S(1)}, u32[]{:S(2)}, u32[]{:S(2)}) collective-permute-start(bf16[128,512]{1,0:T(8,128)(2,1)S(1)} %collective-permute-done.16), channel_id=1, source_target_pairs={{0,8},{2,6},{8,16},{10,2},{16,24},{18,10},{24,28},{26,18},{28,20},... | collective-permute-start | bytes 393224 | tf_op jit(solution)/shard_map/ppermute | solution.py:312
  61.4 1.4 %collective-permute-start.17 = (bf16[128,512]{1,0:T(8,128)(2,1)S(1)}, bf16[128,512]{1,0:T(8,128)(2,1)S(1)}, u32[]{:S(2)}, u32[]{:S(2)}) collective-permute-start(bf16[128,512]{1,0:T(8,128)(2,1)S(1)} %collective-permute-done.16), channel_id=1, source_target_pairs={{0,2},{2,0},{4,6},{6,4},{8,10},{10,8},{12,14},{14,12},{16,18},{18,... | collective-permute-start | bytes 393224 | tf_op jit(solution)/shard_map/ppermute | solution.py:243
  61.5 6.3 %collective-permute-start.22 = (bf16[128,512]{1,0:T(8,128)(2,1)S(1)}, bf16[128,512]{1,0:T(8,128)(2,1)S(1)}, u32[]{:S(2)}, u32[]{:S(2)}) collective-permute-start(bf16[128,512]{1,0:T(8,128)(2,1)S(1)} %collective-permute-done.18), channel_id=1, source_target_pairs={{0,8},{2,6},{8,16},{10,2},{16,24},{18,10},{24,28},{26,18},{28,20},... | collective-permute-start | bytes 393224 | tf_op jit(solution)/shard_map/ppermute | solution.py:312
  62.7 1.4 %collective-permute-start.19 = (bf16[128,512]{1,0:T(8,128)(2,1)S(1)}, bf16[128,512]{1,0:T(8,128)(2,1)S(1)}, u32[]{:S(2)}, u32[]{:S(2)}) collective-permute-start(bf16[128,512]{1,0:T(8,128)(2,1)S(1)} %collective-permute-done.18), channel_id=1, source_target_pairs={{0,2},{2,0},{4,6},{6,4},{8,10},{10,8},{12,14},{14,12},{16,18},{18,... | collective-permute-start | bytes 393224 | tf_op jit(solution)/shard_map/ppermute | solution.py:243
  62.8 5.1 %collective-permute-start.36 = (bf16[128,512]{1,0:T(8,128)(2,1)S(1)}, bf16[128,512]{1,0:T(8,128)(2,1)S(1)}, u32[]{:S(2)}, u32[]{:S(2)}) collective-permute-start(bf16[128,512]{1,0:T(8,128)(2,1)S(1)} %collective-permute-done.32), channel_id=1, source_target_pairs={{0,8},{2,6},{8,16},{10,2},{16,24},{18,10},{24,28},{26,18},{28,20},... | collective-permute-start | bytes 393224 | tf_op jit(solution)/shard_map/ppermute | solution.py:312
  63.9 4.4 %collective-permute-start.33 = (bf16[128,512]{1,0:T(8,128)(2,1)S(1)}, bf16[128,512]{1,0:T(8,128)(2,1)S(1)}, u32[]{:S(2)}, u32[]{:S(2)}) collective-permute-start(bf16[128,512]{1,0:T(8,128)(2,1)S(1)} %collective-permute-done.32), channel_id=1, source_target_pairs={{0,2},{2,0},{4,6},{6,4},{8,10},{10,8},{12,14},{14,12},{16,18},{18,... | collective-permute-start | bytes 393224 | tf_op jit(solution)/shard_map/ppermute | solution.py:243
  64.1 2.5 %collective-permute-start.31 = (bf16[128,512]{1,0:T(8,128)(2,1)S(1)}, bf16[128,512]{1,0:T(8,128)(2,1)S(1)}, u32[]{:S(2)}, u32[]{:S(2)}) collective-permute-start(bf16[128,512]{1,0:T(8,128)(2,1)S(1)} %collective-permute-done.30), channel_id=1, source_target_pairs={{0,2},{2,0},{4,6},{6,4},{8,10},{10,8},{12,14},{14,12},{16,18},{18,... | collective-permute-start | bytes 393224 | tf_op jit(solution)/shard_map/ppermute | solution.py:243
  65.1 5.0 %collective-permute-start.34 = (bf16[128,512]{1,0:T(8,128)(2,1)S(1)}, bf16[128,512]{1,0:T(8,128)(2,1)S(1)}, u32[]{:S(2)}, u32[]{:S(2)}) collective-permute-start(bf16[128,512]{1,0:T(8,128)(2,1)S(1)} %collective-permute-done.30), channel_id=1, source_target_pairs={{0,8},{2,6},{8,16},{10,2},{16,24},{18,10},{24,28},{26,18},{28,20},... | collective-permute-start | bytes 393224 | tf_op jit(solution)/shard_map/ppermute | solution.py:312
  66.6 5.0 %collective-permute-start.24 = (bf16[128,512]{1,0:T(8,128)(2,1)S(1)}, bf16[128,512]{1,0:T(8,128)(2,1)S(1)}, u32[]{:S(2)}, u32[]{:S(2)}) collective-permute-start(bf16[128,512]{1,0:T(8,128)(2,1)S(1)} %collective-permute-done.20), channel_id=1, source_target_pairs={{0,8},{2,6},{8,16},{10,2},{16,24},{18,10},{24,28},{26,18},{28,20},... | collective-permute-start | bytes 393224 | tf_op jit(solution)/shard_map/ppermute | solution.py:312
  67.8 2.3 %collective-permute-start.21 = (bf16[128,512]{1,0:T(8,128)(2,1)S(1)}, bf16[128,512]{1,0:T(8,128)(2,1)S(1)}, u32[]{:S(2)}, u32[]{:S(2)}) collective-permute-start(bf16[128,512]{1,0:T(8,128)(2,1)S(1)} %collective-permute-done.20), channel_id=1, source_target_pairs={{0,2},{2,0},{4,6},{6,4},{8,10},{10,8},{12,14},{14,12},{16,18},{18,... | collective-permute-start | bytes 393224 | tf_op jit(solution)/shard_map/ppermute | solution.py:243
  68.0 3.7 %collective-permute-start.23 = (bf16[128,512]{1,0:T(8,128)(2,1)S(1)}, bf16[128,512]{1,0:T(8,128)(2,1)S(1)}, u32[]{:S(2)}, u32[]{:S(2)}) collective-permute-start(bf16[128,512]{1,0:T(8,128)(2,1)S(1)} %collective-permute-done.22), channel_id=1, source_target_pairs={{0,2},{2,0},{4,6},{6,4},{8,10},{10,8},{12,14},{14,12},{16,18},{18,... | collective-permute-start | bytes 393224 | tf_op jit(solution)/shard_map/ppermute | solution.py:243
  68.4 5.0 %collective-permute-start.40 = (bf16[128,512]{1,0:T(8,128)(2,1)S(1)}, bf16[128,512]{1,0:T(8,128)(2,1)S(1)}, u32[]{:S(2)}, u32[]{:S(2)}) collective-permute-start(bf16[128,512]{1,0:T(8,128)(2,1)S(1)} %collective-permute-done.36), channel_id=1, source_target_pairs={{0,8},{2,6},{8,16},{10,2},{16,24},{18,10},{24,28},{26,18},{28,20},... | collective-permute-start | bytes 393224 | tf_op jit(solution)/shard_map/ppermute | solution.py:312
  70.1 5.0 %collective-permute-start.37 = (bf16[128,512]{1,0:T(8,128)(2,1)S(1)}, bf16[128,512]{1,0:T(8,128)(2,1)S(1)}, u32[]{:S(2)}, u32[]{:S(2)}) collective-permute-start(bf16[128,512]{1,0:T(8,128)(2,1)S(1)} %collective-permute-done.36), channel_id=1, source_target_pairs={{0,2},{2,0},{4,6},{6,4},{8,10},{10,8},{12,14},{14,12},{16,18},{18,... | collective-permute-start | bytes 393224 | tf_op jit(solution)/shard_map/ppermute | solution.py:243
  70.1 5.0 %collective-permute-start.38 = (bf16[128,512]{1,0:T(8,128)(2,1)S(1)}, bf16[128,512]{1,0:T(8,128)(2,1)S(1)}, u32[]{:S(2)}, u32[]{:S(2)}) collective-permute-start(bf16[128,512]{1,0:T(8,128)(2,1)S(1)} %collective-permute-done.34), channel_id=1, source_target_pairs={{0,8},{2,6},{8,16},{10,2},{16,24},{18,10},{24,28},{26,18},{28,20},... | collective-permute-start | bytes 393224 | tf_op jit(solution)/shard_map/ppermute | solution.py:312
  71.6 3.5 %collective-permute-start.35 = (bf16[128,512]{1,0:T(8,128)(2,1)S(1)}, bf16[128,512]{1,0:T(8,128)(2,1)S(1)}, u32[]{:S(2)}, u32[]{:S(2)}) collective-permute-start(bf16[128,512]{1,0:T(8,128)(2,1)S(1)} %collective-permute-done.34), channel_id=1, source_target_pairs={{0,2},{2,0},{4,6},{6,4},{8,10},{10,8},{12,14},{14,12},{16,18},{18,... | collective-permute-start | bytes 393224 | tf_op jit(solution)/shard_map/ppermute | solution.py:243
  71.7 4.8 %collective-permute-start.25 = (bf16[128,512]{1,0:T(8,128)(2,1)S(1)}, bf16[128,512]{1,0:T(8,128)(2,1)S(1)}, u32[]{:S(2)}, u32[]{:S(2)}) collective-permute-start(bf16[128,512]{1,0:T(8,128)(2,1)S(1)} %collective-permute-done.24), channel_id=1, source_target_pairs={{0,2},{2,0},{4,6},{6,4},{8,10},{10,8},{12,14},{14,12},{16,18},{18,... | collective-permute-start | bytes 393224 | tf_op jit(solution)/shard_map/ppermute | solution.py:243
  73.3 3.2 %collective-permute-start.41 = (bf16[128,512]{1,0:T(8,128)(2,1)S(1)}, bf16[128,512]{1,0:T(8,128)(2,1)S(1)}, u32[]{:S(2)}, u32[]{:S(2)}) collective-permute-start(bf16[128,512]{1,0:T(8,128)(2,1)S(1)} %collective-permute-done.40), channel_id=1, source_target_pairs={{0,2},{2,0},{4,6},{6,4},{8,10},{10,8},{12,14},{14,12},{16,18},{18,... | collective-permute-start | bytes 393224 | tf_op jit(solution)/shard_map/ppermute | solution.py:243
  75.1 1.3 %collective-permute-start.39 = (bf16[128,512]{1,0:T(8,128)(2,1)S(1)}, bf16[128,512]{1,0:T(8,128)(2,1)S(1)}, u32[]{:S(2)}, u32[]{:S(2)}) collective-permute-start(bf16[128,512]{1,0:T(8,128)(2,1)S(1)} %collective-permute-done.38), channel_id=1, source_target_pairs={{0,2},{2,0},{4,6},{6,4},{8,10},{10,8},{12,14},{14,12},{16,18},{18,... | collective-permute-start | bytes 393224 | tf_op jit(solution)/shard_map/ppermute | solution.py:243

commit v12 on v11

--- a/solution.py
+++ b/solution.py
@@ -176,6 +176,7 @@
 
 OFFSETS = ((4, 7, 2), (5, 6, 3))
 SHARED = 1
+PAIR_OFFSETS = (0, 3, 2, 1)
 
 
 def pack_kernel(place_ref, inputs_ref, *piece_refs):
@@ -206,7 +207,7 @@
     for hop in range(hops):
         for piece_ref, member in ((near_refs[hop], plane), (far_refs[hop], 1 - plane)):
             put(band_ref, piece_ref, band ^ jnp.where(member == 0, OFFSETS[0][hop], OFFSETS[1][hop]))
-    for offset, pair_ref in enumerate(cot_refs):
+    for offset, pair_ref in zip(PAIR_OFFSETS, cot_refs):
         for part, source in enumerate((band ^ offset, band ^ offset ^ 4)):
             put(cot_ref, pair_ref.at[pl.ds(part * tokens, tokens)], source)
     partial_ref[...] = contract(band_ref[...], cot_ref[...], 0, 0)
@@ -278,7 +279,7 @@
     near = [deal(packed[hop], hop) for hop in hops]
     shared = exchange(packed[-1], SHARED)
     pair = jnp.concatenate([cotangent, far_cot])
-    cots = [pair] + [exchange(pair, offset) for offset in (1, 2, 3)]
+    cots = [pair] + [exchange(pair, offset) for offset in PAIR_OFFSETS[1:]]
     far = [swap_plane(piece) for piece in near]
     (partial_tile,) = call(
         tile_kernel,

time: 79.4 us -> 80.8 us (1.018)
  starting transfers between devices: 42.5 us -> 45.6 us
  waiting for transfers between devices: 17.3 us -> 15.6 us
    ppermute x5, starting transfers between devices: 9.35 us -> 11.7 us  [exchange(): return lax.ppermute(array, 'dp', pairs)]
    ppermute x14, starting transfers between devices: 20.4 us -> 22.3 us  [turn(): return lax.ppermute(array, 'dp', pairs)]
    ppermute x4, waiting for transfers between devices: 6.21 us -> 4.94 us  [swap_plane(): lax.ppermute(array, 'pre', [(c, members - 1 - c) for c in range(members)])]
    ppermute x5, waiting for transfers between devices: 1.36 us -> 2.56 us  [exchange(): return lax.ppermute(array, 'dp', pairs)]
    ppermute x4, starting transfers between devices: 6.98 us -> 5.97 us  [swap_plane(): lax.ppermute(array, 'pre', [(c, members - 1 - c) for c in range(members)])]
    ppermute x3, waiting for transfers between devices: 1.79 us -> 0.86 us  [deal(): return lax.ppermute(array, ('dp', 'pre'), pairs)]
  transfers between devices with their start and end apart: 42 -> 42, of which waited for: 15 -> 13; matrix products, arithmetic and copies ran while one was open for 6% -> 6% of each run, Pallas kernels for 1% -> 1%
where the time goes in v12:
time: 80.8 us; the launch traced here: 80.6 us
  starting transfers between devices  45.6 us (56%)
  waiting for transfers between devices  15.6 us (19%)
  Pallas kernels  9.42 us (12%)
  matrix products  3.6 us (4%)
  other arithmetic  2.81 us (3%)
  local copies, waits for them, and re-layouts  2.23 us (3%)
  between operations  1.38 us (2%)
    ppermute x14, starting transfers between devices, turn(): return lax.ppermute(array, 'dp', pairs)  22.3 us
    ppermute x5, starting transfers between devices, exchange(): return lax.ppermute(array, 'dp', pairs)  11.7 us
    pallas_call x3, Pallas kernels, call(): pl.pallas_call(kernel, out_shape=out_shapes, in_specs=in_specs, out_specs...  9.42 us
    ppermute x4, starting transfers between devices, swap_plane(): lax.ppermute(array, 'pre', [(c, members - 1 - c) for c in range(members)])  5.97 us
    ppermute x4, waiting for transfers between devices, swap_plane(): lax.ppermute(array, 'pre', [(c, members - 1 - c) for c in range(members)])  4.94 us
    ppermute x3, starting transfers between devices, deal(): return lax.ppermute(array, ('dp', 'pre'), pairs)  3.88 us
    ppermute x14, waiting for transfers between devices, turn(): return lax.ppermute(array, 'dp', pairs)  3.71 us
    dot_general x1, matrix products, on_device_paired(): jnp.dot(inputs, weight, preferred_element_type=jnp.float32)  3.6 us
  transfers between devices with their start and end apart: 42, of which 13 were waited for; matrix products, arithmetic and copies ran while one was open for 6% of the time, Pallas kernels for 1%

profile of v12, /device:TPU:0, one launch (start us, length us, event | category | flops | bytes accessed | tf_op | source)
XLA Modules:
  0.0 80.6 jit_solution(12815703274448990861)
XLA Ops:
  0.6 4.1 %collective-permute-start = (bf16[128,512]{1,0:T(8,128)(2,1)}, bf16[128,512]{1,0:T(8,128)(2,1)S(1)}, u32[]{:S(2)}, u32[]{:S(2)}) collective-permute-start(bf16[128,512]{1,0:T(8,128)(2,1)} %param.5), channel_id=1, source_target_pairs={{0,16},{2,18},{4,20},{6,22},{8,24},{10,26},{12,28},{14,30},{16,0},... | collective-permute-start | bytes 393224 | tf_op jit(solution)/shard_map/ppermute | solution.py:275
  4.7 0.1 stack.41.place_ref
  4.8 1.2 %copy-done = bf16[128,4096]{1,0:T(8,128)(2,1)S(1)} copy-done((bf16[128,4096]{1,0:T(8,128)(2,1)S(1)}, bf16[128,4096]{1,0:T(8,128)(2,1)}, u32[]{:S(2)}) %copy-start) | copy-done | bytes 1048600
  6.0 0.6 shard_map.50
  6.6 1.6 %collective-permute-start.1 = (bf16[128,512]{1,0:T(8,128)(2,1)S(1)}, bf16[128,512]{1,0:T(8,128)(2,1)S(1)}, u32[]{:S(2)}, u32[]{:S(2)}) collective-permute-start(bf16[128,512]{1,0:T(8,128)(2,1)S(1)} %get-tuple-element.14), channel_id=1, source_target_pairs={{0,4},{2,6},{4,0},{6,2},{8,12},{10,14},{12,8},{14,10},{16,20},{18,... | collective-permute-start | bytes 393224 | tf_op jit(solution)/shard_map/ppermute | solution.py:275
  8.2 0.3 collective-permute-start.2
  8.6 3.5 %collective-permute-start.3 = (bf16[128,512]{1,0:T(8,128)(2,1)S(1)}, bf16[128,512]{1,0:T(8,128)(2,1)S(1)}, u32[]{:S(2)}, u32[]{:S(2)}) collective-permute-start(bf16[128,512]{1,0:T(8,128)(2,1)S(1)} %get-tuple-element.16), channel_id=1, source_target_pairs={{0,28},{1,25},{2,30},{3,27},{4,24},{5,29},{6,26},{7,31},{8,20},{9,... | collective-permute-start | bytes 393224 | tf_op jit(solution)/shard_map/ppermute | solution.py:259
  12.1 3.6 %convolution_convert_fusion = bf16[128,512]{1,0:T(8,128)(2,1)} fusion(bf16[128,4096]{1,0:T(8,128)(2,1)S(1)} %copy-done, bf16[4096,512]{1,0:T(8,128)(2,1)} %param.4), kind=kOutput, calls=%fused_computation.1 | convolution fusion | flops 536936448 | bytes 5373952 | tf_op jit(solution)/shard_map/dot_general | solution.py:277
  15.8 4.0 %collective-permute-start.10 = (bf16[256,512]{1,0:T(8,128)(2,1)S(1)}, bf16[256,512]{1,0:T(8,128)(2,1)S(1)}, u32[]{:S(2)}, u32[]{:S(2)}) collective-permute-start(bf16[256,512]{1,0:T(8,128)(2,1)S(1)} %constant_dynamic-update-slice_fusion.refs_6_), channel_id=1, source_target_pairs={{0,4},{2,6},{4,0},{6,2},{8,12},{10,14},{12,8},{14,10},{16,20},{18,... | collective-permute-start | bytes 786440 | tf_op jit(solution)/shard_map/ppermute | solution.py:275
  19.7 0.9 %collective-permute-done.2.refs_0_ = bf16[128,512]{1,0:T(8,128)(2,1)S(1)} collective-permute-done((bf16[128,512]{1,0:T(8,128)(2,1)S(1)}, bf16[128,512]{1,0:T(8,128)(2,1)S(1)}, u32[]{:S(2)}, u32[]{:S(2)}) %collective-permute-start.2) | collective-permute-done | bytes 131104 | tf_op jit(solution)/shard_map/ppermute | solution.py:259
  20.6 2.4 %collective-permute-start.5 = (bf16[128,512]{1,0:T(8,128)(2,1)S(1)}, bf16[128,512]{1,0:T(8,128)(2,1)S(1)}, u32[]{:S(2)}, u32[]{:S(2)}) collective-permute-start(bf16[128,512]{1,0:T(8,128)(2,1)S(1)} %collective-permute-done.2.refs_0_), channel_id=1, source_target_pairs={{0,1},{1,0},{2,3},{3,2},{4,5},{5,4},{6,7},{7,6},{8,9},{9,8},{10,11... | collective-permute-start | bytes 393224 | tf_op jit(solution)/shard_map/ppermute | solution.py:247
  23.1 2.0 %collective-permute-start.8 = (bf16[256,512]{1,0:T(8,128)(2,1)S(1)}, bf16[256,512]{1,0:T(8,128)(2,1)S(1)}, u32[]{:S(2)}, u32[]{:S(2)}) collective-permute-start(bf16[256,512]{1,0:T(8,128)(2,1)S(1)} %constant_dynamic-update-slice_fusion.refs_6_), channel_id=1, source_target_pairs={{0,12},{2,14},{4,8},{6,10},{8,4},{10,6},{12,0},{14,2},{16,28},{18,... | collective-permute-start | bytes 786440 | tf_op jit(solution)/shard_map/ppermute | solution.py:275
  25.1 0.9 %collective-permute-start.6 = (bf16[128,512]{1,0:T(8,128)(2,1)S(1)}, bf16[128,512]{1,0:T(8,128)(2,1)S(1)}, u32[]{:S(2)}, u32[]{:S(2)}) collective-permute-start(bf16[128,512]{1,0:T(8,128)(2,1)S(1)} %collective-permute-done.3.refs_1_), channel_id=1, source_target_pairs={{0,1},{1,0},{2,3},{3,2},{4,5},{5,4},{6,7},{7,6},{8,9},{9,8},{10,11... | collective-permute-start | bytes 393224 | tf_op jit(solution)/shard_map/ppermute | solution.py:247
  26.0 2.0 %collective-permute-start.7 = (bf16[128,512]{1,0:T(8,128)(2,1)S(1)}, bf16[128,512]{1,0:T(8,128)(2,1)S(1)}, u32[]{:S(2)}, u32[]{:S(2)}) collective-permute-start(bf16[128,512]{1,0:T(8,128)(2,1)S(1)} %collective-permute-done.4.refs_2_), channel_id=1, source_target_pairs={{0,1},{1,0},{2,3},{3,2},{4,5},{5,4},{6,7},{7,6},{8,9},{9,8},{10,11... | collective-permute-start | bytes 393224 | tf_op jit(solution)/shard_map/ppermute | solution.py:247
  28.1 2.7 %collective-permute-done.6.refs_4_ = bf16[128,512]{1,0:T(8,128)(2,1)S(1)} collective-permute-done((bf16[128,512]{1,0:T(8,128)(2,1)S(1)}, bf16[128,512]{1,0:T(8,128)(2,1)S(1)}, u32[]{:S(2)}, u32[]{:S(2)}) %collective-permute-start.6) | collective-permute-done | bytes 131104 | tf_op jit(solution)/shard_map/ppermute | solution.py:247
  30.8 1.4 %collective-permute-done.7.refs_5_ = bf16[128,512]{1,0:T(8,128)(2,1)S(1)} collective-permute-done((bf16[128,512]{1,0:T(8,128)(2,1)S(1)}, bf16[128,512]{1,0:T(8,128)(2,1)S(1)}, u32[]{:S(2)}, u32[]{:S(2)}) %collective-permute-start.7) | collective-permute-done | bytes 131104 | tf_op jit(solution)/shard_map/ppermute | solution.py:247
  32.2 2.5 %collective-permute-done.8.refs_7_ = bf16[256,512]{1,0:T(8,128)(2,1)S(1)} collective-permute-done((bf16[256,512]{1,0:T(8,128)(2,1)S(1)}, bf16[256,512]{1,0:T(8,128)(2,1)S(1)}, u32[]{:S(2)}, u32[]{:S(2)}) %collective-permute-start.8) | collective-permute-done | bytes 262176 | tf_op jit(solution)/shard_map/ppermute | solution.py:275
  34.7 1.4 %shard_map.51.mine_ref = f32[512,512]{1,0:T(8,128)S(1)} custom-call(s32[2]{0:T(128)S(1)} %pad_add_fusion.1.place_ref, bf16[128,512]{1,0:T(8,128)(2,1)S(1)} %get-tuple-element.13.own_ref, bf16[128,512]{1,0:T(8,128)(2,1)S(1)} %collective-permute-done.1.shared_ref, bf16[128,512]{1,0:T(8,128)(2,1)S(1)} %collective-permute-done.2.refs_0_, ...), custom_call_target="tpu_custom_call" | custom-call | tf_op jit(solution)/shard_map/pallas_call | solution.py:219
  36.6 2.3 %collective-permute-done.11.other_ref = f32[512,512]{1,0:T(8,128)S(1)} collective-permute-done((f32[512,512]{1,0:T(8,128)S(1)}, f32[512,512]{1,0:T(8,128)S(1)}, u32[]{:S(2)}, u32[]{:S(2)}) %collective-permute-start.11) | collective-permute-done | bytes 1048608 | tf_op jit(solution)/shard_map/ppermute | solution.py:244
  38.8 7.4 %shard_map.52 = (bf16[128,512]{1,0:T(8,128)(2,1)S(1)}, bf16[128,512]{1,0:T(8,128)(2,1)S(1)}, bf16[128,512]{1,0:T(8,128)(2,1)S(1)}) custom-call(s32[2]{0:T(128)S(1)} %pad_add_fusion.side_ref, f32[512,512]{1,0:T(8,128)S(1)} %shard_map.51.mine_ref, f32[512,512]{1,0:T(8,128)S(1)} %collective-permute-done.11.other_ref), custom_call_target="tpu_custom_call" | custom-call | tf_op jit(solution)/shard_map/pallas_call | solution.py:219
  46.3 0.6 collective-permute-start.26
  46.9 1.7 %collective-permute-start.12 = (bf16[128,512]{1,0:T(8,128)(2,1)S(1)}, bf16[128,512]{1,0:T(8,128)(2,1)S(1)}, u32[]{:S(2)}, u32[]{:S(2)}) collective-permute-start(bf16[128,512]{1,0:T(8,128)(2,1)S(1)} %get-tuple-element.19), channel_id=1, source_target_pairs={{0,8},{2,6},{8,16},{10,2},{16,24},{18,10},{24,28},{26,18},{28,20},... | collective-permute-start | bytes 393224 | tf_op jit(solution)/shard_map/ppermute | solution.py:313
  48.6 2.2 %collective-permute-start.14 = (bf16[128,512]{1,0:T(8,128)(2,1)S(1)}, bf16[128,512]{1,0:T(8,128)(2,1)S(1)}, u32[]{:S(2)}, u32[]{:S(2)}) collective-permute-start(bf16[128,512]{1,0:T(8,128)(2,1)S(1)} %get-tuple-element.20), channel_id=1, source_target_pairs={{0,8},{2,6},{8,16},{10,2},{16,24},{18,10},{24,28},{26,18},{28,20},... | collective-permute-start | bytes 393224 | tf_op jit(solution)/shard_map/ppermute | solution.py:313
  50.8 0.2 broadcast_in_dim.99.clone.1
  51.1 0.8 collective-permute-done.26
  51.9 1.7 %collective-permute-start.28 = (bf16[128,512]{1,0:T(8,128)(2,1)S(1)}, bf16[128,512]{1,0:T(8,128)(2,1)S(1)}, u32[]{:S(2)}, u32[]{:S(2)}) collective-permute-start(bf16[128,512]{1,0:T(8,128)(2,1)S(1)} %collective-permute-done.26), channel_id=1, source_target_pairs={{0,8},{2,6},{8,16},{10,2},{16,24},{18,10},{24,28},{26,18},{28,20},... | collective-permute-start | bytes 393224 | tf_op jit(solution)/shard_map/ppermute | solution.py:313
  53.6 2.2 %collective-permute-start.16 = (bf16[128,512]{1,0:T(8,128)(2,1)S(1)}, bf16[128,512]{1,0:T(8,128)(2,1)S(1)}, u32[]{:S(2)}, u32[]{:S(2)}) collective-permute-start(bf16[128,512]{1,0:T(8,128)(2,1)S(1)} %collective-permute-done.12), channel_id=1, source_target_pairs={{0,8},{2,6},{8,16},{10,2},{16,24},{18,10},{24,28},{26,18},{28,20},... | collective-permute-start | bytes 393224 | tf_op jit(solution)/shard_map/ppermute | solution.py:313
  55.8 1.7 %collective-permute-start.18 = (bf16[128,512]{1,0:T(8,128)(2,1)S(1)}, bf16[128,512]{1,0:T(8,128)(2,1)S(1)}, u32[]{:S(2)}, u32[]{:S(2)}) collective-permute-start(bf16[128,512]{1,0:T(8,128)(2,1)S(1)} %collective-permute-done.14), channel_id=1, source_target_pairs={{0,8},{2,6},{8,16},{10,2},{16,24},{18,10},{24,28},{26,18},{28,20},... | collective-permute-start | bytes 393224 | tf_op jit(solution)/shard_map/ppermute | solution.py:313
  57.5 0.2 broadcast_in_dim.99.clone
  57.9 1.6 %collective-permute-start.32 = (bf16[128,512]{1,0:T(8,128)(2,1)S(1)}, bf16[128,512]{1,0:T(8,128)(2,1)S(1)}, u32[]{:S(2)}, u32[]{:S(2)}) collective-permute-start(bf16[128,512]{1,0:T(8,128)(2,1)S(1)} %collective-permute-done.28), channel_id=1, source_target_pairs={{0,8},{2,6},{8,16},{10,2},{16,24},{18,10},{24,28},{26,18},{28,20},... | collective-permute-start | bytes 393224 | tf_op jit(solution)/shard_map/ppermute | solution.py:313
  59.6 1.4 %collective-permute-start.30 = (bf16[128,512]{1,0:T(8,128)(2,1)S(1)}, bf16[128,512]{1,0:T(8,128)(2,1)S(1)}, u32[]{:S(2)}, u32[]{:S(2)}) collective-permute-start(bf16[128,512]{1,0:T(8,128)(2,1)S(1)} %collective-permute-done.27), channel_id=1, source_target_pairs={{0,8},{2,6},{8,16},{10,2},{16,24},{18,10},{24,28},{26,18},{28,20},... | collective-permute-start | bytes 393224 | tf_op jit(solution)/shard_map/ppermute | solution.py:313
  61.0 1.7 %collective-permute-start.20 = (bf16[128,512]{1,0:T(8,128)(2,1)S(1)}, bf16[128,512]{1,0:T(8,128)(2,1)S(1)}, u32[]{:S(2)}, u32[]{:S(2)}) collective-permute-start(bf16[128,512]{1,0:T(8,128)(2,1)S(1)} %collective-permute-done.16), channel_id=1, source_target_pairs={{0,8},{2,6},{8,16},{10,2},{16,24},{18,10},{24,28},{26,18},{28,20},... | collective-permute-start | bytes 393224 | tf_op jit(solution)/shard_map/ppermute | solution.py:313
  62.9 1.6 %collective-permute-start.22 = (bf16[128,512]{1,0:T(8,128)(2,1)S(1)}, bf16[128,512]{1,0:T(8,128)(2,1)S(1)}, u32[]{:S(2)}, u32[]{:S(2)}) collective-permute-start(bf16[128,512]{1,0:T(8,128)(2,1)S(1)} %collective-permute-done.18), channel_id=1, source_target_pairs={{0,8},{2,6},{8,16},{10,2},{16,24},{18,10},{24,28},{26,18},{28,20},... | collective-permute-start | bytes 393224 | tf_op jit(solution)/shard_map/ppermute | solution.py:313
  64.6 1.2 %collective-permute-start.36 = (bf16[128,512]{1,0:T(8,128)(2,1)S(1)}, bf16[128,512]{1,0:T(8,128)(2,1)S(1)}, u32[]{:S(2)}, u32[]{:S(2)}) collective-permute-start(bf16[128,512]{1,0:T(8,128)(2,1)S(1)} %collective-permute-done.32), channel_id=1, source_target_pairs={{0,8},{2,6},{8,16},{10,2},{16,24},{18,10},{24,28},{26,18},{28,20},... | collective-permute-start | bytes 393224 | tf_op jit(solution)/shard_map/ppermute | solution.py:313
  65.9 0.5 collective-permute-start.31
  66.5 1.2 %collective-permute-start.34 = (bf16[128,512]{1,0:T(8,128)(2,1)S(1)}, bf16[128,512]{1,0:T(8,128)(2,1)S(1)}, u32[]{:S(2)}, u32[]{:S(2)}) collective-permute-start(bf16[128,512]{1,0:T(8,128)(2,1)S(1)} %collective-permute-done.30), channel_id=1, source_target_pairs={{0,8},{2,6},{8,16},{10,2},{16,24},{18,10},{24,28},{26,18},{28,20},... | collective-permute-start | bytes 393224 | tf_op jit(solution)/shard_map/ppermute | solution.py:313
  67.7 1.5 %collective-permute-start.24 = (bf16[128,512]{1,0:T(8,128)(2,1)S(1)}, bf16[128,512]{1,0:T(8,128)(2,1)S(1)}, u32[]{:S(2)}, u32[]{:S(2)}) collective-permute-start(bf16[128,512]{1,0:T(8,128)(2,1)S(1)} %collective-permute-done.20), channel_id=1, source_target_pairs={{0,8},{2,6},{8,16},{10,2},{16,24},{18,10},{24,28},{26,18},{28,20},... | collective-permute-start | bytes 393224 | tf_op jit(solution)/shard_map/ppermute | solution.py:313
  69.3 0.3 collective-permute-done.36
  69.6 0.2 collective-permute-start.23
  69.8 1.4 %collective-permute-start.40 = (bf16[128,512]{1,0:T(8,128)(2,1)S(1)}, bf16[128,512]{1,0:T(8,128)(2,1)S(1)}, u32[]{:S(2)}, u32[]{:S(2)}) collective-permute-start(bf16[128,512]{1,0:T(8,128)(2,1)S(1)} %collective-permute-done.36), channel_id=1, source_target_pairs={{0,8},{2,6},{8,16},{10,2},{16,24},{18,10},{24,28},{26,18},{28,20},... | collective-permute-start | bytes 393224 | tf_op jit(solution)/shard_map/ppermute | solution.py:313
  71.3 0.2 collective-permute-done.34
  71.5 1.2 %collective-permute-start.38 = (bf16[128,512]{1,0:T(8,128)(2,1)S(1)}, bf16[128,512]{1,0:T(8,128)(2,1)S(1)}, u32[]{:S(2)}, u32[]{:S(2)}) collective-permute-start(bf16[128,512]{1,0:T(8,128)(2,1)S(1)} %collective-permute-done.34), channel_id=1, source_target_pairs={{0,8},{2,6},{8,16},{10,2},{16,24},{18,10},{24,28},{26,18},{28,20},... | collective-permute-start | bytes 393224 | tf_op jit(solution)/shard_map/ppermute | solution.py:313
  72.7 0.2 collective-permute-done.24
  72.9 0.5 collective-permute-start.25
  73.5 1.3 %collective-permute-done.40 = bf16[128,512]{1,0:T(8,128)(2,1)S(1)} collective-permute-done((bf16[128,512]{1,0:T(8,128)(2,1)S(1)}, bf16[128,512]{1,0:T(8,128)(2,1)S(1)}, u32[]{:S(2)}, u32[]{:S(2)}) %collective-permute-start.40) | collective-permute-done | bytes 131104 | tf_op jit(solution)/shard_map/ppermute | solution.py:313
  74.8 1.7 %collective-permute-done.38 = bf16[128,512]{1,0:T(8,128)(2,1)S(1)} collective-permute-done((bf16[128,512]{1,0:T(8,128)(2,1)S(1)}, bf16[128,512]{1,0:T(8,128)(2,1)S(1)}, u32[]{:S(2)}, u32[]{:S(2)}) %collective-permute-start.38) | collective-permute-done | bytes 131104 | tf_op jit(solution)/shard_map/ppermute | solution.py:313
  76.6 1.2 %collective-permute-done.39 = bf16[128,512]{1,0:T(8,128)(2,1)S(1)} collective-permute-done((bf16[128,512]{1,0:T(8,128)(2,1)S(1)}, bf16[128,512]{1,0:T(8,128)(2,1)S(1)}, u32[]{:S(2)}, u32[]{:S(2)}) %collective-permute-start.39) | collective-permute-done | bytes 131104 | tf_op jit(solution)/shard_map/ppermute | solution.py:244
  78.0 2.7 %maximum_select_fusion = bf16[8,256,1024]{2,1,0:T(8,128)(2,1)} fusion(bf16[8,256,512]{2,1,0:T(8,128)(2,1)S(1)} %bitcast.75, bf16[8,256,512]{2,1,0:T(8,128)(2,1)S(1)} %bitcast.76, pred[]{:T(512)S(6)} %eq.44), kind=kLoop, calls=%fused_computation | loop fusion | flops 18874368 | bytes 8388609 | tf_op jit(solution)/shard_map/jit(_where)/select_n | solution.py:335
  (83 shorter events, 1.3 us)
Async XLA Ops:
  0.6 15.1 %collective-permute-start = (bf16[128,512]{1,0:T(8,128)(2,1)}, bf16[128,512]{1,0:T(8,128)(2,1)S(1)}, u32[]{:S(2)}, u32[]{:S(2)}) collective-permute-start(bf16[128,512]{1,0:T(8,128)(2,1)} %param.5), channel_id=1, source_target_pairs={{0,16},{2,18},{4,20},{6,22},{8,24},{10,26},{12,28},{14,30},{16,0},... | collective-permute-start | bytes 393224 | tf_op jit(solution)/shard_map/ppermute | solution.py:275
  4.8 1.2 %copy-start = (bf16[128,4096]{1,0:T(8,128)(2,1)S(1)}, bf16[128,4096]{1,0:T(8,128)(2,1)}, u32[]{:S(2)}) copy-start(bf16[128,4096]{1,0:T(8,128)(2,1)} %inputs_ref.1) | copy-start | bytes 3145732
  6.6 16.4 %collective-permute-start.1 = (bf16[128,512]{1,0:T(8,128)(2,1)S(1)}, bf16[128,512]{1,0:T(8,128)(2,1)S(1)}, u32[]{:S(2)}, u32[]{:S(2)}) collective-permute-start(bf16[128,512]{1,0:T(8,128)(2,1)S(1)} %get-tuple-element.14), channel_id=1, source_target_pairs={{0,4},{2,6},{4,0},{6,2},{8,12},{10,14},{12,8},{14,10},{16,20},{18,... | collective-permute-start | bytes 393224 | tf_op jit(solution)/shard_map/ppermute | solution.py:275
  8.2 12.4 %collective-permute-start.2 = (bf16[128,512]{1,0:T(8,128)(2,1)S(1)}, bf16[128,512]{1,0:T(8,128)(2,1)S(1)}, u32[]{:S(2)}, u32[]{:S(2)}) collective-permute-start(bf16[128,512]{1,0:T(8,128)(2,1)S(1)} %get-tuple-element.15), channel_id=1, source_target_pairs={{0,16},{1,21},{2,18},{3,23},{4,20},{5,17},{6,22},{7,19},{8,24},{9,... | collective-permute-start | bytes 393224 | tf_op jit(solution)/shard_map/ppermute | solution.py:259
  8.6 14.5 %collective-permute-start.3 = (bf16[128,512]{1,0:T(8,128)(2,1)S(1)}, bf16[128,512]{1,0:T(8,128)(2,1)S(1)}, u32[]{:S(2)}, u32[]{:S(2)}) collective-permute-start(bf16[128,512]{1,0:T(8,128)(2,1)S(1)} %get-tuple-element.16), channel_id=1, source_target_pairs={{0,28},{1,25},{2,30},{3,27},{4,24},{5,29},{6,26},{7,31},{8,20},{9,... | collective-permute-start | bytes 393224 | tf_op jit(solution)/shard_map/ppermute | solution.py:259
  12.1 3.6 %copy-start.1 = (bf16[128,512]{1,0:T(8,128)(2,1)S(1)}, bf16[128,512]{1,0:T(8,128)(2,1)}, u32[]{:S(2)}) copy-start(bf16[128,512]{1,0:T(8,128)(2,1)} %param.5) | copy-start | bytes 393220
  12.1 13.0 %collective-permute-start.4 = (bf16[128,512]{1,0:T(8,128)(2,1)S(1)}, bf16[128,512]{1,0:T(8,128)(2,1)S(1)}, u32[]{:S(2)}, u32[]{:S(2)}) collective-permute-start(bf16[128,512]{1,0:T(8,128)(2,1)S(1)} %get-tuple-element.17), channel_id=1, source_target_pairs={{0,8},{1,13},{2,10},{3,15},{4,12},{5,9},{6,14},{7,11},{8,0},{9,5},... | collective-permute-start | bytes 393224 | tf_op jit(solution)/shard_map/ppermute | solution.py:259
  15.8 16.4 %collective-permute-start.10 = (bf16[256,512]{1,0:T(8,128)(2,1)S(1)}, bf16[256,512]{1,0:T(8,128)(2,1)S(1)}, u32[]{:S(2)}, u32[]{:S(2)}) collective-permute-start(bf16[256,512]{1,0:T(8,128)(2,1)S(1)} %constant_dynamic-update-slice_fusion.refs_6_), channel_id=1, source_target_pairs={{0,4},{2,6},{4,0},{6,2},{8,12},{10,14},{12,8},{14,10},{16,20},{18,... | collective-permute-start | bytes 786440 | tf_op jit(solution)/shard_map/ppermute | solution.py:275
  20.6 5.4 %collective-permute-start.5 = (bf16[128,512]{1,0:T(8,128)(2,1)S(1)}, bf16[128,512]{1,0:T(8,128)(2,1)S(1)}, u32[]{:S(2)}, u32[]{:S(2)}) collective-permute-start(bf16[128,512]{1,0:T(8,128)(2,1)S(1)} %collective-permute-done.2.refs_0_), channel_id=1, source_target_pairs={{0,1},{1,0},{2,3},{3,2},{4,5},{5,4},{6,7},{7,6},{8,9},{9,8},{10,11... | collective-permute-start | bytes 393224 | tf_op jit(solution)/shard_map/ppermute | solution.py:247
  23.0 9.1 %collective-permute-start.9 = (bf16[256,512]{1,0:T(8,128)(2,1)S(1)}, bf16[256,512]{1,0:T(8,128)(2,1)S(1)}, u32[]{:S(2)}, u32[]{:S(2)}) collective-permute-start(bf16[256,512]{1,0:T(8,128)(2,1)S(1)} %constant_dynamic-update-slice_fusion.refs_6_), channel_id=1, source_target_pairs={{0,8},{2,10},{4,12},{6,14},{8,0},{10,2},{12,4},{14,6},{16,24},{18,... | collective-permute-start | bytes 786440 | tf_op jit(solution)/shard_map/ppermute | solution.py:275
  23.1 11.7 %collective-permute-start.8 = (bf16[256,512]{1,0:T(8,128)(2,1)S(1)}, bf16[256,512]{1,0:T(8,128)(2,1)S(1)}, u32[]{:S(2)}, u32[]{:S(2)}) collective-permute-start(bf16[256,512]{1,0:T(8,128)(2,1)S(1)} %constant_dynamic-update-slice_fusion.refs_6_), channel_id=1, source_target_pairs={{0,12},{2,14},{4,8},{6,10},{8,4},{10,6},{12,0},{14,2},{16,28},{18,... | collective-permute-start | bytes 786440 | tf_op jit(solution)/shard_map/ppermute | solution.py:275
  25.1 5.7 %collective-permute-start.6 = (bf16[128,512]{1,0:T(8,128)(2,1)S(1)}, bf16[128,512]{1,0:T(8,128)(2,1)S(1)}, u32[]{:S(2)}, u32[]{:S(2)}) collective-permute-start(bf16[128,512]{1,0:T(8,128)(2,1)S(1)} %collective-permute-done.3.refs_1_), channel_id=1, source_target_pairs={{0,1},{1,0},{2,3},{3,2},{4,5},{5,4},{6,7},{7,6},{8,9},{9,8},{10,11... | collective-permute-start | bytes 393224 | tf_op jit(solution)/shard_map/ppermute | solution.py:247
  26.0 6.2 %collective-permute-start.7 = (bf16[128,512]{1,0:T(8,128)(2,1)S(1)}, bf16[128,512]{1,0:T(8,128)(2,1)S(1)}, u32[]{:S(2)}, u32[]{:S(2)}) collective-permute-start(bf16[128,512]{1,0:T(8,128)(2,1)S(1)} %collective-permute-done.4.refs_2_), channel_id=1, source_target_pairs={{0,1},{1,0},{2,3},{3,2},{4,5},{5,4},{6,7},{7,6},{8,9},{9,8},{10,11... | collective-permute-start | bytes 393224 | tf_op jit(solution)/shard_map/ppermute | solution.py:247
  36.1 2.7 %collective-permute-start.11 = (f32[512,512]{1,0:T(8,128)S(1)}, f32[512,512]{1,0:T(8,128)S(1)}, u32[]{:S(2)}, u32[]{:S(2)}) collective-permute-start(f32[512,512]{1,0:T(8,128)S(1)} %shard_map.51.mine_ref), channel_id=1, source_target_pairs={{0,2},{2,0},{4,6},{6,4},{8,10},{10,8},{12,14},{14,12},{16,18},{18,... | collective-permute-start | bytes 3145736 | tf_op jit(solution)/shard_map/ppermute | solution.py:244
  46.3 5.6 %collective-permute-start.26 = (bf16[128,512]{1,0:T(8,128)(2,1)S(1)}, bf16[128,512]{1,0:T(8,128)(2,1)S(1)}, u32[]{:S(2)}, u32[]{:S(2)}) collective-permute-start(bf16[128,512]{1,0:T(8,128)(2,1)S(1)} %get-tuple-element.21), channel_id=1, source_target_pairs={{0,1},{1,0},{2,3},{3,2},{4,5},{5,4},{6,7},{7,6},{8,9},{9,8},{10,11... | collective-permute-start | bytes 393224 | tf_op jit(solution)/shard_map/ppermute | solution.py:247
  46.9 6.7 %collective-permute-start.12 = (bf16[128,512]{1,0:T(8,128)(2,1)S(1)}, bf16[128,512]{1,0:T(8,128)(2,1)S(1)}, u32[]{:S(2)}, u32[]{:S(2)}) collective-permute-start(bf16[128,512]{1,0:T(8,128)(2,1)S(1)} %get-tuple-element.19), channel_id=1, source_target_pairs={{0,8},{2,6},{8,16},{10,2},{16,24},{18,10},{24,28},{26,18},{28,20},... | collective-permute-start | bytes 393224 | tf_op jit(solution)/shard_map/ppermute | solution.py:313
  48.6 7.2 %collective-permute-start.14 = (bf16[128,512]{1,0:T(8,128)(2,1)S(1)}, bf16[128,512]{1,0:T(8,128)(2,1)S(1)}, u32[]{:S(2)}, u32[]{:S(2)}) collective-permute-start(bf16[128,512]{1,0:T(8,128)(2,1)S(1)} %get-tuple-element.20), channel_id=1, source_target_pairs={{0,8},{2,6},{8,16},{10,2},{16,24},{18,10},{24,28},{26,18},{28,20},... | collective-permute-start | bytes 393224 | tf_op jit(solution)/shard_map/ppermute | solution.py:313
  51.9 5.9 %collective-permute-start.28 = (bf16[128,512]{1,0:T(8,128)(2,1)S(1)}, bf16[128,512]{1,0:T(8,128)(2,1)S(1)}, u32[]{:S(2)}, u32[]{:S(2)}) collective-permute-start(bf16[128,512]{1,0:T(8,128)(2,1)S(1)} %collective-permute-done.26), channel_id=1, source_target_pairs={{0,8},{2,6},{8,16},{10,2},{16,24},{18,10},{24,28},{26,18},{28,20},... | collective-permute-start | bytes 393224 | tf_op jit(solution)/shard_map/ppermute | solution.py:313
  53.6 4.2 %collective-permute-start.27 = (bf16[128,512]{1,0:T(8,128)(2,1)S(1)}, bf16[128,512]{1,0:T(8,128)(2,1)S(1)}, u32[]{:S(2)}, u32[]{:S(2)}) collective-permute-start(bf16[128,512]{1,0:T(8,128)(2,1)S(1)} %collective-permute-done.26), channel_id=1, source_target_pairs={{0,2},{2,0},{4,6},{6,4},{8,10},{10,8},{12,14},{14,12},{16,18},{18,... | collective-permute-start | bytes 393224 | tf_op jit(solution)/shard_map/ppermute | solution.py:244
  53.6 5.9 %collective-permute-start.16 = (bf16[128,512]{1,0:T(8,128)(2,1)S(1)}, bf16[128,512]{1,0:T(8,128)(2,1)S(1)}, u32[]{:S(2)}, u32[]{:S(2)}) collective-permute-start(bf16[128,512]{1,0:T(8,128)(2,1)S(1)} %collective-permute-done.12), channel_id=1, source_target_pairs={{0,8},{2,6},{8,16},{10,2},{16,24},{18,10},{24,28},{26,18},{28,20},... | collective-permute-start | bytes 393224 | tf_op jit(solution)/shard_map/ppermute | solution.py:313
  55.8 3.6 %collective-permute-start.13 = (bf16[128,512]{1,0:T(8,128)(2,1)S(1)}, bf16[128,512]{1,0:T(8,128)(2,1)S(1)}, u32[]{:S(2)}, u32[]{:S(2)}) collective-permute-start(bf16[128,512]{1,0:T(8,128)(2,1)S(1)} %collective-permute-done.12), channel_id=1, source_target_pairs={{0,2},{2,0},{4,6},{6,4},{8,10},{10,8},{12,14},{14,12},{16,18},{18,... | collective-permute-start | bytes 393224 | tf_op jit(solution)/shard_map/ppermute | solution.py:244
  55.8 7.0 %collective-permute-start.18 = (bf16[128,512]{1,0:T(8,128)(2,1)S(1)}, bf16[128,512]{1,0:T(8,128)(2,1)S(1)}, u32[]{:S(2)}, u32[]{:S(2)}) collective-permute-start(bf16[128,512]{1,0:T(8,128)(2,1)S(1)} %collective-permute-done.14), channel_id=1, source_target_pairs={{0,8},{2,6},{8,16},{10,2},{16,24},{18,10},{24,28},{26,18},{28,20},... | collective-permute-start | bytes 393224 | tf_op jit(solution)/shard_map/ppermute | solution.py:313
  57.8 3.2 %collective-permute-start.15 = (bf16[128,512]{1,0:T(8,128)(2,1)S(1)}, bf16[128,512]{1,0:T(8,128)(2,1)S(1)}, u32[]{:S(2)}, u32[]{:S(2)}) collective-permute-start(bf16[128,512]{1,0:T(8,128)(2,1)S(1)} %collective-permute-done.14), channel_id=1, source_target_pairs={{0,2},{2,0},{4,6},{6,4},{8,10},{10,8},{12,14},{14,12},{16,18},{18,... | collective-permute-start | bytes 393224 | tf_op jit(solution)/shard_map/ppermute | solution.py:244
  57.9 6.6 %collective-permute-start.32 = (bf16[128,512]{1,0:T(8,128)(2,1)S(1)}, bf16[128,512]{1,0:T(8,128)(2,1)S(1)}, u32[]{:S(2)}, u32[]{:S(2)}) collective-permute-start(bf16[128,512]{1,0:T(8,128)(2,1)S(1)} %collective-permute-done.28), channel_id=1, source_target_pairs={{0,8},{2,6},{8,16},{10,2},{16,24},{18,10},{24,28},{26,18},{28,20},... | collective-permute-start | bytes 393224 | tf_op jit(solution)/shard_map/ppermute | solution.py:313
  59.5 3.4 %collective-permute-start.29 = (bf16[128,512]{1,0:T(8,128)(2,1)S(1)}, bf16[128,512]{1,0:T(8,128)(2,1)S(1)}, u32[]{:S(2)}, u32[]{:S(2)}) collective-permute-start(bf16[128,512]{1,0:T(8,128)(2,1)S(1)} %collective-permute-done.28), channel_id=1, source_target_pairs={{0,2},{2,0},{4,6},{6,4},{8,10},{10,8},{12,14},{14,12},{16,18},{18,... | collective-permute-start | bytes 393224 | tf_op jit(solution)/shard_map/ppermute | solution.py:244
  59.6 6.2 %collective-permute-start.30 = (bf16[128,512]{1,0:T(8,128)(2,1)S(1)}, bf16[128,512]{1,0:T(8,128)(2,1)S(1)}, u32[]{:S(2)}, u32[]{:S(2)}) collective-permute-start(bf16[128,512]{1,0:T(8,128)(2,1)S(1)} %collective-permute-done.27), channel_id=1, source_target_pairs={{0,8},{2,6},{8,16},{10,2},{16,24},{18,10},{24,28},{26,18},{28,20},... | collective-permute-start | bytes 393224 | tf_op jit(solution)/shard_map/ppermute | solution.py:313
  61.0 5.5 %collective-permute-start.20 = (bf16[128,512]{1,0:T(8,128)(2,1)S(1)}, bf16[128,512]{1,0:T(8,128)(2,1)S(1)}, u32[]{:S(2)}, u32[]{:S(2)}) collective-permute-start(bf16[128,512]{1,0:T(8,128)(2,1)S(1)} %collective-permute-done.16), channel_id=1, source_target_pairs={{0,8},{2,6},{8,16},{10,2},{16,24},{18,10},{24,28},{26,18},{28,20},... | collective-permute-start | bytes 393224 | tf_op jit(solution)/shard_map/ppermute | solution.py:313
  62.8 1.8 %collective-permute-start.17 = (bf16[128,512]{1,0:T(8,128)(2,1)S(1)}, bf16[128,512]{1,0:T(8,128)(2,1)S(1)}, u32[]{:S(2)}, u32[]{:S(2)}) collective-permute-start(bf16[128,512]{1,0:T(8,128)(2,1)S(1)} %collective-permute-done.16), channel_id=1, source_target_pairs={{0,2},{2,0},{4,6},{6,4},{8,10},{10,8},{12,14},{14,12},{16,18},{18,... | collective-permute-start | bytes 393224 | tf_op jit(solution)/shard_map/ppermute | solution.py:244
  62.9 6.4 %collective-permute-start.22 = (bf16[128,512]{1,0:T(8,128)(2,1)S(1)}, bf16[128,512]{1,0:T(8,128)(2,1)S(1)}, u32[]{:S(2)}, u32[]{:S(2)}) collective-permute-start(bf16[128,512]{1,0:T(8,128)(2,1)S(1)} %collective-permute-done.18), channel_id=1, source_target_pairs={{0,8},{2,6},{8,16},{10,2},{16,24},{18,10},{24,28},{26,18},{28,20},... | collective-permute-start | bytes 393224 | tf_op jit(solution)/shard_map/ppermute | solution.py:313
  64.5 1.5 %collective-permute-start.19 = (bf16[128,512]{1,0:T(8,128)(2,1)S(1)}, bf16[128,512]{1,0:T(8,128)(2,1)S(1)}, u32[]{:S(2)}, u32[]{:S(2)}) collective-permute-start(bf16[128,512]{1,0:T(8,128)(2,1)S(1)} %collective-permute-done.18), channel_id=1, source_target_pairs={{0,2},{2,0},{4,6},{6,4},{8,10},{10,8},{12,14},{14,12},{16,18},{18,... | collective-permute-start | bytes 393224 | tf_op jit(solution)/shard_map/ppermute | solution.py:244
  64.6 5.0 %collective-permute-start.36 = (bf16[128,512]{1,0:T(8,128)(2,1)S(1)}, bf16[128,512]{1,0:T(8,128)(2,1)S(1)}, u32[]{:S(2)}, u32[]{:S(2)}) collective-permute-start(bf16[128,512]{1,0:T(8,128)(2,1)S(1)} %collective-permute-done.32), channel_id=1, source_target_pairs={{0,8},{2,6},{8,16},{10,2},{16,24},{18,10},{24,28},{26,18},{28,20},... | collective-permute-start | bytes 393224 | tf_op jit(solution)/shard_map/ppermute | solution.py:313
  65.9 4.0 %collective-permute-start.33 = (bf16[128,512]{1,0:T(8,128)(2,1)S(1)}, bf16[128,512]{1,0:T(8,128)(2,1)S(1)}, u32[]{:S(2)}, u32[]{:S(2)}) collective-permute-start(bf16[128,512]{1,0:T(8,128)(2,1)S(1)} %collective-permute-done.32), channel_id=1, source_target_pairs={{0,2},{2,0},{4,6},{6,4},{8,10},{10,8},{12,14},{14,12},{16,18},{18,... | collective-permute-start | bytes 393224 | tf_op jit(solution)/shard_map/ppermute | solution.py:244
  65.9 1.8 %collective-permute-start.31 = (bf16[128,512]{1,0:T(8,128)(2,1)S(1)}, bf16[128,512]{1,0:T(8,128)(2,1)S(1)}, u32[]{:S(2)}, u32[]{:S(2)}) collective-permute-start(bf16[128,512]{1,0:T(8,128)(2,1)S(1)} %collective-permute-done.30), channel_id=1, source_target_pairs={{0,2},{2,0},{4,6},{6,4},{8,10},{10,8},{12,14},{14,12},{16,18},{18,... | collective-permute-start | bytes 393224 | tf_op jit(solution)/shard_map/ppermute | solution.py:244
  66.5 5.0 %collective-permute-start.34 = (bf16[128,512]{1,0:T(8,128)(2,1)S(1)}, bf16[128,512]{1,0:T(8,128)(2,1)S(1)}, u32[]{:S(2)}, u32[]{:S(2)}) collective-permute-start(bf16[128,512]{1,0:T(8,128)(2,1)S(1)} %collective-permute-done.30), channel_id=1, source_target_pairs={{0,8},{2,6},{8,16},{10,2},{16,24},{18,10},{24,28},{26,18},{28,20},... | collective-permute-start | bytes 393224 | tf_op jit(solution)/shard_map/ppermute | solution.py:313
  67.7 5.2 %collective-permute-start.24 = (bf16[128,512]{1,0:T(8,128)(2,1)S(1)}, bf16[128,512]{1,0:T(8,128)(2,1)S(1)}, u32[]{:S(2)}, u32[]{:S(2)}) collective-permute-start(bf16[128,512]{1,0:T(8,128)(2,1)S(1)} %collective-permute-done.20), channel_id=1, source_target_pairs={{0,8},{2,6},{8,16},{10,2},{16,24},{18,10},{24,28},{26,18},{28,20},... | collective-permute-start | bytes 393224 | tf_op jit(solution)/shard_map/ppermute | solution.py:313
  69.3 2.3 %collective-permute-start.21 = (bf16[128,512]{1,0:T(8,128)(2,1)S(1)}, bf16[128,512]{1,0:T(8,128)(2,1)S(1)}, u32[]{:S(2)}, u32[]{:S(2)}) collective-permute-start(bf16[128,512]{1,0:T(8,128)(2,1)S(1)} %collective-permute-done.20), channel_id=1, source_target_pairs={{0,2},{2,0},{4,6},{6,4},{8,10},{10,8},{12,14},{14,12},{16,18},{18,... | collective-permute-start | bytes 393224 | tf_op jit(solution)/shard_map/ppermute | solution.py:244
  69.6 3.3 %collective-permute-start.23 = (bf16[128,512]{1,0:T(8,128)(2,1)S(1)}, bf16[128,512]{1,0:T(8,128)(2,1)S(1)}, u32[]{:S(2)}, u32[]{:S(2)}) collective-permute-start(bf16[128,512]{1,0:T(8,128)(2,1)S(1)} %collective-permute-done.22), channel_id=1, source_target_pairs={{0,2},{2,0},{4,6},{6,4},{8,10},{10,8},{12,14},{14,12},{16,18},{18,... | collective-permute-start | bytes 393224 | tf_op jit(solution)/shard_map/ppermute | solution.py:244
  69.8 5.0 %collective-permute-start.40 = (bf16[128,512]{1,0:T(8,128)(2,1)S(1)}, bf16[128,512]{1,0:T(8,128)(2,1)S(1)}, u32[]{:S(2)}, u32[]{:S(2)}) collective-permute-start(bf16[128,512]{1,0:T(8,128)(2,1)S(1)} %collective-permute-done.36), channel_id=1, source_target_pairs={{0,8},{2,6},{8,16},{10,2},{16,24},{18,10},{24,28},{26,18},{28,20},... | collective-permute-start | bytes 393224 | tf_op jit(solution)/shard_map/ppermute | solution.py:313
  71.5 5.0 %collective-permute-start.37 = (bf16[128,512]{1,0:T(8,128)(2,1)S(1)}, bf16[128,512]{1,0:T(8,128)(2,1)S(1)}, u32[]{:S(2)}, u32[]{:S(2)}) collective-permute-start(bf16[128,512]{1,0:T(8,128)(2,1)S(1)} %collective-permute-done.36), channel_id=1, source_target_pairs={{0,2},{2,0},{4,6},{6,4},{8,10},{10,8},{12,14},{14,12},{16,18},{18,... | collective-permute-start | bytes 393224 | tf_op jit(solution)/shard_map/ppermute | solution.py:244
  71.5 5.0 %collective-permute-start.38 = (bf16[128,512]{1,0:T(8,128)(2,1)S(1)}, bf16[128,512]{1,0:T(8,128)(2,1)S(1)}, u32[]{:S(2)}, u32[]{:S(2)}) collective-permute-start(bf16[128,512]{1,0:T(8,128)(2,1)S(1)} %collective-permute-done.34), channel_id=1, source_target_pairs={{0,8},{2,6},{8,16},{10,2},{16,24},{18,10},{24,28},{26,18},{28,20},... | collective-permute-start | bytes 393224 | tf_op jit(solution)/shard_map/ppermute | solution.py:313
  72.9 3.6 %collective-permute-start.35 = (bf16[128,512]{1,0:T(8,128)(2,1)S(1)}, bf16[128,512]{1,0:T(8,128)(2,1)S(1)}, u32[]{:S(2)}, u32[]{:S(2)}) collective-permute-start(bf16[128,512]{1,0:T(8,128)(2,1)S(1)} %collective-permute-done.34), channel_id=1, source_target_pairs={{0,2},{2,0},{4,6},{6,4},{8,10},{10,8},{12,14},{14,12},{16,18},{18,... | collective-permute-start | bytes 393224 | tf_op jit(solution)/shard_map/ppermute | solution.py:244
  72.9 5.0 %collective-permute-start.25 = (bf16[128,512]{1,0:T(8,128)(2,1)S(1)}, bf16[128,512]{1,0:T(8,128)(2,1)S(1)}, u32[]{:S(2)}, u32[]{:S(2)}) collective-permute-start(bf16[128,512]{1,0:T(8,128)(2,1)S(1)} %collective-permute-done.24), channel_id=1, source_target_pairs={{0,2},{2,0},{4,6},{6,4},{8,10},{10,8},{12,14},{14,12},{16,18},{18,... | collective-permute-start | bytes 393224 | tf_op jit(solution)/shard_map/ppermute | solution.py:244
  74.8 3.1 %collective-permute-start.41 = (bf16[128,512]{1,0:T(8,128)(2,1)S(1)}, bf16[128,512]{1,0:T(8,128)(2,1)S(1)}, u32[]{:S(2)}, u32[]{:S(2)}) collective-permute-start(bf16[128,512]{1,0:T(8,128)(2,1)S(1)} %collective-permute-done.40), channel_id=1, source_target_pairs={{0,2},{2,0},{4,6},{6,4},{8,10},{10,8},{12,14},{14,12},{16,18},{18,... | collective-permute-start | bytes 393224 | tf_op jit(solution)/shard_map/ppermute | solution.py:244
  76.5 1.3 %collective-permute-start.39 = (bf16[128,512]{1,0:T(8,128)(2,1)S(1)}, bf16[128,512]{1,0:T(8,128)(2,1)S(1)}, u32[]{:S(2)}, u32[]{:S(2)}) collective-permute-start(bf16[128,512]{1,0:T(8,128)(2,1)S(1)} %collective-permute-done.38), channel_id=1, source_target_pairs={{0,2},{2,0},{4,6},{6,4},{8,10},{10,8},{12,14},{14,12},{16,18},{18,... | collective-permute-start | bytes 393224 | tf_op jit(solution)/shard_map/ppermute | solution.py:244

commit v13 on v11

--- a/solution.py
+++ b/solution.py
@@ -274,9 +274,10 @@
         return lax.ppermute(array, "dp", pairs)
 
     outputs = jnp.dot(inputs, weight, preferred_element_type=jnp.float32).astype(jnp.bfloat16)
-    far_cot, outputs = lax.optimization_barrier((exchange(cotangent, 4), outputs))
+    far_cot, outputs, shared = lax.optimization_barrier(
+        (exchange(cotangent, 4), outputs, exchange(packed[-1], SHARED))
+    )
     near = [deal(packed[hop], hop) for hop in hops]
-    shared = exchange(packed[-1], SHARED)
     pair = jnp.concatenate([cotangent, far_cot])
     cots = [pair] + [exchange(pair, offset) for offset in (1, 2, 3)]
     far = [swap_plane(piece) for piece in near]

time: 79.4 us -> 81.4 us (1.025)
  waiting for transfers between devices: 17.3 us -> 19.5 us
    ppermute x3, waiting for transfers between devices: 1.79 us -> 4.83 us  [deal(): return lax.ppermute(array, ('dp', 'pre'), pairs)]
    ppermute x4, starting transfers between devices: 6.98 us -> 5.22 us  [swap_plane(): lax.ppermute(array, 'pre', [(c, members - 1 - c) for c in range(members)])]
    ppermute x14, starting transfers between devices: 20.4 us -> 22 us  [turn(): return lax.ppermute(array, 'dp', pairs)]
    ppermute x14, waiting for transfers between devices: 4.28 us -> 2.96 us  [turn(): return lax.ppermute(array, 'dp', pairs)]
    ppermute x5, waiting for transfers between devices: 1.36 us -> 2.64 us  [exchange(): return lax.ppermute(array, 'dp', pairs)]
  transfers between devices with their start and end apart: 42 -> 42, of which waited for: 15 -> 14; matrix products, arithmetic and copies ran while one was open for 6% -> 6% of each run, Pallas kernels for 1% -> 1%
where the time goes in v13:
time: 81.4 us; the launch traced here: 81.2 us
  starting transfers between devices  42.3 us (52%)
  waiting for transfers between devices  19.5 us (24%)
  Pallas kernels  9.42 us (12%)
  matrix products  3.6 us (4%)
  other arithmetic  2.81 us (3%)
  local copies, waits for them, and re-layouts  2.23 us (3%)
  between operations  1.4 us (2%)
    ppermute x14, starting transfers between devices, turn(): return lax.ppermute(array, 'dp', pairs)  22 us
    pallas_call x3, Pallas kernels, call(): pl.pallas_call(kernel, out_shape=out_shapes, in_specs=in_specs, out_specs...  9.42 us
    ppermute x5, starting transfers between devices, exchange(): return lax.ppermute(array, 'dp', pairs)  9.18 us
    ppermute x4, waiting for transfers between devices, swap_plane(): lax.ppermute(array, 'pre', [(c, members - 1 - c) for c in range(members)])  5.41 us
    ppermute x4, starting transfers between devices, swap_plane(): lax.ppermute(array, 'pre', [(c, members - 1 - c) for c in range(members)])  5.22 us
    ppermute x3, waiting for transfers between devices, deal(): return lax.ppermute(array, ('dp', 'pre'), pairs)  4.83 us
    ppermute x3, starting transfers between devices, deal(): return lax.ppermute(array, ('dp', 'pre'), pairs)  3.88 us
    ppermute x16, waiting for transfers between devices, swap_core(): return lax.ppermute(array, 'dp', [(g, g ^ 1) for g in range(groups)])  3.61 us
  transfers between devices with their start and end apart: 42, of which 14 were waited for; matrix products, arithmetic and copies ran while one was open for 6% of the time, Pallas kernels for 1%

profile of v13, /device:TPU:0, one launch (start us, length us, event | category | flops | bytes accessed | tf_op | source)
XLA Modules:
  0.0 81.2 jit_solution(3116991317213905019)
XLA Ops:
  0.6 4.1 %collective-permute-start = (bf16[128,512]{1,0:T(8,128)(2,1)}, bf16[128,512]{1,0:T(8,128)(2,1)S(1)}, u32[]{:S(2)}, u32[]{:S(2)}) collective-permute-start(bf16[128,512]{1,0:T(8,128)(2,1)} %param.5), channel_id=1, source_target_pairs={{0,16},{2,18},{4,20},{6,22},{8,24},{10,26},{12,28},{14,30},{16,0},... | collective-permute-start | bytes 393224 | tf_op jit(solution)/shard_map/ppermute | solution.py:274
  4.7 0.1 stack.37.place_ref
  4.8 1.2 %copy-done = bf16[128,4096]{1,0:T(8,128)(2,1)S(1)} copy-done((bf16[128,4096]{1,0:T(8,128)(2,1)S(1)}, bf16[128,4096]{1,0:T(8,128)(2,1)}, u32[]{:S(2)}) %copy-start) | copy-done | bytes 1048600
  6.0 0.6 shard_map.50
  6.6 1.6 %collective-permute-start.1 = (bf16[128,512]{1,0:T(8,128)(2,1)S(1)}, bf16[128,512]{1,0:T(8,128)(2,1)S(1)}, u32[]{:S(2)}, u32[]{:S(2)}) collective-permute-start(bf16[128,512]{1,0:T(8,128)(2,1)S(1)} %get-tuple-element.13), channel_id=1, source_target_pairs={{0,4},{2,6},{4,0},{6,2},{8,12},{10,14},{12,8},{14,10},{16,20},{18,... | collective-permute-start | bytes 393224 | tf_op jit(solution)/shard_map/ppermute | solution.py:274
  8.2 0.3 collective-permute-start.2
  8.6 3.5 %collective-permute-start.3 = (bf16[128,512]{1,0:T(8,128)(2,1)S(1)}, bf16[128,512]{1,0:T(8,128)(2,1)S(1)}, u32[]{:S(2)}, u32[]{:S(2)}) collective-permute-start(bf16[128,512]{1,0:T(8,128)(2,1)S(1)} %get-tuple-element.18), channel_id=1, source_target_pairs={{0,28},{1,25},{2,30},{3,27},{4,24},{5,29},{6,26},{7,31},{8,20},{9,... | collective-permute-start | bytes 393224 | tf_op jit(solution)/shard_map/ppermute | solution.py:258
  12.1 3.6 %convolution_convert_fusion = bf16[128,512]{1,0:T(8,128)(2,1)} fusion(bf16[128,4096]{1,0:T(8,128)(2,1)S(1)} %copy-done, bf16[4096,512]{1,0:T(8,128)(2,1)} %param.4), kind=kOutput, calls=%fused_computation.1 | convolution fusion | flops 536936448 | bytes 5373952 | tf_op jit(solution)/shard_map/dot_general | solution.py:276
  15.8 4.8 %collective-permute-done.2.refs_0_ = bf16[128,512]{1,0:T(8,128)(2,1)S(1)} collective-permute-done((bf16[128,512]{1,0:T(8,128)(2,1)S(1)}, bf16[128,512]{1,0:T(8,128)(2,1)S(1)}, u32[]{:S(2)}, u32[]{:S(2)}) %collective-permute-start.2) | collective-permute-done | bytes 131104 | tf_op jit(solution)/shard_map/ppermute | solution.py:258
  20.6 2.4 %collective-permute-start.5 = (bf16[128,512]{1,0:T(8,128)(2,1)S(1)}, bf16[128,512]{1,0:T(8,128)(2,1)S(1)}, u32[]{:S(2)}, u32[]{:S(2)}) collective-permute-start(bf16[128,512]{1,0:T(8,128)(2,1)S(1)} %collective-permute-done.2.refs_0_), channel_id=1, source_target_pairs={{0,1},{1,0},{2,3},{3,2},{4,5},{5,4},{6,7},{7,6},{8,9},{9,8},{10,11... | collective-permute-start | bytes 393224 | tf_op jit(solution)/shard_map/ppermute | solution.py:246
  23.0 2.0 %collective-permute-start.9 = (bf16[256,512]{1,0:T(8,128)(2,1)S(1)}, bf16[256,512]{1,0:T(8,128)(2,1)S(1)}, u32[]{:S(2)}, u32[]{:S(2)}) collective-permute-start(bf16[256,512]{1,0:T(8,128)(2,1)S(1)} %constant_dynamic-update-slice_fusion.refs_6_), channel_id=1, source_target_pairs={{0,8},{2,10},{4,12},{6,14},{8,0},{10,2},{12,4},{14,6},{16,24},{18,... | collective-permute-start | bytes 786440 | tf_op jit(solution)/shard_map/ppermute | solution.py:274
  25.0 1.5 %collective-permute-start.8 = (bf16[256,512]{1,0:T(8,128)(2,1)S(1)}, bf16[256,512]{1,0:T(8,128)(2,1)S(1)}, u32[]{:S(2)}, u32[]{:S(2)}) collective-permute-start(bf16[256,512]{1,0:T(8,128)(2,1)S(1)} %constant_dynamic-update-slice_fusion.refs_6_), channel_id=1, source_target_pairs={{0,4},{2,6},{4,0},{6,2},{8,12},{10,14},{12,8},{14,10},{16,20},{18,... | collective-permute-start | bytes 786440 | tf_op jit(solution)/shard_map/ppermute | solution.py:274
  26.5 0.4 collective-permute-done.5.refs_3_
  26.9 2.5 %collective-permute-start.7 = (bf16[128,512]{1,0:T(8,128)(2,1)S(1)}, bf16[128,512]{1,0:T(8,128)(2,1)S(1)}, u32[]{:S(2)}, u32[]{:S(2)}) collective-permute-start(bf16[128,512]{1,0:T(8,128)(2,1)S(1)} %collective-permute-done.4.refs_2_), channel_id=1, source_target_pairs={{0,1},{1,0},{2,3},{3,2},{4,5},{5,4},{6,7},{7,6},{8,9},{9,8},{10,11... | collective-permute-start | bytes 393224 | tf_op jit(solution)/shard_map/ppermute | solution.py:246
  29.4 2.0 %collective-permute-done.6.refs_4_ = bf16[128,512]{1,0:T(8,128)(2,1)S(1)} collective-permute-done((bf16[128,512]{1,0:T(8,128)(2,1)S(1)}, bf16[128,512]{1,0:T(8,128)(2,1)S(1)}, u32[]{:S(2)}, u32[]{:S(2)}) %collective-permute-start.6) | collective-permute-done | bytes 131104 | tf_op jit(solution)/shard_map/ppermute | solution.py:246
  31.5 1.4 %collective-permute-done.7.refs_5_ = bf16[128,512]{1,0:T(8,128)(2,1)S(1)} collective-permute-done((bf16[128,512]{1,0:T(8,128)(2,1)S(1)}, bf16[128,512]{1,0:T(8,128)(2,1)S(1)}, u32[]{:S(2)}, u32[]{:S(2)}) %collective-permute-start.7) | collective-permute-done | bytes 131104 | tf_op jit(solution)/shard_map/ppermute | solution.py:246
  32.9 1.8 %collective-permute-done.9.refs_8_ = bf16[256,512]{1,0:T(8,128)(2,1)S(1)} collective-permute-done((bf16[256,512]{1,0:T(8,128)(2,1)S(1)}, bf16[256,512]{1,0:T(8,128)(2,1)S(1)}, u32[]{:S(2)}, u32[]{:S(2)}) %collective-permute-start.9) | collective-permute-done | bytes 262176 | tf_op jit(solution)/shard_map/ppermute | solution.py:274
  34.6 0.9 %collective-permute-done.8.refs_7_ = bf16[256,512]{1,0:T(8,128)(2,1)S(1)} collective-permute-done((bf16[256,512]{1,0:T(8,128)(2,1)S(1)}, bf16[256,512]{1,0:T(8,128)(2,1)S(1)}, u32[]{:S(2)}, u32[]{:S(2)}) %collective-permute-start.8) | collective-permute-done | bytes 262176 | tf_op jit(solution)/shard_map/ppermute | solution.py:274
  35.5 1.4 %shard_map.51.mine_ref = f32[512,512]{1,0:T(8,128)S(1)} custom-call(s32[2]{0:T(128)S(1)} %pad_add_fusion.1.place_ref, bf16[128,512]{1,0:T(8,128)(2,1)S(1)} %get-tuple-element.15.own_ref, bf16[128,512]{1,0:T(8,128)(2,1)S(1)} %collective-permute-done.1.shared_ref, bf16[128,512]{1,0:T(8,128)(2,1)S(1)} %collective-permute-done.2.refs_0_, ...), custom_call_target="tpu_custom_call" | custom-call | tf_op jit(solution)/shard_map/pallas_call | solution.py:218
  37.3 0.1 pad_add_fusion.side_ref
  37.3 2.3 %collective-permute-done.11.other_ref = f32[512,512]{1,0:T(8,128)S(1)} collective-permute-done((f32[512,512]{1,0:T(8,128)S(1)}, f32[512,512]{1,0:T(8,128)S(1)}, u32[]{:S(2)}, u32[]{:S(2)}) %collective-permute-start.11) | collective-permute-done | bytes 1048608 | tf_op jit(solution)/shard_map/ppermute | solution.py:243
  39.6 7.4 %shard_map.52 = (bf16[128,512]{1,0:T(8,128)(2,1)S(1)}, bf16[128,512]{1,0:T(8,128)(2,1)S(1)}, bf16[128,512]{1,0:T(8,128)(2,1)S(1)}) custom-call(s32[2]{0:T(128)S(1)} %pad_add_fusion.side_ref, f32[512,512]{1,0:T(8,128)S(1)} %shard_map.51.mine_ref, f32[512,512]{1,0:T(8,128)S(1)} %collective-permute-done.11.other_ref), custom_call_target="tpu_custom_call" | custom-call | tf_op jit(solution)/shard_map/pallas_call | solution.py:218
  47.1 0.3 collective-permute-start.26
  47.4 1.3 %collective-permute-start.12 = (bf16[128,512]{1,0:T(8,128)(2,1)S(1)}, bf16[128,512]{1,0:T(8,128)(2,1)S(1)}, u32[]{:S(2)}, u32[]{:S(2)}) collective-permute-start(bf16[128,512]{1,0:T(8,128)(2,1)S(1)} %get-tuple-element.21), channel_id=1, source_target_pairs={{0,8},{2,6},{8,16},{10,2},{16,24},{18,10},{24,28},{26,18},{28,20},... | collective-permute-start | bytes 393224 | tf_op jit(solution)/shard_map/ppermute | solution.py:313
  48.7 2.1 %collective-permute-start.14 = (bf16[128,512]{1,0:T(8,128)(2,1)S(1)}, bf16[128,512]{1,0:T(8,128)(2,1)S(1)}, u32[]{:S(2)}, u32[]{:S(2)}) collective-permute-start(bf16[128,512]{1,0:T(8,128)(2,1)S(1)} %get-tuple-element.22), channel_id=1, source_target_pairs={{0,8},{2,6},{8,16},{10,2},{16,24},{18,10},{24,28},{26,18},{28,20},... | collective-permute-start | bytes 393224 | tf_op jit(solution)/shard_map/ppermute | solution.py:313
  50.8 0.2 broadcast_in_dim.99.clone.1
  51.1 1.6 %collective-permute-done.26 = bf16[128,512]{1,0:T(8,128)(2,1)S(1)} collective-permute-done((bf16[128,512]{1,0:T(8,128)(2,1)S(1)}, bf16[128,512]{1,0:T(8,128)(2,1)S(1)}, u32[]{:S(2)}, u32[]{:S(2)}) %collective-permute-start.26) | collective-permute-done | bytes 131104 | tf_op jit(solution)/shard_map/ppermute | solution.py:246
  52.7 1.0 %collective-permute-start.28 = (bf16[128,512]{1,0:T(8,128)(2,1)S(1)}, bf16[128,512]{1,0:T(8,128)(2,1)S(1)}, u32[]{:S(2)}, u32[]{:S(2)}) collective-permute-start(bf16[128,512]{1,0:T(8,128)(2,1)S(1)} %collective-permute-done.26), channel_id=1, source_target_pairs={{0,8},{2,6},{8,16},{10,2},{16,24},{18,10},{24,28},{26,18},{28,20},... | collective-permute-start | bytes 393224 | tf_op jit(solution)/shard_map/ppermute | solution.py:313
  53.7 2.2 %collective-permute-start.16 = (bf16[128,512]{1,0:T(8,128)(2,1)S(1)}, bf16[128,512]{1,0:T(8,128)(2,1)S(1)}, u32[]{:S(2)}, u32[]{:S(2)}) collective-permute-start(bf16[128,512]{1,0:T(8,128)(2,1)S(1)} %collective-permute-done.12), channel_id=1, source_target_pairs={{0,8},{2,6},{8,16},{10,2},{16,24},{18,10},{24,28},{26,18},{28,20},... | collective-permute-start | bytes 393224 | tf_op jit(solution)/shard_map/ppermute | solution.py:313
  55.9 2.6 %collective-permute-start.18 = (bf16[128,512]{1,0:T(8,128)(2,1)S(1)}, bf16[128,512]{1,0:T(8,128)(2,1)S(1)}, u32[]{:S(2)}, u32[]{:S(2)}) collective-permute-start(bf16[128,512]{1,0:T(8,128)(2,1)S(1)} %collective-permute-done.14), channel_id=1, source_target_pairs={{0,8},{2,6},{8,16},{10,2},{16,24},{18,10},{24,28},{26,18},{28,20},... | collective-permute-start | bytes 393224 | tf_op jit(solution)/shard_map/ppermute | solution.py:313
  58.5 0.2 broadcast_in_dim.99.clone
  58.8 0.7 collective-permute-start.32
  59.7 1.7 %collective-permute-start.30 = (bf16[128,512]{1,0:T(8,128)(2,1)S(1)}, bf16[128,512]{1,0:T(8,128)(2,1)S(1)}, u32[]{:S(2)}, u32[]{:S(2)}) collective-permute-start(bf16[128,512]{1,0:T(8,128)(2,1)S(1)} %collective-permute-done.27), channel_id=1, source_target_pairs={{0,8},{2,6},{8,16},{10,2},{16,24},{18,10},{24,28},{26,18},{28,20},... | collective-permute-start | bytes 393224 | tf_op jit(solution)/shard_map/ppermute | solution.py:313
  61.3 2.3 %collective-permute-start.20 = (bf16[128,512]{1,0:T(8,128)(2,1)S(1)}, bf16[128,512]{1,0:T(8,128)(2,1)S(1)}, u32[]{:S(2)}, u32[]{:S(2)}) collective-permute-start(bf16[128,512]{1,0:T(8,128)(2,1)S(1)} %collective-permute-done.16), channel_id=1, source_target_pairs={{0,8},{2,6},{8,16},{10,2},{16,24},{18,10},{24,28},{26,18},{28,20},... | collective-permute-start | bytes 393224 | tf_op jit(solution)/shard_map/ppermute | solution.py:313
  63.8 1.2 %collective-permute-start.22 = (bf16[128,512]{1,0:T(8,128)(2,1)S(1)}, bf16[128,512]{1,0:T(8,128)(2,1)S(1)}, u32[]{:S(2)}, u32[]{:S(2)}) collective-permute-start(bf16[128,512]{1,0:T(8,128)(2,1)S(1)} %collective-permute-done.18), channel_id=1, source_target_pairs={{0,8},{2,6},{8,16},{10,2},{16,24},{18,10},{24,28},{26,18},{28,20},... | collective-permute-start | bytes 393224 | tf_op jit(solution)/shard_map/ppermute | solution.py:313
  65.2 1.1 %collective-permute-start.36 = (bf16[128,512]{1,0:T(8,128)(2,1)S(1)}, bf16[128,512]{1,0:T(8,128)(2,1)S(1)}, u32[]{:S(2)}, u32[]{:S(2)}) collective-permute-start(bf16[128,512]{1,0:T(8,128)(2,1)S(1)} %collective-permute-done.32), channel_id=1, source_target_pairs={{0,8},{2,6},{8,16},{10,2},{16,24},{18,10},{24,28},{26,18},{28,20},... | collective-permute-start | bytes 393224 | tf_op jit(solution)/shard_map/ppermute | solution.py:313
  66.5 0.4 collective-permute-start.31
  67.0 1.6 %collective-permute-start.34 = (bf16[128,512]{1,0:T(8,128)(2,1)S(1)}, bf16[128,512]{1,0:T(8,128)(2,1)S(1)}, u32[]{:S(2)}, u32[]{:S(2)}) collective-permute-start(bf16[128,512]{1,0:T(8,128)(2,1)S(1)} %collective-permute-done.30), channel_id=1, source_target_pairs={{0,8},{2,6},{8,16},{10,2},{16,24},{18,10},{24,28},{26,18},{28,20},... | collective-permute-start | bytes 393224 | tf_op jit(solution)/shard_map/ppermute | solution.py:313
  68.6 1.4 %collective-permute-start.24 = (bf16[128,512]{1,0:T(8,128)(2,1)S(1)}, bf16[128,512]{1,0:T(8,128)(2,1)S(1)}, u32[]{:S(2)}, u32[]{:S(2)}) collective-permute-start(bf16[128,512]{1,0:T(8,128)(2,1)S(1)} %collective-permute-done.20), channel_id=1, source_target_pairs={{0,8},{2,6},{8,16},{10,2},{16,24},{18,10},{24,28},{26,18},{28,20},... | collective-permute-start | bytes 393224 | tf_op jit(solution)/shard_map/ppermute | solution.py:313
  70.2 0.4 collective-permute-start.23
  70.7 1.2 %collective-permute-start.40 = (bf16[128,512]{1,0:T(8,128)(2,1)S(1)}, bf16[128,512]{1,0:T(8,128)(2,1)S(1)}, u32[]{:S(2)}, u32[]{:S(2)}) collective-permute-start(bf16[128,512]{1,0:T(8,128)(2,1)S(1)} %collective-permute-done.36), channel_id=1, source_target_pairs={{0,8},{2,6},{8,16},{10,2},{16,24},{18,10},{24,28},{26,18},{28,20},... | collective-permute-start | bytes 393224 | tf_op jit(solution)/shard_map/ppermute | solution.py:313
  71.9 0.1 collective-permute-done.34
  72.0 1.6 %collective-permute-start.38 = (bf16[128,512]{1,0:T(8,128)(2,1)S(1)}, bf16[128,512]{1,0:T(8,128)(2,1)S(1)}, u32[]{:S(2)}, u32[]{:S(2)}) collective-permute-start(bf16[128,512]{1,0:T(8,128)(2,1)S(1)} %collective-permute-done.34), channel_id=1, source_target_pairs={{0,8},{2,6},{8,16},{10,2},{16,24},{18,10},{24,28},{26,18},{28,20},... | collective-permute-start | bytes 393224 | tf_op jit(solution)/shard_map/ppermute | solution.py:313
  73.8 0.5 collective-permute-start.25
  74.3 1.4 %collective-permute-done.40 = bf16[128,512]{1,0:T(8,128)(2,1)S(1)} collective-permute-done((bf16[128,512]{1,0:T(8,128)(2,1)S(1)}, bf16[128,512]{1,0:T(8,128)(2,1)S(1)}, u32[]{:S(2)}, u32[]{:S(2)}) %collective-permute-start.40) | collective-permute-done | bytes 131104 | tf_op jit(solution)/shard_map/ppermute | solution.py:313
  75.7 1.4 %collective-permute-done.38 = bf16[128,512]{1,0:T(8,128)(2,1)S(1)} collective-permute-done((bf16[128,512]{1,0:T(8,128)(2,1)S(1)}, bf16[128,512]{1,0:T(8,128)(2,1)S(1)}, u32[]{:S(2)}, u32[]{:S(2)}) %collective-permute-start.38) | collective-permute-done | bytes 131104 | tf_op jit(solution)/shard_map/ppermute | solution.py:313
  77.2 1.2 %collective-permute-done.39 = bf16[128,512]{1,0:T(8,128)(2,1)S(1)} collective-permute-done((bf16[128,512]{1,0:T(8,128)(2,1)S(1)}, bf16[128,512]{1,0:T(8,128)(2,1)S(1)}, u32[]{:S(2)}, u32[]{:S(2)}) %collective-permute-start.39) | collective-permute-done | bytes 131104 | tf_op jit(solution)/shard_map/ppermute | solution.py:243
  78.5 2.7 %maximum_select_fusion = bf16[8,256,1024]{2,1,0:T(8,128)(2,1)} fusion(bf16[8,256,512]{2,1,0:T(8,128)(2,1)S(1)} %bitcast.75, bf16[8,256,512]{2,1,0:T(8,128)(2,1)S(1)} %bitcast.76, pred[]{:T(512)S(6)} %eq.44), kind=kLoop, calls=%fused_computation | loop fusion | flops 18874368 | bytes 8388609 | tf_op jit(solution)/shard_map/jit(_where)/select_n | solution.py:335
  (83 shorter events, 1.4 us)
Async XLA Ops:
  0.6 15.1 %collective-permute-start = (bf16[128,512]{1,0:T(8,128)(2,1)}, bf16[128,512]{1,0:T(8,128)(2,1)S(1)}, u32[]{:S(2)}, u32[]{:S(2)}) collective-permute-start(bf16[128,512]{1,0:T(8,128)(2,1)} %param.5), channel_id=1, source_target_pairs={{0,16},{2,18},{4,20},{6,22},{8,24},{10,26},{12,28},{14,30},{16,0},... | collective-permute-start | bytes 393224 | tf_op jit(solution)/shard_map/ppermute | solution.py:274
  4.8 1.2 %copy-start = (bf16[128,4096]{1,0:T(8,128)(2,1)S(1)}, bf16[128,4096]{1,0:T(8,128)(2,1)}, u32[]{:S(2)}) copy-start(bf16[128,4096]{1,0:T(8,128)(2,1)} %inputs_ref.1) | copy-start | bytes 3145732
  6.6 9.1 %collective-permute-start.1 = (bf16[128,512]{1,0:T(8,128)(2,1)S(1)}, bf16[128,512]{1,0:T(8,128)(2,1)S(1)}, u32[]{:S(2)}, u32[]{:S(2)}) collective-permute-start(bf16[128,512]{1,0:T(8,128)(2,1)S(1)} %get-tuple-element.13), channel_id=1, source_target_pairs={{0,4},{2,6},{4,0},{6,2},{8,12},{10,14},{12,8},{14,10},{16,20},{18,... | collective-permute-start | bytes 393224 | tf_op jit(solution)/shard_map/ppermute | solution.py:274
  8.2 12.4 %collective-permute-start.2 = (bf16[128,512]{1,0:T(8,128)(2,1)S(1)}, bf16[128,512]{1,0:T(8,128)(2,1)S(1)}, u32[]{:S(2)}, u32[]{:S(2)}) collective-permute-start(bf16[128,512]{1,0:T(8,128)(2,1)S(1)} %get-tuple-element.17), channel_id=1, source_target_pairs={{0,16},{1,21},{2,18},{3,23},{4,20},{5,17},{6,22},{7,19},{8,24},{9,... | collective-permute-start | bytes 393224 | tf_op jit(solution)/shard_map/ppermute | solution.py:258
  8.6 16.4 %collective-permute-start.3 = (bf16[128,512]{1,0:T(8,128)(2,1)S(1)}, bf16[128,512]{1,0:T(8,128)(2,1)S(1)}, u32[]{:S(2)}, u32[]{:S(2)}) collective-permute-start(bf16[128,512]{1,0:T(8,128)(2,1)S(1)} %get-tuple-element.18), channel_id=1, source_target_pairs={{0,28},{1,25},{2,30},{3,27},{4,24},{5,29},{6,26},{7,31},{8,20},{9,... | collective-permute-start | bytes 393224 | tf_op jit(solution)/shard_map/ppermute | solution.py:258
  12.1 3.6 %copy-start.1 = (bf16[128,512]{1,0:T(8,128)(2,1)S(1)}, bf16[128,512]{1,0:T(8,128)(2,1)}, u32[]{:S(2)}) copy-start(bf16[128,512]{1,0:T(8,128)(2,1)} %param.5) | copy-start | bytes 393220
  12.1 14.4 %collective-permute-start.4 = (bf16[128,512]{1,0:T(8,128)(2,1)S(1)}, bf16[128,512]{1,0:T(8,128)(2,1)S(1)}, u32[]{:S(2)}, u32[]{:S(2)}) collective-permute-start(bf16[128,512]{1,0:T(8,128)(2,1)S(1)} %get-tuple-element.19), channel_id=1, source_target_pairs={{0,8},{1,13},{2,10},{3,15},{4,12},{5,9},{6,14},{7,11},{8,0},{9,5},... | collective-permute-start | bytes 393224 | tf_op jit(solution)/shard_map/ppermute | solution.py:258
  20.6 6.3 %collective-permute-start.5 = (bf16[128,512]{1,0:T(8,128)(2,1)S(1)}, bf16[128,512]{1,0:T(8,128)(2,1)S(1)}, u32[]{:S(2)}, u32[]{:S(2)}) collective-permute-start(bf16[128,512]{1,0:T(8,128)(2,1)S(1)} %collective-permute-done.2.refs_0_), channel_id=1, source_target_pairs={{0,1},{1,0},{2,3},{3,2},{4,5},{5,4},{6,7},{7,6},{8,9},{9,8},{10,11... | collective-permute-start | bytes 393224 | tf_op jit(solution)/shard_map/ppermute | solution.py:246
  23.0 9.9 %collective-permute-start.10 = (bf16[256,512]{1,0:T(8,128)(2,1)S(1)}, bf16[256,512]{1,0:T(8,128)(2,1)S(1)}, u32[]{:S(2)}, u32[]{:S(2)}) collective-permute-start(bf16[256,512]{1,0:T(8,128)(2,1)S(1)} %constant_dynamic-update-slice_fusion.refs_6_), channel_id=1, source_target_pairs={{0,12},{2,14},{4,8},{6,10},{8,4},{10,6},{12,0},{14,2},{16,28},{18,... | collective-permute-start | bytes 786440 | tf_op jit(solution)/shard_map/ppermute | solution.py:274
  23.0 11.6 %collective-permute-start.9 = (bf16[256,512]{1,0:T(8,128)(2,1)S(1)}, bf16[256,512]{1,0:T(8,128)(2,1)S(1)}, u32[]{:S(2)}, u32[]{:S(2)}) collective-permute-start(bf16[256,512]{1,0:T(8,128)(2,1)S(1)} %constant_dynamic-update-slice_fusion.refs_6_), channel_id=1, source_target_pairs={{0,8},{2,10},{4,12},{6,14},{8,0},{10,2},{12,4},{14,6},{16,24},{18,... | collective-permute-start | bytes 786440 | tf_op jit(solution)/shard_map/ppermute | solution.py:274
  25.0 10.5 %collective-permute-start.8 = (bf16[256,512]{1,0:T(8,128)(2,1)S(1)}, bf16[256,512]{1,0:T(8,128)(2,1)S(1)}, u32[]{:S(2)}, u32[]{:S(2)}) collective-permute-start(bf16[256,512]{1,0:T(8,128)(2,1)S(1)} %constant_dynamic-update-slice_fusion.refs_6_), channel_id=1, source_target_pairs={{0,4},{2,6},{4,0},{6,2},{8,12},{10,14},{12,8},{14,10},{16,20},{18,... | collective-permute-start | bytes 786440 | tf_op jit(solution)/shard_map/ppermute | solution.py:274
  26.5 5.0 %collective-permute-start.6 = (bf16[128,512]{1,0:T(8,128)(2,1)S(1)}, bf16[128,512]{1,0:T(8,128)(2,1)S(1)}, u32[]{:S(2)}, u32[]{:S(2)}) collective-permute-start(bf16[128,512]{1,0:T(8,128)(2,1)S(1)} %collective-permute-done.3.refs_1_), channel_id=1, source_target_pairs={{0,1},{1,0},{2,3},{3,2},{4,5},{5,4},{6,7},{7,6},{8,9},{9,8},{10,11... | collective-permute-start | bytes 393224 | tf_op jit(solution)/shard_map/ppermute | solution.py:246
  26.9 6.0 %collective-permute-start.7 = (bf16[128,512]{1,0:T(8,128)(2,1)S(1)}, bf16[128,512]{1,0:T(8,128)(2,1)S(1)}, u32[]{:S(2)}, u32[]{:S(2)}) collective-permute-start(bf16[128,512]{1,0:T(8,128)(2,1)S(1)} %collective-permute-done.4.refs_2_), channel_id=1, source_target_pairs={{0,1},{1,0},{2,3},{3,2},{4,5},{5,4},{6,7},{7,6},{8,9},{9,8},{10,11... | collective-permute-start | bytes 393224 | tf_op jit(solution)/shard_map/ppermute | solution.py:246
  36.9 2.7 %collective-permute-start.11 = (f32[512,512]{1,0:T(8,128)S(1)}, f32[512,512]{1,0:T(8,128)S(1)}, u32[]{:S(2)}, u32[]{:S(2)}) collective-permute-start(f32[512,512]{1,0:T(8,128)S(1)} %shard_map.51.mine_ref), channel_id=1, source_target_pairs={{0,2},{2,0},{4,6},{6,4},{8,10},{10,8},{12,14},{14,12},{16,18},{18,... | collective-permute-start | bytes 3145736 | tf_op jit(solution)/shard_map/ppermute | solution.py:243
  47.1 5.6 %collective-permute-start.26 = (bf16[128,512]{1,0:T(8,128)(2,1)S(1)}, bf16[128,512]{1,0:T(8,128)(2,1)S(1)}, u32[]{:S(2)}, u32[]{:S(2)}) collective-permute-start(bf16[128,512]{1,0:T(8,128)(2,1)S(1)} %get-tuple-element.23), channel_id=1, source_target_pairs={{0,1},{1,0},{2,3},{3,2},{4,5},{5,4},{6,7},{7,6},{8,9},{9,8},{10,11... | collective-permute-start | bytes 393224 | tf_op jit(solution)/shard_map/ppermute | solution.py:246
  47.4 6.3 %collective-permute-start.12 = (bf16[128,512]{1,0:T(8,128)(2,1)S(1)}, bf16[128,512]{1,0:T(8,128)(2,1)S(1)}, u32[]{:S(2)}, u32[]{:S(2)}) collective-permute-start(bf16[128,512]{1,0:T(8,128)(2,1)S(1)} %get-tuple-element.21), channel_id=1, source_target_pairs={{0,8},{2,6},{8,16},{10,2},{16,24},{18,10},{24,28},{26,18},{28,20},... | collective-permute-start | bytes 393224 | tf_op jit(solution)/shard_map/ppermute | solution.py:313
  48.7 7.2 %collective-permute-start.14 = (bf16[128,512]{1,0:T(8,128)(2,1)S(1)}, bf16[128,512]{1,0:T(8,128)(2,1)S(1)}, u32[]{:S(2)}, u32[]{:S(2)}) collective-permute-start(bf16[128,512]{1,0:T(8,128)(2,1)S(1)} %get-tuple-element.22), channel_id=1, source_target_pairs={{0,8},{2,6},{8,16},{10,2},{16,24},{18,10},{24,28},{26,18},{28,20},... | collective-permute-start | bytes 393224 | tf_op jit(solution)/shard_map/ppermute | solution.py:313
  52.7 6.0 %collective-permute-start.28 = (bf16[128,512]{1,0:T(8,128)(2,1)S(1)}, bf16[128,512]{1,0:T(8,128)(2,1)S(1)}, u32[]{:S(2)}, u32[]{:S(2)}) collective-permute-start(bf16[128,512]{1,0:T(8,128)(2,1)S(1)} %collective-permute-done.26), channel_id=1, source_target_pairs={{0,8},{2,6},{8,16},{10,2},{16,24},{18,10},{24,28},{26,18},{28,20},... | collective-permute-start | bytes 393224 | tf_op jit(solution)/shard_map/ppermute | solution.py:313
  53.7 5.1 %collective-permute-start.27 = (bf16[128,512]{1,0:T(8,128)(2,1)S(1)}, bf16[128,512]{1,0:T(8,128)(2,1)S(1)}, u32[]{:S(2)}, u32[]{:S(2)}) collective-permute-start(bf16[128,512]{1,0:T(8,128)(2,1)S(1)} %collective-permute-done.26), channel_id=1, source_target_pairs={{0,2},{2,0},{4,6},{6,4},{8,10},{10,8},{12,14},{14,12},{16,18},{18,... | collective-permute-start | bytes 393224 | tf_op jit(solution)/shard_map/ppermute | solution.py:243
  53.7 6.0 %collective-permute-start.16 = (bf16[128,512]{1,0:T(8,128)(2,1)S(1)}, bf16[128,512]{1,0:T(8,128)(2,1)S(1)}, u32[]{:S(2)}, u32[]{:S(2)}) collective-permute-start(bf16[128,512]{1,0:T(8,128)(2,1)S(1)} %collective-permute-done.12), channel_id=1, source_target_pairs={{0,8},{2,6},{8,16},{10,2},{16,24},{18,10},{24,28},{26,18},{28,20},... | collective-permute-start | bytes 393224 | tf_op jit(solution)/shard_map/ppermute | solution.py:313
  55.9 3.6 %collective-permute-start.13 = (bf16[128,512]{1,0:T(8,128)(2,1)S(1)}, bf16[128,512]{1,0:T(8,128)(2,1)S(1)}, u32[]{:S(2)}, u32[]{:S(2)}) collective-permute-start(bf16[128,512]{1,0:T(8,128)(2,1)S(1)} %collective-permute-done.12), channel_id=1, source_target_pairs={{0,2},{2,0},{4,6},{6,4},{8,10},{10,8},{12,14},{14,12},{16,18},{18,... | collective-permute-start | bytes 393224 | tf_op jit(solution)/shard_map/ppermute | solution.py:243
  55.9 7.8 %collective-permute-start.18 = (bf16[128,512]{1,0:T(8,128)(2,1)S(1)}, bf16[128,512]{1,0:T(8,128)(2,1)S(1)}, u32[]{:S(2)}, u32[]{:S(2)}) collective-permute-start(bf16[128,512]{1,0:T(8,128)(2,1)S(1)} %collective-permute-done.14), channel_id=1, source_target_pairs={{0,8},{2,6},{8,16},{10,2},{16,24},{18,10},{24,28},{26,18},{28,20},... | collective-permute-start | bytes 393224 | tf_op jit(solution)/shard_map/ppermute | solution.py:313
  58.7 2.6 %collective-permute-start.15 = (bf16[128,512]{1,0:T(8,128)(2,1)S(1)}, bf16[128,512]{1,0:T(8,128)(2,1)S(1)}, u32[]{:S(2)}, u32[]{:S(2)}) collective-permute-start(bf16[128,512]{1,0:T(8,128)(2,1)S(1)} %collective-permute-done.14), channel_id=1, source_target_pairs={{0,2},{2,0},{4,6},{6,4},{8,10},{10,8},{12,14},{14,12},{16,18},{18,... | collective-permute-start | bytes 393224 | tf_op jit(solution)/shard_map/ppermute | solution.py:243
  58.8 6.3 %collective-permute-start.32 = (bf16[128,512]{1,0:T(8,128)(2,1)S(1)}, bf16[128,512]{1,0:T(8,128)(2,1)S(1)}, u32[]{:S(2)}, u32[]{:S(2)}) collective-permute-start(bf16[128,512]{1,0:T(8,128)(2,1)S(1)} %collective-permute-done.28), channel_id=1, source_target_pairs={{0,8},{2,6},{8,16},{10,2},{16,24},{18,10},{24,28},{26,18},{28,20},... | collective-permute-start | bytes 393224 | tf_op jit(solution)/shard_map/ppermute | solution.py:313
  59.5 4.3 %collective-permute-start.29 = (bf16[128,512]{1,0:T(8,128)(2,1)S(1)}, bf16[128,512]{1,0:T(8,128)(2,1)S(1)}, u32[]{:S(2)}, u32[]{:S(2)}) collective-permute-start(bf16[128,512]{1,0:T(8,128)(2,1)S(1)} %collective-permute-done.28), channel_id=1, source_target_pairs={{0,2},{2,0},{4,6},{6,4},{8,10},{10,8},{12,14},{14,12},{16,18},{18,... | collective-permute-start | bytes 393224 | tf_op jit(solution)/shard_map/ppermute | solution.py:243
  59.7 6.7 %collective-permute-start.30 = (bf16[128,512]{1,0:T(8,128)(2,1)S(1)}, bf16[128,512]{1,0:T(8,128)(2,1)S(1)}, u32[]{:S(2)}, u32[]{:S(2)}) collective-permute-start(bf16[128,512]{1,0:T(8,128)(2,1)S(1)} %collective-permute-done.27), channel_id=1, source_target_pairs={{0,8},{2,6},{8,16},{10,2},{16,24},{18,10},{24,28},{26,18},{28,20},... | collective-permute-start | bytes 393224 | tf_op jit(solution)/shard_map/ppermute | solution.py:313
  61.3 5.7 %collective-permute-start.20 = (bf16[128,512]{1,0:T(8,128)(2,1)S(1)}, bf16[128,512]{1,0:T(8,128)(2,1)S(1)}, u32[]{:S(2)}, u32[]{:S(2)}) collective-permute-start(bf16[128,512]{1,0:T(8,128)(2,1)S(1)} %collective-permute-done.16), channel_id=1, source_target_pairs={{0,8},{2,6},{8,16},{10,2},{16,24},{18,10},{24,28},{26,18},{28,20},... | collective-permute-start | bytes 393224 | tf_op jit(solution)/shard_map/ppermute | solution.py:313
  63.7 1.5 %collective-permute-start.17 = (bf16[128,512]{1,0:T(8,128)(2,1)S(1)}, bf16[128,512]{1,0:T(8,128)(2,1)S(1)}, u32[]{:S(2)}, u32[]{:S(2)}) collective-permute-start(bf16[128,512]{1,0:T(8,128)(2,1)S(1)} %collective-permute-done.16), channel_id=1, source_target_pairs={{0,2},{2,0},{4,6},{6,4},{8,10},{10,8},{12,14},{14,12},{16,18},{18,... | collective-permute-start | bytes 393224 | tf_op jit(solution)/shard_map/ppermute | solution.py:243
  63.8 6.3 %collective-permute-start.22 = (bf16[128,512]{1,0:T(8,128)(2,1)S(1)}, bf16[128,512]{1,0:T(8,128)(2,1)S(1)}, u32[]{:S(2)}, u32[]{:S(2)}) collective-permute-start(bf16[128,512]{1,0:T(8,128)(2,1)S(1)} %collective-permute-done.18), channel_id=1, source_target_pairs={{0,8},{2,6},{8,16},{10,2},{16,24},{18,10},{24,28},{26,18},{28,20},... | collective-permute-start | bytes 393224 | tf_op jit(solution)/shard_map/ppermute | solution.py:313
  65.1 1.4 %collective-permute-start.19 = (bf16[128,512]{1,0:T(8,128)(2,1)S(1)}, bf16[128,512]{1,0:T(8,128)(2,1)S(1)}, u32[]{:S(2)}, u32[]{:S(2)}) collective-permute-start(bf16[128,512]{1,0:T(8,128)(2,1)S(1)} %collective-permute-done.18), channel_id=1, source_target_pairs={{0,2},{2,0},{4,6},{6,4},{8,10},{10,8},{12,14},{14,12},{16,18},{18,... | collective-permute-start | bytes 393224 | tf_op jit(solution)/shard_map/ppermute | solution.py:243
  65.2 5.1 %collective-permute-start.36 = (bf16[128,512]{1,0:T(8,128)(2,1)S(1)}, bf16[128,512]{1,0:T(8,128)(2,1)S(1)}, u32[]{:S(2)}, u32[]{:S(2)}) collective-permute-start(bf16[128,512]{1,0:T(8,128)(2,1)S(1)} %collective-permute-done.32), channel_id=1, source_target_pairs={{0,8},{2,6},{8,16},{10,2},{16,24},{18,10},{24,28},{26,18},{28,20},... | collective-permute-start | bytes 393224 | tf_op jit(solution)/shard_map/ppermute | solution.py:313
  66.4 4.3 %collective-permute-start.33 = (bf16[128,512]{1,0:T(8,128)(2,1)S(1)}, bf16[128,512]{1,0:T(8,128)(2,1)S(1)}, u32[]{:S(2)}, u32[]{:S(2)}) collective-permute-start(bf16[128,512]{1,0:T(8,128)(2,1)S(1)} %collective-permute-done.32), channel_id=1, source_target_pairs={{0,2},{2,0},{4,6},{6,4},{8,10},{10,8},{12,14},{14,12},{16,18},{18,... | collective-permute-start | bytes 393224 | tf_op jit(solution)/shard_map/ppermute | solution.py:243
  66.5 2.1 %collective-permute-start.31 = (bf16[128,512]{1,0:T(8,128)(2,1)S(1)}, bf16[128,512]{1,0:T(8,128)(2,1)S(1)}, u32[]{:S(2)}, u32[]{:S(2)}) collective-permute-start(bf16[128,512]{1,0:T(8,128)(2,1)S(1)} %collective-permute-done.30), channel_id=1, source_target_pairs={{0,2},{2,0},{4,6},{6,4},{8,10},{10,8},{12,14},{14,12},{16,18},{18,... | collective-permute-start | bytes 393224 | tf_op jit(solution)/shard_map/ppermute | solution.py:243
  67.0 5.0 %collective-permute-start.34 = (bf16[128,512]{1,0:T(8,128)(2,1)S(1)}, bf16[128,512]{1,0:T(8,128)(2,1)S(1)}, u32[]{:S(2)}, u32[]{:S(2)}) collective-permute-start(bf16[128,512]{1,0:T(8,128)(2,1)S(1)} %collective-permute-done.30), channel_id=1, source_target_pairs={{0,8},{2,6},{8,16},{10,2},{16,24},{18,10},{24,28},{26,18},{28,20},... | collective-permute-start | bytes 393224 | tf_op jit(solution)/shard_map/ppermute | solution.py:313
  68.6 5.0 %collective-permute-start.24 = (bf16[128,512]{1,0:T(8,128)(2,1)S(1)}, bf16[128,512]{1,0:T(8,128)(2,1)S(1)}, u32[]{:S(2)}, u32[]{:S(2)}) collective-permute-start(bf16[128,512]{1,0:T(8,128)(2,1)S(1)} %collective-permute-done.20), channel_id=1, source_target_pairs={{0,8},{2,6},{8,16},{10,2},{16,24},{18,10},{24,28},{26,18},{28,20},... | collective-permute-start | bytes 393224 | tf_op jit(solution)/shard_map/ppermute | solution.py:313
  70.1 1.9 %collective-permute-start.21 = (bf16[128,512]{1,0:T(8,128)(2,1)S(1)}, bf16[128,512]{1,0:T(8,128)(2,1)S(1)}, u32[]{:S(2)}, u32[]{:S(2)}) collective-permute-start(bf16[128,512]{1,0:T(8,128)(2,1)S(1)} %collective-permute-done.20), channel_id=1, source_target_pairs={{0,2},{2,0},{4,6},{6,4},{8,10},{10,8},{12,14},{14,12},{16,18},{18,... | collective-permute-start | bytes 393224 | tf_op jit(solution)/shard_map/ppermute | solution.py:243
  70.2 3.5 %collective-permute-start.23 = (bf16[128,512]{1,0:T(8,128)(2,1)S(1)}, bf16[128,512]{1,0:T(8,128)(2,1)S(1)}, u32[]{:S(2)}, u32[]{:S(2)}) collective-permute-start(bf16[128,512]{1,0:T(8,128)(2,1)S(1)} %collective-permute-done.22), channel_id=1, source_target_pairs={{0,2},{2,0},{4,6},{6,4},{8,10},{10,8},{12,14},{14,12},{16,18},{18,... | collective-permute-start | bytes 393224 | tf_op jit(solution)/shard_map/ppermute | solution.py:243
  70.7 5.0 %collective-permute-start.40 = (bf16[128,512]{1,0:T(8,128)(2,1)S(1)}, bf16[128,512]{1,0:T(8,128)(2,1)S(1)}, u32[]{:S(2)}, u32[]{:S(2)}) collective-permute-start(bf16[128,512]{1,0:T(8,128)(2,1)S(1)} %collective-permute-done.36), channel_id=1, source_target_pairs={{0,8},{2,6},{8,16},{10,2},{16,24},{18,10},{24,28},{26,18},{28,20},... | collective-permute-start | bytes 393224 | tf_op jit(solution)/shard_map/ppermute | solution.py:313
  72.0 5.1 %collective-permute-start.37 = (bf16[128,512]{1,0:T(8,128)(2,1)S(1)}, bf16[128,512]{1,0:T(8,128)(2,1)S(1)}, u32[]{:S(2)}, u32[]{:S(2)}) collective-permute-start(bf16[128,512]{1,0:T(8,128)(2,1)S(1)} %collective-permute-done.36), channel_id=1, source_target_pairs={{0,2},{2,0},{4,6},{6,4},{8,10},{10,8},{12,14},{14,12},{16,18},{18,... | collective-permute-start | bytes 393224 | tf_op jit(solution)/shard_map/ppermute | solution.py:243
  72.0 5.0 %collective-permute-start.38 = (bf16[128,512]{1,0:T(8,128)(2,1)S(1)}, bf16[128,512]{1,0:T(8,128)(2,1)S(1)}, u32[]{:S(2)}, u32[]{:S(2)}) collective-permute-start(bf16[128,512]{1,0:T(8,128)(2,1)S(1)} %collective-permute-done.34), channel_id=1, source_target_pairs={{0,8},{2,6},{8,16},{10,2},{16,24},{18,10},{24,28},{26,18},{28,20},... | collective-permute-start | bytes 393224 | tf_op jit(solution)/shard_map/ppermute | solution.py:313
  73.7 3.4 %collective-permute-start.35 = (bf16[128,512]{1,0:T(8,128)(2,1)S(1)}, bf16[128,512]{1,0:T(8,128)(2,1)S(1)}, u32[]{:S(2)}, u32[]{:S(2)}) collective-permute-start(bf16[128,512]{1,0:T(8,128)(2,1)S(1)} %collective-permute-done.34), channel_id=1, source_target_pairs={{0,2},{2,0},{4,6},{6,4},{8,10},{10,8},{12,14},{14,12},{16,18},{18,... | collective-permute-start | bytes 393224 | tf_op jit(solution)/shard_map/ppermute | solution.py:243
  73.8 4.7 %collective-permute-start.25 = (bf16[128,512]{1,0:T(8,128)(2,1)S(1)}, bf16[128,512]{1,0:T(8,128)(2,1)S(1)}, u32[]{:S(2)}, u32[]{:S(2)}) collective-permute-start(bf16[128,512]{1,0:T(8,128)(2,1)S(1)} %collective-permute-done.24), channel_id=1, source_target_pairs={{0,2},{2,0},{4,6},{6,4},{8,10},{10,8},{12,14},{14,12},{16,18},{18,... | collective-permute-start | bytes 393224 | tf_op jit(solution)/shard_map/ppermute | solution.py:243
  75.6 2.8 %collective-permute-start.41 = (bf16[128,512]{1,0:T(8,128)(2,1)S(1)}, bf16[128,512]{1,0:T(8,128)(2,1)S(1)}, u32[]{:S(2)}, u32[]{:S(2)}) collective-permute-start(bf16[128,512]{1,0:T(8,128)(2,1)S(1)} %collective-permute-done.40), channel_id=1, source_target_pairs={{0,2},{2,0},{4,6},{6,4},{8,10},{10,8},{12,14},{14,12},{16,18},{18,... | collective-permute-start | bytes 393224 | tf_op jit(solution)/shard_map/ppermute | solution.py:243
  77.1 1.3 %collective-permute-start.39 = (bf16[128,512]{1,0:T(8,128)(2,1)S(1)}, bf16[128,512]{1,0:T(8,128)(2,1)S(1)}, u32[]{:S(2)}, u32[]{:S(2)}) collective-permute-start(bf16[128,512]{1,0:T(8,128)(2,1)S(1)} %collective-permute-done.38), channel_id=1, source_target_pairs={{0,2},{2,0},{4,6},{6,4},{8,10},{10,8},{12,14},{14,12},{16,18},{18,... | collective-permute-start | bytes 393224 | tf_op jit(solution)/shard_map/ppermute | solution.py:243

commit v14 on v11

--- a/solution.py
+++ b/solution.py
@@ -157,12 +157,12 @@
     return roots
 
 
-def update_kernel(side_ref, mine_ref, other_ref, near_ref, next_ref, far_ref, left_ref):
+def update_kernel(place_ref, mine_ref, other_ref, near_ref, next_ref, far_ref, left_ref):
     tile = mine_ref[...] + other_ref[...]
     tile_half = tile.astype(jnp.bfloat16)
     left_ref[...], right = inverse_roots(tile)
     rows = near_ref.shape[0]
-    core, plane = side_ref[0], side_ref[1]
+    core, plane = place_ref[0], place_ref[1]
     for out_ref, part in (
         (near_ref, 2 * plane + core),
         (next_ref, 2 * plane + 1 - core),
@@ -189,12 +189,13 @@
     return jnp.where(position < bands // 2, 2 * position, 2 * (bands - 1 - position) + 1)
 
 
-def tile_kernel(place_ref, own_ref, shared_ref, *refs):
+def tile_kernel(place_ref, own_ref, *refs):
     hops = len(OFFSETS[0])
     near_refs, far_refs = refs[:hops], refs[hops : 2 * hops]
-    cot_refs = refs[2 * hops : -3]
+    shared_ref = refs[2 * hops]
+    cot_refs = refs[2 * hops + 1 : -3]
     partial_ref, band_ref, cot_ref = refs[-3:]
-    plane, band = place_ref[0], place_ref[1]
+    plane, band = place_ref[1], place_ref[2]
     tokens = own_ref.shape[0]
 
     def put(to_ref, piece_ref, source):
@@ -280,25 +281,25 @@
     pair = jnp.concatenate([cotangent, far_cot])
     cots = [pair] + [exchange(pair, offset) for offset in (1, 2, 3)]
     far = [swap_plane(piece) for piece in near]
+    place = jnp.stack([core, plane, band]).astype(jnp.int32)
     (partial_tile,) = call(
         tile_kernel,
         [jax.ShapeDtypeStruct((BLOCK, BLOCK), jnp.float32)],
         [pltpu.VMEM((bands * tokens, BLOCK), inputs.dtype)] * 2,
-        jnp.stack([plane, band]).astype(jnp.int32),
+        place,
         own_band,
-        shared,
         *near,
         *far,
+        shared,
         *cots,
     )
     other_partial = swap_core(partial_tile)
-    side = jnp.stack([core, plane]).astype(jnp.int32)
     rows = BLOCK // members // cores
     near_piece, next_piece, far_piece = call(
         update_kernel,
         [jax.ShapeDtypeStruct((rows, BLOCK), jnp.bfloat16)] * 3,
         [pltpu.VMEM((BLOCK, BLOCK), jnp.bfloat16)],
-        side,
+        place,
         partial_tile,
         other_partial,
     )

time: 79.4 us -> 79.8 us (level)
    ppermute x3, starting transfers between devices: 3.88 us -> 4.96 us  [deal(): return lax.ppermute(array, ('dp', 'pre'), pairs)]
    ppermute x4, starting transfers between devices: 6.98 us -> 5.97 us  [swap_plane(): lax.ppermute(array, 'pre', [(c, members - 1 - c) for c in range(members)])]
    ppermute x4, waiting for transfers between devices: 6.21 us -> 7.04 us  [swap_plane(): lax.ppermute(array, 'pre', [(c, members - 1 - c) for c in range(members)])]
  transfers between devices with their start and end apart: 42 -> 42, of which waited for: 15 -> 12; matrix products, arithmetic and copies ran while one was open for 6% -> 6% of each run, Pallas kernels for 1% -> 1%
where the time goes in v14:
time: 79.8 us; the launch traced here: 79.6 us
  starting transfers between devices  42.2 us (53%)
  waiting for transfers between devices  18 us (23%)
  Pallas kernels  9.46 us (12%)
  matrix products  3.62 us (5%)
  other arithmetic  2.71 us (3%)
  local copies, waits for them, and re-layouts  2.23 us (3%)
  between operations  1.37 us (2%)
    ppermute x14, starting transfers between devices, turn(): return lax.ppermute(array, 'dp', pairs)  20.5 us
    pallas_call x3, Pallas kernels, call(): pl.pallas_call(kernel, out_shape=out_shapes, in_specs=in_specs, out_specs...  9.46 us
    ppermute x5, starting transfers between devices, exchange(): return lax.ppermute(array, 'dp', pairs)  9 us
    ppermute x4, waiting for transfers between devices, swap_plane(): lax.ppermute(array, 'pre', [(c, members - 1 - c) for c in range(members)])  7.04 us
    ppermute x4, starting transfers between devices, swap_plane(): lax.ppermute(array, 'pre', [(c, members - 1 - c) for c in range(members)])  5.97 us
    ppermute x3, starting transfers between devices, deal(): return lax.ppermute(array, ('dp', 'pre'), pairs)  4.96 us
    ppermute x14, waiting for transfers between devices, turn(): return lax.ppermute(array, 'dp', pairs)  3.72 us
    ppermute x16, waiting for transfers between devices, swap_core(): return lax.ppermute(array, 'dp', [(g, g ^ 1) for g in range(groups)])  3.63 us
  transfers between devices with their start and end apart: 42, of which 12 were waited for; matrix products, arithmetic and copies ran while one was open for 6% of the time, Pallas kernels for 1%

profile of v14, /device:TPU:0, one launch (start us, length us, event | category | flops | bytes accessed | tf_op | source)
XLA Modules:
  0.0 79.6 jit_solution(13496236958734407712)
XLA Ops:
  0.6 4.1 %collective-permute-start = (bf16[128,512]{1,0:T(8,128)(2,1)}, bf16[128,512]{1,0:T(8,128)(2,1)S(1)}, u32[]{:S(2)}, u32[]{:S(2)}) collective-permute-start(bf16[128,512]{1,0:T(8,128)(2,1)} %param.5), channel_id=1, source_target_pairs={{0,16},{2,18},{4,20},{6,22},{8,24},{10,26},{12,28},{14,30},{16,0},... | collective-permute-start | bytes 393224 | tf_op jit(solution)/shard_map/ppermute | solution.py:275
  4.7 0.1 stack.36.place_ref
  4.8 1.2 %copy-done = bf16[128,4096]{1,0:T(8,128)(2,1)S(1)} copy-done((bf16[128,4096]{1,0:T(8,128)(2,1)S(1)}, bf16[128,4096]{1,0:T(8,128)(2,1)}, u32[]{:S(2)}) %copy-start) | copy-done | bytes 1048600
  6.0 0.6 shard_map.50
  6.6 0.1 collective-permute-start.1
  6.7 4.8 %collective-permute-start.2 = (bf16[128,512]{1,0:T(8,128)(2,1)S(1)}, bf16[128,512]{1,0:T(8,128)(2,1)S(1)}, u32[]{:S(2)}, u32[]{:S(2)}) collective-permute-start(bf16[128,512]{1,0:T(8,128)(2,1)S(1)} %get-tuple-element.15), channel_id=1, source_target_pairs={{0,28},{1,25},{2,30},{3,27},{4,24},{5,29},{6,26},{7,31},{8,20},{9,... | collective-permute-start | bytes 393224 | tf_op jit(solution)/shard_map/ppermute | solution.py:259
  11.6 0.5 collective-permute-start.7
  12.1 3.6 %convolution_convert_fusion = bf16[128,512]{1,0:T(8,128)(2,1)} fusion(bf16[128,4096]{1,0:T(8,128)(2,1)S(1)} %copy-done, bf16[4096,512]{1,0:T(8,128)(2,1)} %param.4), kind=kOutput, calls=%fused_computation.1 | convolution fusion | flops 536936448 | bytes 5373952 | tf_op jit(solution)/shard_map/dot_general | solution.py:277
  15.7 1.9 %collective-permute-done = bf16[128,512]{1,0:T(8,128)(2,1)S(1)} collective-permute-done((bf16[128,512]{1,0:T(8,128)(2,1)}, bf16[128,512]{1,0:T(8,128)(2,1)S(1)}, u32[]{:S(2)}, u32[]{:S(2)}) %collective-permute-start) | collective-permute-done | bytes 131104 | tf_op jit(solution)/shard_map/ppermute | solution.py:275
  17.7 1.2 %collective-permute-start.10 = (bf16[256,512]{1,0:T(8,128)(2,1)S(1)}, bf16[256,512]{1,0:T(8,128)(2,1)S(1)}, u32[]{:S(2)}, u32[]{:S(2)}) collective-permute-start(bf16[256,512]{1,0:T(8,128)(2,1)S(1)} %constant_dynamic-update-slice_fusion.refs_7_), channel_id=1, source_target_pairs={{0,12},{2,14},{4,8},{6,10},{8,4},{10,6},{12,0},{14,2},{16,28},{18,... | collective-permute-start | bytes 786440 | tf_op jit(solution)/shard_map/ppermute | solution.py:275
  18.9 1.7 %collective-permute-done.1.refs_0_ = bf16[128,512]{1,0:T(8,128)(2,1)S(1)} collective-permute-done((bf16[128,512]{1,0:T(8,128)(2,1)S(1)}, bf16[128,512]{1,0:T(8,128)(2,1)S(1)}, u32[]{:S(2)}, u32[]{:S(2)}) %collective-permute-start.1) | collective-permute-done | bytes 131104 | tf_op jit(solution)/shard_map/ppermute | solution.py:259
  20.6 2.8 %collective-permute-start.4 = (bf16[128,512]{1,0:T(8,128)(2,1)S(1)}, bf16[128,512]{1,0:T(8,128)(2,1)S(1)}, u32[]{:S(2)}, u32[]{:S(2)}) collective-permute-start(bf16[128,512]{1,0:T(8,128)(2,1)S(1)} %collective-permute-done.1.refs_0_), channel_id=1, source_target_pairs={{0,1},{1,0},{2,3},{3,2},{4,5},{5,4},{6,7},{7,6},{8,9},{9,8},{10,11... | collective-permute-start | bytes 393224 | tf_op jit(solution)/shard_map/ppermute | solution.py:247
  23.3 2.7 %collective-permute-start.9 = (bf16[256,512]{1,0:T(8,128)(2,1)S(1)}, bf16[256,512]{1,0:T(8,128)(2,1)S(1)}, u32[]{:S(2)}, u32[]{:S(2)}) collective-permute-start(bf16[256,512]{1,0:T(8,128)(2,1)S(1)} %constant_dynamic-update-slice_fusion.refs_7_), channel_id=1, source_target_pairs={{0,8},{2,10},{4,12},{6,14},{8,0},{10,2},{12,4},{14,6},{16,24},{18,... | collective-permute-start | bytes 786440 | tf_op jit(solution)/shard_map/ppermute | solution.py:275
  26.0 0.5 collective-permute-start.8
  26.6 2.0 %collective-permute-start.6 = (bf16[128,512]{1,0:T(8,128)(2,1)S(1)}, bf16[128,512]{1,0:T(8,128)(2,1)S(1)}, u32[]{:S(2)}, u32[]{:S(2)}) collective-permute-start(bf16[128,512]{1,0:T(8,128)(2,1)S(1)} %collective-permute-done.3.refs_2_), channel_id=1, source_target_pairs={{0,1},{1,0},{2,3},{3,2},{4,5},{5,4},{6,7},{7,6},{8,9},{9,8},{10,11... | collective-permute-start | bytes 393224 | tf_op jit(solution)/shard_map/ppermute | solution.py:247
  28.6 0.1 pad_add_fusion.place_ref
  28.7 4.1 %collective-permute-done.5.refs_4_ = bf16[128,512]{1,0:T(8,128)(2,1)S(1)} collective-permute-done((bf16[128,512]{1,0:T(8,128)(2,1)S(1)}, bf16[128,512]{1,0:T(8,128)(2,1)S(1)}, u32[]{:S(2)}, u32[]{:S(2)}) %collective-permute-start.5) | collective-permute-done | bytes 131104 | tf_op jit(solution)/shard_map/ppermute | solution.py:247
  32.7 1.4 %collective-permute-done.6.refs_5_ = bf16[128,512]{1,0:T(8,128)(2,1)S(1)} collective-permute-done((bf16[128,512]{1,0:T(8,128)(2,1)S(1)}, bf16[128,512]{1,0:T(8,128)(2,1)S(1)}, u32[]{:S(2)}, u32[]{:S(2)}) %collective-permute-start.6) | collective-permute-done | bytes 131104 | tf_op jit(solution)/shard_map/ppermute | solution.py:247
  34.2 1.4 %shard_map.51.mine_ref = f32[512,512]{1,0:T(8,128)S(1)} custom-call(s32[3]{0:T(128)S(1)} %pad_add_fusion.place_ref, bf16[128,512]{1,0:T(8,128)(2,1)S(1)} %get-tuple-element.13.own_ref, bf16[128,512]{1,0:T(8,128)(2,1)S(1)} %collective-permute-done.1.refs_0_, bf16[128,512]{1,0:T(8,128)(2,1)S(1)} %collective-permute-done.2.refs_1_, ...), custom_call_target="tpu_custom_call" | custom-call | tf_op jit(solution)/shard_map/pallas_call | solution.py:219
  35.9 2.4 %collective-permute-done.11.other_ref = f32[512,512]{1,0:T(8,128)S(1)} collective-permute-done((f32[512,512]{1,0:T(8,128)S(1)}, f32[512,512]{1,0:T(8,128)S(1)}, u32[]{:S(2)}, u32[]{:S(2)}) %collective-permute-start.11) | collective-permute-done | bytes 1048608 | tf_op jit(solution)/shard_map/ppermute | solution.py:244
  38.3 7.5 %shard_map.52 = (bf16[128,512]{1,0:T(8,128)(2,1)S(1)}, bf16[128,512]{1,0:T(8,128)(2,1)S(1)}, bf16[128,512]{1,0:T(8,128)(2,1)S(1)}) custom-call(s32[3]{0:T(128)S(1)} %pad_add_fusion.place_ref, f32[512,512]{1,0:T(8,128)S(1)} %shard_map.51.mine_ref, f32[512,512]{1,0:T(8,128)S(1)} %collective-permute-done.11.other_ref), custom_call_target="tpu_custom_call" | custom-call | tf_op jit(solution)/shard_map/pallas_call | solution.py:219
  45.8 1.2 %collective-permute-start.26 = (bf16[128,512]{1,0:T(8,128)(2,1)S(1)}, bf16[128,512]{1,0:T(8,128)(2,1)S(1)}, u32[]{:S(2)}, u32[]{:S(2)}) collective-permute-start(bf16[128,512]{1,0:T(8,128)(2,1)S(1)} %get-tuple-element.21), channel_id=1, source_target_pairs={{0,1},{1,0},{2,3},{3,2},{4,5},{5,4},{6,7},{7,6},{8,9},{9,8},{10,11... | collective-permute-start | bytes 393224 | tf_op jit(solution)/shard_map/ppermute | solution.py:247
  46.9 2.6 %collective-permute-start.14 = (bf16[128,512]{1,0:T(8,128)(2,1)S(1)}, bf16[128,512]{1,0:T(8,128)(2,1)S(1)}, u32[]{:S(2)}, u32[]{:S(2)}) collective-permute-start(bf16[128,512]{1,0:T(8,128)(2,1)S(1)} %get-tuple-element.20), channel_id=1, source_target_pairs={{0,8},{2,6},{8,16},{10,2},{16,24},{18,10},{24,28},{26,18},{28,20},... | collective-permute-start | bytes 393224 | tf_op jit(solution)/shard_map/ppermute | solution.py:313
  49.5 0.2 broadcast_in_dim.99.clone.1
  49.8 1.6 %collective-permute-done.26 = bf16[128,512]{1,0:T(8,128)(2,1)S(1)} collective-permute-done((bf16[128,512]{1,0:T(8,128)(2,1)S(1)}, bf16[128,512]{1,0:T(8,128)(2,1)S(1)}, u32[]{:S(2)}, u32[]{:S(2)}) %collective-permute-start.26) | collective-permute-done | bytes 131104 | tf_op jit(solution)/shard_map/ppermute | solution.py:247
  51.4 0.6 collective-permute-start.28
  52.0 2.8 %collective-permute-start.16 = (bf16[128,512]{1,0:T(8,128)(2,1)S(1)}, bf16[128,512]{1,0:T(8,128)(2,1)S(1)}, u32[]{:S(2)}, u32[]{:S(2)}) collective-permute-start(bf16[128,512]{1,0:T(8,128)(2,1)S(1)} %collective-permute-done.12), channel_id=1, source_target_pairs={{0,8},{2,6},{8,16},{10,2},{16,24},{18,10},{24,28},{26,18},{28,20},... | collective-permute-start | bytes 393224 | tf_op jit(solution)/shard_map/ppermute | solution.py:313
  54.8 1.7 %collective-permute-start.18 = (bf16[128,512]{1,0:T(8,128)(2,1)S(1)}, bf16[128,512]{1,0:T(8,128)(2,1)S(1)}, u32[]{:S(2)}, u32[]{:S(2)}) collective-permute-start(bf16[128,512]{1,0:T(8,128)(2,1)S(1)} %collective-permute-done.14), channel_id=1, source_target_pairs={{0,8},{2,6},{8,16},{10,2},{16,24},{18,10},{24,28},{26,18},{28,20},... | collective-permute-start | bytes 393224 | tf_op jit(solution)/shard_map/ppermute | solution.py:313
  56.5 0.2 broadcast_in_dim.99.clone
  56.9 1.6 %collective-permute-start.32 = (bf16[128,512]{1,0:T(8,128)(2,1)S(1)}, bf16[128,512]{1,0:T(8,128)(2,1)S(1)}, u32[]{:S(2)}, u32[]{:S(2)}) collective-permute-start(bf16[128,512]{1,0:T(8,128)(2,1)S(1)} %collective-permute-done.28), channel_id=1, source_target_pairs={{0,8},{2,6},{8,16},{10,2},{16,24},{18,10},{24,28},{26,18},{28,20},... | collective-permute-start | bytes 393224 | tf_op jit(solution)/shard_map/ppermute | solution.py:313
  58.6 1.4 %collective-permute-start.30 = (bf16[128,512]{1,0:T(8,128)(2,1)S(1)}, bf16[128,512]{1,0:T(8,128)(2,1)S(1)}, u32[]{:S(2)}, u32[]{:S(2)}) collective-permute-start(bf16[128,512]{1,0:T(8,128)(2,1)S(1)} %collective-permute-done.27), channel_id=1, source_target_pairs={{0,8},{2,6},{8,16},{10,2},{16,24},{18,10},{24,28},{26,18},{28,20},... | collective-permute-start | bytes 393224 | tf_op jit(solution)/shard_map/ppermute | solution.py:313
  60.0 1.7 %collective-permute-start.20 = (bf16[128,512]{1,0:T(8,128)(2,1)S(1)}, bf16[128,512]{1,0:T(8,128)(2,1)S(1)}, u32[]{:S(2)}, u32[]{:S(2)}) collective-permute-start(bf16[128,512]{1,0:T(8,128)(2,1)S(1)} %collective-permute-done.16), channel_id=1, source_target_pairs={{0,8},{2,6},{8,16},{10,2},{16,24},{18,10},{24,28},{26,18},{28,20},... | collective-permute-start | bytes 393224 | tf_op jit(solution)/shard_map/ppermute | solution.py:313
  61.9 1.6 %collective-permute-start.22 = (bf16[128,512]{1,0:T(8,128)(2,1)S(1)}, bf16[128,512]{1,0:T(8,128)(2,1)S(1)}, u32[]{:S(2)}, u32[]{:S(2)}) collective-permute-start(bf16[128,512]{1,0:T(8,128)(2,1)S(1)} %collective-permute-done.18), channel_id=1, source_target_pairs={{0,8},{2,6},{8,16},{10,2},{16,24},{18,10},{24,28},{26,18},{28,20},... | collective-permute-start | bytes 393224 | tf_op jit(solution)/shard_map/ppermute | solution.py:313
  63.6 1.2 %collective-permute-start.36 = (bf16[128,512]{1,0:T(8,128)(2,1)S(1)}, bf16[128,512]{1,0:T(8,128)(2,1)S(1)}, u32[]{:S(2)}, u32[]{:S(2)}) collective-permute-start(bf16[128,512]{1,0:T(8,128)(2,1)S(1)} %collective-permute-done.32), channel_id=1, source_target_pairs={{0,8},{2,6},{8,16},{10,2},{16,24},{18,10},{24,28},{26,18},{28,20},... | collective-permute-start | bytes 393224 | tf_op jit(solution)/shard_map/ppermute | solution.py:313
  65.0 0.5 collective-permute-start.31
  65.5 1.2 %collective-permute-start.34 = (bf16[128,512]{1,0:T(8,128)(2,1)S(1)}, bf16[128,512]{1,0:T(8,128)(2,1)S(1)}, u32[]{:S(2)}, u32[]{:S(2)}) collective-permute-start(bf16[128,512]{1,0:T(8,128)(2,1)S(1)} %collective-permute-done.30), channel_id=1, source_target_pairs={{0,8},{2,6},{8,16},{10,2},{16,24},{18,10},{24,28},{26,18},{28,20},... | collective-permute-start | bytes 393224 | tf_op jit(solution)/shard_map/ppermute | solution.py:313
  66.7 1.5 %collective-permute-start.24 = (bf16[128,512]{1,0:T(8,128)(2,1)S(1)}, bf16[128,512]{1,0:T(8,128)(2,1)S(1)}, u32[]{:S(2)}, u32[]{:S(2)}) collective-permute-start(bf16[128,512]{1,0:T(8,128)(2,1)S(1)} %collective-permute-done.20), channel_id=1, source_target_pairs={{0,8},{2,6},{8,16},{10,2},{16,24},{18,10},{24,28},{26,18},{28,20},... | collective-permute-start | bytes 393224 | tf_op jit(solution)/shard_map/ppermute | solution.py:313
  68.4 0.3 collective-permute-done.36
  68.6 0.2 collective-permute-start.23
  68.9 1.4 %collective-permute-start.40 = (bf16[128,512]{1,0:T(8,128)(2,1)S(1)}, bf16[128,512]{1,0:T(8,128)(2,1)S(1)}, u32[]{:S(2)}, u32[]{:S(2)}) collective-permute-start(bf16[128,512]{1,0:T(8,128)(2,1)S(1)} %collective-permute-done.36), channel_id=1, source_target_pairs={{0,8},{2,6},{8,16},{10,2},{16,24},{18,10},{24,28},{26,18},{28,20},... | collective-permute-start | bytes 393224 | tf_op jit(solution)/shard_map/ppermute | solution.py:313
  70.3 0.2 collective-permute-done.34
  70.5 1.1 %collective-permute-start.38 = (bf16[128,512]{1,0:T(8,128)(2,1)S(1)}, bf16[128,512]{1,0:T(8,128)(2,1)S(1)}, u32[]{:S(2)}, u32[]{:S(2)}) collective-permute-start(bf16[128,512]{1,0:T(8,128)(2,1)S(1)} %collective-permute-done.34), channel_id=1, source_target_pairs={{0,8},{2,6},{8,16},{10,2},{16,24},{18,10},{24,28},{26,18},{28,20},... | collective-permute-start | bytes 393224 | tf_op jit(solution)/shard_map/ppermute | solution.py:313
  71.7 0.2 collective-permute-done.24
  71.9 0.5 collective-permute-start.25
  72.5 1.3 %collective-permute-done.40 = bf16[128,512]{1,0:T(8,128)(2,1)S(1)} collective-permute-done((bf16[128,512]{1,0:T(8,128)(2,1)S(1)}, bf16[128,512]{1,0:T(8,128)(2,1)S(1)}, u32[]{:S(2)}, u32[]{:S(2)}) %collective-permute-start.40) | collective-permute-done | bytes 131104 | tf_op jit(solution)/shard_map/ppermute | solution.py:313
  73.8 1.7 %collective-permute-done.38 = bf16[128,512]{1,0:T(8,128)(2,1)S(1)} collective-permute-done((bf16[128,512]{1,0:T(8,128)(2,1)S(1)}, bf16[128,512]{1,0:T(8,128)(2,1)S(1)}, u32[]{:S(2)}, u32[]{:S(2)}) %collective-permute-start.38) | collective-permute-done | bytes 131104 | tf_op jit(solution)/shard_map/ppermute | solution.py:313
  75.6 1.2 %collective-permute-done.39 = bf16[128,512]{1,0:T(8,128)(2,1)S(1)} collective-permute-done((bf16[128,512]{1,0:T(8,128)(2,1)S(1)}, bf16[128,512]{1,0:T(8,128)(2,1)S(1)}, u32[]{:S(2)}, u32[]{:S(2)}) %collective-permute-start.39) | collective-permute-done | bytes 131104 | tf_op jit(solution)/shard_map/ppermute | solution.py:244
  77.0 2.6 %maximum_select_fusion = bf16[8,256,1024]{2,1,0:T(8,128)(2,1)} fusion(bf16[8,256,512]{2,1,0:T(8,128)(2,1)S(1)} %bitcast.75, bf16[8,256,512]{2,1,0:T(8,128)(2,1)S(1)} %bitcast.76, pred[]{:T(512)S(6)} %eq.44), kind=kLoop, calls=%fused_computation | loop fusion | flops 18874368 | bytes 8388609 | tf_op jit(solution)/shard_map/jit(_where)/select_n | solution.py:335
  (82 shorter events, 1.1 us)
Async XLA Ops:
  0.6 17.1 %collective-permute-start = (bf16[128,512]{1,0:T(8,128)(2,1)}, bf16[128,512]{1,0:T(8,128)(2,1)S(1)}, u32[]{:S(2)}, u32[]{:S(2)}) collective-permute-start(bf16[128,512]{1,0:T(8,128)(2,1)} %param.5), channel_id=1, source_target_pairs={{0,16},{2,18},{4,20},{6,22},{8,24},{10,26},{12,28},{14,30},{16,0},... | collective-permute-start | bytes 393224 | tf_op jit(solution)/shard_map/ppermute | solution.py:275
  4.8 1.2 %copy-start = (bf16[128,4096]{1,0:T(8,128)(2,1)S(1)}, bf16[128,4096]{1,0:T(8,128)(2,1)}, u32[]{:S(2)}) copy-start(bf16[128,4096]{1,0:T(8,128)(2,1)} %inputs_ref.1) | copy-start | bytes 3145732
  6.6 13.9 %collective-permute-start.1 = (bf16[128,512]{1,0:T(8,128)(2,1)S(1)}, bf16[128,512]{1,0:T(8,128)(2,1)S(1)}, u32[]{:S(2)}, u32[]{:S(2)}) collective-permute-start(bf16[128,512]{1,0:T(8,128)(2,1)S(1)} %get-tuple-element.14), channel_id=1, source_target_pairs={{0,16},{1,21},{2,18},{3,23},{4,20},{5,17},{6,22},{7,19},{8,24},{9,... | collective-permute-start | bytes 393224 | tf_op jit(solution)/shard_map/ppermute | solution.py:259
  6.7 16.6 %collective-permute-start.2 = (bf16[128,512]{1,0:T(8,128)(2,1)S(1)}, bf16[128,512]{1,0:T(8,128)(2,1)S(1)}, u32[]{:S(2)}, u32[]{:S(2)}) collective-permute-start(bf16[128,512]{1,0:T(8,128)(2,1)S(1)} %get-tuple-element.15), channel_id=1, source_target_pairs={{0,28},{1,25},{2,30},{3,27},{4,24},{5,29},{6,26},{7,31},{8,20},{9,... | collective-permute-start | bytes 393224 | tf_op jit(solution)/shard_map/ppermute | solution.py:259
  11.6 14.4 %collective-permute-start.3 = (bf16[128,512]{1,0:T(8,128)(2,1)S(1)}, bf16[128,512]{1,0:T(8,128)(2,1)S(1)}, u32[]{:S(2)}, u32[]{:S(2)}) collective-permute-start(bf16[128,512]{1,0:T(8,128)(2,1)S(1)} %get-tuple-element.16), channel_id=1, source_target_pairs={{0,8},{1,13},{2,10},{3,15},{4,12},{5,9},{6,14},{7,11},{8,0},{9,5},... | collective-permute-start | bytes 393224 | tf_op jit(solution)/shard_map/ppermute | solution.py:259
  11.6 4.1 %copy-start.1 = (bf16[128,512]{1,0:T(8,128)(2,1)S(1)}, bf16[128,512]{1,0:T(8,128)(2,1)}, u32[]{:S(2)}) copy-start(bf16[128,512]{1,0:T(8,128)(2,1)} %param.5) | copy-start | bytes 393220
  11.6 15.0 %collective-permute-start.7 = (bf16[128,512]{1,0:T(8,128)(2,1)S(1)}, bf16[128,512]{1,0:T(8,128)(2,1)S(1)}, u32[]{:S(2)}, u32[]{:S(2)}) collective-permute-start(bf16[128,512]{1,0:T(8,128)(2,1)S(1)} %get-tuple-element.17), channel_id=1, source_target_pairs={{0,4},{2,6},{4,0},{6,2},{8,12},{10,14},{12,8},{14,10},{16,20},{18,... | collective-permute-start | bytes 393224 | tf_op jit(solution)/shard_map/ppermute | solution.py:275
  17.7 16.5 %collective-permute-start.10 = (bf16[256,512]{1,0:T(8,128)(2,1)S(1)}, bf16[256,512]{1,0:T(8,128)(2,1)S(1)}, u32[]{:S(2)}, u32[]{:S(2)}) collective-permute-start(bf16[256,512]{1,0:T(8,128)(2,1)S(1)} %constant_dynamic-update-slice_fusion.refs_7_), channel_id=1, source_target_pairs={{0,12},{2,14},{4,8},{6,10},{8,4},{10,6},{12,0},{14,2},{16,28},{18,... | collective-permute-start | bytes 786440 | tf_op jit(solution)/shard_map/ppermute | solution.py:275
  20.6 6.0 %collective-permute-start.4 = (bf16[128,512]{1,0:T(8,128)(2,1)S(1)}, bf16[128,512]{1,0:T(8,128)(2,1)S(1)}, u32[]{:S(2)}, u32[]{:S(2)}) collective-permute-start(bf16[128,512]{1,0:T(8,128)(2,1)S(1)} %collective-permute-done.1.refs_0_), channel_id=1, source_target_pairs={{0,1},{1,0},{2,3},{3,2},{4,5},{5,4},{6,7},{7,6},{8,9},{9,8},{10,11... | collective-permute-start | bytes 393224 | tf_op jit(solution)/shard_map/ppermute | solution.py:247
  23.3 10.8 %collective-permute-start.9 = (bf16[256,512]{1,0:T(8,128)(2,1)S(1)}, bf16[256,512]{1,0:T(8,128)(2,1)S(1)}, u32[]{:S(2)}, u32[]{:S(2)}) collective-permute-start(bf16[256,512]{1,0:T(8,128)(2,1)S(1)} %constant_dynamic-update-slice_fusion.refs_7_), channel_id=1, source_target_pairs={{0,8},{2,10},{4,12},{6,14},{8,0},{10,2},{12,4},{14,6},{16,24},{18,... | collective-permute-start | bytes 786440 | tf_op jit(solution)/shard_map/ppermute | solution.py:275
  26.0 8.1 %collective-permute-start.8 = (bf16[256,512]{1,0:T(8,128)(2,1)S(1)}, bf16[256,512]{1,0:T(8,128)(2,1)S(1)}, u32[]{:S(2)}, u32[]{:S(2)}) collective-permute-start(bf16[256,512]{1,0:T(8,128)(2,1)S(1)} %constant_dynamic-update-slice_fusion.refs_7_), channel_id=1, source_target_pairs={{0,4},{2,6},{4,0},{6,2},{8,12},{10,14},{12,8},{14,10},{16,20},{18,... | collective-permute-start | bytes 786440 | tf_op jit(solution)/shard_map/ppermute | solution.py:275
  26.6 6.2 %collective-permute-start.5 = (bf16[128,512]{1,0:T(8,128)(2,1)S(1)}, bf16[128,512]{1,0:T(8,128)(2,1)S(1)}, u32[]{:S(2)}, u32[]{:S(2)}) collective-permute-start(bf16[128,512]{1,0:T(8,128)(2,1)S(1)} %collective-permute-done.2.refs_1_), channel_id=1, source_target_pairs={{0,1},{1,0},{2,3},{3,2},{4,5},{5,4},{6,7},{7,6},{8,9},{9,8},{10,11... | collective-permute-start | bytes 393224 | tf_op jit(solution)/shard_map/ppermute | solution.py:247
  26.6 7.6 %collective-permute-start.6 = (bf16[128,512]{1,0:T(8,128)(2,1)S(1)}, bf16[128,512]{1,0:T(8,128)(2,1)S(1)}, u32[]{:S(2)}, u32[]{:S(2)}) collective-permute-start(bf16[128,512]{1,0:T(8,128)(2,1)S(1)} %collective-permute-done.3.refs_2_), channel_id=1, source_target_pairs={{0,1},{1,0},{2,3},{3,2},{4,5},{5,4},{6,7},{7,6},{8,9},{9,8},{10,11... | collective-permute-start | bytes 393224 | tf_op jit(solution)/shard_map/ppermute | solution.py:247
  35.6 2.7 %collective-permute-start.11 = (f32[512,512]{1,0:T(8,128)S(1)}, f32[512,512]{1,0:T(8,128)S(1)}, u32[]{:S(2)}, u32[]{:S(2)}) collective-permute-start(f32[512,512]{1,0:T(8,128)S(1)} %shard_map.51.mine_ref), channel_id=1, source_target_pairs={{0,2},{2,0},{4,6},{6,4},{8,10},{10,8},{12,14},{14,12},{16,18},{18,... | collective-permute-start | bytes 3145736 | tf_op jit(solution)/shard_map/ppermute | solution.py:244
  45.8 5.6 %collective-permute-start.26 = (bf16[128,512]{1,0:T(8,128)(2,1)S(1)}, bf16[128,512]{1,0:T(8,128)(2,1)S(1)}, u32[]{:S(2)}, u32[]{:S(2)}) collective-permute-start(bf16[128,512]{1,0:T(8,128)(2,1)S(1)} %get-tuple-element.21), channel_id=1, source_target_pairs={{0,1},{1,0},{2,3},{3,2},{4,5},{5,4},{6,7},{7,6},{8,9},{9,8},{10,11... | collective-permute-start | bytes 393224 | tf_op jit(solution)/shard_map/ppermute | solution.py:247
  46.9 5.1 %collective-permute-start.12 = (bf16[128,512]{1,0:T(8,128)(2,1)S(1)}, bf16[128,512]{1,0:T(8,128)(2,1)S(1)}, u32[]{:S(2)}, u32[]{:S(2)}) collective-permute-start(bf16[128,512]{1,0:T(8,128)(2,1)S(1)} %get-tuple-element.19), channel_id=1, source_target_pairs={{0,8},{2,6},{8,16},{10,2},{16,24},{18,10},{24,28},{26,18},{28,20},... | collective-permute-start | bytes 393224 | tf_op jit(solution)/shard_map/ppermute | solution.py:313
  46.9 7.9 %collective-permute-start.14 = (bf16[128,512]{1,0:T(8,128)(2,1)S(1)}, bf16[128,512]{1,0:T(8,128)(2,1)S(1)}, u32[]{:S(2)}, u32[]{:S(2)}) collective-permute-start(bf16[128,512]{1,0:T(8,128)(2,1)S(1)} %get-tuple-element.20), channel_id=1, source_target_pairs={{0,8},{2,6},{8,16},{10,2},{16,24},{18,10},{24,28},{26,18},{28,20},... | collective-permute-start | bytes 393224 | tf_op jit(solution)/shard_map/ppermute | solution.py:313
  51.4 5.4 %collective-permute-start.28 = (bf16[128,512]{1,0:T(8,128)(2,1)S(1)}, bf16[128,512]{1,0:T(8,128)(2,1)S(1)}, u32[]{:S(2)}, u32[]{:S(2)}) collective-permute-start(bf16[128,512]{1,0:T(8,128)(2,1)S(1)} %collective-permute-done.26), channel_id=1, source_target_pairs={{0,8},{2,6},{8,16},{10,2},{16,24},{18,10},{24,28},{26,18},{28,20},... | collective-permute-start | bytes 393224 | tf_op jit(solution)/shard_map/ppermute | solution.py:313
  52.0 4.9 %collective-permute-start.27 = (bf16[128,512]{1,0:T(8,128)(2,1)S(1)}, bf16[128,512]{1,0:T(8,128)(2,1)S(1)}, u32[]{:S(2)}, u32[]{:S(2)}) collective-permute-start(bf16[128,512]{1,0:T(8,128)(2,1)S(1)} %collective-permute-done.26), channel_id=1, source_target_pairs={{0,2},{2,0},{4,6},{6,4},{8,10},{10,8},{12,14},{14,12},{16,18},{18,... | collective-permute-start | bytes 393224 | tf_op jit(solution)/shard_map/ppermute | solution.py:244
  52.0 6.6 %collective-permute-start.16 = (bf16[128,512]{1,0:T(8,128)(2,1)S(1)}, bf16[128,512]{1,0:T(8,128)(2,1)S(1)}, u32[]{:S(2)}, u32[]{:S(2)}) collective-permute-start(bf16[128,512]{1,0:T(8,128)(2,1)S(1)} %collective-permute-done.12), channel_id=1, source_target_pairs={{0,8},{2,6},{8,16},{10,2},{16,24},{18,10},{24,28},{26,18},{28,20},... | collective-permute-start | bytes 393224 | tf_op jit(solution)/shard_map/ppermute | solution.py:313
  54.8 3.7 %collective-permute-start.13 = (bf16[128,512]{1,0:T(8,128)(2,1)S(1)}, bf16[128,512]{1,0:T(8,128)(2,1)S(1)}, u32[]{:S(2)}, u32[]{:S(2)}) collective-permute-start(bf16[128,512]{1,0:T(8,128)(2,1)S(1)} %collective-permute-done.12), channel_id=1, source_target_pairs={{0,2},{2,0},{4,6},{6,4},{8,10},{10,8},{12,14},{14,12},{16,18},{18,... | collective-permute-start | bytes 393224 | tf_op jit(solution)/shard_map/ppermute | solution.py:244
  54.8 7.0 %collective-permute-start.18 = (bf16[128,512]{1,0:T(8,128)(2,1)S(1)}, bf16[128,512]{1,0:T(8,128)(2,1)S(1)}, u32[]{:S(2)}, u32[]{:S(2)}) collective-permute-start(bf16[128,512]{1,0:T(8,128)(2,1)S(1)} %collective-permute-done.14), channel_id=1, source_target_pairs={{0,8},{2,6},{8,16},{10,2},{16,24},{18,10},{24,28},{26,18},{28,20},... | collective-permute-start | bytes 393224 | tf_op jit(solution)/shard_map/ppermute | solution.py:313
  56.8 3.2 %collective-permute-start.15 = (bf16[128,512]{1,0:T(8,128)(2,1)S(1)}, bf16[128,512]{1,0:T(8,128)(2,1)S(1)}, u32[]{:S(2)}, u32[]{:S(2)}) collective-permute-start(bf16[128,512]{1,0:T(8,128)(2,1)S(1)} %collective-permute-done.14), channel_id=1, source_target_pairs={{0,2},{2,0},{4,6},{6,4},{8,10},{10,8},{12,14},{14,12},{16,18},{18,... | collective-permute-start | bytes 393224 | tf_op jit(solution)/shard_map/ppermute | solution.py:244
  56.9 6.6 %collective-permute-start.32 = (bf16[128,512]{1,0:T(8,128)(2,1)S(1)}, bf16[128,512]{1,0:T(8,128)(2,1)S(1)}, u32[]{:S(2)}, u32[]{:S(2)}) collective-permute-start(bf16[128,512]{1,0:T(8,128)(2,1)S(1)} %collective-permute-done.28), channel_id=1, source_target_pairs={{0,8},{2,6},{8,16},{10,2},{16,24},{18,10},{24,28},{26,18},{28,20},... | collective-permute-start | bytes 393224 | tf_op jit(solution)/shard_map/ppermute | solution.py:313
  58.5 3.4 %collective-permute-start.29 = (bf16[128,512]{1,0:T(8,128)(2,1)S(1)}, bf16[128,512]{1,0:T(8,128)(2,1)S(1)}, u32[]{:S(2)}, u32[]{:S(2)}) collective-permute-start(bf16[128,512]{1,0:T(8,128)(2,1)S(1)} %collective-permute-done.28), channel_id=1, source_target_pairs={{0,2},{2,0},{4,6},{6,4},{8,10},{10,8},{12,14},{14,12},{16,18},{18,... | collective-permute-start | bytes 393224 | tf_op jit(solution)/shard_map/ppermute | solution.py:244
  58.6 6.2 %collective-permute-start.30 = (bf16[128,512]{1,0:T(8,128)(2,1)S(1)}, bf16[128,512]{1,0:T(8,128)(2,1)S(1)}, u32[]{:S(2)}, u32[]{:S(2)}) collective-permute-start(bf16[128,512]{1,0:T(8,128)(2,1)S(1)} %collective-permute-done.27), channel_id=1, source_target_pairs={{0,8},{2,6},{8,16},{10,2},{16,24},{18,10},{24,28},{26,18},{28,20},... | collective-permute-start | bytes 393224 | tf_op jit(solution)/shard_map/ppermute | solution.py:313
  60.0 5.5 %collective-permute-start.20 = (bf16[128,512]{1,0:T(8,128)(2,1)S(1)}, bf16[128,512]{1,0:T(8,128)(2,1)S(1)}, u32[]{:S(2)}, u32[]{:S(2)}) collective-permute-start(bf16[128,512]{1,0:T(8,128)(2,1)S(1)} %collective-permute-done.16), channel_id=1, source_target_pairs={{0,8},{2,6},{8,16},{10,2},{16,24},{18,10},{24,28},{26,18},{28,20},... | collective-permute-start | bytes 393224 | tf_op jit(solution)/shard_map/ppermute | solution.py:313
  61.8 1.8 %collective-permute-start.17 = (bf16[128,512]{1,0:T(8,128)(2,1)S(1)}, bf16[128,512]{1,0:T(8,128)(2,1)S(1)}, u32[]{:S(2)}, u32[]{:S(2)}) collective-permute-start(bf16[128,512]{1,0:T(8,128)(2,1)S(1)} %collective-permute-done.16), channel_id=1, source_target_pairs={{0,2},{2,0},{4,6},{6,4},{8,10},{10,8},{12,14},{14,12},{16,18},{18,... | collective-permute-start | bytes 393224 | tf_op jit(solution)/shard_map/ppermute | solution.py:244
  61.9 6.4 %collective-permute-start.22 = (bf16[128,512]{1,0:T(8,128)(2,1)S(1)}, bf16[128,512]{1,0:T(8,128)(2,1)S(1)}, u32[]{:S(2)}, u32[]{:S(2)}) collective-permute-start(bf16[128,512]{1,0:T(8,128)(2,1)S(1)} %collective-permute-done.18), channel_id=1, source_target_pairs={{0,8},{2,6},{8,16},{10,2},{16,24},{18,10},{24,28},{26,18},{28,20},... | collective-permute-start | bytes 393224 | tf_op jit(solution)/shard_map/ppermute | solution.py:313
  63.5 1.5 %collective-permute-start.19 = (bf16[128,512]{1,0:T(8,128)(2,1)S(1)}, bf16[128,512]{1,0:T(8,128)(2,1)S(1)}, u32[]{:S(2)}, u32[]{:S(2)}) collective-permute-start(bf16[128,512]{1,0:T(8,128)(2,1)S(1)} %collective-permute-done.18), channel_id=1, source_target_pairs={{0,2},{2,0},{4,6},{6,4},{8,10},{10,8},{12,14},{14,12},{16,18},{18,... | collective-permute-start | bytes 393224 | tf_op jit(solution)/shard_map/ppermute | solution.py:244
  63.6 5.0 %collective-permute-start.36 = (bf16[128,512]{1,0:T(8,128)(2,1)S(1)}, bf16[128,512]{1,0:T(8,128)(2,1)S(1)}, u32[]{:S(2)}, u32[]{:S(2)}) collective-permute-start(bf16[128,512]{1,0:T(8,128)(2,1)S(1)} %collective-permute-done.32), channel_id=1, source_target_pairs={{0,8},{2,6},{8,16},{10,2},{16,24},{18,10},{24,28},{26,18},{28,20},... | collective-permute-start | bytes 393224 | tf_op jit(solution)/shard_map/ppermute | solution.py:313
  64.9 4.0 %collective-permute-start.33 = (bf16[128,512]{1,0:T(8,128)(2,1)S(1)}, bf16[128,512]{1,0:T(8,128)(2,1)S(1)}, u32[]{:S(2)}, u32[]{:S(2)}) collective-permute-start(bf16[128,512]{1,0:T(8,128)(2,1)S(1)} %collective-permute-done.32), channel_id=1, source_target_pairs={{0,2},{2,0},{4,6},{6,4},{8,10},{10,8},{12,14},{14,12},{16,18},{18,... | collective-permute-start | bytes 393224 | tf_op jit(solution)/shard_map/ppermute | solution.py:244
  65.0 1.7 %collective-permute-start.31 = (bf16[128,512]{1,0:T(8,128)(2,1)S(1)}, bf16[128,512]{1,0:T(8,128)(2,1)S(1)}, u32[]{:S(2)}, u32[]{:S(2)}) collective-permute-start(bf16[128,512]{1,0:T(8,128)(2,1)S(1)} %collective-permute-done.30), channel_id=1, source_target_pairs={{0,2},{2,0},{4,6},{6,4},{8,10},{10,8},{12,14},{14,12},{16,18},{18,... | collective-permute-start | bytes 393224 | tf_op jit(solution)/shard_map/ppermute | solution.py:244
  65.5 5.0 %collective-permute-start.34 = (bf16[128,512]{1,0:T(8,128)(2,1)S(1)}, bf16[128,512]{1,0:T(8,128)(2,1)S(1)}, u32[]{:S(2)}, u32[]{:S(2)}) collective-permute-start(bf16[128,512]{1,0:T(8,128)(2,1)S(1)} %collective-permute-done.30), channel_id=1, source_target_pairs={{0,8},{2,6},{8,16},{10,2},{16,24},{18,10},{24,28},{26,18},{28,20},... | collective-permute-start | bytes 393224 | tf_op jit(solution)/shard_map/ppermute | solution.py:313
  66.7 5.2 %collective-permute-start.24 = (bf16[128,512]{1,0:T(8,128)(2,1)S(1)}, bf16[128,512]{1,0:T(8,128)(2,1)S(1)}, u32[]{:S(2)}, u32[]{:S(2)}) collective-permute-start(bf16[128,512]{1,0:T(8,128)(2,1)S(1)} %collective-permute-done.20), channel_id=1, source_target_pairs={{0,8},{2,6},{8,16},{10,2},{16,24},{18,10},{24,28},{26,18},{28,20},... | collective-permute-start | bytes 393224 | tf_op jit(solution)/shard_map/ppermute | solution.py:313
  68.3 2.3 %collective-permute-start.21 = (bf16[128,512]{1,0:T(8,128)(2,1)S(1)}, bf16[128,512]{1,0:T(8,128)(2,1)S(1)}, u32[]{:S(2)}, u32[]{:S(2)}) collective-permute-start(bf16[128,512]{1,0:T(8,128)(2,1)S(1)} %collective-permute-done.20), channel_id=1, source_target_pairs={{0,2},{2,0},{4,6},{6,4},{8,10},{10,8},{12,14},{14,12},{16,18},{18,... | collective-permute-start | bytes 393224 | tf_op jit(solution)/shard_map/ppermute | solution.py:244
  68.6 3.3 %collective-permute-start.23 = (bf16[128,512]{1,0:T(8,128)(2,1)S(1)}, bf16[128,512]{1,0:T(8,128)(2,1)S(1)}, u32[]{:S(2)}, u32[]{:S(2)}) collective-permute-start(bf16[128,512]{1,0:T(8,128)(2,1)S(1)} %collective-permute-done.22), channel_id=1, source_target_pairs={{0,2},{2,0},{4,6},{6,4},{8,10},{10,8},{12,14},{14,12},{16,18},{18,... | collective-permute-start | bytes 393224 | tf_op jit(solution)/shard_map/ppermute | solution.py:244
  68.9 5.0 %collective-permute-start.40 = (bf16[128,512]{1,0:T(8,128)(2,1)S(1)}, bf16[128,512]{1,0:T(8,128)(2,1)S(1)}, u32[]{:S(2)}, u32[]{:S(2)}) collective-permute-start(bf16[128,512]{1,0:T(8,128)(2,1)S(1)} %collective-permute-done.36), channel_id=1, source_target_pairs={{0,8},{2,6},{8,16},{10,2},{16,24},{18,10},{24,28},{26,18},{28,20},... | collective-permute-start | bytes 393224 | tf_op jit(solution)/shard_map/ppermute | solution.py:313
  70.5 5.0 %collective-permute-start.37 = (bf16[128,512]{1,0:T(8,128)(2,1)S(1)}, bf16[128,512]{1,0:T(8,128)(2,1)S(1)}, u32[]{:S(2)}, u32[]{:S(2)}) collective-permute-start(bf16[128,512]{1,0:T(8,128)(2,1)S(1)} %collective-permute-done.36), channel_id=1, source_target_pairs={{0,2},{2,0},{4,6},{6,4},{8,10},{10,8},{12,14},{14,12},{16,18},{18,... | collective-permute-start | bytes 393224 | tf_op jit(solution)/shard_map/ppermute | solution.py:244
  70.5 5.0 %collective-permute-start.38 = (bf16[128,512]{1,0:T(8,128)(2,1)S(1)}, bf16[128,512]{1,0:T(8,128)(2,1)S(1)}, u32[]{:S(2)}, u32[]{:S(2)}) collective-permute-start(bf16[128,512]{1,0:T(8,128)(2,1)S(1)} %collective-permute-done.34), channel_id=1, source_target_pairs={{0,8},{2,6},{8,16},{10,2},{16,24},{18,10},{24,28},{26,18},{28,20},... | collective-permute-start | bytes 393224 | tf_op jit(solution)/shard_map/ppermute | solution.py:313
  71.9 3.6 %collective-permute-start.35 = (bf16[128,512]{1,0:T(8,128)(2,1)S(1)}, bf16[128,512]{1,0:T(8,128)(2,1)S(1)}, u32[]{:S(2)}, u32[]{:S(2)}) collective-permute-start(bf16[128,512]{1,0:T(8,128)(2,1)S(1)} %collective-permute-done.34), channel_id=1, source_target_pairs={{0,2},{2,0},{4,6},{6,4},{8,10},{10,8},{12,14},{14,12},{16,18},{18,... | collective-permute-start | bytes 393224 | tf_op jit(solution)/shard_map/ppermute | solution.py:244
  71.9 5.0 %collective-permute-start.25 = (bf16[128,512]{1,0:T(8,128)(2,1)S(1)}, bf16[128,512]{1,0:T(8,128)(2,1)S(1)}, u32[]{:S(2)}, u32[]{:S(2)}) collective-permute-start(bf16[128,512]{1,0:T(8,128)(2,1)S(1)} %collective-permute-done.24), channel_id=1, source_target_pairs={{0,2},{2,0},{4,6},{6,4},{8,10},{10,8},{12,14},{14,12},{16,18},{18,... | collective-permute-start | bytes 393224 | tf_op jit(solution)/shard_map/ppermute | solution.py:244
  73.8 3.1 %collective-permute-start.41 = (bf16[128,512]{1,0:T(8,128)(2,1)S(1)}, bf16[128,512]{1,0:T(8,128)(2,1)S(1)}, u32[]{:S(2)}, u32[]{:S(2)}) collective-permute-start(bf16[128,512]{1,0:T(8,128)(2,1)S(1)} %collective-permute-done.40), channel_id=1, source_target_pairs={{0,2},{2,0},{4,6},{6,4},{8,10},{10,8},{12,14},{14,12},{16,18},{18,... | collective-permute-start | bytes 393224 | tf_op jit(solution)/shard_map/ppermute | solution.py:244
  75.5 1.3 %collective-permute-start.39 = (bf16[128,512]{1,0:T(8,128)(2,1)S(1)}, bf16[128,512]{1,0:T(8,128)(2,1)S(1)}, u32[]{:S(2)}, u32[]{:S(2)}) collective-permute-start(bf16[128,512]{1,0:T(8,128)(2,1)S(1)} %collective-permute-done.38), channel_id=1, source_target_pairs={{0,2},{2,0},{4,6},{6,4},{8,10},{10,8},{12,14},{14,12},{16,18},{18,... | collective-permute-start | bytes 393224 | tf_op jit(solution)/shard_map/ppermute | solution.py:244

commit v15 on v11

--- a/solution.py
+++ b/solution.py
@@ -163,15 +163,14 @@
     left_ref[...], right = inverse_roots(tile)
     rows = near_ref.shape[0]
     core, plane = side_ref[0], side_ref[1]
-    for out_ref, part in (
-        (near_ref, 2 * plane + core),
-        (next_ref, 2 * plane + 1 - core),
-        (far_ref, 2 * (1 - plane) + core),
-    ):
-        left = left_ref[pl.ds(pl.multiple_of(part * rows, rows), rows), :]
-        half = contract(left, tile_half, 1, 0).astype(jnp.bfloat16)
-        piece = contract(half, right, 1, 0) * math.sqrt(BLOCK)
-        out_ref[...] = piece.astype(jnp.bfloat16)
+    parts = (2 * plane + core, 2 * plane + 1 - core, 2 * (1 - plane) + core)
+    left = jnp.concatenate(
+        [left_ref[pl.ds(pl.multiple_of(part * rows, rows), rows), :] for part in parts]
+    )
+    half = contract(left, tile_half, 1, 0).astype(jnp.bfloat16)
+    pieces = (contract(half, right, 1, 0) * math.sqrt(BLOCK)).astype(jnp.bfloat16)
+    for number, out_ref in enumerate((near_ref, next_ref, far_ref)):
+        out_ref[...] = pieces[number * rows : (number + 1) * rows]
 
 
 OFFSETS = ((4, 7, 2), (5, 6, 3))

time: 79.4 us -> 79.1 us (level)
  transfers between devices with their start and end apart: 42 -> 42, of which waited for: 15 -> 14; matrix products, arithmetic and copies ran while one was open for 6% -> 6% of each run, Pallas kernels for 1% -> 1%
where the time goes in v15:
time: 79.1 us; the launch traced here: 79 us
  starting transfers between devices  42.5 us (54%)
  waiting for transfers between devices  17.3 us (22%)
  Pallas kernels  9.13 us (12%)
  matrix products  3.6 us (5%)
  other arithmetic  2.81 us (4%)
  local copies, waits for them, and re-layouts  2.23 us (3%)
  between operations  1.36 us (2%)
    ppermute x14, starting transfers between devices, turn(): return lax.ppermute(array, 'dp', pairs)  20.4 us
    ppermute x5, starting transfers between devices, exchange(): return lax.ppermute(array, 'dp', pairs)  9.35 us
    pallas_call x3, Pallas kernels, call(): pl.pallas_call(kernel, out_shape=out_shapes, in_specs=in_specs, out_specs...  9.13 us
    ppermute x4, starting transfers between devices, swap_plane(): lax.ppermute(array, 'pre', [(c, members - 1 - c) for c in range(members)])  6.98 us
    ppermute x4, waiting for transfers between devices, swap_plane(): lax.ppermute(array, 'pre', [(c, members - 1 - c) for c in range(members)])  6.21 us
    ppermute x14, waiting for transfers between devices, turn(): return lax.ppermute(array, 'dp', pairs)  4.28 us
    ppermute x3, starting transfers between devices, deal(): return lax.ppermute(array, ('dp', 'pre'), pairs)  3.88 us
    ppermute x16, waiting for transfers between devices, swap_core(): return lax.ppermute(array, 'dp', [(g, g ^ 1) for g in range(groups)])  3.65 us
  transfers between devices with their start and end apart: 42, of which 14 were waited for; matrix products, arithmetic and copies ran while one was open for 6% of the time, Pallas kernels for 1%

profile of v15, /device:TPU:0, one launch (start us, length us, event | category | flops | bytes accessed | tf_op | source)
XLA Modules:
  0.0 79.0 jit_solution(3571721379518359514)
XLA Ops:
  0.6 4.1 %collective-permute-start = (bf16[128,512]{1,0:T(8,128)(2,1)}, bf16[128,512]{1,0:T(8,128)(2,1)S(1)}, u32[]{:S(2)}, u32[]{:S(2)}) collective-permute-start(bf16[128,512]{1,0:T(8,128)(2,1)} %param.5), channel_id=1, source_target_pairs={{0,16},{2,18},{4,20},{6,22},{8,24},{10,26},{12,28},{14,30},{16,0},... | collective-permute-start | bytes 393224 | tf_op jit(solution)/shard_map/ppermute | solution.py:273
  4.8 1.2 %copy-done = bf16[128,4096]{1,0:T(8,128)(2,1)S(1)} copy-done((bf16[128,4096]{1,0:T(8,128)(2,1)S(1)}, bf16[128,4096]{1,0:T(8,128)(2,1)}, u32[]{:S(2)}) %copy-start) | copy-done | bytes 1048600
  6.0 0.6 shard_map.50
  6.6 1.6 %collective-permute-start.1 = (bf16[128,512]{1,0:T(8,128)(2,1)S(1)}, bf16[128,512]{1,0:T(8,128)(2,1)S(1)}, u32[]{:S(2)}, u32[]{:S(2)}) collective-permute-start(bf16[128,512]{1,0:T(8,128)(2,1)S(1)} %get-tuple-element.14), channel_id=1, source_target_pairs={{0,4},{2,6},{4,0},{6,2},{8,12},{10,14},{12,8},{14,10},{16,20},{18,... | collective-permute-start | bytes 393224 | tf_op jit(solution)/shard_map/ppermute | solution.py:273
  8.2 0.3 collective-permute-start.2
  8.6 3.5 %collective-permute-start.3 = (bf16[128,512]{1,0:T(8,128)(2,1)S(1)}, bf16[128,512]{1,0:T(8,128)(2,1)S(1)}, u32[]{:S(2)}, u32[]{:S(2)}) collective-permute-start(bf16[128,512]{1,0:T(8,128)(2,1)S(1)} %get-tuple-element.16), channel_id=1, source_target_pairs={{0,28},{1,25},{2,30},{3,27},{4,24},{5,29},{6,26},{7,31},{8,20},{9,... | collective-permute-start | bytes 393224 | tf_op jit(solution)/shard_map/ppermute | solution.py:257
  12.1 3.6 %convolution_convert_fusion = bf16[128,512]{1,0:T(8,128)(2,1)} fusion(bf16[128,4096]{1,0:T(8,128)(2,1)S(1)} %copy-done, bf16[4096,512]{1,0:T(8,128)(2,1)} %param.4), kind=kOutput, calls=%fused_computation.1 | convolution fusion | flops 536936448 | bytes 5373952 | tf_op jit(solution)/shard_map/dot_general | solution.py:275
  15.8 3.0 %collective-permute-start.10 = (bf16[256,512]{1,0:T(8,128)(2,1)S(1)}, bf16[256,512]{1,0:T(8,128)(2,1)S(1)}, u32[]{:S(2)}, u32[]{:S(2)}) collective-permute-start(bf16[256,512]{1,0:T(8,128)(2,1)S(1)} %constant_dynamic-update-slice_fusion.refs_6_), channel_id=1, source_target_pairs={{0,12},{2,14},{4,8},{6,10},{8,4},{10,6},{12,0},{14,2},{16,28},{18,... | collective-permute-start | bytes 786440 | tf_op jit(solution)/shard_map/ppermute | solution.py:273
  18.8 1.8 %collective-permute-done.2.refs_0_ = bf16[128,512]{1,0:T(8,128)(2,1)S(1)} collective-permute-done((bf16[128,512]{1,0:T(8,128)(2,1)S(1)}, bf16[128,512]{1,0:T(8,128)(2,1)S(1)}, u32[]{:S(2)}, u32[]{:S(2)}) %collective-permute-start.2) | collective-permute-done | bytes 131104 | tf_op jit(solution)/shard_map/ppermute | solution.py:257
  20.6 2.4 %collective-permute-start.5 = (bf16[128,512]{1,0:T(8,128)(2,1)S(1)}, bf16[128,512]{1,0:T(8,128)(2,1)S(1)}, u32[]{:S(2)}, u32[]{:S(2)}) collective-permute-start(bf16[128,512]{1,0:T(8,128)(2,1)S(1)} %collective-permute-done.2.refs_0_), channel_id=1, source_target_pairs={{0,1},{1,0},{2,3},{3,2},{4,5},{5,4},{6,7},{7,6},{8,9},{9,8},{10,11... | collective-permute-start | bytes 393224 | tf_op jit(solution)/shard_map/ppermute | solution.py:245
  23.0 0.6 collective-permute-start.8
  23.6 1.0 %collective-permute-start.6 = (bf16[128,512]{1,0:T(8,128)(2,1)S(1)}, bf16[128,512]{1,0:T(8,128)(2,1)S(1)}, u32[]{:S(2)}, u32[]{:S(2)}) collective-permute-start(bf16[128,512]{1,0:T(8,128)(2,1)S(1)} %collective-permute-done.3.refs_1_), channel_id=1, source_target_pairs={{0,1},{1,0},{2,3},{3,2},{4,5},{5,4},{6,7},{7,6},{8,9},{9,8},{10,11... | collective-permute-start | bytes 393224 | tf_op jit(solution)/shard_map/ppermute | solution.py:245
  24.6 2.3 %collective-permute-done.5.refs_3_ = bf16[128,512]{1,0:T(8,128)(2,1)S(1)} collective-permute-done((bf16[128,512]{1,0:T(8,128)(2,1)S(1)}, bf16[128,512]{1,0:T(8,128)(2,1)S(1)}, u32[]{:S(2)}, u32[]{:S(2)}) %collective-permute-start.5) | collective-permute-done | bytes 131104 | tf_op jit(solution)/shard_map/ppermute | solution.py:245
  26.8 2.5 %collective-permute-start.7 = (bf16[128,512]{1,0:T(8,128)(2,1)S(1)}, bf16[128,512]{1,0:T(8,128)(2,1)S(1)}, u32[]{:S(2)}, u32[]{:S(2)}) collective-permute-start(bf16[128,512]{1,0:T(8,128)(2,1)S(1)} %collective-permute-done.4.refs_2_), channel_id=1, source_target_pairs={{0,1},{1,0},{2,3},{3,2},{4,5},{5,4},{6,7},{7,6},{8,9},{9,8},{10,11... | collective-permute-start | bytes 393224 | tf_op jit(solution)/shard_map/ppermute | solution.py:245
  29.4 0.6 collective-permute-done.6.refs_4_
  30.0 2.2 %collective-permute-done.7.refs_5_ = bf16[128,512]{1,0:T(8,128)(2,1)S(1)} collective-permute-done((bf16[128,512]{1,0:T(8,128)(2,1)S(1)}, bf16[128,512]{1,0:T(8,128)(2,1)S(1)}, u32[]{:S(2)}, u32[]{:S(2)}) %collective-permute-start.7) | collective-permute-done | bytes 131104 | tf_op jit(solution)/shard_map/ppermute | solution.py:245
  32.3 1.4 %collective-permute-done.8.refs_7_ = bf16[256,512]{1,0:T(8,128)(2,1)S(1)} collective-permute-done((bf16[256,512]{1,0:T(8,128)(2,1)S(1)}, bf16[256,512]{1,0:T(8,128)(2,1)S(1)}, u32[]{:S(2)}, u32[]{:S(2)}) %collective-permute-start.8) | collective-permute-done | bytes 262176 | tf_op jit(solution)/shard_map/ppermute | solution.py:273
  33.6 1.4 %shard_map.51.mine_ref = f32[512,512]{1,0:T(8,128)S(1)} custom-call(s32[2]{0:T(128)S(1)} %pad_add_fusion.1.place_ref, bf16[128,512]{1,0:T(8,128)(2,1)S(1)} %get-tuple-element.13.own_ref, bf16[128,512]{1,0:T(8,128)(2,1)S(1)} %collective-permute-done.1.shared_ref, bf16[128,512]{1,0:T(8,128)(2,1)S(1)} %collective-permute-done.2.refs_0_, ...), custom_call_target="tpu_custom_call" | custom-call | tf_op jit(solution)/shard_map/pallas_call | solution.py:217
  35.5 2.3 %collective-permute-done.11.other_ref = f32[512,512]{1,0:T(8,128)S(1)} collective-permute-done((f32[512,512]{1,0:T(8,128)S(1)}, f32[512,512]{1,0:T(8,128)S(1)}, u32[]{:S(2)}, u32[]{:S(2)}) %collective-permute-start.11) | collective-permute-done | bytes 1048608 | tf_op jit(solution)/shard_map/ppermute | solution.py:242
  37.8 7.1 %shard_map.52 = (bf16[128,512]{1,0:T(8,128)(2,1)S(1)}, bf16[128,512]{1,0:T(8,128)(2,1)S(1)}, bf16[128,512]{1,0:T(8,128)(2,1)S(1)}) custom-call(s32[2]{0:T(128)S(1)} %pad_add_fusion.side_ref, f32[512,512]{1,0:T(8,128)S(1)} %shard_map.51.mine_ref, f32[512,512]{1,0:T(8,128)S(1)} %collective-permute-done.11.other_ref), custom_call_target="tpu_custom_call" | custom-call | tf_op jit(solution)/shard_map/pallas_call | solution.py:217
  44.9 1.1 %collective-permute-start.26 = (bf16[128,512]{1,0:T(8,128)(2,1)S(1)}, bf16[128,512]{1,0:T(8,128)(2,1)S(1)}, u32[]{:S(2)}, u32[]{:S(2)}) collective-permute-start(bf16[128,512]{1,0:T(8,128)(2,1)S(1)} %get-tuple-element.21), channel_id=1, source_target_pairs={{0,1},{1,0},{2,3},{3,2},{4,5},{5,4},{6,7},{7,6},{8,9},{9,8},{10,11... | collective-permute-start | bytes 393224 | tf_op jit(solution)/shard_map/ppermute | solution.py:245
  46.1 3.1 %collective-permute-start.14 = (bf16[128,512]{1,0:T(8,128)(2,1)S(1)}, bf16[128,512]{1,0:T(8,128)(2,1)S(1)}, u32[]{:S(2)}, u32[]{:S(2)}) collective-permute-start(bf16[128,512]{1,0:T(8,128)(2,1)S(1)} %get-tuple-element.20), channel_id=1, source_target_pairs={{0,8},{2,6},{8,16},{10,2},{16,24},{18,10},{24,28},{26,18},{28,20},... | collective-permute-start | bytes 393224 | tf_op jit(solution)/shard_map/ppermute | solution.py:311
  49.2 0.2 broadcast_in_dim.99.clone.1
  49.5 1.1 %collective-permute-done.26 = bf16[128,512]{1,0:T(8,128)(2,1)S(1)} collective-permute-done((bf16[128,512]{1,0:T(8,128)(2,1)S(1)}, bf16[128,512]{1,0:T(8,128)(2,1)S(1)}, u32[]{:S(2)}, u32[]{:S(2)}) %collective-permute-start.26) | collective-permute-done | bytes 131104 | tf_op jit(solution)/shard_map/ppermute | solution.py:245
  50.5 1.1 %collective-permute-start.28 = (bf16[128,512]{1,0:T(8,128)(2,1)S(1)}, bf16[128,512]{1,0:T(8,128)(2,1)S(1)}, u32[]{:S(2)}, u32[]{:S(2)}) collective-permute-start(bf16[128,512]{1,0:T(8,128)(2,1)S(1)} %collective-permute-done.26), channel_id=1, source_target_pairs={{0,8},{2,6},{8,16},{10,2},{16,24},{18,10},{24,28},{26,18},{28,20},... | collective-permute-start | bytes 393224 | tf_op jit(solution)/shard_map/ppermute | solution.py:311
  51.6 3.1 %collective-permute-start.16 = (bf16[128,512]{1,0:T(8,128)(2,1)S(1)}, bf16[128,512]{1,0:T(8,128)(2,1)S(1)}, u32[]{:S(2)}, u32[]{:S(2)}) collective-permute-start(bf16[128,512]{1,0:T(8,128)(2,1)S(1)} %collective-permute-done.12), channel_id=1, source_target_pairs={{0,8},{2,6},{8,16},{10,2},{16,24},{18,10},{24,28},{26,18},{28,20},... | collective-permute-start | bytes 393224 | tf_op jit(solution)/shard_map/ppermute | solution.py:311
  54.7 0.5 collective-permute-start.18
  55.2 0.2 broadcast_in_dim.99.clone
  55.5 1.8 %collective-permute-start.32 = (bf16[128,512]{1,0:T(8,128)(2,1)S(1)}, bf16[128,512]{1,0:T(8,128)(2,1)S(1)}, u32[]{:S(2)}, u32[]{:S(2)}) collective-permute-start(bf16[128,512]{1,0:T(8,128)(2,1)S(1)} %collective-permute-done.28), channel_id=1, source_target_pairs={{0,8},{2,6},{8,16},{10,2},{16,24},{18,10},{24,28},{26,18},{28,20},... | collective-permute-start | bytes 393224 | tf_op jit(solution)/shard_map/ppermute | solution.py:311
  57.5 2.4 %collective-permute-start.30 = (bf16[128,512]{1,0:T(8,128)(2,1)S(1)}, bf16[128,512]{1,0:T(8,128)(2,1)S(1)}, u32[]{:S(2)}, u32[]{:S(2)}) collective-permute-start(bf16[128,512]{1,0:T(8,128)(2,1)S(1)} %collective-permute-done.27), channel_id=1, source_target_pairs={{0,8},{2,6},{8,16},{10,2},{16,24},{18,10},{24,28},{26,18},{28,20},... | collective-permute-start | bytes 393224 | tf_op jit(solution)/shard_map/ppermute | solution.py:311
  59.9 1.2 %collective-permute-start.20 = (bf16[128,512]{1,0:T(8,128)(2,1)S(1)}, bf16[128,512]{1,0:T(8,128)(2,1)S(1)}, u32[]{:S(2)}, u32[]{:S(2)}) collective-permute-start(bf16[128,512]{1,0:T(8,128)(2,1)S(1)} %collective-permute-done.16), channel_id=1, source_target_pairs={{0,8},{2,6},{8,16},{10,2},{16,24},{18,10},{24,28},{26,18},{28,20},... | collective-permute-start | bytes 393224 | tf_op jit(solution)/shard_map/ppermute | solution.py:311
  61.2 1.1 %collective-permute-start.22 = (bf16[128,512]{1,0:T(8,128)(2,1)S(1)}, bf16[128,512]{1,0:T(8,128)(2,1)S(1)}, u32[]{:S(2)}, u32[]{:S(2)}) collective-permute-start(bf16[128,512]{1,0:T(8,128)(2,1)S(1)} %collective-permute-done.18), channel_id=1, source_target_pairs={{0,8},{2,6},{8,16},{10,2},{16,24},{18,10},{24,28},{26,18},{28,20},... | collective-permute-start | bytes 393224 | tf_op jit(solution)/shard_map/ppermute | solution.py:311
  62.5 1.1 %collective-permute-start.36 = (bf16[128,512]{1,0:T(8,128)(2,1)S(1)}, bf16[128,512]{1,0:T(8,128)(2,1)S(1)}, u32[]{:S(2)}, u32[]{:S(2)}) collective-permute-start(bf16[128,512]{1,0:T(8,128)(2,1)S(1)} %collective-permute-done.32), channel_id=1, source_target_pairs={{0,8},{2,6},{8,16},{10,2},{16,24},{18,10},{24,28},{26,18},{28,20},... | collective-permute-start | bytes 393224 | tf_op jit(solution)/shard_map/ppermute | solution.py:311
  63.7 0.1 collective-permute-start.33
  63.8 0.4 collective-permute-start.31
  64.3 0.6 collective-permute-done.20
  64.9 1.4 %collective-permute-start.34 = (bf16[128,512]{1,0:T(8,128)(2,1)S(1)}, bf16[128,512]{1,0:T(8,128)(2,1)S(1)}, u32[]{:S(2)}, u32[]{:S(2)}) collective-permute-start(bf16[128,512]{1,0:T(8,128)(2,1)S(1)} %collective-permute-done.30), channel_id=1, source_target_pairs={{0,8},{2,6},{8,16},{10,2},{16,24},{18,10},{24,28},{26,18},{28,20},... | collective-permute-start | bytes 393224 | tf_op jit(solution)/shard_map/ppermute | solution.py:311
  66.3 1.2 %collective-permute-start.24 = (bf16[128,512]{1,0:T(8,128)(2,1)S(1)}, bf16[128,512]{1,0:T(8,128)(2,1)S(1)}, u32[]{:S(2)}, u32[]{:S(2)}) collective-permute-start(bf16[128,512]{1,0:T(8,128)(2,1)S(1)} %collective-permute-done.20), channel_id=1, source_target_pairs={{0,8},{2,6},{8,16},{10,2},{16,24},{18,10},{24,28},{26,18},{28,20},... | collective-permute-start | bytes 393224 | tf_op jit(solution)/shard_map/ppermute | solution.py:311
  67.6 0.1 collective-permute-done.36
  67.7 0.4 collective-permute-start.23
  68.1 1.0 %collective-permute-start.40 = (bf16[128,512]{1,0:T(8,128)(2,1)S(1)}, bf16[128,512]{1,0:T(8,128)(2,1)S(1)}, u32[]{:S(2)}, u32[]{:S(2)}) collective-permute-start(bf16[128,512]{1,0:T(8,128)(2,1)S(1)} %collective-permute-done.36), channel_id=1, source_target_pairs={{0,8},{2,6},{8,16},{10,2},{16,24},{18,10},{24,28},{26,18},{28,20},... | collective-permute-start | bytes 393224 | tf_op jit(solution)/shard_map/ppermute | solution.py:311
  69.2 0.7 collective-permute-done.34
  69.8 1.4 %collective-permute-start.38 = (bf16[128,512]{1,0:T(8,128)(2,1)S(1)}, bf16[128,512]{1,0:T(8,128)(2,1)S(1)}, u32[]{:S(2)}, u32[]{:S(2)}) collective-permute-start(bf16[128,512]{1,0:T(8,128)(2,1)S(1)} %collective-permute-done.34), channel_id=1, source_target_pairs={{0,8},{2,6},{8,16},{10,2},{16,24},{18,10},{24,28},{26,18},{28,20},... | collective-permute-start | bytes 393224 | tf_op jit(solution)/shard_map/ppermute | solution.py:311
  71.4 0.5 collective-permute-start.25
  71.9 1.1 %collective-permute-done.40 = bf16[128,512]{1,0:T(8,128)(2,1)S(1)} collective-permute-done((bf16[128,512]{1,0:T(8,128)(2,1)S(1)}, bf16[128,512]{1,0:T(8,128)(2,1)S(1)}, u32[]{:S(2)}, u32[]{:S(2)}) %collective-permute-start.40) | collective-permute-done | bytes 131104 | tf_op jit(solution)/shard_map/ppermute | solution.py:311
  73.1 1.7 %collective-permute-done.38 = bf16[128,512]{1,0:T(8,128)(2,1)S(1)} collective-permute-done((bf16[128,512]{1,0:T(8,128)(2,1)S(1)}, bf16[128,512]{1,0:T(8,128)(2,1)S(1)}, u32[]{:S(2)}, u32[]{:S(2)}) %collective-permute-start.38) | collective-permute-done | bytes 131104 | tf_op jit(solution)/shard_map/ppermute | solution.py:311
  74.9 1.2 %collective-permute-done.39 = bf16[128,512]{1,0:T(8,128)(2,1)S(1)} collective-permute-done((bf16[128,512]{1,0:T(8,128)(2,1)S(1)}, bf16[128,512]{1,0:T(8,128)(2,1)S(1)}, u32[]{:S(2)}, u32[]{:S(2)}) %collective-permute-start.39) | collective-permute-done | bytes 131104 | tf_op jit(solution)/shard_map/ppermute | solution.py:242
  76.3 2.7 %maximum_select_fusion = bf16[8,256,1024]{2,1,0:T(8,128)(2,1)} fusion(bf16[8,256,512]{2,1,0:T(8,128)(2,1)S(1)} %bitcast.75, bf16[8,256,512]{2,1,0:T(8,128)(2,1)S(1)} %bitcast.76, pred[]{:T(512)S(6)} %eq.44), kind=kLoop, calls=%fused_computation | loop fusion | flops 18874368 | bytes 8388609 | tf_op jit(solution)/shard_map/jit(_where)/select_n | solution.py:333
  (83 shorter events, 1.6 us)
Async XLA Ops:
  0.6 15.1 %collective-permute-start = (bf16[128,512]{1,0:T(8,128)(2,1)}, bf16[128,512]{1,0:T(8,128)(2,1)S(1)}, u32[]{:S(2)}, u32[]{:S(2)}) collective-permute-start(bf16[128,512]{1,0:T(8,128)(2,1)} %param.5), channel_id=1, source_target_pairs={{0,16},{2,18},{4,20},{6,22},{8,24},{10,26},{12,28},{14,30},{16,0},... | collective-permute-start | bytes 393224 | tf_op jit(solution)/shard_map/ppermute | solution.py:273
  4.8 1.2 %copy-start = (bf16[128,4096]{1,0:T(8,128)(2,1)S(1)}, bf16[128,4096]{1,0:T(8,128)(2,1)}, u32[]{:S(2)}) copy-start(bf16[128,4096]{1,0:T(8,128)(2,1)} %inputs_ref.1) | copy-start | bytes 3145732
  6.6 16.4 %collective-permute-start.1 = (bf16[128,512]{1,0:T(8,128)(2,1)S(1)}, bf16[128,512]{1,0:T(8,128)(2,1)S(1)}, u32[]{:S(2)}, u32[]{:S(2)}) collective-permute-start(bf16[128,512]{1,0:T(8,128)(2,1)S(1)} %get-tuple-element.14), channel_id=1, source_target_pairs={{0,4},{2,6},{4,0},{6,2},{8,12},{10,14},{12,8},{14,10},{16,20},{18,... | collective-permute-start | bytes 393224 | tf_op jit(solution)/shard_map/ppermute | solution.py:273
  8.2 12.4 %collective-permute-start.2 = (bf16[128,512]{1,0:T(8,128)(2,1)S(1)}, bf16[128,512]{1,0:T(8,128)(2,1)S(1)}, u32[]{:S(2)}, u32[]{:S(2)}) collective-permute-start(bf16[128,512]{1,0:T(8,128)(2,1)S(1)} %get-tuple-element.15), channel_id=1, source_target_pairs={{0,16},{1,21},{2,18},{3,23},{4,20},{5,17},{6,22},{7,19},{8,24},{9,... | collective-permute-start | bytes 393224 | tf_op jit(solution)/shard_map/ppermute | solution.py:257
  8.6 14.4 %collective-permute-start.3 = (bf16[128,512]{1,0:T(8,128)(2,1)S(1)}, bf16[128,512]{1,0:T(8,128)(2,1)S(1)}, u32[]{:S(2)}, u32[]{:S(2)}) collective-permute-start(bf16[128,512]{1,0:T(8,128)(2,1)S(1)} %get-tuple-element.16), channel_id=1, source_target_pairs={{0,28},{1,25},{2,30},{3,27},{4,24},{5,29},{6,26},{7,31},{8,20},{9,... | collective-permute-start | bytes 393224 | tf_op jit(solution)/shard_map/ppermute | solution.py:257
  12.1 3.6 %copy-start.1 = (bf16[128,512]{1,0:T(8,128)(2,1)S(1)}, bf16[128,512]{1,0:T(8,128)(2,1)}, u32[]{:S(2)}) copy-start(bf16[128,512]{1,0:T(8,128)(2,1)} %param.5) | copy-start | bytes 393220
  12.1 11.5 %collective-permute-start.4 = (bf16[128,512]{1,0:T(8,128)(2,1)S(1)}, bf16[128,512]{1,0:T(8,128)(2,1)S(1)}, u32[]{:S(2)}, u32[]{:S(2)}) collective-permute-start(bf16[128,512]{1,0:T(8,128)(2,1)S(1)} %get-tuple-element.17), channel_id=1, source_target_pairs={{0,8},{1,13},{2,10},{3,15},{4,12},{5,9},{6,14},{7,11},{8,0},{9,5},... | collective-permute-start | bytes 393224 | tf_op jit(solution)/shard_map/ppermute | solution.py:257
  15.8 16.5 %collective-permute-start.10 = (bf16[256,512]{1,0:T(8,128)(2,1)S(1)}, bf16[256,512]{1,0:T(8,128)(2,1)S(1)}, u32[]{:S(2)}, u32[]{:S(2)}) collective-permute-start(bf16[256,512]{1,0:T(8,128)(2,1)S(1)} %constant_dynamic-update-slice_fusion.refs_6_), channel_id=1, source_target_pairs={{0,12},{2,14},{4,8},{6,10},{8,4},{10,6},{12,0},{14,2},{16,28},{18,... | collective-permute-start | bytes 786440 | tf_op jit(solution)/shard_map/ppermute | solution.py:273
  20.6 6.2 %collective-permute-start.5 = (bf16[128,512]{1,0:T(8,128)(2,1)S(1)}, bf16[128,512]{1,0:T(8,128)(2,1)S(1)}, u32[]{:S(2)}, u32[]{:S(2)}) collective-permute-start(bf16[128,512]{1,0:T(8,128)(2,1)S(1)} %collective-permute-done.2.refs_0_), channel_id=1, source_target_pairs={{0,1},{1,0},{2,3},{3,2},{4,5},{5,4},{6,7},{7,6},{8,9},{9,8},{10,11... | collective-permute-start | bytes 393224 | tf_op jit(solution)/shard_map/ppermute | solution.py:245
  23.0 9.3 %collective-permute-start.9 = (bf16[256,512]{1,0:T(8,128)(2,1)S(1)}, bf16[256,512]{1,0:T(8,128)(2,1)S(1)}, u32[]{:S(2)}, u32[]{:S(2)}) collective-permute-start(bf16[256,512]{1,0:T(8,128)(2,1)S(1)} %constant_dynamic-update-slice_fusion.refs_6_), channel_id=1, source_target_pairs={{0,8},{2,10},{4,12},{6,14},{8,0},{10,2},{12,4},{14,6},{16,24},{18,... | collective-permute-start | bytes 786440 | tf_op jit(solution)/shard_map/ppermute | solution.py:273
  23.0 10.6 %collective-permute-start.8 = (bf16[256,512]{1,0:T(8,128)(2,1)S(1)}, bf16[256,512]{1,0:T(8,128)(2,1)S(1)}, u32[]{:S(2)}, u32[]{:S(2)}) collective-permute-start(bf16[256,512]{1,0:T(8,128)(2,1)S(1)} %constant_dynamic-update-slice_fusion.refs_6_), channel_id=1, source_target_pairs={{0,4},{2,6},{4,0},{6,2},{8,12},{10,14},{12,8},{14,10},{16,20},{18,... | collective-permute-start | bytes 786440 | tf_op jit(solution)/shard_map/ppermute | solution.py:273
  23.6 6.4 %collective-permute-start.6 = (bf16[128,512]{1,0:T(8,128)(2,1)S(1)}, bf16[128,512]{1,0:T(8,128)(2,1)S(1)}, u32[]{:S(2)}, u32[]{:S(2)}) collective-permute-start(bf16[128,512]{1,0:T(8,128)(2,1)S(1)} %collective-permute-done.3.refs_1_), channel_id=1, source_target_pairs={{0,1},{1,0},{2,3},{3,2},{4,5},{5,4},{6,7},{7,6},{8,9},{9,8},{10,11... | collective-permute-start | bytes 393224 | tf_op jit(solution)/shard_map/ppermute | solution.py:245
  26.8 5.4 %collective-permute-start.7 = (bf16[128,512]{1,0:T(8,128)(2,1)S(1)}, bf16[128,512]{1,0:T(8,128)(2,1)S(1)}, u32[]{:S(2)}, u32[]{:S(2)}) collective-permute-start(bf16[128,512]{1,0:T(8,128)(2,1)S(1)} %collective-permute-done.4.refs_2_), channel_id=1, source_target_pairs={{0,1},{1,0},{2,3},{3,2},{4,5},{5,4},{6,7},{7,6},{8,9},{9,8},{10,11... | collective-permute-start | bytes 393224 | tf_op jit(solution)/shard_map/ppermute | solution.py:245
  35.0 2.7 %collective-permute-start.11 = (f32[512,512]{1,0:T(8,128)S(1)}, f32[512,512]{1,0:T(8,128)S(1)}, u32[]{:S(2)}, u32[]{:S(2)}) collective-permute-start(f32[512,512]{1,0:T(8,128)S(1)} %shard_map.51.mine_ref), channel_id=1, source_target_pairs={{0,2},{2,0},{4,6},{6,4},{8,10},{10,8},{12,14},{14,12},{16,18},{18,... | collective-permute-start | bytes 3145736 | tf_op jit(solution)/shard_map/ppermute | solution.py:242
  44.9 5.6 %collective-permute-start.26 = (bf16[128,512]{1,0:T(8,128)(2,1)S(1)}, bf16[128,512]{1,0:T(8,128)(2,1)S(1)}, u32[]{:S(2)}, u32[]{:S(2)}) collective-permute-start(bf16[128,512]{1,0:T(8,128)(2,1)S(1)} %get-tuple-element.21), channel_id=1, source_target_pairs={{0,1},{1,0},{2,3},{3,2},{4,5},{5,4},{6,7},{7,6},{8,9},{9,8},{10,11... | collective-permute-start | bytes 393224 | tf_op jit(solution)/shard_map/ppermute | solution.py:245
  46.1 5.5 %collective-permute-start.12 = (bf16[128,512]{1,0:T(8,128)(2,1)S(1)}, bf16[128,512]{1,0:T(8,128)(2,1)S(1)}, u32[]{:S(2)}, u32[]{:S(2)}) collective-permute-start(bf16[128,512]{1,0:T(8,128)(2,1)S(1)} %get-tuple-element.19), channel_id=1, source_target_pairs={{0,8},{2,6},{8,16},{10,2},{16,24},{18,10},{24,28},{26,18},{28,20},... | collective-permute-start | bytes 393224 | tf_op jit(solution)/shard_map/ppermute | solution.py:311
  46.1 8.6 %collective-permute-start.14 = (bf16[128,512]{1,0:T(8,128)(2,1)S(1)}, bf16[128,512]{1,0:T(8,128)(2,1)S(1)}, u32[]{:S(2)}, u32[]{:S(2)}) collective-permute-start(bf16[128,512]{1,0:T(8,128)(2,1)S(1)} %get-tuple-element.20), channel_id=1, source_target_pairs={{0,8},{2,6},{8,16},{10,2},{16,24},{18,10},{24,28},{26,18},{28,20},... | collective-permute-start | bytes 393224 | tf_op jit(solution)/shard_map/ppermute | solution.py:311
  50.5 5.0 %collective-permute-start.28 = (bf16[128,512]{1,0:T(8,128)(2,1)S(1)}, bf16[128,512]{1,0:T(8,128)(2,1)S(1)}, u32[]{:S(2)}, u32[]{:S(2)}) collective-permute-start(bf16[128,512]{1,0:T(8,128)(2,1)S(1)} %collective-permute-done.26), channel_id=1, source_target_pairs={{0,8},{2,6},{8,16},{10,2},{16,24},{18,10},{24,28},{26,18},{28,20},... | collective-permute-start | bytes 393224 | tf_op jit(solution)/shard_map/ppermute | solution.py:311
  51.6 3.9 %collective-permute-start.27 = (bf16[128,512]{1,0:T(8,128)(2,1)S(1)}, bf16[128,512]{1,0:T(8,128)(2,1)S(1)}, u32[]{:S(2)}, u32[]{:S(2)}) collective-permute-start(bf16[128,512]{1,0:T(8,128)(2,1)S(1)} %collective-permute-done.26), channel_id=1, source_target_pairs={{0,2},{2,0},{4,6},{6,4},{8,10},{10,8},{12,14},{14,12},{16,18},{18,... | collective-permute-start | bytes 393224 | tf_op jit(solution)/shard_map/ppermute | solution.py:242
  51.6 5.9 %collective-permute-start.16 = (bf16[128,512]{1,0:T(8,128)(2,1)S(1)}, bf16[128,512]{1,0:T(8,128)(2,1)S(1)}, u32[]{:S(2)}, u32[]{:S(2)}) collective-permute-start(bf16[128,512]{1,0:T(8,128)(2,1)S(1)} %collective-permute-done.12), channel_id=1, source_target_pairs={{0,8},{2,6},{8,16},{10,2},{16,24},{18,10},{24,28},{26,18},{28,20},... | collective-permute-start | bytes 393224 | tf_op jit(solution)/shard_map/ppermute | solution.py:311
  54.7 2.7 %collective-permute-start.13 = (bf16[128,512]{1,0:T(8,128)(2,1)S(1)}, bf16[128,512]{1,0:T(8,128)(2,1)S(1)}, u32[]{:S(2)}, u32[]{:S(2)}) collective-permute-start(bf16[128,512]{1,0:T(8,128)(2,1)S(1)} %collective-permute-done.12), channel_id=1, source_target_pairs={{0,2},{2,0},{4,6},{6,4},{8,10},{10,8},{12,14},{14,12},{16,18},{18,... | collective-permute-start | bytes 393224 | tf_op jit(solution)/shard_map/ppermute | solution.py:242
  54.7 6.4 %collective-permute-start.18 = (bf16[128,512]{1,0:T(8,128)(2,1)S(1)}, bf16[128,512]{1,0:T(8,128)(2,1)S(1)}, u32[]{:S(2)}, u32[]{:S(2)}) collective-permute-start(bf16[128,512]{1,0:T(8,128)(2,1)S(1)} %collective-permute-done.14), channel_id=1, source_target_pairs={{0,8},{2,6},{8,16},{10,2},{16,24},{18,10},{24,28},{26,18},{28,20},... | collective-permute-start | bytes 393224 | tf_op jit(solution)/shard_map/ppermute | solution.py:311
  55.5 4.4 %collective-permute-start.15 = (bf16[128,512]{1,0:T(8,128)(2,1)S(1)}, bf16[128,512]{1,0:T(8,128)(2,1)S(1)}, u32[]{:S(2)}, u32[]{:S(2)}) collective-permute-start(bf16[128,512]{1,0:T(8,128)(2,1)S(1)} %collective-permute-done.14), channel_id=1, source_target_pairs={{0,2},{2,0},{4,6},{6,4},{8,10},{10,8},{12,14},{14,12},{16,18},{18,... | collective-permute-start | bytes 393224 | tf_op jit(solution)/shard_map/ppermute | solution.py:242
  55.5 6.8 %collective-permute-start.32 = (bf16[128,512]{1,0:T(8,128)(2,1)S(1)}, bf16[128,512]{1,0:T(8,128)(2,1)S(1)}, u32[]{:S(2)}, u32[]{:S(2)}) collective-permute-start(bf16[128,512]{1,0:T(8,128)(2,1)S(1)} %collective-permute-done.28), channel_id=1, source_target_pairs={{0,8},{2,6},{8,16},{10,2},{16,24},{18,10},{24,28},{26,18},{28,20},... | collective-permute-start | bytes 393224 | tf_op jit(solution)/shard_map/ppermute | solution.py:311
  57.4 3.8 %collective-permute-start.29 = (bf16[128,512]{1,0:T(8,128)(2,1)S(1)}, bf16[128,512]{1,0:T(8,128)(2,1)S(1)}, u32[]{:S(2)}, u32[]{:S(2)}) collective-permute-start(bf16[128,512]{1,0:T(8,128)(2,1)S(1)} %collective-permute-done.28), channel_id=1, source_target_pairs={{0,2},{2,0},{4,6},{6,4},{8,10},{10,8},{12,14},{14,12},{16,18},{18,... | collective-permute-start | bytes 393224 | tf_op jit(solution)/shard_map/ppermute | solution.py:242
  57.5 6.1 %collective-permute-start.30 = (bf16[128,512]{1,0:T(8,128)(2,1)S(1)}, bf16[128,512]{1,0:T(8,128)(2,1)S(1)}, u32[]{:S(2)}, u32[]{:S(2)}) collective-permute-start(bf16[128,512]{1,0:T(8,128)(2,1)S(1)} %collective-permute-done.27), channel_id=1, source_target_pairs={{0,8},{2,6},{8,16},{10,2},{16,24},{18,10},{24,28},{26,18},{28,20},... | collective-permute-start | bytes 393224 | tf_op jit(solution)/shard_map/ppermute | solution.py:311
  59.9 5.0 %collective-permute-start.20 = (bf16[128,512]{1,0:T(8,128)(2,1)S(1)}, bf16[128,512]{1,0:T(8,128)(2,1)S(1)}, u32[]{:S(2)}, u32[]{:S(2)}) collective-permute-start(bf16[128,512]{1,0:T(8,128)(2,1)S(1)} %collective-permute-done.16), channel_id=1, source_target_pairs={{0,8},{2,6},{8,16},{10,2},{16,24},{18,10},{24,28},{26,18},{28,20},... | collective-permute-start | bytes 393224 | tf_op jit(solution)/shard_map/ppermute | solution.py:311
  61.1 1.4 %collective-permute-start.17 = (bf16[128,512]{1,0:T(8,128)(2,1)S(1)}, bf16[128,512]{1,0:T(8,128)(2,1)S(1)}, u32[]{:S(2)}, u32[]{:S(2)}) collective-permute-start(bf16[128,512]{1,0:T(8,128)(2,1)S(1)} %collective-permute-done.16), channel_id=1, source_target_pairs={{0,2},{2,0},{4,6},{6,4},{8,10},{10,8},{12,14},{14,12},{16,18},{18,... | collective-permute-start | bytes 393224 | tf_op jit(solution)/shard_map/ppermute | solution.py:242
  61.2 6.3 %collective-permute-start.22 = (bf16[128,512]{1,0:T(8,128)(2,1)S(1)}, bf16[128,512]{1,0:T(8,128)(2,1)S(1)}, u32[]{:S(2)}, u32[]{:S(2)}) collective-permute-start(bf16[128,512]{1,0:T(8,128)(2,1)S(1)} %collective-permute-done.18), channel_id=1, source_target_pairs={{0,8},{2,6},{8,16},{10,2},{16,24},{18,10},{24,28},{26,18},{28,20},... | collective-permute-start | bytes 393224 | tf_op jit(solution)/shard_map/ppermute | solution.py:311
  62.4 1.4 %collective-permute-start.19 = (bf16[128,512]{1,0:T(8,128)(2,1)S(1)}, bf16[128,512]{1,0:T(8,128)(2,1)S(1)}, u32[]{:S(2)}, u32[]{:S(2)}) collective-permute-start(bf16[128,512]{1,0:T(8,128)(2,1)S(1)} %collective-permute-done.18), channel_id=1, source_target_pairs={{0,2},{2,0},{4,6},{6,4},{8,10},{10,8},{12,14},{14,12},{16,18},{18,... | collective-permute-start | bytes 393224 | tf_op jit(solution)/shard_map/ppermute | solution.py:242
  62.5 5.1 %collective-permute-start.36 = (bf16[128,512]{1,0:T(8,128)(2,1)S(1)}, bf16[128,512]{1,0:T(8,128)(2,1)S(1)}, u32[]{:S(2)}, u32[]{:S(2)}) collective-permute-start(bf16[128,512]{1,0:T(8,128)(2,1)S(1)} %collective-permute-done.32), channel_id=1, source_target_pairs={{0,8},{2,6},{8,16},{10,2},{16,24},{18,10},{24,28},{26,18},{28,20},... | collective-permute-start | bytes 393224 | tf_op jit(solution)/shard_map/ppermute | solution.py:311
  63.7 4.4 %collective-permute-start.33 = (bf16[128,512]{1,0:T(8,128)(2,1)S(1)}, bf16[128,512]{1,0:T(8,128)(2,1)S(1)}, u32[]{:S(2)}, u32[]{:S(2)}) collective-permute-start(bf16[128,512]{1,0:T(8,128)(2,1)S(1)} %collective-permute-done.32), channel_id=1, source_target_pairs={{0,2},{2,0},{4,6},{6,4},{8,10},{10,8},{12,14},{14,12},{16,18},{18,... | collective-permute-start | bytes 393224 | tf_op jit(solution)/shard_map/ppermute | solution.py:242
  63.8 2.5 %collective-permute-start.31 = (bf16[128,512]{1,0:T(8,128)(2,1)S(1)}, bf16[128,512]{1,0:T(8,128)(2,1)S(1)}, u32[]{:S(2)}, u32[]{:S(2)}) collective-permute-start(bf16[128,512]{1,0:T(8,128)(2,1)S(1)} %collective-permute-done.30), channel_id=1, source_target_pairs={{0,2},{2,0},{4,6},{6,4},{8,10},{10,8},{12,14},{14,12},{16,18},{18,... | collective-permute-start | bytes 393224 | tf_op jit(solution)/shard_map/ppermute | solution.py:242
  64.9 5.0 %collective-permute-start.34 = (bf16[128,512]{1,0:T(8,128)(2,1)S(1)}, bf16[128,512]{1,0:T(8,128)(2,1)S(1)}, u32[]{:S(2)}, u32[]{:S(2)}) collective-permute-start(bf16[128,512]{1,0:T(8,128)(2,1)S(1)} %collective-permute-done.30), channel_id=1, source_target_pairs={{0,8},{2,6},{8,16},{10,2},{16,24},{18,10},{24,28},{26,18},{28,20},... | collective-permute-start | bytes 393224 | tf_op jit(solution)/shard_map/ppermute | solution.py:311
  66.3 5.0 %collective-permute-start.24 = (bf16[128,512]{1,0:T(8,128)(2,1)S(1)}, bf16[128,512]{1,0:T(8,128)(2,1)S(1)}, u32[]{:S(2)}, u32[]{:S(2)}) collective-permute-start(bf16[128,512]{1,0:T(8,128)(2,1)S(1)} %collective-permute-done.20), channel_id=1, source_target_pairs={{0,8},{2,6},{8,16},{10,2},{16,24},{18,10},{24,28},{26,18},{28,20},... | collective-permute-start | bytes 393224 | tf_op jit(solution)/shard_map/ppermute | solution.py:311
  67.5 2.3 %collective-permute-start.21 = (bf16[128,512]{1,0:T(8,128)(2,1)S(1)}, bf16[128,512]{1,0:T(8,128)(2,1)S(1)}, u32[]{:S(2)}, u32[]{:S(2)}) collective-permute-start(bf16[128,512]{1,0:T(8,128)(2,1)S(1)} %collective-permute-done.20), channel_id=1, source_target_pairs={{0,2},{2,0},{4,6},{6,4},{8,10},{10,8},{12,14},{14,12},{16,18},{18,... | collective-permute-start | bytes 393224 | tf_op jit(solution)/shard_map/ppermute | solution.py:242
  67.7 3.7 %collective-permute-start.23 = (bf16[128,512]{1,0:T(8,128)(2,1)S(1)}, bf16[128,512]{1,0:T(8,128)(2,1)S(1)}, u32[]{:S(2)}, u32[]{:S(2)}) collective-permute-start(bf16[128,512]{1,0:T(8,128)(2,1)S(1)} %collective-permute-done.22), channel_id=1, source_target_pairs={{0,2},{2,0},{4,6},{6,4},{8,10},{10,8},{12,14},{14,12},{16,18},{18,... | collective-permute-start | bytes 393224 | tf_op jit(solution)/shard_map/ppermute | solution.py:242
  68.1 5.0 %collective-permute-start.40 = (bf16[128,512]{1,0:T(8,128)(2,1)S(1)}, bf16[128,512]{1,0:T(8,128)(2,1)S(1)}, u32[]{:S(2)}, u32[]{:S(2)}) collective-permute-start(bf16[128,512]{1,0:T(8,128)(2,1)S(1)} %collective-permute-done.36), channel_id=1, source_target_pairs={{0,8},{2,6},{8,16},{10,2},{16,24},{18,10},{24,28},{26,18},{28,20},... | collective-permute-start | bytes 393224 | tf_op jit(solution)/shard_map/ppermute | solution.py:311
  69.8 5.0 %collective-permute-start.37 = (bf16[128,512]{1,0:T(8,128)(2,1)S(1)}, bf16[128,512]{1,0:T(8,128)(2,1)S(1)}, u32[]{:S(2)}, u32[]{:S(2)}) collective-permute-start(bf16[128,512]{1,0:T(8,128)(2,1)S(1)} %collective-permute-done.36), channel_id=1, source_target_pairs={{0,2},{2,0},{4,6},{6,4},{8,10},{10,8},{12,14},{14,12},{16,18},{18,... | collective-permute-start | bytes 393224 | tf_op jit(solution)/shard_map/ppermute | solution.py:242
  69.8 5.0 %collective-permute-start.38 = (bf16[128,512]{1,0:T(8,128)(2,1)S(1)}, bf16[128,512]{1,0:T(8,128)(2,1)S(1)}, u32[]{:S(2)}, u32[]{:S(2)}) collective-permute-start(bf16[128,512]{1,0:T(8,128)(2,1)S(1)} %collective-permute-done.34), channel_id=1, source_target_pairs={{0,8},{2,6},{8,16},{10,2},{16,24},{18,10},{24,28},{26,18},{28,20},... | collective-permute-start | bytes 393224 | tf_op jit(solution)/shard_map/ppermute | solution.py:311
  71.3 3.5 %collective-permute-start.35 = (bf16[128,512]{1,0:T(8,128)(2,1)S(1)}, bf16[128,512]{1,0:T(8,128)(2,1)S(1)}, u32[]{:S(2)}, u32[]{:S(2)}) collective-permute-start(bf16[128,512]{1,0:T(8,128)(2,1)S(1)} %collective-permute-done.34), channel_id=1, source_target_pairs={{0,2},{2,0},{4,6},{6,4},{8,10},{10,8},{12,14},{14,12},{16,18},{18,... | collective-permute-start | bytes 393224 | tf_op jit(solution)/shard_map/ppermute | solution.py:242
  71.4 4.8 %collective-permute-start.25 = (bf16[128,512]{1,0:T(8,128)(2,1)S(1)}, bf16[128,512]{1,0:T(8,128)(2,1)S(1)}, u32[]{:S(2)}, u32[]{:S(2)}) collective-permute-start(bf16[128,512]{1,0:T(8,128)(2,1)S(1)} %collective-permute-done.24), channel_id=1, source_target_pairs={{0,2},{2,0},{4,6},{6,4},{8,10},{10,8},{12,14},{14,12},{16,18},{18,... | collective-permute-start | bytes 393224 | tf_op jit(solution)/shard_map/ppermute | solution.py:242
  73.1 3.2 %collective-permute-start.41 = (bf16[128,512]{1,0:T(8,128)(2,1)S(1)}, bf16[128,512]{1,0:T(8,128)(2,1)S(1)}, u32[]{:S(2)}, u32[]{:S(2)}) collective-permute-start(bf16[128,512]{1,0:T(8,128)(2,1)S(1)} %collective-permute-done.40), channel_id=1, source_target_pairs={{0,2},{2,0},{4,6},{6,4},{8,10},{10,8},{12,14},{14,12},{16,18},{18,... | collective-permute-start | bytes 393224 | tf_op jit(solution)/shard_map/ppermute | solution.py:242
  74.8 1.3 %collective-permute-start.39 = (bf16[128,512]{1,0:T(8,128)(2,1)S(1)}, bf16[128,512]{1,0:T(8,128)(2,1)S(1)}, u32[]{:S(2)}, u32[]{:S(2)}) collective-permute-start(bf16[128,512]{1,0:T(8,128)(2,1)S(1)} %collective-permute-done.38), channel_id=1, source_target_pairs={{0,2},{2,0},{4,6},{6,4},{8,10},{10,8},{12,14},{14,12},{16,18},{18,... | collective-permute-start | bytes 393224 | tf_op jit(solution)/shard_map/ppermute | solution.py:242

commit v16 on v15

--- a/solution.py
+++ b/solution.py
@@ -175,6 +175,7 @@
 
 OFFSETS = ((4, 7, 2), (5, 6, 3))
 SHARED = 1
+PAIR_OFFSETS = (0, 2, 1, 3)
 
 
 def pack_kernel(place_ref, inputs_ref, *piece_refs):
@@ -205,7 +206,7 @@
     for hop in range(hops):
         for piece_ref, member in ((near_refs[hop], plane), (far_refs[hop], 1 - plane)):
             put(band_ref, piece_ref, band ^ jnp.where(member == 0, OFFSETS[0][hop], OFFSETS[1][hop]))
-    for offset, pair_ref in enumerate(cot_refs):
+    for offset, pair_ref in zip(PAIR_OFFSETS, cot_refs):
         for part, source in enumerate((band ^ offset, band ^ offset ^ 4)):
             put(cot_ref, pair_ref.at[pl.ds(part * tokens, tokens)], source)
     partial_ref[...] = contract(band_ref[...], cot_ref[...], 0, 0)
@@ -277,7 +278,7 @@
     near = [deal(packed[hop], hop) for hop in hops]
     shared = exchange(packed[-1], SHARED)
     pair = jnp.concatenate([cotangent, far_cot])
-    cots = [pair] + [exchange(pair, offset) for offset in (1, 2, 3)]
+    cots = [pair] + [exchange(pair, offset) for offset in PAIR_OFFSETS[1:]]
     far = [swap_plane(piece) for piece in near]
     (partial_tile,) = call(
         tile_kernel,

time: 79.1 us -> 79 us (level)
  waiting for transfers between devices: 17.3 us -> 14.5 us
  starting transfers between devices: 42.5 us -> 45.1 us
    ppermute x5, starting transfers between devices: 9.35 us -> 12 us  [exchange(): return lax.ppermute(array, 'dp', pairs)]
    ppermute x14, waiting for transfers between devices: 4.28 us -> 2.96 us  [turn(): return lax.ppermute(array, 'dp', pairs)]
    ppermute x4, starting transfers between devices: 6.98 us -> 5.72 us  [swap_plane(): lax.ppermute(array, 'pre', [(c, members - 1 - c) for c in range(members)])]
    ppermute x14, starting transfers between devices: 20.4 us -> 21.6 us  [turn(): return lax.ppermute(array, 'dp', pairs)]
    ppermute x5, waiting for transfers between devices: 1.36 us -> 0.49 us  [exchange(): return lax.ppermute(array, 'dp', pairs)]
  transfers between devices with their start and end apart: 42 -> 42, of which waited for: 14 -> 12; matrix products, arithmetic and copies ran while one was open for 6% -> 6% of each run, Pallas kernels for 1% -> 1%
where the time goes in v16:
time: 79 us; the launch traced here: 78.8 us
  starting transfers between devices  45.1 us (57%)
  waiting for transfers between devices  14.5 us (18%)
  Pallas kernels  9.13 us (12%)
  matrix products  3.6 us (5%)
  other arithmetic  2.81 us (4%)
  local copies, waits for them, and re-layouts  2.23 us (3%)
  between operations  1.4 us (2%)
    ppermute x14, starting transfers between devices, turn(): return lax.ppermute(array, 'dp', pairs)  21.6 us
    ppermute x5, starting transfers between devices, exchange(): return lax.ppermute(array, 'dp', pairs)  12 us
    pallas_call x3, Pallas kernels, call(): pl.pallas_call(kernel, out_shape=out_shapes, in_specs=in_specs, out_specs...  9.13 us
    ppermute x4, starting transfers between devices, swap_plane(): lax.ppermute(array, 'pre', [(c, members - 1 - c) for c in range(members)])  5.72 us
    ppermute x4, waiting for transfers between devices, swap_plane(): lax.ppermute(array, 'pre', [(c, members - 1 - c) for c in range(members)])  5.67 us
    ppermute x3, starting transfers between devices, deal(): return lax.ppermute(array, ('dp', 'pre'), pairs)  3.88 us
    ppermute x16, waiting for transfers between devices, swap_core(): return lax.ppermute(array, 'dp', [(g, g ^ 1) for g in range(groups)])  3.61 us
    dot_general x1, matrix products, on_device_paired(): jnp.dot(inputs, weight, preferred_element_type=jnp.float32)  3.6 us
  transfers between devices with their start and end apart: 42, of which 12 were waited for; matrix products, arithmetic and copies ran while one was open for 6% of the time, Pallas kernels for 1%

profile of v16, /device:TPU:0, one launch (start us, length us, event | category | flops | bytes accessed | tf_op | source)
XLA Modules:
  0.0 78.8 jit_solution(1497614762220021090)
XLA Ops:
  0.6 4.1 %collective-permute-start = (bf16[128,512]{1,0:T(8,128)(2,1)}, bf16[128,512]{1,0:T(8,128)(2,1)S(1)}, u32[]{:S(2)}, u32[]{:S(2)}) collective-permute-start(bf16[128,512]{1,0:T(8,128)(2,1)} %param.5), channel_id=1, source_target_pairs={{0,16},{2,18},{4,20},{6,22},{8,24},{10,26},{12,28},{14,30},{16,0},... | collective-permute-start | bytes 393224 | tf_op jit(solution)/shard_map/ppermute | solution.py:274
  4.7 0.1 stack.41.place_ref
  4.8 1.2 %copy-done = bf16[128,4096]{1,0:T(8,128)(2,1)S(1)} copy-done((bf16[128,4096]{1,0:T(8,128)(2,1)S(1)}, bf16[128,4096]{1,0:T(8,128)(2,1)}, u32[]{:S(2)}) %copy-start) | copy-done | bytes 1048600
  6.0 0.6 shard_map.50
  6.6 1.6 %collective-permute-start.1 = (bf16[128,512]{1,0:T(8,128)(2,1)S(1)}, bf16[128,512]{1,0:T(8,128)(2,1)S(1)}, u32[]{:S(2)}, u32[]{:S(2)}) collective-permute-start(bf16[128,512]{1,0:T(8,128)(2,1)S(1)} %get-tuple-element.14), channel_id=1, source_target_pairs={{0,4},{2,6},{4,0},{6,2},{8,12},{10,14},{12,8},{14,10},{16,20},{18,... | collective-permute-start | bytes 393224 | tf_op jit(solution)/shard_map/ppermute | solution.py:274
  8.2 0.3 collective-permute-start.2
  8.6 3.5 %collective-permute-start.3 = (bf16[128,512]{1,0:T(8,128)(2,1)S(1)}, bf16[128,512]{1,0:T(8,128)(2,1)S(1)}, u32[]{:S(2)}, u32[]{:S(2)}) collective-permute-start(bf16[128,512]{1,0:T(8,128)(2,1)S(1)} %get-tuple-element.16), channel_id=1, source_target_pairs={{0,28},{1,25},{2,30},{3,27},{4,24},{5,29},{6,26},{7,31},{8,20},{9,... | collective-permute-start | bytes 393224 | tf_op jit(solution)/shard_map/ppermute | solution.py:258
  12.1 3.6 %convolution_convert_fusion = bf16[128,512]{1,0:T(8,128)(2,1)} fusion(bf16[128,4096]{1,0:T(8,128)(2,1)S(1)} %copy-done, bf16[4096,512]{1,0:T(8,128)(2,1)} %param.4), kind=kOutput, calls=%fused_computation.1 | convolution fusion | flops 536936448 | bytes 5373952 | tf_op jit(solution)/shard_map/dot_general | solution.py:276
  15.8 3.0 %collective-permute-start.10 = (bf16[256,512]{1,0:T(8,128)(2,1)S(1)}, bf16[256,512]{1,0:T(8,128)(2,1)S(1)}, u32[]{:S(2)}, u32[]{:S(2)}) collective-permute-start(bf16[256,512]{1,0:T(8,128)(2,1)S(1)} %constant_dynamic-update-slice_fusion.refs_6_), channel_id=1, source_target_pairs={{0,12},{2,14},{4,8},{6,10},{8,4},{10,6},{12,0},{14,2},{16,28},{18,... | collective-permute-start | bytes 786440 | tf_op jit(solution)/shard_map/ppermute | solution.py:274
  18.8 1.8 %collective-permute-done.2.refs_0_ = bf16[128,512]{1,0:T(8,128)(2,1)S(1)} collective-permute-done((bf16[128,512]{1,0:T(8,128)(2,1)S(1)}, bf16[128,512]{1,0:T(8,128)(2,1)S(1)}, u32[]{:S(2)}, u32[]{:S(2)}) %collective-permute-start.2) | collective-permute-done | bytes 131104 | tf_op jit(solution)/shard_map/ppermute | solution.py:258
  20.6 2.4 %collective-permute-start.5 = (bf16[128,512]{1,0:T(8,128)(2,1)S(1)}, bf16[128,512]{1,0:T(8,128)(2,1)S(1)}, u32[]{:S(2)}, u32[]{:S(2)}) collective-permute-start(bf16[128,512]{1,0:T(8,128)(2,1)S(1)} %collective-permute-done.2.refs_0_), channel_id=1, source_target_pairs={{0,1},{1,0},{2,3},{3,2},{4,5},{5,4},{6,7},{7,6},{8,9},{9,8},{10,11... | collective-permute-start | bytes 393224 | tf_op jit(solution)/shard_map/ppermute | solution.py:246
  23.0 0.5 collective-permute-start.9
  23.5 2.7 %collective-permute-start.8 = (bf16[256,512]{1,0:T(8,128)(2,1)S(1)}, bf16[256,512]{1,0:T(8,128)(2,1)S(1)}, u32[]{:S(2)}, u32[]{:S(2)}) collective-permute-start(bf16[256,512]{1,0:T(8,128)(2,1)S(1)} %constant_dynamic-update-slice_fusion.refs_6_), channel_id=1, source_target_pairs={{0,8},{2,10},{4,12},{6,14},{8,0},{10,2},{12,4},{14,6},{16,24},{18,... | collective-permute-start | bytes 786440 | tf_op jit(solution)/shard_map/ppermute | solution.py:274
  26.3 2.0 %collective-permute-start.7 = (bf16[128,512]{1,0:T(8,128)(2,1)S(1)}, bf16[128,512]{1,0:T(8,128)(2,1)S(1)}, u32[]{:S(2)}, u32[]{:S(2)}) collective-permute-start(bf16[128,512]{1,0:T(8,128)(2,1)S(1)} %collective-permute-done.4.refs_2_), channel_id=1, source_target_pairs={{0,1},{1,0},{2,3},{3,2},{4,5},{5,4},{6,7},{7,6},{8,9},{9,8},{10,11... | collective-permute-start | bytes 393224 | tf_op jit(solution)/shard_map/ppermute | solution.py:246
  28.3 0.1 pad_add_fusion.1.place_ref
  28.4 3.2 %collective-permute-done.6.refs_4_ = bf16[128,512]{1,0:T(8,128)(2,1)S(1)} collective-permute-done((bf16[128,512]{1,0:T(8,128)(2,1)S(1)}, bf16[128,512]{1,0:T(8,128)(2,1)S(1)}, u32[]{:S(2)}, u32[]{:S(2)}) %collective-permute-start.6) | collective-permute-done | bytes 131104 | tf_op jit(solution)/shard_map/ppermute | solution.py:246
  31.6 1.4 %collective-permute-done.7.refs_5_ = bf16[128,512]{1,0:T(8,128)(2,1)S(1)} collective-permute-done((bf16[128,512]{1,0:T(8,128)(2,1)S(1)}, bf16[128,512]{1,0:T(8,128)(2,1)S(1)}, u32[]{:S(2)}, u32[]{:S(2)}) %collective-permute-start.7) | collective-permute-done | bytes 131104 | tf_op jit(solution)/shard_map/ppermute | solution.py:246
  33.0 0.5 collective-permute-done.9.refs_8_
  33.5 1.4 %shard_map.51.mine_ref = f32[512,512]{1,0:T(8,128)S(1)} custom-call(s32[2]{0:T(128)S(1)} %pad_add_fusion.1.place_ref, bf16[128,512]{1,0:T(8,128)(2,1)S(1)} %get-tuple-element.13.own_ref, bf16[128,512]{1,0:T(8,128)(2,1)S(1)} %collective-permute-done.1.shared_ref, bf16[128,512]{1,0:T(8,128)(2,1)S(1)} %collective-permute-done.2.refs_0_, ...), custom_call_target="tpu_custom_call" | custom-call | tf_op jit(solution)/shard_map/pallas_call | solution.py:218
  35.3 0.1 pad_add_fusion.side_ref
  35.3 2.3 %collective-permute-done.11.other_ref = f32[512,512]{1,0:T(8,128)S(1)} collective-permute-done((f32[512,512]{1,0:T(8,128)S(1)}, f32[512,512]{1,0:T(8,128)S(1)}, u32[]{:S(2)}, u32[]{:S(2)}) %collective-permute-start.11) | collective-permute-done | bytes 1048608 | tf_op jit(solution)/shard_map/ppermute | solution.py:243
  37.6 7.1 %shard_map.52 = (bf16[128,512]{1,0:T(8,128)(2,1)S(1)}, bf16[128,512]{1,0:T(8,128)(2,1)S(1)}, bf16[128,512]{1,0:T(8,128)(2,1)S(1)}) custom-call(s32[2]{0:T(128)S(1)} %pad_add_fusion.side_ref, f32[512,512]{1,0:T(8,128)S(1)} %shard_map.51.mine_ref, f32[512,512]{1,0:T(8,128)S(1)} %collective-permute-done.11.other_ref), custom_call_target="tpu_custom_call" | custom-call | tf_op jit(solution)/shard_map/pallas_call | solution.py:218
  44.8 1.3 %collective-permute-start.26 = (bf16[128,512]{1,0:T(8,128)(2,1)S(1)}, bf16[128,512]{1,0:T(8,128)(2,1)S(1)}, u32[]{:S(2)}, u32[]{:S(2)}) collective-permute-start(bf16[128,512]{1,0:T(8,128)(2,1)S(1)} %get-tuple-element.21), channel_id=1, source_target_pairs={{0,1},{1,0},{2,3},{3,2},{4,5},{5,4},{6,7},{7,6},{8,9},{9,8},{10,11... | collective-permute-start | bytes 393224 | tf_op jit(solution)/shard_map/ppermute | solution.py:246
  46.1 0.1 collective-permute-start.12
  46.1 2.9 %collective-permute-start.14 = (bf16[128,512]{1,0:T(8,128)(2,1)S(1)}, bf16[128,512]{1,0:T(8,128)(2,1)S(1)}, u32[]{:S(2)}, u32[]{:S(2)}) collective-permute-start(bf16[128,512]{1,0:T(8,128)(2,1)S(1)} %get-tuple-element.20), channel_id=1, source_target_pairs={{0,8},{2,6},{8,16},{10,2},{16,24},{18,10},{24,28},{26,18},{28,20},... | collective-permute-start | bytes 393224 | tf_op jit(solution)/shard_map/ppermute | solution.py:312
  49.1 0.2 broadcast_in_dim.99.clone.1
  49.3 1.0 %collective-permute-done.26 = bf16[128,512]{1,0:T(8,128)(2,1)S(1)} collective-permute-done((bf16[128,512]{1,0:T(8,128)(2,1)S(1)}, bf16[128,512]{1,0:T(8,128)(2,1)S(1)}, u32[]{:S(2)}, u32[]{:S(2)}) %collective-permute-start.26) | collective-permute-done | bytes 131104 | tf_op jit(solution)/shard_map/ppermute | solution.py:246
  50.4 1.2 %collective-permute-start.28 = (bf16[128,512]{1,0:T(8,128)(2,1)S(1)}, bf16[128,512]{1,0:T(8,128)(2,1)S(1)}, u32[]{:S(2)}, u32[]{:S(2)}) collective-permute-start(bf16[128,512]{1,0:T(8,128)(2,1)S(1)} %collective-permute-done.26), channel_id=1, source_target_pairs={{0,8},{2,6},{8,16},{10,2},{16,24},{18,10},{24,28},{26,18},{28,20},... | collective-permute-start | bytes 393224 | tf_op jit(solution)/shard_map/ppermute | solution.py:312
  51.6 2.8 %collective-permute-start.16 = (bf16[128,512]{1,0:T(8,128)(2,1)S(1)}, bf16[128,512]{1,0:T(8,128)(2,1)S(1)}, u32[]{:S(2)}, u32[]{:S(2)}) collective-permute-start(bf16[128,512]{1,0:T(8,128)(2,1)S(1)} %collective-permute-done.12), channel_id=1, source_target_pairs={{0,8},{2,6},{8,16},{10,2},{16,24},{18,10},{24,28},{26,18},{28,20},... | collective-permute-start | bytes 393224 | tf_op jit(solution)/shard_map/ppermute | solution.py:312
  54.4 1.7 %collective-permute-start.18 = (bf16[128,512]{1,0:T(8,128)(2,1)S(1)}, bf16[128,512]{1,0:T(8,128)(2,1)S(1)}, u32[]{:S(2)}, u32[]{:S(2)}) collective-permute-start(bf16[128,512]{1,0:T(8,128)(2,1)S(1)} %collective-permute-done.14), channel_id=1, source_target_pairs={{0,8},{2,6},{8,16},{10,2},{16,24},{18,10},{24,28},{26,18},{28,20},... | collective-permute-start | bytes 393224 | tf_op jit(solution)/shard_map/ppermute | solution.py:312
  56.1 0.2 broadcast_in_dim.99.clone
  56.4 0.6 collective-permute-start.32
  57.2 2.4 %collective-permute-start.30 = (bf16[128,512]{1,0:T(8,128)(2,1)S(1)}, bf16[128,512]{1,0:T(8,128)(2,1)S(1)}, u32[]{:S(2)}, u32[]{:S(2)}) collective-permute-start(bf16[128,512]{1,0:T(8,128)(2,1)S(1)} %collective-permute-done.27), channel_id=1, source_target_pairs={{0,8},{2,6},{8,16},{10,2},{16,24},{18,10},{24,28},{26,18},{28,20},... | collective-permute-start | bytes 393224 | tf_op jit(solution)/shard_map/ppermute | solution.py:312
  59.6 1.7 %collective-permute-start.20 = (bf16[128,512]{1,0:T(8,128)(2,1)S(1)}, bf16[128,512]{1,0:T(8,128)(2,1)S(1)}, u32[]{:S(2)}, u32[]{:S(2)}) collective-permute-start(bf16[128,512]{1,0:T(8,128)(2,1)S(1)} %collective-permute-done.16), channel_id=1, source_target_pairs={{0,8},{2,6},{8,16},{10,2},{16,24},{18,10},{24,28},{26,18},{28,20},... | collective-permute-start | bytes 393224 | tf_op jit(solution)/shard_map/ppermute | solution.py:312
  61.4 1.2 %collective-permute-start.22 = (bf16[128,512]{1,0:T(8,128)(2,1)S(1)}, bf16[128,512]{1,0:T(8,128)(2,1)S(1)}, u32[]{:S(2)}, u32[]{:S(2)}) collective-permute-start(bf16[128,512]{1,0:T(8,128)(2,1)S(1)} %collective-permute-done.18), channel_id=1, source_target_pairs={{0,8},{2,6},{8,16},{10,2},{16,24},{18,10},{24,28},{26,18},{28,20},... | collective-permute-start | bytes 393224 | tf_op jit(solution)/shard_map/ppermute | solution.py:312
  62.8 1.1 %collective-permute-start.36 = (bf16[128,512]{1,0:T(8,128)(2,1)S(1)}, bf16[128,512]{1,0:T(8,128)(2,1)S(1)}, u32[]{:S(2)}, u32[]{:S(2)}) collective-permute-start(bf16[128,512]{1,0:T(8,128)(2,1)S(1)} %collective-permute-done.32), channel_id=1, source_target_pairs={{0,8},{2,6},{8,16},{10,2},{16,24},{18,10},{24,28},{26,18},{28,20},... | collective-permute-start | bytes 393224 | tf_op jit(solution)/shard_map/ppermute | solution.py:312
  64.1 0.4 collective-permute-start.31
  64.6 1.6 %collective-permute-start.34 = (bf16[128,512]{1,0:T(8,128)(2,1)S(1)}, bf16[128,512]{1,0:T(8,128)(2,1)S(1)}, u32[]{:S(2)}, u32[]{:S(2)}) collective-permute-start(bf16[128,512]{1,0:T(8,128)(2,1)S(1)} %collective-permute-done.30), channel_id=1, source_target_pairs={{0,8},{2,6},{8,16},{10,2},{16,24},{18,10},{24,28},{26,18},{28,20},... | collective-permute-start | bytes 393224 | tf_op jit(solution)/shard_map/ppermute | solution.py:312
  66.3 1.4 %collective-permute-start.24 = (bf16[128,512]{1,0:T(8,128)(2,1)S(1)}, bf16[128,512]{1,0:T(8,128)(2,1)S(1)}, u32[]{:S(2)}, u32[]{:S(2)}) collective-permute-start(bf16[128,512]{1,0:T(8,128)(2,1)S(1)} %collective-permute-done.20), channel_id=1, source_target_pairs={{0,8},{2,6},{8,16},{10,2},{16,24},{18,10},{24,28},{26,18},{28,20},... | collective-permute-start | bytes 393224 | tf_op jit(solution)/shard_map/ppermute | solution.py:312
  67.9 0.4 collective-permute-start.23
  68.3 1.2 %collective-permute-start.40 = (bf16[128,512]{1,0:T(8,128)(2,1)S(1)}, bf16[128,512]{1,0:T(8,128)(2,1)S(1)}, u32[]{:S(2)}, u32[]{:S(2)}) collective-permute-start(bf16[128,512]{1,0:T(8,128)(2,1)S(1)} %collective-permute-done.36), channel_id=1, source_target_pairs={{0,8},{2,6},{8,16},{10,2},{16,24},{18,10},{24,28},{26,18},{28,20},... | collective-permute-start | bytes 393224 | tf_op jit(solution)/shard_map/ppermute | solution.py:312
  69.5 0.1 collective-permute-done.34
  69.6 1.6 %collective-permute-start.38 = (bf16[128,512]{1,0:T(8,128)(2,1)S(1)}, bf16[128,512]{1,0:T(8,128)(2,1)S(1)}, u32[]{:S(2)}, u32[]{:S(2)}) collective-permute-start(bf16[128,512]{1,0:T(8,128)(2,1)S(1)} %collective-permute-done.34), channel_id=1, source_target_pairs={{0,8},{2,6},{8,16},{10,2},{16,24},{18,10},{24,28},{26,18},{28,20},... | collective-permute-start | bytes 393224 | tf_op jit(solution)/shard_map/ppermute | solution.py:312
  71.4 0.5 collective-permute-start.25
  71.9 1.4 %collective-permute-done.40 = bf16[128,512]{1,0:T(8,128)(2,1)S(1)} collective-permute-done((bf16[128,512]{1,0:T(8,128)(2,1)S(1)}, bf16[128,512]{1,0:T(8,128)(2,1)S(1)}, u32[]{:S(2)}, u32[]{:S(2)}) %collective-permute-start.40) | collective-permute-done | bytes 131104 | tf_op jit(solution)/shard_map/ppermute | solution.py:312
  73.3 1.4 %collective-permute-done.38 = bf16[128,512]{1,0:T(8,128)(2,1)S(1)} collective-permute-done((bf16[128,512]{1,0:T(8,128)(2,1)S(1)}, bf16[128,512]{1,0:T(8,128)(2,1)S(1)}, u32[]{:S(2)}, u32[]{:S(2)}) %collective-permute-start.38) | collective-permute-done | bytes 131104 | tf_op jit(solution)/shard_map/ppermute | solution.py:312
  74.8 1.2 %collective-permute-done.39 = bf16[128,512]{1,0:T(8,128)(2,1)S(1)} collective-permute-done((bf16[128,512]{1,0:T(8,128)(2,1)S(1)}, bf16[128,512]{1,0:T(8,128)(2,1)S(1)}, u32[]{:S(2)}, u32[]{:S(2)}) %collective-permute-start.39) | collective-permute-done | bytes 131104 | tf_op jit(solution)/shard_map/ppermute | solution.py:243
  76.2 2.7 %maximum_select_fusion = bf16[8,256,1024]{2,1,0:T(8,128)(2,1)} fusion(bf16[8,256,512]{2,1,0:T(8,128)(2,1)S(1)} %bitcast.75, bf16[8,256,512]{2,1,0:T(8,128)(2,1)S(1)} %bitcast.76, pred[]{:T(512)S(6)} %eq.44), kind=kLoop, calls=%fused_computation | loop fusion | flops 18874368 | bytes 8388609 | tf_op jit(solution)/shard_map/jit(_where)/select_n | solution.py:334
  (83 shorter events, 1.3 us)
Async XLA Ops:
  0.6 15.1 %collective-permute-start = (bf16[128,512]{1,0:T(8,128)(2,1)}, bf16[128,512]{1,0:T(8,128)(2,1)S(1)}, u32[]{:S(2)}, u32[]{:S(2)}) collective-permute-start(bf16[128,512]{1,0:T(8,128)(2,1)} %param.5), channel_id=1, source_target_pairs={{0,16},{2,18},{4,20},{6,22},{8,24},{10,26},{12,28},{14,30},{16,0},... | collective-permute-start | bytes 393224 | tf_op jit(solution)/shard_map/ppermute | solution.py:274
  4.8 1.2 %copy-start = (bf16[128,4096]{1,0:T(8,128)(2,1)S(1)}, bf16[128,4096]{1,0:T(8,128)(2,1)}, u32[]{:S(2)}) copy-start(bf16[128,4096]{1,0:T(8,128)(2,1)} %inputs_ref.1) | copy-start | bytes 3145732
  6.6 16.4 %collective-permute-start.1 = (bf16[128,512]{1,0:T(8,128)(2,1)S(1)}, bf16[128,512]{1,0:T(8,128)(2,1)S(1)}, u32[]{:S(2)}, u32[]{:S(2)}) collective-permute-start(bf16[128,512]{1,0:T(8,128)(2,1)S(1)} %get-tuple-element.14), channel_id=1, source_target_pairs={{0,4},{2,6},{4,0},{6,2},{8,12},{10,14},{12,8},{14,10},{16,20},{18,... | collective-permute-start | bytes 393224 | tf_op jit(solution)/shard_map/ppermute | solution.py:274
  8.2 12.4 %collective-permute-start.2 = (bf16[128,512]{1,0:T(8,128)(2,1)S(1)}, bf16[128,512]{1,0:T(8,128)(2,1)S(1)}, u32[]{:S(2)}, u32[]{:S(2)}) collective-permute-start(bf16[128,512]{1,0:T(8,128)(2,1)S(1)} %get-tuple-element.15), channel_id=1, source_target_pairs={{0,16},{1,21},{2,18},{3,23},{4,20},{5,17},{6,22},{7,19},{8,24},{9,... | collective-permute-start | bytes 393224 | tf_op jit(solution)/shard_map/ppermute | solution.py:258
  8.6 15.0 %collective-permute-start.3 = (bf16[128,512]{1,0:T(8,128)(2,1)S(1)}, bf16[128,512]{1,0:T(8,128)(2,1)S(1)}, u32[]{:S(2)}, u32[]{:S(2)}) collective-permute-start(bf16[128,512]{1,0:T(8,128)(2,1)S(1)} %get-tuple-element.16), channel_id=1, source_target_pairs={{0,28},{1,25},{2,30},{3,27},{4,24},{5,29},{6,26},{7,31},{8,20},{9,... | collective-permute-start | bytes 393224 | tf_op jit(solution)/shard_map/ppermute | solution.py:258
  12.1 3.6 %copy-start.1 = (bf16[128,512]{1,0:T(8,128)(2,1)S(1)}, bf16[128,512]{1,0:T(8,128)(2,1)}, u32[]{:S(2)}) copy-start(bf16[128,512]{1,0:T(8,128)(2,1)} %param.5) | copy-start | bytes 393220
  12.1 14.2 %collective-permute-start.4 = (bf16[128,512]{1,0:T(8,128)(2,1)S(1)}, bf16[128,512]{1,0:T(8,128)(2,1)S(1)}, u32[]{:S(2)}, u32[]{:S(2)}) collective-permute-start(bf16[128,512]{1,0:T(8,128)(2,1)S(1)} %get-tuple-element.17), channel_id=1, source_target_pairs={{0,8},{1,13},{2,10},{3,15},{4,12},{5,9},{6,14},{7,11},{8,0},{9,5},... | collective-permute-start | bytes 393224 | tf_op jit(solution)/shard_map/ppermute | solution.py:258
  15.8 17.2 %collective-permute-start.10 = (bf16[256,512]{1,0:T(8,128)(2,1)S(1)}, bf16[256,512]{1,0:T(8,128)(2,1)S(1)}, u32[]{:S(2)}, u32[]{:S(2)}) collective-permute-start(bf16[256,512]{1,0:T(8,128)(2,1)S(1)} %constant_dynamic-update-slice_fusion.refs_6_), channel_id=1, source_target_pairs={{0,12},{2,14},{4,8},{6,10},{8,4},{10,6},{12,0},{14,2},{16,28},{18,... | collective-permute-start | bytes 786440 | tf_op jit(solution)/shard_map/ppermute | solution.py:274
  20.6 5.7 %collective-permute-start.5 = (bf16[128,512]{1,0:T(8,128)(2,1)S(1)}, bf16[128,512]{1,0:T(8,128)(2,1)S(1)}, u32[]{:S(2)}, u32[]{:S(2)}) collective-permute-start(bf16[128,512]{1,0:T(8,128)(2,1)S(1)} %collective-permute-done.2.refs_0_), channel_id=1, source_target_pairs={{0,1},{1,0},{2,3},{3,2},{4,5},{5,4},{6,7},{7,6},{8,9},{9,8},{10,11... | collective-permute-start | bytes 393224 | tf_op jit(solution)/shard_map/ppermute | solution.py:246
  23.0 10.5 %collective-permute-start.9 = (bf16[256,512]{1,0:T(8,128)(2,1)S(1)}, bf16[256,512]{1,0:T(8,128)(2,1)S(1)}, u32[]{:S(2)}, u32[]{:S(2)}) collective-permute-start(bf16[256,512]{1,0:T(8,128)(2,1)S(1)} %constant_dynamic-update-slice_fusion.refs_6_), channel_id=1, source_target_pairs={{0,4},{2,6},{4,0},{6,2},{8,12},{10,14},{12,8},{14,10},{16,20},{18,... | collective-permute-start | bytes 786440 | tf_op jit(solution)/shard_map/ppermute | solution.py:274
  23.5 9.9 %collective-permute-start.8 = (bf16[256,512]{1,0:T(8,128)(2,1)S(1)}, bf16[256,512]{1,0:T(8,128)(2,1)S(1)}, u32[]{:S(2)}, u32[]{:S(2)}) collective-permute-start(bf16[256,512]{1,0:T(8,128)(2,1)S(1)} %constant_dynamic-update-slice_fusion.refs_6_), channel_id=1, source_target_pairs={{0,8},{2,10},{4,12},{6,14},{8,0},{10,2},{12,4},{14,6},{16,24},{18,... | collective-permute-start | bytes 786440 | tf_op jit(solution)/shard_map/ppermute | solution.py:274
  26.3 5.3 %collective-permute-start.6 = (bf16[128,512]{1,0:T(8,128)(2,1)S(1)}, bf16[128,512]{1,0:T(8,128)(2,1)S(1)}, u32[]{:S(2)}, u32[]{:S(2)}) collective-permute-start(bf16[128,512]{1,0:T(8,128)(2,1)S(1)} %collective-permute-done.3.refs_1_), channel_id=1, source_target_pairs={{0,1},{1,0},{2,3},{3,2},{4,5},{5,4},{6,7},{7,6},{8,9},{9,8},{10,11... | collective-permute-start | bytes 393224 | tf_op jit(solution)/shard_map/ppermute | solution.py:246
  26.3 6.7 %collective-permute-start.7 = (bf16[128,512]{1,0:T(8,128)(2,1)S(1)}, bf16[128,512]{1,0:T(8,128)(2,1)S(1)}, u32[]{:S(2)}, u32[]{:S(2)}) collective-permute-start(bf16[128,512]{1,0:T(8,128)(2,1)S(1)} %collective-permute-done.4.refs_2_), channel_id=1, source_target_pairs={{0,1},{1,0},{2,3},{3,2},{4,5},{5,4},{6,7},{7,6},{8,9},{9,8},{10,11... | collective-permute-start | bytes 393224 | tf_op jit(solution)/shard_map/ppermute | solution.py:246
  34.9 2.7 %collective-permute-start.11 = (f32[512,512]{1,0:T(8,128)S(1)}, f32[512,512]{1,0:T(8,128)S(1)}, u32[]{:S(2)}, u32[]{:S(2)}) collective-permute-start(f32[512,512]{1,0:T(8,128)S(1)} %shard_map.51.mine_ref), channel_id=1, source_target_pairs={{0,2},{2,0},{4,6},{6,4},{8,10},{10,8},{12,14},{14,12},{16,18},{18,... | collective-permute-start | bytes 3145736 | tf_op jit(solution)/shard_map/ppermute | solution.py:243
  44.8 5.6 %collective-permute-start.26 = (bf16[128,512]{1,0:T(8,128)(2,1)S(1)}, bf16[128,512]{1,0:T(8,128)(2,1)S(1)}, u32[]{:S(2)}, u32[]{:S(2)}) collective-permute-start(bf16[128,512]{1,0:T(8,128)(2,1)S(1)} %get-tuple-element.21), channel_id=1, source_target_pairs={{0,1},{1,0},{2,3},{3,2},{4,5},{5,4},{6,7},{7,6},{8,9},{9,8},{10,11... | collective-permute-start | bytes 393224 | tf_op jit(solution)/shard_map/ppermute | solution.py:246
  46.1 5.5 %collective-permute-start.12 = (bf16[128,512]{1,0:T(8,128)(2,1)S(1)}, bf16[128,512]{1,0:T(8,128)(2,1)S(1)}, u32[]{:S(2)}, u32[]{:S(2)}) collective-permute-start(bf16[128,512]{1,0:T(8,128)(2,1)S(1)} %get-tuple-element.19), channel_id=1, source_target_pairs={{0,8},{2,6},{8,16},{10,2},{16,24},{18,10},{24,28},{26,18},{28,20},... | collective-permute-start | bytes 393224 | tf_op jit(solution)/shard_map/ppermute | solution.py:312
  46.1 8.3 %collective-permute-start.14 = (bf16[128,512]{1,0:T(8,128)(2,1)S(1)}, bf16[128,512]{1,0:T(8,128)(2,1)S(1)}, u32[]{:S(2)}, u32[]{:S(2)}) collective-permute-start(bf16[128,512]{1,0:T(8,128)(2,1)S(1)} %get-tuple-element.20), channel_id=1, source_target_pairs={{0,8},{2,6},{8,16},{10,2},{16,24},{18,10},{24,28},{26,18},{28,20},... | collective-permute-start | bytes 393224 | tf_op jit(solution)/shard_map/ppermute | solution.py:312
  50.4 6.0 %collective-permute-start.28 = (bf16[128,512]{1,0:T(8,128)(2,1)S(1)}, bf16[128,512]{1,0:T(8,128)(2,1)S(1)}, u32[]{:S(2)}, u32[]{:S(2)}) collective-permute-start(bf16[128,512]{1,0:T(8,128)(2,1)S(1)} %collective-permute-done.26), channel_id=1, source_target_pairs={{0,8},{2,6},{8,16},{10,2},{16,24},{18,10},{24,28},{26,18},{28,20},... | collective-permute-start | bytes 393224 | tf_op jit(solution)/shard_map/ppermute | solution.py:312
  51.6 4.8 %collective-permute-start.27 = (bf16[128,512]{1,0:T(8,128)(2,1)S(1)}, bf16[128,512]{1,0:T(8,128)(2,1)S(1)}, u32[]{:S(2)}, u32[]{:S(2)}) collective-permute-start(bf16[128,512]{1,0:T(8,128)(2,1)S(1)} %collective-permute-done.26), channel_id=1, source_target_pairs={{0,2},{2,0},{4,6},{6,4},{8,10},{10,8},{12,14},{14,12},{16,18},{18,... | collective-permute-start | bytes 393224 | tf_op jit(solution)/shard_map/ppermute | solution.py:243
  51.6 5.6 %collective-permute-start.16 = (bf16[128,512]{1,0:T(8,128)(2,1)S(1)}, bf16[128,512]{1,0:T(8,128)(2,1)S(1)}, u32[]{:S(2)}, u32[]{:S(2)}) collective-permute-start(bf16[128,512]{1,0:T(8,128)(2,1)S(1)} %collective-permute-done.12), channel_id=1, source_target_pairs={{0,8},{2,6},{8,16},{10,2},{16,24},{18,10},{24,28},{26,18},{28,20},... | collective-permute-start | bytes 393224 | tf_op jit(solution)/shard_map/ppermute | solution.py:312
  54.4 2.7 %collective-permute-start.13 = (bf16[128,512]{1,0:T(8,128)(2,1)S(1)}, bf16[128,512]{1,0:T(8,128)(2,1)S(1)}, u32[]{:S(2)}, u32[]{:S(2)}) collective-permute-start(bf16[128,512]{1,0:T(8,128)(2,1)S(1)} %collective-permute-done.12), channel_id=1, source_target_pairs={{0,2},{2,0},{4,6},{6,4},{8,10},{10,8},{12,14},{14,12},{16,18},{18,... | collective-permute-start | bytes 393224 | tf_op jit(solution)/shard_map/ppermute | solution.py:243
  54.4 6.9 %collective-permute-start.18 = (bf16[128,512]{1,0:T(8,128)(2,1)S(1)}, bf16[128,512]{1,0:T(8,128)(2,1)S(1)}, u32[]{:S(2)}, u32[]{:S(2)}) collective-permute-start(bf16[128,512]{1,0:T(8,128)(2,1)S(1)} %collective-permute-done.14), channel_id=1, source_target_pairs={{0,8},{2,6},{8,16},{10,2},{16,24},{18,10},{24,28},{26,18},{28,20},... | collective-permute-start | bytes 393224 | tf_op jit(solution)/shard_map/ppermute | solution.py:312
  56.3 3.3 %collective-permute-start.15 = (bf16[128,512]{1,0:T(8,128)(2,1)S(1)}, bf16[128,512]{1,0:T(8,128)(2,1)S(1)}, u32[]{:S(2)}, u32[]{:S(2)}) collective-permute-start(bf16[128,512]{1,0:T(8,128)(2,1)S(1)} %collective-permute-done.14), channel_id=1, source_target_pairs={{0,2},{2,0},{4,6},{6,4},{8,10},{10,8},{12,14},{14,12},{16,18},{18,... | collective-permute-start | bytes 393224 | tf_op jit(solution)/shard_map/ppermute | solution.py:243
  56.4 6.3 %collective-permute-start.32 = (bf16[128,512]{1,0:T(8,128)(2,1)S(1)}, bf16[128,512]{1,0:T(8,128)(2,1)S(1)}, u32[]{:S(2)}, u32[]{:S(2)}) collective-permute-start(bf16[128,512]{1,0:T(8,128)(2,1)S(1)} %collective-permute-done.28), channel_id=1, source_target_pairs={{0,8},{2,6},{8,16},{10,2},{16,24},{18,10},{24,28},{26,18},{28,20},... | collective-permute-start | bytes 393224 | tf_op jit(solution)/shard_map/ppermute | solution.py:312
  57.1 4.3 %collective-permute-start.29 = (bf16[128,512]{1,0:T(8,128)(2,1)S(1)}, bf16[128,512]{1,0:T(8,128)(2,1)S(1)}, u32[]{:S(2)}, u32[]{:S(2)}) collective-permute-start(bf16[128,512]{1,0:T(8,128)(2,1)S(1)} %collective-permute-done.28), channel_id=1, source_target_pairs={{0,2},{2,0},{4,6},{6,4},{8,10},{10,8},{12,14},{14,12},{16,18},{18,... | collective-permute-start | bytes 393224 | tf_op jit(solution)/shard_map/ppermute | solution.py:243
  57.2 6.8 %collective-permute-start.30 = (bf16[128,512]{1,0:T(8,128)(2,1)S(1)}, bf16[128,512]{1,0:T(8,128)(2,1)S(1)}, u32[]{:S(2)}, u32[]{:S(2)}) collective-permute-start(bf16[128,512]{1,0:T(8,128)(2,1)S(1)} %collective-permute-done.27), channel_id=1, source_target_pairs={{0,8},{2,6},{8,16},{10,2},{16,24},{18,10},{24,28},{26,18},{28,20},... | collective-permute-start | bytes 393224 | tf_op jit(solution)/shard_map/ppermute | solution.py:312
  59.6 5.0 %collective-permute-start.20 = (bf16[128,512]{1,0:T(8,128)(2,1)S(1)}, bf16[128,512]{1,0:T(8,128)(2,1)S(1)}, u32[]{:S(2)}, u32[]{:S(2)}) collective-permute-start(bf16[128,512]{1,0:T(8,128)(2,1)S(1)} %collective-permute-done.16), channel_id=1, source_target_pairs={{0,8},{2,6},{8,16},{10,2},{16,24},{18,10},{24,28},{26,18},{28,20},... | collective-permute-start | bytes 393224 | tf_op jit(solution)/shard_map/ppermute | solution.py:312
  61.3 1.5 %collective-permute-start.17 = (bf16[128,512]{1,0:T(8,128)(2,1)S(1)}, bf16[128,512]{1,0:T(8,128)(2,1)S(1)}, u32[]{:S(2)}, u32[]{:S(2)}) collective-permute-start(bf16[128,512]{1,0:T(8,128)(2,1)S(1)} %collective-permute-done.16), channel_id=1, source_target_pairs={{0,2},{2,0},{4,6},{6,4},{8,10},{10,8},{12,14},{14,12},{16,18},{18,... | collective-permute-start | bytes 393224 | tf_op jit(solution)/shard_map/ppermute | solution.py:243
  61.4 6.3 %collective-permute-start.22 = (bf16[128,512]{1,0:T(8,128)(2,1)S(1)}, bf16[128,512]{1,0:T(8,128)(2,1)S(1)}, u32[]{:S(2)}, u32[]{:S(2)}) collective-permute-start(bf16[128,512]{1,0:T(8,128)(2,1)S(1)} %collective-permute-done.18), channel_id=1, source_target_pairs={{0,8},{2,6},{8,16},{10,2},{16,24},{18,10},{24,28},{26,18},{28,20},... | collective-permute-start | bytes 393224 | tf_op jit(solution)/shard_map/ppermute | solution.py:312
  62.7 1.4 %collective-permute-start.19 = (bf16[128,512]{1,0:T(8,128)(2,1)S(1)}, bf16[128,512]{1,0:T(8,128)(2,1)S(1)}, u32[]{:S(2)}, u32[]{:S(2)}) collective-permute-start(bf16[128,512]{1,0:T(8,128)(2,1)S(1)} %collective-permute-done.18), channel_id=1, source_target_pairs={{0,2},{2,0},{4,6},{6,4},{8,10},{10,8},{12,14},{14,12},{16,18},{18,... | collective-permute-start | bytes 393224 | tf_op jit(solution)/shard_map/ppermute | solution.py:243
  62.8 5.1 %collective-permute-start.36 = (bf16[128,512]{1,0:T(8,128)(2,1)S(1)}, bf16[128,512]{1,0:T(8,128)(2,1)S(1)}, u32[]{:S(2)}, u32[]{:S(2)}) collective-permute-start(bf16[128,512]{1,0:T(8,128)(2,1)S(1)} %collective-permute-done.32), channel_id=1, source_target_pairs={{0,8},{2,6},{8,16},{10,2},{16,24},{18,10},{24,28},{26,18},{28,20},... | collective-permute-start | bytes 393224 | tf_op jit(solution)/shard_map/ppermute | solution.py:312
  64.0 4.3 %collective-permute-start.33 = (bf16[128,512]{1,0:T(8,128)(2,1)S(1)}, bf16[128,512]{1,0:T(8,128)(2,1)S(1)}, u32[]{:S(2)}, u32[]{:S(2)}) collective-permute-start(bf16[128,512]{1,0:T(8,128)(2,1)S(1)} %collective-permute-done.32), channel_id=1, source_target_pairs={{0,2},{2,0},{4,6},{6,4},{8,10},{10,8},{12,14},{14,12},{16,18},{18,... | collective-permute-start | bytes 393224 | tf_op jit(solution)/shard_map/ppermute | solution.py:243
  64.1 2.1 %collective-permute-start.31 = (bf16[128,512]{1,0:T(8,128)(2,1)S(1)}, bf16[128,512]{1,0:T(8,128)(2,1)S(1)}, u32[]{:S(2)}, u32[]{:S(2)}) collective-permute-start(bf16[128,512]{1,0:T(8,128)(2,1)S(1)} %collective-permute-done.30), channel_id=1, source_target_pairs={{0,2},{2,0},{4,6},{6,4},{8,10},{10,8},{12,14},{14,12},{16,18},{18,... | collective-permute-start | bytes 393224 | tf_op jit(solution)/shard_map/ppermute | solution.py:243
  64.6 5.0 %collective-permute-start.34 = (bf16[128,512]{1,0:T(8,128)(2,1)S(1)}, bf16[128,512]{1,0:T(8,128)(2,1)S(1)}, u32[]{:S(2)}, u32[]{:S(2)}) collective-permute-start(bf16[128,512]{1,0:T(8,128)(2,1)S(1)} %collective-permute-done.30), channel_id=1, source_target_pairs={{0,8},{2,6},{8,16},{10,2},{16,24},{18,10},{24,28},{26,18},{28,20},... | collective-permute-start | bytes 393224 | tf_op jit(solution)/shard_map/ppermute | solution.py:312
  66.3 5.0 %collective-permute-start.24 = (bf16[128,512]{1,0:T(8,128)(2,1)S(1)}, bf16[128,512]{1,0:T(8,128)(2,1)S(1)}, u32[]{:S(2)}, u32[]{:S(2)}) collective-permute-start(bf16[128,512]{1,0:T(8,128)(2,1)S(1)} %collective-permute-done.20), channel_id=1, source_target_pairs={{0,8},{2,6},{8,16},{10,2},{16,24},{18,10},{24,28},{26,18},{28,20},... | collective-permute-start | bytes 393224 | tf_op jit(solution)/shard_map/ppermute | solution.py:312
  67.7 1.9 %collective-permute-start.21 = (bf16[128,512]{1,0:T(8,128)(2,1)S(1)}, bf16[128,512]{1,0:T(8,128)(2,1)S(1)}, u32[]{:S(2)}, u32[]{:S(2)}) collective-permute-start(bf16[128,512]{1,0:T(8,128)(2,1)S(1)} %collective-permute-done.20), channel_id=1, source_target_pairs={{0,2},{2,0},{4,6},{6,4},{8,10},{10,8},{12,14},{14,12},{16,18},{18,... | collective-permute-start | bytes 393224 | tf_op jit(solution)/shard_map/ppermute | solution.py:243
  67.9 3.5 %collective-permute-start.23 = (bf16[128,512]{1,0:T(8,128)(2,1)S(1)}, bf16[128,512]{1,0:T(8,128)(2,1)S(1)}, u32[]{:S(2)}, u32[]{:S(2)}) collective-permute-start(bf16[128,512]{1,0:T(8,128)(2,1)S(1)} %collective-permute-done.22), channel_id=1, source_target_pairs={{0,2},{2,0},{4,6},{6,4},{8,10},{10,8},{12,14},{14,12},{16,18},{18,... | collective-permute-start | bytes 393224 | tf_op jit(solution)/shard_map/ppermute | solution.py:243
  68.3 5.0 %collective-permute-start.40 = (bf16[128,512]{1,0:T(8,128)(2,1)S(1)}, bf16[128,512]{1,0:T(8,128)(2,1)S(1)}, u32[]{:S(2)}, u32[]{:S(2)}) collective-permute-start(bf16[128,512]{1,0:T(8,128)(2,1)S(1)} %collective-permute-done.36), channel_id=1, source_target_pairs={{0,8},{2,6},{8,16},{10,2},{16,24},{18,10},{24,28},{26,18},{28,20},... | collective-permute-start | bytes 393224 | tf_op jit(solution)/shard_map/ppermute | solution.py:312
  69.6 5.1 %collective-permute-start.37 = (bf16[128,512]{1,0:T(8,128)(2,1)S(1)}, bf16[128,512]{1,0:T(8,128)(2,1)S(1)}, u32[]{:S(2)}, u32[]{:S(2)}) collective-permute-start(bf16[128,512]{1,0:T(8,128)(2,1)S(1)} %collective-permute-done.36), channel_id=1, source_target_pairs={{0,2},{2,0},{4,6},{6,4},{8,10},{10,8},{12,14},{14,12},{16,18},{18,... | collective-permute-start | bytes 393224 | tf_op jit(solution)/shard_map/ppermute | solution.py:243
  69.6 5.0 %collective-permute-start.38 = (bf16[128,512]{1,0:T(8,128)(2,1)S(1)}, bf16[128,512]{1,0:T(8,128)(2,1)S(1)}, u32[]{:S(2)}, u32[]{:S(2)}) collective-permute-start(bf16[128,512]{1,0:T(8,128)(2,1)S(1)} %collective-permute-done.34), channel_id=1, source_target_pairs={{0,8},{2,6},{8,16},{10,2},{16,24},{18,10},{24,28},{26,18},{28,20},... | collective-permute-start | bytes 393224 | tf_op jit(solution)/shard_map/ppermute | solution.py:312
  71.3 3.4 %collective-permute-start.35 = (bf16[128,512]{1,0:T(8,128)(2,1)S(1)}, bf16[128,512]{1,0:T(8,128)(2,1)S(1)}, u32[]{:S(2)}, u32[]{:S(2)}) collective-permute-start(bf16[128,512]{1,0:T(8,128)(2,1)S(1)} %collective-permute-done.34), channel_id=1, source_target_pairs={{0,2},{2,0},{4,6},{6,4},{8,10},{10,8},{12,14},{14,12},{16,18},{18,... | collective-permute-start | bytes 393224 | tf_op jit(solution)/shard_map/ppermute | solution.py:243
  71.4 4.7 %collective-permute-start.25 = (bf16[128,512]{1,0:T(8,128)(2,1)S(1)}, bf16[128,512]{1,0:T(8,128)(2,1)S(1)}, u32[]{:S(2)}, u32[]{:S(2)}) collective-permute-start(bf16[128,512]{1,0:T(8,128)(2,1)S(1)} %collective-permute-done.24), channel_id=1, source_target_pairs={{0,2},{2,0},{4,6},{6,4},{8,10},{10,8},{12,14},{14,12},{16,18},{18,... | collective-permute-start | bytes 393224 | tf_op jit(solution)/shard_map/ppermute | solution.py:243
  73.3 2.8 %collective-permute-start.41 = (bf16[128,512]{1,0:T(8,128)(2,1)S(1)}, bf16[128,512]{1,0:T(8,128)(2,1)S(1)}, u32[]{:S(2)}, u32[]{:S(2)}) collective-permute-start(bf16[128,512]{1,0:T(8,128)(2,1)S(1)} %collective-permute-done.40), channel_id=1, source_target_pairs={{0,2},{2,0},{4,6},{6,4},{8,10},{10,8},{12,14},{14,12},{16,18},{18,... | collective-permute-start | bytes 393224 | tf_op jit(solution)/shard_map/ppermute | solution.py:243
  74.7 1.3 %collective-permute-start.39 = (bf16[128,512]{1,0:T(8,128)(2,1)S(1)}, bf16[128,512]{1,0:T(8,128)(2,1)S(1)}, u32[]{:S(2)}, u32[]{:S(2)}) collective-permute-start(bf16[128,512]{1,0:T(8,128)(2,1)S(1)} %collective-permute-done.38), channel_id=1, source_target_pairs={{0,2},{2,0},{4,6},{6,4},{8,10},{10,8},{12,14},{14,12},{16,18},{18,... | collective-permute-start | bytes 393224 | tf_op jit(solution)/shard_map/ppermute | solution.py:243
